TPU v7x, 32 devices: a whole 2x2x4 slice. The times are simulated.
32 devices in a mesh: grp: 4 (over y, core), dev: 8 (over z, x).
Axes of the slice: x: 2, y: 2, z: 4, core: 2. Of those that a mesh axis runs over, the one named last changes fastest.
Arguments:
- conc_old: float32 [128, 256, 256], P('grp', 'dev'), may hold values from 0.5 to 2
- phi_old: float32 [128, 256, 256], P('grp', 'dev'), may hold values from -6 to 6
- solid_pot: float32 [128, 256, 256], P('grp', 'dev'), may hold values from -4.5 to 6
- phase_label: int32 [128, 256, 256], P('grp', 'dev'), may hold values from 0 to 2
- iface_block: int32 [4, 2048], P('grp', 'dev'), may hold values from 0 to 2047
- iface_owner: int32 [4, 2048, 1], P('grp', 'dev'), may hold values from 0 to 7; in each aligned block of 256 rows (0 to 255, 256 to 511, ..., all dimensions but the last counted through in order) at most 64 rows name the same one
Outputs:
- concentration: float32 [128, 256, 256], P('grp', 'dev')
- flux: float32 [128, 256, 256], P('grp', 'dev')
- potential: float32 [128, 256, 256], P('grp', 'dev')
Inputs may be any that keep to these rules, and one draw needn't show every extreme that they name: `iface_owner`: among the 256 entries of one index of dev, no owner is named more than 64 times, a bound that some block reaches.
All inputs are finite; a program needn't handle non-finite values.
Results may differ from a plain program's by a relative error of at most 0.0005.
Values sent between devices are 32-bit elements; how exact they have to be, the bound alone decides.
No kernel may reach another device: no remote copies, remote signals or barrier semaphores. Data moves between devices by JAX's collectives and lax.ppermute only.
A program may use at most 64 MiB of HBM per device.

v0:
```python
import jax
import jax.numpy as jnp
from jax import lax
from jax.experimental import pallas as pl
from jax.experimental.pallas import tpu as pltpu
from jax.sharding import PartitionSpec as P


F32 = jnp.float32
MASS = 0.05
OMEGA = 0.8
DIFFUSION_TABLE = (1.5, 0.1, 0.4)
CONDUCT_TABLE = (1.0, 0.3, 0.6)
KINETIC_TABLE = (0.2, 1.0, 0.5)
SWEEPS = 4
COARSE_SWEEPS = 8
COARSE_NEAR = 8
HALO = 4
LANES = 128
VMEM_LIMIT = 28 * 1024 * 1024


def shaped(*shape):
    return jax.ShapeDtypeStruct(shape, F32)


WHOLE = pl.BlockSpec(memory_space=pltpu.VMEM)
FAR = pl.BlockSpec(memory_space=pltpu.HBM)


def call(kernel, outs, args, scratch=(), in_specs=None, out_specs=None, flops=10**6, name=None):
    size = sum(4 * a.size for a in args) + sum(4 * o.size for o in outs)
    return pl.pallas_call(
        kernel,
        out_shape=tuple(outs),
        in_specs=in_specs or [WHOLE] * len(args),
        out_specs=tuple(out_specs or [WHOLE] * len(outs)),
        scratch_shapes=list(scratch),
        compiler_params=pltpu.CompilerParams(vmem_limit_bytes=VMEM_LIMIT),
        cost_estimate=pl.CostEstimate(flops=flops, bytes_accessed=size, transcendentals=0),
        name=name,
    )(*args)


def vmem(*shape):
    return pltpu.VMEM(shape, F32)


def iota(shape, dim):
    return lax.broadcasted_iota(jnp.int32, shape, dim)


def pick(label, table):
    return jnp.where(label == 0, table[0], jnp.where(label == 1, table[1], table[2])).astype(F32)


def loop(low, high, body, unroll=8):
    steps = (high - low) // unroll

    def step(i, carry):
        for u in range(unroll):
            body(low + i * unroll + u)
        return carry

    if steps > 1:
        lax.fori_loop(0, steps, step, 0)
    else:
        steps = 0
    for x in range(low + steps * unroll, high):
        body(x)


def even(axis):
    return lax.rem(lax.axis_index(axis), 2) == 0


def along_y(v):
    return pltpu.roll(v, 1, 0) + pltpu.roll(v, v.shape[0] - 1, 0)


def along_z(v):
    low, high = v[:, :LANES], v[:, LANES:]
    lane = iota(low.shape, 1)
    first, last = lane == 0, lane == LANES - 1
    low_up, high_up = pltpu.roll(low, 1, 1), pltpu.roll(high, 1, 1)
    low_down, high_down = pltpu.roll(low, LANES - 1, 1), pltpu.roll(high, LANES - 1, 1)
    low_sum = jnp.where(first, 0.0, low_up) + jnp.where(last, high_down, low_down)
    high_sum = jnp.where(first, low_up, high_up) + jnp.where(last, 0.0, high_down)
    return jnp.concatenate([low_sum, high_sum], axis=1)


def upper(shape=(8, 256)):
    return iota(shape, 0) < HALO


def twice(tile, scratch):
    for h in range(2):
        part = tile[:, h * LANES : (h + 1) * LANES]
        scratch[h, pl.ds(0, 8, stride=2), :] = part
        scratch[h, pl.ds(1, 8, stride=2), :] = part
    return jnp.concatenate([scratch[0], scratch[1]], axis=1)


def pair_rows(v, scratch):
    half = v.shape[0] // 2
    parts = []
    for h in range(2):
        scratch[h] = v[:, h * LANES : (h + 1) * LANES]
        parts.append(scratch[h, pl.ds(0, half, stride=2), :] + scratch[h, pl.ds(1, half, stride=2), :])
    return jnp.concatenate(parts, axis=1)


def either(flag, if_true, if_false):
    return jnp.where(flag, if_true, if_false)


def y_sides(r_a, r_b, at, count):
    flag = even("dev")
    a, b = r_a[at : at + count, :], r_b[at : at + count, :]
    return either(flag, a, b), either(flag, b, a)


def x_sides(r_a, r_b, index):
    flag = even("grp")
    a, b = r_a[index], r_b[index]
    return either(flag, a, b), either(flag, b, a)


def send_y(pay_a, pay_b, at, first, last):
    flag = even("dev")
    n = first.shape[0]
    pay_a[at : at + n, :] = either(flag, last, first)
    pay_b[at : at + n, :] = either(flag, first, last)


def send_x(pay_a, pay_b, index, first, last):
    flag = even("grp")
    pay_a[index] = either(flag, last, first)
    pay_b[index] = either(flag, first, last)


def halo_tile(after, before):
    parts = [after]
    if after.shape[0] < HALO:
        parts.append(jnp.zeros((2 * HALO - 2 * after.shape[0], after.shape[1]), F32))
    return jnp.concatenate(parts + [before], axis=0)


def first_pack_kernel(conc, label, owner, block, pay_a, pay_b, c_first, c_last, l_first, l_last, sems):
    nx = conc.shape[0]
    copies = []
    for i, (ref, at, to) in enumerate(((conc, 0, c_first), (conc, 24, c_last), (label, 0, l_first), (label, 24, l_last))):
        copies.append(pltpu.make_async_copy(ref.at[:, pl.ds(at, 8), :], to, sems.at[i]))
        copies[-1].start()
    named = jnp.concatenate([owner[...], block[...], jnp.zeros((6, 256), jnp.int32)], axis=0).astype(F32)
    pay_a[7 * nx : 7 * nx + 8, :] = named
    pay_b[7 * nx : 7 * nx + 8, :] = named
    for c in copies:
        c.wait()
    for x in range(nx):
        send_y(pay_a, pay_b, 7 * x, c_first[x, 0:4, :], c_last[x, 4:8, :])
        send_y(pay_a, pay_b, 7 * x + 4, l_first[x, 0:3, :].astype(F32), l_last[x, 5:8, :].astype(F32))


def own_kernel(conc, label, phi, mid, coarse, pay_a, pay_b, pairs, pairs_2):
    nx = conc.shape[0]
    half = nx // 2

    def coarsen(i):
        total = conc[2 * i] * pick(label[2 * i], CONDUCT_TABLE) + conc[2 * i + 1] * pick(label[2 * i + 1], CONDUCT_TABLE)
        mid[i] = 0.25 * pair_rows(total, pairs.at[i])

    loop(0, half, coarsen, 4)
    for i in range(half // 2):
        coarse[i] = 0.25 * pair_rows(mid[2 * i] + mid[2 * i + 1], pairs_2.at[i])
    for k in range(HALO):
        for t in range(4):
            rows = slice(8 * t, 8 * t + 8)
            send_x(pay_a, pay_b, 4 * k + t, phi[k, rows, :], phi[nx - HALO + k, rows, :])
        for t in range(2):
            rows = slice(8 * t, 8 * t + 8)
            send_x(pay_a, pay_b, 16 + 2 * k + t, mid[k, rows, :], mid[half - HALO + k, rows, :])


def first_pack_x_kernel(conc, label, r_a, r_b, token, pay_a, pay_b):
    nx = conc.shape[0]

    def plane(ref, k, t, offset, count):
        if t < 4:
            return ref[k, 8 * t : 8 * t + 8, :].astype(F32)
        return halo_tile(*y_sides(r_a, r_b, 7 * k + offset, count))

    for t in range(5):
        for k in range(HALO):
            send_x(pay_a, pay_b, 5 * k + t, plane(conc, k, t, 0, 4), plane(conc, nx - HALO + k, t, 0, 4))
        for k in range(3):
            send_x(pay_a, pay_b, 20 + 5 * k + t, plane(label, k, t, 4, 3), plane(label, nx - 3 + k, t, 4, 3))


def second_pack_kernel(phi, mid, coarse, x_a, x_b, pay_a, pay_b, pay_c, pay_d):
    nx = phi.shape[0]
    half = nx // 2
    for x in range(nx):
        send_y(pay_a, pay_b, 4 * (HALO + x), phi[x, 0:4, :], phi[x, 28:32, :])
    for k in range(HALO):
        for t, at in ((0, slice(0, 4)), (3, slice(4, 8))):
            after, before = x_sides(x_a, x_b, 4 * k + t)
            if t == 0:
                first_after, first_before = after[at], before[at]
            else:
                last_after, last_before = after[at], before[at]
        send_y(pay_a, pay_b, 4 * k, first_before, last_before)
        send_y(pay_a, pay_b, 4 * (HALO + nx + k), first_after, last_after)
    base = 4 * (nx + 2 * HALO)
    for x in range(half):
        send_y(pay_a, pay_b, base + 4 * (HALO + x), mid[x, 0:4, :], mid[x, 12:16, :])
    for k in range(HALO):
        first_after, first_before = (v[0:4] for v in x_sides(x_a, x_b, 16 + 2 * k))
        last_after, last_before = (v[4:8] for v in x_sides(x_a, x_b, 16 + 2 * k + 1))
        send_y(pay_a, pay_b, base + 4 * k, first_before, last_before)
        send_y(pay_a, pay_b, base + 4 * (HALO + half + k), first_after, last_after)
    base += 4 * (half + 2 * HALO)
    for x in range(8):
        pay_a[base + 8 * x : base + 8 * x + 8, :] = coarse[x]
        pay_b[base + 8 * x : base + 8 * x + 8, :] = coarse[x]
    far_edges(coarse, pay_c, pay_d)


def far_edges(field, pay_c, pay_d):
    flag = low_pair()
    for x in range(8):
        first, last = field[x, 0:1, :], field[x, 7:8, :]
        pay_c[x : x + 1, :] = either(flag, last, first)
        pay_d[x : x + 1, :] = either(flag, first, last)


def low_pair():
    return lax.rem(lax.axis_index("dev"), 4) < 2


def wide_plane(own, r_a, r_b, r_c, r_d, base, x):
    flag = low_pair()
    c, d = r_c[x : x + 1, :], r_d[x : x + 1, :]
    after, before = y_sides(r_a, r_b, base + 8 * x, 8)
    gap = jnp.zeros((6, 256), F32)
    return jnp.concatenate([own[x], after, either(flag, c, d), gap, either(flag, d, c), before], axis=0)


def sweeps_kernel(conc, label, y_a, y_b, x_a, x_b, out, one, two, gain, base):
    nx = conc.shape[0]
    ratio = tuple(d / (1.0 + 6.0 * d) for d in DIFFUSION_TABLE)
    inverse = tuple(1.0 / (1.0 + 6.0 * d) for d in DIFFUSION_TABLE)

    def put(x, rows, c, lab):
        one[x, rows, :] = c
        gain[x, rows, :] = jnp.where(c > 0.0, pick(lab, ratio), 0.0)
        base[x, rows, :] = c * pick(lab, inverse)

    def own(i):
        put(HALO + i, slice(0, 32), conc[i], label[i])

    loop(0, nx, own)
    for i in range(nx):
        c = halo_tile(*y_sides(y_a, y_b, 7 * i, 4))
        lab = halo_tile(*y_sides(y_a, y_b, 7 * i + 4, 3))
        put(HALO + i, slice(32, 40), c, lab)
    for t in range(5):
        rows = slice(8 * t, 8 * t + 8)
        for k in range(HALO):
            c_after, c_before = x_sides(x_a, x_b, 5 * k + t)
            l_after = x_sides(x_a, x_b, 20 + 5 * min(k, 2) + t)[0]
            l_before = x_sides(x_a, x_b, 20 + 5 * max(k - 1, 0) + t)[1]
            put(k, rows, c_before, l_before)
            put(HALO + nx + k, rows, c_after, l_after)

    def stencil(old, x):
        mid = old[x]
        return base[x] + gain[x] * ((old[x - 1] + old[x + 1]) + (along_y(mid) + along_z(mid)))

    fields = (one, two)
    for s in range(1, SWEEPS):
        old, new = fields[(s - 1) % 2], fields[s % 2]

        def sweep(x, old=old, new=new):
            new[x] = stencil(old, x)

        loop(s, nx + 2 * HALO - s, sweep)

    old = fields[(SWEEPS - 1) % 2]

    def last(i):
        out[i] = stencil(old, HALO + i)[0:32, :]

    loop(0, nx, last)


def flux_kernel(conc, label, phi, solid, lists, flux, pay_a, pay_b, marked):
    nx = conc.shape[0]
    entries = lists.shape[0] // 2 * 256
    owner = jnp.concatenate([lists[2 * i : 2 * i + 1, :] for i in range(entries // 256)], axis=1)
    block = jnp.concatenate([lists[2 * i + 1 : 2 * i + 2, :] for i in range(entries // 256)], axis=1)
    here = lax.axis_index("dev")
    block = jnp.where(owner.astype(jnp.int32) == here, block.astype(jnp.int32), -1)
    hit_row = (iota((32, entries), 0) == lax.shift_right_arithmetic(block, 6)).astype(jnp.bfloat16)
    hit_column = (iota((LANES, entries), 0) == lax.rem(block, 64)).astype(jnp.bfloat16)
    named = lax.dot_general(hit_row, hit_column, (((1,), (1,)), ((), ())), preferred_element_type=F32)
    for i in range(32):
        marked[i] = jnp.broadcast_to(named[i : i + 1, :], (8, LANES))
    is_row = lax.div(iota((32, LANES), 1), 2) == iota((32, LANES), 0)
    spread = (lax.rem(iota((LANES, 256), 0), 2) == lax.div(iota((LANES, 256), 1), LANES)).astype(jnp.bfloat16)

    def plane(i):
        marks = jnp.where(is_row, jnp.concatenate([marked[i]] * 4, axis=0), 0.0).astype(jnp.bfloat16)
        listed = jnp.dot(marks, spread, preferred_element_type=F32) > 0.5
        drive = 0.5 * (solid[i] - phi[i])
        logc = jnp.log(conc[i])
        value = jnp.exp(drive + 0.4 * logc) - jnp.exp(0.6 * logc - drive)
        flux[i] = jnp.where(listed, pick(label[i], KINETIC_TABLE) * value, 0.0)

    loop(0, nx, plane, 4)
    for x in range(nx):
        send_y(pay_a, pay_b, 3 * x, flux[x, 0:3, :], flux[x, 29:32, :])


def store_kernel(conc, flux, conc_out, flux_out, token, sems):
    copies = []
    for i, (ref, to) in enumerate(((conc, conc_out), (flux, flux_out))):
        for j in range(4):
            rows = pl.ds(8 * j, 8)
            copies.append(pltpu.make_async_copy(ref.at[rows], to.at[rows], sems.at[4 * i + j]))
            copies[-1].start()
    token[...] = jnp.zeros(token.shape, F32)
    for c in copies:
        c.wait()


def ready_kernel(conc, label, phi, y_a, y_b, x_a, x_b, yy_a, yy_b, xx_a, xx_b, weight, scale, share, start, token, field):
    nx = conc.shape[0]
    token[...] = jnp.zeros(token.shape, F32)

    def put(x, rows, c, lab, p):
        conduct = c * pick(lab, CONDUCT_TABLE)
        factor = OMEGA / (MASS + 6.0 * conduct)
        weight[x, rows, :] = conduct * factor
        scale[x, rows, :] = factor
        share[x, rows, :] = MASS * p * factor
        field[x, rows, :] = p

    def own(i):
        put(HALO + i, slice(0, 32), conc[i], label[i], phi[i])

    loop(0, nx, own, 4)
    low = slice(32, 40)
    for i in range(nx):
        c = halo_tile(*y_sides(y_a, y_b, 7 * i, 4))
        lab = halo_tile(*y_sides(y_a, y_b, 7 * i + 4, 3))
        put(HALO + i, low, c, lab, halo_tile(*y_sides(yy_a, yy_b, 4 * (HALO + i), 4)))
    for t in range(5):
        rows = slice(8 * t, 8 * t + 8)
        for k in range(HALO):
            c_after, c_before = x_sides(x_a, x_b, 5 * k + t)
            l_after = x_sides(x_a, x_b, 20 + 5 * min(k, 2) + t)[0]
            l_before = x_sides(x_a, x_b, 20 + 5 * max(k - 1, 0) + t)[1]
            if t < 4:
                p_after, p_before = x_sides(xx_a, xx_b, 4 * k + t)
            else:
                p_after = halo_tile(*y_sides(yy_a, yy_b, 4 * (HALO + nx + k), 4))
                p_before = halo_tile(*y_sides(yy_a, yy_b, 4 * k, 4))
            put(k, rows, c_before, l_before, p_before)
            put(HALO + nx + k, rows, c_after, l_after, p_after)

    def sweep(x):
        p = field[x]
        around = (field[x - 1] + field[x + 1]) + (along_y(p) + along_z(p))
        start[x] = 0.2 * p + share[x] + weight[x] * around

    loop(1, nx + 2 * HALO - 1, sweep)


def flux_pack_x_kernel(flux, r_a, r_b, token, token_2, pay_a, pay_b):
    nx = flux.shape[0]

    def tile(x, t):
        if t < 4:
            return flux[x, 8 * t : 8 * t + 8, :]
        return halo_tile(*y_sides(r_a, r_b, 3 * x, 3))

    for k in range(3):
        for t in range(5):
            send_x(pay_a, pay_b, 5 * k + t, tile(k, t), tile(nx - 3 + k, t))


def potential_kernel(
    flux, y_a, y_b, x_a, x_b, weight, scale, share, start, after_two, source, source_mid, pay_a, pay_b, field, pairs
):
    nx = flux.shape[0]
    half = nx // 2

    def put(x, rows, f):
        part = scale[x, rows, :] * f
        source[x, rows, :] = share[x, rows, :] + part
        field[x, rows, :] = start[x, rows, :] + part

    def own(i):
        put(HALO + i, slice(0, 32), flux[i])

    loop(0, nx, own)
    for i in range(nx):
        put(HALO + i, slice(32, 40), halo_tile(*y_sides(y_a, y_b, 3 * i, 3)))
    for k in range(3):
        for t in range(5):
            rows = slice(8 * t, 8 * t + 8)
            after, before = x_sides(x_a, x_b, 5 * k + t)
            put(1 + k, rows, before)
            put(HALO + nx + k, rows, after)

    def around(values, x):
        v = values[x]
        return v, weight[x] * ((values[x - 1] + values[x + 1]) + (along_y(v) + along_z(v)))

    def sweep(x):
        v, near = around(field, x)
        after_two[x] = 0.2 * v + (source[x] + near)

    loop(2, nx + 2 * HALO - 2, sweep)

    def remainder(x):
        v, near = around(after_two, x)
        return ((source[x] - OMEGA * v) + near)[0:32, :] / scale[x, 0:32, :]

    def coarsen(i):
        x = HALO + 2 * i
        source_mid[i] = 0.25 * pair_rows(remainder(x) + remainder(x + 1), pairs.at[i])

    loop(0, half, coarsen, 4)
    for x in range(half):
        send_y(pay_a, pay_b, 4 * x, source_mid[x, 0:4, :], source_mid[x, 12:16, :])


def mid_pack_x_kernel(field, r_a, r_b, token, pay_a, pay_b):
    n = field.shape[0]

    def tile(x, t):
        if t < 2:
            return field[x, 8 * t : 8 * t + 8, :]
        return halo_tile(*y_sides(r_a, r_b, 4 * x, 4))

    for k in range(HALO):
        for t in range(3):
            send_x(pay_a, pay_b, 3 * k + t, tile(k, t), tile(n - HALO + k, t))


def mid_kernel(
    source_own, conduct_own, yy_a, yy_b, xx_a, xx_b, y_a, y_b, x_a, x_b, rho, load,
    after_two, source, weight, coarse, pay_a, pay_b, pay_c, pay_d, part, scale, pairs, pairs_2,
):
    n = source_own.shape[0]
    base = 4 * (2 * n + 2 * HALO)

    def put(x, rows, b, conduct):
        factor = OMEGA / (MASS + 3.0 * conduct)
        weight[x, rows, :] = conduct * factor
        scale[x, rows, :] = factor
        source[x, rows, :] = factor * b

    def far(x):
        return halo_tile(*y_sides(yy_a, yy_b, base + 4 * x, 4))

    for i in range(n):
        put(HALO + i, slice(0, 16), source_own[i], conduct_own[i])
        put(HALO + i, slice(16, 24), halo_tile(*y_sides(y_a, y_b, 4 * i, 4)), far(HALO + i))
    for k in range(HALO):
        for t in range(3):
            rows = slice(8 * t, 8 * t + 8)
            b_after, b_before = x_sides(x_a, x_b, 3 * k + t)
            if t < 2:
                c_after, c_before = x_sides(xx_a, xx_b, 16 + 2 * k + t)
            else:
                c_after, c_before = far(HALO + n + k), far(k)
            put(k, rows, b_before, c_before)
            put(HALO + n + k, rows, b_after, c_after)

    def around(values, x):
        v = values[x]
        return v, weight[x] * (0.25 * ((values[x - 1] + values[x + 1]) + along_y(v)) + along_z(v))

    def sweep(x):
        v, near = around(source, x)
        after_two[x] = 0.2 * v + (source[x] + near)

    loop(1, n + 2 * HALO - 1, sweep, 11)

    def remainder(x):
        v, near = around(after_two, x)
        return ((source[x] - OMEGA * v) + near)[0:16, :] / scale[x, 0:16, :]

    total = jnp.zeros((8, 256), F32)
    for i in range(n // 2):
        x = HALO + 2 * i
        value = 0.25 * pair_rows(remainder(x) + remainder(x + 1), pairs.at[i])
        coarse[i] = value
        pay_a[8 * i : 8 * i + 8, :] = value
        pay_b[8 * i : 8 * i + 8, :] = value
        total += rho[i] * value
    sums = jnp.concatenate([total[:, :LANES] + total[:, LANES:], load[...]], axis=1)
    pay_a[64:72, :] = sums
    pay_b[64:72, :] = sums
    part[...] = sums
    far_edges(coarse, pay_c, pay_d)


COARSE_W = 0.0625


def coarse_sum(values, x):
    v = values[x]
    inner = along_y(v)
    if x > 0:
        inner = inner + values[x - 1]
    if x < len(values) - 1:
        inner = inner + values[x + 1]
    return COARSE_W * inner + along_z(v)


def coarse_ready_kernel(own, r_a, r_b, r_c, r_d, weight, scale, rho, load, token, one, two, conduct):
    token[...] = jnp.zeros(token.shape, F32)
    base = r_a.shape[0] - 64
    for x in range(8):
        k = wide_plane(own, r_a, r_b, r_c, r_d, base, x)
        factor = OMEGA / (MASS + 2.25 * k)
        conduct[x] = k
        weight[x] = k * factor
        scale[x] = factor
        one[x] = jnp.ones(k.shape, F32)
    fields = (one, two)
    for s in range(COARSE_SWEEPS):
        old, new = fields[s % 2], fields[(s + 1) % 2]
        for x in range(8):
            near = [conduct[i] * old[i] if 0 <= i < 8 else None for i in (x - 1, x, x + 1)]
            inner = along_y(near[1])
            for other in (near[0], near[2]):
                if other is not None:
                    inner = inner + other
            new[x] = 0.2 * old[x] + scale[x] * (COARSE_W * inner + along_z(near[1]))
    last = fields[COARSE_SWEEPS % 2]
    peer, peers = lax.axis_index("dev"), lax.axis_size("dev")
    row, z = iota((8, 256), 0), iota((8, 256), 1)
    edge_y = ((row == 0) & (peer == 0)) | ((row == 7) & (peer == peers - 1))
    edge = edge_y.astype(F32) * COARSE_W + ((z == 0) | (z == 255)).astype(F32)
    total = jnp.zeros((8, 256), F32)
    for x in range(8):
        rho[x] = last[x, 0:8, :]
        total += MASS + own[x] * (edge + (COARSE_W if x in (0, 7) else 0.0))
    load[...] = total[:, :LANES] + total[:, LANES:]


def coarse_kernel(own, r_a, r_b, r_c, r_d, weight, scale, error, source, one, two):
    for x in range(8):
        source[x] = scale[x] * wide_plane(own, r_a, r_b, r_c, r_d, 0, x)
    old = source
    for s in range(1, COARSE_SWEEPS):
        new = one if s % 2 else two
        planes = [old.at[x] for x in range(8)]
        for x in range(8):
            v = old[x]
            inner = along_y(v)
            if x > 0:
                inner = inner + old[x - 1]
            if x < 7:
                inner = inner + old[x + 1]
            new[x] = 0.2 * v + (source[x] + weight[x] * (COARSE_W * inner + along_z(v)))
        old = new
    for x in range(8):
        error[x, 0:8, :] = old[x, 0:8, :]
        error[x, 8:16, :] = jnp.where(upper(), old[x, 8:16, :], old[x, 24:32, :])


def shift_kernel(error, sums, out, pay_a, pay_b):
    resid = jnp.sum(sums[:, :LANES])
    load = jnp.sum(sums[:, LANES:])
    shift_c = jnp.full((16, 256), resid, F32) / jnp.full((16, 256), load, F32)
    for x in range(8):
        out[x] = error[x] + shift_c
    for k in range(2):
        send_x(pay_a, pay_b, k, out[k], out[6 + k])


def finish_kernel(
    error, x_a, x_b, mid_two, mid_source, mid_weight, fine_two, fine_source, fine_weight,
    out, one, two, fine_one, fine_last, dup, dup_2, result, sems,
):
    n = mid_two.shape[0]
    nf = fine_two.shape[0]
    nx = out.shape[0]

    def squeeze(tile):
        return jnp.where(iota((8, 256), 0) < 2, tile, pltpu.roll(tile, 4, 0))

    after, before = x_sides(x_a, x_b, slice(0, 2))
    for c in range(-2, 10):
        plane = before[c + 2] if c < 0 else (after[c - 8] if c >= 8 else error[c])
        room = dup.at[c + 2]
        spread = jnp.concatenate([twice(plane[0:8], room.at[0]), twice(squeeze(plane[8:16]), room.at[1])[0:8]], axis=0)
        for x in (2 * c + HALO, 2 * c + 1 + HALO):
            one[x] = jnp.where(mid_weight[x] > 0.0, mid_two[x] + spread, 0.0)

    def around(values, weights, x, w):
        v = values[x]
        inner = (values[x - 1] + values[x + 1]) + along_y(v)
        return 0.2 * v + weights[x] * (w * inner + along_z(v))

    for s, (old, new) in ((2, (one, two)), (3, (two, one))):

        def sweep(x, old=old, new=new):
            new[x] = mid_source[x] + around(old, mid_weight, x, 0.25)

        loop(s, n - s, sweep, 10)

    def lift(m):
        plane = one[m]
        room = dup_2.at[m]
        spread = jnp.concatenate(
            [twice(plane[0:8], room.at[0]), twice(plane[8:16], room.at[1]), twice(squeeze(plane[16:24]), room.at[2])[0:8]],
            axis=0,
        )
        x = 2 * m - HALO
        fine_one[x] = fine_two[x] + spread
        fine_one[x + 1] = fine_two[x + 1] + spread

    loop(3, n - 3, lift, 6)

    def sweep_one(x):
        fine_last[x] = fine_source[x] + around(fine_one, fine_weight, x, 1.0)

    loop(3, nf - 3, sweep_one)
    copies = []
    for j in range(nx // 8):

        def sweep_two(i):
            x = HALO + i
            result[i] = (fine_source[x] + around(fine_last, fine_weight, x, 1.0))[0:32, :]

        for i in range(8 * j, 8 * j + 8):
            sweep_two(i)
        rows = pl.ds(8 * j, 8)
        copies.append(pltpu.make_async_copy(result.at[rows], out.at[rows], sems.at[j]))
        copies[-1].start()
    for c in copies:
        c.wait()


def both_ways(pairs):
    return pairs + [(j, i) for i, j in pairs]


def swap(pay_a, pay_b, axis):
    size = lax.axis_size(axis)
    pairs_a = [(i, i + 1) for i in range(0, size - 1, 2)]
    pairs_b = [(i, i + 1) for i in range(1, size - 1, 2)]
    return lax.ppermute(pay_a, axis, both_ways(pairs_a)), lax.ppermute(pay_b, axis, both_ways(pairs_b))


def swap_far(pay_c, pay_d):
    size = lax.axis_size("dev")
    pairs_c = [(i, i + 2) for i in range(size - 2) if i % 4 < 2]
    pairs_d = [(i, i + 2) for i in range(size - 2) if i % 4 >= 2]
    return lax.ppermute(pay_c, "dev", both_ways(pairs_c)), lax.ppermute(pay_d, "dev", both_ways(pairs_d))


def exchange(value, distance):
    return lax.ppermute(value, "dev", [(i, i ^ distance) for i in range(lax.axis_size("dev"))])


def body(conc_old, phi_old, solid_pot, phase_label, iface_block, iface_owner):
    peers = lax.axis_size("dev")
    nx = conc_old.shape[0]
    half = nx // 2
    quarter = nx // 4
    ext = (nx + 2 * HALO, nx + 2 * HALO, 256)
    ext_mid = (half + 2 * HALO, half + 2 * HALO, 256)
    token_shape = shaped(8, LANES)

    pay_a, pay_b = call(
        first_pack_kernel,
        [shaped(7 * nx + 8, 256)] * 2,
        [conc_old, phase_label, iface_owner.reshape(1, -1), iface_block],
        [vmem(nx, 8, 256)] * 2 + [pltpu.VMEM((nx, 8, 256), jnp.int32)] * 2 + [pltpu.SemaphoreType.DMA((4,))],
        in_specs=[FAR, FAR, WHOLE, WHOLE],
        name="first_pack",
    )
    own_lists = pay_a[7 * nx : 7 * nx + 2]
    y_a, y_b = swap(pay_a, pay_b, "dev")
    conduct_mid, conduct_coarse, pay_a, pay_b = call(
        own_kernel,
        [shaped(half, half, 256), shaped(quarter, quarter, 256), shaped(24, 8, 256), shaped(24, 8, 256)],
        [conc_old, phase_label, phi_old],
        [vmem(half, 2, nx, LANES), vmem(quarter, 2, half, LANES)],
        name="own",
    )
    xx_a, xx_b = swap(pay_a, pay_b, "grp")
    pay_a, pay_b = call(
        first_pack_x_kernel,
        [shaped(35, 8, 256)] * 2,
        [conc_old, phase_label, y_a, y_b, conduct_coarse],
        name="first_pack_x",
    )
    x_a, x_b = swap(pay_a, pay_b, "grp")
    lists = jnp.concatenate([own_lists, y_a[7 * nx : 7 * nx + 2]], axis=0)
    distance = 2
    while distance < peers:
        lists = jnp.concatenate([lists, exchange(lists, distance)], axis=0)
        distance *= 2
    wide_rows = 4 * (nx + half + 4 * HALO) + 64
    pay_a, pay_b, pay_c, pay_d = call(
        second_pack_kernel,
        [shaped(wide_rows, 256)] * 2 + [shaped(8, 256)] * 2,
        [phi_old, conduct_mid, conduct_coarse, xx_a, xx_b],
        name="second_pack",
    )
    yy_a, yy_b = swap(pay_a, pay_b, "dev")
    yy_c, yy_d = swap_far(pay_c, pay_d)

    (conc_new,) = call(
        sweeps_kernel,
        [shaped(nx, nx, 256)],
        [conc_old, phase_label, y_a, y_b, x_a, x_b],
        [vmem(*ext)] * 4,
        name="sweeps",
    )
    flux_own, pay_a, pay_b = call(
        flux_kernel,
        [shaped(nx, nx, 256), shaped(3 * nx, 256), shaped(3 * nx, 256)],
        [conc_new, phase_label, phi_old, solid_pot, lists],
        [vmem(32, 8, LANES)],
        name="flux",
    )
    f_a, f_b = swap(pay_a, pay_b, "dev")
    concentration, flux, stored = call(
        store_kernel,
        [shaped(nx, nx, 256), shaped(nx, nx, 256), token_shape],
        [conc_new, flux_own],
        [pltpu.SemaphoreType.DMA((8,))],
        out_specs=[FAR, FAR, WHOLE],
        name="store",
    )
    weight, scale, share, start, made = call(
        ready_kernel,
        [shaped(*ext)] * 4 + [token_shape],
        [conc_old, phase_label, phi_old, y_a, y_b, x_a, x_b, yy_a, yy_b, xx_a, xx_b],
        [vmem(*ext)],
        name="ready",
    )
    pay_a, pay_b = call(
        flux_pack_x_kernel, [shaped(15, 8, 256)] * 2, [flux_own, f_a, f_b, stored, made], name="flux_pack_x"
    )
    fx_a, fx_b = swap(pay_a, pay_b, "grp")
    fine_two, fine_source, source_mid, pay_a, pay_b = call(
        potential_kernel,
        [shaped(*ext), shaped(*ext), shaped(half, half, 256), shaped(4 * half, 256), shaped(4 * half, 256)],
        [flux_own, f_a, f_b, fx_a, fx_b, weight, scale, share, start],
        [vmem(*ext), vmem(half, 2, nx, LANES)],
        name="potential",
    )
    m_a, m_b = swap(pay_a, pay_b, "dev")
    wide = (quarter, 32, 256)
    weight_coarse, scale_coarse, rho, load, made = call(
        coarse_ready_kernel,
        [shaped(*wide), shaped(*wide), shaped(quarter, quarter, 256), shaped(8, LANES), token_shape],
        [conduct_coarse, yy_a, yy_b, yy_c, yy_d],
        [vmem(*wide)] * 3,
        name="coarse_ready",
    )
    pay_a, pay_b = call(
        mid_pack_x_kernel, [shaped(3 * HALO, 8, 256)] * 2, [source_mid, m_a, m_b, made], name="mid_pack_x"
    )
    mx_a, mx_b = swap(pay_a, pay_b, "grp")
    mid_two, mid_source, mid_weight, source_coarse, pay_a, pay_b, pay_c, pay_d, sums = call(
        mid_kernel,
        [shaped(*ext_mid)] * 3
        + [shaped(quarter, quarter, 256), shaped(72, 256), shaped(72, 256)]
        + [shaped(8, 256)] * 3,
        [source_mid, conduct_mid, yy_a, yy_b, xx_a, xx_b, m_a, m_b, mx_a, mx_b, rho, load],
        [vmem(*ext_mid), vmem(8, 2, half, LANES), vmem(8, 2, half, LANES)],
        name="middle",
    )
    c_a, c_b = swap(pay_a, pay_b, "dev")
    c_c, c_d = swap_far(pay_c, pay_d)
    (error,) = call(
        coarse_kernel,
        [shaped(8, 16, 256)],
        [source_coarse, c_a, c_b, c_c, c_d, weight_coarse, scale_coarse],
        [vmem(*wide)] * 3,
        name="coarse",
    )
    sums = sums + c_a[64:72]
    distance = 2
    while distance < peers:
        sums = sums + exchange(sums, distance)
        distance *= 2
    error, pay_a, pay_b = call(
        shift_kernel, [shaped(8, 16, 256), shaped(2, 16, 256), shaped(2, 16, 256)], [error, sums], name="shift"
    )
    e_a, e_b = swap(pay_a, pay_b, "grp")
    (potential,) = call(
        finish_kernel,
        [shaped(nx, nx, 256)],
        [error, e_a, e_b, mid_two, mid_source, mid_weight, fine_two, fine_source, weight],
        [vmem(*ext_mid)] * 2
        + [vmem(*ext)] * 2
        + [vmem(12, 2, 2, 16, LANES), vmem(half + 2 * HALO, 3, 2, 16, LANES), vmem(nx, nx, 256)]
        + [pltpu.SemaphoreType.DMA((4,))],
        out_specs=[FAR],
        name="finish",
    )
    return (concentration, flux, potential)


def solution(mesh):
    brick = P("grp", "dev", None)
    return jax.shard_map(
        body,
        mesh=mesh,
        in_specs=(brick, brick, brick, brick, P("grp", "dev"), brick),
        out_specs=(brick, brick, brick),
        check_vma=False,
    )
```

profile of v0, /device:TPU:1, one launch (start us, length us, event | category | flops | bytes accessed | tf_op | source)
XLA Modules:
  0.0 99.7 jit_solution(17151338496330722992)
XLA Ops:
  0.6 1.2 %copy-done = s32[32,32,256]{2,1,0:T(8,128)S(1)} copy-done((s32[32,32,256]{2,1,0:T(8,128)S(1)}, s32[32,32,256]{2,1,0:T(8,128)}, u32[]{:S(2)}) %copy-start) | copy-done | bytes 1048600
  1.9 1.2 %copy-done.2 = f32[32,32,256]{2,1,0:T(8,128)S(1)} copy-done((f32[32,32,256]{2,1,0:T(8,128)S(1)}, f32[32,32,256]{2,1,0:T(8,128)}, u32[]{:S(2)}) %copy-start.2) | copy-done | bytes 1048600
  4.7 2.1 %collective-permute-start = (f32[232,256]{1,0:T(8,128)S(1)}, f32[232,256]{1,0:T(8,128)S(1)}, u32[]{:S(2)}, u32[]{:S(2)}) collective-permute-start(f32[232,256]{1,0:T(8,128)S(1)} %get-tuple-element.52), channel_id=1, source_target_pairs={{0,1},{2,3},{4,5},{6,7},{1,0},{3,2},{5,4},{7,6},{8,9},{10,11},{12,... | collective-permute-start | bytes 712712 | tf_op jit(solution)/shard_map/ppermute | solution.py:660
  7.9 1.0 %collective-permute-start.8 = (f32[24,8,256]{2,1,0:T(8,128)S(1)}, f32[24,8,256]{2,1,0:T(8,128)S(1)}, u32[]{:S(2)}, u32[]{:S(2)}) collective-permute-start(f32[24,8,256]{2,1,0:T(8,128)S(1)} %get-tuple-element.64), channel_id=1, source_target_pairs={{0,8},{16,24},{8,0},{24,16},{1,9},{17,25},{9,1},{25,17},{2,10},{18... | collective-permute-start | bytes 589832 | tf_op jit(solution)/shard_map/ppermute | solution.py:660
  8.9 3.0 %collective-permute-start.9 = (f32[24,8,256]{2,1,0:T(8,128)S(1)}, f32[24,8,256]{2,1,0:T(8,128)S(1)}, u32[]{:S(2)}, u32[]{:S(2)}) collective-permute-start(f32[24,8,256]{2,1,0:T(8,128)S(1)} %get-tuple-element.65), channel_id=1, source_target_pairs={{8,16},{16,8},{9,17},{17,9},{10,18},{18,10},{11,19},{19,11},{12,20... | collective-permute-start | bytes 589832 | tf_op jit(solution)/shard_map/ppermute | solution.py:660
  11.9 4.4 %collective-permute-done.r_a.y_a = f32[232,256]{1,0:T(8,128)S(1)} collective-permute-done((f32[232,256]{1,0:T(8,128)S(1)}, f32[232,256]{1,0:T(8,128)S(1)}, u32[]{:S(2)}, u32[]{:S(2)}) %collective-permute-start) | collective-permute-done | bytes 237600 | tf_op jit(solution)/shard_map/ppermute | solution.py:660
  16.5 1.6 %collective-permute-start.2 = (f32[35,8,256]{2,1,0:T(8,128)S(1)}, f32[35,8,256]{2,1,0:T(8,128)S(1)}, u32[]{:S(2)}, u32[]{:S(2)}) collective-permute-start(f32[35,8,256]{2,1,0:T(8,128)S(1)} %get-tuple-element.55), channel_id=1, source_target_pairs={{0,8},{16,24},{8,0},{24,16},{1,9},{17,25},{9,1},{25,17},{2,10},{18... | collective-permute-start | bytes 860168 | tf_op jit(solution)/shard_map/ppermute | solution.py:660
  18.1 3.2 %collective-permute-start.3 = (f32[35,8,256]{2,1,0:T(8,128)S(1)}, f32[35,8,256]{2,1,0:T(8,128)S(1)}, u32[]{:S(2)}, u32[]{:S(2)}) collective-permute-start(f32[35,8,256]{2,1,0:T(8,128)S(1)} %get-tuple-element.56), channel_id=1, source_target_pairs={{8,16},{16,8},{9,17},{17,9},{10,18},{18,10},{11,19},{19,11},{12,20... | collective-permute-start | bytes 860168 | tf_op jit(solution)/shard_map/ppermute | solution.py:660
  21.3 2.4 %collective-permute-start.4 = (f32[4,256]{1,0:T(4,128)S(1)}, f32[4,256]{1,0:T(4,128)S(1)}, u32[]{:S(2)}, u32[]{:S(2)}) collective-permute-start(f32[4,256]{1,0:T(4,128)S(1)} %pad_maximum_fusion.2), channel_id=1, source_target_pairs={{0,2},{1,3},{2,0},{3,1},{4,6},{5,7},{6,4},{7,5},{8,10},{9,11},{10,... | collective-permute-start | bytes 12296 | tf_op jit(solution)/shard_map/ppermute | solution.py:671
  23.8 1.3 %collective-permute-start.10 = (f32[320,256]{1,0:T(8,128)S(1)}, f32[320,256]{1,0:T(8,128)S(1)}, u32[]{:S(2)}, u32[]{:S(2)}) collective-permute-start(f32[320,256]{1,0:T(8,128)S(1)} %get-tuple-element.66), channel_id=1, source_target_pairs={{0,1},{2,3},{4,5},{6,7},{1,0},{3,2},{5,4},{7,6},{8,9},{10,11},{12,... | collective-permute-start | bytes 983048 | tf_op jit(solution)/shard_map/ppermute | solution.py:660
  25.8 2.5 %collective-permute-start.5 = (f32[8,256]{1,0:T(8,128)S(1)}, f32[8,256]{1,0:T(8,128)S(1)}, u32[]{:S(2)}, u32[]{:S(2)}) collective-permute-start(f32[8,256]{1,0:T(8,128)S(1)} %pad_maximum_fusion.1), channel_id=1, source_target_pairs={{0,4},{1,5},{2,6},{3,7},{4,0},{5,1},{6,2},{7,3},{8,12},{9,13},{10,... | collective-permute-start | bytes 24584 | tf_op jit(solution)/shard_map/ppermute | solution.py:671
  28.2 6.6 %collective-permute-done.5 = f32[8,256]{1,0:T(8,128)S(1)} collective-permute-done((f32[8,256]{1,0:T(8,128)S(1)}, f32[8,256]{1,0:T(8,128)S(1)}, u32[]{:S(2)}, u32[]{:S(2)}) %collective-permute-start.5) | collective-permute-done | bytes 8224 | tf_op jit(solution)/shard_map/ppermute | solution.py:671
  34.9 4.9 %sweeps.1.conc = f32[32,32,256]{2,1,0:T(8,128)S(1)} custom-call(f32[32,32,256]{2,1,0:T(8,128)S(1)} %copy-done.3, s32[32,32,256]{2,1,0:T(8,128)S(1)} %copy-done.1, f32[232,256]{1,0:T(8,128)S(1)} %collective-permute-done.r_a.y_a, f32[232,256]{1,0:T(8,128)S(1)} %collective-permute-done.1.r_b.y_b, f32[35,8,256]{2,1,0:T(8,128)S(1)} %collective-permute-done.2.x_a, ...), custom_call_target="tpu_custom_call" | custom-call | flops 1000000 | bytes 4194304 | tf_op jit(solution)/shard_map/sweeps/pallas_call | solution.py:33
  39.8 1.7 %flux.1 = (f32[32,32,256]{2,1,0:T(8,128)S(1)}, f32[96,256]{1,0:T(8,128)S(1)}, f32[96,256]{1,0:T(8,128)S(1)}) custom-call(f32[32,32,256]{2,1,0:T(8,128)S(1)} %sweeps.1.conc, s32[32,32,256]{2,1,0:T(8,128)S(1)} %copy-done.1, f32[32,32,256]{2,1,0:T(8,128)S(1)} %copy-done.4, f32[32,32,256]{2,1,0:T(8,128)S(1)} %copy-done.5, f32[16,256]{1,0:T(8,128)S(1)} %pad_maximum_fusion.lists), custom_call_target="tpu_custom_call" | custom-call | flops 1000000 | bytes 5455872 | tf_op jit(solution)/shard_map/flux/pallas_call | solution.py:33
  42.3 1.4 %store.1 = (f32[32,32,256]{2,1,0:T(8,128)}, f32[32,32,256]{2,1,0:T(8,128)}, f32[8,128]{1,0:T(8,128)S(1)}) custom-call(f32[32,32,256]{2,1,0:T(8,128)S(1)} %sweeps.1.conc, f32[32,32,256]{2,1,0:T(8,128)S(1)} %get-tuple-element.57.flux), custom_call_target="tpu_custom_call" | custom-call | flops 1000000 | bytes 4198400 | tf_op jit(solution)/shard_map/store/pallas_call | solution.py:33
  43.7 2.2 %ready.1 = (f32[40,40,256]{2,1,0:T(8,128)S(1)}, f32[40,40,256]{2,1,0:T(8,128)S(1)}, f32[40,40,256]{2,1,0:T(8,128)S(1)}, f32[40,40,256]{2,1,0:T(8,128)S(1)}, f32[8,128]{1,0:T(8,128)S(1)}) custom-call(f32[32,32,256]{2,1,0:T(8,128)S(1)} %copy-done.3, s32[32,32,256]{2,1,0:T(8,128)S(1)} %copy-done.1, f32[32,32,256]{2,1,0:T(8,128)S(1)} %copy-done.4, ...), custom_call_target="tpu_custom_call" | custom-call | flops 1000000 | bytes 11800576 | tf_op jit(solution)/shard_map/ready/pallas_call | solution.py:33
  46.0 3.2 %collective-permute-start.13 = (f32[15,8,256]{2,1,0:T(8,128)S(1)}, f32[15,8,256]{2,1,0:T(8,128)S(1)}, u32[]{:S(2)}, u32[]{:S(2)}) collective-permute-start(f32[15,8,256]{2,1,0:T(8,128)S(1)} %get-tuple-element.70), channel_id=1, source_target_pairs={{8,16},{16,8},{9,17},{17,9},{10,18},{18,10},{11,19},{19,11},{12,20... | collective-permute-start | bytes 368648 | tf_op jit(solution)/shard_map/ppermute | solution.py:660
  49.3 3.0 %collective-permute-done.13.x_b = f32[15,8,256]{2,1,0:T(8,128)S(1)} collective-permute-done((f32[15,8,256]{2,1,0:T(8,128)S(1)}, f32[15,8,256]{2,1,0:T(8,128)S(1)}, u32[]{:S(2)}, u32[]{:S(2)}) %collective-permute-start.13) | collective-permute-done | bytes 122912 | tf_op jit(solution)/shard_map/ppermute | solution.py:660
  52.2 2.7 %potential.1 = (f32[40,40,256]{2,1,0:T(8,128)S(1)}, f32[40,40,256]{2,1,0:T(8,128)S(1)}, f32[16,16,256]{2,1,0:T(8,128)S(1)}, f32[64,256]{1,0:T(8,128)S(1)}, f32[64,256]{1,0:T(8,128)S(1)}) custom-call(f32[32,32,256]{2,1,0:T(8,128)S(1)} %get-tuple-element.57.flux, f32[96,256]{1,0:T(8,128)S(1)} %collective-permute-done.6.r_a.y_a, ...), custom_call_target="tpu_custom_call" | custom-call | flops 1000000 | bytes 11714560 | tf_op jit(solution)/shard_map/potential/pallas_call | solution.py:33
  54.9 5.2 %collective-permute-start.14 = (f32[64,256]{1,0:T(8,128)S(1)}, f32[64,256]{1,0:T(8,128)S(1)}, u32[]{:S(2)}, u32[]{:S(2)}) collective-permute-start(f32[64,256]{1,0:T(8,128)S(1)} %get-tuple-element.76), channel_id=1, source_target_pairs={{0,1},{2,3},{4,5},{6,7},{1,0},{3,2},{5,4},{7,6},{8,9},{10,11},{12,... | collective-permute-start | bytes 196616 | tf_op jit(solution)/shard_map/ppermute | solution.py:660
  60.8 4.0 %collective-permute-start.16 = (f32[8,256]{1,0:T(8,128)S(1)}, f32[8,256]{1,0:T(8,128)S(1)}, u32[]{:S(2)}, u32[]{:S(2)}) collective-permute-start(f32[8,256]{1,0:T(8,128)S(1)} %get-tuple-element.78), channel_id=1, source_target_pairs={{0,2},{1,3},{4,6},{5,7},{2,0},{3,1},{6,4},{7,5},{8,10},{9,11},{12,... | collective-permute-start | bytes 24584 | tf_op jit(solution)/shard_map/ppermute | solution.py:667
  66.5 1.2 %coarse_ready.1 = (f32[8,32,256]{2,1,0:T(8,128)S(1)}, f32[8,32,256]{2,1,0:T(8,128)S(1)}, f32[8,8,256]{2,1,0:T(8,128)S(1)}, f32[8,128]{1,0:T(8,128)S(1)}, f32[8,128]{1,0:T(8,128)S(1)}) custom-call(f32[8,8,256]{2,1,0:T(8,128)S(1)} %get-tuple-element.54.token.coarse.own, f32[320,256]{1,0:T(8,128)S(1)} %collective-permute-done.10.yy_a.r_a, ...), custom_call_target="tpu_custom_call" | custom-call | flops 1000000 | bytes 1335296 | tf_op jit(solution)/shard_map/coarse_ready/pallas_call | solution.py:33
  67.8 3.4 %collective-permute-start.19 = (f32[12,8,256]{2,1,0:T(8,128)S(1)}, f32[12,8,256]{2,1,0:T(8,128)S(1)}, u32[]{:S(2)}, u32[]{:S(2)}) collective-permute-start(f32[12,8,256]{2,1,0:T(8,128)S(1)} %get-tuple-element.82), channel_id=1, source_target_pairs={{8,16},{16,8},{9,17},{17,9},{10,18},{18,10},{11,19},{19,11},{12,20... | collective-permute-start | bytes 294920 | tf_op jit(solution)/shard_map/ppermute | solution.py:660
  71.2 2.8 %collective-permute-done.19.x_b = f32[12,8,256]{2,1,0:T(8,128)S(1)} collective-permute-done((f32[12,8,256]{2,1,0:T(8,128)S(1)}, f32[12,8,256]{2,1,0:T(8,128)S(1)}, u32[]{:S(2)}, u32[]{:S(2)}) %collective-permute-start.19) | collective-permute-done | bytes 98336 | tf_op jit(solution)/shard_map/ppermute | solution.py:660
  74.9 2.2 %collective-permute-start.20 = (f32[72,256]{1,0:T(8,128)S(1)}, f32[72,256]{1,0:T(8,128)S(1)}, u32[]{:S(2)}, u32[]{:S(2)}) collective-permute-start(f32[72,256]{1,0:T(8,128)S(1)} %get-tuple-element.86), channel_id=1, source_target_pairs={{0,1},{2,3},{4,5},{6,7},{1,0},{3,2},{5,4},{7,6},{8,9},{10,11},{12,... | collective-permute-start | bytes 221192 | tf_op jit(solution)/shard_map/ppermute | solution.py:660
  77.8 1.1 %collective-permute-done.20.r_a = f32[72,256]{1,0:T(8,128)S(1)} collective-permute-done((f32[72,256]{1,0:T(8,128)S(1)}, f32[72,256]{1,0:T(8,128)S(1)}, u32[]{:S(2)}, u32[]{:S(2)}) %collective-permute-start.20) | collective-permute-done | bytes 73760 | tf_op jit(solution)/shard_map/ppermute | solution.py:660
  78.8 4.2 %collective-permute-start.24 = (f32[8,256]{1,0:T(8,128)S(1)}, f32[8,256]{1,0:T(8,128)S(1)}, u32[]{:S(2)}, u32[]{:S(2)}) collective-permute-start(f32[8,256]{1,0:T(8,128)S(1)} %slice_add_fusion), channel_id=1, source_target_pairs={{0,2},{1,3},{2,0},{3,1},{4,6},{5,7},{6,4},{7,5},{8,10},{9,11},{10,... | collective-permute-start | bytes 24584 | tf_op jit(solution)/shard_map/ppermute | solution.py:671
  84.3 3.3 %collective-permute-start.25 = (f32[8,256]{1,0:T(8,128)S(1)}, f32[8,256]{1,0:T(8,128)S(1)}, u32[]{:S(2)}, u32[]{:S(2)}) collective-permute-start(f32[8,256]{1,0:T(8,128)S(1)} %add.10), channel_id=1, source_target_pairs={{0,4},{1,5},{2,6},{3,7},{4,0},{5,1},{6,2},{7,3},{8,12},{9,13},{10,... | collective-permute-start | bytes 24584 | tf_op jit(solution)/shard_map/ppermute | solution.py:671
  87.7 1.1 %coarse.1.error = f32[8,16,256]{2,1,0:T(8,128)S(1)} custom-call(f32[8,8,256]{2,1,0:T(8,128)S(1)} %get-tuple-element.85.own, f32[72,256]{1,0:T(8,128)S(1)} %collective-permute-done.20.r_a, f32[72,256]{1,0:T(8,128)S(1)} %collective-permute-done.21.r_b, f32[8,256]{1,0:T(8,128)S(1)} %collective-permute-done.22.r_c, f32[8,256]{1,0:T(8,128)S(1)} %collective-permute-done.23.r_d, ...), custom_call_target="tpu_custom_call" | custom-call | flops 1000000 | bytes 884736 | tf_op jit(solution)/shard_map/coarse/pallas_call | solution.py:33
  89.0 5.5 %collective-permute-start.27 = (f32[2,16,256]{2,1,0:T(8,128)S(1)}, f32[2,16,256]{2,1,0:T(8,128)S(1)}, u32[]{:S(2)}, u32[]{:S(2)}) collective-permute-start(f32[2,16,256]{2,1,0:T(8,128)S(1)} %get-tuple-element.95), channel_id=1, source_target_pairs={{8,16},{16,8},{9,17},{17,9},{10,18},{18,10},{11,19},{19,11},{12,20... | collective-permute-start | bytes 98312 | tf_op jit(solution)/shard_map/ppermute | solution.py:660
  94.5 1.6 %collective-permute-done.27.x_b = f32[2,16,256]{2,1,0:T(8,128)S(1)} collective-permute-done((f32[2,16,256]{2,1,0:T(8,128)S(1)}, f32[2,16,256]{2,1,0:T(8,128)S(1)}, u32[]{:S(2)}, u32[]{:S(2)}) %collective-permute-start.27) | collective-permute-done | bytes 32800 | tf_op jit(solution)/shard_map/ppermute | solution.py:660
  96.1 3.6 %finish.1 = f32[32,32,256]{2,1,0:T(8,128)} custom-call(f32[8,16,256]{2,1,0:T(8,128)S(1)} %get-tuple-element.93.error, f32[2,16,256]{2,1,0:T(8,128)S(1)} %collective-permute-done.26.x_a, f32[2,16,256]{2,1,0:T(8,128)S(1)} %collective-permute-done.27.x_b, f32[24,24,256]{2,1,0:T(8,128)S(1)} %get-tuple-element.96.mid_two, ...), custom_call_target="tpu_custom_call" | custom-call | flops 1000000 | bytes 7929856 | tf_op jit(solution)/shard_map/finish/pallas_call | solution.py:33
  (64 shorter events, 9.9 us)
Async XLA Ops:
  4.4 3.1 %copy-start.4 = (f32[32,32,256]{2,1,0:T(8,128)S(1)}, f32[32,32,256]{2,1,0:T(8,128)}, u32[]{:S(2)}) copy-start(f32[32,32,256]{2,1,0:T(8,128)} %phi.7) | copy-start | bytes 3145732
  4.7 11.6 %collective-permute-start = (f32[232,256]{1,0:T(8,128)S(1)}, f32[232,256]{1,0:T(8,128)S(1)}, u32[]{:S(2)}, u32[]{:S(2)}) collective-permute-start(f32[232,256]{1,0:T(8,128)S(1)} %get-tuple-element.52), channel_id=1, source_target_pairs={{0,1},{2,3},{4,5},{6,7},{1,0},{3,2},{5,4},{7,6},{8,9},{10,11},{12,... | collective-permute-start | bytes 712712 | tf_op jit(solution)/shard_map/ppermute | solution.py:660
  6.8 9.5 %collective-permute-start.1 = (f32[232,256]{1,0:T(8,128)S(1)}, f32[232,256]{1,0:T(8,128)S(1)}, u32[]{:S(2)}, u32[]{:S(2)}) collective-permute-start(f32[232,256]{1,0:T(8,128)S(1)} %get-tuple-element.53), channel_id=1, source_target_pairs={{1,2},{3,4},{5,6},{2,1},{4,3},{6,5},{9,10},{11,12},{13,14},{10,9},... | collective-permute-start | bytes 712712 | tf_op jit(solution)/shard_map/ppermute | solution.py:660
  7.9 15.8 %collective-permute-start.8 = (f32[24,8,256]{2,1,0:T(8,128)S(1)}, f32[24,8,256]{2,1,0:T(8,128)S(1)}, u32[]{:S(2)}, u32[]{:S(2)}) collective-permute-start(f32[24,8,256]{2,1,0:T(8,128)S(1)} %get-tuple-element.64), channel_id=1, source_target_pairs={{0,8},{16,24},{8,0},{24,16},{1,9},{17,25},{9,1},{25,17},{2,10},{18... | collective-permute-start | bytes 589832 | tf_op jit(solution)/shard_map/ppermute | solution.py:660
  8.9 14.8 %collective-permute-start.9 = (f32[24,8,256]{2,1,0:T(8,128)S(1)}, f32[24,8,256]{2,1,0:T(8,128)S(1)}, u32[]{:S(2)}, u32[]{:S(2)}) collective-permute-start(f32[24,8,256]{2,1,0:T(8,128)S(1)} %get-tuple-element.65), channel_id=1, source_target_pairs={{8,16},{16,8},{9,17},{17,9},{10,18},{18,10},{11,19},{19,11},{12,20... | collective-permute-start | bytes 589832 | tf_op jit(solution)/shard_map/ppermute | solution.py:660
  16.4 18.5 %copy-start.1 = (s32[32,32,256]{2,1,0:T(8,128)S(1)}, s32[32,32,256]{2,1,0:T(8,128)}, u32[]{:S(2)}) copy-start(s32[32,32,256]{2,1,0:T(8,128)} %label.11) | copy-start | bytes 3145732
  16.4 18.5 %copy-start.3 = (f32[32,32,256]{2,1,0:T(8,128)S(1)}, f32[32,32,256]{2,1,0:T(8,128)}, u32[]{:S(2)}) copy-start(f32[32,32,256]{2,1,0:T(8,128)} %conc.9) | copy-start | bytes 3145732
  16.5 18.4 %collective-permute-start.2 = (f32[35,8,256]{2,1,0:T(8,128)S(1)}, f32[35,8,256]{2,1,0:T(8,128)S(1)}, u32[]{:S(2)}, u32[]{:S(2)}) collective-permute-start(f32[35,8,256]{2,1,0:T(8,128)S(1)} %get-tuple-element.55), channel_id=1, source_target_pairs={{0,8},{16,24},{8,0},{24,16},{1,9},{17,25},{9,1},{25,17},{2,10},{18... | collective-permute-start | bytes 860168 | tf_op jit(solution)/shard_map/ppermute | solution.py:660
  18.1 16.8 %collective-permute-start.3 = (f32[35,8,256]{2,1,0:T(8,128)S(1)}, f32[35,8,256]{2,1,0:T(8,128)S(1)}, u32[]{:S(2)}, u32[]{:S(2)}) collective-permute-start(f32[35,8,256]{2,1,0:T(8,128)S(1)} %get-tuple-element.56), channel_id=1, source_target_pairs={{8,16},{16,8},{9,17},{17,9},{10,18},{18,10},{11,19},{19,11},{12,20... | collective-permute-start | bytes 860168 | tf_op jit(solution)/shard_map/ppermute | solution.py:660
  21.3 4.5 %collective-permute-start.4 = (f32[4,256]{1,0:T(4,128)S(1)}, f32[4,256]{1,0:T(4,128)S(1)}, u32[]{:S(2)}, u32[]{:S(2)}) collective-permute-start(f32[4,256]{1,0:T(4,128)S(1)} %pad_maximum_fusion.2), channel_id=1, source_target_pairs={{0,2},{1,3},{2,0},{3,1},{4,6},{5,7},{6,4},{7,5},{8,10},{9,11},{10,... | collective-permute-start | bytes 12296 | tf_op jit(solution)/shard_map/ppermute | solution.py:671
  23.8 19.9 %collective-permute-start.10 = (f32[320,256]{1,0:T(8,128)S(1)}, f32[320,256]{1,0:T(8,128)S(1)}, u32[]{:S(2)}, u32[]{:S(2)}) collective-permute-start(f32[320,256]{1,0:T(8,128)S(1)} %get-tuple-element.66), channel_id=1, source_target_pairs={{0,1},{2,3},{4,5},{6,7},{1,0},{3,2},{5,4},{7,6},{8,9},{10,11},{12,... | collective-permute-start | bytes 983048 | tf_op jit(solution)/shard_map/ppermute | solution.py:660
  25.1 18.6 %collective-permute-start.11 = (f32[320,256]{1,0:T(8,128)S(1)}, f32[320,256]{1,0:T(8,128)S(1)}, u32[]{:S(2)}, u32[]{:S(2)}) collective-permute-start(f32[320,256]{1,0:T(8,128)S(1)} %get-tuple-element.67), channel_id=1, source_target_pairs={{1,2},{3,4},{5,6},{2,1},{4,3},{6,5},{9,10},{11,12},{13,14},{10,9},... | collective-permute-start | bytes 983048 | tf_op jit(solution)/shard_map/ppermute | solution.py:660
  25.8 9.0 %collective-permute-start.5 = (f32[8,256]{1,0:T(8,128)S(1)}, f32[8,256]{1,0:T(8,128)S(1)}, u32[]{:S(2)}, u32[]{:S(2)}) collective-permute-start(f32[8,256]{1,0:T(8,128)S(1)} %pad_maximum_fusion.1), channel_id=1, source_target_pairs={{0,4},{1,5},{2,6},{3,7},{4,0},{5,1},{6,2},{7,3},{8,12},{9,13},{10,... | collective-permute-start | bytes 24584 | tf_op jit(solution)/shard_map/ppermute | solution.py:671
  34.8 4.9 %copy-start.5 = (f32[32,32,256]{2,1,0:T(8,128)S(1)}, f32[32,32,256]{2,1,0:T(8,128)}, u32[]{:S(2)}) copy-start(f32[32,32,256]{2,1,0:T(8,128)} %solid.1) | copy-start | bytes 3145732
  41.5 4.4 %collective-permute-start.6 = (f32[96,256]{1,0:T(8,128)S(1)}, f32[96,256]{1,0:T(8,128)S(1)}, u32[]{:S(2)}, u32[]{:S(2)}) collective-permute-start(f32[96,256]{1,0:T(8,128)S(1)} %get-tuple-element.60), channel_id=1, source_target_pairs={{0,1},{2,3},{4,5},{6,7},{1,0},{3,2},{5,4},{7,6},{8,9},{10,11},{12,... | collective-permute-start | bytes 294920 | tf_op jit(solution)/shard_map/ppermute | solution.py:660
  41.6 4.3 %collective-permute-start.7 = (f32[96,256]{1,0:T(8,128)S(1)}, f32[96,256]{1,0:T(8,128)S(1)}, u32[]{:S(2)}, u32[]{:S(2)}) collective-permute-start(f32[96,256]{1,0:T(8,128)S(1)} %get-tuple-element.61), channel_id=1, source_target_pairs={{1,2},{3,4},{5,6},{2,1},{4,3},{6,5},{9,10},{11,12},{13,14},{10,9},... | collective-permute-start | bytes 294920 | tf_op jit(solution)/shard_map/ppermute | solution.py:660
  45.9 3.3 %collective-permute-start.12 = (f32[15,8,256]{2,1,0:T(8,128)S(1)}, f32[15,8,256]{2,1,0:T(8,128)S(1)}, u32[]{:S(2)}, u32[]{:S(2)}) collective-permute-start(f32[15,8,256]{2,1,0:T(8,128)S(1)} %get-tuple-element.69), channel_id=1, source_target_pairs={{0,8},{16,24},{8,0},{24,16},{1,9},{17,25},{9,1},{25,17},{2,10},{18... | collective-permute-start | bytes 368648 | tf_op jit(solution)/shard_map/ppermute | solution.py:660
  46.0 6.2 %collective-permute-start.13 = (f32[15,8,256]{2,1,0:T(8,128)S(1)}, f32[15,8,256]{2,1,0:T(8,128)S(1)}, u32[]{:S(2)}, u32[]{:S(2)}) collective-permute-start(f32[15,8,256]{2,1,0:T(8,128)S(1)} %get-tuple-element.70), channel_id=1, source_target_pairs={{8,16},{16,8},{9,17},{17,9},{10,18},{18,10},{11,19},{19,11},{12,20... | collective-permute-start | bytes 368648 | tf_op jit(solution)/shard_map/ppermute | solution.py:660
  54.9 12.7 %collective-permute-start.14 = (f32[64,256]{1,0:T(8,128)S(1)}, f32[64,256]{1,0:T(8,128)S(1)}, u32[]{:S(2)}, u32[]{:S(2)}) collective-permute-start(f32[64,256]{1,0:T(8,128)S(1)} %get-tuple-element.76), channel_id=1, source_target_pairs={{0,1},{2,3},{4,5},{6,7},{1,0},{3,2},{5,4},{7,6},{8,9},{10,11},{12,... | collective-permute-start | bytes 196616 | tf_op jit(solution)/shard_map/ppermute | solution.py:660
  60.1 7.5 %collective-permute-start.15 = (f32[64,256]{1,0:T(8,128)S(1)}, f32[64,256]{1,0:T(8,128)S(1)}, u32[]{:S(2)}, u32[]{:S(2)}) collective-permute-start(f32[64,256]{1,0:T(8,128)S(1)} %get-tuple-element.77), channel_id=1, source_target_pairs={{1,2},{3,4},{5,6},{2,1},{4,3},{6,5},{9,10},{11,12},{13,14},{10,9},... | collective-permute-start | bytes 196616 | tf_op jit(solution)/shard_map/ppermute | solution.py:660
  60.8 5.7 %collective-permute-start.16 = (f32[8,256]{1,0:T(8,128)S(1)}, f32[8,256]{1,0:T(8,128)S(1)}, u32[]{:S(2)}, u32[]{:S(2)}) collective-permute-start(f32[8,256]{1,0:T(8,128)S(1)} %get-tuple-element.78), channel_id=1, source_target_pairs={{0,2},{1,3},{4,6},{5,7},{2,0},{3,1},{6,4},{7,5},{8,10},{9,11},{12,... | collective-permute-start | bytes 24584 | tf_op jit(solution)/shard_map/ppermute | solution.py:667
  64.8 1.7 %collective-permute-start.17 = (f32[8,256]{1,0:T(8,128)S(1)}, f32[8,256]{1,0:T(8,128)S(1)}, u32[]{:S(2)}, u32[]{:S(2)}) collective-permute-start(f32[8,256]{1,0:T(8,128)S(1)} %get-tuple-element.79), channel_id=1, source_target_pairs={{2,4},{3,5},{4,2},{5,3},{10,12},{11,13},{12,10},{13,11},{18,20},{1... | collective-permute-start | bytes 24584 | tf_op jit(solution)/shard_map/ppermute | solution.py:667
  67.7 3.5 %collective-permute-start.18 = (f32[12,8,256]{2,1,0:T(8,128)S(1)}, f32[12,8,256]{2,1,0:T(8,128)S(1)}, u32[]{:S(2)}, u32[]{:S(2)}) collective-permute-start(f32[12,8,256]{2,1,0:T(8,128)S(1)} %get-tuple-element.81), channel_id=1, source_target_pairs={{0,8},{16,24},{8,0},{24,16},{1,9},{17,25},{9,1},{25,17},{2,10},{18... | collective-permute-start | bytes 294920 | tf_op jit(solution)/shard_map/ppermute | solution.py:660
  67.8 6.2 %collective-permute-start.19 = (f32[12,8,256]{2,1,0:T(8,128)S(1)}, f32[12,8,256]{2,1,0:T(8,128)S(1)}, u32[]{:S(2)}, u32[]{:S(2)}) collective-permute-start(f32[12,8,256]{2,1,0:T(8,128)S(1)} %get-tuple-element.82), channel_id=1, source_target_pairs={{8,16},{16,8},{9,17},{17,9},{10,18},{18,10},{11,19},{19,11},{12,20... | collective-permute-start | bytes 294920 | tf_op jit(solution)/shard_map/ppermute | solution.py:660
  74.9 4.0 %collective-permute-start.20 = (f32[72,256]{1,0:T(8,128)S(1)}, f32[72,256]{1,0:T(8,128)S(1)}, u32[]{:S(2)}, u32[]{:S(2)}) collective-permute-start(f32[72,256]{1,0:T(8,128)S(1)} %get-tuple-element.86), channel_id=1, source_target_pairs={{0,1},{2,3},{4,5},{6,7},{1,0},{3,2},{5,4},{7,6},{8,9},{10,11},{12,... | collective-permute-start | bytes 221192 | tf_op jit(solution)/shard_map/ppermute | solution.py:660
  77.1 10.6 %collective-permute-start.21 = (f32[72,256]{1,0:T(8,128)S(1)}, f32[72,256]{1,0:T(8,128)S(1)}, u32[]{:S(2)}, u32[]{:S(2)}) collective-permute-start(f32[72,256]{1,0:T(8,128)S(1)} %get-tuple-element.87), channel_id=1, source_target_pairs={{1,2},{3,4},{5,6},{2,1},{4,3},{6,5},{9,10},{11,12},{13,14},{10,9},... | collective-permute-start | bytes 221192 | tf_op jit(solution)/shard_map/ppermute | solution.py:660
  78.8 5.5 %collective-permute-start.24 = (f32[8,256]{1,0:T(8,128)S(1)}, f32[8,256]{1,0:T(8,128)S(1)}, u32[]{:S(2)}, u32[]{:S(2)}) collective-permute-start(f32[8,256]{1,0:T(8,128)S(1)} %slice_add_fusion), channel_id=1, source_target_pairs={{0,2},{1,3},{2,0},{3,1},{4,6},{5,7},{6,4},{7,5},{8,10},{9,11},{10,... | collective-permute-start | bytes 24584 | tf_op jit(solution)/shard_map/ppermute | solution.py:671
  83.0 4.6 %collective-permute-start.22 = (f32[8,256]{1,0:T(8,128)S(1)}, f32[8,256]{1,0:T(8,128)S(1)}, u32[]{:S(2)}, u32[]{:S(2)}) collective-permute-start(f32[8,256]{1,0:T(8,128)S(1)} %get-tuple-element.88), channel_id=1, source_target_pairs={{0,2},{1,3},{4,6},{5,7},{2,0},{3,1},{6,4},{7,5},{8,10},{9,11},{12,... | collective-permute-start | bytes 24584 | tf_op jit(solution)/shard_map/ppermute | solution.py:667
  83.1 4.6 %collective-permute-start.23 = (f32[8,256]{1,0:T(8,128)S(1)}, f32[8,256]{1,0:T(8,128)S(1)}, u32[]{:S(2)}, u32[]{:S(2)}) collective-permute-start(f32[8,256]{1,0:T(8,128)S(1)} %get-tuple-element.89), channel_id=1, source_target_pairs={{2,4},{3,5},{4,2},{5,3},{10,12},{11,13},{12,10},{13,11},{18,20},{1... | collective-permute-start | bytes 24584 | tf_op jit(solution)/shard_map/ppermute | solution.py:667
  84.3 4.5 %collective-permute-start.25 = (f32[8,256]{1,0:T(8,128)S(1)}, f32[8,256]{1,0:T(8,128)S(1)}, u32[]{:S(2)}, u32[]{:S(2)}) collective-permute-start(f32[8,256]{1,0:T(8,128)S(1)} %add.10), channel_id=1, source_target_pairs={{0,4},{1,5},{2,6},{3,7},{4,0},{5,1},{6,2},{7,3},{8,12},{9,13},{10,... | collective-permute-start | bytes 24584 | tf_op jit(solution)/shard_map/ppermute | solution.py:671
  89.0 5.5 %collective-permute-start.26 = (f32[2,16,256]{2,1,0:T(8,128)S(1)}, f32[2,16,256]{2,1,0:T(8,128)S(1)}, u32[]{:S(2)}, u32[]{:S(2)}) collective-permute-start(f32[2,16,256]{2,1,0:T(8,128)S(1)} %get-tuple-element.94), channel_id=1, source_target_pairs={{0,8},{16,24},{8,0},{24,16},{1,9},{17,25},{9,1},{25,17},{2,10},{18... | collective-permute-start | bytes 98312 | tf_op jit(solution)/shard_map/ppermute | solution.py:660
  89.0 7.0 %collective-permute-start.27 = (f32[2,16,256]{2,1,0:T(8,128)S(1)}, f32[2,16,256]{2,1,0:T(8,128)S(1)}, u32[]{:S(2)}, u32[]{:S(2)}) collective-permute-start(f32[2,16,256]{2,1,0:T(8,128)S(1)} %get-tuple-element.95), channel_id=1, source_target_pairs={{8,16},{16,8},{9,17},{17,9},{10,18},{18,10},{11,19},{19,11},{12,20... | collective-permute-start | bytes 98312 | tf_op jit(solution)/shard_map/ppermute | solution.py:660
  (4 other events, 3.8 us)
where the time goes:
time: 101 us; the launch traced here: 99.7 us
  starting transfers between devices  53.1 us (53%)
  waiting for transfers between devices  21.1 us (21%)
  Pallas kernels  20.7 us (20%)
  local copies, waits for them, and re-layouts  3.82 us (4%)
  between operations  1.06 us (1%)
    ppermute x10, starting transfers between devices, swap(): lax.ppermute(pay_b, axis, both_ways(pairs_b))  21.6 us
    pallas_call x16, Pallas kernels, call(): pl.pallas_call(kernel, out_shape=tuple(outs), in_specs=in_specs or [WHOLE...  20.7 us
    ppermute x10, starting transfers between devices, swap(): lax.ppermute(pay_a, axis, both_ways(pairs_a))  13.7 us
    ppermute x4, starting transfers between devices, exchange(): lax.ppermute(value, 'dev', [(i, i ^ distance) for i in range(lax.axis_siz...  12.4 us
    ppermute x10, waiting for transfers between devices, swap(): lax.ppermute(pay_b, axis, both_ways(pairs_b))  7.36 us
    ppermute x4, waiting for transfers between devices, exchange(): lax.ppermute(value, 'dev', [(i, i ^ distance) for i in range(lax.axis_siz...  7.17 us
    ppermute x10, waiting for transfers between devices, swap(): lax.ppermute(pay_a, axis, both_ways(pairs_a))  5.54 us
    ppermute x2, starting transfers between devices, swap_far(): lax.ppermute(pay_c, 'dev', both_ways(pairs_c))  4.05 us
  transfers between devices with their start and end apart: 28, of which 8 were waited for; matrix products, arithmetic and copies ran while one was open for 0% of the time, Pallas kernels for 13%

commit v1 on v0

--- a/solution.py
+++ b/solution.py
@@ -18,6 +18,7 @@
 HALO = 4
 LANES = 128
 VMEM_LIMIT = 28 * 1024 * 1024
+VMEM_MOST = 58 * 1024 * 1024
 
 
 def shaped(*shape):
@@ -28,7 +29,7 @@
 FAR = pl.BlockSpec(memory_space=pltpu.HBM)
 
 
-def call(kernel, outs, args, scratch=(), in_specs=None, out_specs=None, flops=10**6, name=None):
+def call(kernel, outs, args, scratch=(), in_specs=None, out_specs=None, limit=VMEM_LIMIT, flops=10**6, name=None):
     size = sum(4 * a.size for a in args) + sum(4 * o.size for o in outs)
     return pl.pallas_call(
         kernel,
@@ -36,7 +37,7 @@
         in_specs=in_specs or [WHOLE] * len(args),
         out_specs=tuple(out_specs or [WHOLE] * len(outs)),
         scratch_shapes=list(scratch),
-        compiler_params=pltpu.CompilerParams(vmem_limit_bytes=VMEM_LIMIT),
+        compiler_params=pltpu.CompilerParams(vmem_limit_bytes=limit),
         cost_estimate=pl.CostEstimate(flops=flops, bytes_accessed=size, transcendentals=0),
         name=name,
     )(*args)
@@ -146,17 +147,21 @@
     return jnp.concatenate(parts + [before], axis=0)
 
 
-def first_pack_kernel(conc, label, owner, block, pay_a, pay_b, c_first, c_last, l_first, l_last, sems):
+def first_pack_kernel(
+    conc, label, owner, block, pay_a, pay_b, own_lists, c_first, c_last, l_first, l_last, own_owner, own_block, sems
+):
     nx = conc.shape[0]
-    copies = []
+    copies = [pltpu.make_async_copy(owner, own_owner, sems.at[4]), pltpu.make_async_copy(block, own_block, sems.at[5])]
     for i, (ref, at, to) in enumerate(((conc, 0, c_first), (conc, 24, c_last), (label, 0, l_first), (label, 24, l_last))):
         copies.append(pltpu.make_async_copy(ref.at[:, pl.ds(at, 8), :], to, sems.at[i]))
-        copies[-1].start()
-    named = jnp.concatenate([owner[...], block[...], jnp.zeros((6, 256), jnp.int32)], axis=0).astype(F32)
+    for c in copies:
+        c.start()
+    for c in copies:
+        c.wait()
+    named = jnp.concatenate([own_owner[...], own_block[...], jnp.zeros((6, 256), jnp.int32)], axis=0).astype(F32)
+    own_lists[...] = named
     pay_a[7 * nx : 7 * nx + 8, :] = named
     pay_b[7 * nx : 7 * nx + 8, :] = named
-    for c in copies:
-        c.wait()
     for x in range(nx):
         send_y(pay_a, pay_b, 7 * x, c_first[x, 0:4, :], c_last[x, 4:8, :])
         send_y(pay_a, pay_b, 7 * x + 4, l_first[x, 0:3, :].astype(F32), l_last[x, 5:8, :].astype(F32))
@@ -197,7 +202,7 @@
             send_x(pay_a, pay_b, 20 + 5 * k + t, plane(label, k, t, 4, 3), plane(label, nx - 3 + k, t, 4, 3))
 
 
-def second_pack_kernel(phi, mid, coarse, x_a, x_b, pay_a, pay_b, pay_c, pay_d):
+def second_pack_kernel(phi, mid, coarse, x_a, x_b, token, pay_a, pay_b):
     nx = phi.shape[0]
     half = nx // 2
     for x in range(nx):
@@ -223,27 +228,11 @@
     for x in range(8):
         pay_a[base + 8 * x : base + 8 * x + 8, :] = coarse[x]
         pay_b[base + 8 * x : base + 8 * x + 8, :] = coarse[x]
-    far_edges(coarse, pay_c, pay_d)
-
-
-def far_edges(field, pay_c, pay_d):
-    flag = low_pair()
-    for x in range(8):
-        first, last = field[x, 0:1, :], field[x, 7:8, :]
-        pay_c[x : x + 1, :] = either(flag, last, first)
-        pay_d[x : x + 1, :] = either(flag, first, last)
-
-
-def low_pair():
-    return lax.rem(lax.axis_index("dev"), 4) < 2
-
-
-def wide_plane(own, r_a, r_b, r_c, r_d, base, x):
-    flag = low_pair()
-    c, d = r_c[x : x + 1, :], r_d[x : x + 1, :]
-    after, before = y_sides(r_a, r_b, base + 8 * x, 8)
+
+
+def wide_rows(own, after_own, before_own, after, before):
     gap = jnp.zeros((6, 256), F32)
-    return jnp.concatenate([own[x], after, either(flag, c, d), gap, either(flag, d, c), before], axis=0)
+    return jnp.concatenate([own, after_own, after, gap, before, before_own], axis=0)
 
 
 def sweeps_kernel(conc, label, y_a, y_b, x_a, x_b, out, one, two, gain, base):
@@ -294,7 +283,9 @@
     loop(0, nx, last)
 
 
-def flux_kernel(conc, label, phi, solid, lists, flux, pay_a, pay_b, marked):
+def flux_kernel(conc, label, phi, solid, *rest):
+    lists_refs, (flux, pay_a, pay_b, marked) = rest[:-4], rest[-4:]
+    lists = jnp.concatenate([r[...] for r in lists_refs], axis=0)
     nx = conc.shape[0]
     entries = lists.shape[0] // 2 * 256
     owner = jnp.concatenate([lists[2 * i : 2 * i + 1, :] for i in range(entries // 256)], axis=1)
@@ -452,16 +443,17 @@
 
 def mid_kernel(
     source_own, conduct_own, yy_a, yy_b, xx_a, xx_b, y_a, y_b, x_a, x_b, rho, load,
-    after_two, source, weight, coarse, pay_a, pay_b, pay_c, pay_d, part, scale, pairs, pairs_2,
+    after_two, source, weight, coarse, conduct, pay_a, pay_b, part, scale, mid_conduct, pairs, pairs_2,
 ):
     n = source_own.shape[0]
     base = 4 * (2 * n + 2 * HALO)
 
-    def put(x, rows, b, conduct):
-        factor = OMEGA / (MASS + 3.0 * conduct)
-        weight[x, rows, :] = conduct * factor
+    def put(x, rows, b, k):
+        factor = OMEGA / (MASS + 3.0 * k)
+        weight[x, rows, :] = k * factor
         scale[x, rows, :] = factor
         source[x, rows, :] = factor * b
+        mid_conduct[x, rows, :] = k
 
     def far(x):
         return halo_tile(*y_sides(yy_a, yy_b, base + 4 * x, 4))
@@ -492,45 +484,35 @@
 
     def remainder(x):
         v, near = around(after_two, x)
-        return ((source[x] - OMEGA * v) + near)[0:16, :] / scale[x, 0:16, :]
+        return ((source[x] - OMEGA * v) + near) / scale[x]
 
     total = jnp.zeros((8, 256), F32)
     for i in range(n // 2):
         x = HALO + 2 * i
         value = 0.25 * pair_rows(remainder(x) + remainder(x + 1), pairs.at[i])
+        k = 0.25 * pair_rows(mid_conduct[x] + mid_conduct[x + 1], pairs_2.at[i])
         coarse[i] = value
-        pay_a[8 * i : 8 * i + 8, :] = value
-        pay_b[8 * i : 8 * i + 8, :] = value
-        total += rho[i] * value
+        conduct[i] = k
+        send_y(pay_a, pay_b, 9 * i, value[1:9], jnp.concatenate([value[11:12], value[0:7]], axis=0))
+        send_y(pay_a, pay_b, 9 * i + 8, k[8:9], k[11:12])
+        total += rho[i] * value[0:8]
     sums = jnp.concatenate([total[:, :LANES] + total[:, LANES:], load[...]], axis=1)
-    pay_a[64:72, :] = sums
-    pay_b[64:72, :] = sums
+    pay_a[72:80, :] = sums
+    pay_b[72:80, :] = sums
     part[...] = sums
-    far_edges(coarse, pay_c, pay_d)
 
 
 COARSE_W = 0.0625
 
 
-def coarse_sum(values, x):
-    v = values[x]
-    inner = along_y(v)
-    if x > 0:
-        inner = inner + values[x - 1]
-    if x < len(values) - 1:
-        inner = inner + values[x + 1]
-    return COARSE_W * inner + along_z(v)
-
-
-def coarse_ready_kernel(own, r_a, r_b, r_c, r_d, weight, scale, rho, load, token, one, two, conduct):
+def coarse_ready_kernel(own, r_a, r_b, rho, load, token, one, two, conduct, scale):
     token[...] = jnp.zeros(token.shape, F32)
     base = r_a.shape[0] - 64
     for x in range(8):
-        k = wide_plane(own, r_a, r_b, r_c, r_d, base, x)
-        factor = OMEGA / (MASS + 2.25 * k)
+        after, before = y_sides(r_a, r_b, base + 8 * x, 8)
+        k = jnp.concatenate([own[x], after, jnp.zeros((8, 256), F32), before], axis=0)
         conduct[x] = k
-        weight[x] = k * factor
-        scale[x] = factor
+        scale[x] = OMEGA / (MASS + 2.25 * k)
         one[x] = jnp.ones(k.shape, F32)
     fields = (one, two)
     for s in range(COARSE_SWEEPS):
@@ -554,13 +536,22 @@
     load[...] = total[:, :LANES] + total[:, LANES:]
 
 
-def coarse_kernel(own, r_a, r_b, r_c, r_d, weight, scale, error, source, one, two):
+def coarse_kernel(own, conduct, far_a, far_b, r_a, r_b, error, source, weight, one, two):
+    base = far_a.shape[0] - 64
     for x in range(8):
-        source[x] = scale[x] * wide_plane(own, r_a, r_b, r_c, r_d, 0, x)
+        after, before = y_sides(r_a, r_b, 9 * x, 8)
+        b = wide_rows(own[x, 0:8, :], own[x, 8:9, :], own[x, 11:12, :], after, before)
+        last_after, last_before = y_sides(r_a, r_b, 9 * x + 8, 1)
+        after, before = y_sides(far_a, far_b, base + 8 * x, 8)
+        after = jnp.concatenate([after[1:8], last_after], axis=0)
+        before = jnp.concatenate([last_before, before[0:7]], axis=0)
+        k = wide_rows(conduct[x, 0:8, :], conduct[x, 8:9, :], conduct[x, 11:12, :], after, before)
+        factor = OMEGA / (MASS + 2.25 * k)
+        weight[x] = k * factor
+        source[x] = factor * b
     old = source
     for s in range(1, COARSE_SWEEPS):
         new = one if s % 2 else two
-        planes = [old.at[x] for x in range(8)]
         for x in range(8):
             v = old[x]
             inner = along_y(v)
@@ -657,14 +648,8 @@
     size = lax.axis_size(axis)
     pairs_a = [(i, i + 1) for i in range(0, size - 1, 2)]
     pairs_b = [(i, i + 1) for i in range(1, size - 1, 2)]
-    return lax.ppermute(pay_a, axis, both_ways(pairs_a)), lax.ppermute(pay_b, axis, both_ways(pairs_b))
-
-
-def swap_far(pay_c, pay_d):
-    size = lax.axis_size("dev")
-    pairs_c = [(i, i + 2) for i in range(size - 2) if i % 4 < 2]
-    pairs_d = [(i, i + 2) for i in range(size - 2) if i % 4 >= 2]
-    return lax.ppermute(pay_c, "dev", both_ways(pairs_c)), lax.ppermute(pay_d, "dev", both_ways(pairs_d))
+    from_b = lax.ppermute(pay_b, axis, both_ways(pairs_b))
+    return lax.ppermute(pay_a, axis, both_ways(pairs_a)), from_b
 
 
 def exchange(value, distance):
@@ -680,15 +665,18 @@
     ext_mid = (half + 2 * HALO, half + 2 * HALO, 256)
     token_shape = shaped(8, LANES)
 
-    pay_a, pay_b = call(
+    pay_a, pay_b, own_lists = call(
         first_pack_kernel,
-        [shaped(7 * nx + 8, 256)] * 2,
+        [shaped(7 * nx + 8, 256)] * 2 + [shaped(8, 256)],
         [conc_old, phase_label, iface_owner.reshape(1, -1), iface_block],
-        [vmem(nx, 8, 256)] * 2 + [pltpu.VMEM((nx, 8, 256), jnp.int32)] * 2 + [pltpu.SemaphoreType.DMA((4,))],
-        in_specs=[FAR, FAR, WHOLE, WHOLE],
+        [vmem(nx, 8, 256)] * 2
+        + [pltpu.VMEM((nx, 8, 256), jnp.int32)] * 2
+        + [pltpu.VMEM((1, 256), jnp.int32)] * 2
+        + [pltpu.SemaphoreType.DMA((6,))],
+        in_specs=[FAR] * 4,
+        limit=VMEM_MOST,
         name="first_pack",
     )
-    own_lists = pay_a[7 * nx : 7 * nx + 2]
     y_a, y_b = swap(pay_a, pay_b, "dev")
     conduct_mid, conduct_coarse, pay_a, pay_b = call(
         own_kernel,
@@ -705,20 +693,22 @@
         name="first_pack_x",
     )
     x_a, x_b = swap(pay_a, pay_b, "grp")
-    lists = jnp.concatenate([own_lists, y_a[7 * nx : 7 * nx + 2]], axis=0)
+    lists = jnp.concatenate([own_lists[0:2], y_a[7 * nx : 7 * nx + 2]], axis=0)
+    pieces = [lists]
     distance = 2
     while distance < peers:
-        lists = jnp.concatenate([lists, exchange(lists, distance)], axis=0)
+        if distance > 2:
+            lists = jnp.concatenate(pieces, axis=0)
+        pieces.append(exchange(lists, distance))
         distance *= 2
-    wide_rows = 4 * (nx + half + 4 * HALO) + 64
-    pay_a, pay_b, pay_c, pay_d = call(
+    far_rows = 4 * (nx + half + 4 * HALO) + 64
+    pay_a, pay_b = call(
         second_pack_kernel,
-        [shaped(wide_rows, 256)] * 2 + [shaped(8, 256)] * 2,
-        [phi_old, conduct_mid, conduct_coarse, xx_a, xx_b],
+        [shaped(far_rows, 256)] * 2,
+        [phi_old, conduct_mid, conduct_coarse, xx_a, xx_b, lists],
         name="second_pack",
     )
     yy_a, yy_b = swap(pay_a, pay_b, "dev")
-    yy_c, yy_d = swap_far(pay_c, pay_d)
 
     (conc_new,) = call(
         sweeps_kernel,
@@ -730,7 +720,7 @@
     flux_own, pay_a, pay_b = call(
         flux_kernel,
         [shaped(nx, nx, 256), shaped(3 * nx, 256), shaped(3 * nx, 256)],
-        [conc_new, phase_label, phi_old, solid_pot, lists],
+        [conc_new, phase_label, phi_old, solid_pot] + pieces,
         [vmem(32, 8, LANES)],
         name="flux",
     )
@@ -763,36 +753,34 @@
     )
     m_a, m_b = swap(pay_a, pay_b, "dev")
     wide = (quarter, 32, 256)
-    weight_coarse, scale_coarse, rho, load, made = call(
+    rho, load, made = call(
         coarse_ready_kernel,
-        [shaped(*wide), shaped(*wide), shaped(quarter, quarter, 256), shaped(8, LANES), token_shape],
-        [conduct_coarse, yy_a, yy_b, yy_c, yy_d],
-        [vmem(*wide)] * 3,
+        [shaped(quarter, quarter, 256), shaped(8, LANES), token_shape],
+        [conduct_coarse, yy_a, yy_b],
+        [vmem(*wide)] * 4,
         name="coarse_ready",
     )
     pay_a, pay_b = call(
         mid_pack_x_kernel, [shaped(3 * HALO, 8, 256)] * 2, [source_mid, m_a, m_b, made], name="mid_pack_x"
     )
     mx_a, mx_b = swap(pay_a, pay_b, "grp")
-    mid_two, mid_source, mid_weight, source_coarse, pay_a, pay_b, pay_c, pay_d, sums = call(
+    mid_two, mid_source, mid_weight, source_coarse, wide_coarse, pay_a, pay_b, sums = call(
         mid_kernel,
         [shaped(*ext_mid)] * 3
-        + [shaped(quarter, quarter, 256), shaped(72, 256), shaped(72, 256)]
-        + [shaped(8, 256)] * 3,
+        + [shaped(quarter, 12, 256), shaped(quarter, 12, 256), shaped(80, 256), shaped(80, 256), shaped(8, 256)],
         [source_mid, conduct_mid, yy_a, yy_b, xx_a, xx_b, m_a, m_b, mx_a, mx_b, rho, load],
-        [vmem(*ext_mid), vmem(8, 2, half, LANES), vmem(8, 2, half, LANES)],
+        [vmem(*ext_mid)] * 2 + [vmem(8, 2, half + 2 * HALO, LANES)] * 2,
         name="middle",
     )
     c_a, c_b = swap(pay_a, pay_b, "dev")
-    c_c, c_d = swap_far(pay_c, pay_d)
     (error,) = call(
         coarse_kernel,
         [shaped(8, 16, 256)],
-        [source_coarse, c_a, c_b, c_c, c_d, weight_coarse, scale_coarse],
-        [vmem(*wide)] * 3,
+        [source_coarse, wide_coarse, yy_a, yy_b, c_a, c_b],
+        [vmem(*wide)] * 4,
         name="coarse",
     )
-    sums = sums + c_a[64:72]
+    sums = sums + c_a[72:80]
     distance = 2
     while distance < peers:
         sums = sums + exchange(sums, distance)

time: 101 us -> 90.8 us (0.90)
  starting transfers between devices: 53.1 us -> 47.8 us
  waiting for transfers between devices: 21.1 us -> 16.6 us
  Pallas kernels: 20.7 us -> 23 us
  local copies, waits for them, and re-layouts: 3.82 us -> 1.94 us
    ppermute x4, waiting for transfers between devices: 7.17 us -> 2.96 us  [exchange(): lax.ppermute(value, 'dev', [(i, i ^ distance) for i in range(lax.axis_siz...]
    ppermute x4, starting transfers between devices: 12.4 us -> 8.95 us  [exchange(): lax.ppermute(value, 'dev', [(i, i ^ distance) for i in range(lax.axis_siz...]
    unnamed x16 -> x10, local copies, waits for them, and re-layouts: 3.82 us -> 1.24 us
    pallas_call x16, Pallas kernels: 20.7 us -> 23 us  [call(): pl.pallas_call(kernel, out_shape=tuple(outs), in_specs=in_specs or [WHOLE...]
    ppermute x24 -> x20, starting transfers between devices: 40.7 us -> 38.8 us  [the longest x10 20.1 us: swap(): from_b = lax.ppermute(pay_b, axis, both_ways(pairs_b))]
    ppermute x24 -> x20, waiting for transfers between devices: 13.9 us -> 13.6 us  [the longest x10 9.62 us: swap(): from_b = lax.ppermute(pay_b, axis, both_ways(pairs_b))]
  transfers between devices with their start and end apart: 28 -> 24, of which waited for: 8 -> 8; matrix products, arithmetic and copies ran while one was open for 0% -> 1% of each run, Pallas kernels for 13% -> 14%
where the time goes in v1:
time: 90.8 us; the launch traced here: 90.3 us
  starting transfers between devices  47.8 us (53%)
  Pallas kernels  23 us (25%)
  waiting for transfers between devices  16.6 us (18%)
  local copies, waits for them, and re-layouts  1.94 us (2%)
  between operations  1.02 us (1%)
    pallas_call x16, Pallas kernels, call(): pl.pallas_call(kernel, out_shape=tuple(outs), in_specs=in_specs or [WHOLE...  23 us
    ppermute x10, starting transfers between devices, swap(): from_b = lax.ppermute(pay_b, axis, both_ways(pairs_b))  20.1 us
    ppermute x10, starting transfers between devices, swap(): return (lax.ppermute(pay_a, axis, both_ways(pairs_a)), from_b)  18.7 us
    ppermute x10, waiting for transfers between devices, swap(): from_b = lax.ppermute(pay_b, axis, both_ways(pairs_b))  9.62 us
    ppermute x4, starting transfers between devices, exchange(): lax.ppermute(value, 'dev', [(i, i ^ distance) for i in range(lax.axis_siz...  8.95 us
    ppermute x10, waiting for transfers between devices, swap(): return (lax.ppermute(pay_a, axis, both_ways(pairs_a)), from_b)  4.01 us
    ppermute x4, waiting for transfers between devices, exchange(): lax.ppermute(value, 'dev', [(i, i ^ distance) for i in range(lax.axis_siz...  2.96 us
  transfers between devices with their start and end apart: 24, of which 8 were waited for; matrix products, arithmetic and copies ran while one was open for 1% of the time, Pallas kernels for 14%

profile of v1, /device:TPU:1, one launch (start us, length us, event | category | flops | bytes accessed | tf_op | source)
XLA Modules:
  0.0 90.3 jit_solution(10361495280335101825)
XLA Ops:
  0.7 2.3 %first_pack.1 = (f32[232,256]{1,0:T(8,128)}, f32[232,256]{1,0:T(8,128)}, f32[8,256]{1,0:T(8,128)}) custom-call(f32[32,32,256]{2,1,0:T(8,128)} %conc.9, s32[32,32,256]{2,1,0:T(8,128)} %label.11, s32[1,256]{1,0:T(1,128)} %bitcast.1, s32[1,256]{1,0:T(1,128)} %block.1), custom_call_target="tpu_custom_call" | custom-call | flops 1000000 | bytes 2582528 | tf_op jit(solution)/shard_map/first_pack/pallas_call | solution.py:34
  3.0 2.1 %collective-permute-start = (f32[232,256]{1,0:T(8,128)}, f32[232,256]{1,0:T(8,128)S(1)}, u32[]{:S(2)}, u32[]{:S(2)}) collective-permute-start(f32[232,256]{1,0:T(8,128)} %get-tuple-element.48), channel_id=1, source_target_pairs={{0,1},{2,3},{4,5},{6,7},{1,0},{3,2},{5,4},{7,6},{8,9},{10,11},{12,... | collective-permute-start | bytes 712712 | tf_op jit(solution)/shard_map/ppermute | solution.py:652
  5.8 1.2 %copy-done.2 = f32[32,32,256]{2,1,0:T(8,128)S(1)} copy-done((f32[32,32,256]{2,1,0:T(8,128)S(1)}, f32[32,32,256]{2,1,0:T(8,128)}, u32[]{:S(2)}) %copy-start.2) | copy-done | bytes 1048600
  8.4 3.0 %collective-permute-start.9 = (f32[24,8,256]{2,1,0:T(8,128)S(1)}, f32[24,8,256]{2,1,0:T(8,128)S(1)}, u32[]{:S(2)}, u32[]{:S(2)}) collective-permute-start(f32[24,8,256]{2,1,0:T(8,128)S(1)} %get-tuple-element.62), channel_id=1, source_target_pairs={{8,16},{16,8},{9,17},{17,9},{10,18},{18,10},{11,19},{19,11},{12,20... | collective-permute-start | bytes 589832 | tf_op jit(solution)/shard_map/ppermute | solution.py:651
  12.1 2.8 %collective-permute-done.r_a.y_a = f32[232,256]{1,0:T(8,128)S(1)} collective-permute-done((f32[232,256]{1,0:T(8,128)}, f32[232,256]{1,0:T(8,128)S(1)}, u32[]{:S(2)}, u32[]{:S(2)}) %collective-permute-start) | collective-permute-done | bytes 237600 | tf_op jit(solution)/shard_map/ppermute | solution.py:652
  15.0 1.4 %collective-permute-start.4 = (f32[4,256]{1,0:T(4,128)S(1)}, f32[4,256]{1,0:T(4,128)S(1)}, u32[]{:S(2)}, u32[]{:S(2)}) collective-permute-start(f32[4,256]{1,0:T(4,128)S(1)} %pad_maximum_fusion.1.rest_0_), channel_id=1, source_target_pairs={{0,2},{1,3},{2,0},{3,1},{4,6},{5,7},{6,4},{7,5},{8,10},{9,11},{10,... | collective-permute-start | bytes 12296 | tf_op jit(solution)/shard_map/ppermute | solution.py:656
  16.4 2.8 %collective-permute-start.2 = (f32[35,8,256]{2,1,0:T(8,128)S(1)}, f32[35,8,256]{2,1,0:T(8,128)S(1)}, u32[]{:S(2)}, u32[]{:S(2)}) collective-permute-start(f32[35,8,256]{2,1,0:T(8,128)S(1)} %get-tuple-element.51), channel_id=1, source_target_pairs={{0,8},{16,24},{8,0},{24,16},{1,9},{17,25},{9,1},{25,17},{2,10},{18... | collective-permute-start | bytes 860168 | tf_op jit(solution)/shard_map/ppermute | solution.py:652
  19.2 3.0 %collective-permute-start.3 = (f32[35,8,256]{2,1,0:T(8,128)S(1)}, f32[35,8,256]{2,1,0:T(8,128)S(1)}, u32[]{:S(2)}, u32[]{:S(2)}) collective-permute-start(f32[35,8,256]{2,1,0:T(8,128)S(1)} %get-tuple-element.52), channel_id=1, source_target_pairs={{8,16},{16,8},{9,17},{17,9},{10,18},{18,10},{11,19},{19,11},{12,20... | collective-permute-start | bytes 860168 | tf_op jit(solution)/shard_map/ppermute | solution.py:651
  22.4 1.3 %collective-permute-start.10 = (f32[320,256]{1,0:T(8,128)S(1)}, f32[320,256]{1,0:T(8,128)S(1)}, u32[]{:S(2)}, u32[]{:S(2)}) collective-permute-start(f32[320,256]{1,0:T(8,128)S(1)} %get-tuple-element.63), channel_id=1, source_target_pairs={{0,1},{2,3},{4,5},{6,7},{1,0},{3,2},{5,4},{7,6},{8,9},{10,11},{12,... | collective-permute-start | bytes 983048 | tf_op jit(solution)/shard_map/ppermute | solution.py:652
  24.5 2.4 %collective-permute-start.5 = (f32[8,256]{1,0:T(8,128)S(1)}, f32[8,256]{1,0:T(8,128)S(1)}, u32[]{:S(2)}, u32[]{:S(2)}) collective-permute-start(f32[8,256]{1,0:T(8,128)S(1)} %pad_maximum_fusion.token), channel_id=1, source_target_pairs={{0,4},{1,5},{2,6},{3,7},{4,0},{5,1},{6,2},{7,3},{8,12},{9,13},{10,... | collective-permute-start | bytes 24584 | tf_op jit(solution)/shard_map/ppermute | solution.py:656
  27.4 4.9 %sweeps.1.conc = f32[32,32,256]{2,1,0:T(8,128)S(1)} custom-call(f32[32,32,256]{2,1,0:T(8,128)S(1)} %copy-done.1, s32[32,32,256]{2,1,0:T(8,128)S(1)} %copy-done, f32[232,256]{1,0:T(8,128)S(1)} %collective-permute-done.r_a.y_a, f32[232,256]{1,0:T(8,128)S(1)} %collective-permute-done.1.r_b.y_b, f32[35,8,256]{2,1,0:T(8,128)S(1)} %collective-permute-done.2.x_a, ...), custom_call_target="tpu_custom_call" | custom-call | flops 1000000 | bytes 4194304 | tf_op jit(solution)/shard_map/sweeps/pallas_call | solution.py:34
  32.3 1.9 %collective-permute-done.5.rest_2_ = f32[8,256]{1,0:T(8,128)S(1)} collective-permute-done((f32[8,256]{1,0:T(8,128)S(1)}, f32[8,256]{1,0:T(8,128)S(1)}, u32[]{:S(2)}, u32[]{:S(2)}) %collective-permute-start.5) | collective-permute-done | bytes 8224 | tf_op jit(solution)/shard_map/ppermute | solution.py:656
  34.2 1.7 %flux.1 = (f32[32,32,256]{2,1,0:T(8,128)S(1)}, f32[96,256]{1,0:T(8,128)S(1)}, f32[96,256]{1,0:T(8,128)S(1)}) custom-call(f32[32,32,256]{2,1,0:T(8,128)S(1)} %sweeps.1.conc, s32[32,32,256]{2,1,0:T(8,128)S(1)} %copy-done, f32[32,32,256]{2,1,0:T(8,128)S(1)} %copy-done.2, f32[32,32,256]{2,1,0:T(8,128)S(1)} %copy-done.4, f32[4,256]{1,0:T(4,128)S(1)} %pad_maximum_fusion.1.rest_0_, ...), custom_call_target="tpu_custom_call" | custom-call | flops 1000000 | bytes 5455872 | tf_op jit(solution)/shard_map/flux/pallas_call | solution.py:34
  37.0 1.4 %store.1 = (f32[32,32,256]{2,1,0:T(8,128)}, f32[32,32,256]{2,1,0:T(8,128)}, f32[8,128]{1,0:T(8,128)S(1)}) custom-call(f32[32,32,256]{2,1,0:T(8,128)S(1)} %sweeps.1.conc, f32[32,32,256]{2,1,0:T(8,128)S(1)} %get-tuple-element.54.flux), custom_call_target="tpu_custom_call" | custom-call | flops 1000000 | bytes 4198400 | tf_op jit(solution)/shard_map/store/pallas_call | solution.py:34
  38.4 2.2 %ready.1 = (f32[40,40,256]{2,1,0:T(8,128)S(1)}, f32[40,40,256]{2,1,0:T(8,128)S(1)}, f32[40,40,256]{2,1,0:T(8,128)S(1)}, f32[40,40,256]{2,1,0:T(8,128)S(1)}, f32[8,128]{1,0:T(8,128)S(1)}) custom-call(f32[32,32,256]{2,1,0:T(8,128)S(1)} %copy-done.1, s32[32,32,256]{2,1,0:T(8,128)S(1)} %copy-done, f32[32,32,256]{2,1,0:T(8,128)S(1)} %copy-done.3, ...), custom_call_target="tpu_custom_call" | custom-call | flops 1000000 | bytes 11800576 | tf_op jit(solution)/shard_map/ready/pallas_call | solution.py:34
  40.7 1.6 %collective-permute-start.12 = (f32[15,8,256]{2,1,0:T(8,128)S(1)}, f32[15,8,256]{2,1,0:T(8,128)S(1)}, u32[]{:S(2)}, u32[]{:S(2)}) collective-permute-start(f32[15,8,256]{2,1,0:T(8,128)S(1)} %get-tuple-element.66), channel_id=1, source_target_pairs={{0,8},{16,24},{8,0},{24,16},{1,9},{17,25},{9,1},{25,17},{2,10},{18... | collective-permute-start | bytes 368648 | tf_op jit(solution)/shard_map/ppermute | solution.py:652
  42.3 2.0 %collective-permute-start.13 = (f32[15,8,256]{2,1,0:T(8,128)S(1)}, f32[15,8,256]{2,1,0:T(8,128)S(1)}, u32[]{:S(2)}, u32[]{:S(2)}) collective-permute-start(f32[15,8,256]{2,1,0:T(8,128)S(1)} %get-tuple-element.67), channel_id=1, source_target_pairs={{8,16},{16,8},{9,17},{17,9},{10,18},{18,10},{11,19},{19,11},{12,20... | collective-permute-start | bytes 368648 | tf_op jit(solution)/shard_map/ppermute | solution.py:651
  44.3 4.2 %collective-permute-done.13.x_b = f32[15,8,256]{2,1,0:T(8,128)S(1)} collective-permute-done((f32[15,8,256]{2,1,0:T(8,128)S(1)}, f32[15,8,256]{2,1,0:T(8,128)S(1)}, u32[]{:S(2)}, u32[]{:S(2)}) %collective-permute-start.13) | collective-permute-done | bytes 122912 | tf_op jit(solution)/shard_map/ppermute | solution.py:651
  48.5 2.7 %potential.1 = (f32[40,40,256]{2,1,0:T(8,128)S(1)}, f32[40,40,256]{2,1,0:T(8,128)S(1)}, f32[16,16,256]{2,1,0:T(8,128)S(1)}, f32[64,256]{1,0:T(8,128)S(1)}, f32[64,256]{1,0:T(8,128)S(1)}) custom-call(f32[32,32,256]{2,1,0:T(8,128)S(1)} %get-tuple-element.54.flux, f32[96,256]{1,0:T(8,128)S(1)} %collective-permute-done.6.r_a.y_a, ...), custom_call_target="tpu_custom_call" | custom-call | flops 1000000 | bytes 11714560 | tf_op jit(solution)/shard_map/potential/pallas_call | solution.py:34
  51.1 4.6 %collective-permute-start.14 = (f32[64,256]{1,0:T(8,128)S(1)}, f32[64,256]{1,0:T(8,128)S(1)}, u32[]{:S(2)}, u32[]{:S(2)}) collective-permute-start(f32[64,256]{1,0:T(8,128)S(1)} %get-tuple-element.73), channel_id=1, source_target_pairs={{0,1},{2,3},{4,5},{6,7},{1,0},{3,2},{5,4},{7,6},{8,9},{10,11},{12,... | collective-permute-start | bytes 196616 | tf_op jit(solution)/shard_map/ppermute | solution.py:652
  56.4 1.2 %coarse_ready.1 = (f32[8,8,256]{2,1,0:T(8,128)S(1)}, f32[8,128]{1,0:T(8,128)S(1)}, f32[8,128]{1,0:T(8,128)S(1)}) custom-call(f32[8,8,256]{2,1,0:T(8,128)S(1)} %get-tuple-element.50.token.coarse.own, f32[320,256]{1,0:T(8,128)S(1)} %collective-permute-done.10.yy_a.r_a.far_a, f32[320,256]{1,0:T(8,128)S(1)} %collective-permute-done.11.yy_b.r_b.far_b), custom_call_target="tpu_custom_call" | custom-call | flops 1000000 | bytes 794624 | tf_op jit(solution)/shard_map/coarse_ready/pallas_call | solution.py:34
  57.7 2.6 %collective-permute-start.17 = (f32[12,8,256]{2,1,0:T(8,128)S(1)}, f32[12,8,256]{2,1,0:T(8,128)S(1)}, u32[]{:S(2)}, u32[]{:S(2)}) collective-permute-start(f32[12,8,256]{2,1,0:T(8,128)S(1)} %get-tuple-element.77), channel_id=1, source_target_pairs={{8,16},{16,8},{9,17},{17,9},{10,18},{18,10},{11,19},{19,11},{12,20... | collective-permute-start | bytes 294920 | tf_op jit(solution)/shard_map/ppermute | solution.py:651
  60.3 3.4 %collective-permute-done.17.x_b = f32[12,8,256]{2,1,0:T(8,128)S(1)} collective-permute-done((f32[12,8,256]{2,1,0:T(8,128)S(1)}, f32[12,8,256]{2,1,0:T(8,128)S(1)}, u32[]{:S(2)}, u32[]{:S(2)}) %collective-permute-start.17) | collective-permute-done | bytes 98336 | tf_op jit(solution)/shard_map/ppermute | solution.py:651
  63.7 1.0 %middle.1 = (f32[24,24,256]{2,1,0:T(8,128)S(1)}, f32[24,24,256]{2,1,0:T(8,128)S(1)}, f32[24,24,256]{2,1,0:T(8,128)S(1)}, f32[8,12,256]{2,1,0:T(8,128)S(1)}, f32[...) custom-call(f32[16,16,256]{2,1,0:T(8,128)S(1)} %get-tuple-element.72.field.source_o, ...), custom_call_target="tpu_custom_call" | custom-call | flops 1000000 | bytes 4108288 | tf_op jit(solution)/shard_map/middle/pallas_call | solution.py:34
  64.7 5.0 %collective-permute-start.18 = (f32[80,256]{1,0:T(8,128)S(1)}, f32[80,256]{1,0:T(8,128)S(1)}, u32[]{:S(2)}, u32[]{:S(2)}) collective-permute-start(f32[80,256]{1,0:T(8,128)S(1)} %get-tuple-element.82), channel_id=1, source_target_pairs={{0,1},{2,3},{4,5},{6,7},{1,0},{3,2},{5,4},{7,6},{8,9},{10,11},{12,... | collective-permute-start | bytes 245768 | tf_op jit(solution)/shard_map/ppermute | solution.py:652
  70.4 1.2 %collective-permute-done.18.r_a = f32[80,256]{1,0:T(8,128)S(1)} collective-permute-done((f32[80,256]{1,0:T(8,128)S(1)}, f32[80,256]{1,0:T(8,128)S(1)}, u32[]{:S(2)}, u32[]{:S(2)}) %collective-permute-start.18) | collective-permute-done | bytes 81952 | tf_op jit(solution)/shard_map/ppermute | solution.py:652
  71.5 2.6 %collective-permute-start.20 = (f32[8,256]{1,0:T(8,128)S(1)}, f32[8,256]{1,0:T(8,128)S(1)}, u32[]{:S(2)}, u32[]{:S(2)}) collective-permute-start(f32[8,256]{1,0:T(8,128)S(1)} %slice_add_fusion), channel_id=1, source_target_pairs={{0,2},{1,3},{2,0},{3,1},{4,6},{5,7},{6,4},{7,5},{8,10},{9,11},{10,... | collective-permute-start | bytes 24584 | tf_op jit(solution)/shard_map/ppermute | solution.py:656
  75.2 2.5 %collective-permute-start.21 = (f32[8,256]{1,0:T(8,128)S(1)}, f32[8,256]{1,0:T(8,128)S(1)}, u32[]{:S(2)}, u32[]{:S(2)}) collective-permute-start(f32[8,256]{1,0:T(8,128)S(1)} %add.10), channel_id=1, source_target_pairs={{0,4},{1,5},{2,6},{3,7},{4,0},{5,1},{6,2},{7,3},{8,12},{9,13},{10,... | collective-permute-start | bytes 24584 | tf_op jit(solution)/shard_map/ppermute | solution.py:656
  77.7 1.2 %coarse.1.error = f32[8,16,256]{2,1,0:T(8,128)S(1)} custom-call(f32[8,12,256]{2,1,0:T(8,128)S(1)} %get-tuple-element.80.own, f32[8,12,256]{2,1,0:T(8,128)S(1)} %get-tuple-element.81.conduct, f32[320,256]{1,0:T(8,128)S(1)} %collective-permute-done.10.yy_a.r_a.far_a, f32[320,256]{1,0:T(8,128)S(1)} %collective-permute-done.11.yy_b.r_b.far_b, ...), custom_call_target="tpu_custom_call" | custom-call | flops 1000000 | bytes 1146880 | tf_op jit(solution)/shard_map/coarse/pallas_call | solution.py:34
  79.2 5.9 %collective-permute-start.23 = (f32[2,16,256]{2,1,0:T(8,128)S(1)}, f32[2,16,256]{2,1,0:T(8,128)S(1)}, u32[]{:S(2)}, u32[]{:S(2)}) collective-permute-start(f32[2,16,256]{2,1,0:T(8,128)S(1)} %get-tuple-element.87), channel_id=1, source_target_pairs={{8,16},{16,8},{9,17},{17,9},{10,18},{18,10},{11,19},{19,11},{12,20... | collective-permute-start | bytes 98312 | tf_op jit(solution)/shard_map/ppermute | solution.py:651
  85.1 1.6 %collective-permute-done.23.x_b = f32[2,16,256]{2,1,0:T(8,128)S(1)} collective-permute-done((f32[2,16,256]{2,1,0:T(8,128)S(1)}, f32[2,16,256]{2,1,0:T(8,128)S(1)}, u32[]{:S(2)}, u32[]{:S(2)}) %collective-permute-start.23) | collective-permute-done | bytes 32800 | tf_op jit(solution)/shard_map/ppermute | solution.py:651
  86.7 3.6 %finish.1 = f32[32,32,256]{2,1,0:T(8,128)} custom-call(f32[8,16,256]{2,1,0:T(8,128)S(1)} %get-tuple-element.85.error, f32[2,16,256]{2,1,0:T(8,128)S(1)} %collective-permute-done.22.x_a, f32[2,16,256]{2,1,0:T(8,128)S(1)} %collective-permute-done.23.x_b, f32[24,24,256]{2,1,0:T(8,128)S(1)} %get-tuple-element.88.mid_two, ...), custom_call_target="tpu_custom_call" | custom-call | flops 1000000 | bytes 7929856 | tf_op jit(solution)/shard_map/finish/pallas_call | solution.py:34
  (49 shorter events, 8.0 us)
Async XLA Ops:
  0.6 5.1 %copy-start.1 = (f32[32,32,256]{2,1,0:T(8,128)S(1)}, f32[32,32,256]{2,1,0:T(8,128)}, u32[]{:S(2)}) copy-start(f32[32,32,256]{2,1,0:T(8,128)} %conc.9) | copy-start | bytes 3145732
  0.6 5.1 %copy-start = (s32[32,32,256]{2,1,0:T(8,128)S(1)}, s32[32,32,256]{2,1,0:T(8,128)}, u32[]{:S(2)}) copy-start(s32[32,32,256]{2,1,0:T(8,128)} %label.11) | copy-start | bytes 3145732
  3.0 12.0 %collective-permute-start = (f32[232,256]{1,0:T(8,128)}, f32[232,256]{1,0:T(8,128)S(1)}, u32[]{:S(2)}, u32[]{:S(2)}) collective-permute-start(f32[232,256]{1,0:T(8,128)} %get-tuple-element.48), channel_id=1, source_target_pairs={{0,1},{2,3},{4,5},{6,7},{1,0},{3,2},{5,4},{7,6},{8,9},{10,11},{12,... | collective-permute-start | bytes 712712 | tf_op jit(solution)/shard_map/ppermute | solution.py:652
  5.1 11.2 %collective-permute-start.1 = (f32[232,256]{1,0:T(8,128)}, f32[232,256]{1,0:T(8,128)S(1)}, u32[]{:S(2)}, u32[]{:S(2)}) collective-permute-start(f32[232,256]{1,0:T(8,128)} %get-tuple-element.49), channel_id=1, source_target_pairs={{1,2},{3,4},{5,6},{2,1},{4,3},{6,5},{9,10},{11,12},{13,14},{10,9},... | collective-permute-start | bytes 712712 | tf_op jit(solution)/shard_map/ppermute | solution.py:651
  5.8 1.2 %copy-start.2 = (f32[32,32,256]{2,1,0:T(8,128)S(1)}, f32[32,32,256]{2,1,0:T(8,128)}, u32[]{:S(2)}) copy-start(f32[32,32,256]{2,1,0:T(8,128)} %phi.7) | copy-start | bytes 3145732
  7.3 14.9 %collective-permute-start.8 = (f32[24,8,256]{2,1,0:T(8,128)S(1)}, f32[24,8,256]{2,1,0:T(8,128)S(1)}, u32[]{:S(2)}, u32[]{:S(2)}) collective-permute-start(f32[24,8,256]{2,1,0:T(8,128)S(1)} %get-tuple-element.61), channel_id=1, source_target_pairs={{0,8},{16,24},{8,0},{24,16},{1,9},{17,25},{9,1},{25,17},{2,10},{18... | collective-permute-start | bytes 589832 | tf_op jit(solution)/shard_map/ppermute | solution.py:652
  8.4 13.9 %collective-permute-start.9 = (f32[24,8,256]{2,1,0:T(8,128)S(1)}, f32[24,8,256]{2,1,0:T(8,128)S(1)}, u32[]{:S(2)}, u32[]{:S(2)}) collective-permute-start(f32[24,8,256]{2,1,0:T(8,128)S(1)} %get-tuple-element.62), channel_id=1, source_target_pairs={{8,16},{16,8},{9,17},{17,9},{10,18},{18,10},{11,19},{19,11},{12,20... | collective-permute-start | bytes 589832 | tf_op jit(solution)/shard_map/ppermute | solution.py:651
  15.0 7.3 %collective-permute-start.4 = (f32[4,256]{1,0:T(4,128)S(1)}, f32[4,256]{1,0:T(4,128)S(1)}, u32[]{:S(2)}, u32[]{:S(2)}) collective-permute-start(f32[4,256]{1,0:T(4,128)S(1)} %pad_maximum_fusion.1.rest_0_), channel_id=1, source_target_pairs={{0,2},{1,3},{2,0},{3,1},{4,6},{5,7},{6,4},{7,5},{8,10},{9,11},{10,... | collective-permute-start | bytes 12296 | tf_op jit(solution)/shard_map/ppermute | solution.py:656
  16.4 10.6 %collective-permute-start.2 = (f32[35,8,256]{2,1,0:T(8,128)S(1)}, f32[35,8,256]{2,1,0:T(8,128)S(1)}, u32[]{:S(2)}, u32[]{:S(2)}) collective-permute-start(f32[35,8,256]{2,1,0:T(8,128)S(1)} %get-tuple-element.51), channel_id=1, source_target_pairs={{0,8},{16,24},{8,0},{24,16},{1,9},{17,25},{9,1},{25,17},{2,10},{18... | collective-permute-start | bytes 860168 | tf_op jit(solution)/shard_map/ppermute | solution.py:652
  19.2 8.2 %collective-permute-start.3 = (f32[35,8,256]{2,1,0:T(8,128)S(1)}, f32[35,8,256]{2,1,0:T(8,128)S(1)}, u32[]{:S(2)}, u32[]{:S(2)}) collective-permute-start(f32[35,8,256]{2,1,0:T(8,128)S(1)} %get-tuple-element.52), channel_id=1, source_target_pairs={{8,16},{16,8},{9,17},{17,9},{10,18},{18,10},{11,19},{19,11},{12,20... | collective-permute-start | bytes 860168 | tf_op jit(solution)/shard_map/ppermute | solution.py:651
  22.4 16.0 %collective-permute-start.10 = (f32[320,256]{1,0:T(8,128)S(1)}, f32[320,256]{1,0:T(8,128)S(1)}, u32[]{:S(2)}, u32[]{:S(2)}) collective-permute-start(f32[320,256]{1,0:T(8,128)S(1)} %get-tuple-element.63), channel_id=1, source_target_pairs={{0,1},{2,3},{4,5},{6,7},{1,0},{3,2},{5,4},{7,6},{8,9},{10,11},{12,... | collective-permute-start | bytes 983048 | tf_op jit(solution)/shard_map/ppermute | solution.py:652
  23.7 10.5 %copy-start.4 = (f32[32,32,256]{2,1,0:T(8,128)S(1)}, f32[32,32,256]{2,1,0:T(8,128)}, u32[]{:S(2)}) copy-start(f32[32,32,256]{2,1,0:T(8,128)} %solid.1) | copy-start | bytes 3145732
  23.7 14.7 %collective-permute-start.11 = (f32[320,256]{1,0:T(8,128)S(1)}, f32[320,256]{1,0:T(8,128)S(1)}, u32[]{:S(2)}, u32[]{:S(2)}) collective-permute-start(f32[320,256]{1,0:T(8,128)S(1)} %get-tuple-element.64), channel_id=1, source_target_pairs={{1,2},{3,4},{5,6},{2,1},{4,3},{6,5},{9,10},{11,12},{13,14},{10,9},... | collective-permute-start | bytes 983048 | tf_op jit(solution)/shard_map/ppermute | solution.py:651
  24.5 9.7 %collective-permute-start.5 = (f32[8,256]{1,0:T(8,128)S(1)}, f32[8,256]{1,0:T(8,128)S(1)}, u32[]{:S(2)}, u32[]{:S(2)}) collective-permute-start(f32[8,256]{1,0:T(8,128)S(1)} %pad_maximum_fusion.token), channel_id=1, source_target_pairs={{0,4},{1,5},{2,6},{3,7},{4,0},{5,1},{6,2},{7,3},{8,12},{9,13},{10,... | collective-permute-start | bytes 24584 | tf_op jit(solution)/shard_map/ppermute | solution.py:656
  36.0 2.4 %copy-start.3 = (f32[32,32,256]{2,1,0:T(8,128)S(1)}, f32[32,32,256]{2,1,0:T(8,128)}, u32[]{:S(2)}) copy-start(f32[32,32,256]{2,1,0:T(8,128)} %phi.7) | copy-start | bytes 3145732
  36.0 4.6 %collective-permute-start.6 = (f32[96,256]{1,0:T(8,128)S(1)}, f32[96,256]{1,0:T(8,128)S(1)}, u32[]{:S(2)}, u32[]{:S(2)}) collective-permute-start(f32[96,256]{1,0:T(8,128)S(1)} %get-tuple-element.57), channel_id=1, source_target_pairs={{0,1},{2,3},{4,5},{6,7},{1,0},{3,2},{5,4},{7,6},{8,9},{10,11},{12,... | collective-permute-start | bytes 294920 | tf_op jit(solution)/shard_map/ppermute | solution.py:652
  36.2 4.4 %collective-permute-start.7 = (f32[96,256]{1,0:T(8,128)S(1)}, f32[96,256]{1,0:T(8,128)S(1)}, u32[]{:S(2)}, u32[]{:S(2)}) collective-permute-start(f32[96,256]{1,0:T(8,128)S(1)} %get-tuple-element.58), channel_id=1, source_target_pairs={{1,2},{3,4},{5,6},{2,1},{4,3},{6,5},{9,10},{11,12},{13,14},{10,9},... | collective-permute-start | bytes 294920 | tf_op jit(solution)/shard_map/ppermute | solution.py:651
  40.7 3.6 %collective-permute-start.12 = (f32[15,8,256]{2,1,0:T(8,128)S(1)}, f32[15,8,256]{2,1,0:T(8,128)S(1)}, u32[]{:S(2)}, u32[]{:S(2)}) collective-permute-start(f32[15,8,256]{2,1,0:T(8,128)S(1)} %get-tuple-element.66), channel_id=1, source_target_pairs={{0,8},{16,24},{8,0},{24,16},{1,9},{17,25},{9,1},{25,17},{2,10},{18... | collective-permute-start | bytes 368648 | tf_op jit(solution)/shard_map/ppermute | solution.py:652
  42.3 6.2 %collective-permute-start.13 = (f32[15,8,256]{2,1,0:T(8,128)S(1)}, f32[15,8,256]{2,1,0:T(8,128)S(1)}, u32[]{:S(2)}, u32[]{:S(2)}) collective-permute-start(f32[15,8,256]{2,1,0:T(8,128)S(1)} %get-tuple-element.67), channel_id=1, source_target_pairs={{8,16},{16,8},{9,17},{17,9},{10,18},{18,10},{11,19},{19,11},{12,20... | collective-permute-start | bytes 368648 | tf_op jit(solution)/shard_map/ppermute | solution.py:651
  51.1 6.4 %collective-permute-start.14 = (f32[64,256]{1,0:T(8,128)S(1)}, f32[64,256]{1,0:T(8,128)S(1)}, u32[]{:S(2)}, u32[]{:S(2)}) collective-permute-start(f32[64,256]{1,0:T(8,128)S(1)} %get-tuple-element.73), channel_id=1, source_target_pairs={{0,1},{2,3},{4,5},{6,7},{1,0},{3,2},{5,4},{7,6},{8,9},{10,11},{12,... | collective-permute-start | bytes 196616 | tf_op jit(solution)/shard_map/ppermute | solution.py:652
  55.7 1.9 %collective-permute-start.15 = (f32[64,256]{1,0:T(8,128)S(1)}, f32[64,256]{1,0:T(8,128)S(1)}, u32[]{:S(2)}, u32[]{:S(2)}) collective-permute-start(f32[64,256]{1,0:T(8,128)S(1)} %get-tuple-element.74), channel_id=1, source_target_pairs={{1,2},{3,4},{5,6},{2,1},{4,3},{6,5},{9,10},{11,12},{13,14},{10,9},... | collective-permute-start | bytes 196616 | tf_op jit(solution)/shard_map/ppermute | solution.py:651
  57.7 2.7 %collective-permute-start.16 = (f32[12,8,256]{2,1,0:T(8,128)S(1)}, f32[12,8,256]{2,1,0:T(8,128)S(1)}, u32[]{:S(2)}, u32[]{:S(2)}) collective-permute-start(f32[12,8,256]{2,1,0:T(8,128)S(1)} %get-tuple-element.76), channel_id=1, source_target_pairs={{0,8},{16,24},{8,0},{24,16},{1,9},{17,25},{9,1},{25,17},{2,10},{18... | collective-permute-start | bytes 294920 | tf_op jit(solution)/shard_map/ppermute | solution.py:652
  57.7 5.9 %collective-permute-start.17 = (f32[12,8,256]{2,1,0:T(8,128)S(1)}, f32[12,8,256]{2,1,0:T(8,128)S(1)}, u32[]{:S(2)}, u32[]{:S(2)}) collective-permute-start(f32[12,8,256]{2,1,0:T(8,128)S(1)} %get-tuple-element.77), channel_id=1, source_target_pairs={{8,16},{16,8},{9,17},{17,9},{10,18},{18,10},{11,19},{19,11},{12,20... | collective-permute-start | bytes 294920 | tf_op jit(solution)/shard_map/ppermute | solution.py:651
  64.7 6.8 %collective-permute-start.18 = (f32[80,256]{1,0:T(8,128)S(1)}, f32[80,256]{1,0:T(8,128)S(1)}, u32[]{:S(2)}, u32[]{:S(2)}) collective-permute-start(f32[80,256]{1,0:T(8,128)S(1)} %get-tuple-element.82), channel_id=1, source_target_pairs={{0,1},{2,3},{4,5},{6,7},{1,0},{3,2},{5,4},{7,6},{8,9},{10,11},{12,... | collective-permute-start | bytes 245768 | tf_op jit(solution)/shard_map/ppermute | solution.py:652
  69.7 8.0 %collective-permute-start.19 = (f32[80,256]{1,0:T(8,128)S(1)}, f32[80,256]{1,0:T(8,128)S(1)}, u32[]{:S(2)}, u32[]{:S(2)}) collective-permute-start(f32[80,256]{1,0:T(8,128)S(1)} %get-tuple-element.83), channel_id=1, source_target_pairs={{1,2},{3,4},{5,6},{2,1},{4,3},{6,5},{9,10},{11,12},{13,14},{10,9},... | collective-permute-start | bytes 245768 | tf_op jit(solution)/shard_map/ppermute | solution.py:651
  71.5 3.7 %collective-permute-start.20 = (f32[8,256]{1,0:T(8,128)S(1)}, f32[8,256]{1,0:T(8,128)S(1)}, u32[]{:S(2)}, u32[]{:S(2)}) collective-permute-start(f32[8,256]{1,0:T(8,128)S(1)} %slice_add_fusion), channel_id=1, source_target_pairs={{0,2},{1,3},{2,0},{3,1},{4,6},{5,7},{6,4},{7,5},{8,10},{9,11},{10,... | collective-permute-start | bytes 24584 | tf_op jit(solution)/shard_map/ppermute | solution.py:656
  75.2 3.7 %collective-permute-start.21 = (f32[8,256]{1,0:T(8,128)S(1)}, f32[8,256]{1,0:T(8,128)S(1)}, u32[]{:S(2)}, u32[]{:S(2)}) collective-permute-start(f32[8,256]{1,0:T(8,128)S(1)} %add.10), channel_id=1, source_target_pairs={{0,4},{1,5},{2,6},{3,7},{4,0},{5,1},{6,2},{7,3},{8,12},{9,13},{10,... | collective-permute-start | bytes 24584 | tf_op jit(solution)/shard_map/ppermute | solution.py:656
  79.1 6.0 %collective-permute-start.22 = (f32[2,16,256]{2,1,0:T(8,128)S(1)}, f32[2,16,256]{2,1,0:T(8,128)S(1)}, u32[]{:S(2)}, u32[]{:S(2)}) collective-permute-start(f32[2,16,256]{2,1,0:T(8,128)S(1)} %get-tuple-element.86), channel_id=1, source_target_pairs={{0,8},{16,24},{8,0},{24,16},{1,9},{17,25},{9,1},{25,17},{2,10},{18... | collective-permute-start | bytes 98312 | tf_op jit(solution)/shard_map/ppermute | solution.py:652
  79.2 7.5 %collective-permute-start.23 = (f32[2,16,256]{2,1,0:T(8,128)S(1)}, f32[2,16,256]{2,1,0:T(8,128)S(1)}, u32[]{:S(2)}, u32[]{:S(2)}) collective-permute-start(f32[2,16,256]{2,1,0:T(8,128)S(1)} %get-tuple-element.87), channel_id=1, source_target_pairs={{8,16},{16,8},{9,17},{17,9},{10,18},{18,10},{11,19},{19,11},{12,20... | collective-permute-start | bytes 98312 | tf_op jit(solution)/shard_map/ppermute | solution.py:651

commit v2 on v1

--- a/solution.py
+++ b/solution.py
@@ -29,7 +29,7 @@
 FAR = pl.BlockSpec(memory_space=pltpu.HBM)
 
 
-def call(kernel, outs, args, scratch=(), in_specs=None, out_specs=None, limit=VMEM_LIMIT, flops=10**6, name=None):
+def call(kernel, outs, args, scratch=(), in_specs=None, out_specs=None, limit=VMEM_LIMIT, aliases=None, flops=10**6, name=None):
     size = sum(4 * a.size for a in args) + sum(4 * o.size for o in outs)
     return pl.pallas_call(
         kernel,
@@ -37,6 +37,7 @@
         in_specs=in_specs or [WHOLE] * len(args),
         out_specs=tuple(out_specs or [WHOLE] * len(outs)),
         scratch_shapes=list(scratch),
+        input_output_aliases=aliases or {},
         compiler_params=pltpu.CompilerParams(vmem_limit_bytes=limit),
         cost_estimate=pl.CostEstimate(flops=flops, bytes_accessed=size, transcendentals=0),
         name=name,
@@ -71,8 +72,8 @@
         body(x)
 
 
-def even(axis):
-    return lax.rem(lax.axis_index(axis), 2) == 0
+def odd(axis):
+    return lax.rem(lax.axis_index(axis), 2) == 1
 
 
 def along_y(v):
@@ -116,26 +117,26 @@
 
 
 def y_sides(r_a, r_b, at, count):
-    flag = even("dev")
+    flag = odd("dev")
     a, b = r_a[at : at + count, :], r_b[at : at + count, :]
     return either(flag, a, b), either(flag, b, a)
 
 
 def x_sides(r_a, r_b, index):
-    flag = even("grp")
+    flag = odd("grp")
     a, b = r_a[index], r_b[index]
     return either(flag, a, b), either(flag, b, a)
 
 
 def send_y(pay_a, pay_b, at, first, last):
-    flag = even("dev")
+    flag = odd("dev")
     n = first.shape[0]
     pay_a[at : at + n, :] = either(flag, last, first)
     pay_b[at : at + n, :] = either(flag, first, last)
 
 
 def send_x(pay_a, pay_b, index, first, last):
-    flag = even("grp")
+    flag = odd("grp")
     pay_a[index] = either(flag, last, first)
     pay_b[index] = either(flag, first, last)
 
@@ -159,9 +160,8 @@
     for c in copies:
         c.wait()
     named = jnp.concatenate([own_owner[...], own_block[...], jnp.zeros((6, 256), jnp.int32)], axis=0).astype(F32)
-    own_lists[...] = named
-    pay_a[7 * nx : 7 * nx + 8, :] = named
-    pay_b[7 * nx : 7 * nx + 8, :] = named
+    for j in range(own_lists.shape[0]):
+        own_lists[j] = named
     for x in range(nx):
         send_y(pay_a, pay_b, 7 * x, c_first[x, 0:4, :], c_last[x, 4:8, :])
         send_y(pay_a, pay_b, 7 * x + 4, l_first[x, 0:3, :].astype(F32), l_last[x, 5:8, :].astype(F32))
@@ -202,7 +202,7 @@
             send_x(pay_a, pay_b, 20 + 5 * k + t, plane(label, k, t, 4, 3), plane(label, nx - 3 + k, t, 4, 3))
 
 
-def second_pack_kernel(phi, mid, coarse, x_a, x_b, token, pay_a, pay_b):
+def second_pack_kernel(phi, mid, coarse, x_a, x_b, pay_a, pay_b):
     nx = phi.shape[0]
     half = nx // 2
     for x in range(nx):
@@ -283,13 +283,11 @@
     loop(0, nx, last)
 
 
-def flux_kernel(conc, label, phi, solid, *rest):
-    lists_refs, (flux, pay_a, pay_b, marked) = rest[:-4], rest[-4:]
-    lists = jnp.concatenate([r[...] for r in lists_refs], axis=0)
+def flux_kernel(conc, label, phi, solid, lists, flux, pay_a, pay_b, marked):
     nx = conc.shape[0]
-    entries = lists.shape[0] // 2 * 256
-    owner = jnp.concatenate([lists[2 * i : 2 * i + 1, :] for i in range(entries // 256)], axis=1)
-    block = jnp.concatenate([lists[2 * i + 1 : 2 * i + 2, :] for i in range(entries // 256)], axis=1)
+    entries = lists.shape[0] * 256
+    owner = jnp.concatenate([lists[i, 0:1, :] for i in range(lists.shape[0])], axis=1)
+    block = jnp.concatenate([lists[i, 1:2, :] for i in range(lists.shape[0])], axis=1)
     here = lax.axis_index("dev")
     block = jnp.where(owner.astype(jnp.int32) == here, block.astype(jnp.int32), -1)
     hit_row = (iota((32, entries), 0) == lax.shift_right_arithmetic(block, 6)).astype(jnp.bfloat16)
@@ -381,16 +379,13 @@
             send_x(pay_a, pay_b, 5 * k + t, tile(k, t), tile(nx - 3 + k, t))
 
 
-def potential_kernel(
-    flux, y_a, y_b, x_a, x_b, weight, scale, share, start, after_two, source, source_mid, pay_a, pay_b, field, pairs
-):
+def potential_inner_kernel(flux, y_a, y_b, weight, scale, share, start, after_two, source, first, source_mid, pairs):
     nx = flux.shape[0]
-    half = nx // 2
 
     def put(x, rows, f):
         part = scale[x, rows, :] * f
         source[x, rows, :] = share[x, rows, :] + part
-        field[x, rows, :] = start[x, rows, :] + part
+        first[x, rows, :] = start[x, rows, :] + part
 
     def own(i):
         put(HALO + i, slice(0, 32), flux[i])
@@ -398,22 +393,16 @@
     loop(0, nx, own)
     for i in range(nx):
         put(HALO + i, slice(32, 40), halo_tile(*y_sides(y_a, y_b, 3 * i, 3)))
-    for k in range(3):
-        for t in range(5):
-            rows = slice(8 * t, 8 * t + 8)
-            after, before = x_sides(x_a, x_b, 5 * k + t)
-            put(1 + k, rows, before)
-            put(HALO + nx + k, rows, after)
 
     def around(values, x):
         v = values[x]
         return v, weight[x] * ((values[x - 1] + values[x + 1]) + (along_y(v) + along_z(v)))
 
     def sweep(x):
-        v, near = around(field, x)
+        v, near = around(first, x)
         after_two[x] = 0.2 * v + (source[x] + near)
 
-    loop(2, nx + 2 * HALO - 2, sweep)
+    loop(HALO + 1, HALO + nx - 1, sweep)
 
     def remainder(x):
         v, near = around(after_two, x)
@@ -423,7 +412,47 @@
         x = HALO + 2 * i
         source_mid[i] = 0.25 * pair_rows(remainder(x) + remainder(x + 1), pairs.at[i])
 
-    loop(0, half, coarsen, 4)
+    loop(1, nx // 2 - 1, coarsen, 4)
+
+
+def potential_edge_kernel(
+    x_a, x_b, weight, scale, share, start, inner_two, inner_source, inner_first, inner_mid,
+    edge_two, edge_source, source_mid, pay_a, pay_b, first, pairs,
+):
+    half = source_mid.shape[0]
+    nx = 2 * half
+    for side, face in ((0, HALO), (1, HALO + nx)):
+        base = 8 * side + HALO - face
+        for k in range(3):
+            x = face - 3 + k if side == 0 else face + k
+            for t in range(5):
+                rows = slice(8 * t, 8 * t + 8)
+                part = scale[x, rows, :] * x_sides(x_a, x_b, 5 * k + t)[1 - side]
+                edge_source[base + x, rows, :] = share[x, rows, :] + part
+                first[base + x, rows, :] = start[x, rows, :] + part
+
+        def first_of(x, base=base):
+            return inner_first[x] if HALO <= x < HALO + nx else first[base + x]
+
+        def source_of(x, base=base):
+            return inner_source[x] if HALO <= x < HALO + nx else edge_source[base + x]
+
+        def two_of(x, base=base):
+            return inner_two[x] if HALO < x < HALO + nx - 1 else edge_two[base + x]
+
+        for x in range(face - 2, face + 1) if side == 0 else range(face - 1, face + 2):
+            v = first_of(x)
+            near = weight[x] * ((first_of(x - 1) + first_of(x + 1)) + (along_y(v) + along_z(v)))
+            edge_two[base + x] = 0.2 * v + (source_of(x) + near)
+        total = 0.0
+        at = face if side == 0 else face - 2
+        for x in (at, at + 1):
+            v = two_of(x)
+            near = weight[x] * ((two_of(x - 1) + two_of(x + 1)) + (along_y(v) + along_z(v)))
+            total = total + ((source_of(x) - OMEGA * v) + near)[0:32, :] / scale[x, 0:32, :]
+        source_mid[0 if side == 0 else half - 1] = 0.25 * pair_rows(total, pairs.at[side])
+    for x in range(1, half - 1):
+        source_mid[x] = inner_mid[x]
     for x in range(half):
         send_y(pay_a, pay_b, 4 * x, source_mid[x, 0:4, :], source_mid[x, 12:16, :])
 
@@ -576,80 +605,139 @@
         send_x(pay_a, pay_b, k, out[k], out[6 + k])
 
 
-def finish_kernel(
-    error, x_a, x_b, mid_two, mid_source, mid_weight, fine_two, fine_source, fine_weight,
-    out, one, two, fine_one, fine_last, dup, dup_2, result, sems,
+def squeeze(tile):
+    return jnp.where(iota((8, 256), 0) < 2, tile, pltpu.roll(tile, 4, 0))
+
+
+def spread_coarse(plane, room):
+    return jnp.concatenate([twice(plane[0:8], room.at[0]), twice(squeeze(plane[8:16]), room.at[1])[0:8]], axis=0)
+
+
+def spread_mid(plane, room):
+    parts = [twice(plane[0:8], room.at[0]), twice(plane[8:16], room.at[1]), twice(squeeze(plane[16:24]), room.at[2])[0:8]]
+    return jnp.concatenate(parts, axis=0)
+
+
+def smoothed(before, v, after, weight, source, w):
+    inner = (before + after) + along_y(v)
+    return source + (0.2 * v + weight * (w * inner + along_z(v)))
+
+
+def finish_inner_kernel(
+    error, mid_two, mid_source, mid_weight, fine_two, fine_source, fine_weight,
+    out, zero, one, fine_one, fine_last, two, dup, dup_2, result, sems,
 ):
     n = mid_two.shape[0]
     nf = fine_two.shape[0]
-    nx = out.shape[0]
-
-    def squeeze(tile):
-        return jnp.where(iota((8, 256), 0) < 2, tile, pltpu.roll(tile, 4, 0))
-
-    after, before = x_sides(x_a, x_b, slice(0, 2))
-    for c in range(-2, 10):
-        plane = before[c + 2] if c < 0 else (after[c - 8] if c >= 8 else error[c])
-        room = dup.at[c + 2]
-        spread = jnp.concatenate([twice(plane[0:8], room.at[0]), twice(squeeze(plane[8:16]), room.at[1])[0:8]], axis=0)
+    for c in range(8):
+        spread = spread_coarse(error[c], dup.at[c])
         for x in (2 * c + HALO, 2 * c + 1 + HALO):
-            one[x] = jnp.where(mid_weight[x] > 0.0, mid_two[x] + spread, 0.0)
-
-    def around(values, weights, x, w):
-        v = values[x]
-        inner = (values[x - 1] + values[x + 1]) + along_y(v)
-        return 0.2 * v + weights[x] * (w * inner + along_z(v))
-
-    for s, (old, new) in ((2, (one, two)), (3, (two, one))):
-
-        def sweep(x, old=old, new=new):
-            new[x] = mid_source[x] + around(old, mid_weight, x, 0.25)
-
-        loop(s, n - s, sweep, 10)
+            zero[x] = jnp.where(mid_weight[x] > 0.0, mid_two[x] + spread, 0.0)
+
+    def sweep_mid(x, old, new):
+        new[x] = smoothed(old[x - 1], old[x], old[x + 1], mid_weight[x], mid_source[x], 0.25)
+
+    for x in range(HALO + 1, n - HALO - 1):
+        sweep_mid(x, zero, one)
+    for x in range(HALO + 2, n - HALO - 2):
+        sweep_mid(x, one, two)
 
     def lift(m):
-        plane = one[m]
-        room = dup_2.at[m]
-        spread = jnp.concatenate(
-            [twice(plane[0:8], room.at[0]), twice(plane[8:16], room.at[1]), twice(squeeze(plane[16:24]), room.at[2])[0:8]],
-            axis=0,
-        )
+        spread = spread_mid(two[m], dup_2.at[m])
         x = 2 * m - HALO
         fine_one[x] = fine_two[x] + spread
         fine_one[x + 1] = fine_two[x + 1] + spread
 
-    loop(3, n - 3, lift, 6)
+    loop(HALO + 2, n - HALO - 2, lift, 6)
 
     def sweep_one(x):
-        fine_last[x] = fine_source[x] + around(fine_one, fine_weight, x, 1.0)
-
-    loop(3, nf - 3, sweep_one)
+        fine_last[x] = smoothed(fine_one[x - 1], fine_one[x], fine_one[x + 1], fine_weight[x], fine_source[x], 1.0)
+
+    low, high = 2 * HALO + 1, nf - 2 * HALO - 1
+    loop(low, high, sweep_one, 11)
     copies = []
-    for j in range(nx // 8):
-
-        def sweep_two(i):
-            x = HALO + i
-            result[i] = (fine_source[x] + around(fine_last, fine_weight, x, 1.0))[0:32, :]
-
-        for i in range(8 * j, 8 * j + 8):
-            sweep_two(i)
-        rows = pl.ds(8 * j, 8)
+    low, high = low + 1, high - 1
+    for j in range(2):
+        mid = low + (high - low) // 2
+        for x in range(low, mid) if j == 0 else range(mid, high):
+            v = smoothed(fine_last[x - 1], fine_last[x], fine_last[x + 1], fine_weight[x], fine_source[x], 1.0)
+            result[x - HALO] = v[0:32, :]
+        rows = pl.ds(low - HALO, mid - low) if j == 0 else pl.ds(mid - HALO, high - mid)
         copies.append(pltpu.make_async_copy(result.at[rows], out.at[rows], sems.at[j]))
         copies[-1].start()
     for c in copies:
         c.wait()
 
 
+def finish_edge_kernel(
+    x_a, x_b, mid_two, mid_source, mid_weight, fine_two, edge_two, fine_source, edge_source, fine_weight,
+    zero, one, fine_one, fine_last, begun, out, zero_edge, one_edge, fine_edge, last_edge, dup, dup_2, result, sems,
+):
+    n = mid_two.shape[0]
+    nf = fine_two.shape[0]
+    nx = nf - 2 * HALO
+    copies = []
+    planes = x_sides(x_a, x_b, slice(0, 2))
+    for side in (0, 1):
+        sign = 1 if side == 0 else -1
+        at = lambda k, side=side: HALO + k if side == 0 else n - HALO - 1 - k
+        fine = lambda k, side=side: HALO + k if side == 0 else nf - HALO - 1 - k
+        base = 8 * side + (0 if side == 0 else HALO - HALO - nx)
+        for c in range(2):
+            plane = planes[1 - side][c]
+            spread = spread_coarse(plane, dup.at[2 * side + c])
+            first = 2 * c if side == 0 else n - HALO + 2 * c
+            for x in (first, first + 1):
+                zero_edge[x] = jnp.where(mid_weight[x] > 0.0, mid_two[x] + spread, 0.0)
+
+        def zero_of(k):
+            return zero[at(k)] if k >= 0 else zero_edge[at(k)]
+
+        def one_of(k):
+            return one[at(k)] if k >= 1 else one_edge[at(k)]
+
+        for k in range(-2, 1):
+            x = at(k)
+            one_edge[x] = smoothed(zero_of(k - 1), zero_of(k), zero_of(k + 1), mid_weight[x], mid_source[x], 0.25)
+        for k in range(-1, 2):
+            x = at(k)
+            value = smoothed(one_of(k - 1), one_of(k), one_of(k + 1), mid_weight[x], mid_source[x], 0.25)
+            spread = spread_mid(value, dup_2.at[3 * side + k + 1])
+            for f in (fine(2 * k), fine(2 * k + 1)):
+                inside = HALO < f < nf - HALO - 1
+                before = fine_two[f] if inside else edge_two[base + f]
+                fine_edge[f] = before + spread
+
+        def fine_of(k):
+            return fine_one[fine(k)] if k >= 4 else fine_edge[fine(k)]
+
+        def last_of(k):
+            return fine_last[fine(k)] if k >= 5 else last_edge[fine(k)]
+
+        for k in range(-1, 5):
+            f = fine(k)
+            source = fine_source[f] if HALO <= f < nf - HALO else edge_source[base + f]
+            last_edge[f] = smoothed(fine_of(k - 1), fine_of(k), fine_of(k + 1), fine_weight[f], source, 1.0)
+        for k in range(6):
+            f = fine(k)
+            v = smoothed(last_of(k - 1), last_of(k), last_of(k + 1), fine_weight[f], fine_source[f], 1.0)
+            result[f - HALO] = v[0:32, :]
+        rows = pl.ds(0, 6) if side == 0 else pl.ds(nx - 6, 6)
+        copies.append(pltpu.make_async_copy(result.at[rows], out.at[rows], sems.at[side]))
+        copies[-1].start()
+    for c in copies:
+        c.wait()
+
+
 def both_ways(pairs):
     return pairs + [(j, i) for i, j in pairs]
 
 
 def swap(pay_a, pay_b, axis):
     size = lax.axis_size(axis)
-    pairs_a = [(i, i + 1) for i in range(0, size - 1, 2)]
-    pairs_b = [(i, i + 1) for i in range(1, size - 1, 2)]
-    from_b = lax.ppermute(pay_b, axis, both_ways(pairs_b))
-    return lax.ppermute(pay_a, axis, both_ways(pairs_a)), from_b
+    pairs_a = [(i, i + 1) for i in range(1, size - 1, 2)]
+    pairs_b = [(i, i + 1) for i in range(0, size - 1, 2)]
+    return lax.ppermute(pay_a, axis, both_ways(pairs_a)), lax.ppermute(pay_b, axis, both_ways(pairs_b))
 
 
 def exchange(value, distance):
@@ -667,7 +755,7 @@
 
     pay_a, pay_b, own_lists = call(
         first_pack_kernel,
-        [shaped(7 * nx + 8, 256)] * 2 + [shaped(8, 256)],
+        [shaped(7 * nx, 256)] * 2 + [shaped(peers, 8, 256)],
         [conc_old, phase_label, iface_owner.reshape(1, -1), iface_block],
         [vmem(nx, 8, 256)] * 2
         + [pltpu.VMEM((nx, 8, 256), jnp.int32)] * 2
@@ -686,26 +774,19 @@
         name="own",
     )
     xx_a, xx_b = swap(pay_a, pay_b, "grp")
+    lists = lax.all_to_all(own_lists, "dev", split_axis=0, concat_axis=0, tiled=True)
     pay_a, pay_b = call(
         first_pack_x_kernel,
         [shaped(35, 8, 256)] * 2,
-        [conc_old, phase_label, y_a, y_b, conduct_coarse],
+        [conc_old, phase_label, y_a, y_b, lists],
         name="first_pack_x",
     )
     x_a, x_b = swap(pay_a, pay_b, "grp")
-    lists = jnp.concatenate([own_lists[0:2], y_a[7 * nx : 7 * nx + 2]], axis=0)
-    pieces = [lists]
-    distance = 2
-    while distance < peers:
-        if distance > 2:
-            lists = jnp.concatenate(pieces, axis=0)
-        pieces.append(exchange(lists, distance))
-        distance *= 2
     far_rows = 4 * (nx + half + 4 * HALO) + 64
     pay_a, pay_b = call(
         second_pack_kernel,
         [shaped(far_rows, 256)] * 2,
-        [phi_old, conduct_mid, conduct_coarse, xx_a, xx_b, lists],
+        [phi_old, conduct_mid, conduct_coarse, xx_a, xx_b],
         name="second_pack",
     )
     yy_a, yy_b = swap(pay_a, pay_b, "dev")
@@ -720,7 +801,7 @@
     flux_own, pay_a, pay_b = call(
         flux_kernel,
         [shaped(nx, nx, 256), shaped(3 * nx, 256), shaped(3 * nx, 256)],
-        [conc_new, phase_label, phi_old, solid_pot] + pieces,
+        [conc_new, phase_label, phi_old, solid_pot, lists],
         [vmem(32, 8, LANES)],
         name="flux",
     )
@@ -744,12 +825,20 @@
         flux_pack_x_kernel, [shaped(15, 8, 256)] * 2, [flux_own, f_a, f_b, stored, made], name="flux_pack_x"
     )
     fx_a, fx_b = swap(pay_a, pay_b, "grp")
-    fine_two, fine_source, source_mid, pay_a, pay_b = call(
-        potential_kernel,
-        [shaped(*ext), shaped(*ext), shaped(half, half, 256), shaped(4 * half, 256), shaped(4 * half, 256)],
-        [flux_own, f_a, f_b, fx_a, fx_b, weight, scale, share, start],
-        [vmem(*ext), vmem(half, 2, nx, LANES)],
-        name="potential",
+    fine_two, fine_source, fine_first, inner_mid = call(
+        potential_inner_kernel,
+        [shaped(*ext)] * 3 + [shaped(half, half, 256)],
+        [flux_own, f_a, f_b, weight, scale, share, start],
+        [vmem(half, 2, nx, LANES)],
+        name="potential_inner",
+    )
+    edge = (16, nx + 2 * HALO, 256)
+    edge_two, edge_source, source_mid, pay_a, pay_b = call(
+        potential_edge_kernel,
+        [shaped(*edge), shaped(*edge), shaped(half, half, 256), shaped(4 * half, 256), shaped(4 * half, 256)],
+        [fx_a, fx_b, weight, scale, share, start, fine_two, fine_source, fine_first, inner_mid],
+        [vmem(*edge), vmem(2, 2, nx, LANES)],
+        name="potential_edge",
     )
     m_a, m_b = swap(pay_a, pay_b, "dev")
     wide = (quarter, 32, 256)
@@ -780,7 +869,7 @@
         [vmem(*wide)] * 4,
         name="coarse",
     )
-    sums = sums + c_a[72:80]
+    sums = sums + c_b[72:80]
     distance = 2
     while distance < peers:
         sums = sums + exchange(sums, distance)
@@ -789,16 +878,28 @@
         shift_kernel, [shaped(8, 16, 256), shaped(2, 16, 256), shaped(2, 16, 256)], [error, sums], name="shift"
     )
     e_a, e_b = swap(pay_a, pay_b, "grp")
+    begun, zero, one, fine_one, fine_last = call(
+        finish_inner_kernel,
+        [shaped(nx, nx, 256), shaped(*ext_mid), shaped(*ext_mid), shaped(*ext), shaped(*ext)],
+        [error, mid_two, mid_source, mid_weight, fine_two, fine_source, weight],
+        [vmem(*ext_mid), vmem(8, 2, 2, 16, LANES), vmem(half + 2 * HALO, 3, 2, 16, LANES), vmem(nx, nx, 256)]
+        + [pltpu.SemaphoreType.DMA((2,))],
+        out_specs=[FAR] + [WHOLE] * 4,
+        name="finish_inner",
+    )
+    finish_args = [e_a, e_b, mid_two, mid_source, mid_weight, fine_two, edge_two, fine_source, edge_source, weight]
+    finish_args += [zero, one, fine_one, fine_last, begun]
     (potential,) = call(
-        finish_kernel,
+        finish_edge_kernel,
         [shaped(nx, nx, 256)],
-        [error, e_a, e_b, mid_two, mid_source, mid_weight, fine_two, fine_source, weight],
-        [vmem(*ext_mid)] * 2
-        + [vmem(*ext)] * 2
-        + [vmem(12, 2, 2, 16, LANES), vmem(half + 2 * HALO, 3, 2, 16, LANES), vmem(nx, nx, 256)]
-        + [pltpu.SemaphoreType.DMA((4,))],
+        finish_args,
+        [vmem(*ext_mid), vmem(*ext_mid), vmem(*ext), vmem(*ext)]
+        + [vmem(4, 2, 2, 16, LANES), vmem(6, 3, 2, 16, LANES), vmem(nx, nx, 256)]
+        + [pltpu.SemaphoreType.DMA((2,))],
+        in_specs=[WHOLE] * (len(finish_args) - 1) + [FAR],
         out_specs=[FAR],
-        name="finish",
+        aliases={len(finish_args) - 1: 0},
+        name="finish_edge",
     )
     return (concentration, flux, potential)
 

time: 90.8 us -> 92.6 us (1.020)
  blocking collectives: 0 us -> 10.1 us
  starting transfers between devices: 47.8 us -> 41.4 us
  waiting for transfers between devices: 16.6 us -> 14.8 us
    all_to_all x0 -> x1, blocking collectives: none -> 10.1 us  [body(): lax.all_to_all(own_lists, 'dev', split_axis=0, concat_axis=0, tiled=True)]
    ppermute x4 -> x2, starting transfers between devices: 8.95 us -> 3.22 us  [exchange(): lax.ppermute(value, 'dev', [(i, i ^ distance) for i in range(lax.axis_siz...]
    ppermute x20, waiting for transfers between devices: 13.6 us -> 12.4 us  [the longest x10 6.67 us: swap(): lax.ppermute(pay_b, axis, both_ways(pairs_b))]
    ppermute x4 -> x2, waiting for transfers between devices: 2.96 us -> 2.33 us  [exchange(): lax.ppermute(value, 'dev', [(i, i ^ distance) for i in range(lax.axis_siz...]
    pallas_call x16 -> x18, Pallas kernels: 23 us -> 23.3 us  [call(): pl.pallas_call(kernel, out_shape=tuple(outs), in_specs=in_specs or [WHOLE...]
  transfers between devices with their start and end apart: 24 -> 22, of which waited for: 8 -> 8; matrix products, arithmetic and copies ran while one was open for 1% -> 0% of each run, Pallas kernels for 14% -> 19%
where the time goes in v2:
time: 92.6 us; the launch traced here: 91.8 us
  starting transfers between devices  41.4 us (45%)
  Pallas kernels  23.3 us (25%)
  waiting for transfers between devices  14.8 us (16%)
  blocking collectives  10.1 us (11%)
  local copies, waits for them, and re-layouts  1.25 us (1%)
  between operations  0.99 us (1%)
    pallas_call x18, Pallas kernels, call(): pl.pallas_call(kernel, out_shape=tuple(outs), in_specs=in_specs or [WHOLE...  23.3 us
    ppermute x10, starting transfers between devices, swap(): lax.ppermute(pay_a, axis, both_ways(pairs_a))  21.7 us
    ppermute x10, starting transfers between devices, swap(): lax.ppermute(pay_b, axis, both_ways(pairs_b))  16.5 us
    all_to_all x1, blocking collectives, body(): lax.all_to_all(own_lists, 'dev', split_axis=0, concat_axis=0, tiled=True)  10.1 us
    ppermute x10, waiting for transfers between devices, swap(): lax.ppermute(pay_b, axis, both_ways(pairs_b))  6.67 us
    ppermute x10, waiting for transfers between devices, swap(): lax.ppermute(pay_a, axis, both_ways(pairs_a))  5.76 us
    ppermute x2, starting transfers between devices, exchange(): lax.ppermute(value, 'dev', [(i, i ^ distance) for i in range(lax.axis_siz...  3.22 us
    ppermute x2, waiting for transfers between devices, exchange(): lax.ppermute(value, 'dev', [(i, i ^ distance) for i in range(lax.axis_siz...  2.33 us
  transfers between devices with their start and end apart: 22, of which 8 were waited for; matrix products, arithmetic and copies ran while one was open for 0% of the time, Pallas kernels for 19%

profile of v2, /device:TPU:1, one launch (start us, length us, event | category | flops | bytes accessed | tf_op | source)
XLA Modules:
  0.0 91.8 jit_solution(16482834438864824307)
XLA Ops:
  0.7 2.3 %first_pack.1 = (f32[224,256]{1,0:T(8,128)}, f32[224,256]{1,0:T(8,128)}, f32[8,8,256]{2,1,0:T(8,128)}) custom-call(f32[32,32,256]{2,1,0:T(8,128)} %conc.9, s32[32,32,256]{2,1,0:T(8,128)} %label.11, s32[1,256]{1,0:T(1,128)} %bitcast.1, s32[1,256]{1,0:T(1,128)} %block.1), custom_call_target="tpu_custom_call" | custom-call | flops 1000000 | bytes 2623488 | tf_op jit(solution)/shard_map/first_pack/pallas_call | solution.py:34
  3.7 4.6 %collective-permute-start.1 = (f32[224,256]{1,0:T(8,128)}, f32[224,256]{1,0:T(8,128)S(1)}, u32[]{:S(2)}, u32[]{:S(2)}) collective-permute-start(f32[224,256]{1,0:T(8,128)} %get-tuple-element.58), channel_id=1, source_target_pairs={{0,1},{2,3},{4,5},{6,7},{1,0},{3,2},{5,4},{7,6},{8,9},{10,11},{12,... | collective-permute-start | bytes 688136 | tf_op jit(solution)/shard_map/ppermute | solution.py:740
  8.3 1.2 %copy-done.2 = f32[32,32,256]{2,1,0:T(8,128)S(1)} copy-done((f32[32,32,256]{2,1,0:T(8,128)S(1)}, f32[32,32,256]{2,1,0:T(8,128)}, u32[]{:S(2)}) %copy-start.2) | copy-done | bytes 1048600
  9.8 4.3 %collective-permute-start.6 = (f32[24,8,256]{2,1,0:T(8,128)S(1)}, f32[24,8,256]{2,1,0:T(8,128)S(1)}, u32[]{:S(2)}, u32[]{:S(2)}) collective-permute-start(f32[24,8,256]{2,1,0:T(8,128)S(1)} %get-tuple-element.70), channel_id=1, source_target_pairs={{8,16},{16,8},{9,17},{17,9},{10,18},{18,10},{11,19},{19,11},{12,20... | collective-permute-start | bytes 589832 | tf_op jit(solution)/shard_map/ppermute | solution.py:740
  14.2 10.1 %all_to_all.5.token.lists = f32[8,8,256]{2,1,0:T(8,128)S(1)} all-to-all(f32[8,8,256]{2,1,0:T(8,128)S(1)} %copy-done.5), channel_id=1, replica_groups=mesh['grp'=4,'dev'=8] {'dev'}, dimensions={0} | all-to-all | bytes 131072 | tf_op jit(solution)/shard_map/all_to_all | solution.py:777
  24.4 3.2 %collective-permute-start.2 = (f32[35,8,256]{2,1,0:T(8,128)S(1)}, f32[35,8,256]{2,1,0:T(8,128)S(1)}, u32[]{:S(2)}, u32[]{:S(2)}) collective-permute-start(f32[35,8,256]{2,1,0:T(8,128)S(1)} %get-tuple-element.60), channel_id=1, source_target_pairs={{8,16},{16,8},{9,17},{17,9},{10,18},{18,10},{11,19},{19,11},{12,20... | collective-permute-start | bytes 860168 | tf_op jit(solution)/shard_map/ppermute | solution.py:740
  28.6 2.4 %collective-permute-start.9 = (f32[320,256]{1,0:T(8,128)S(1)}, f32[320,256]{1,0:T(8,128)S(1)}, u32[]{:S(2)}, u32[]{:S(2)}) collective-permute-start(f32[320,256]{1,0:T(8,128)S(1)} %get-tuple-element.73), channel_id=1, source_target_pairs={{0,1},{2,3},{4,5},{6,7},{1,0},{3,2},{5,4},{7,6},{8,9},{10,11},{12,... | collective-permute-start | bytes 983048 | tf_op jit(solution)/shard_map/ppermute | solution.py:740
  31.0 1.3 %collective-permute-done.2.x_a = f32[35,8,256]{2,1,0:T(8,128)S(1)} collective-permute-done((f32[35,8,256]{2,1,0:T(8,128)S(1)}, f32[35,8,256]{2,1,0:T(8,128)S(1)}, u32[]{:S(2)}, u32[]{:S(2)}) %collective-permute-start.2) | collective-permute-done | bytes 286752 | tf_op jit(solution)/shard_map/ppermute | solution.py:740
  32.3 4.9 %sweeps.1.conc = f32[32,32,256]{2,1,0:T(8,128)S(1)} custom-call(f32[32,32,256]{2,1,0:T(8,128)S(1)} %copy-done.1, s32[32,32,256]{2,1,0:T(8,128)S(1)} %copy-done, f32[224,256]{1,0:T(8,128)S(1)} %collective-permute-done.r_a.y_a, f32[224,256]{1,0:T(8,128)S(1)} %collective-permute-done.1.r_b.y_b, f32[35,8,256]{2,1,0:T(8,128)S(1)} %collective-permute-done.2.x_a, ...), custom_call_target="tpu_custom_call" | custom-call | flops 1000000 | bytes 4177920 | tf_op jit(solution)/shard_map/sweeps/pallas_call | solution.py:34
  37.2 1.7 %flux.1 = (f32[32,32,256]{2,1,0:T(8,128)S(1)}, f32[96,256]{1,0:T(8,128)S(1)}, f32[96,256]{1,0:T(8,128)S(1)}) custom-call(f32[32,32,256]{2,1,0:T(8,128)S(1)} %sweeps.1.conc, s32[32,32,256]{2,1,0:T(8,128)S(1)} %copy-done, f32[32,32,256]{2,1,0:T(8,128)S(1)} %copy-done.2, f32[32,32,256]{2,1,0:T(8,128)S(1)} %copy-done.4, f32[8,8,256]{2,1,0:T(8,128)S(1)} %all_to_all.5.token.lists), custom_call_target="tpu_custom_call" | custom-call | flops 1000000 | bytes 5505024 | tf_op jit(solution)/shard_map/flux/pallas_call | solution.py:34
  39.8 2.3 %collective-permute-start.5 = (f32[96,256]{1,0:T(8,128)S(1)}, f32[96,256]{1,0:T(8,128)S(1)}, u32[]{:S(2)}, u32[]{:S(2)}) collective-permute-start(f32[96,256]{1,0:T(8,128)S(1)} %get-tuple-element.66), channel_id=1, source_target_pairs={{0,1},{2,3},{4,5},{6,7},{1,0},{3,2},{5,4},{7,6},{8,9},{10,11},{12,... | collective-permute-start | bytes 294920 | tf_op jit(solution)/shard_map/ppermute | solution.py:740
  42.1 1.4 %store.1 = (f32[32,32,256]{2,1,0:T(8,128)}, f32[32,32,256]{2,1,0:T(8,128)}, f32[8,128]{1,0:T(8,128)S(1)}) custom-call(f32[32,32,256]{2,1,0:T(8,128)S(1)} %sweeps.1.conc, f32[32,32,256]{2,1,0:T(8,128)S(1)} %get-tuple-element.62.flux), custom_call_target="tpu_custom_call" | custom-call | flops 1000000 | bytes 4198400 | tf_op jit(solution)/shard_map/store/pallas_call | solution.py:34
  43.5 3.8 %collective-permute-done.9.yy_b.r_b.far_b = f32[320,256]{1,0:T(8,128)S(1)} collective-permute-done((f32[320,256]{1,0:T(8,128)S(1)}, f32[320,256]{1,0:T(8,128)S(1)}, u32[]{:S(2)}, u32[]{:S(2)}) %collective-permute-start.9) | collective-permute-done | bytes 327712 | tf_op jit(solution)/shard_map/ppermute | solution.py:740
  47.3 2.1 %ready.1 = (f32[40,40,256]{2,1,0:T(8,128)S(1)}, f32[40,40,256]{2,1,0:T(8,128)S(1)}, f32[40,40,256]{2,1,0:T(8,128)S(1)}, f32[40,40,256]{2,1,0:T(8,128)S(1)}, f32[8,128]{1,0:T(8,128)S(1)}) custom-call(f32[32,32,256]{2,1,0:T(8,128)S(1)} %copy-done.1, s32[32,32,256]{2,1,0:T(8,128)S(1)} %copy-done, f32[32,32,256]{2,1,0:T(8,128)S(1)} %copy-done.3, ...), custom_call_target="tpu_custom_call" | custom-call | flops 1000000 | bytes 11784192 | tf_op jit(solution)/shard_map/ready/pallas_call | solution.py:34
  49.5 2.7 %collective-permute-start.10 = (f32[15,8,256]{2,1,0:T(8,128)S(1)}, f32[15,8,256]{2,1,0:T(8,128)S(1)}, u32[]{:S(2)}, u32[]{:S(2)}) collective-permute-start(f32[15,8,256]{2,1,0:T(8,128)S(1)} %get-tuple-element.75), channel_id=1, source_target_pairs={{8,16},{16,8},{9,17},{17,9},{10,18},{18,10},{11,19},{19,11},{12,20... | collective-permute-start | bytes 368648 | tf_op jit(solution)/shard_map/ppermute | solution.py:740
  52.3 2.1 %potential_inner.1 = (f32[40,40,256]{2,1,0:T(8,128)S(1)}, f32[40,40,256]{2,1,0:T(8,128)S(1)}, f32[40,40,256]{2,1,0:T(8,128)S(1)}, f32[16,16,256]{2,1,0:T(8,128)S(1)}) custom-call(f32[32,32,256]{2,1,0:T(8,128)S(1)} %get-tuple-element.62.flux, f32[96,256]{1,0:T(8,128)S(1)} %collective-permute-done.4.r_a.y_a, f32[96,256]{1,0:T(8,128)S(1)} %collective-permute-done.5.r_b.y_b, ...), custom_call_target="tpu_custom_call" | custom-call | flops 1000000 | bytes 12976128 | tf_op jit(solution)/shard_map/potential_inner/pallas_call | solution.py:34
  54.5 1.2 %collective-permute-done.10.x_a = f32[15,8,256]{2,1,0:T(8,128)S(1)} collective-permute-done((f32[15,8,256]{2,1,0:T(8,128)S(1)}, f32[15,8,256]{2,1,0:T(8,128)S(1)}, u32[]{:S(2)}, u32[]{:S(2)}) %collective-permute-start.10) | collective-permute-done | bytes 122912 | tf_op jit(solution)/shard_map/ppermute | solution.py:740
  56.8 4.5 %collective-permute-start.13 = (f32[64,256]{1,0:T(8,128)S(1)}, f32[64,256]{1,0:T(8,128)S(1)}, u32[]{:S(2)}, u32[]{:S(2)}) collective-permute-start(f32[64,256]{1,0:T(8,128)S(1)} %get-tuple-element.87), channel_id=1, source_target_pairs={{0,1},{2,3},{4,5},{6,7},{1,0},{3,2},{5,4},{7,6},{8,9},{10,11},{12,... | collective-permute-start | bytes 196616 | tf_op jit(solution)/shard_map/ppermute | solution.py:740
  61.3 1.2 %coarse_ready.1 = (f32[8,8,256]{2,1,0:T(8,128)S(1)}, f32[8,128]{1,0:T(8,128)S(1)}, f32[8,128]{1,0:T(8,128)S(1)}) custom-call(f32[8,8,256]{2,1,0:T(8,128)S(1)} %get-tuple-element.69.coarse.own, f32[320,256]{1,0:T(8,128)S(1)} %collective-permute-done.8.yy_a.r_a.far_a, f32[320,256]{1,0:T(8,128)S(1)} %collective-permute-done.9.yy_b.r_b.far_b), custom_call_target="tpu_custom_call" | custom-call | flops 1000000 | bytes 794624 | tf_op jit(solution)/shard_map/coarse_ready/pallas_call | solution.py:34
  62.5 1.6 %collective-permute-done.13.r_b.y_b = f32[64,256]{1,0:T(8,128)S(1)} collective-permute-done((f32[64,256]{1,0:T(8,128)S(1)}, f32[64,256]{1,0:T(8,128)S(1)}, u32[]{:S(2)}, u32[]{:S(2)}) %collective-permute-start.13) | collective-permute-done | bytes 65568 | tf_op jit(solution)/shard_map/ppermute | solution.py:740
  64.2 2.7 %collective-permute-start.14 = (f32[12,8,256]{2,1,0:T(8,128)S(1)}, f32[12,8,256]{2,1,0:T(8,128)S(1)}, u32[]{:S(2)}, u32[]{:S(2)}) collective-permute-start(f32[12,8,256]{2,1,0:T(8,128)S(1)} %get-tuple-element.89), channel_id=1, source_target_pairs={{8,16},{16,8},{9,17},{17,9},{10,18},{18,10},{11,19},{19,11},{12,20... | collective-permute-start | bytes 294920 | tf_op jit(solution)/shard_map/ppermute | solution.py:740
  67.0 3.2 %collective-permute-done.14.x_a = f32[12,8,256]{2,1,0:T(8,128)S(1)} collective-permute-done((f32[12,8,256]{2,1,0:T(8,128)S(1)}, f32[12,8,256]{2,1,0:T(8,128)S(1)}, u32[]{:S(2)}, u32[]{:S(2)}) %collective-permute-start.14) | collective-permute-done | bytes 98336 | tf_op jit(solution)/shard_map/ppermute | solution.py:740
  70.1 1.0 %middle.1 = (f32[24,24,256]{2,1,0:T(8,128)S(1)}, f32[24,24,256]{2,1,0:T(8,128)S(1)}, f32[24,24,256]{2,1,0:T(8,128)S(1)}, f32[8,12,256]{2,1,0:T(8,128)S(1)}, f32[...) custom-call(f32[16,16,256]{2,1,0:T(8,128)S(1)} %get-tuple-element.85.field.source_o, ...), custom_call_target="tpu_custom_call" | custom-call | flops 1000000 | bytes 4108288 | tf_op jit(solution)/shard_map/middle/pallas_call | solution.py:34
  71.2 2.3 %collective-permute-start.17 = (f32[80,256]{1,0:T(8,128)S(1)}, f32[80,256]{1,0:T(8,128)S(1)}, u32[]{:S(2)}, u32[]{:S(2)}) collective-permute-start(f32[80,256]{1,0:T(8,128)S(1)} %get-tuple-element.96), channel_id=1, source_target_pairs={{0,1},{2,3},{4,5},{6,7},{1,0},{3,2},{5,4},{7,6},{8,9},{10,11},{12,... | collective-permute-start | bytes 245768 | tf_op jit(solution)/shard_map/ppermute | solution.py:740
  74.1 1.2 %collective-permute-done.17.r_b = f32[80,256]{1,0:T(8,128)S(1)} collective-permute-done((f32[80,256]{1,0:T(8,128)S(1)}, f32[80,256]{1,0:T(8,128)S(1)}, u32[]{:S(2)}, u32[]{:S(2)}) %collective-permute-start.17) | collective-permute-done | bytes 81952 | tf_op jit(solution)/shard_map/ppermute | solution.py:740
  75.3 1.4 %collective-permute-start.18 = (f32[8,256]{1,0:T(8,128)S(1)}, f32[8,256]{1,0:T(8,128)S(1)}, u32[]{:S(2)}, u32[]{:S(2)}) collective-permute-start(f32[8,256]{1,0:T(8,128)S(1)} %slice_add_fusion), channel_id=1, source_target_pairs={{0,2},{1,3},{2,0},{3,1},{4,6},{5,7},{6,4},{7,5},{8,10},{9,11},{10,... | collective-permute-start | bytes 24584 | tf_op jit(solution)/shard_map/ppermute | solution.py:744
  76.6 1.8 %collective-permute-done.18 = f32[8,256]{1,0:T(8,128)S(1)} collective-permute-done((f32[8,256]{1,0:T(8,128)S(1)}, f32[8,256]{1,0:T(8,128)S(1)}, u32[]{:S(2)}, u32[]{:S(2)}) %collective-permute-start.18) | collective-permute-done | bytes 8224 | tf_op jit(solution)/shard_map/ppermute | solution.py:744
  78.5 1.9 %collective-permute-start.19 = (f32[8,256]{1,0:T(8,128)S(1)}, f32[8,256]{1,0:T(8,128)S(1)}, u32[]{:S(2)}, u32[]{:S(2)}) collective-permute-start(f32[8,256]{1,0:T(8,128)S(1)} %add.10), channel_id=1, source_target_pairs={{0,4},{1,5},{2,6},{3,7},{4,0},{5,1},{6,2},{7,3},{8,12},{9,13},{10,... | collective-permute-start | bytes 24584 | tf_op jit(solution)/shard_map/ppermute | solution.py:744
  80.3 1.2 %coarse.1.error = f32[8,16,256]{2,1,0:T(8,128)S(1)} custom-call(f32[8,12,256]{2,1,0:T(8,128)S(1)} %get-tuple-element.93.own, f32[8,12,256]{2,1,0:T(8,128)S(1)} %get-tuple-element.94.conduct, f32[320,256]{1,0:T(8,128)S(1)} %collective-permute-done.8.yy_a.r_a.far_a, f32[320,256]{1,0:T(8,128)S(1)} %collective-permute-done.9.yy_b.r_b.far_b, ...), custom_call_target="tpu_custom_call" | custom-call | flops 1000000 | bytes 1146880 | tf_op jit(solution)/shard_map/coarse/pallas_call | solution.py:34
  82.2 5.3 %collective-permute-start.20 = (f32[2,16,256]{2,1,0:T(8,128)S(1)}, f32[2,16,256]{2,1,0:T(8,128)S(1)}, u32[]{:S(2)}, u32[]{:S(2)}) collective-permute-start(f32[2,16,256]{2,1,0:T(8,128)S(1)} %get-tuple-element.98), channel_id=1, source_target_pairs={{8,16},{16,8},{9,17},{17,9},{10,18},{18,10},{11,19},{19,11},{12,20... | collective-permute-start | bytes 98312 | tf_op jit(solution)/shard_map/ppermute | solution.py:740
  87.5 2.5 %finish_inner.1 = (f32[32,32,256]{2,1,0:T(8,128)}, f32[24,24,256]{2,1,0:T(8,128)S(1)}, f32[24,24,256]{2,1,0:T(8,128)S(1)}, f32[40,40,256]{2,1,0:T(8,128)S(1)}, f32[40,40,256]{2,1,0:T(8,128)S(1)}) custom-call(f32[8,16,256]{2,1,0:T(8,128)S(1)} %get-tuple-element.105.error, f32[24,24,256]{2,1,0:T(8,128)S(1)} %get-tuple-element.100.mid_two, ...), custom_call_target="tpu_custom_call" | custom-call | flops 1000000 | bytes 12320768 | tf_op jit(solution)/shard_map/finish_inner/pallas_call | solution.py:34
  90.1 1.7 %finish_edge.1 = f32[32,32,256]{2,1,0:T(8,128)} custom-call(f32[2,16,256]{2,1,0:T(8,128)S(1)} %collective-permute-done.20.x_a, f32[2,16,256]{2,1,0:T(8,128)S(1)} %collective-permute-done.21.x_b, f32[24,24,256]{2,1,0:T(8,128)S(1)} %get-tuple-element.100.mid_two, f32[24,24,256]{2,1,0:T(8,128)S(1)} %get-tuple-element.101.mid_source, ...), custom_call_target="tpu_custom_call", output_to_operand_aliasing={{}: (14, {})} | custom-call | flops 1000000 | bytes 14614528 | tf_op jit(solution)/shard_map/finish_edge/pallas_call | solution.py:34
  (46 shorter events, 5.6 us)
Async XLA Ops:
  0.6 7.7 %copy-start.1 = (f32[32,32,256]{2,1,0:T(8,128)S(1)}, f32[32,32,256]{2,1,0:T(8,128)}, u32[]{:S(2)}) copy-start(f32[32,32,256]{2,1,0:T(8,128)} %conc.9) | copy-start | bytes 3145732
  0.6 7.6 %copy-start = (s32[32,32,256]{2,1,0:T(8,128)S(1)}, s32[32,32,256]{2,1,0:T(8,128)}, u32[]{:S(2)}) copy-start(s32[32,32,256]{2,1,0:T(8,128)} %label.11) | copy-start | bytes 3145732
  3.0 21.3 %collective-permute-start = (f32[224,256]{1,0:T(8,128)}, f32[224,256]{1,0:T(8,128)S(1)}, u32[]{:S(2)}, u32[]{:S(2)}) collective-permute-start(f32[224,256]{1,0:T(8,128)} %get-tuple-element.57), channel_id=1, source_target_pairs={{1,2},{3,4},{5,6},{2,1},{4,3},{6,5},{9,10},{11,12},{13,14},{10,9},... | collective-permute-start | bytes 688136 | tf_op jit(solution)/shard_map/ppermute | solution.py:740
  3.7 20.6 %collective-permute-start.1 = (f32[224,256]{1,0:T(8,128)}, f32[224,256]{1,0:T(8,128)S(1)}, u32[]{:S(2)}, u32[]{:S(2)}) collective-permute-start(f32[224,256]{1,0:T(8,128)} %get-tuple-element.58), channel_id=1, source_target_pairs={{0,1},{2,3},{4,5},{6,7},{1,0},{3,2},{5,4},{7,6},{8,9},{10,11},{12,... | collective-permute-start | bytes 688136 | tf_op jit(solution)/shard_map/ppermute | solution.py:740
  8.3 1.2 %copy-start.2 = (f32[32,32,256]{2,1,0:T(8,128)S(1)}, f32[32,32,256]{2,1,0:T(8,128)}, u32[]{:S(2)}) copy-start(f32[32,32,256]{2,1,0:T(8,128)} %phi.7) | copy-start | bytes 3145732
  9.5 4.7 %copy-start.5 = (f32[8,8,256]{2,1,0:T(8,128)S(1)}, f32[8,8,256]{2,1,0:T(8,128)}, u32[]{:S(2)}) copy-start(f32[8,8,256]{2,1,0:T(8,128)} %get-tuple-element.59) | copy-start | bytes 196612
  9.8 17.8 %collective-permute-start.6 = (f32[24,8,256]{2,1,0:T(8,128)S(1)}, f32[24,8,256]{2,1,0:T(8,128)S(1)}, u32[]{:S(2)}, u32[]{:S(2)}) collective-permute-start(f32[24,8,256]{2,1,0:T(8,128)S(1)} %get-tuple-element.70), channel_id=1, source_target_pairs={{8,16},{16,8},{9,17},{17,9},{10,18},{18,10},{11,19},{19,11},{12,20... | collective-permute-start | bytes 589832 | tf_op jit(solution)/shard_map/ppermute | solution.py:740
  14.1 13.6 %collective-permute-start.7 = (f32[24,8,256]{2,1,0:T(8,128)S(1)}, f32[24,8,256]{2,1,0:T(8,128)S(1)}, u32[]{:S(2)}, u32[]{:S(2)}) collective-permute-start(f32[24,8,256]{2,1,0:T(8,128)S(1)} %get-tuple-element.71), channel_id=1, source_target_pairs={{0,8},{16,24},{8,0},{24,16},{1,9},{17,25},{9,1},{25,17},{2,10},{18... | collective-permute-start | bytes 589832 | tf_op jit(solution)/shard_map/ppermute | solution.py:740
  24.4 8.0 %collective-permute-start.2 = (f32[35,8,256]{2,1,0:T(8,128)S(1)}, f32[35,8,256]{2,1,0:T(8,128)S(1)}, u32[]{:S(2)}, u32[]{:S(2)}) collective-permute-start(f32[35,8,256]{2,1,0:T(8,128)S(1)} %get-tuple-element.60), channel_id=1, source_target_pairs={{8,16},{16,8},{9,17},{17,9},{10,18},{18,10},{11,19},{19,11},{12,20... | collective-permute-start | bytes 860168 | tf_op jit(solution)/shard_map/ppermute | solution.py:740
  27.6 4.7 %collective-permute-start.3 = (f32[35,8,256]{2,1,0:T(8,128)S(1)}, f32[35,8,256]{2,1,0:T(8,128)S(1)}, u32[]{:S(2)}, u32[]{:S(2)}) collective-permute-start(f32[35,8,256]{2,1,0:T(8,128)S(1)} %get-tuple-element.61), channel_id=1, source_target_pairs={{0,8},{16,24},{8,0},{24,16},{1,9},{17,25},{9,1},{25,17},{2,10},{18... | collective-permute-start | bytes 860168 | tf_op jit(solution)/shard_map/ppermute | solution.py:740
  27.9 15.6 %collective-permute-start.8 = (f32[320,256]{1,0:T(8,128)S(1)}, f32[320,256]{1,0:T(8,128)S(1)}, u32[]{:S(2)}, u32[]{:S(2)}) collective-permute-start(f32[320,256]{1,0:T(8,128)S(1)} %get-tuple-element.72), channel_id=1, source_target_pairs={{1,2},{3,4},{5,6},{2,1},{4,3},{6,5},{9,10},{11,12},{13,14},{10,9},... | collective-permute-start | bytes 983048 | tf_op jit(solution)/shard_map/ppermute | solution.py:740
  28.5 8.7 %copy-start.4 = (f32[32,32,256]{2,1,0:T(8,128)S(1)}, f32[32,32,256]{2,1,0:T(8,128)}, u32[]{:S(2)}) copy-start(f32[32,32,256]{2,1,0:T(8,128)} %solid.1) | copy-start | bytes 3145732
  28.6 18.8 %collective-permute-start.9 = (f32[320,256]{1,0:T(8,128)S(1)}, f32[320,256]{1,0:T(8,128)S(1)}, u32[]{:S(2)}, u32[]{:S(2)}) collective-permute-start(f32[320,256]{1,0:T(8,128)S(1)} %get-tuple-element.73), channel_id=1, source_target_pairs={{0,1},{2,3},{4,5},{6,7},{1,0},{3,2},{5,4},{7,6},{8,9},{10,11},{12,... | collective-permute-start | bytes 983048 | tf_op jit(solution)/shard_map/ppermute | solution.py:740
  39.0 8.4 %copy-start.3 = (f32[32,32,256]{2,1,0:T(8,128)S(1)}, f32[32,32,256]{2,1,0:T(8,128)}, u32[]{:S(2)}) copy-start(f32[32,32,256]{2,1,0:T(8,128)} %phi.7) | copy-start | bytes 3145732
  39.0 10.5 %collective-permute-start.4 = (f32[96,256]{1,0:T(8,128)S(1)}, f32[96,256]{1,0:T(8,128)S(1)}, u32[]{:S(2)}, u32[]{:S(2)}) collective-permute-start(f32[96,256]{1,0:T(8,128)S(1)} %get-tuple-element.65), channel_id=1, source_target_pairs={{1,2},{3,4},{5,6},{2,1},{4,3},{6,5},{9,10},{11,12},{13,14},{10,9},... | collective-permute-start | bytes 294920 | tf_op jit(solution)/shard_map/ppermute | solution.py:740
  39.8 9.7 %collective-permute-start.5 = (f32[96,256]{1,0:T(8,128)S(1)}, f32[96,256]{1,0:T(8,128)S(1)}, u32[]{:S(2)}, u32[]{:S(2)}) collective-permute-start(f32[96,256]{1,0:T(8,128)S(1)} %get-tuple-element.66), channel_id=1, source_target_pairs={{0,1},{2,3},{4,5},{6,7},{1,0},{3,2},{5,4},{7,6},{8,9},{10,11},{12,... | collective-permute-start | bytes 294920 | tf_op jit(solution)/shard_map/ppermute | solution.py:740
  49.5 6.2 %collective-permute-start.10 = (f32[15,8,256]{2,1,0:T(8,128)S(1)}, f32[15,8,256]{2,1,0:T(8,128)S(1)}, u32[]{:S(2)}, u32[]{:S(2)}) collective-permute-start(f32[15,8,256]{2,1,0:T(8,128)S(1)} %get-tuple-element.75), channel_id=1, source_target_pairs={{8,16},{16,8},{9,17},{17,9},{10,18},{18,10},{11,19},{19,11},{12,20... | collective-permute-start | bytes 368648 | tf_op jit(solution)/shard_map/ppermute | solution.py:740
  52.2 3.5 %collective-permute-start.11 = (f32[15,8,256]{2,1,0:T(8,128)S(1)}, f32[15,8,256]{2,1,0:T(8,128)S(1)}, u32[]{:S(2)}, u32[]{:S(2)}) collective-permute-start(f32[15,8,256]{2,1,0:T(8,128)S(1)} %get-tuple-element.76), channel_id=1, source_target_pairs={{0,8},{16,24},{8,0},{24,16},{1,9},{17,25},{9,1},{25,17},{2,10},{18... | collective-permute-start | bytes 368648 | tf_op jit(solution)/shard_map/ppermute | solution.py:740
  56.1 6.4 %collective-permute-start.12 = (f32[64,256]{1,0:T(8,128)S(1)}, f32[64,256]{1,0:T(8,128)S(1)}, u32[]{:S(2)}, u32[]{:S(2)}) collective-permute-start(f32[64,256]{1,0:T(8,128)S(1)} %get-tuple-element.86), channel_id=1, source_target_pairs={{1,2},{3,4},{5,6},{2,1},{4,3},{6,5},{9,10},{11,12},{13,14},{10,9},... | collective-permute-start | bytes 196616 | tf_op jit(solution)/shard_map/ppermute | solution.py:740
  56.8 7.4 %collective-permute-start.13 = (f32[64,256]{1,0:T(8,128)S(1)}, f32[64,256]{1,0:T(8,128)S(1)}, u32[]{:S(2)}, u32[]{:S(2)}) collective-permute-start(f32[64,256]{1,0:T(8,128)S(1)} %get-tuple-element.87), channel_id=1, source_target_pairs={{0,1},{2,3},{4,5},{6,7},{1,0},{3,2},{5,4},{7,6},{8,9},{10,11},{12,... | collective-permute-start | bytes 196616 | tf_op jit(solution)/shard_map/ppermute | solution.py:740
  64.2 5.9 %collective-permute-start.14 = (f32[12,8,256]{2,1,0:T(8,128)S(1)}, f32[12,8,256]{2,1,0:T(8,128)S(1)}, u32[]{:S(2)}, u32[]{:S(2)}) collective-permute-start(f32[12,8,256]{2,1,0:T(8,128)S(1)} %get-tuple-element.89), channel_id=1, source_target_pairs={{8,16},{16,8},{9,17},{17,9},{10,18},{18,10},{11,19},{19,11},{12,20... | collective-permute-start | bytes 294920 | tf_op jit(solution)/shard_map/ppermute | solution.py:740
  66.9 3.2 %collective-permute-start.15 = (f32[12,8,256]{2,1,0:T(8,128)S(1)}, f32[12,8,256]{2,1,0:T(8,128)S(1)}, u32[]{:S(2)}, u32[]{:S(2)}) collective-permute-start(f32[12,8,256]{2,1,0:T(8,128)S(1)} %get-tuple-element.90), channel_id=1, source_target_pairs={{0,8},{16,24},{8,0},{24,16},{1,9},{17,25},{9,1},{25,17},{2,10},{18... | collective-permute-start | bytes 294920 | tf_op jit(solution)/shard_map/ppermute | solution.py:740
  71.2 4.1 %collective-permute-start.17 = (f32[80,256]{1,0:T(8,128)S(1)}, f32[80,256]{1,0:T(8,128)S(1)}, u32[]{:S(2)}, u32[]{:S(2)}) collective-permute-start(f32[80,256]{1,0:T(8,128)S(1)} %get-tuple-element.96), channel_id=1, source_target_pairs={{0,1},{2,3},{4,5},{6,7},{1,0},{3,2},{5,4},{7,6},{8,9},{10,11},{12,... | collective-permute-start | bytes 245768 | tf_op jit(solution)/shard_map/ppermute | solution.py:740
  73.4 6.9 %collective-permute-start.16 = (f32[80,256]{1,0:T(8,128)S(1)}, f32[80,256]{1,0:T(8,128)S(1)}, u32[]{:S(2)}, u32[]{:S(2)}) collective-permute-start(f32[80,256]{1,0:T(8,128)S(1)} %get-tuple-element.95), channel_id=1, source_target_pairs={{1,2},{3,4},{5,6},{2,1},{4,3},{6,5},{9,10},{11,12},{13,14},{10,9},... | collective-permute-start | bytes 245768 | tf_op jit(solution)/shard_map/ppermute | solution.py:740
  75.3 3.2 %collective-permute-start.18 = (f32[8,256]{1,0:T(8,128)S(1)}, f32[8,256]{1,0:T(8,128)S(1)}, u32[]{:S(2)}, u32[]{:S(2)}) collective-permute-start(f32[8,256]{1,0:T(8,128)S(1)} %slice_add_fusion), channel_id=1, source_target_pairs={{0,2},{1,3},{2,0},{3,1},{4,6},{5,7},{6,4},{7,5},{8,10},{9,11},{10,... | collective-permute-start | bytes 24584 | tf_op jit(solution)/shard_map/ppermute | solution.py:744
  78.5 3.6 %collective-permute-start.19 = (f32[8,256]{1,0:T(8,128)S(1)}, f32[8,256]{1,0:T(8,128)S(1)}, u32[]{:S(2)}, u32[]{:S(2)}) collective-permute-start(f32[8,256]{1,0:T(8,128)S(1)} %add.10), channel_id=1, source_target_pairs={{0,4},{1,5},{2,6},{3,7},{4,0},{5,1},{6,2},{7,3},{8,12},{9,13},{10,... | collective-permute-start | bytes 24584 | tf_op jit(solution)/shard_map/ppermute | solution.py:744
  82.2 7.9 %collective-permute-start.20 = (f32[2,16,256]{2,1,0:T(8,128)S(1)}, f32[2,16,256]{2,1,0:T(8,128)S(1)}, u32[]{:S(2)}, u32[]{:S(2)}) collective-permute-start(f32[2,16,256]{2,1,0:T(8,128)S(1)} %get-tuple-element.98), channel_id=1, source_target_pairs={{8,16},{16,8},{9,17},{17,9},{10,18},{18,10},{11,19},{19,11},{12,20... | collective-permute-start | bytes 98312 | tf_op jit(solution)/shard_map/ppermute | solution.py:740
  87.5 2.6 %collective-permute-start.21 = (f32[2,16,256]{2,1,0:T(8,128)S(1)}, f32[2,16,256]{2,1,0:T(8,128)S(1)}, u32[]{:S(2)}, u32[]{:S(2)}) collective-permute-start(f32[2,16,256]{2,1,0:T(8,128)S(1)} %get-tuple-element.99), channel_id=1, source_target_pairs={{0,8},{16,24},{8,0},{24,16},{1,9},{17,25},{9,1},{25,17},{2,10},{18... | collective-permute-start | bytes 98312 | tf_op jit(solution)/shard_map/ppermute | solution.py:740

commit v3 on v2

--- a/solution.py
+++ b/solution.py
@@ -153,18 +153,17 @@
 ):
     nx = conc.shape[0]
     copies = [pltpu.make_async_copy(owner, own_owner, sems.at[4]), pltpu.make_async_copy(block, own_block, sems.at[5])]
-    for i, (ref, at, to) in enumerate(((conc, 0, c_first), (conc, 24, c_last), (label, 0, l_first), (label, 24, l_last))):
-        copies.append(pltpu.make_async_copy(ref.at[:, pl.ds(at, 8), :], to, sems.at[i]))
+    for i, (ref, at, to) in enumerate(((conc, 0, c_first), (conc, 28, c_last), (label, 0, l_first), (label, 28, l_last))):
+        copies.append(pltpu.make_async_copy(ref.at[:, pl.ds(at, 4), :], to, sems.at[i]))
     for c in copies:
         c.start()
     for c in copies:
         c.wait()
     named = jnp.concatenate([own_owner[...], own_block[...], jnp.zeros((6, 256), jnp.int32)], axis=0).astype(F32)
-    for j in range(own_lists.shape[0]):
-        own_lists[j] = named
+    own_lists[...] = named
     for x in range(nx):
-        send_y(pay_a, pay_b, 7 * x, c_first[x, 0:4, :], c_last[x, 4:8, :])
-        send_y(pay_a, pay_b, 7 * x + 4, l_first[x, 0:3, :].astype(F32), l_last[x, 5:8, :].astype(F32))
+        send_y(pay_a, pay_b, 7 * x, c_first[x], c_last[x])
+        send_y(pay_a, pay_b, 7 * x + 4, l_first[x, 0:3, :].astype(F32), l_last[x, 1:4, :].astype(F32))
 
 
 def own_kernel(conc, label, phi, mid, coarse, pay_a, pay_b, pairs, pairs_2):
@@ -202,32 +201,49 @@
             send_x(pay_a, pay_b, 20 + 5 * k + t, plane(label, k, t, 4, 3), plane(label, nx - 3 + k, t, 4, 3))
 
 
-def second_pack_kernel(phi, mid, coarse, x_a, x_b, pay_a, pay_b):
+def corner_rows(n, reach):
+    counts = [min(HALO, k + reach) for k in range(HALO)]
+    counts = counts + [HALO] * n + counts[::-1]
+    return counts, [sum(counts[:i]) for i in range(len(counts))]
+
+
+def second_rows(nx):
+    phi, mid = (sum(corner_rows(n, reach)[0]) for n, reach in ((nx, 0), (nx // 2, 1)))
+    return phi, phi + mid, phi + mid + 64
+
+
+def second_pack_kernel(phi, mid, coarse, lists, x_a, x_b, pay_a, pay_b, token):
     nx = phi.shape[0]
-    half = nx // 2
-    for x in range(nx):
-        send_y(pay_a, pay_b, 4 * (HALO + x), phi[x, 0:4, :], phi[x, 28:32, :])
-    for k in range(HALO):
-        for t, at in ((0, slice(0, 4)), (3, slice(4, 8))):
-            after, before = x_sides(x_a, x_b, 4 * k + t)
-            if t == 0:
-                first_after, first_before = after[at], before[at]
-            else:
-                last_after, last_before = after[at], before[at]
-        send_y(pay_a, pay_b, 4 * k, first_before, last_before)
-        send_y(pay_a, pay_b, 4 * (HALO + nx + k), first_after, last_after)
-    base = 4 * (nx + 2 * HALO)
-    for x in range(half):
-        send_y(pay_a, pay_b, base + 4 * (HALO + x), mid[x, 0:4, :], mid[x, 12:16, :])
-    for k in range(HALO):
-        first_after, first_before = (v[0:4] for v in x_sides(x_a, x_b, 16 + 2 * k))
-        last_after, last_before = (v[4:8] for v in x_sides(x_a, x_b, 16 + 2 * k + 1))
-        send_y(pay_a, pay_b, base + 4 * k, first_before, last_before)
-        send_y(pay_a, pay_b, base + 4 * (HALO + half + k), first_after, last_after)
-    base += 4 * (half + 2 * HALO)
+    starts = second_rows(nx)
+
+    def put(own, n, reach, index, base):
+        counts, at = corner_rows(n, reach)
+        tiles = own.shape[1] // 8
+        for x in range(n):
+            send_y(pay_a, pay_b, base + at[HALO + x], own[x, 0:4, :], own[x, 8 * tiles - 4 : 8 * tiles, :])
+        for k in range(HALO):
+            first_after, first_before = x_sides(x_a, x_b, index + tiles * k)
+            last_after, last_before = x_sides(x_a, x_b, index + tiles * k + tiles - 1)
+            for x, first, last in ((k, first_before, last_before), (HALO + n + k, first_after, last_after)):
+                if counts[x]:
+                    send_y(pay_a, pay_b, base + at[x], first[0 : counts[x]], last[8 - counts[x] : 8])
+
+    put(phi, nx, 0, 0, 0)
+    put(mid, nx // 2, 1, 16, starts[0])
+    base = starts[1]
     for x in range(8):
         pay_a[base + 8 * x : base + 8 * x + 8, :] = coarse[x]
         pay_b[base + 8 * x : base + 8 * x + 8, :] = coarse[x]
+    base = starts[2]
+    pay_b[base : base + lists.shape[0], :] = lists[...]
+    token[...] = jnp.zeros(token.shape, F32)
+
+
+def second_halo(r_a, r_b, n, reach, x, base):
+    counts, at = corner_rows(n, reach)
+    if not counts[x]:
+        return jnp.zeros((8, 256), F32)
+    return halo_tile(*y_sides(r_a, r_b, base + at[x], counts[x]))
 
 
 def wide_rows(own, after_own, before_own, after, before):
@@ -283,42 +299,58 @@
     loop(0, nx, last)
 
 
-def flux_kernel(conc, label, phi, solid, lists, flux, pay_a, pay_b, marked):
+def flux_kernel(conc, label, phi, solid, flux, pay_a, pay_b):
     nx = conc.shape[0]
-    entries = lists.shape[0] * 256
-    owner = jnp.concatenate([lists[i, 0:1, :] for i in range(lists.shape[0])], axis=1)
-    block = jnp.concatenate([lists[i, 1:2, :] for i in range(lists.shape[0])], axis=1)
-    here = lax.axis_index("dev")
-    block = jnp.where(owner.astype(jnp.int32) == here, block.astype(jnp.int32), -1)
-    hit_row = (iota((32, entries), 0) == lax.shift_right_arithmetic(block, 6)).astype(jnp.bfloat16)
-    hit_column = (iota((LANES, entries), 0) == lax.rem(block, 64)).astype(jnp.bfloat16)
-    named = lax.dot_general(hit_row, hit_column, (((1,), (1,)), ((), ())), preferred_element_type=F32)
-    for i in range(32):
-        marked[i] = jnp.broadcast_to(named[i : i + 1, :], (8, LANES))
-    is_row = lax.div(iota((32, LANES), 1), 2) == iota((32, LANES), 0)
-    spread = (lax.rem(iota((LANES, 256), 0), 2) == lax.div(iota((LANES, 256), 1), LANES)).astype(jnp.bfloat16)
 
     def plane(i):
-        marks = jnp.where(is_row, jnp.concatenate([marked[i]] * 4, axis=0), 0.0).astype(jnp.bfloat16)
-        listed = jnp.dot(marks, spread, preferred_element_type=F32) > 0.5
         drive = 0.5 * (solid[i] - phi[i])
         logc = jnp.log(conc[i])
         value = jnp.exp(drive + 0.4 * logc) - jnp.exp(0.6 * logc - drive)
-        flux[i] = jnp.where(listed, pick(label[i], KINETIC_TABLE) * value, 0.0)
+        flux[i] = pick(label[i], KINETIC_TABLE) * value
 
     loop(0, nx, plane, 4)
     for x in range(nx):
         send_y(pay_a, pay_b, 3 * x, flux[x, 0:3, :], flux[x, 29:32, :])
 
 
-def store_kernel(conc, flux, conc_out, flux_out, token, sems):
-    copies = []
-    for i, (ref, to) in enumerate(((conc, conc_out), (flux, flux_out))):
-        for j in range(4):
-            rows = pl.ds(8 * j, 8)
-            copies.append(pltpu.make_async_copy(ref.at[rows], to.at[rows], sems.at[4 * i + j]))
-            copies[-1].start()
-    token[...] = jnp.zeros(token.shape, F32)
+def store_kernel(conc, flux_all, lists, far, conc_out, flux_out, flux, halo_mask, marked, sems):
+    nx = conc.shape[0]
+    copies = [pltpu.make_async_copy(conc, conc_out, sems.at[4])]
+    copies[0].start()
+    rows = lists.shape[0]
+    pieces = [lists[i : i + 1, :] for i in range(rows)] + [far[i : i + 1, :] for i in range(far.shape[0] - rows, far.shape[0])]
+    owner = jnp.concatenate(pieces[0::2], axis=1).astype(jnp.int32)
+    block = jnp.concatenate(pieces[1::2], axis=1).astype(jnp.int32)
+    entries = owner.shape[1]
+    hit_column = (iota((LANES, entries), 0) == lax.rem(block, 64)).astype(jnp.bfloat16)
+    at_row = lax.shift_right_arithmetic(block, 6)
+    here = lax.axis_index("dev")
+    for j in range(3):
+        mine = jnp.where(owner == here + j - 1, at_row, -1)
+        hit_row = (iota((nx, entries), 0) == mine).astype(jnp.bfloat16)
+        named = lax.dot_general(hit_row, hit_column, (((1,), (1,)), ((), ())), preferred_element_type=F32)
+        for i in range(nx):
+            marked[j, i] = jnp.broadcast_to(named[i : i + 1, :], (8, LANES))
+    is_row = lax.div(iota((32, LANES), 1), 2) == iota((32, LANES), 0)
+    row, pair = iota((8, LANES), 0), lax.div(iota((8, LANES), 1), 2)
+    is_after = (row < 3) & (pair == row)
+    is_before = (row >= 5) & (pair == row + 24)
+    spread = (lax.rem(iota((LANES, 256), 0), 2) == lax.div(iota((LANES, 256), 1), LANES)).astype(jnp.bfloat16)
+
+    def plane(i):
+        marks = jnp.where(is_row, jnp.concatenate([marked[1, i]] * 4, axis=0), 0.0)
+        beyond = jnp.where(is_after, marked[2, i], jnp.where(is_before, marked[0, i], 0.0))
+        marks = jnp.concatenate([marks, beyond], axis=0).astype(jnp.bfloat16)
+        listed = jnp.dot(marks, spread, preferred_element_type=F32) > 0.5
+        flux[i] = jnp.where(listed[0:32], flux_all[i], 0.0)
+        halo_mask[i] = jnp.where(listed[32:40], 1.0, 0.0)
+
+    for j in range(4):
+        part = nx // 4
+        loop(part * j, part * (j + 1), plane, 4)
+        rows = pl.ds(part * j, part)
+        copies.append(pltpu.make_async_copy(flux.at[rows], flux_out.at[rows], sems.at[j]))
+        copies[-1].start()
     for c in copies:
         c.wait()
 
@@ -343,7 +375,7 @@
     for i in range(nx):
         c = halo_tile(*y_sides(y_a, y_b, 7 * i, 4))
         lab = halo_tile(*y_sides(y_a, y_b, 7 * i + 4, 3))
-        put(HALO + i, low, c, lab, halo_tile(*y_sides(yy_a, yy_b, 4 * (HALO + i), 4)))
+        put(HALO + i, low, c, lab, second_halo(yy_a, yy_b, nx, 0, HALO + i, 0))
     for t in range(5):
         rows = slice(8 * t, 8 * t + 8)
         for k in range(HALO):
@@ -353,8 +385,8 @@
             if t < 4:
                 p_after, p_before = x_sides(xx_a, xx_b, 4 * k + t)
             else:
-                p_after = halo_tile(*y_sides(yy_a, yy_b, 4 * (HALO + nx + k), 4))
-                p_before = halo_tile(*y_sides(yy_a, yy_b, 4 * k, 4))
+                p_after = second_halo(yy_a, yy_b, nx, 0, HALO + nx + k, 0)
+                p_before = second_halo(yy_a, yy_b, nx, 0, k, 0)
             put(k, rows, c_before, l_before, p_before)
             put(HALO + nx + k, rows, c_after, l_after, p_after)
 
@@ -366,20 +398,20 @@
     loop(1, nx + 2 * HALO - 1, sweep)
 
 
-def flux_pack_x_kernel(flux, r_a, r_b, token, token_2, pay_a, pay_b):
+def flux_pack_x_kernel(flux, r_a, r_b, mask, token, pay_a, pay_b):
     nx = flux.shape[0]
 
     def tile(x, t):
         if t < 4:
             return flux[x, 8 * t : 8 * t + 8, :]
-        return halo_tile(*y_sides(r_a, r_b, 3 * x, 3))
+        return mask[x] * halo_tile(*y_sides(r_a, r_b, 3 * x, 3))
 
     for k in range(3):
         for t in range(5):
             send_x(pay_a, pay_b, 5 * k + t, tile(k, t), tile(nx - 3 + k, t))
 
 
-def potential_inner_kernel(flux, y_a, y_b, weight, scale, share, start, after_two, source, first, source_mid, pairs):
+def potential_inner_kernel(flux, mask, y_a, y_b, weight, scale, share, start, after_two, source, first, source_mid, pairs):
     nx = flux.shape[0]
 
     def put(x, rows, f):
@@ -392,7 +424,7 @@
 
     loop(0, nx, own)
     for i in range(nx):
-        put(HALO + i, slice(32, 40), halo_tile(*y_sides(y_a, y_b, 3 * i, 3)))
+        put(HALO + i, slice(32, 40), mask[i] * halo_tile(*y_sides(y_a, y_b, 3 * i, 3)))
 
     def around(values, x):
         v = values[x]
@@ -475,7 +507,7 @@
     after_two, source, weight, coarse, conduct, pay_a, pay_b, part, scale, mid_conduct, pairs, pairs_2,
 ):
     n = source_own.shape[0]
-    base = 4 * (2 * n + 2 * HALO)
+    base = second_rows(2 * n)[0]
 
     def put(x, rows, b, k):
         factor = OMEGA / (MASS + 3.0 * k)
@@ -485,7 +517,7 @@
         mid_conduct[x, rows, :] = k
 
     def far(x):
-        return halo_tile(*y_sides(yy_a, yy_b, base + 4 * x, 4))
+        return second_halo(yy_a, yy_b, n, 1, x, base)
 
     for i in range(n):
         put(HALO + i, slice(0, 16), source_own[i], conduct_own[i])
@@ -525,10 +557,7 @@
         send_y(pay_a, pay_b, 9 * i, value[1:9], jnp.concatenate([value[11:12], value[0:7]], axis=0))
         send_y(pay_a, pay_b, 9 * i + 8, k[8:9], k[11:12])
         total += rho[i] * value[0:8]
-    sums = jnp.concatenate([total[:, :LANES] + total[:, LANES:], load[...]], axis=1)
-    pay_a[72:80, :] = sums
-    pay_b[72:80, :] = sums
-    part[...] = sums
+    part[...] = jnp.concatenate([total[:, :LANES] + total[:, LANES:], load[...]], axis=1)
 
 
 COARSE_W = 0.0625
@@ -565,6 +594,10 @@
     load[...] = total[:, :LANES] + total[:, LANES:]
 
 
+def late_kernel(pay, token, out):
+    out[...] = pay[...]
+
+
 def coarse_kernel(own, conduct, far_a, far_b, r_a, r_b, error, source, weight, one, two):
     base = far_a.shape[0] - 64
     for x in range(8):
@@ -755,10 +788,10 @@
 
     pay_a, pay_b, own_lists = call(
         first_pack_kernel,
-        [shaped(7 * nx, 256)] * 2 + [shaped(peers, 8, 256)],
+        [shaped(7 * nx, 256)] * 2 + [shaped(8, 256)],
         [conc_old, phase_label, iface_owner.reshape(1, -1), iface_block],
-        [vmem(nx, 8, 256)] * 2
-        + [pltpu.VMEM((nx, 8, 256), jnp.int32)] * 2
+        [vmem(nx, HALO, 256)] * 2
+        + [pltpu.VMEM((nx, HALO, 256), jnp.int32)] * 2
         + [pltpu.VMEM((1, 256), jnp.int32)] * 2
         + [pltpu.SemaphoreType.DMA((6,))],
         in_specs=[FAR] * 4,
@@ -774,22 +807,26 @@
         name="own",
     )
     xx_a, xx_b = swap(pay_a, pay_b, "grp")
-    lists = lax.all_to_all(own_lists, "dev", split_axis=0, concat_axis=0, tiled=True)
+    lists = own_lists[0:2]
+    distance = peers // 2
+    while distance > 1:
+        lists = jnp.concatenate([lists, exchange(lists, distance)], axis=0)
+        distance //= 2
+    far_rows = second_rows(nx)[2]
+    pay_a, pay_b, sent = call(
+        second_pack_kernel,
+        [shaped(far_rows, 256), shaped(far_rows + peers, 256), token_shape],
+        [phi_old, conduct_mid, conduct_coarse, lists, xx_a, xx_b],
+        name="second_pack",
+    )
+    yy_a, yy_b = swap(pay_a, pay_b, "dev")
     pay_a, pay_b = call(
         first_pack_x_kernel,
         [shaped(35, 8, 256)] * 2,
-        [conc_old, phase_label, y_a, y_b, lists],
+        [conc_old, phase_label, y_a, y_b, sent],
         name="first_pack_x",
     )
     x_a, x_b = swap(pay_a, pay_b, "grp")
-    far_rows = 4 * (nx + half + 4 * HALO) + 64
-    pay_a, pay_b = call(
-        second_pack_kernel,
-        [shaped(far_rows, 256)] * 2,
-        [phi_old, conduct_mid, conduct_coarse, xx_a, xx_b],
-        name="second_pack",
-    )
-    yy_a, yy_b = swap(pay_a, pay_b, "dev")
 
     (conc_new,) = call(
         sweeps_kernel,
@@ -798,20 +835,19 @@
         [vmem(*ext)] * 4,
         name="sweeps",
     )
-    flux_own, pay_a, pay_b = call(
+    flux_all, pay_a, pay_b = call(
         flux_kernel,
         [shaped(nx, nx, 256), shaped(3 * nx, 256), shaped(3 * nx, 256)],
-        [conc_new, phase_label, phi_old, solid_pot, lists],
-        [vmem(32, 8, LANES)],
+        [conc_new, phase_label, phi_old, solid_pot],
         name="flux",
     )
     f_a, f_b = swap(pay_a, pay_b, "dev")
-    concentration, flux, stored = call(
+    concentration, flux, flux_own, halo_mask = call(
         store_kernel,
-        [shaped(nx, nx, 256), shaped(nx, nx, 256), token_shape],
-        [conc_new, flux_own],
-        [pltpu.SemaphoreType.DMA((8,))],
-        out_specs=[FAR, FAR, WHOLE],
+        [shaped(nx, nx, 256), shaped(nx, nx, 256), shaped(nx, nx, 256), shaped(nx, 8, 256)],
+        [conc_new, flux_all, lists, yy_b],
+        [vmem(3, nx, 8, LANES), pltpu.SemaphoreType.DMA((5,))],
+        out_specs=[FAR, FAR, WHOLE, WHOLE],
         name="store",
     )
     weight, scale, share, start, made = call(
@@ -822,13 +858,13 @@
         name="ready",
     )
     pay_a, pay_b = call(
-        flux_pack_x_kernel, [shaped(15, 8, 256)] * 2, [flux_own, f_a, f_b, stored, made], name="flux_pack_x"
+        flux_pack_x_kernel, [shaped(15, 8, 256)] * 2, [flux_own, f_a, f_b, halo_mask, made], name="flux_pack_x"
     )
     fx_a, fx_b = swap(pay_a, pay_b, "grp")
     fine_two, fine_source, fine_first, inner_mid = call(
         potential_inner_kernel,
         [shaped(*ext)] * 3 + [shaped(half, half, 256)],
-        [flux_own, f_a, f_b, weight, scale, share, start],
+        [flux_own, halo_mask, f_a, f_b, weight, scale, share, start],
         [vmem(half, 2, nx, LANES)],
         name="potential_inner",
     )
@@ -856,11 +892,17 @@
     mid_two, mid_source, mid_weight, source_coarse, wide_coarse, pay_a, pay_b, sums = call(
         mid_kernel,
         [shaped(*ext_mid)] * 3
-        + [shaped(quarter, 12, 256), shaped(quarter, 12, 256), shaped(80, 256), shaped(80, 256), shaped(8, 256)],
+        + [shaped(quarter, 12, 256), shaped(quarter, 12, 256), shaped(72, 256), shaped(72, 256), shaped(8, 256)],
         [source_mid, conduct_mid, yy_a, yy_b, xx_a, xx_b, m_a, m_b, mx_a, mx_b, rho, load],
         [vmem(*ext_mid)] * 2 + [vmem(8, 2, half + 2 * HALO, LANES)] * 2,
         name="middle",
     )
+    early = sums = sums + exchange(sums, 1)
+    distance = 2
+    while distance < peers:
+        sums = sums + exchange(sums, distance)
+        distance *= 2
+    (pay_b,) = call(late_kernel, [shaped(72, 256)], [pay_b, early], name="late")
     c_a, c_b = swap(pay_a, pay_b, "dev")
     (error,) = call(
         coarse_kernel,
@@ -869,11 +911,6 @@
         [vmem(*wide)] * 4,
         name="coarse",
     )
-    sums = sums + c_b[72:80]
-    distance = 2
-    while distance < peers:
-        sums = sums + exchange(sums, distance)
-        distance *= 2
     error, pay_a, pay_b = call(
         shift_kernel, [shaped(8, 16, 256), shaped(2, 16, 256), shaped(2, 16, 256)], [error, sums], name="shift"
     )

time: 92.6 us -> 92.3 us (level)
  blocking collectives: 10.1 us -> 0 us
  starting transfers between devices: 41.4 us -> 49.8 us
    all_to_all x1 -> x0, blocking collectives: 10.1 us -> none  [body(): lax.all_to_all(own_lists, 'dev', split_axis=0, concat_axis=0, tiled=True)]
    ppermute x2 -> x5, waiting for transfers between devices: 2.33 us -> 8.02 us  [exchange(): lax.ppermute(value, 'dev', [(i, i ^ distance) for i in range(lax.axis_siz...]
    ppermute x10, waiting for transfers between devices: 6.67 us -> 2.04 us  [swap(): lax.ppermute(pay_b, axis, both_ways(pairs_b))]
    ppermute x10, starting transfers between devices: 21.7 us -> 25.4 us  [swap(): lax.ppermute(pay_a, axis, both_ways(pairs_a))]
    ppermute x2 -> x5, starting transfers between devices: 3.22 us -> 6.47 us  [exchange(): lax.ppermute(value, 'dev', [(i, i ^ distance) for i in range(lax.axis_siz...]
    ppermute x10, starting transfers between devices: 16.5 us -> 17.9 us  [swap(): lax.ppermute(pay_b, axis, both_ways(pairs_b))]
    ppermute x10, waiting for transfers between devices: 5.76 us -> 4.82 us  [swap(): lax.ppermute(pay_a, axis, both_ways(pairs_a))]
    pallas_call x18 -> x19, Pallas kernels: 23.3 us -> 23.8 us  [call(): pl.pallas_call(kernel, out_shape=tuple(outs), in_specs=in_specs or [WHOLE...]
  transfers between devices with their start and end apart: 22 -> 25, of which waited for: 8 -> 10; matrix products, arithmetic and copies ran while one was open for 0% -> 0% of each run, Pallas kernels for 19% -> 19%
where the time goes in v3:
time: 92.3 us; the launch traced here: 91.4 us
  starting transfers between devices  49.8 us (54%)
  Pallas kernels  23.8 us (26%)
  waiting for transfers between devices  14.9 us (16%)
  local copies, waits for them, and re-layouts  1.94 us (2%)
  between operations  1 us (1%)
    ppermute x10, starting transfers between devices, swap(): lax.ppermute(pay_a, axis, both_ways(pairs_a))  25.4 us
    pallas_call x19, Pallas kernels, call(): pl.pallas_call(kernel, out_shape=tuple(outs), in_specs=in_specs or [WHOLE...  23.8 us
    ppermute x10, starting transfers between devices, swap(): lax.ppermute(pay_b, axis, both_ways(pairs_b))  17.9 us
    ppermute x5, waiting for transfers between devices, exchange(): lax.ppermute(value, 'dev', [(i, i ^ distance) for i in range(lax.axis_siz...  8.02 us
    ppermute x5, starting transfers between devices, exchange(): lax.ppermute(value, 'dev', [(i, i ^ distance) for i in range(lax.axis_siz...  6.47 us
    ppermute x10, waiting for transfers between devices, swap(): lax.ppermute(pay_a, axis, both_ways(pairs_a))  4.82 us
    ppermute x10, waiting for transfers between devices, swap(): lax.ppermute(pay_b, axis, both_ways(pairs_b))  2.04 us
  transfers between devices with their start and end apart: 25, of which 10 were waited for; matrix products, arithmetic and copies ran while one was open for 0% of the time, Pallas kernels for 19%

profile of v3, /device:TPU:1, one launch (start us, length us, event | category | flops | bytes accessed | tf_op | source)
XLA Modules:
  0.0 91.4 jit_solution(15859203366195841202)
XLA Ops:
  0.7 2.2 %first_pack.1 = (f32[224,256]{1,0:T(8,128)}, f32[224,256]{1,0:T(8,128)}, f32[8,256]{1,0:T(8,128)}) custom-call(f32[32,32,256]{2,1,0:T(8,128)} %conc.9, s32[32,32,256]{2,1,0:T(8,128)} %label.11, s32[1,256]{1,0:T(1,128)} %bitcast.1, s32[1,256]{1,0:T(1,128)} %block.1), custom_call_target="tpu_custom_call" | custom-call | flops 1000000 | bytes 2566144 | tf_op jit(solution)/shard_map/first_pack/pallas_call | solution.py:34
  3.5 3.1 %collective-permute-start.2 = (f32[2,256]{1,0:T(2,128)S(1)}, f32[2,256]{1,0:T(2,128)S(1)}, u32[]{:S(2)}, u32[]{:S(2)}) collective-permute-start(f32[2,256]{1,0:T(2,128)S(1)} %slice.3), channel_id=1, source_target_pairs={{0,4},{1,5},{2,6},{3,7},{4,0},{5,1},{6,2},{7,3},{8,12},{9,13},{10,... | collective-permute-start | bytes 6152 | tf_op jit(solution)/shard_map/ppermute | solution.py:777
  7.3 3.8 %collective-permute-start.1 = (f32[224,256]{1,0:T(8,128)}, f32[224,256]{1,0:T(8,128)S(1)}, u32[]{:S(2)}, u32[]{:S(2)}) collective-permute-start(f32[224,256]{1,0:T(8,128)} %get-tuple-element.60), channel_id=1, source_target_pairs={{0,1},{2,3},{4,5},{6,7},{1,0},{3,2},{5,4},{7,6},{8,9},{10,11},{12,... | collective-permute-start | bytes 688136 | tf_op jit(solution)/shard_map/ppermute | solution.py:773
  11.1 1.2 %copy-done.2 = f32[32,32,256]{2,1,0:T(8,128)S(1)} copy-done((f32[32,32,256]{2,1,0:T(8,128)S(1)}, f32[32,32,256]{2,1,0:T(8,128)}, u32[]{:S(2)}) %copy-start.2) | copy-done | bytes 1048600
  12.7 4.5 %collective-permute-start.4 = (f32[24,8,256]{2,1,0:T(8,128)S(1)}, f32[24,8,256]{2,1,0:T(8,128)S(1)}, u32[]{:S(2)}, u32[]{:S(2)}) collective-permute-start(f32[24,8,256]{2,1,0:T(8,128)S(1)} %get-tuple-element.64), channel_id=1, source_target_pairs={{8,16},{16,8},{9,17},{17,9},{10,18},{18,10},{11,19},{19,11},{12,20... | collective-permute-start | bytes 589832 | tf_op jit(solution)/shard_map/ppermute | solution.py:773
  17.4 2.4 %collective-permute-done.3 = f32[4,256]{1,0:T(4,128)S(1)} collective-permute-done((f32[4,256]{1,0:T(4,128)S(1)}, f32[4,256]{1,0:T(4,128)S(1)}, u32[]{:S(2)}, u32[]{:S(2)}) %collective-permute-start.3) | collective-permute-done | bytes 4128 | tf_op jit(solution)/shard_map/ppermute | solution.py:777
  21.3 3.5 %collective-permute-start.6 = (f32[35,8,256]{2,1,0:T(8,128)S(1)}, f32[35,8,256]{2,1,0:T(8,128)S(1)}, u32[]{:S(2)}, u32[]{:S(2)}) collective-permute-start(f32[35,8,256]{2,1,0:T(8,128)S(1)} %get-tuple-element.67), channel_id=1, source_target_pairs={{8,16},{16,8},{9,17},{17,9},{10,18},{18,10},{11,19},{19,11},{12,20... | collective-permute-start | bytes 860168 | tf_op jit(solution)/shard_map/ppermute | solution.py:773
  24.9 2.2 %collective-permute-start.8 = (f32[296,256]{1,0:T(8,128)S(1)}, f32[296,256]{1,0:T(8,128)S(1)}, u32[]{:S(2)}, u32[]{:S(2)}) collective-permute-start(f32[296,256]{1,0:T(8,128)S(1)} %get-tuple-element.70), channel_id=1, source_target_pairs={{0,1},{2,3},{4,5},{6,7},{1,0},{3,2},{5,4},{7,6},{8,9},{10,11},{12,... | collective-permute-start | bytes 909320 | tf_op jit(solution)/shard_map/ppermute | solution.py:773
  27.1 0.8 collective-permute-start.11
  27.9 1.7 %collective-permute-done.6.x_a = f32[35,8,256]{2,1,0:T(8,128)S(1)} collective-permute-done((f32[35,8,256]{2,1,0:T(8,128)S(1)}, f32[35,8,256]{2,1,0:T(8,128)S(1)}, u32[]{:S(2)}, u32[]{:S(2)}) %collective-permute-start.6) | collective-permute-done | bytes 286752 | tf_op jit(solution)/shard_map/ppermute | solution.py:773
  29.5 4.9 %sweeps.1.conc = f32[32,32,256]{2,1,0:T(8,128)S(1)} custom-call(f32[32,32,256]{2,1,0:T(8,128)S(1)} %copy-done.1, s32[32,32,256]{2,1,0:T(8,128)S(1)} %copy-done, f32[224,256]{1,0:T(8,128)S(1)} %collective-permute-done.r_a.y_a, f32[224,256]{1,0:T(8,128)S(1)} %collective-permute-done.1.r_b.y_b, f32[35,8,256]{2,1,0:T(8,128)S(1)} %collective-permute-done.6.x_a, ...), custom_call_target="tpu_custom_call" | custom-call | flops 1000000 | bytes 4177920 | tf_op jit(solution)/shard_map/sweeps/pallas_call | solution.py:34
  35.3 0.8 collective-permute-start.9
  36.1 4.7 %collective-permute-start.10 = (f32[96,256]{1,0:T(8,128)S(1)}, f32[96,256]{1,0:T(8,128)S(1)}, u32[]{:S(2)}, u32[]{:S(2)}) collective-permute-start(f32[96,256]{1,0:T(8,128)S(1)} %get-tuple-element.75), channel_id=1, source_target_pairs={{0,1},{2,3},{4,5},{6,7},{1,0},{3,2},{5,4},{7,6},{8,9},{10,11},{12,... | collective-permute-start | bytes 294920 | tf_op jit(solution)/shard_map/ppermute | solution.py:773
  40.7 2.7 %store.1 = (f32[32,32,256]{2,1,0:T(8,128)}, f32[32,32,256]{2,1,0:T(8,128)}, f32[32,32,256]{2,1,0:T(8,128)S(1)}, f32[32,8,256]{2,1,0:T(8,128)S(1)}) custom-call(f32[32,32,256]{2,1,0:T(8,128)S(1)} %sweeps.1.conc, f32[32,32,256]{2,1,0:T(8,128)S(1)} %get-tuple-element.69.flux_all, f32[8,256]{1,0:T(8,128)S(1)} %pad_maximum_fusion.lists, ...), custom_call_target="tpu_custom_call" | custom-call | flops 1000000 | bytes 5816320 | tf_op jit(solution)/shard_map/store/pallas_call | solution.py:34
  43.5 2.2 %ready.1 = (f32[40,40,256]{2,1,0:T(8,128)S(1)}, f32[40,40,256]{2,1,0:T(8,128)S(1)}, f32[40,40,256]{2,1,0:T(8,128)S(1)}, f32[40,40,256]{2,1,0:T(8,128)S(1)}, f32[8,128]{1,0:T(8,128)S(1)}) custom-call(f32[32,32,256]{2,1,0:T(8,128)S(1)} %copy-done.1, s32[32,32,256]{2,1,0:T(8,128)S(1)} %copy-done, f32[32,32,256]{2,1,0:T(8,128)S(1)} %copy-done.3, ...), custom_call_target="tpu_custom_call" | custom-call | flops 1000000 | bytes 11726848 | tf_op jit(solution)/shard_map/ready/pallas_call | solution.py:34
  45.7 3.8 %collective-permute-start.12 = (f32[15,8,256]{2,1,0:T(8,128)S(1)}, f32[15,8,256]{2,1,0:T(8,128)S(1)}, u32[]{:S(2)}, u32[]{:S(2)}) collective-permute-start(f32[15,8,256]{2,1,0:T(8,128)S(1)} %get-tuple-element.79), channel_id=1, source_target_pairs={{8,16},{16,8},{9,17},{17,9},{10,18},{18,10},{11,19},{19,11},{12,20... | collective-permute-start | bytes 368648 | tf_op jit(solution)/shard_map/ppermute | solution.py:773
  49.6 2.2 %potential_inner.1 = (f32[40,40,256]{2,1,0:T(8,128)S(1)}, f32[40,40,256]{2,1,0:T(8,128)S(1)}, f32[40,40,256]{2,1,0:T(8,128)S(1)}, f32[16,16,256]{2,1,0:T(8,128)S(1)}) custom-call(f32[32,32,256]{2,1,0:T(8,128)S(1)} %get-tuple-element.73.flux, f32[32,8,256]{2,1,0:T(8,128)S(1)} %get-tuple-element.76.mask, f32[96,256]{1,0:T(8,128)S(1)} %collective-permute-done.9.r_a.y_a, ...), custom_call_target="tpu_custom_call" | custom-call | flops 1000000 | bytes 13238272 | tf_op jit(solution)/shard_map/potential_inner/pallas_call | solution.py:34
  53.2 4.5 %collective-permute-start.15 = (f32[64,256]{1,0:T(8,128)S(1)}, f32[64,256]{1,0:T(8,128)S(1)}, u32[]{:S(2)}, u32[]{:S(2)}) collective-permute-start(f32[64,256]{1,0:T(8,128)S(1)} %get-tuple-element.91), channel_id=1, source_target_pairs={{0,1},{2,3},{4,5},{6,7},{1,0},{3,2},{5,4},{7,6},{8,9},{10,11},{12,... | collective-permute-start | bytes 196616 | tf_op jit(solution)/shard_map/ppermute | solution.py:773
  57.7 1.2 %coarse_ready.1 = (f32[8,8,256]{2,1,0:T(8,128)S(1)}, f32[8,128]{1,0:T(8,128)S(1)}, f32[8,128]{1,0:T(8,128)S(1)}) custom-call(f32[8,8,256]{2,1,0:T(8,128)S(1)} %get-tuple-element.62.coarse.own, f32[288,256]{1,0:T(8,128)S(1)} %collective-permute-done.11.yy_a.r_a.far_a, f32[296,256]{1,0:T(8,128)S(1)} %collective-permute-done.8.far.yy_b.r_b.far_b), custom_call_target="tpu_custom_call" | custom-call | flops 1000000 | bytes 737280 | tf_op jit(solution)/shard_map/coarse_ready/pallas_call | solution.py:34
  58.9 1.6 %collective-permute-done.15.r_b.y_b = f32[64,256]{1,0:T(8,128)S(1)} collective-permute-done((f32[64,256]{1,0:T(8,128)S(1)}, f32[64,256]{1,0:T(8,128)S(1)}, u32[]{:S(2)}, u32[]{:S(2)}) %collective-permute-start.15) | collective-permute-done | bytes 65568 | tf_op jit(solution)/shard_map/ppermute | solution.py:773
  60.5 3.7 %collective-permute-start.16 = (f32[12,8,256]{2,1,0:T(8,128)S(1)}, f32[12,8,256]{2,1,0:T(8,128)S(1)}, u32[]{:S(2)}, u32[]{:S(2)}) collective-permute-start(f32[12,8,256]{2,1,0:T(8,128)S(1)} %get-tuple-element.93), channel_id=1, source_target_pairs={{8,16},{16,8},{9,17},{17,9},{10,18},{18,10},{11,19},{19,11},{12,20... | collective-permute-start | bytes 294920 | tf_op jit(solution)/shard_map/ppermute | solution.py:773
  64.3 2.2 %collective-permute-done.16.x_a = f32[12,8,256]{2,1,0:T(8,128)S(1)} collective-permute-done((f32[12,8,256]{2,1,0:T(8,128)S(1)}, f32[12,8,256]{2,1,0:T(8,128)S(1)}, u32[]{:S(2)}, u32[]{:S(2)}) %collective-permute-start.16) | collective-permute-done | bytes 98336 | tf_op jit(solution)/shard_map/ppermute | solution.py:773
  66.5 1.1 %middle.1 = (f32[24,24,256]{2,1,0:T(8,128)S(1)}, f32[24,24,256]{2,1,0:T(8,128)S(1)}, f32[24,24,256]{2,1,0:T(8,128)S(1)}, f32[8,12,256]{2,1,0:T(8,128)S(1)}, f32[...) custom-call(f32[16,16,256]{2,1,0:T(8,128)S(1)} %get-tuple-element.89.field.source_o, ...), custom_call_target="tpu_custom_call" | custom-call | flops 1000000 | bytes 4034560 | tf_op jit(solution)/shard_map/middle/pallas_call | solution.py:34
  67.6 2.2 %collective-permute-start.19 = (f32[8,256]{1,0:T(8,128)S(1)}, f32[8,256]{1,0:T(8,128)S(1)}, u32[]{:S(2)}, u32[]{:S(2)}) collective-permute-start(f32[8,256]{1,0:T(8,128)S(1)} %get-tuple-element.101), channel_id=1, source_target_pairs={{0,1},{1,0},{2,3},{3,2},{4,5},{5,4},{6,7},{7,6},{8,9},{9,8},{10,11... | collective-permute-start | bytes 24584 | tf_op jit(solution)/shard_map/ppermute | solution.py:777
  70.8 2.5 %collective-permute-start.20 = (f32[72,256]{1,0:T(8,128)S(1)}, f32[72,256]{1,0:T(8,128)S(1)}, u32[]{:S(2)}, u32[]{:S(2)}) collective-permute-start(f32[72,256]{1,0:T(8,128)S(1)} %late.1), channel_id=1, source_target_pairs={{0,1},{2,3},{4,5},{6,7},{1,0},{3,2},{5,4},{7,6},{8,9},{10,11},{12,... | collective-permute-start | bytes 221192 | tf_op jit(solution)/shard_map/ppermute | solution.py:773
  73.4 2.8 %collective-permute-done.21 = f32[8,256]{1,0:T(8,128)S(1)} collective-permute-done((f32[8,256]{1,0:T(8,128)S(1)}, f32[8,256]{1,0:T(8,128)S(1)}, u32[]{:S(2)}, u32[]{:S(2)}) %collective-permute-start.21) | collective-permute-done | bytes 8224 | tf_op jit(solution)/shard_map/ppermute | solution.py:777
  76.1 1.0 %collective-permute-start.22 = (f32[8,256]{1,0:T(8,128)S(1)}, f32[8,256]{1,0:T(8,128)S(1)}, u32[]{:S(2)}, u32[]{:S(2)}) collective-permute-start(f32[8,256]{1,0:T(8,128)S(1)} %add.10), channel_id=1, source_target_pairs={{0,4},{1,5},{2,6},{3,7},{4,0},{5,1},{6,2},{7,3},{8,12},{9,13},{10,... | collective-permute-start | bytes 24584 | tf_op jit(solution)/shard_map/ppermute | solution.py:777
  77.1 2.4 %collective-permute-done.22 = f32[8,256]{1,0:T(8,128)S(1)} collective-permute-done((f32[8,256]{1,0:T(8,128)S(1)}, f32[8,256]{1,0:T(8,128)S(1)}, u32[]{:S(2)}, u32[]{:S(2)}) %collective-permute-start.22) | collective-permute-done | bytes 8224 | tf_op jit(solution)/shard_map/ppermute | solution.py:777
  79.6 1.2 %coarse.1.error = f32[8,16,256]{2,1,0:T(8,128)S(1)} custom-call(f32[8,12,256]{2,1,0:T(8,128)S(1)} %get-tuple-element.97.own, f32[8,12,256]{2,1,0:T(8,128)S(1)} %get-tuple-element.98.conduct, f32[288,256]{1,0:T(8,128)S(1)} %collective-permute-done.11.yy_a.r_a.far_a, f32[296,256]{1,0:T(8,128)S(1)} %collective-permute-done.8.far.yy_b.r_b.far_b, ...), custom_call_target="tpu_custom_call" | custom-call | flops 1000000 | bytes 1073152 | tf_op jit(solution)/shard_map/coarse/pallas_call | solution.py:34
  80.9 6.3 %collective-permute-start.23 = (f32[2,16,256]{2,1,0:T(8,128)S(1)}, f32[2,16,256]{2,1,0:T(8,128)S(1)}, u32[]{:S(2)}, u32[]{:S(2)}) collective-permute-start(f32[2,16,256]{2,1,0:T(8,128)S(1)} %get-tuple-element.102), channel_id=1, source_target_pairs={{8,16},{16,8},{9,17},{17,9},{10,18},{18,10},{11,19},{19,11},{12,20... | collective-permute-start | bytes 98312 | tf_op jit(solution)/shard_map/ppermute | solution.py:773
  87.2 2.5 %finish_inner.1 = (f32[32,32,256]{2,1,0:T(8,128)}, f32[24,24,256]{2,1,0:T(8,128)S(1)}, f32[24,24,256]{2,1,0:T(8,128)S(1)}, f32[40,40,256]{2,1,0:T(8,128)S(1)}, f32[40,40,256]{2,1,0:T(8,128)S(1)}) custom-call(f32[8,16,256]{2,1,0:T(8,128)S(1)} %get-tuple-element.109.error, f32[24,24,256]{2,1,0:T(8,128)S(1)} %get-tuple-element.104.mid_two, ...), custom_call_target="tpu_custom_call" | custom-call | flops 1000000 | bytes 12320768 | tf_op jit(solution)/shard_map/finish_inner/pallas_call | solution.py:34
  89.8 1.7 %finish_edge.1 = f32[32,32,256]{2,1,0:T(8,128)} custom-call(f32[2,16,256]{2,1,0:T(8,128)S(1)} %collective-permute-done.23.x_a, f32[2,16,256]{2,1,0:T(8,128)S(1)} %collective-permute-done.24.x_b, f32[24,24,256]{2,1,0:T(8,128)S(1)} %get-tuple-element.104.mid_two, f32[24,24,256]{2,1,0:T(8,128)S(1)} %get-tuple-element.105.mid_source, ...), custom_call_target="tpu_custom_call", output_to_operand_aliasing={{}: (14, {})} | custom-call | flops 1000000 | bytes 14614528 | tf_op jit(solution)/shard_map/finish_edge/pallas_call | solution.py:34
  (53 shorter events, 7.0 us)
Async XLA Ops:
  0.6 10.5 %copy-start.1 = (f32[32,32,256]{2,1,0:T(8,128)S(1)}, f32[32,32,256]{2,1,0:T(8,128)}, u32[]{:S(2)}) copy-start(f32[32,32,256]{2,1,0:T(8,128)} %conc.9) | copy-start | bytes 3145732
  0.6 10.5 %copy-start = (s32[32,32,256]{2,1,0:T(8,128)S(1)}, s32[32,32,256]{2,1,0:T(8,128)}, u32[]{:S(2)}) copy-start(s32[32,32,256]{2,1,0:T(8,128)} %label.11) | copy-start | bytes 3145732
  3.5 13.8 %collective-permute-start.2 = (f32[2,256]{1,0:T(2,128)S(1)}, f32[2,256]{1,0:T(2,128)S(1)}, u32[]{:S(2)}, u32[]{:S(2)}) collective-permute-start(f32[2,256]{1,0:T(2,128)S(1)} %slice.3), channel_id=1, source_target_pairs={{0,4},{1,5},{2,6},{3,7},{4,0},{5,1},{6,2},{7,3},{8,12},{9,13},{10,... | collective-permute-start | bytes 6152 | tf_op jit(solution)/shard_map/ppermute | solution.py:777
  6.7 14.1 %collective-permute-start = (f32[224,256]{1,0:T(8,128)}, f32[224,256]{1,0:T(8,128)S(1)}, u32[]{:S(2)}, u32[]{:S(2)}) collective-permute-start(f32[224,256]{1,0:T(8,128)} %get-tuple-element.59), channel_id=1, source_target_pairs={{1,2},{3,4},{5,6},{2,1},{4,3},{6,5},{9,10},{11,12},{13,14},{10,9},... | collective-permute-start | bytes 688136 | tf_op jit(solution)/shard_map/ppermute | solution.py:773
  7.3 13.9 %collective-permute-start.1 = (f32[224,256]{1,0:T(8,128)}, f32[224,256]{1,0:T(8,128)S(1)}, u32[]{:S(2)}, u32[]{:S(2)}) collective-permute-start(f32[224,256]{1,0:T(8,128)} %get-tuple-element.60), channel_id=1, source_target_pairs={{0,1},{2,3},{4,5},{6,7},{1,0},{3,2},{5,4},{7,6},{8,9},{10,11},{12,... | collective-permute-start | bytes 688136 | tf_op jit(solution)/shard_map/ppermute | solution.py:773
  11.1 1.2 %copy-start.2 = (f32[32,32,256]{2,1,0:T(8,128)S(1)}, f32[32,32,256]{2,1,0:T(8,128)}, u32[]{:S(2)}) copy-start(f32[32,32,256]{2,1,0:T(8,128)} %phi.7) | copy-start | bytes 3145732
  12.7 7.9 %collective-permute-start.4 = (f32[24,8,256]{2,1,0:T(8,128)S(1)}, f32[24,8,256]{2,1,0:T(8,128)S(1)}, u32[]{:S(2)}, u32[]{:S(2)}) collective-permute-start(f32[24,8,256]{2,1,0:T(8,128)S(1)} %get-tuple-element.64), channel_id=1, source_target_pairs={{8,16},{16,8},{9,17},{17,9},{10,18},{18,10},{11,19},{19,11},{12,20... | collective-permute-start | bytes 589832 | tf_op jit(solution)/shard_map/ppermute | solution.py:773
  17.2 3.3 %collective-permute-start.5 = (f32[24,8,256]{2,1,0:T(8,128)S(1)}, f32[24,8,256]{2,1,0:T(8,128)S(1)}, u32[]{:S(2)}, u32[]{:S(2)}) collective-permute-start(f32[24,8,256]{2,1,0:T(8,128)S(1)} %get-tuple-element.65), channel_id=1, source_target_pairs={{0,8},{16,24},{8,0},{24,16},{1,9},{17,25},{9,1},{25,17},{2,10},{18... | collective-permute-start | bytes 589832 | tf_op jit(solution)/shard_map/ppermute | solution.py:773
  17.3 2.5 %collective-permute-start.3 = (f32[4,256]{1,0:T(4,128)S(1)}, f32[4,256]{1,0:T(4,128)S(1)}, u32[]{:S(2)}, u32[]{:S(2)}) collective-permute-start(f32[4,256]{1,0:T(4,128)S(1)} %pad_maximum_fusion.1), channel_id=1, source_target_pairs={{0,2},{1,3},{2,0},{3,1},{4,6},{5,7},{6,4},{7,5},{8,10},{9,11},{10,... | collective-permute-start | bytes 12296 | tf_op jit(solution)/shard_map/ppermute | solution.py:777
  21.3 8.2 %collective-permute-start.6 = (f32[35,8,256]{2,1,0:T(8,128)S(1)}, f32[35,8,256]{2,1,0:T(8,128)S(1)}, u32[]{:S(2)}, u32[]{:S(2)}) collective-permute-start(f32[35,8,256]{2,1,0:T(8,128)S(1)} %get-tuple-element.67), channel_id=1, source_target_pairs={{8,16},{16,8},{9,17},{17,9},{10,18},{18,10},{11,19},{19,11},{12,20... | collective-permute-start | bytes 860168 | tf_op jit(solution)/shard_map/ppermute | solution.py:773
  24.8 4.7 %collective-permute-start.7 = (f32[35,8,256]{2,1,0:T(8,128)S(1)}, f32[35,8,256]{2,1,0:T(8,128)S(1)}, u32[]{:S(2)}, u32[]{:S(2)}) collective-permute-start(f32[35,8,256]{2,1,0:T(8,128)S(1)} %get-tuple-element.68), channel_id=1, source_target_pairs={{0,8},{16,24},{8,0},{24,16},{1,9},{17,25},{9,1},{25,17},{2,10},{18... | collective-permute-start | bytes 860168 | tf_op jit(solution)/shard_map/ppermute | solution.py:773
  24.9 15.8 %collective-permute-start.8 = (f32[296,256]{1,0:T(8,128)S(1)}, f32[296,256]{1,0:T(8,128)S(1)}, u32[]{:S(2)}, u32[]{:S(2)}) collective-permute-start(f32[296,256]{1,0:T(8,128)S(1)} %get-tuple-element.70), channel_id=1, source_target_pairs={{0,1},{2,3},{4,5},{6,7},{1,0},{3,2},{5,4},{7,6},{8,9},{10,11},{12,... | collective-permute-start | bytes 909320 | tf_op jit(solution)/shard_map/ppermute | solution.py:773
  27.1 7.4 %copy-start.4 = (f32[32,32,256]{2,1,0:T(8,128)S(1)}, f32[32,32,256]{2,1,0:T(8,128)}, u32[]{:S(2)}) copy-start(f32[32,32,256]{2,1,0:T(8,128)} %solid.1) | copy-start | bytes 3145732
  27.1 16.4 %collective-permute-start.11 = (f32[288,256]{1,0:T(8,128)S(1)}, f32[288,256]{1,0:T(8,128)S(1)}, u32[]{:S(2)}, u32[]{:S(2)}) collective-permute-start(f32[288,256]{1,0:T(8,128)S(1)} %get-tuple-element.77), channel_id=1, source_target_pairs={{1,2},{3,4},{5,6},{2,1},{4,3},{6,5},{9,10},{11,12},{13,14},{10,9},... | collective-permute-start | bytes 884744 | tf_op jit(solution)/shard_map/ppermute | solution.py:773
  35.2 8.3 %copy-start.3 = (f32[32,32,256]{2,1,0:T(8,128)S(1)}, f32[32,32,256]{2,1,0:T(8,128)}, u32[]{:S(2)}) copy-start(f32[32,32,256]{2,1,0:T(8,128)} %phi.7) | copy-start | bytes 3145732
  35.3 10.4 %collective-permute-start.9 = (f32[96,256]{1,0:T(8,128)S(1)}, f32[96,256]{1,0:T(8,128)S(1)}, u32[]{:S(2)}, u32[]{:S(2)}) collective-permute-start(f32[96,256]{1,0:T(8,128)S(1)} %get-tuple-element.74), channel_id=1, source_target_pairs={{1,2},{3,4},{5,6},{2,1},{4,3},{6,5},{9,10},{11,12},{13,14},{10,9},... | collective-permute-start | bytes 294920 | tf_op jit(solution)/shard_map/ppermute | solution.py:773
  36.1 9.6 %collective-permute-start.10 = (f32[96,256]{1,0:T(8,128)S(1)}, f32[96,256]{1,0:T(8,128)S(1)}, u32[]{:S(2)}, u32[]{:S(2)}) collective-permute-start(f32[96,256]{1,0:T(8,128)S(1)} %get-tuple-element.75), channel_id=1, source_target_pairs={{0,1},{2,3},{4,5},{6,7},{1,0},{3,2},{5,4},{7,6},{8,9},{10,11},{12,... | collective-permute-start | bytes 294920 | tf_op jit(solution)/shard_map/ppermute | solution.py:773
  45.7 6.3 %collective-permute-start.12 = (f32[15,8,256]{2,1,0:T(8,128)S(1)}, f32[15,8,256]{2,1,0:T(8,128)S(1)}, u32[]{:S(2)}, u32[]{:S(2)}) collective-permute-start(f32[15,8,256]{2,1,0:T(8,128)S(1)} %get-tuple-element.79), channel_id=1, source_target_pairs={{8,16},{16,8},{9,17},{17,9},{10,18},{18,10},{11,19},{19,11},{12,20... | collective-permute-start | bytes 368648 | tf_op jit(solution)/shard_map/ppermute | solution.py:773
  49.5 2.6 %collective-permute-start.13 = (f32[15,8,256]{2,1,0:T(8,128)S(1)}, f32[15,8,256]{2,1,0:T(8,128)S(1)}, u32[]{:S(2)}, u32[]{:S(2)}) collective-permute-start(f32[15,8,256]{2,1,0:T(8,128)S(1)} %get-tuple-element.80), channel_id=1, source_target_pairs={{0,8},{16,24},{8,0},{24,16},{1,9},{17,25},{9,1},{25,17},{2,10},{18... | collective-permute-start | bytes 368648 | tf_op jit(solution)/shard_map/ppermute | solution.py:773
  52.5 6.4 %collective-permute-start.14 = (f32[64,256]{1,0:T(8,128)S(1)}, f32[64,256]{1,0:T(8,128)S(1)}, u32[]{:S(2)}, u32[]{:S(2)}) collective-permute-start(f32[64,256]{1,0:T(8,128)S(1)} %get-tuple-element.90), channel_id=1, source_target_pairs={{1,2},{3,4},{5,6},{2,1},{4,3},{6,5},{9,10},{11,12},{13,14},{10,9},... | collective-permute-start | bytes 196616 | tf_op jit(solution)/shard_map/ppermute | solution.py:773
  53.2 7.3 %collective-permute-start.15 = (f32[64,256]{1,0:T(8,128)S(1)}, f32[64,256]{1,0:T(8,128)S(1)}, u32[]{:S(2)}, u32[]{:S(2)}) collective-permute-start(f32[64,256]{1,0:T(8,128)S(1)} %get-tuple-element.91), channel_id=1, source_target_pairs={{0,1},{2,3},{4,5},{6,7},{1,0},{3,2},{5,4},{7,6},{8,9},{10,11},{12,... | collective-permute-start | bytes 196616 | tf_op jit(solution)/shard_map/ppermute | solution.py:773
  60.5 6.0 %collective-permute-start.16 = (f32[12,8,256]{2,1,0:T(8,128)S(1)}, f32[12,8,256]{2,1,0:T(8,128)S(1)}, u32[]{:S(2)}, u32[]{:S(2)}) collective-permute-start(f32[12,8,256]{2,1,0:T(8,128)S(1)} %get-tuple-element.93), channel_id=1, source_target_pairs={{8,16},{16,8},{9,17},{17,9},{10,18},{18,10},{11,19},{19,11},{12,20... | collective-permute-start | bytes 294920 | tf_op jit(solution)/shard_map/ppermute | solution.py:773
  64.2 2.3 %collective-permute-start.17 = (f32[12,8,256]{2,1,0:T(8,128)S(1)}, f32[12,8,256]{2,1,0:T(8,128)S(1)}, u32[]{:S(2)}, u32[]{:S(2)}) collective-permute-start(f32[12,8,256]{2,1,0:T(8,128)S(1)} %get-tuple-element.94), channel_id=1, source_target_pairs={{0,8},{16,24},{8,0},{24,16},{1,9},{17,25},{9,1},{25,17},{2,10},{18... | collective-permute-start | bytes 294920 | tf_op jit(solution)/shard_map/ppermute | solution.py:773
  67.6 3.3 %collective-permute-start.19 = (f32[8,256]{1,0:T(8,128)S(1)}, f32[8,256]{1,0:T(8,128)S(1)}, u32[]{:S(2)}, u32[]{:S(2)}) collective-permute-start(f32[8,256]{1,0:T(8,128)S(1)} %get-tuple-element.101), channel_id=1, source_target_pairs={{0,1},{1,0},{2,3},{3,2},{4,5},{5,4},{6,7},{7,6},{8,9},{9,8},{10,11... | collective-permute-start | bytes 24584 | tf_op jit(solution)/shard_map/ppermute | solution.py:777
  69.8 9.8 %collective-permute-start.18 = (f32[72,256]{1,0:T(8,128)S(1)}, f32[72,256]{1,0:T(8,128)S(1)}, u32[]{:S(2)}, u32[]{:S(2)}) collective-permute-start(f32[72,256]{1,0:T(8,128)S(1)} %get-tuple-element.99), channel_id=1, source_target_pairs={{1,2},{3,4},{5,6},{2,1},{4,3},{6,5},{9,10},{11,12},{13,14},{10,9},... | collective-permute-start | bytes 221192 | tf_op jit(solution)/shard_map/ppermute | solution.py:773
  70.8 8.7 %collective-permute-start.20 = (f32[72,256]{1,0:T(8,128)S(1)}, f32[72,256]{1,0:T(8,128)S(1)}, u32[]{:S(2)}, u32[]{:S(2)}) collective-permute-start(f32[72,256]{1,0:T(8,128)S(1)} %late.1), channel_id=1, source_target_pairs={{0,1},{2,3},{4,5},{6,7},{1,0},{3,2},{5,4},{7,6},{8,9},{10,11},{12,... | collective-permute-start | bytes 221192 | tf_op jit(solution)/shard_map/ppermute | solution.py:773
  73.3 2.8 %collective-permute-start.21 = (f32[8,256]{1,0:T(8,128)S(1)}, f32[8,256]{1,0:T(8,128)S(1)}, u32[]{:S(2)}, u32[]{:S(2)}) collective-permute-start(f32[8,256]{1,0:T(8,128)S(1)} %add.9.token), channel_id=1, source_target_pairs={{0,2},{1,3},{2,0},{3,1},{4,6},{5,7},{6,4},{7,5},{8,10},{9,11},{10,... | collective-permute-start | bytes 24584 | tf_op jit(solution)/shard_map/ppermute | solution.py:777
  76.1 3.4 %collective-permute-start.22 = (f32[8,256]{1,0:T(8,128)S(1)}, f32[8,256]{1,0:T(8,128)S(1)}, u32[]{:S(2)}, u32[]{:S(2)}) collective-permute-start(f32[8,256]{1,0:T(8,128)S(1)} %add.10), channel_id=1, source_target_pairs={{0,4},{1,5},{2,6},{3,7},{4,0},{5,1},{6,2},{7,3},{8,12},{9,13},{10,... | collective-permute-start | bytes 24584 | tf_op jit(solution)/shard_map/ppermute | solution.py:777
  80.9 8.9 %collective-permute-start.23 = (f32[2,16,256]{2,1,0:T(8,128)S(1)}, f32[2,16,256]{2,1,0:T(8,128)S(1)}, u32[]{:S(2)}, u32[]{:S(2)}) collective-permute-start(f32[2,16,256]{2,1,0:T(8,128)S(1)} %get-tuple-element.102), channel_id=1, source_target_pairs={{8,16},{16,8},{9,17},{17,9},{10,18},{18,10},{11,19},{19,11},{12,20... | collective-permute-start | bytes 98312 | tf_op jit(solution)/shard_map/ppermute | solution.py:773
  87.1 2.6 %collective-permute-start.24 = (f32[2,16,256]{2,1,0:T(8,128)S(1)}, f32[2,16,256]{2,1,0:T(8,128)S(1)}, u32[]{:S(2)}, u32[]{:S(2)}) collective-permute-start(f32[2,16,256]{2,1,0:T(8,128)S(1)} %get-tuple-element.103), channel_id=1, source_target_pairs={{0,8},{16,24},{8,0},{24,16},{1,9},{17,25},{9,1},{25,17},{2,10},{18... | collective-permute-start | bytes 98312 | tf_op jit(solution)/shard_map/ppermute | solution.py:773

commit v4 on v3

--- a/solution.py
+++ b/solution.py
@@ -10,6 +10,8 @@
 MASS = 0.05
 OMEGA = 0.8
 DIFFUSION_TABLE = (1.5, 0.1, 0.4)
+RATIO_TABLE = tuple(d / (1.0 + 6.0 * d) for d in DIFFUSION_TABLE)
+INVERSE_TABLE = tuple(1.0 / (1.0 + 6.0 * d) for d in DIFFUSION_TABLE)
 CONDUCT_TABLE = (1.0, 0.3, 0.6)
 KINETIC_TABLE = (0.2, 1.0, 0.5)
 SWEEPS = 4
@@ -166,9 +168,16 @@
         send_y(pay_a, pay_b, 7 * x + 4, l_first[x, 0:3, :].astype(F32), l_last[x, 1:4, :].astype(F32))
 
 
-def own_kernel(conc, label, phi, mid, coarse, pay_a, pay_b, pairs, pairs_2):
+def own_kernel(conc, label, phi, named, mid, coarse, pay_a, pay_b, lists, gain, base, pairs, pairs_2):
     nx = conc.shape[0]
     half = nx // 2
+    lists[...] = named[0:2, :]
+
+    def coefficients(i):
+        gain[i] = pick(label[i], RATIO_TABLE)
+        base[i] = conc[i] * pick(label[i], INVERSE_TABLE)
+
+    loop(0, nx, coefficients, 4)
 
     def coarsen(i):
         total = conc[2 * i] * pick(label[2 * i], CONDUCT_TABLE) + conc[2 * i + 1] * pick(label[2 * i + 1], CONDUCT_TABLE)
@@ -212,7 +221,7 @@
     return phi, phi + mid, phi + mid + 64
 
 
-def second_pack_kernel(phi, mid, coarse, lists, x_a, x_b, pay_a, pay_b, token):
+def second_pack_kernel(phi, mid, coarse, lists, x_a, x_b, pay_a, pay_b):
     nx = phi.shape[0]
     starts = second_rows(nx)
 
@@ -236,7 +245,6 @@
         pay_b[base + 8 * x : base + 8 * x + 8, :] = coarse[x]
     base = starts[2]
     pay_b[base : base + lists.shape[0], :] = lists[...]
-    token[...] = jnp.zeros(token.shape, F32)
 
 
 def second_halo(r_a, r_b, n, reach, x, base):
@@ -251,24 +259,26 @@
     return jnp.concatenate([own, after_own, after, gap, before, before_own], axis=0)
 
 
-def sweeps_kernel(conc, label, y_a, y_b, x_a, x_b, out, one, two, gain, base):
+def sweeps_kernel(conc, label, gain_own, base_own, y_a, y_b, x_a, x_b, out, one, two, gain_far, base_far, gain_x, base_x):
     nx = conc.shape[0]
-    ratio = tuple(d / (1.0 + 6.0 * d) for d in DIFFUSION_TABLE)
-    inverse = tuple(1.0 / (1.0 + 6.0 * d) for d in DIFFUSION_TABLE)
-
-    def put(x, rows, c, lab):
-        one[x, rows, :] = c
-        gain[x, rows, :] = jnp.where(c > 0.0, pick(lab, ratio), 0.0)
-        base[x, rows, :] = c * pick(lab, inverse)
 
     def own(i):
-        put(HALO + i, slice(0, 32), conc[i], label[i])
+        one[HALO + i, 0:32, :] = conc[i]
 
     loop(0, nx, own)
     for i in range(nx):
         c = halo_tile(*y_sides(y_a, y_b, 7 * i, 4))
         lab = halo_tile(*y_sides(y_a, y_b, 7 * i + 4, 3))
-        put(HALO + i, slice(32, 40), c, lab)
+        one[HALO + i, 32:40, :] = c
+        gain_far[i] = jnp.where(c > 0.0, pick(lab, RATIO_TABLE), 0.0)
+        base_far[i] = c * pick(lab, INVERSE_TABLE)
+
+    def put(x, rows, c, lab):
+        one[x, rows, :] = c
+        at = x if x < HALO else x - nx
+        gain_x[at, rows, :] = jnp.where(c > 0.0, pick(lab, RATIO_TABLE), 0.0)
+        base_x[at, rows, :] = c * pick(lab, INVERSE_TABLE)
+
     for t in range(5):
         rows = slice(8 * t, 8 * t + 8)
         for k in range(HALO):
@@ -278,23 +288,28 @@
             put(k, rows, c_before, l_before)
             put(HALO + nx + k, rows, c_after, l_after)
 
-    def stencil(old, x):
+    def neighbours(old, x):
         mid = old[x]
-        return base[x] + gain[x] * ((old[x - 1] + old[x + 1]) + (along_y(mid) + along_z(mid)))
+        return (old[x - 1] + old[x + 1]) + (along_y(mid) + along_z(mid))
 
     fields = (one, two)
     for s in range(1, SWEEPS):
         old, new = fields[(s - 1) % 2], fields[s % 2]
 
-        def sweep(x, old=old, new=new):
-            new[x] = stencil(old, x)
-
-        loop(s, nx + 2 * HALO - s, sweep)
+        def sweep(i, old=old, new=new):
+            gain = jnp.concatenate([gain_own[i], gain_far[i]], axis=0)
+            base = jnp.concatenate([base_own[i], base_far[i]], axis=0)
+            new[HALO + i] = base + gain * neighbours(old, HALO + i)
+
+        loop(0, nx, sweep)
+        for k in range(s, HALO):
+            for x, at in ((k, k), (2 * HALO + nx - 1 - k, 2 * HALO - 1 - k)):
+                new[x] = base_x[at] + gain_x[at] * neighbours(old, x)
 
     old = fields[(SWEEPS - 1) % 2]
 
     def last(i):
-        out[i] = stencil(old, HALO + i)[0:32, :]
+        out[i] = base_own[i] + gain_own[i] * neighbours(old, HALO + i)[0:32, :]
 
     loop(0, nx, last)
 
@@ -313,10 +328,8 @@
         send_y(pay_a, pay_b, 3 * x, flux[x, 0:3, :], flux[x, 29:32, :])
 
 
-def store_kernel(conc, flux_all, lists, far, conc_out, flux_out, flux, halo_mask, marked, sems):
-    nx = conc.shape[0]
-    copies = [pltpu.make_async_copy(conc, conc_out, sems.at[4])]
-    copies[0].start()
+def mask_kernel(flux_all, lists, far, flux, halo_mask, marked):
+    nx = flux_all.shape[0]
     rows = lists.shape[0]
     pieces = [lists[i : i + 1, :] for i in range(rows)] + [far[i : i + 1, :] for i in range(far.shape[0] - rows, far.shape[0])]
     owner = jnp.concatenate(pieces[0::2], axis=1).astype(jnp.int32)
@@ -345,17 +358,22 @@
         flux[i] = jnp.where(listed[0:32], flux_all[i], 0.0)
         halo_mask[i] = jnp.where(listed[32:40], 1.0, 0.0)
 
-    for j in range(4):
-        part = nx // 4
-        loop(part * j, part * (j + 1), plane, 4)
-        rows = pl.ds(part * j, part)
-        copies.append(pltpu.make_async_copy(flux.at[rows], flux_out.at[rows], sems.at[j]))
-        copies[-1].start()
+    loop(0, nx, plane, 4)
+
+
+def store_kernel(conc, flux, conc_out, flux_out, token, sems):
+    copies = []
+    for i, (ref, to) in enumerate(((conc, conc_out), (flux, flux_out))):
+        for j in range(4):
+            rows = pl.ds(8 * j, 8)
+            copies.append(pltpu.make_async_copy(ref.at[rows], to.at[rows], sems.at[4 * i + j]))
+            copies[-1].start()
+    token[...] = jnp.zeros(token.shape, F32)
     for c in copies:
         c.wait()
 
 
-def ready_kernel(conc, label, phi, y_a, y_b, x_a, x_b, yy_a, yy_b, xx_a, xx_b, weight, scale, share, start, token, field):
+def ready_kernel(conc, label, phi, y_a, y_b, x_a, x_b, yy_a, yy_b, xx_a, xx_b, weight, scale, field, token):
     nx = conc.shape[0]
     token[...] = jnp.zeros(token.shape, F32)
 
@@ -364,7 +382,6 @@
         factor = OMEGA / (MASS + 6.0 * conduct)
         weight[x, rows, :] = conduct * factor
         scale[x, rows, :] = factor
-        share[x, rows, :] = MASS * p * factor
         field[x, rows, :] = p
 
     def own(i):
@@ -390,13 +407,6 @@
             put(k, rows, c_before, l_before, p_before)
             put(HALO + nx + k, rows, c_after, l_after, p_after)
 
-    def sweep(x):
-        p = field[x]
-        around = (field[x - 1] + field[x + 1]) + (along_y(p) + along_z(p))
-        start[x] = 0.2 * p + share[x] + weight[x] * around
-
-    loop(1, nx + 2 * HALO - 1, sweep)
-
 
 def flux_pack_x_kernel(flux, r_a, r_b, mask, token, pay_a, pay_b):
     nx = flux.shape[0]
@@ -411,20 +421,24 @@
             send_x(pay_a, pay_b, 5 * k + t, tile(k, t), tile(nx - 3 + k, t))
 
 
-def potential_inner_kernel(flux, mask, y_a, y_b, weight, scale, share, start, after_two, source, first, source_mid, pairs):
+def first_sweep(field, weight, scale, x, rows, flux):
+    p = field[x]
+    near = (field[x - 1] + field[x + 1]) + (along_y(p) + along_z(p))
+    b = scale[x, rows, :] * (MASS * p[rows, :] + flux)
+    return b, 0.2 * p[rows, :] + weight[x, rows, :] * near[rows, :] + b
+
+
+def potential_inner_kernel(flux, mask, y_a, y_b, weight, scale, field, after_two, source, first, source_mid, far, pairs):
     nx = flux.shape[0]
-
-    def put(x, rows, f):
-        part = scale[x, rows, :] * f
-        source[x, rows, :] = share[x, rows, :] + part
-        first[x, rows, :] = start[x, rows, :] + part
+    for i in range(nx):
+        far[i] = mask[i] * halo_tile(*y_sides(y_a, y_b, 3 * i, 3))
 
     def own(i):
-        put(HALO + i, slice(0, 32), flux[i])
+        x = HALO + i
+        f = jnp.concatenate([flux[i], far[i]], axis=0)
+        source[x], first[x] = first_sweep(field, weight, scale, x, slice(0, 40), f)
 
     loop(0, nx, own)
-    for i in range(nx):
-        put(HALO + i, slice(32, 40), mask[i] * halo_tile(*y_sides(y_a, y_b, 3 * i, 3)))
 
     def around(values, x):
         v = values[x]
@@ -448,7 +462,7 @@
 
 
 def potential_edge_kernel(
-    x_a, x_b, weight, scale, share, start, inner_two, inner_source, inner_first, inner_mid,
+    x_a, x_b, weight, scale, field, inner_two, inner_source, inner_first, inner_mid,
     edge_two, edge_source, source_mid, pay_a, pay_b, first, pairs,
 ):
     half = source_mid.shape[0]
@@ -457,11 +471,8 @@
         base = 8 * side + HALO - face
         for k in range(3):
             x = face - 3 + k if side == 0 else face + k
-            for t in range(5):
-                rows = slice(8 * t, 8 * t + 8)
-                part = scale[x, rows, :] * x_sides(x_a, x_b, 5 * k + t)[1 - side]
-                edge_source[base + x, rows, :] = share[x, rows, :] + part
-                first[base + x, rows, :] = start[x, rows, :] + part
+            f = jnp.concatenate([x_sides(x_a, x_b, 5 * k + t)[1 - side] for t in range(5)], axis=0)
+            edge_source[base + x], first[base + x] = first_sweep(field, weight, scale, x, slice(0, 40), f)
 
         def first_of(x, base=base):
             return inner_first[x] if HALO <= x < HALO + nx else first[base + x]
@@ -489,7 +500,7 @@
         send_y(pay_a, pay_b, 4 * x, source_mid[x, 0:4, :], source_mid[x, 12:16, :])
 
 
-def mid_pack_x_kernel(field, r_a, r_b, token, pay_a, pay_b):
+def mid_pack_x_kernel(field, r_a, r_b, token, token_2, pay_a, pay_b):
     n = field.shape[0]
 
     def tile(x, t):
@@ -557,7 +568,9 @@
         send_y(pay_a, pay_b, 9 * i, value[1:9], jnp.concatenate([value[11:12], value[0:7]], axis=0))
         send_y(pay_a, pay_b, 9 * i + 8, k[8:9], k[11:12])
         total += rho[i] * value[0:8]
-    part[...] = jnp.concatenate([total[:, :LANES] + total[:, LANES:], load[...]], axis=1)
+    sums = jnp.concatenate([total[:, :LANES] + total[:, LANES:], load[...]], axis=1)
+    pay_b[72:80, :] = sums
+    part[...] = sums
 
 
 COARSE_W = 0.0625
@@ -594,10 +607,6 @@
     load[...] = total[:, :LANES] + total[:, LANES:]
 
 
-def late_kernel(pay, token, out):
-    out[...] = pay[...]
-
-
 def coarse_kernel(own, conduct, far_a, far_b, r_a, r_b, error, source, weight, one, two):
     base = far_a.shape[0] - 64
     for x in range(8):
@@ -799,31 +808,31 @@
         name="first_pack",
     )
     y_a, y_b = swap(pay_a, pay_b, "dev")
-    conduct_mid, conduct_coarse, pay_a, pay_b = call(
+    conduct_mid, conduct_coarse, pay_a, pay_b, lists, gain, base = call(
         own_kernel,
-        [shaped(half, half, 256), shaped(quarter, quarter, 256), shaped(24, 8, 256), shaped(24, 8, 256)],
-        [conc_old, phase_label, phi_old],
+        [shaped(half, half, 256), shaped(quarter, quarter, 256), shaped(24, 8, 256), shaped(24, 8, 256)]
+        + [shaped(2, 256), shaped(nx, nx, 256), shaped(nx, nx, 256)],
+        [conc_old, phase_label, phi_old, own_lists],
         [vmem(half, 2, nx, LANES), vmem(quarter, 2, half, LANES)],
         name="own",
     )
     xx_a, xx_b = swap(pay_a, pay_b, "grp")
-    lists = own_lists[0:2]
     distance = peers // 2
     while distance > 1:
         lists = jnp.concatenate([lists, exchange(lists, distance)], axis=0)
         distance //= 2
     far_rows = second_rows(nx)[2]
-    pay_a, pay_b, sent = call(
+    far_pay = call(
         second_pack_kernel,
-        [shaped(far_rows, 256), shaped(far_rows + peers, 256), token_shape],
+        [shaped(far_rows, 256), shaped(far_rows + peers, 256)],
         [phi_old, conduct_mid, conduct_coarse, lists, xx_a, xx_b],
         name="second_pack",
     )
-    yy_a, yy_b = swap(pay_a, pay_b, "dev")
+    yy_a, yy_b = swap(*far_pay, "dev")
     pay_a, pay_b = call(
         first_pack_x_kernel,
         [shaped(35, 8, 256)] * 2,
-        [conc_old, phase_label, y_a, y_b, sent],
+        [conc_old, phase_label, y_a, y_b, conduct_coarse],
         name="first_pack_x",
     )
     x_a, x_b = swap(pay_a, pay_b, "grp")
@@ -831,8 +840,8 @@
     (conc_new,) = call(
         sweeps_kernel,
         [shaped(nx, nx, 256)],
-        [conc_old, phase_label, y_a, y_b, x_a, x_b],
-        [vmem(*ext)] * 4,
+        [conc_old, phase_label, gain, base, y_a, y_b, x_a, x_b],
+        [vmem(*ext)] * 2 + [vmem(nx, 8, 256)] * 2 + [vmem(2 * HALO, nx + 2 * HALO, 256)] * 2,
         name="sweeps",
     )
     flux_all, pay_a, pay_b = call(
@@ -842,19 +851,17 @@
         name="flux",
     )
     f_a, f_b = swap(pay_a, pay_b, "dev")
-    concentration, flux, flux_own, halo_mask = call(
-        store_kernel,
-        [shaped(nx, nx, 256), shaped(nx, nx, 256), shaped(nx, nx, 256), shaped(nx, 8, 256)],
-        [conc_new, flux_all, lists, yy_b],
-        [vmem(3, nx, 8, LANES), pltpu.SemaphoreType.DMA((5,))],
-        out_specs=[FAR, FAR, WHOLE, WHOLE],
-        name="store",
-    )
-    weight, scale, share, start, made = call(
+    flux_own, halo_mask = call(
+        mask_kernel,
+        [shaped(nx, nx, 256), shaped(nx, 8, 256)],
+        [flux_all, lists, yy_b],
+        [vmem(3, nx, 8, LANES)],
+        name="mask",
+    )
+    weight, scale, field, made = call(
         ready_kernel,
-        [shaped(*ext)] * 4 + [token_shape],
+        [shaped(*ext)] * 3 + [token_shape],
         [conc_old, phase_label, phi_old, y_a, y_b, x_a, x_b, yy_a, yy_b, xx_a, xx_b],
-        [vmem(*ext)],
         name="ready",
     )
     pay_a, pay_b = call(
@@ -864,19 +871,27 @@
     fine_two, fine_source, fine_first, inner_mid = call(
         potential_inner_kernel,
         [shaped(*ext)] * 3 + [shaped(half, half, 256)],
-        [flux_own, halo_mask, f_a, f_b, weight, scale, share, start],
-        [vmem(half, 2, nx, LANES)],
+        [flux_own, halo_mask, f_a, f_b, weight, scale, field],
+        [vmem(nx, 8, 256), vmem(half, 2, nx, LANES)],
         name="potential_inner",
     )
     edge = (16, nx + 2 * HALO, 256)
     edge_two, edge_source, source_mid, pay_a, pay_b = call(
         potential_edge_kernel,
         [shaped(*edge), shaped(*edge), shaped(half, half, 256), shaped(4 * half, 256), shaped(4 * half, 256)],
-        [fx_a, fx_b, weight, scale, share, start, fine_two, fine_source, fine_first, inner_mid],
+        [fx_a, fx_b, weight, scale, field, fine_two, fine_source, fine_first, inner_mid],
         [vmem(*edge), vmem(2, 2, nx, LANES)],
         name="potential_edge",
     )
     m_a, m_b = swap(pay_a, pay_b, "dev")
+    concentration, flux, stored = call(
+        store_kernel,
+        [shaped(nx, nx, 256), shaped(nx, nx, 256), token_shape],
+        [conc_new, flux_own],
+        [pltpu.SemaphoreType.DMA((8,))],
+        out_specs=[FAR, FAR, WHOLE],
+        name="store",
+    )
     wide = (quarter, 32, 256)
     rho, load, made = call(
         coarse_ready_kernel,
@@ -886,24 +901,23 @@
         name="coarse_ready",
     )
     pay_a, pay_b = call(
-        mid_pack_x_kernel, [shaped(3 * HALO, 8, 256)] * 2, [source_mid, m_a, m_b, made], name="mid_pack_x"
+        mid_pack_x_kernel, [shaped(3 * HALO, 8, 256)] * 2, [source_mid, m_a, m_b, made, stored], name="mid_pack_x"
     )
     mx_a, mx_b = swap(pay_a, pay_b, "grp")
     mid_two, mid_source, mid_weight, source_coarse, wide_coarse, pay_a, pay_b, sums = call(
         mid_kernel,
         [shaped(*ext_mid)] * 3
-        + [shaped(quarter, 12, 256), shaped(quarter, 12, 256), shaped(72, 256), shaped(72, 256), shaped(8, 256)],
+        + [shaped(quarter, 12, 256), shaped(quarter, 12, 256), shaped(72, 256), shaped(80, 256), shaped(8, 256)],
         [source_mid, conduct_mid, yy_a, yy_b, xx_a, xx_b, m_a, m_b, mx_a, mx_b, rho, load],
         [vmem(*ext_mid)] * 2 + [vmem(8, 2, half + 2 * HALO, LANES)] * 2,
         name="middle",
     )
-    early = sums = sums + exchange(sums, 1)
+    c_a, c_b = swap(pay_a, pay_b, "dev")
+    sums = sums + c_b[72:80]
     distance = 2
     while distance < peers:
         sums = sums + exchange(sums, distance)
         distance *= 2
-    (pay_b,) = call(late_kernel, [shaped(72, 256)], [pay_b, early], name="late")
-    c_a, c_b = swap(pay_a, pay_b, "dev")
     (error,) = call(
         coarse_kernel,
         [shaped(8, 16, 256)],

time: 92.3 us -> 86 us (0.932)
  waiting for transfers between devices: 14.9 us -> 10.1 us
  starting transfers between devices: 49.8 us -> 47.8 us
    ppermute x5 -> x4, waiting for transfers between devices: 8.02 us -> 1.73 us  [exchange(): lax.ppermute(value, 'dev', [(i, i ^ distance) for i in range(lax.axis_siz...]
    ppermute x10, starting transfers between devices: 25.4 us -> 22.2 us  [swap(): lax.ppermute(pay_a, axis, both_ways(pairs_a))]
    ppermute x10, waiting for transfers between devices: 2.04 us -> 3.28 us  [swap(): lax.ppermute(pay_b, axis, both_ways(pairs_b))]
    unnamed x10 -> x12, local copies, waits for them, and re-layouts: 1.24 us -> 1.94 us
    ppermute x5 -> x4, starting transfers between devices: 6.47 us -> 6.78 us  [exchange(): lax.ppermute(value, 'dev', [(i, i ^ distance) for i in range(lax.axis_siz...]
  transfers between devices with their start and end apart: 25 -> 24, of which waited for: 10 -> 8; matrix products, arithmetic and copies ran while one was open for 0% -> 0% of each run, Pallas kernels for 19% -> 22%
where the time goes in v4:
time: 86 us; the launch traced here: 85.1 us
  starting transfers between devices  47.8 us (56%)
  Pallas kernels  24.2 us (28%)
  waiting for transfers between devices  10.1 us (12%)
  local copies, waits for them, and re-layouts  1.94 us (2%)
  between operations  1.03 us (1%)
    pallas_call x19, Pallas kernels, call(): pl.pallas_call(kernel, out_shape=tuple(outs), in_specs=in_specs or [WHOLE...  24.2 us
    ppermute x10, starting transfers between devices, swap(): lax.ppermute(pay_a, axis, both_ways(pairs_a))  22.2 us
    ppermute x10, starting transfers between devices, swap(): lax.ppermute(pay_b, axis, both_ways(pairs_b))  18.8 us
    ppermute x4, starting transfers between devices, exchange(): lax.ppermute(value, 'dev', [(i, i ^ distance) for i in range(lax.axis_siz...  6.78 us
    ppermute x10, waiting for transfers between devices, swap(): lax.ppermute(pay_a, axis, both_ways(pairs_a))  5.07 us
    ppermute x10, waiting for transfers between devices, swap(): lax.ppermute(pay_b, axis, both_ways(pairs_b))  3.28 us
    unnamed x12, local copies, waits for them, and re-layouts  1.94 us
    ppermute x4, waiting for transfers between devices, exchange(): lax.ppermute(value, 'dev', [(i, i ^ distance) for i in range(lax.axis_siz...  1.73 us
  transfers between devices with their start and end apart: 24, of which 8 were waited for; matrix products, arithmetic and copies ran while one was open for 0% of the time, Pallas kernels for 22%

profile of v4, /device:TPU:1, one launch (start us, length us, event | category | flops | bytes accessed | tf_op | source)
XLA Modules:
  0.0 85.1 jit_solution(485361523165312208)
XLA Ops:
  0.7 2.2 %first_pack.1 = (f32[224,256]{1,0:T(8,128)}, f32[224,256]{1,0:T(8,128)}, f32[8,256]{1,0:T(8,128)}) custom-call(f32[32,32,256]{2,1,0:T(8,128)} %conc.9, s32[32,32,256]{2,1,0:T(8,128)} %label.11, s32[1,256]{1,0:T(1,128)} %bitcast.1, s32[1,256]{1,0:T(1,128)} %block.1), custom_call_target="tpu_custom_call" | custom-call | flops 1000000 | bytes 2566144 | tf_op jit(solution)/shard_map/first_pack/pallas_call | solution.py:36
  3.5 4.6 %collective-permute-start.1 = (f32[224,256]{1,0:T(8,128)}, f32[224,256]{1,0:T(8,128)S(1)}, u32[]{:S(2)}, u32[]{:S(2)}) collective-permute-start(f32[224,256]{1,0:T(8,128)} %get-tuple-element.65), channel_id=1, source_target_pairs={{0,1},{2,3},{4,5},{6,7},{1,0},{3,2},{5,4},{7,6},{8,9},{10,11},{12,... | collective-permute-start | bytes 688136 | tf_op jit(solution)/shard_map/ppermute | solution.py:782
  8.1 1.2 %copy-done.2 = f32[32,32,256]{2,1,0:T(8,128)S(1)} copy-done((f32[32,32,256]{2,1,0:T(8,128)S(1)}, f32[32,32,256]{2,1,0:T(8,128)}, u32[]{:S(2)}) %copy-start.2) | copy-done | bytes 1048600
  9.3 0.7 copy-done.5
  10.7 2.4 %collective-permute-start.4 = (f32[2,256]{1,0:T(2,128)S(1)}, f32[2,256]{1,0:T(2,128)S(1)}, u32[]{:S(2)}, u32[]{:S(2)}) collective-permute-start(f32[2,256]{1,0:T(2,128)S(1)} %get-tuple-element.70), channel_id=1, source_target_pairs={{0,4},{1,5},{2,6},{3,7},{4,0},{5,1},{6,2},{7,3},{8,12},{9,13},{10,... | collective-permute-start | bytes 6152 | tf_op jit(solution)/shard_map/ppermute | solution.py:786
  13.1 4.5 %collective-permute-start.6 = (f32[24,8,256]{2,1,0:T(8,128)S(1)}, f32[24,8,256]{2,1,0:T(8,128)S(1)}, u32[]{:S(2)}, u32[]{:S(2)}) collective-permute-start(f32[24,8,256]{2,1,0:T(8,128)S(1)} %get-tuple-element.72), channel_id=1, source_target_pairs={{8,16},{16,8},{9,17},{17,9},{10,18},{18,10},{11,19},{19,11},{12,20... | collective-permute-start | bytes 589832 | tf_op jit(solution)/shard_map/ppermute | solution.py:782
  18.3 3.5 %collective-permute-start.2 = (f32[35,8,256]{2,1,0:T(8,128)S(1)}, f32[35,8,256]{2,1,0:T(8,128)S(1)}, u32[]{:S(2)}, u32[]{:S(2)}) collective-permute-start(f32[35,8,256]{2,1,0:T(8,128)S(1)} %get-tuple-element.67), channel_id=1, source_target_pairs={{8,16},{16,8},{9,17},{17,9},{10,18},{18,10},{11,19},{19,11},{12,20... | collective-permute-start | bytes 860168 | tf_op jit(solution)/shard_map/ppermute | solution.py:782
  22.1 2.2 %collective-permute-start.8 = (f32[296,256]{1,0:T(8,128)S(1)}, f32[296,256]{1,0:T(8,128)S(1)}, u32[]{:S(2)}, u32[]{:S(2)}) collective-permute-start(f32[296,256]{1,0:T(8,128)S(1)} %get-tuple-element.74), channel_id=1, source_target_pairs={{0,1},{2,3},{4,5},{6,7},{1,0},{3,2},{5,4},{7,6},{8,9},{10,11},{12,... | collective-permute-start | bytes 909320 | tf_op jit(solution)/shard_map/ppermute | solution.py:782
  25.0 1.6 %collective-permute-done.2.x_a = f32[35,8,256]{2,1,0:T(8,128)S(1)} collective-permute-done((f32[35,8,256]{2,1,0:T(8,128)S(1)}, f32[35,8,256]{2,1,0:T(8,128)S(1)}, u32[]{:S(2)}, u32[]{:S(2)}) %collective-permute-start.2) | collective-permute-done | bytes 286752 | tf_op jit(solution)/shard_map/ppermute | solution.py:782
  26.5 4.7 %sweeps.1.conc = f32[32,32,256]{2,1,0:T(8,128)S(1)} custom-call(f32[32,32,256]{2,1,0:T(8,128)S(1)} %copy-done.1, s32[32,32,256]{2,1,0:T(8,128)S(1)} %copy-done, f32[32,32,256]{2,1,0:T(8,128)S(1)} %get-tuple-element.62.gain_own, f32[32,32,256]{2,1,0:T(8,128)S(1)} %get-tuple-element.63.base_own, f32[224,256]{1,0:T(8,128)S(1)} %collective-permute-done.r_a.y_a, ...), custom_call_target="tpu_custom_call" | custom-call | flops 1000000 | bytes 6275072 | tf_op jit(solution)/shard_map/sweeps/pallas_call | solution.py:36
  31.3 0.8 flux.1
  32.7 4.7 %collective-permute-start.10 = (f32[96,256]{1,0:T(8,128)S(1)}, f32[96,256]{1,0:T(8,128)S(1)}, u32[]{:S(2)}, u32[]{:S(2)}) collective-permute-start(f32[96,256]{1,0:T(8,128)S(1)} %get-tuple-element.79), channel_id=1, source_target_pairs={{0,1},{2,3},{4,5},{6,7},{1,0},{3,2},{5,4},{7,6},{8,9},{10,11},{12,... | collective-permute-start | bytes 294920 | tf_op jit(solution)/shard_map/ppermute | solution.py:782
  37.4 2.0 %mask.1 = (f32[32,32,256]{2,1,0:T(8,128)S(1)}, f32[32,8,256]{2,1,0:T(8,128)S(1)}) custom-call(f32[32,32,256]{2,1,0:T(8,128)S(1)} %get-tuple-element.69.flux_all, f32[8,256]{1,0:T(8,128)S(1)} %pad_maximum_fusion.lists, f32[296,256]{1,0:T(8,128)S(1)} %collective-permute-done.8.far.yy_b.r_b.far_b), custom_call_target="tpu_custom_call" | custom-call | flops 1000000 | bytes 2670592 | tf_op jit(solution)/shard_map/mask/pallas_call | solution.py:36
  39.4 0.9 %ready.1 = (f32[40,40,256]{2,1,0:T(8,128)S(1)}, f32[40,40,256]{2,1,0:T(8,128)S(1)}, f32[40,40,256]{2,1,0:T(8,128)S(1)}, f32[8,128]{1,0:T(8,128)S(1)}) custom-call(f32[32,32,256]{2,1,0:T(8,128)S(1)} %copy-done.1, s32[32,32,256]{2,1,0:T(8,128)S(1)} %copy-done, f32[32,32,256]{2,1,0:T(8,128)S(1)} %copy-done.3, f32[224,256]{1,0:T(8,128)S(1)} %collective-permute-done.r_a.y_a, ...), custom_call_target="tpu_custom_call" | custom-call | flops 1000000 | bytes 10088448 | tf_op jit(solution)/shard_map/ready/pallas_call | solution.py:36
  40.3 1.5 %collective-permute-done.10.r_b.y_b = f32[96,256]{1,0:T(8,128)S(1)} collective-permute-done((f32[96,256]{1,0:T(8,128)S(1)}, f32[96,256]{1,0:T(8,128)S(1)}, u32[]{:S(2)}, u32[]{:S(2)}) %collective-permute-start.10) | collective-permute-done | bytes 98336 | tf_op jit(solution)/shard_map/ppermute | solution.py:782
  41.9 2.5 %collective-permute-start.12 = (f32[15,8,256]{2,1,0:T(8,128)S(1)}, f32[15,8,256]{2,1,0:T(8,128)S(1)}, u32[]{:S(2)}, u32[]{:S(2)}) collective-permute-start(f32[15,8,256]{2,1,0:T(8,128)S(1)} %get-tuple-element.83), channel_id=1, source_target_pairs={{8,16},{16,8},{9,17},{17,9},{10,18},{18,10},{11,19},{19,11},{12,20... | collective-permute-start | bytes 368648 | tf_op jit(solution)/shard_map/ppermute | solution.py:782
  44.4 3.0 %potential_inner.1 = (f32[40,40,256]{2,1,0:T(8,128)S(1)}, f32[40,40,256]{2,1,0:T(8,128)S(1)}, f32[40,40,256]{2,1,0:T(8,128)S(1)}, f32[16,16,256]{2,1,0:T(8,128)S(1)}) custom-call(f32[32,32,256]{2,1,0:T(8,128)S(1)} %get-tuple-element.75.flux, f32[32,8,256]{2,1,0:T(8,128)S(1)} %get-tuple-element.80.mask, f32[96,256]{1,0:T(8,128)S(1)} %collective-permute-done.9.r_a.y_a, ...), custom_call_target="tpu_custom_call" | custom-call | flops 1000000 | bytes 11599872 | tf_op jit(solution)/shard_map/potential_inner/pallas_call | solution.py:36
  49.3 4.8 %collective-permute-start.15 = (f32[64,256]{1,0:T(8,128)S(1)}, f32[64,256]{1,0:T(8,128)S(1)}, u32[]{:S(2)}, u32[]{:S(2)}) collective-permute-start(f32[64,256]{1,0:T(8,128)S(1)} %get-tuple-element.94), channel_id=1, source_target_pairs={{0,1},{2,3},{4,5},{6,7},{1,0},{3,2},{5,4},{7,6},{8,9},{10,11},{12,... | collective-permute-start | bytes 196616 | tf_op jit(solution)/shard_map/ppermute | solution.py:782
  54.1 1.2 %coarse_ready.1 = (f32[8,8,256]{2,1,0:T(8,128)S(1)}, f32[8,128]{1,0:T(8,128)S(1)}, f32[8,128]{1,0:T(8,128)S(1)}) custom-call(f32[8,8,256]{2,1,0:T(8,128)S(1)} %get-tuple-element.66.token.coarse.own, f32[288,256]{1,0:T(8,128)S(1)} %collective-permute-done.11.yy_a.r_a.far_a, f32[296,256]{1,0:T(8,128)S(1)} %collective-permute-done.8.far.yy_b.r_b.far_b), custom_call_target="tpu_custom_call" | custom-call | flops 1000000 | bytes 737280 | tf_op jit(solution)/shard_map/coarse_ready/pallas_call | solution.py:36
  55.3 1.4 %store.1 = (f32[32,32,256]{2,1,0:T(8,128)}, f32[32,32,256]{2,1,0:T(8,128)}, f32[8,128]{1,0:T(8,128)S(1)}) custom-call(f32[32,32,256]{2,1,0:T(8,128)S(1)} %sweeps.1.conc, f32[32,32,256]{2,1,0:T(8,128)S(1)} %get-tuple-element.75.flux), custom_call_target="tpu_custom_call" | custom-call | flops 1000000 | bytes 4198400 | tf_op jit(solution)/shard_map/store/pallas_call | solution.py:36
  56.9 3.0 %collective-permute-start.16 = (f32[12,8,256]{2,1,0:T(8,128)S(1)}, f32[12,8,256]{2,1,0:T(8,128)S(1)}, u32[]{:S(2)}, u32[]{:S(2)}) collective-permute-start(f32[12,8,256]{2,1,0:T(8,128)S(1)} %get-tuple-element.97), channel_id=1, source_target_pairs={{8,16},{16,8},{9,17},{17,9},{10,18},{18,10},{11,19},{19,11},{12,20... | collective-permute-start | bytes 294920 | tf_op jit(solution)/shard_map/ppermute | solution.py:782
  60.0 2.8 %collective-permute-done.16.x_a = f32[12,8,256]{2,1,0:T(8,128)S(1)} collective-permute-done((f32[12,8,256]{2,1,0:T(8,128)S(1)}, f32[12,8,256]{2,1,0:T(8,128)S(1)}, u32[]{:S(2)}, u32[]{:S(2)}) %collective-permute-start.16) | collective-permute-done | bytes 98336 | tf_op jit(solution)/shard_map/ppermute | solution.py:782
  62.9 1.1 %middle.1 = (f32[24,24,256]{2,1,0:T(8,128)S(1)}, f32[24,24,256]{2,1,0:T(8,128)S(1)}, f32[24,24,256]{2,1,0:T(8,128)S(1)}, f32[8,12,256]{2,1,0:T(8,128)S(1)}, f32[...) custom-call(f32[16,16,256]{2,1,0:T(8,128)S(1)} %get-tuple-element.92.field.source_o, ...), custom_call_target="tpu_custom_call" | custom-call | flops 1000000 | bytes 4042752 | tf_op jit(solution)/shard_map/middle/pallas_call | solution.py:36
  63.9 2.3 %collective-permute-start.19 = (f32[80,256]{1,0:T(8,128)S(1)}, f32[80,256]{1,0:T(8,128)S(1)}, u32[]{:S(2)}, u32[]{:S(2)}) collective-permute-start(f32[80,256]{1,0:T(8,128)S(1)} %get-tuple-element.104), channel_id=1, source_target_pairs={{0,1},{2,3},{4,5},{6,7},{1,0},{3,2},{5,4},{7,6},{8,9},{10,11},{12,... | collective-permute-start | bytes 245768 | tf_op jit(solution)/shard_map/ppermute | solution.py:782
  66.9 1.2 %collective-permute-done.19.r_b = f32[80,256]{1,0:T(8,128)S(1)} collective-permute-done((f32[80,256]{1,0:T(8,128)S(1)}, f32[80,256]{1,0:T(8,128)S(1)}, u32[]{:S(2)}, u32[]{:S(2)}) %collective-permute-start.19) | collective-permute-done | bytes 81952 | tf_op jit(solution)/shard_map/ppermute | solution.py:782
  68.1 1.5 %collective-permute-start.20 = (f32[8,256]{1,0:T(8,128)S(1)}, f32[8,256]{1,0:T(8,128)S(1)}, u32[]{:S(2)}, u32[]{:S(2)}) collective-permute-start(f32[8,256]{1,0:T(8,128)S(1)} %slice_add_fusion), channel_id=1, source_target_pairs={{0,2},{1,3},{2,0},{3,1},{4,6},{5,7},{6,4},{7,5},{8,10},{9,11},{10,... | collective-permute-start | bytes 24584 | tf_op jit(solution)/shard_map/ppermute | solution.py:786
  69.6 1.7 %collective-permute-done.20 = f32[8,256]{1,0:T(8,128)S(1)} collective-permute-done((f32[8,256]{1,0:T(8,128)S(1)}, f32[8,256]{1,0:T(8,128)S(1)}, u32[]{:S(2)}, u32[]{:S(2)}) %collective-permute-start.20) | collective-permute-done | bytes 8224 | tf_op jit(solution)/shard_map/ppermute | solution.py:786
  71.3 2.8 %collective-permute-start.21 = (f32[8,256]{1,0:T(8,128)S(1)}, f32[8,256]{1,0:T(8,128)S(1)}, u32[]{:S(2)}, u32[]{:S(2)}) collective-permute-start(f32[8,256]{1,0:T(8,128)S(1)} %add.10), channel_id=1, source_target_pairs={{0,4},{1,5},{2,6},{3,7},{4,0},{5,1},{6,2},{7,3},{8,12},{9,13},{10,... | collective-permute-start | bytes 24584 | tf_op jit(solution)/shard_map/ppermute | solution.py:786
  74.1 1.2 %coarse.1.error = f32[8,16,256]{2,1,0:T(8,128)S(1)} custom-call(f32[8,12,256]{2,1,0:T(8,128)S(1)} %get-tuple-element.101.own, f32[8,12,256]{2,1,0:T(8,128)S(1)} %get-tuple-element.102.conduct, f32[288,256]{1,0:T(8,128)S(1)} %collective-permute-done.11.yy_a.r_a.far_a, f32[296,256]{1,0:T(8,128)S(1)} %collective-permute-done.8.far.yy_b.r_b.far_b, ...), custom_call_target="tpu_custom_call" | custom-call | flops 1000000 | bytes 1081344 | tf_op jit(solution)/shard_map/coarse/pallas_call | solution.py:36
  75.4 5.3 %collective-permute-start.22 = (f32[2,16,256]{2,1,0:T(8,128)S(1)}, f32[2,16,256]{2,1,0:T(8,128)S(1)}, u32[]{:S(2)}, u32[]{:S(2)}) collective-permute-start(f32[2,16,256]{2,1,0:T(8,128)S(1)} %get-tuple-element.106), channel_id=1, source_target_pairs={{8,16},{16,8},{9,17},{17,9},{10,18},{18,10},{11,19},{19,11},{12,20... | collective-permute-start | bytes 98312 | tf_op jit(solution)/shard_map/ppermute | solution.py:782
  80.8 2.5 %finish_inner.1 = (f32[32,32,256]{2,1,0:T(8,128)}, f32[24,24,256]{2,1,0:T(8,128)S(1)}, f32[24,24,256]{2,1,0:T(8,128)S(1)}, f32[40,40,256]{2,1,0:T(8,128)S(1)}, f32[40,40,256]{2,1,0:T(8,128)S(1)}) custom-call(f32[8,16,256]{2,1,0:T(8,128)S(1)} %get-tuple-element.113.error, f32[24,24,256]{2,1,0:T(8,128)S(1)} %get-tuple-element.108.mid_two, ...), custom_call_target="tpu_custom_call" | custom-call | flops 1000000 | bytes 12320768 | tf_op jit(solution)/shard_map/finish_inner/pallas_call | solution.py:36
  83.4 1.7 %finish_edge.1 = f32[32,32,256]{2,1,0:T(8,128)} custom-call(f32[2,16,256]{2,1,0:T(8,128)S(1)} %collective-permute-done.22.x_a, f32[2,16,256]{2,1,0:T(8,128)S(1)} %collective-permute-done.23.x_b, f32[24,24,256]{2,1,0:T(8,128)S(1)} %get-tuple-element.108.mid_two, f32[24,24,256]{2,1,0:T(8,128)S(1)} %get-tuple-element.109.mid_source, ...), custom_call_target="tpu_custom_call", output_to_operand_aliasing={{}: (14, {})} | custom-call | flops 1000000 | bytes 14614528 | tf_op jit(solution)/shard_map/finish_edge/pallas_call | solution.py:36
  (52 shorter events, 6.7 us)
Async XLA Ops:
  0.6 7.5 %copy-start = (s32[32,32,256]{2,1,0:T(8,128)S(1)}, s32[32,32,256]{2,1,0:T(8,128)}, u32[]{:S(2)}) copy-start(s32[32,32,256]{2,1,0:T(8,128)} %label.11) | copy-start | bytes 3145732
  0.6 7.5 %copy-start.1 = (f32[32,32,256]{2,1,0:T(8,128)S(1)}, f32[32,32,256]{2,1,0:T(8,128)}, u32[]{:S(2)}) copy-start(f32[32,32,256]{2,1,0:T(8,128)} %conc.9) | copy-start | bytes 3145732
  2.8 15.0 %collective-permute-start = (f32[224,256]{1,0:T(8,128)}, f32[224,256]{1,0:T(8,128)S(1)}, u32[]{:S(2)}, u32[]{:S(2)}) collective-permute-start(f32[224,256]{1,0:T(8,128)} %get-tuple-element.64), channel_id=1, source_target_pairs={{1,2},{3,4},{5,6},{2,1},{4,3},{6,5},{9,10},{11,12},{13,14},{10,9},... | collective-permute-start | bytes 688136 | tf_op jit(solution)/shard_map/ppermute | solution.py:782
  3.5 14.7 %collective-permute-start.1 = (f32[224,256]{1,0:T(8,128)}, f32[224,256]{1,0:T(8,128)S(1)}, u32[]{:S(2)}, u32[]{:S(2)}) collective-permute-start(f32[224,256]{1,0:T(8,128)} %get-tuple-element.65), channel_id=1, source_target_pairs={{0,1},{2,3},{4,5},{6,7},{1,0},{3,2},{5,4},{7,6},{8,9},{10,11},{12,... | collective-permute-start | bytes 688136 | tf_op jit(solution)/shard_map/ppermute | solution.py:782
  8.1 1.2 %copy-start.2 = (f32[32,32,256]{2,1,0:T(8,128)S(1)}, f32[32,32,256]{2,1,0:T(8,128)}, u32[]{:S(2)}) copy-start(f32[32,32,256]{2,1,0:T(8,128)} %phi.7) | copy-start | bytes 3145732
  9.3 0.7 copy-start.5
  10.7 11.3 %copy-start.3 = (f32[32,32,256]{2,1,0:T(8,128)S(1)}, f32[32,32,256]{2,1,0:T(8,128)}, u32[]{:S(2)}) copy-start(f32[32,32,256]{2,1,0:T(8,128)} %phi.7) | copy-start | bytes 3145732
  10.7 7.0 %collective-permute-start.4 = (f32[2,256]{1,0:T(2,128)S(1)}, f32[2,256]{1,0:T(2,128)S(1)}, u32[]{:S(2)}, u32[]{:S(2)}) collective-permute-start(f32[2,256]{1,0:T(2,128)S(1)} %get-tuple-element.70), channel_id=1, source_target_pairs={{0,4},{1,5},{2,6},{3,7},{4,0},{5,1},{6,2},{7,3},{8,12},{9,13},{10,... | collective-permute-start | bytes 6152 | tf_op jit(solution)/shard_map/ppermute | solution.py:786
  13.1 8.9 %collective-permute-start.6 = (f32[24,8,256]{2,1,0:T(8,128)S(1)}, f32[24,8,256]{2,1,0:T(8,128)S(1)}, u32[]{:S(2)}, u32[]{:S(2)}) collective-permute-start(f32[24,8,256]{2,1,0:T(8,128)S(1)} %get-tuple-element.72), channel_id=1, source_target_pairs={{8,16},{16,8},{9,17},{17,9},{10,18},{18,10},{11,19},{19,11},{12,20... | collective-permute-start | bytes 589832 | tf_op jit(solution)/shard_map/ppermute | solution.py:782
  17.6 4.3 %collective-permute-start.7 = (f32[24,8,256]{2,1,0:T(8,128)S(1)}, f32[24,8,256]{2,1,0:T(8,128)S(1)}, u32[]{:S(2)}, u32[]{:S(2)}) collective-permute-start(f32[24,8,256]{2,1,0:T(8,128)S(1)} %get-tuple-element.73), channel_id=1, source_target_pairs={{0,8},{16,24},{8,0},{24,16},{1,9},{17,25},{9,1},{25,17},{2,10},{18... | collective-permute-start | bytes 589832 | tf_op jit(solution)/shard_map/ppermute | solution.py:782
  17.7 4.2 %collective-permute-start.5 = (f32[4,256]{1,0:T(4,128)S(1)}, f32[4,256]{1,0:T(4,128)S(1)}, u32[]{:S(2)}, u32[]{:S(2)}) collective-permute-start(f32[4,256]{1,0:T(4,128)S(1)} %pad_maximum_fusion.1), channel_id=1, source_target_pairs={{0,2},{1,3},{2,0},{3,1},{4,6},{5,7},{6,4},{7,5},{8,10},{9,11},{10,... | collective-permute-start | bytes 12296 | tf_op jit(solution)/shard_map/ppermute | solution.py:786
  18.3 8.2 %collective-permute-start.2 = (f32[35,8,256]{2,1,0:T(8,128)S(1)}, f32[35,8,256]{2,1,0:T(8,128)S(1)}, u32[]{:S(2)}, u32[]{:S(2)}) collective-permute-start(f32[35,8,256]{2,1,0:T(8,128)S(1)} %get-tuple-element.67), channel_id=1, source_target_pairs={{8,16},{16,8},{9,17},{17,9},{10,18},{18,10},{11,19},{19,11},{12,20... | collective-permute-start | bytes 860168 | tf_op jit(solution)/shard_map/ppermute | solution.py:782
  21.8 4.7 %collective-permute-start.3 = (f32[35,8,256]{2,1,0:T(8,128)S(1)}, f32[35,8,256]{2,1,0:T(8,128)S(1)}, u32[]{:S(2)}, u32[]{:S(2)}) collective-permute-start(f32[35,8,256]{2,1,0:T(8,128)S(1)} %get-tuple-element.68), channel_id=1, source_target_pairs={{0,8},{16,24},{8,0},{24,16},{1,9},{17,25},{9,1},{25,17},{2,10},{18... | collective-permute-start | bytes 860168 | tf_op jit(solution)/shard_map/ppermute | solution.py:782
  22.1 15.3 %collective-permute-start.8 = (f32[296,256]{1,0:T(8,128)S(1)}, f32[296,256]{1,0:T(8,128)S(1)}, u32[]{:S(2)}, u32[]{:S(2)}) collective-permute-start(f32[296,256]{1,0:T(8,128)S(1)} %get-tuple-element.74), channel_id=1, source_target_pairs={{0,1},{2,3},{4,5},{6,7},{1,0},{3,2},{5,4},{7,6},{8,9},{10,11},{12,... | collective-permute-start | bytes 909320 | tf_op jit(solution)/shard_map/ppermute | solution.py:782
  24.3 15.1 %collective-permute-start.11 = (f32[288,256]{1,0:T(8,128)S(1)}, f32[288,256]{1,0:T(8,128)S(1)}, u32[]{:S(2)}, u32[]{:S(2)}) collective-permute-start(f32[288,256]{1,0:T(8,128)S(1)} %get-tuple-element.81), channel_id=1, source_target_pairs={{1,2},{3,4},{5,6},{2,1},{4,3},{6,5},{9,10},{11,12},{13,14},{10,9},... | collective-permute-start | bytes 884744 | tf_op jit(solution)/shard_map/ppermute | solution.py:782
  26.5 4.7 %copy-start.4 = (f32[32,32,256]{2,1,0:T(8,128)S(1)}, f32[32,32,256]{2,1,0:T(8,128)}, u32[]{:S(2)}) copy-start(f32[32,32,256]{2,1,0:T(8,128)} %solid.1) | copy-start | bytes 3145732
  32.1 8.3 %collective-permute-start.9 = (f32[96,256]{1,0:T(8,128)S(1)}, f32[96,256]{1,0:T(8,128)S(1)}, u32[]{:S(2)}, u32[]{:S(2)}) collective-permute-start(f32[96,256]{1,0:T(8,128)S(1)} %get-tuple-element.78), channel_id=1, source_target_pairs={{1,2},{3,4},{5,6},{2,1},{4,3},{6,5},{9,10},{11,12},{13,14},{10,9},... | collective-permute-start | bytes 294920 | tf_op jit(solution)/shard_map/ppermute | solution.py:782
  32.7 9.1 %collective-permute-start.10 = (f32[96,256]{1,0:T(8,128)S(1)}, f32[96,256]{1,0:T(8,128)S(1)}, u32[]{:S(2)}, u32[]{:S(2)}) collective-permute-start(f32[96,256]{1,0:T(8,128)S(1)} %get-tuple-element.79), channel_id=1, source_target_pairs={{0,1},{2,3},{4,5},{6,7},{1,0},{3,2},{5,4},{7,6},{8,9},{10,11},{12,... | collective-permute-start | bytes 294920 | tf_op jit(solution)/shard_map/ppermute | solution.py:782
  41.9 6.2 %collective-permute-start.12 = (f32[15,8,256]{2,1,0:T(8,128)S(1)}, f32[15,8,256]{2,1,0:T(8,128)S(1)}, u32[]{:S(2)}, u32[]{:S(2)}) collective-permute-start(f32[15,8,256]{2,1,0:T(8,128)S(1)} %get-tuple-element.83), channel_id=1, source_target_pairs={{8,16},{16,8},{9,17},{17,9},{10,18},{18,10},{11,19},{19,11},{12,20... | collective-permute-start | bytes 368648 | tf_op jit(solution)/shard_map/ppermute | solution.py:782
  44.3 3.7 %collective-permute-start.13 = (f32[15,8,256]{2,1,0:T(8,128)S(1)}, f32[15,8,256]{2,1,0:T(8,128)S(1)}, u32[]{:S(2)}, u32[]{:S(2)}) collective-permute-start(f32[15,8,256]{2,1,0:T(8,128)S(1)} %get-tuple-element.84), channel_id=1, source_target_pairs={{0,8},{16,24},{8,0},{24,16},{1,9},{17,25},{9,1},{25,17},{2,10},{18... | collective-permute-start | bytes 368648 | tf_op jit(solution)/shard_map/ppermute | solution.py:782
  48.7 8.0 %collective-permute-start.14 = (f32[64,256]{1,0:T(8,128)S(1)}, f32[64,256]{1,0:T(8,128)S(1)}, u32[]{:S(2)}, u32[]{:S(2)}) collective-permute-start(f32[64,256]{1,0:T(8,128)S(1)} %get-tuple-element.93), channel_id=1, source_target_pairs={{1,2},{3,4},{5,6},{2,1},{4,3},{6,5},{9,10},{11,12},{13,14},{10,9},... | collective-permute-start | bytes 196616 | tf_op jit(solution)/shard_map/ppermute | solution.py:782
  49.3 7.6 %collective-permute-start.15 = (f32[64,256]{1,0:T(8,128)S(1)}, f32[64,256]{1,0:T(8,128)S(1)}, u32[]{:S(2)}, u32[]{:S(2)}) collective-permute-start(f32[64,256]{1,0:T(8,128)S(1)} %get-tuple-element.94), channel_id=1, source_target_pairs={{0,1},{2,3},{4,5},{6,7},{1,0},{3,2},{5,4},{7,6},{8,9},{10,11},{12,... | collective-permute-start | bytes 196616 | tf_op jit(solution)/shard_map/ppermute | solution.py:782
  56.9 5.9 %collective-permute-start.16 = (f32[12,8,256]{2,1,0:T(8,128)S(1)}, f32[12,8,256]{2,1,0:T(8,128)S(1)}, u32[]{:S(2)}, u32[]{:S(2)}) collective-permute-start(f32[12,8,256]{2,1,0:T(8,128)S(1)} %get-tuple-element.97), channel_id=1, source_target_pairs={{8,16},{16,8},{9,17},{17,9},{10,18},{18,10},{11,19},{19,11},{12,20... | collective-permute-start | bytes 294920 | tf_op jit(solution)/shard_map/ppermute | solution.py:782
  59.9 2.9 %collective-permute-start.17 = (f32[12,8,256]{2,1,0:T(8,128)S(1)}, f32[12,8,256]{2,1,0:T(8,128)S(1)}, u32[]{:S(2)}, u32[]{:S(2)}) collective-permute-start(f32[12,8,256]{2,1,0:T(8,128)S(1)} %get-tuple-element.98), channel_id=1, source_target_pairs={{0,8},{16,24},{8,0},{24,16},{1,9},{17,25},{9,1},{25,17},{2,10},{18... | collective-permute-start | bytes 294920 | tf_op jit(solution)/shard_map/ppermute | solution.py:782
  63.9 4.1 %collective-permute-start.19 = (f32[80,256]{1,0:T(8,128)S(1)}, f32[80,256]{1,0:T(8,128)S(1)}, u32[]{:S(2)}, u32[]{:S(2)}) collective-permute-start(f32[80,256]{1,0:T(8,128)S(1)} %get-tuple-element.104), channel_id=1, source_target_pairs={{0,1},{2,3},{4,5},{6,7},{1,0},{3,2},{5,4},{7,6},{8,9},{10,11},{12,... | collective-permute-start | bytes 245768 | tf_op jit(solution)/shard_map/ppermute | solution.py:782
  66.2 7.9 %collective-permute-start.18 = (f32[72,256]{1,0:T(8,128)S(1)}, f32[72,256]{1,0:T(8,128)S(1)}, u32[]{:S(2)}, u32[]{:S(2)}) collective-permute-start(f32[72,256]{1,0:T(8,128)S(1)} %get-tuple-element.103), channel_id=1, source_target_pairs={{1,2},{3,4},{5,6},{2,1},{4,3},{6,5},{9,10},{11,12},{13,14},{10,9},... | collective-permute-start | bytes 221192 | tf_op jit(solution)/shard_map/ppermute | solution.py:782
  68.1 3.3 %collective-permute-start.20 = (f32[8,256]{1,0:T(8,128)S(1)}, f32[8,256]{1,0:T(8,128)S(1)}, u32[]{:S(2)}, u32[]{:S(2)}) collective-permute-start(f32[8,256]{1,0:T(8,128)S(1)} %slice_add_fusion), channel_id=1, source_target_pairs={{0,2},{1,3},{2,0},{3,1},{4,6},{5,7},{6,4},{7,5},{8,10},{9,11},{10,... | collective-permute-start | bytes 24584 | tf_op jit(solution)/shard_map/ppermute | solution.py:786
  71.3 4.0 %collective-permute-start.21 = (f32[8,256]{1,0:T(8,128)S(1)}, f32[8,256]{1,0:T(8,128)S(1)}, u32[]{:S(2)}, u32[]{:S(2)}) collective-permute-start(f32[8,256]{1,0:T(8,128)S(1)} %add.10), channel_id=1, source_target_pairs={{0,4},{1,5},{2,6},{3,7},{4,0},{5,1},{6,2},{7,3},{8,12},{9,13},{10,... | collective-permute-start | bytes 24584 | tf_op jit(solution)/shard_map/ppermute | solution.py:786
  75.4 7.9 %collective-permute-start.22 = (f32[2,16,256]{2,1,0:T(8,128)S(1)}, f32[2,16,256]{2,1,0:T(8,128)S(1)}, u32[]{:S(2)}, u32[]{:S(2)}) collective-permute-start(f32[2,16,256]{2,1,0:T(8,128)S(1)} %get-tuple-element.106), channel_id=1, source_target_pairs={{8,16},{16,8},{9,17},{17,9},{10,18},{18,10},{11,19},{19,11},{12,20... | collective-permute-start | bytes 98312 | tf_op jit(solution)/shard_map/ppermute | solution.py:782
  80.8 2.6 %collective-permute-start.23 = (f32[2,16,256]{2,1,0:T(8,128)S(1)}, f32[2,16,256]{2,1,0:T(8,128)S(1)}, u32[]{:S(2)}, u32[]{:S(2)}) collective-permute-start(f32[2,16,256]{2,1,0:T(8,128)S(1)} %get-tuple-element.107), channel_id=1, source_target_pairs={{0,8},{16,24},{8,0},{24,16},{1,9},{17,25},{9,1},{25,17},{2,10},{18... | collective-permute-start | bytes 98312 | tf_op jit(solution)/shard_map/ppermute | solution.py:782

commit v5 on v4

--- a/solution.py
+++ b/solution.py
@@ -259,71 +259,93 @@
     return jnp.concatenate([own, after_own, after, gap, before, before_own], axis=0)
 
 
-def sweeps_kernel(conc, label, gain_own, base_own, y_a, y_b, x_a, x_b, out, one, two, gain_far, base_far, gain_x, base_x):
+def flux_plane(c, solid, phi, label):
+    drive = 0.5 * (solid - phi)
+    logc = jnp.log(c)
+    return pick(label, KINETIC_TABLE) * (jnp.exp(drive + 0.4 * logc) - jnp.exp(0.6 * logc - drive))
+
+
+def around_plane(before, v, after):
+    return (before + after) + (along_y(v) + along_z(v))
+
+
+def sweeps_inner_kernel(
+    conc, label, phi, solid, gain, base, y_a, y_b, zero, first, second, third, gain_far, base_far, out, flux
+):
     nx = conc.shape[0]
 
     def own(i):
-        one[HALO + i, 0:32, :] = conc[i]
+        zero[i, 0:32, :] = conc[i]
 
     loop(0, nx, own)
     for i in range(nx):
         c = halo_tile(*y_sides(y_a, y_b, 7 * i, 4))
         lab = halo_tile(*y_sides(y_a, y_b, 7 * i + 4, 3))
-        one[HALO + i, 32:40, :] = c
+        zero[i, 32:40, :] = c
         gain_far[i] = jnp.where(c > 0.0, pick(lab, RATIO_TABLE), 0.0)
         base_far[i] = c * pick(lab, INVERSE_TABLE)
-
-    def put(x, rows, c, lab):
-        one[x, rows, :] = c
-        at = x if x < HALO else x - nx
-        gain_x[at, rows, :] = jnp.where(c > 0.0, pick(lab, RATIO_TABLE), 0.0)
-        base_x[at, rows, :] = c * pick(lab, INVERSE_TABLE)
-
-    for t in range(5):
-        rows = slice(8 * t, 8 * t + 8)
-        for k in range(HALO):
-            c_after, c_before = x_sides(x_a, x_b, 5 * k + t)
-            l_after = x_sides(x_a, x_b, 20 + 5 * min(k, 2) + t)[0]
-            l_before = x_sides(x_a, x_b, 20 + 5 * max(k - 1, 0) + t)[1]
-            put(k, rows, c_before, l_before)
-            put(HALO + nx + k, rows, c_after, l_after)
-
-    def neighbours(old, x):
-        mid = old[x]
-        return (old[x - 1] + old[x + 1]) + (along_y(mid) + along_z(mid))
-
-    fields = (one, two)
+    fields = (zero, first, second, third)
     for s in range(1, SWEEPS):
-        old, new = fields[(s - 1) % 2], fields[s % 2]
+        old, new = fields[s - 1], fields[s]
 
         def sweep(i, old=old, new=new):
-            gain = jnp.concatenate([gain_own[i], gain_far[i]], axis=0)
-            base = jnp.concatenate([base_own[i], base_far[i]], axis=0)
-            new[HALO + i] = base + gain * neighbours(old, HALO + i)
-
-        loop(0, nx, sweep)
-        for k in range(s, HALO):
-            for x, at in ((k, k), (2 * HALO + nx - 1 - k, 2 * HALO - 1 - k)):
-                new[x] = base_x[at] + gain_x[at] * neighbours(old, x)
-
-    old = fields[(SWEEPS - 1) % 2]
+            g = jnp.concatenate([gain[i], gain_far[i]], axis=0)
+            b = jnp.concatenate([base[i], base_far[i]], axis=0)
+            new[i] = b + g * around_plane(old[i - 1], old[i], old[i + 1])
+
+        loop(s, nx - s, sweep)
 
     def last(i):
-        out[i] = base_own[i] + gain_own[i] * neighbours(old, HALO + i)[0:32, :]
-
-    loop(0, nx, last)
-
-
-def flux_kernel(conc, label, phi, solid, flux, pay_a, pay_b):
-    nx = conc.shape[0]
-
-    def plane(i):
-        drive = 0.5 * (solid[i] - phi[i])
-        logc = jnp.log(conc[i])
-        value = jnp.exp(drive + 0.4 * logc) - jnp.exp(0.6 * logc - drive)
-        flux[i] = pick(label[i], KINETIC_TABLE) * value
-
-    loop(0, nx, plane, 4)
+        c = base[i] + gain[i] * around_plane(third[i - 1], third[i], third[i + 1])[0:32, :]
+        out[i] = c
+        flux[i] = flux_plane(c, solid[i], phi[i], label[i])
+
+    loop(SWEEPS, nx - SWEEPS, last, 4)
+
+
+def sweeps_edge_kernel(
+    x_a, x_b, label, phi, solid, gain, base, zero, first, second, third, gain_far, base_far, out_inner, flux_inner,
+    out, flux, pay_a, pay_b, zero_x, first_x, second_x, third_x,
+):
+    nx = out.shape[0]
+    inner = (zero, first, second, third)
+    edge = (zero_x, first_x, second_x, third_x)
+
+    def copy(i):
+        out[i] = out_inner[i]
+        flux[i] = flux_inner[i]
+
+    loop(SWEEPS, nx - SWEEPS, copy)
+    for side in range(2):
+        plane = lambda k, side=side: k if side == 0 else nx - 1 - k
+        row = lambda k, side=side: 8 * side + HALO + k
+        far = lambda k, index, side=side: x_sides(x_a, x_b, index)[1 - side]
+        gains, bases = {}, {}
+        for j in range(1, HALO + 1):
+            k = HALO - j if side == 0 else j - 1
+            zero_x[row(-j)] = jnp.concatenate([far(k, 5 * k + t) for t in range(5)], axis=0)
+            if j < HALO:
+                k = HALO - 1 - j if side == 0 else j - 1
+                lab = jnp.concatenate([far(k, 20 + 5 * k + t) for t in range(5)], axis=0)
+                c = zero_x[row(-j)]
+                gains[-j] = jnp.where(c > 0.0, pick(lab, RATIO_TABLE), 0.0)
+                bases[-j] = c * pick(lab, INVERSE_TABLE)
+        for k in range(SWEEPS):
+            gains[k] = jnp.concatenate([gain[plane(k)], gain_far[plane(k)]], axis=0)
+            bases[k] = jnp.concatenate([base[plane(k)], base_far[plane(k)]], axis=0)
+        for s in range(1, SWEEPS + 1):
+
+            def old(k, s=s):
+                return inner[s - 1][plane(k)] if k >= s - 1 else edge[s - 1][row(k)]
+
+            for k in range(s - SWEEPS, s):
+                c = bases[k] + gains[k] * around_plane(old(k - 1), old(k), old(k + 1))
+                if s < SWEEPS:
+                    edge[s][row(k)] = c
+                else:
+                    c = c[0:32, :]
+                    out[plane(k)] = c
+                    flux[plane(k)] = flux_plane(c, solid[plane(k)], phi[plane(k)], label[plane(k)])
     for x in range(nx):
         send_y(pay_a, pay_b, 3 * x, flux[x, 0:3, :], flux[x, 29:32, :])
 
@@ -637,7 +659,9 @@
         error[x, 8:16, :] = jnp.where(upper(), old[x, 8:16, :], old[x, 24:32, :])
 
 
-def shift_kernel(error, sums, out, pay_a, pay_b):
+def shift_kernel(error, *rest):
+    terms, (out, pay_a, pay_b) = rest[:-3], rest[-3:]
+    sums = sum(t[...] for t in terms)
     resid = jnp.sum(sums[:, :LANES])
     load = jnp.sum(sums[:, LANES:])
     shift_c = jnp.full((16, 256), resid, F32) / jnp.full((16, 256), load, F32)
@@ -837,18 +861,20 @@
     )
     x_a, x_b = swap(pay_a, pay_b, "grp")
 
-    (conc_new,) = call(
-        sweeps_kernel,
-        [shaped(nx, nx, 256)],
-        [conc_old, phase_label, gain, base, y_a, y_b, x_a, x_b],
-        [vmem(*ext)] * 2 + [vmem(nx, 8, 256)] * 2 + [vmem(2 * HALO, nx + 2 * HALO, 256)] * 2,
-        name="sweeps",
-    )
-    flux_all, pay_a, pay_b = call(
-        flux_kernel,
-        [shaped(nx, nx, 256), shaped(3 * nx, 256), shaped(3 * nx, 256)],
-        [conc_new, phase_label, phi_old, solid_pot],
-        name="flux",
+    ext_y = (nx, nx + 2 * HALO, 256)
+    zero, first, second, third, gain_far, base_far, conc_inner, flux_inner = call(
+        sweeps_inner_kernel,
+        [shaped(*ext_y)] * 4 + [shaped(nx, 8, 256)] * 2 + [shaped(nx, nx, 256)] * 2,
+        [conc_old, phase_label, phi_old, solid_pot, gain, base, y_a, y_b],
+        name="sweeps_inner",
+    )
+    edge_args = [x_a, x_b, phase_label, phi_old, solid_pot, gain, base, zero, first, second, third]
+    conc_new, flux_all, pay_a, pay_b = call(
+        sweeps_edge_kernel,
+        [shaped(nx, nx, 256), shaped(nx, nx, 256), shaped(3 * nx, 256), shaped(3 * nx, 256)],
+        edge_args + [gain_far, base_far, conc_inner, flux_inner],
+        [vmem(16, nx + 2 * HALO, 256)] * 4,
+        name="sweeps_edge",
     )
     f_a, f_b = swap(pay_a, pay_b, "dev")
     flux_own, halo_mask = call(
@@ -914,10 +940,7 @@
     )
     c_a, c_b = swap(pay_a, pay_b, "dev")
     sums = sums + c_b[72:80]
-    distance = 2
-    while distance < peers:
-        sums = sums + exchange(sums, distance)
-        distance *= 2
+    others = [exchange(sums, distance) for distance in range(2, peers, 2)]
     (error,) = call(
         coarse_kernel,
         [shaped(8, 16, 256)],
@@ -926,7 +949,7 @@
         name="coarse",
     )
     error, pay_a, pay_b = call(
-        shift_kernel, [shaped(8, 16, 256), shaped(2, 16, 256), shaped(2, 16, 256)], [error, sums], name="shift"
+        shift_kernel, [shaped(8, 16, 256), shaped(2, 16, 256), shaped(2, 16, 256)], [error, sums] + others, name="shift"
     )
     e_a, e_b = swap(pay_a, pay_b, "grp")
     begun, zero, one, fine_one, fine_last = call(

time: 86 us -> 88.5 us (1.029)
  starting transfers between devices: 47.8 us -> 51.4 us
  waiting for transfers between devices: 10.1 us -> 9.01 us
    ppermute x10, starting transfers between devices: 22.2 us -> 25.8 us  [swap(): lax.ppermute(pay_a, axis, both_ways(pairs_a))]
    ppermute x10, waiting for transfers between devices: 5.07 us -> 2.33 us  [swap(): lax.ppermute(pay_a, axis, both_ways(pairs_a))]
    ppermute x4 -> x5, waiting for transfers between devices: 1.73 us -> 3.12 us  [exchange(): lax.ppermute(value, 'dev', [(i, i ^ distance) for i in range(lax.axis_siz...]
    ppermute x4 -> x5, starting transfers between devices: 6.78 us -> 6.36 us  [exchange(): lax.ppermute(value, 'dev', [(i, i ^ distance) for i in range(lax.axis_siz...]
  transfers between devices with their start and end apart: 24 -> 25, of which waited for: 8 -> 6; matrix products, arithmetic and copies ran while one was open for 0% -> 0% of each run, Pallas kernels for 22% -> 21%
where the time goes in v5:
time: 88.5 us; the launch traced here: 87.6 us
  starting transfers between devices  51.4 us (58%)
  Pallas kernels  24.1 us (27%)
  waiting for transfers between devices  9.01 us (10%)
  local copies, waits for them, and re-layouts  1.94 us (2%)
  between operations  1.07 us (1%)
    ppermute x10, starting transfers between devices, swap(): lax.ppermute(pay_a, axis, both_ways(pairs_a))  25.8 us
    pallas_call x19, Pallas kernels, call(): pl.pallas_call(kernel, out_shape=tuple(outs), in_specs=in_specs or [WHOLE...  24.1 us
    ppermute x10, starting transfers between devices, swap(): lax.ppermute(pay_b, axis, both_ways(pairs_b))  19.3 us
    ppermute x5, starting transfers between devices, exchange(): lax.ppermute(value, 'dev', [(i, i ^ distance) for i in range(lax.axis_siz...  6.36 us
    ppermute x10, waiting for transfers between devices, swap(): lax.ppermute(pay_b, axis, both_ways(pairs_b))  3.55 us
    ppermute x5, waiting for transfers between devices, exchange(): lax.ppermute(value, 'dev', [(i, i ^ distance) for i in range(lax.axis_siz...  3.12 us
    ppermute x10, waiting for transfers between devices, swap(): lax.ppermute(pay_a, axis, both_ways(pairs_a))  2.33 us
    unnamed x12, local copies, waits for them, and re-layouts  1.94 us
  transfers between devices with their start and end apart: 25, of which 6 were waited for; matrix products, arithmetic and copies ran while one was open for 0% of the time, Pallas kernels for 21%

profile of v5, /device:TPU:1, one launch (start us, length us, event | category | flops | bytes accessed | tf_op | source)
XLA Modules:
  0.0 87.6 jit_solution(10333528789085013057)
XLA Ops:
  0.7 2.2 %first_pack.1 = (f32[224,256]{1,0:T(8,128)}, f32[224,256]{1,0:T(8,128)}, f32[8,256]{1,0:T(8,128)}) custom-call(f32[32,32,256]{2,1,0:T(8,128)} %conc.9, s32[32,32,256]{2,1,0:T(8,128)} %label.11, s32[1,256]{1,0:T(1,128)} %bitcast.1, s32[1,256]{1,0:T(1,128)} %block.1), custom_call_target="tpu_custom_call" | custom-call | flops 1000000 | bytes 2566144 | tf_op jit(solution)/shard_map/first_pack/pallas_call | solution.py:36
  2.8 0.7 collective-permute-start
  3.5 4.6 %collective-permute-start.1 = (f32[224,256]{1,0:T(8,128)}, f32[224,256]{1,0:T(8,128)S(1)}, u32[]{:S(2)}, u32[]{:S(2)}) collective-permute-start(f32[224,256]{1,0:T(8,128)} %get-tuple-element.71), channel_id=1, source_target_pairs={{0,1},{2,3},{4,5},{6,7},{1,0},{3,2},{5,4},{7,6},{8,9},{10,11},{12,... | collective-permute-start | bytes 688136 | tf_op jit(solution)/shard_map/ppermute | solution.py:806
  8.1 1.2 %copy-done.2 = f32[32,32,256]{2,1,0:T(8,128)S(1)} copy-done((f32[32,32,256]{2,1,0:T(8,128)S(1)}, f32[32,32,256]{2,1,0:T(8,128)}, u32[]{:S(2)}) %copy-start.2) | copy-done | bytes 1048600
  9.3 0.7 copy-done.5
  10.7 2.4 %collective-permute-start.4 = (f32[2,256]{1,0:T(2,128)S(1)}, f32[2,256]{1,0:T(2,128)S(1)}, u32[]{:S(2)}, u32[]{:S(2)}) collective-permute-start(f32[2,256]{1,0:T(2,128)S(1)} %get-tuple-element.88), channel_id=1, source_target_pairs={{0,4},{1,5},{2,6},{3,7},{4,0},{5,1},{6,2},{7,3},{8,12},{9,13},{10,... | collective-permute-start | bytes 6152 | tf_op jit(solution)/shard_map/ppermute | solution.py:810
  13.1 4.5 %collective-permute-start.6 = (f32[24,8,256]{2,1,0:T(8,128)S(1)}, f32[24,8,256]{2,1,0:T(8,128)S(1)}, u32[]{:S(2)}, u32[]{:S(2)}) collective-permute-start(f32[24,8,256]{2,1,0:T(8,128)S(1)} %get-tuple-element.90), channel_id=1, source_target_pairs={{8,16},{16,8},{9,17},{17,9},{10,18},{18,10},{11,19},{19,11},{12,20... | collective-permute-start | bytes 589832 | tf_op jit(solution)/shard_map/ppermute | solution.py:806
  18.3 3.7 %collective-permute-start.2 = (f32[35,8,256]{2,1,0:T(8,128)S(1)}, f32[35,8,256]{2,1,0:T(8,128)S(1)}, u32[]{:S(2)}, u32[]{:S(2)}) collective-permute-start(f32[35,8,256]{2,1,0:T(8,128)S(1)} %get-tuple-element.74), channel_id=1, source_target_pairs={{8,16},{16,8},{9,17},{17,9},{10,18},{18,10},{11,19},{19,11},{12,20... | collective-permute-start | bytes 860168 | tf_op jit(solution)/shard_map/ppermute | solution.py:806
  22.3 2.2 %collective-permute-start.8 = (f32[296,256]{1,0:T(8,128)S(1)}, f32[296,256]{1,0:T(8,128)S(1)}, u32[]{:S(2)}, u32[]{:S(2)}) collective-permute-start(f32[296,256]{1,0:T(8,128)S(1)} %get-tuple-element.92), channel_id=1, source_target_pairs={{0,1},{2,3},{4,5},{6,7},{1,0},{3,2},{5,4},{7,6},{8,9},{10,11},{12,... | collective-permute-start | bytes 909320 | tf_op jit(solution)/shard_map/ppermute | solution.py:806
  25.1 4.1 %sweeps_inner.1 = (f32[32,40,256]{2,1,0:T(8,128)S(1)}, f32[32,40,256]{2,1,0:T(8,128)S(1)}, f32[32,40,256]{2,1,0:T(8,128)S(1)}, f32[32,40,256]{2,1,0:T(8,128)S(1)...) custom-call(f32[32,32,256]{2,1,0:T(8,128)S(1)} %copy-done.1, ...), custom_call_target="tpu_custom_call" | custom-call | flops 1000000 | bytes 14614528 | tf_op jit(solution)/shard_map/sweeps_inner/pallas_call | solution.py:36
  29.2 1.2 %sweeps_edge.1 = (f32[32,32,256]{2,1,0:T(8,128)S(1)}, f32[32,32,256]{2,1,0:T(8,128)S(1)}, f32[96,256]{1,0:T(8,128)S(1)}, f32[96,256]{1,0:T(8,128)S(1)}) custom-call(f32[35,8,256]{2,1,0:T(8,128)S(1)} %collective-permute-done.2.x_a, f32[35,8,256]{2,1,0:T(8,128)S(1)} %collective-permute-done.3.x_b, s32[32,32,256]{2,1,0:T(8,128)S(1)} %copy-done, ...), custom_call_target="tpu_custom_call" | custom-call | flops 1000000 | bytes 15974400 | tf_op jit(solution)/shard_map/sweeps_edge/pallas_call | solution.py:36
  31.1 5.0 %collective-permute-start.10 = (f32[96,256]{1,0:T(8,128)S(1)}, f32[96,256]{1,0:T(8,128)S(1)}, u32[]{:S(2)}, u32[]{:S(2)}) collective-permute-start(f32[96,256]{1,0:T(8,128)S(1)} %get-tuple-element.97), channel_id=1, source_target_pairs={{0,1},{2,3},{4,5},{6,7},{1,0},{3,2},{5,4},{7,6},{8,9},{10,11},{12,... | collective-permute-start | bytes 294920 | tf_op jit(solution)/shard_map/ppermute | solution.py:806
  36.8 2.0 %mask.1 = (f32[32,32,256]{2,1,0:T(8,128)S(1)}, f32[32,8,256]{2,1,0:T(8,128)S(1)}) custom-call(f32[32,32,256]{2,1,0:T(8,128)S(1)} %get-tuple-element.87.flux_all, f32[8,256]{1,0:T(8,128)S(1)} %pad_maximum_fusion.lists, f32[296,256]{1,0:T(8,128)S(1)} %collective-permute-done.8.far.yy_b.r_b.far_b), custom_call_target="tpu_custom_call" | custom-call | flops 1000000 | bytes 2670592 | tf_op jit(solution)/shard_map/mask/pallas_call | solution.py:36
  38.8 0.9 ready.1
  39.7 1.3 %collective-permute-done.10.r_b.y_b = f32[96,256]{1,0:T(8,128)S(1)} collective-permute-done((f32[96,256]{1,0:T(8,128)S(1)}, f32[96,256]{1,0:T(8,128)S(1)}, u32[]{:S(2)}, u32[]{:S(2)}) %collective-permute-start.10) | collective-permute-done | bytes 98336 | tf_op jit(solution)/shard_map/ppermute | solution.py:806
  41.1 4.4 %collective-permute-start.12 = (f32[15,8,256]{2,1,0:T(8,128)S(1)}, f32[15,8,256]{2,1,0:T(8,128)S(1)}, u32[]{:S(2)}, u32[]{:S(2)}) collective-permute-start(f32[15,8,256]{2,1,0:T(8,128)S(1)} %get-tuple-element.101), channel_id=1, source_target_pairs={{8,16},{16,8},{9,17},{17,9},{10,18},{18,10},{11,19},{19,11},{12,20... | collective-permute-start | bytes 368648 | tf_op jit(solution)/shard_map/ppermute | solution.py:806
  45.6 3.1 %potential_inner.1 = (f32[40,40,256]{2,1,0:T(8,128)S(1)}, f32[40,40,256]{2,1,0:T(8,128)S(1)}, f32[40,40,256]{2,1,0:T(8,128)S(1)}, f32[16,16,256]{2,1,0:T(8,128)S(1)}) custom-call(f32[32,32,256]{2,1,0:T(8,128)S(1)} %get-tuple-element.93.flux, f32[32,8,256]{2,1,0:T(8,128)S(1)} %get-tuple-element.98.mask, f32[96,256]{1,0:T(8,128)S(1)} %collective-permute-done.9.r_a.y_a, ...), custom_call_target="tpu_custom_call" | custom-call | flops 1000000 | bytes 11599872 | tf_op jit(solution)/shard_map/potential_inner/pallas_call | solution.py:36
  50.0 4.9 %collective-permute-start.15 = (f32[64,256]{1,0:T(8,128)S(1)}, f32[64,256]{1,0:T(8,128)S(1)}, u32[]{:S(2)}, u32[]{:S(2)}) collective-permute-start(f32[64,256]{1,0:T(8,128)S(1)} %get-tuple-element.112), channel_id=1, source_target_pairs={{0,1},{2,3},{4,5},{6,7},{1,0},{3,2},{5,4},{7,6},{8,9},{10,11},{12,... | collective-permute-start | bytes 196616 | tf_op jit(solution)/shard_map/ppermute | solution.py:806
  54.9 1.2 %coarse_ready.1 = (f32[8,8,256]{2,1,0:T(8,128)S(1)}, f32[8,128]{1,0:T(8,128)S(1)}, f32[8,128]{1,0:T(8,128)S(1)}) custom-call(f32[8,8,256]{2,1,0:T(8,128)S(1)} %get-tuple-element.73.token.coarse.own, f32[288,256]{1,0:T(8,128)S(1)} %collective-permute-done.11.yy_a.r_a.far_a, f32[296,256]{1,0:T(8,128)S(1)} %collective-permute-done.8.far.yy_b.r_b.far_b), custom_call_target="tpu_custom_call" | custom-call | flops 1000000 | bytes 737280 | tf_op jit(solution)/shard_map/coarse_ready/pallas_call | solution.py:36
  56.1 1.4 %store.1 = (f32[32,32,256]{2,1,0:T(8,128)}, f32[32,32,256]{2,1,0:T(8,128)}, f32[8,128]{1,0:T(8,128)S(1)}) custom-call(f32[32,32,256]{2,1,0:T(8,128)S(1)} %get-tuple-element.86.conc, f32[32,32,256]{2,1,0:T(8,128)S(1)} %get-tuple-element.93.flux), custom_call_target="tpu_custom_call" | custom-call | flops 1000000 | bytes 4198400 | tf_op jit(solution)/shard_map/store/pallas_call | solution.py:36
  57.6 3.5 %collective-permute-start.16 = (f32[12,8,256]{2,1,0:T(8,128)S(1)}, f32[12,8,256]{2,1,0:T(8,128)S(1)}, u32[]{:S(2)}, u32[]{:S(2)}) collective-permute-start(f32[12,8,256]{2,1,0:T(8,128)S(1)} %get-tuple-element.115), channel_id=1, source_target_pairs={{8,16},{16,8},{9,17},{17,9},{10,18},{18,10},{11,19},{19,11},{12,20... | collective-permute-start | bytes 294920 | tf_op jit(solution)/shard_map/ppermute | solution.py:806
  61.2 2.3 %collective-permute-done.16.x_a = f32[12,8,256]{2,1,0:T(8,128)S(1)} collective-permute-done((f32[12,8,256]{2,1,0:T(8,128)S(1)}, f32[12,8,256]{2,1,0:T(8,128)S(1)}, u32[]{:S(2)}, u32[]{:S(2)}) %collective-permute-start.16) | collective-permute-done | bytes 98336 | tf_op jit(solution)/shard_map/ppermute | solution.py:806
  63.5 1.1 %middle.1 = (f32[24,24,256]{2,1,0:T(8,128)S(1)}, f32[24,24,256]{2,1,0:T(8,128)S(1)}, f32[24,24,256]{2,1,0:T(8,128)S(1)}, f32[8,12,256]{2,1,0:T(8,128)S(1)}, f32[...) custom-call(f32[16,16,256]{2,1,0:T(8,128)S(1)} %get-tuple-element.110.field.source_, ...), custom_call_target="tpu_custom_call" | custom-call | flops 1000000 | bytes 4042752 | tf_op jit(solution)/shard_map/middle/pallas_call | solution.py:36
  64.6 2.2 %collective-permute-start.19 = (f32[80,256]{1,0:T(8,128)S(1)}, f32[80,256]{1,0:T(8,128)S(1)}, u32[]{:S(2)}, u32[]{:S(2)}) collective-permute-start(f32[80,256]{1,0:T(8,128)S(1)} %get-tuple-element.122), channel_id=1, source_target_pairs={{0,1},{2,3},{4,5},{6,7},{1,0},{3,2},{5,4},{7,6},{8,9},{10,11},{12,... | collective-permute-start | bytes 245768 | tf_op jit(solution)/shard_map/ppermute | solution.py:806
  67.5 1.2 %collective-permute-done.19.r_b = f32[80,256]{1,0:T(8,128)S(1)} collective-permute-done((f32[80,256]{1,0:T(8,128)S(1)}, f32[80,256]{1,0:T(8,128)S(1)}, u32[]{:S(2)}, u32[]{:S(2)}) %collective-permute-start.19) | collective-permute-done | bytes 81952 | tf_op jit(solution)/shard_map/ppermute | solution.py:806
  68.6 1.5 %collective-permute-start.20 = (f32[8,256]{1,0:T(8,128)S(1)}, f32[8,256]{1,0:T(8,128)S(1)}, u32[]{:S(2)}, u32[]{:S(2)}) collective-permute-start(f32[8,256]{1,0:T(8,128)S(1)} %slice_add_fusion.rest_0_), channel_id=1, source_target_pairs={{0,2},{1,3},{2,0},{3,1},{4,6},{5,7},{6,4},{7,5},{8,10},{9,11},{10,... | collective-permute-start | bytes 24584 | tf_op jit(solution)/shard_map/ppermute | solution.py:810
  70.2 2.4 %collective-permute-start.21 = (f32[8,256]{1,0:T(8,128)S(1)}, f32[8,256]{1,0:T(8,128)S(1)}, u32[]{:S(2)}, u32[]{:S(2)}) collective-permute-start(f32[8,256]{1,0:T(8,128)S(1)} %slice_add_fusion.rest_0_), channel_id=1, source_target_pairs={{0,4},{1,5},{2,6},{3,7},{4,0},{5,1},{6,2},{7,3},{8,12},{9,13},{10,... | collective-permute-start | bytes 24584 | tf_op jit(solution)/shard_map/ppermute | solution.py:810
  72.6 1.2 %coarse.1.error = f32[8,16,256]{2,1,0:T(8,128)S(1)} custom-call(f32[8,12,256]{2,1,0:T(8,128)S(1)} %get-tuple-element.119.own, f32[8,12,256]{2,1,0:T(8,128)S(1)} %get-tuple-element.120.conduct, f32[288,256]{1,0:T(8,128)S(1)} %collective-permute-done.11.yy_a.r_a.far_a, f32[296,256]{1,0:T(8,128)S(1)} %collective-permute-done.8.far.yy_b.r_b.far_b, ...), custom_call_target="tpu_custom_call" | custom-call | flops 1000000 | bytes 1081344 | tf_op jit(solution)/shard_map/coarse/pallas_call | solution.py:36
  73.7 3.1 %collective-permute-done.22.rest_3_ = f32[8,256]{1,0:T(8,128)S(1)} collective-permute-done((f32[8,256]{1,0:T(8,128)S(1)}, f32[8,256]{1,0:T(8,128)S(1)}, u32[]{:S(2)}, u32[]{:S(2)}) %collective-permute-start.22) | collective-permute-done | bytes 8224 | tf_op jit(solution)/shard_map/ppermute | solution.py:810
  77.0 6.3 %collective-permute-start.23 = (f32[2,16,256]{2,1,0:T(8,128)S(1)}, f32[2,16,256]{2,1,0:T(8,128)S(1)}, u32[]{:S(2)}, u32[]{:S(2)}) collective-permute-start(f32[2,16,256]{2,1,0:T(8,128)S(1)} %get-tuple-element.124), channel_id=1, source_target_pairs={{8,16},{16,8},{9,17},{17,9},{10,18},{18,10},{11,19},{19,11},{12,20... | collective-permute-start | bytes 98312 | tf_op jit(solution)/shard_map/ppermute | solution.py:806
  83.4 2.5 %finish_inner.1 = (f32[32,32,256]{2,1,0:T(8,128)}, f32[24,24,256]{2,1,0:T(8,128)S(1)}, f32[24,24,256]{2,1,0:T(8,128)S(1)}, f32[40,40,256]{2,1,0:T(8,128)S(1)}, f32[40,40,256]{2,1,0:T(8,128)S(1)}) custom-call(f32[8,16,256]{2,1,0:T(8,128)S(1)} %get-tuple-element.131.error, f32[24,24,256]{2,1,0:T(8,128)S(1)} %get-tuple-element.126.mid_two, ...), custom_call_target="tpu_custom_call" | custom-call | flops 1000000 | bytes 12320768 | tf_op jit(solution)/shard_map/finish_inner/pallas_call | solution.py:36
  86.0 1.7 %finish_edge.1 = f32[32,32,256]{2,1,0:T(8,128)} custom-call(f32[2,16,256]{2,1,0:T(8,128)S(1)} %collective-permute-done.23.x_a, f32[2,16,256]{2,1,0:T(8,128)S(1)} %collective-permute-done.24.x_b, f32[24,24,256]{2,1,0:T(8,128)S(1)} %get-tuple-element.126.mid_two, f32[24,24,256]{2,1,0:T(8,128)S(1)} %get-tuple-element.127.mid_source, ...), custom_call_target="tpu_custom_call", output_to_operand_aliasing={{}: (14, {})} | custom-call | flops 1000000 | bytes 14614528 | tf_op jit(solution)/shard_map/finish_edge/pallas_call | solution.py:36
  (52 shorter events, 5.9 us)
Async XLA Ops:
  0.6 7.5 %copy-start.1 = (f32[32,32,256]{2,1,0:T(8,128)S(1)}, f32[32,32,256]{2,1,0:T(8,128)}, u32[]{:S(2)}) copy-start(f32[32,32,256]{2,1,0:T(8,128)} %conc.9) | copy-start | bytes 3145732
  0.6 7.5 %copy-start = (s32[32,32,256]{2,1,0:T(8,128)S(1)}, s32[32,32,256]{2,1,0:T(8,128)}, u32[]{:S(2)}) copy-start(s32[32,32,256]{2,1,0:T(8,128)} %label.11) | copy-start | bytes 3145732
  2.8 15.0 %collective-permute-start = (f32[224,256]{1,0:T(8,128)}, f32[224,256]{1,0:T(8,128)S(1)}, u32[]{:S(2)}, u32[]{:S(2)}) collective-permute-start(f32[224,256]{1,0:T(8,128)} %get-tuple-element.70), channel_id=1, source_target_pairs={{1,2},{3,4},{5,6},{2,1},{4,3},{6,5},{9,10},{11,12},{13,14},{10,9},... | collective-permute-start | bytes 688136 | tf_op jit(solution)/shard_map/ppermute | solution.py:806
  3.5 14.7 %collective-permute-start.1 = (f32[224,256]{1,0:T(8,128)}, f32[224,256]{1,0:T(8,128)S(1)}, u32[]{:S(2)}, u32[]{:S(2)}) collective-permute-start(f32[224,256]{1,0:T(8,128)} %get-tuple-element.71), channel_id=1, source_target_pairs={{0,1},{2,3},{4,5},{6,7},{1,0},{3,2},{5,4},{7,6},{8,9},{10,11},{12,... | collective-permute-start | bytes 688136 | tf_op jit(solution)/shard_map/ppermute | solution.py:806
  8.1 1.2 %copy-start.2 = (f32[32,32,256]{2,1,0:T(8,128)S(1)}, f32[32,32,256]{2,1,0:T(8,128)}, u32[]{:S(2)}) copy-start(f32[32,32,256]{2,1,0:T(8,128)} %phi.9) | copy-start | bytes 3145732
  9.3 0.7 copy-start.5
  10.7 11.4 %copy-start.3 = (f32[32,32,256]{2,1,0:T(8,128)S(1)}, f32[32,32,256]{2,1,0:T(8,128)}, u32[]{:S(2)}) copy-start(f32[32,32,256]{2,1,0:T(8,128)} %phi.9) | copy-start | bytes 3145732
  10.7 7.0 %collective-permute-start.4 = (f32[2,256]{1,0:T(2,128)S(1)}, f32[2,256]{1,0:T(2,128)S(1)}, u32[]{:S(2)}, u32[]{:S(2)}) collective-permute-start(f32[2,256]{1,0:T(2,128)S(1)} %get-tuple-element.88), channel_id=1, source_target_pairs={{0,4},{1,5},{2,6},{3,7},{4,0},{5,1},{6,2},{7,3},{8,12},{9,13},{10,... | collective-permute-start | bytes 6152 | tf_op jit(solution)/shard_map/ppermute | solution.py:810
  13.1 9.0 %collective-permute-start.6 = (f32[24,8,256]{2,1,0:T(8,128)S(1)}, f32[24,8,256]{2,1,0:T(8,128)S(1)}, u32[]{:S(2)}, u32[]{:S(2)}) collective-permute-start(f32[24,8,256]{2,1,0:T(8,128)S(1)} %get-tuple-element.90), channel_id=1, source_target_pairs={{8,16},{16,8},{9,17},{17,9},{10,18},{18,10},{11,19},{19,11},{12,20... | collective-permute-start | bytes 589832 | tf_op jit(solution)/shard_map/ppermute | solution.py:806
  17.6 4.5 %collective-permute-start.7 = (f32[24,8,256]{2,1,0:T(8,128)S(1)}, f32[24,8,256]{2,1,0:T(8,128)S(1)}, u32[]{:S(2)}, u32[]{:S(2)}) collective-permute-start(f32[24,8,256]{2,1,0:T(8,128)S(1)} %get-tuple-element.91), channel_id=1, source_target_pairs={{0,8},{16,24},{8,0},{24,16},{1,9},{17,25},{9,1},{25,17},{2,10},{18... | collective-permute-start | bytes 589832 | tf_op jit(solution)/shard_map/ppermute | solution.py:806
  17.7 4.3 %collective-permute-start.5 = (f32[4,256]{1,0:T(4,128)S(1)}, f32[4,256]{1,0:T(4,128)S(1)}, u32[]{:S(2)}, u32[]{:S(2)}) collective-permute-start(f32[4,256]{1,0:T(4,128)S(1)} %pad_maximum_fusion.1), channel_id=1, source_target_pairs={{0,2},{1,3},{2,0},{3,1},{4,6},{5,7},{6,4},{7,5},{8,10},{9,11},{10,... | collective-permute-start | bytes 12296 | tf_op jit(solution)/shard_map/ppermute | solution.py:810
  18.2 6.9 %copy-start.4 = (f32[32,32,256]{2,1,0:T(8,128)S(1)}, f32[32,32,256]{2,1,0:T(8,128)}, u32[]{:S(2)}) copy-start(f32[32,32,256]{2,1,0:T(8,128)} %solid.3) | copy-start | bytes 3145732
  18.3 10.9 %collective-permute-start.2 = (f32[35,8,256]{2,1,0:T(8,128)S(1)}, f32[35,8,256]{2,1,0:T(8,128)S(1)}, u32[]{:S(2)}, u32[]{:S(2)}) collective-permute-start(f32[35,8,256]{2,1,0:T(8,128)S(1)} %get-tuple-element.74), channel_id=1, source_target_pairs={{8,16},{16,8},{9,17},{17,9},{10,18},{18,10},{11,19},{19,11},{12,20... | collective-permute-start | bytes 860168 | tf_op jit(solution)/shard_map/ppermute | solution.py:806
  22.0 7.3 %collective-permute-start.3 = (f32[35,8,256]{2,1,0:T(8,128)S(1)}, f32[35,8,256]{2,1,0:T(8,128)S(1)}, u32[]{:S(2)}, u32[]{:S(2)}) collective-permute-start(f32[35,8,256]{2,1,0:T(8,128)S(1)} %get-tuple-element.75), channel_id=1, source_target_pairs={{0,8},{16,24},{8,0},{24,16},{1,9},{17,25},{9,1},{25,17},{2,10},{18... | collective-permute-start | bytes 860168 | tf_op jit(solution)/shard_map/ppermute | solution.py:806
  22.3 14.5 %collective-permute-start.8 = (f32[296,256]{1,0:T(8,128)S(1)}, f32[296,256]{1,0:T(8,128)S(1)}, u32[]{:S(2)}, u32[]{:S(2)}) collective-permute-start(f32[296,256]{1,0:T(8,128)S(1)} %get-tuple-element.92), channel_id=1, source_target_pairs={{0,1},{2,3},{4,5},{6,7},{1,0},{3,2},{5,4},{7,6},{8,9},{10,11},{12,... | collective-permute-start | bytes 909320 | tf_op jit(solution)/shard_map/ppermute | solution.py:806
  24.4 14.4 %collective-permute-start.11 = (f32[288,256]{1,0:T(8,128)S(1)}, f32[288,256]{1,0:T(8,128)S(1)}, u32[]{:S(2)}, u32[]{:S(2)}) collective-permute-start(f32[288,256]{1,0:T(8,128)S(1)} %get-tuple-element.99), channel_id=1, source_target_pairs={{1,2},{3,4},{5,6},{2,1},{4,3},{6,5},{9,10},{11,12},{13,14},{10,9},... | collective-permute-start | bytes 884744 | tf_op jit(solution)/shard_map/ppermute | solution.py:806
  30.5 9.3 %collective-permute-start.9 = (f32[96,256]{1,0:T(8,128)S(1)}, f32[96,256]{1,0:T(8,128)S(1)}, u32[]{:S(2)}, u32[]{:S(2)}) collective-permute-start(f32[96,256]{1,0:T(8,128)S(1)} %get-tuple-element.96), channel_id=1, source_target_pairs={{1,2},{3,4},{5,6},{2,1},{4,3},{6,5},{9,10},{11,12},{13,14},{10,9},... | collective-permute-start | bytes 294920 | tf_op jit(solution)/shard_map/ppermute | solution.py:806
  31.1 9.9 %collective-permute-start.10 = (f32[96,256]{1,0:T(8,128)S(1)}, f32[96,256]{1,0:T(8,128)S(1)}, u32[]{:S(2)}, u32[]{:S(2)}) collective-permute-start(f32[96,256]{1,0:T(8,128)S(1)} %get-tuple-element.97), channel_id=1, source_target_pairs={{0,1},{2,3},{4,5},{6,7},{1,0},{3,2},{5,4},{7,6},{8,9},{10,11},{12,... | collective-permute-start | bytes 294920 | tf_op jit(solution)/shard_map/ppermute | solution.py:806
  41.1 7.6 %collective-permute-start.12 = (f32[15,8,256]{2,1,0:T(8,128)S(1)}, f32[15,8,256]{2,1,0:T(8,128)S(1)}, u32[]{:S(2)}, u32[]{:S(2)}) collective-permute-start(f32[15,8,256]{2,1,0:T(8,128)S(1)} %get-tuple-element.101), channel_id=1, source_target_pairs={{8,16},{16,8},{9,17},{17,9},{10,18},{18,10},{11,19},{19,11},{12,20... | collective-permute-start | bytes 368648 | tf_op jit(solution)/shard_map/ppermute | solution.py:806
  45.5 3.2 %collective-permute-start.13 = (f32[15,8,256]{2,1,0:T(8,128)S(1)}, f32[15,8,256]{2,1,0:T(8,128)S(1)}, u32[]{:S(2)}, u32[]{:S(2)}) collective-permute-start(f32[15,8,256]{2,1,0:T(8,128)S(1)} %get-tuple-element.102), channel_id=1, source_target_pairs={{0,8},{16,24},{8,0},{24,16},{1,9},{17,25},{9,1},{25,17},{2,10},{18... | collective-permute-start | bytes 368648 | tf_op jit(solution)/shard_map/ppermute | solution.py:806
  49.3 8.2 %collective-permute-start.14 = (f32[64,256]{1,0:T(8,128)S(1)}, f32[64,256]{1,0:T(8,128)S(1)}, u32[]{:S(2)}, u32[]{:S(2)}) collective-permute-start(f32[64,256]{1,0:T(8,128)S(1)} %get-tuple-element.111), channel_id=1, source_target_pairs={{1,2},{3,4},{5,6},{2,1},{4,3},{6,5},{9,10},{11,12},{13,14},{10,9},... | collective-permute-start | bytes 196616 | tf_op jit(solution)/shard_map/ppermute | solution.py:806
  50.0 7.5 %collective-permute-start.15 = (f32[64,256]{1,0:T(8,128)S(1)}, f32[64,256]{1,0:T(8,128)S(1)}, u32[]{:S(2)}, u32[]{:S(2)}) collective-permute-start(f32[64,256]{1,0:T(8,128)S(1)} %get-tuple-element.112), channel_id=1, source_target_pairs={{0,1},{2,3},{4,5},{6,7},{1,0},{3,2},{5,4},{7,6},{8,9},{10,11},{12,... | collective-permute-start | bytes 196616 | tf_op jit(solution)/shard_map/ppermute | solution.py:806
  57.6 5.9 %collective-permute-start.16 = (f32[12,8,256]{2,1,0:T(8,128)S(1)}, f32[12,8,256]{2,1,0:T(8,128)S(1)}, u32[]{:S(2)}, u32[]{:S(2)}) collective-permute-start(f32[12,8,256]{2,1,0:T(8,128)S(1)} %get-tuple-element.115), channel_id=1, source_target_pairs={{8,16},{16,8},{9,17},{17,9},{10,18},{18,10},{11,19},{19,11},{12,20... | collective-permute-start | bytes 294920 | tf_op jit(solution)/shard_map/ppermute | solution.py:806
  61.1 2.4 %collective-permute-start.17 = (f32[12,8,256]{2,1,0:T(8,128)S(1)}, f32[12,8,256]{2,1,0:T(8,128)S(1)}, u32[]{:S(2)}, u32[]{:S(2)}) collective-permute-start(f32[12,8,256]{2,1,0:T(8,128)S(1)} %get-tuple-element.116), channel_id=1, source_target_pairs={{0,8},{16,24},{8,0},{24,16},{1,9},{17,25},{9,1},{25,17},{2,10},{18... | collective-permute-start | bytes 294920 | tf_op jit(solution)/shard_map/ppermute | solution.py:806
  64.6 4.0 %collective-permute-start.19 = (f32[80,256]{1,0:T(8,128)S(1)}, f32[80,256]{1,0:T(8,128)S(1)}, u32[]{:S(2)}, u32[]{:S(2)}) collective-permute-start(f32[80,256]{1,0:T(8,128)S(1)} %get-tuple-element.122), channel_id=1, source_target_pairs={{0,1},{2,3},{4,5},{6,7},{1,0},{3,2},{5,4},{7,6},{8,9},{10,11},{12,... | collective-permute-start | bytes 245768 | tf_op jit(solution)/shard_map/ppermute | solution.py:806
  66.8 5.8 %collective-permute-start.18 = (f32[72,256]{1,0:T(8,128)S(1)}, f32[72,256]{1,0:T(8,128)S(1)}, u32[]{:S(2)}, u32[]{:S(2)}) collective-permute-start(f32[72,256]{1,0:T(8,128)S(1)} %get-tuple-element.121), channel_id=1, source_target_pairs={{1,2},{3,4},{5,6},{2,1},{4,3},{6,5},{9,10},{11,12},{13,14},{10,9},... | collective-permute-start | bytes 221192 | tf_op jit(solution)/shard_map/ppermute | solution.py:806
  68.6 5.1 %collective-permute-start.20 = (f32[8,256]{1,0:T(8,128)S(1)}, f32[8,256]{1,0:T(8,128)S(1)}, u32[]{:S(2)}, u32[]{:S(2)}) collective-permute-start(f32[8,256]{1,0:T(8,128)S(1)} %slice_add_fusion.rest_0_), channel_id=1, source_target_pairs={{0,2},{1,3},{2,0},{3,1},{4,6},{5,7},{6,4},{7,5},{8,10},{9,11},{10,... | collective-permute-start | bytes 24584 | tf_op jit(solution)/shard_map/ppermute | solution.py:810
  70.2 3.5 %collective-permute-start.21 = (f32[8,256]{1,0:T(8,128)S(1)}, f32[8,256]{1,0:T(8,128)S(1)}, u32[]{:S(2)}, u32[]{:S(2)}) collective-permute-start(f32[8,256]{1,0:T(8,128)S(1)} %slice_add_fusion.rest_0_), channel_id=1, source_target_pairs={{0,4},{1,5},{2,6},{3,7},{4,0},{5,1},{6,2},{7,3},{8,12},{9,13},{10,... | collective-permute-start | bytes 24584 | tf_op jit(solution)/shard_map/ppermute | solution.py:810
  72.5 4.3 %collective-permute-start.22 = (f32[8,256]{1,0:T(8,128)S(1)}, f32[8,256]{1,0:T(8,128)S(1)}, u32[]{:S(2)}, u32[]{:S(2)}) collective-permute-start(f32[8,256]{1,0:T(8,128)S(1)} %slice_add_fusion.rest_0_), channel_id=1, source_target_pairs={{0,6},{1,7},{2,4},{3,5},{4,2},{5,3},{6,0},{7,1},{8,14},{9,15},{10,... | collective-permute-start | bytes 24584 | tf_op jit(solution)/shard_map/ppermute | solution.py:810
  77.0 8.9 %collective-permute-start.23 = (f32[2,16,256]{2,1,0:T(8,128)S(1)}, f32[2,16,256]{2,1,0:T(8,128)S(1)}, u32[]{:S(2)}, u32[]{:S(2)}) collective-permute-start(f32[2,16,256]{2,1,0:T(8,128)S(1)} %get-tuple-element.124), channel_id=1, source_target_pairs={{8,16},{16,8},{9,17},{17,9},{10,18},{18,10},{11,19},{19,11},{12,20... | collective-permute-start | bytes 98312 | tf_op jit(solution)/shard_map/ppermute | solution.py:806
  83.3 2.6 %collective-permute-start.24 = (f32[2,16,256]{2,1,0:T(8,128)S(1)}, f32[2,16,256]{2,1,0:T(8,128)S(1)}, u32[]{:S(2)}, u32[]{:S(2)}) collective-permute-start(f32[2,16,256]{2,1,0:T(8,128)S(1)} %get-tuple-element.125), channel_id=1, source_target_pairs={{0,8},{16,24},{8,0},{24,16},{1,9},{17,25},{9,1},{25,17},{2,10},{18... | collective-permute-start | bytes 98312 | tf_op jit(solution)/shard_map/ppermute | solution.py:806

commit v6 on v5

--- a/solution.py
+++ b/solution.py
@@ -216,42 +216,43 @@
     return counts, [sum(counts[:i]) for i in range(len(counts))]
 
 
-def second_rows(nx):
-    phi, mid = (sum(corner_rows(n, reach)[0]) for n, reach in ((nx, 0), (nx // 2, 1)))
-    return phi, phi + mid, phi + mid + 64
-
-
-def second_pack_kernel(phi, mid, coarse, lists, x_a, x_b, pay_a, pay_b):
-    nx = phi.shape[0]
-    starts = second_rows(nx)
-
-    def put(own, n, reach, index, base):
-        counts, at = corner_rows(n, reach)
-        tiles = own.shape[1] // 8
-        for x in range(n):
-            send_y(pay_a, pay_b, base + at[HALO + x], own[x, 0:4, :], own[x, 8 * tiles - 4 : 8 * tiles, :])
-        for k in range(HALO):
-            first_after, first_before = x_sides(x_a, x_b, index + tiles * k)
-            last_after, last_before = x_sides(x_a, x_b, index + tiles * k + tiles - 1)
-            for x, first, last in ((k, first_before, last_before), (HALO + n + k, first_after, last_after)):
-                if counts[x]:
-                    send_y(pay_a, pay_b, base + at[x], first[0 : counts[x]], last[8 - counts[x] : 8])
-
-    put(phi, nx, 0, 0, 0)
-    put(mid, nx // 2, 1, 16, starts[0])
-    base = starts[1]
+def extended_rows(n, reach):
+    return sum(corner_rows(n, reach)[0])
+
+
+def send_extended(pay_a, pay_b, own, x_a, x_b, index, reach):
+    n = own.shape[0]
+    counts, at = corner_rows(n, reach)
+    tiles = own.shape[1] // 8
+    for x in range(n):
+        send_y(pay_a, pay_b, at[HALO + x], own[x, 0:4, :], own[x, 8 * tiles - 4 : 8 * tiles, :])
+    for k in range(HALO):
+        first_after, first_before = x_sides(x_a, x_b, index + tiles * k)
+        last_after, last_before = x_sides(x_a, x_b, index + tiles * k + tiles - 1)
+        for x, first, last in ((k, first_before, last_before), (HALO + n + k, first_after, last_after)):
+            if counts[x]:
+                send_y(pay_a, pay_b, at[x], first[0 : counts[x]], last[8 - counts[x] : 8])
+
+
+def second_pack_kernel(phi, lists, x_a, x_b, pay_a, pay_b):
+    send_extended(pay_a, pay_b, phi, x_a, x_b, 0, 0)
+    base = pay_a.shape[0]
+    pay_b[base : base + lists.shape[0], :] = lists[...]
+
+
+def third_pack_kernel(mid, coarse, x_a, x_b, pay_a, pay_b):
+    send_extended(pay_a, pay_b, mid, x_a, x_b, 16, 1)
+    base = pay_a.shape[0] - 64
     for x in range(8):
         pay_a[base + 8 * x : base + 8 * x + 8, :] = coarse[x]
         pay_b[base + 8 * x : base + 8 * x + 8, :] = coarse[x]
-    base = starts[2]
-    pay_b[base : base + lists.shape[0], :] = lists[...]
-
-
-def second_halo(r_a, r_b, n, reach, x, base):
+
+
+def second_halo(r_a, r_b, n, reach, x):
     counts, at = corner_rows(n, reach)
     if not counts[x]:
         return jnp.zeros((8, 256), F32)
-    return halo_tile(*y_sides(r_a, r_b, base + at[x], counts[x]))
+    return halo_tile(*y_sides(r_a, r_b, at[x], counts[x]))
 
 
 def wide_rows(own, after_own, before_own, after, before):
@@ -357,15 +358,15 @@
     owner = jnp.concatenate(pieces[0::2], axis=1).astype(jnp.int32)
     block = jnp.concatenate(pieces[1::2], axis=1).astype(jnp.int32)
     entries = owner.shape[1]
-    hit_column = (iota((LANES, entries), 0) == lax.rem(block, 64)).astype(jnp.bfloat16)
-    at_row = lax.shift_right_arithmetic(block, 6)
-    here = lax.axis_index("dev")
+    hit_column = (iota((64, entries), 0) == lax.rem(block, 64)).astype(jnp.bfloat16)
+    reach = owner - lax.axis_index("dev") + 1
+    at_row = jnp.where((reach >= 0) & (reach < 3), reach * nx + lax.shift_right_arithmetic(block, 6), -1)
+    hit_row = (iota((3 * nx, entries), 0) == at_row).astype(jnp.bfloat16)
+    named = lax.dot_general(hit_row, hit_column, (((1,), (1,)), ((), ())), preferred_element_type=F32)
+    named = jnp.concatenate([named, jnp.zeros((3 * nx, LANES - 64), F32)], axis=1)
     for j in range(3):
-        mine = jnp.where(owner == here + j - 1, at_row, -1)
-        hit_row = (iota((nx, entries), 0) == mine).astype(jnp.bfloat16)
-        named = lax.dot_general(hit_row, hit_column, (((1,), (1,)), ((), ())), preferred_element_type=F32)
         for i in range(nx):
-            marked[j, i] = jnp.broadcast_to(named[i : i + 1, :], (8, LANES))
+            marked[j, i] = jnp.broadcast_to(named[j * nx + i : j * nx + i + 1, :], (8, LANES))
     is_row = lax.div(iota((32, LANES), 1), 2) == iota((32, LANES), 0)
     row, pair = iota((8, LANES), 0), lax.div(iota((8, LANES), 1), 2)
     is_after = (row < 3) & (pair == row)
@@ -380,7 +381,7 @@
         flux[i] = jnp.where(listed[0:32], flux_all[i], 0.0)
         halo_mask[i] = jnp.where(listed[32:40], 1.0, 0.0)
 
-    loop(0, nx, plane, 4)
+    loop(0, nx, plane, 16)
 
 
 def store_kernel(conc, flux, conc_out, flux_out, token, sems):
@@ -414,7 +415,7 @@
     for i in range(nx):
         c = halo_tile(*y_sides(y_a, y_b, 7 * i, 4))
         lab = halo_tile(*y_sides(y_a, y_b, 7 * i + 4, 3))
-        put(HALO + i, low, c, lab, second_halo(yy_a, yy_b, nx, 0, HALO + i, 0))
+        put(HALO + i, low, c, lab, second_halo(yy_a, yy_b, nx, 0, HALO + i))
     for t in range(5):
         rows = slice(8 * t, 8 * t + 8)
         for k in range(HALO):
@@ -424,8 +425,8 @@
             if t < 4:
                 p_after, p_before = x_sides(xx_a, xx_b, 4 * k + t)
             else:
-                p_after = second_halo(yy_a, yy_b, nx, 0, HALO + nx + k, 0)
-                p_before = second_halo(yy_a, yy_b, nx, 0, k, 0)
+                p_after = second_halo(yy_a, yy_b, nx, 0, HALO + nx + k)
+                p_before = second_halo(yy_a, yy_b, nx, 0, k)
             put(k, rows, c_before, l_before, p_before)
             put(HALO + nx + k, rows, c_after, l_after, p_after)
 
@@ -522,7 +523,7 @@
         send_y(pay_a, pay_b, 4 * x, source_mid[x, 0:4, :], source_mid[x, 12:16, :])
 
 
-def mid_pack_x_kernel(field, r_a, r_b, token, token_2, pay_a, pay_b):
+def mid_pack_x_kernel(field, r_a, r_b, token, pay_a, pay_b):
     n = field.shape[0]
 
     def tile(x, t):
@@ -540,7 +541,6 @@
     after_two, source, weight, coarse, conduct, pay_a, pay_b, part, scale, mid_conduct, pairs, pairs_2,
 ):
     n = source_own.shape[0]
-    base = second_rows(2 * n)[0]
 
     def put(x, rows, b, k):
         factor = OMEGA / (MASS + 3.0 * k)
@@ -550,7 +550,7 @@
         mid_conduct[x, rows, :] = k
 
     def far(x):
-        return second_halo(yy_a, yy_b, n, 1, x, base)
+        return second_halo(yy_a, yy_b, n, 1, x)
 
     for i in range(n):
         put(HALO + i, slice(0, 16), source_own[i], conduct_own[i])
@@ -598,8 +598,7 @@
 COARSE_W = 0.0625
 
 
-def coarse_ready_kernel(own, r_a, r_b, rho, load, token, one, two, conduct, scale):
-    token[...] = jnp.zeros(token.shape, F32)
+def coarse_ready_kernel(own, r_a, r_b, rho, load, one, two, conduct, scale):
     base = r_a.shape[0] - 64
     for x in range(8):
         after, before = y_sides(r_a, r_b, base + 8 * x, 8)
@@ -845,11 +844,11 @@
     while distance > 1:
         lists = jnp.concatenate([lists, exchange(lists, distance)], axis=0)
         distance //= 2
-    far_rows = second_rows(nx)[2]
+    rows = extended_rows(nx, 0)
     far_pay = call(
         second_pack_kernel,
-        [shaped(far_rows, 256), shaped(far_rows + peers, 256)],
-        [phi_old, conduct_mid, conduct_coarse, lists, xx_a, xx_b],
+        [shaped(rows, 256), shaped(rows + peers, 256)],
+        [phi_old, lists, xx_a, xx_b],
         name="second_pack",
     )
     yy_a, yy_b = swap(*far_pay, "dev")
@@ -910,6 +909,11 @@
         name="potential_edge",
     )
     m_a, m_b = swap(pay_a, pay_b, "dev")
+    rows = extended_rows(half, 1) + 64
+    far_pay = call(
+        third_pack_kernel, [shaped(rows, 256)] * 2, [conduct_mid, conduct_coarse, xx_a, xx_b], name="third_pack"
+    )
+    k_a, k_b = swap(*far_pay, "dev")
     concentration, flux, stored = call(
         store_kernel,
         [shaped(nx, nx, 256), shaped(nx, nx, 256), token_shape],
@@ -919,32 +923,32 @@
         name="store",
     )
     wide = (quarter, 32, 256)
-    rho, load, made = call(
+    rho, load = call(
         coarse_ready_kernel,
-        [shaped(quarter, quarter, 256), shaped(8, LANES), token_shape],
-        [conduct_coarse, yy_a, yy_b],
+        [shaped(quarter, quarter, 256), shaped(8, LANES)],
+        [conduct_coarse, k_a, k_b],
         [vmem(*wide)] * 4,
         name="coarse_ready",
     )
     pay_a, pay_b = call(
-        mid_pack_x_kernel, [shaped(3 * HALO, 8, 256)] * 2, [source_mid, m_a, m_b, made, stored], name="mid_pack_x"
+        mid_pack_x_kernel, [shaped(3 * HALO, 8, 256)] * 2, [source_mid, m_a, m_b, stored], name="mid_pack_x"
     )
     mx_a, mx_b = swap(pay_a, pay_b, "grp")
     mid_two, mid_source, mid_weight, source_coarse, wide_coarse, pay_a, pay_b, sums = call(
         mid_kernel,
         [shaped(*ext_mid)] * 3
         + [shaped(quarter, 12, 256), shaped(quarter, 12, 256), shaped(72, 256), shaped(80, 256), shaped(8, 256)],
-        [source_mid, conduct_mid, yy_a, yy_b, xx_a, xx_b, m_a, m_b, mx_a, mx_b, rho, load],
+        [source_mid, conduct_mid, k_a, k_b, xx_a, xx_b, m_a, m_b, mx_a, mx_b, rho, load],
         [vmem(*ext_mid)] * 2 + [vmem(8, 2, half + 2 * HALO, LANES)] * 2,
         name="middle",
     )
     c_a, c_b = swap(pay_a, pay_b, "dev")
     sums = sums + c_b[72:80]
-    others = [exchange(sums, distance) for distance in range(2, peers, 2)]
+    others = [exchange(sums, distance) for distance in range(peers - 2, 0, -2)]
     (error,) = call(
         coarse_kernel,
         [shaped(8, 16, 256)],
-        [source_coarse, wide_coarse, yy_a, yy_b, c_a, c_b],
+        [source_coarse, wide_coarse, k_a, k_b, c_a, c_b],
         [vmem(*wide)] * 4,
         name="coarse",
     )

time: 88.5 us -> 94.2 us (1.064)
  waiting for transfers between devices: 9.01 us -> 16.6 us
  Pallas kernels: 24.1 us -> 22.8 us
    ppermute x10 -> x11, waiting for transfers between devices: 3.55 us -> 12.3 us  [swap(): lax.ppermute(pay_b, axis, both_ways(pairs_b))]
    ppermute x10 -> x11, starting transfers between devices: 25.8 us -> 21.5 us  [swap(): lax.ppermute(pay_a, axis, both_ways(pairs_a))]
    ppermute x10 -> x11, starting transfers between devices: 19.3 us -> 21.2 us  [swap(): lax.ppermute(pay_b, axis, both_ways(pairs_b))]
    ppermute x5, starting transfers between devices: 6.36 us -> 8.17 us  [exchange(): lax.ppermute(value, 'dev', [(i, i ^ distance) for i in range(lax.axis_siz...]
    ppermute x5, waiting for transfers between devices: 3.12 us -> 1.42 us  [exchange(): lax.ppermute(value, 'dev', [(i, i ^ distance) for i in range(lax.axis_siz...]
    pallas_call x19 -> x20, Pallas kernels: 24.1 us -> 22.8 us  [call(): pl.pallas_call(kernel, out_shape=tuple(outs), in_specs=in_specs or [WHOLE...]
    ppermute x10 -> x11, waiting for transfers between devices: 2.33 us -> 2.93 us  [swap(): lax.ppermute(pay_a, axis, both_ways(pairs_a))]
  transfers between devices with their start and end apart: 25 -> 27, of which waited for: 6 -> 9; matrix products, arithmetic and copies ran while one was open for 0% -> 0% of each run, Pallas kernels for 21% -> 18%
where the time goes in v6:
time: 94.2 us; the launch traced here: 93.3 us
  starting transfers between devices  50.9 us (54%)
  Pallas kernels  22.8 us (24%)
  waiting for transfers between devices  16.6 us (18%)
  local copies, waits for them, and re-layouts  1.94 us (2%)
  between operations  1.02 us (1%)
    pallas_call x20, Pallas kernels, call(): pl.pallas_call(kernel, out_shape=tuple(outs), in_specs=in_specs or [WHOLE...  22.8 us
    ppermute x11, starting transfers between devices, swap(): lax.ppermute(pay_a, axis, both_ways(pairs_a))  21.5 us
    ppermute x11, starting transfers between devices, swap(): lax.ppermute(pay_b, axis, both_ways(pairs_b))  21.2 us
    ppermute x11, waiting for transfers between devices, swap(): lax.ppermute(pay_b, axis, both_ways(pairs_b))  12.3 us
    ppermute x5, starting transfers between devices, exchange(): lax.ppermute(value, 'dev', [(i, i ^ distance) for i in range(lax.axis_siz...  8.17 us
    ppermute x11, waiting for transfers between devices, swap(): lax.ppermute(pay_a, axis, both_ways(pairs_a))  2.93 us
    unnamed x12, local copies, waits for them, and re-layouts  1.94 us
  transfers between devices with their start and end apart: 27, of which 9 were waited for; matrix products, arithmetic and copies ran while one was open for 0% of the time, Pallas kernels for 18%

profile of v6, /device:TPU:1, one launch (start us, length us, event | category | flops | bytes accessed | tf_op | source)
XLA Modules:
  0.0 93.3 jit_solution(6318018154257836552)
XLA Ops:
  0.7 2.2 %first_pack.1 = (f32[224,256]{1,0:T(8,128)}, f32[224,256]{1,0:T(8,128)}, f32[8,256]{1,0:T(8,128)}) custom-call(f32[32,32,256]{2,1,0:T(8,128)} %conc.9, s32[32,32,256]{2,1,0:T(8,128)} %label.11, s32[1,256]{1,0:T(1,128)} %bitcast.1, s32[1,256]{1,0:T(1,128)} %block.1), custom_call_target="tpu_custom_call" | custom-call | flops 1000000 | bytes 2566144 | tf_op jit(solution)/shard_map/first_pack/pallas_call | solution.py:36
  3.5 4.6 %collective-permute-start.1 = (f32[224,256]{1,0:T(8,128)}, f32[224,256]{1,0:T(8,128)S(1)}, u32[]{:S(2)}, u32[]{:S(2)}) collective-permute-start(f32[224,256]{1,0:T(8,128)} %get-tuple-element.72), channel_id=1, source_target_pairs={{0,1},{2,3},{4,5},{6,7},{1,0},{3,2},{5,4},{7,6},{8,9},{10,11},{12,... | collective-permute-start | bytes 688136 | tf_op jit(solution)/shard_map/ppermute | solution.py:805
  8.1 1.2 %copy-done.2 = f32[32,32,256]{2,1,0:T(8,128)S(1)} copy-done((f32[32,32,256]{2,1,0:T(8,128)S(1)}, f32[32,32,256]{2,1,0:T(8,128)}, u32[]{:S(2)}) %copy-start.2) | copy-done | bytes 1048600
  10.7 7.5 %collective-permute-done.1.r_b.y_b = f32[224,256]{1,0:T(8,128)S(1)} collective-permute-done((f32[224,256]{1,0:T(8,128)}, f32[224,256]{1,0:T(8,128)S(1)}, u32[]{:S(2)}, u32[]{:S(2)}) %collective-permute-start.1) | collective-permute-done | bytes 229408 | tf_op jit(solution)/shard_map/ppermute | solution.py:805
  18.3 3.7 %collective-permute-start.2 = (f32[35,8,256]{2,1,0:T(8,128)S(1)}, f32[35,8,256]{2,1,0:T(8,128)S(1)}, u32[]{:S(2)}, u32[]{:S(2)}) collective-permute-start(f32[35,8,256]{2,1,0:T(8,128)S(1)} %get-tuple-element.75), channel_id=1, source_target_pairs={{8,16},{16,8},{9,17},{17,9},{10,18},{18,10},{11,19},{19,11},{12,20... | collective-permute-start | bytes 860168 | tf_op jit(solution)/shard_map/ppermute | solution.py:805
  22.0 3.3 %collective-permute-start.4 = (f32[2,256]{1,0:T(2,128)S(1)}, f32[2,256]{1,0:T(2,128)S(1)}, u32[]{:S(2)}, u32[]{:S(2)}) collective-permute-start(f32[2,256]{1,0:T(2,128)S(1)} %get-tuple-element.89), channel_id=1, source_target_pairs={{0,4},{1,5},{2,6},{3,7},{4,0},{5,1},{6,2},{7,3},{8,12},{9,13},{10,... | collective-permute-start | bytes 6152 | tf_op jit(solution)/shard_map/ppermute | solution.py:809
  25.3 2.3 %collective-permute-start.6 = (f32[24,8,256]{2,1,0:T(8,128)S(1)}, f32[24,8,256]{2,1,0:T(8,128)S(1)}, u32[]{:S(2)}, u32[]{:S(2)}) collective-permute-start(f32[24,8,256]{2,1,0:T(8,128)S(1)} %get-tuple-element.90), channel_id=1, source_target_pairs={{8,16},{16,8},{9,17},{17,9},{10,18},{18,10},{11,19},{19,11},{12,20... | collective-permute-start | bytes 589832 | tf_op jit(solution)/shard_map/ppermute | solution.py:805
  27.7 1.4 %collective-permute-start.5 = (f32[4,256]{1,0:T(4,128)S(1)}, f32[4,256]{1,0:T(4,128)S(1)}, u32[]{:S(2)}, u32[]{:S(2)}) collective-permute-start(f32[4,256]{1,0:T(4,128)S(1)} %pad_maximum_fusion.1), channel_id=1, source_target_pairs={{0,2},{1,3},{2,0},{3,1},{4,6},{5,7},{6,4},{7,5},{8,10},{9,11},{10,... | collective-permute-start | bytes 12296 | tf_op jit(solution)/shard_map/ppermute | solution.py:809
  29.1 1.2 %collective-permute-done.5 = f32[4,256]{1,0:T(4,128)S(1)} collective-permute-done((f32[4,256]{1,0:T(4,128)S(1)}, f32[4,256]{1,0:T(4,128)S(1)}, u32[]{:S(2)}, u32[]{:S(2)}) %collective-permute-start.5) | collective-permute-done | bytes 4128 | tf_op jit(solution)/shard_map/ppermute | solution.py:809
  30.2 2.0 %collective-permute-done.6.x_a.xx_a = f32[24,8,256]{2,1,0:T(8,128)S(1)} collective-permute-done((f32[24,8,256]{2,1,0:T(8,128)S(1)}, f32[24,8,256]{2,1,0:T(8,128)S(1)}, u32[]{:S(2)}, u32[]{:S(2)}) %collective-permute-start.6) | collective-permute-done | bytes 196640 | tf_op jit(solution)/shard_map/ppermute | solution.py:805
  32.4 1.3 %collective-permute-start.8 = (f32[148,256]{1,0:T(8,128)S(1)}, f32[148,256]{1,0:T(8,128)S(1)}, u32[]{:S(2)}, u32[]{:S(2)}) collective-permute-start(f32[148,256]{1,0:T(8,128)S(1)} %get-tuple-element.92), channel_id=1, source_target_pairs={{0,1},{2,3},{4,5},{6,7},{1,0},{3,2},{5,4},{7,6},{8,9},{10,11},{12,... | collective-permute-start | bytes 454664 | tf_op jit(solution)/shard_map/ppermute | solution.py:805
  34.3 4.1 %sweeps_inner.1 = (f32[32,40,256]{2,1,0:T(8,128)S(1)}, f32[32,40,256]{2,1,0:T(8,128)S(1)}, f32[32,40,256]{2,1,0:T(8,128)S(1)}, f32[32,40,256]{2,1,0:T(8,128)S(1)...) custom-call(f32[32,32,256]{2,1,0:T(8,128)S(1)} %copy-done.1, ...), custom_call_target="tpu_custom_call" | custom-call | flops 1000000 | bytes 14614528 | tf_op jit(solution)/shard_map/sweeps_inner/pallas_call | solution.py:36
  38.4 1.2 %sweeps_edge.1 = (f32[32,32,256]{2,1,0:T(8,128)S(1)}, f32[32,32,256]{2,1,0:T(8,128)S(1)}, f32[96,256]{1,0:T(8,128)S(1)}, f32[96,256]{1,0:T(8,128)S(1)}) custom-call(f32[35,8,256]{2,1,0:T(8,128)S(1)} %collective-permute-done.2.x_a, f32[35,8,256]{2,1,0:T(8,128)S(1)} %collective-permute-done.3.x_b, s32[32,32,256]{2,1,0:T(8,128)S(1)} %copy-done, ...), custom_call_target="tpu_custom_call" | custom-call | flops 1000000 | bytes 15974400 | tf_op jit(solution)/shard_map/sweeps_edge/pallas_call | solution.py:36
  40.3 5.2 %collective-permute-start.10 = (f32[96,256]{1,0:T(8,128)S(1)}, f32[96,256]{1,0:T(8,128)S(1)}, u32[]{:S(2)}, u32[]{:S(2)}) collective-permute-start(f32[96,256]{1,0:T(8,128)S(1)} %get-tuple-element.97), channel_id=1, source_target_pairs={{0,1},{2,3},{4,5},{6,7},{1,0},{3,2},{5,4},{7,6},{8,9},{10,11},{12,... | collective-permute-start | bytes 294920 | tf_op jit(solution)/shard_map/ppermute | solution.py:805
  47.3 2.1 %collective-permute-done.10.r_b.y_b = f32[96,256]{1,0:T(8,128)S(1)} collective-permute-done((f32[96,256]{1,0:T(8,128)S(1)}, f32[96,256]{1,0:T(8,128)S(1)}, u32[]{:S(2)}, u32[]{:S(2)}) %collective-permute-start.10) | collective-permute-done | bytes 98336 | tf_op jit(solution)/shard_map/ppermute | solution.py:805
  49.4 2.3 %collective-permute-start.12 = (f32[15,8,256]{2,1,0:T(8,128)S(1)}, f32[15,8,256]{2,1,0:T(8,128)S(1)}, u32[]{:S(2)}, u32[]{:S(2)}) collective-permute-start(f32[15,8,256]{2,1,0:T(8,128)S(1)} %get-tuple-element.101), channel_id=1, source_target_pairs={{8,16},{16,8},{9,17},{17,9},{10,18},{18,10},{11,19},{19,11},{12,20... | collective-permute-start | bytes 368648 | tf_op jit(solution)/shard_map/ppermute | solution.py:805
  51.8 3.0 %potential_inner.1 = (f32[40,40,256]{2,1,0:T(8,128)S(1)}, f32[40,40,256]{2,1,0:T(8,128)S(1)}, f32[40,40,256]{2,1,0:T(8,128)S(1)}, f32[16,16,256]{2,1,0:T(8,128)S(1)}) custom-call(f32[32,32,256]{2,1,0:T(8,128)S(1)} %get-tuple-element.93.flux, f32[32,8,256]{2,1,0:T(8,128)S(1)} %get-tuple-element.98.mask, f32[96,256]{1,0:T(8,128)S(1)} %collective-permute-done.9.r_a.y_a, ...), custom_call_target="tpu_custom_call" | custom-call | flops 1000000 | bytes 11599872 | tf_op jit(solution)/shard_map/potential_inner/pallas_call | solution.py:36
  56.8 5.1 %collective-permute-start.17 = (f32[64,256]{1,0:T(8,128)S(1)}, f32[64,256]{1,0:T(8,128)S(1)}, u32[]{:S(2)}, u32[]{:S(2)}) collective-permute-start(f32[64,256]{1,0:T(8,128)S(1)} %get-tuple-element.115), channel_id=1, source_target_pairs={{0,1},{2,3},{4,5},{6,7},{1,0},{3,2},{5,4},{7,6},{8,9},{10,11},{12,... | collective-permute-start | bytes 196616 | tf_op jit(solution)/shard_map/ppermute | solution.py:805
  62.7 2.5 %collective-permute-start.15 = (f32[148,256]{1,0:T(8,128)S(1)}, f32[148,256]{1,0:T(8,128)S(1)}, u32[]{:S(2)}, u32[]{:S(2)}) collective-permute-start(f32[148,256]{1,0:T(8,128)S(1)} %get-tuple-element.113), channel_id=1, source_target_pairs={{0,1},{2,3},{4,5},{6,7},{1,0},{3,2},{5,4},{7,6},{8,9},{10,11},{12,... | collective-permute-start | bytes 454664 | tf_op jit(solution)/shard_map/ppermute | solution.py:805
  65.2 1.4 %store.1 = (f32[32,32,256]{2,1,0:T(8,128)}, f32[32,32,256]{2,1,0:T(8,128)}, f32[8,128]{1,0:T(8,128)S(1)}) custom-call(f32[32,32,256]{2,1,0:T(8,128)S(1)} %get-tuple-element.87.conc, f32[32,32,256]{2,1,0:T(8,128)S(1)} %get-tuple-element.93.flux), custom_call_target="tpu_custom_call" | custom-call | flops 1000000 | bytes 4198400 | tf_op jit(solution)/shard_map/store/pallas_call | solution.py:36
  66.7 4.2 %collective-permute-start.18 = (f32[12,8,256]{2,1,0:T(8,128)S(1)}, f32[12,8,256]{2,1,0:T(8,128)S(1)}, u32[]{:S(2)}, u32[]{:S(2)}) collective-permute-start(f32[12,8,256]{2,1,0:T(8,128)S(1)} %get-tuple-element.117), channel_id=1, source_target_pairs={{8,16},{16,8},{9,17},{17,9},{10,18},{18,10},{11,19},{19,11},{12,20... | collective-permute-start | bytes 294920 | tf_op jit(solution)/shard_map/ppermute | solution.py:805
  71.0 1.0 %collective-permute-done.15.r_b.yy_b.far_b = f32[148,256]{1,0:T(8,128)S(1)} collective-permute-done((f32[148,256]{1,0:T(8,128)S(1)}, f32[148,256]{1,0:T(8,128)S(1)}, u32[]{:S(2)}, u32[]{:S(2)}) %collective-permute-start.15) | collective-permute-done | bytes 151584 | tf_op jit(solution)/shard_map/ppermute | solution.py:805
  71.9 1.2 %coarse_ready.1 = (f32[8,8,256]{2,1,0:T(8,128)S(1)}, f32[8,128]{1,0:T(8,128)S(1)}) custom-call(f32[8,8,256]{2,1,0:T(8,128)S(1)} %get-tuple-element.74.token.coarse.own, f32[148,256]{1,0:T(8,128)S(1)} %collective-permute-done.14.r_a.yy_a.far_a, f32[148,256]{1,0:T(8,128)S(1)} %collective-permute-done.15.r_b.yy_b.far_b), custom_call_target="tpu_custom_call" | custom-call | flops 1000000 | bytes 438272 | tf_op jit(solution)/shard_map/coarse_ready/pallas_call | solution.py:36
  73.2 1.1 %middle.1 = (f32[24,24,256]{2,1,0:T(8,128)S(1)}, f32[24,24,256]{2,1,0:T(8,128)S(1)}, f32[24,24,256]{2,1,0:T(8,128)S(1)}, f32[8,12,256]{2,1,0:T(8,128)S(1)}, f32[...) custom-call(f32[16,16,256]{2,1,0:T(8,128)S(1)} %get-tuple-element.110.field.source_, ...), custom_call_target="tpu_custom_call" | custom-call | flops 1000000 | bytes 3747840 | tf_op jit(solution)/shard_map/middle/pallas_call | solution.py:36
  74.2 2.2 %collective-permute-start.21 = (f32[80,256]{1,0:T(8,128)S(1)}, f32[80,256]{1,0:T(8,128)S(1)}, u32[]{:S(2)}, u32[]{:S(2)}) collective-permute-start(f32[80,256]{1,0:T(8,128)S(1)} %get-tuple-element.124), channel_id=1, source_target_pairs={{0,1},{2,3},{4,5},{6,7},{1,0},{3,2},{5,4},{7,6},{8,9},{10,11},{12,... | collective-permute-start | bytes 245768 | tf_op jit(solution)/shard_map/ppermute | solution.py:805
  77.1 1.7 %collective-permute-done.21.r_b = f32[80,256]{1,0:T(8,128)S(1)} collective-permute-done((f32[80,256]{1,0:T(8,128)S(1)}, f32[80,256]{1,0:T(8,128)S(1)}, u32[]{:S(2)}, u32[]{:S(2)}) %collective-permute-start.21) | collective-permute-done | bytes 81952 | tf_op jit(solution)/shard_map/ppermute | solution.py:805
  78.9 1.5 %collective-permute-start.22 = (f32[8,256]{1,0:T(8,128)S(1)}, f32[8,256]{1,0:T(8,128)S(1)}, u32[]{:S(2)}, u32[]{:S(2)}) collective-permute-start(f32[8,256]{1,0:T(8,128)S(1)} %slice_add_fusion.rest_0_), channel_id=1, source_target_pairs={{0,6},{1,7},{2,4},{3,5},{4,2},{5,3},{6,0},{7,1},{8,14},{9,15},{10,... | collective-permute-start | bytes 24584 | tf_op jit(solution)/shard_map/ppermute | solution.py:809
  81.0 1.4 %collective-permute-start.24 = (f32[8,256]{1,0:T(8,128)S(1)}, f32[8,256]{1,0:T(8,128)S(1)}, u32[]{:S(2)}, u32[]{:S(2)}) collective-permute-start(f32[8,256]{1,0:T(8,128)S(1)} %slice_add_fusion.rest_0_), channel_id=1, source_target_pairs={{0,2},{1,3},{2,0},{3,1},{4,6},{5,7},{6,4},{7,5},{8,10},{9,11},{10,... | collective-permute-start | bytes 24584 | tf_op jit(solution)/shard_map/ppermute | solution.py:809
  82.4 1.2 %coarse.1.error = f32[8,16,256]{2,1,0:T(8,128)S(1)} custom-call(f32[8,12,256]{2,1,0:T(8,128)S(1)} %get-tuple-element.121.own, f32[8,12,256]{2,1,0:T(8,128)S(1)} %get-tuple-element.122.conduct, f32[148,256]{1,0:T(8,128)S(1)} %collective-permute-done.14.r_a.yy_a.far_a, f32[148,256]{1,0:T(8,128)S(1)} %collective-permute-done.15.r_b.yy_b.far_b, ...), custom_call_target="tpu_custom_call" | custom-call | flops 1000000 | bytes 786432 | tf_op jit(solution)/shard_map/coarse/pallas_call | solution.py:36
  84.0 5.0 %collective-permute-start.25 = (f32[2,16,256]{2,1,0:T(8,128)S(1)}, f32[2,16,256]{2,1,0:T(8,128)S(1)}, u32[]{:S(2)}, u32[]{:S(2)}) collective-permute-start(f32[2,16,256]{2,1,0:T(8,128)S(1)} %get-tuple-element.126), channel_id=1, source_target_pairs={{8,16},{16,8},{9,17},{17,9},{10,18},{18,10},{11,19},{19,11},{12,20... | collective-permute-start | bytes 98312 | tf_op jit(solution)/shard_map/ppermute | solution.py:805
  89.1 2.5 %finish_inner.1 = (f32[32,32,256]{2,1,0:T(8,128)}, f32[24,24,256]{2,1,0:T(8,128)S(1)}, f32[24,24,256]{2,1,0:T(8,128)S(1)}, f32[40,40,256]{2,1,0:T(8,128)S(1)}, f32[40,40,256]{2,1,0:T(8,128)S(1)}) custom-call(f32[8,16,256]{2,1,0:T(8,128)S(1)} %get-tuple-element.133.error, f32[24,24,256]{2,1,0:T(8,128)S(1)} %get-tuple-element.128.mid_two, ...), custom_call_target="tpu_custom_call" | custom-call | flops 1000000 | bytes 12320768 | tf_op jit(solution)/shard_map/finish_inner/pallas_call | solution.py:36
  91.6 1.7 %finish_edge.1 = f32[32,32,256]{2,1,0:T(8,128)} custom-call(f32[2,16,256]{2,1,0:T(8,128)S(1)} %collective-permute-done.25.x_a, f32[2,16,256]{2,1,0:T(8,128)S(1)} %collective-permute-done.26.x_b, f32[24,24,256]{2,1,0:T(8,128)S(1)} %get-tuple-element.128.mid_two, f32[24,24,256]{2,1,0:T(8,128)S(1)} %get-tuple-element.129.mid_source, ...), custom_call_target="tpu_custom_call", output_to_operand_aliasing={{}: (14, {})} | custom-call | flops 1000000 | bytes 14614528 | tf_op jit(solution)/shard_map/finish_edge/pallas_call | solution.py:36
  (57 shorter events, 10.3 us)
Async XLA Ops:
  0.6 7.5 %copy-start.1 = (f32[32,32,256]{2,1,0:T(8,128)S(1)}, f32[32,32,256]{2,1,0:T(8,128)}, u32[]{:S(2)}) copy-start(f32[32,32,256]{2,1,0:T(8,128)} %conc.9) | copy-start | bytes 3145732
  0.6 7.5 %copy-start = (s32[32,32,256]{2,1,0:T(8,128)S(1)}, s32[32,32,256]{2,1,0:T(8,128)}, u32[]{:S(2)}) copy-start(s32[32,32,256]{2,1,0:T(8,128)} %label.11) | copy-start | bytes 3145732
  2.8 7.9 %collective-permute-start = (f32[224,256]{1,0:T(8,128)}, f32[224,256]{1,0:T(8,128)S(1)}, u32[]{:S(2)}, u32[]{:S(2)}) collective-permute-start(f32[224,256]{1,0:T(8,128)} %get-tuple-element.71), channel_id=1, source_target_pairs={{1,2},{3,4},{5,6},{2,1},{4,3},{6,5},{9,10},{11,12},{13,14},{10,9},... | collective-permute-start | bytes 688136 | tf_op jit(solution)/shard_map/ppermute | solution.py:805
  3.5 14.7 %collective-permute-start.1 = (f32[224,256]{1,0:T(8,128)}, f32[224,256]{1,0:T(8,128)S(1)}, u32[]{:S(2)}, u32[]{:S(2)}) collective-permute-start(f32[224,256]{1,0:T(8,128)} %get-tuple-element.72), channel_id=1, source_target_pairs={{0,1},{2,3},{4,5},{6,7},{1,0},{3,2},{5,4},{7,6},{8,9},{10,11},{12,... | collective-permute-start | bytes 688136 | tf_op jit(solution)/shard_map/ppermute | solution.py:805
  8.1 1.2 %copy-start.2 = (f32[32,32,256]{2,1,0:T(8,128)S(1)}, f32[32,32,256]{2,1,0:T(8,128)}, u32[]{:S(2)}) copy-start(f32[32,32,256]{2,1,0:T(8,128)} %phi.9) | copy-start | bytes 3145732
  10.7 21.6 %copy-start.3 = (f32[32,32,256]{2,1,0:T(8,128)S(1)}, f32[32,32,256]{2,1,0:T(8,128)}, u32[]{:S(2)}) copy-start(f32[32,32,256]{2,1,0:T(8,128)} %phi.9) | copy-start | bytes 3145732
  18.2 16.1 %copy-start.4 = (f32[32,32,256]{2,1,0:T(8,128)S(1)}, f32[32,32,256]{2,1,0:T(8,128)}, u32[]{:S(2)}) copy-start(f32[32,32,256]{2,1,0:T(8,128)} %solid.3) | copy-start | bytes 3145732
  18.3 20.1 %collective-permute-start.2 = (f32[35,8,256]{2,1,0:T(8,128)S(1)}, f32[35,8,256]{2,1,0:T(8,128)S(1)}, u32[]{:S(2)}, u32[]{:S(2)}) collective-permute-start(f32[35,8,256]{2,1,0:T(8,128)S(1)} %get-tuple-element.75), channel_id=1, source_target_pairs={{8,16},{16,8},{9,17},{17,9},{10,18},{18,10},{11,19},{19,11},{12,20... | collective-permute-start | bytes 860168 | tf_op jit(solution)/shard_map/ppermute | solution.py:805
  22.0 16.5 %collective-permute-start.3 = (f32[35,8,256]{2,1,0:T(8,128)S(1)}, f32[35,8,256]{2,1,0:T(8,128)S(1)}, u32[]{:S(2)}, u32[]{:S(2)}) collective-permute-start(f32[35,8,256]{2,1,0:T(8,128)S(1)} %get-tuple-element.76), channel_id=1, source_target_pairs={{0,8},{16,24},{8,0},{24,16},{1,9},{17,25},{9,1},{25,17},{2,10},{18... | collective-permute-start | bytes 860168 | tf_op jit(solution)/shard_map/ppermute | solution.py:805
  22.0 5.7 %collective-permute-start.4 = (f32[2,256]{1,0:T(2,128)S(1)}, f32[2,256]{1,0:T(2,128)S(1)}, u32[]{:S(2)}, u32[]{:S(2)}) collective-permute-start(f32[2,256]{1,0:T(2,128)S(1)} %get-tuple-element.89), channel_id=1, source_target_pairs={{0,4},{1,5},{2,6},{3,7},{4,0},{5,1},{6,2},{7,3},{8,12},{9,13},{10,... | collective-permute-start | bytes 6152 | tf_op jit(solution)/shard_map/ppermute | solution.py:809
  25.3 7.0 %collective-permute-start.6 = (f32[24,8,256]{2,1,0:T(8,128)S(1)}, f32[24,8,256]{2,1,0:T(8,128)S(1)}, u32[]{:S(2)}, u32[]{:S(2)}) collective-permute-start(f32[24,8,256]{2,1,0:T(8,128)S(1)} %get-tuple-element.90), channel_id=1, source_target_pairs={{8,16},{16,8},{9,17},{17,9},{10,18},{18,10},{11,19},{19,11},{12,20... | collective-permute-start | bytes 589832 | tf_op jit(solution)/shard_map/ppermute | solution.py:805
  27.6 4.7 %collective-permute-start.7 = (f32[24,8,256]{2,1,0:T(8,128)S(1)}, f32[24,8,256]{2,1,0:T(8,128)S(1)}, u32[]{:S(2)}, u32[]{:S(2)}) collective-permute-start(f32[24,8,256]{2,1,0:T(8,128)S(1)} %get-tuple-element.91), channel_id=1, source_target_pairs={{0,8},{16,24},{8,0},{24,16},{1,9},{17,25},{9,1},{25,17},{2,10},{18... | collective-permute-start | bytes 589832 | tf_op jit(solution)/shard_map/ppermute | solution.py:805
  27.7 2.5 %collective-permute-start.5 = (f32[4,256]{1,0:T(4,128)S(1)}, f32[4,256]{1,0:T(4,128)S(1)}, u32[]{:S(2)}, u32[]{:S(2)}) collective-permute-start(f32[4,256]{1,0:T(4,128)S(1)} %pad_maximum_fusion.1), channel_id=1, source_target_pairs={{0,2},{1,3},{2,0},{3,1},{4,6},{5,7},{6,4},{7,5},{8,10},{9,11},{10,... | collective-permute-start | bytes 12296 | tf_op jit(solution)/shard_map/ppermute | solution.py:809
  32.4 13.1 %collective-permute-start.8 = (f32[148,256]{1,0:T(8,128)S(1)}, f32[148,256]{1,0:T(8,128)S(1)}, u32[]{:S(2)}, u32[]{:S(2)}) collective-permute-start(f32[148,256]{1,0:T(8,128)S(1)} %get-tuple-element.92), channel_id=1, source_target_pairs={{0,1},{2,3},{4,5},{6,7},{1,0},{3,2},{5,4},{7,6},{8,9},{10,11},{12,... | collective-permute-start | bytes 454664 | tf_op jit(solution)/shard_map/ppermute | solution.py:805
  33.7 12.7 %collective-permute-start.11 = (f32[140,256]{1,0:T(8,128)S(1)}, f32[140,256]{1,0:T(8,128)S(1)}, u32[]{:S(2)}, u32[]{:S(2)}) collective-permute-start(f32[140,256]{1,0:T(8,128)S(1)} %get-tuple-element.99), channel_id=1, source_target_pairs={{1,2},{3,4},{5,6},{2,1},{4,3},{6,5},{9,10},{11,12},{13,14},{10,9},... | collective-permute-start | bytes 430088 | tf_op jit(solution)/shard_map/ppermute | solution.py:805
  39.7 7.6 %collective-permute-start.9 = (f32[96,256]{1,0:T(8,128)S(1)}, f32[96,256]{1,0:T(8,128)S(1)}, u32[]{:S(2)}, u32[]{:S(2)}) collective-permute-start(f32[96,256]{1,0:T(8,128)S(1)} %get-tuple-element.96), channel_id=1, source_target_pairs={{1,2},{3,4},{5,6},{2,1},{4,3},{6,5},{9,10},{11,12},{13,14},{10,9},... | collective-permute-start | bytes 294920 | tf_op jit(solution)/shard_map/ppermute | solution.py:805
  40.3 9.0 %collective-permute-start.10 = (f32[96,256]{1,0:T(8,128)S(1)}, f32[96,256]{1,0:T(8,128)S(1)}, u32[]{:S(2)}, u32[]{:S(2)}) collective-permute-start(f32[96,256]{1,0:T(8,128)S(1)} %get-tuple-element.97), channel_id=1, source_target_pairs={{0,1},{2,3},{4,5},{6,7},{1,0},{3,2},{5,4},{7,6},{8,9},{10,11},{12,... | collective-permute-start | bytes 294920 | tf_op jit(solution)/shard_map/ppermute | solution.py:805
  49.4 6.2 %collective-permute-start.12 = (f32[15,8,256]{2,1,0:T(8,128)S(1)}, f32[15,8,256]{2,1,0:T(8,128)S(1)}, u32[]{:S(2)}, u32[]{:S(2)}) collective-permute-start(f32[15,8,256]{2,1,0:T(8,128)S(1)} %get-tuple-element.101), channel_id=1, source_target_pairs={{8,16},{16,8},{9,17},{17,9},{10,18},{18,10},{11,19},{19,11},{12,20... | collective-permute-start | bytes 368648 | tf_op jit(solution)/shard_map/ppermute | solution.py:805
  51.7 3.9 %collective-permute-start.13 = (f32[15,8,256]{2,1,0:T(8,128)S(1)}, f32[15,8,256]{2,1,0:T(8,128)S(1)}, u32[]{:S(2)}, u32[]{:S(2)}) collective-permute-start(f32[15,8,256]{2,1,0:T(8,128)S(1)} %get-tuple-element.102), channel_id=1, source_target_pairs={{0,8},{16,24},{8,0},{24,16},{1,9},{17,25},{9,1},{25,17},{2,10},{18... | collective-permute-start | bytes 368648 | tf_op jit(solution)/shard_map/ppermute | solution.py:805
  56.2 10.4 %collective-permute-start.16 = (f32[64,256]{1,0:T(8,128)S(1)}, f32[64,256]{1,0:T(8,128)S(1)}, u32[]{:S(2)}, u32[]{:S(2)}) collective-permute-start(f32[64,256]{1,0:T(8,128)S(1)} %get-tuple-element.114), channel_id=1, source_target_pairs={{1,2},{3,4},{5,6},{2,1},{4,3},{6,5},{9,10},{11,12},{13,14},{10,9},... | collective-permute-start | bytes 196616 | tf_op jit(solution)/shard_map/ppermute | solution.py:805
  56.8 9.8 %collective-permute-start.17 = (f32[64,256]{1,0:T(8,128)S(1)}, f32[64,256]{1,0:T(8,128)S(1)}, u32[]{:S(2)}, u32[]{:S(2)}) collective-permute-start(f32[64,256]{1,0:T(8,128)S(1)} %get-tuple-element.115), channel_id=1, source_target_pairs={{0,1},{2,3},{4,5},{6,7},{1,0},{3,2},{5,4},{7,6},{8,9},{10,11},{12,... | collective-permute-start | bytes 196616 | tf_op jit(solution)/shard_map/ppermute | solution.py:805
  62.0 8.9 %collective-permute-start.14 = (f32[148,256]{1,0:T(8,128)S(1)}, f32[148,256]{1,0:T(8,128)S(1)}, u32[]{:S(2)}, u32[]{:S(2)}) collective-permute-start(f32[148,256]{1,0:T(8,128)S(1)} %get-tuple-element.112), channel_id=1, source_target_pairs={{1,2},{3,4},{5,6},{2,1},{4,3},{6,5},{9,10},{11,12},{13,14},{10,9},... | collective-permute-start | bytes 454664 | tf_op jit(solution)/shard_map/ppermute | solution.py:805
  62.7 9.2 %collective-permute-start.15 = (f32[148,256]{1,0:T(8,128)S(1)}, f32[148,256]{1,0:T(8,128)S(1)}, u32[]{:S(2)}, u32[]{:S(2)}) collective-permute-start(f32[148,256]{1,0:T(8,128)S(1)} %get-tuple-element.113), channel_id=1, source_target_pairs={{0,1},{2,3},{4,5},{6,7},{1,0},{3,2},{5,4},{7,6},{8,9},{10,11},{12,... | collective-permute-start | bytes 454664 | tf_op jit(solution)/shard_map/ppermute | solution.py:805
  66.7 6.5 %collective-permute-start.18 = (f32[12,8,256]{2,1,0:T(8,128)S(1)}, f32[12,8,256]{2,1,0:T(8,128)S(1)}, u32[]{:S(2)}, u32[]{:S(2)}) collective-permute-start(f32[12,8,256]{2,1,0:T(8,128)S(1)} %get-tuple-element.117), channel_id=1, source_target_pairs={{8,16},{16,8},{9,17},{17,9},{10,18},{18,10},{11,19},{19,11},{12,20... | collective-permute-start | bytes 294920 | tf_op jit(solution)/shard_map/ppermute | solution.py:805
  70.9 2.3 %collective-permute-start.19 = (f32[12,8,256]{2,1,0:T(8,128)S(1)}, f32[12,8,256]{2,1,0:T(8,128)S(1)}, u32[]{:S(2)}, u32[]{:S(2)}) collective-permute-start(f32[12,8,256]{2,1,0:T(8,128)S(1)} %get-tuple-element.118), channel_id=1, source_target_pairs={{0,8},{16,24},{8,0},{24,16},{1,9},{17,25},{9,1},{25,17},{2,10},{18... | collective-permute-start | bytes 294920 | tf_op jit(solution)/shard_map/ppermute | solution.py:805
  74.2 4.6 %collective-permute-start.21 = (f32[80,256]{1,0:T(8,128)S(1)}, f32[80,256]{1,0:T(8,128)S(1)}, u32[]{:S(2)}, u32[]{:S(2)}) collective-permute-start(f32[80,256]{1,0:T(8,128)S(1)} %get-tuple-element.124), channel_id=1, source_target_pairs={{0,1},{2,3},{4,5},{6,7},{1,0},{3,2},{5,4},{7,6},{8,9},{10,11},{12,... | collective-permute-start | bytes 245768 | tf_op jit(solution)/shard_map/ppermute | solution.py:805
  76.5 5.9 %collective-permute-start.20 = (f32[72,256]{1,0:T(8,128)S(1)}, f32[72,256]{1,0:T(8,128)S(1)}, u32[]{:S(2)}, u32[]{:S(2)}) collective-permute-start(f32[72,256]{1,0:T(8,128)S(1)} %get-tuple-element.123), channel_id=1, source_target_pairs={{1,2},{3,4},{5,6},{2,1},{4,3},{6,5},{9,10},{11,12},{13,14},{10,9},... | collective-permute-start | bytes 221192 | tf_op jit(solution)/shard_map/ppermute | solution.py:805
  78.9 4.7 %collective-permute-start.22 = (f32[8,256]{1,0:T(8,128)S(1)}, f32[8,256]{1,0:T(8,128)S(1)}, u32[]{:S(2)}, u32[]{:S(2)}) collective-permute-start(f32[8,256]{1,0:T(8,128)S(1)} %slice_add_fusion.rest_0_), channel_id=1, source_target_pairs={{0,6},{1,7},{2,4},{3,5},{4,2},{5,3},{6,0},{7,1},{8,14},{9,15},{10,... | collective-permute-start | bytes 24584 | tf_op jit(solution)/shard_map/ppermute | solution.py:809
  80.4 3.5 %collective-permute-start.23 = (f32[8,256]{1,0:T(8,128)S(1)}, f32[8,256]{1,0:T(8,128)S(1)}, u32[]{:S(2)}, u32[]{:S(2)}) collective-permute-start(f32[8,256]{1,0:T(8,128)S(1)} %slice_add_fusion.rest_0_), channel_id=1, source_target_pairs={{0,4},{1,5},{2,6},{3,7},{4,0},{5,1},{6,2},{7,3},{8,12},{9,13},{10,... | collective-permute-start | bytes 24584 | tf_op jit(solution)/shard_map/ppermute | solution.py:809
  81.0 2.9 %collective-permute-start.24 = (f32[8,256]{1,0:T(8,128)S(1)}, f32[8,256]{1,0:T(8,128)S(1)}, u32[]{:S(2)}, u32[]{:S(2)}) collective-permute-start(f32[8,256]{1,0:T(8,128)S(1)} %slice_add_fusion.rest_0_), channel_id=1, source_target_pairs={{0,2},{1,3},{2,0},{3,1},{4,6},{5,7},{6,4},{7,5},{8,10},{9,11},{10,... | collective-permute-start | bytes 24584 | tf_op jit(solution)/shard_map/ppermute | solution.py:809
  84.0 7.6 %collective-permute-start.25 = (f32[2,16,256]{2,1,0:T(8,128)S(1)}, f32[2,16,256]{2,1,0:T(8,128)S(1)}, u32[]{:S(2)}, u32[]{:S(2)}) collective-permute-start(f32[2,16,256]{2,1,0:T(8,128)S(1)} %get-tuple-element.126), channel_id=1, source_target_pairs={{8,16},{16,8},{9,17},{17,9},{10,18},{18,10},{11,19},{19,11},{12,20... | collective-permute-start | bytes 98312 | tf_op jit(solution)/shard_map/ppermute | solution.py:805
  89.0 2.6 %collective-permute-start.26 = (f32[2,16,256]{2,1,0:T(8,128)S(1)}, f32[2,16,256]{2,1,0:T(8,128)S(1)}, u32[]{:S(2)}, u32[]{:S(2)}) collective-permute-start(f32[2,16,256]{2,1,0:T(8,128)S(1)} %get-tuple-element.127), channel_id=1, source_target_pairs={{0,8},{16,24},{8,0},{24,16},{1,9},{17,25},{9,1},{25,17},{2,10},{18... | collective-permute-start | bytes 98312 | tf_op jit(solution)/shard_map/ppermute | solution.py:805
  (1 other events, 0.7 us)

commit v7 on v5

--- a/solution.py
+++ b/solution.py
@@ -31,7 +31,7 @@
 FAR = pl.BlockSpec(memory_space=pltpu.HBM)
 
 
-def call(kernel, outs, args, scratch=(), in_specs=None, out_specs=None, limit=VMEM_LIMIT, aliases=None, flops=10**6, name=None):
+def call(kernel, outs, args, scratch=(), in_specs=None, out_specs=None, limit=VMEM_LIMIT, aliases=None, name=None):
     size = sum(4 * a.size for a in args) + sum(4 * o.size for o in outs)
     return pl.pallas_call(
         kernel,
@@ -41,7 +41,7 @@
         scratch_shapes=list(scratch),
         input_output_aliases=aliases or {},
         compiler_params=pltpu.CompilerParams(vmem_limit_bytes=limit),
-        cost_estimate=pl.CostEstimate(flops=flops, bytes_accessed=size, transcendentals=0),
+        cost_estimate=pl.CostEstimate(flops=10**6, bytes_accessed=size, transcendentals=0),
         name=name,
     )(*args)
 
@@ -218,10 +218,10 @@
 
 def second_rows(nx):
     phi, mid = (sum(corner_rows(n, reach)[0]) for n, reach in ((nx, 0), (nx // 2, 1)))
-    return phi, phi + mid, phi + mid + 64
-
-
-def second_pack_kernel(phi, mid, coarse, lists, x_a, x_b, pay_a, pay_b):
+    return phi, phi + mid
+
+
+def second_pack_kernel(phi, mid, x_a, x_b, pay_a, pay_b):
     nx = phi.shape[0]
     starts = second_rows(nx)
 
@@ -239,12 +239,6 @@
 
     put(phi, nx, 0, 0, 0)
     put(mid, nx // 2, 1, 16, starts[0])
-    base = starts[1]
-    for x in range(8):
-        pay_a[base + 8 * x : base + 8 * x + 8, :] = coarse[x]
-        pay_b[base + 8 * x : base + 8 * x + 8, :] = coarse[x]
-    base = starts[2]
-    pay_b[base : base + lists.shape[0], :] = lists[...]
 
 
 def second_halo(r_a, r_b, n, reach, x, base):
@@ -304,7 +298,7 @@
 
 
 def sweeps_edge_kernel(
-    x_a, x_b, label, phi, solid, gain, base, zero, first, second, third, gain_far, base_far, out_inner, flux_inner,
+    x_a, x_b, label, phi, solid, gain, base, zero, first, second, third, gain_far, base_far, out_inner, flux_inner, lists,
     out, flux, pay_a, pay_b, zero_x, first_x, second_x, third_x,
 ):
     nx = out.shape[0]
@@ -348,24 +342,25 @@
                     flux[plane(k)] = flux_plane(c, solid[plane(k)], phi[plane(k)], label[plane(k)])
     for x in range(nx):
         send_y(pay_a, pay_b, 3 * x, flux[x, 0:3, :], flux[x, 29:32, :])
-
-
-def mask_kernel(flux_all, lists, far, flux, halo_mask, marked):
+    pay_b[3 * nx : 3 * nx + lists.shape[0], :] = lists[...]
+
+
+def mask_kernel(flux_all, lists, far, token, token_2, flux, halo_mask, marked):
     nx = flux_all.shape[0]
     rows = lists.shape[0]
     pieces = [lists[i : i + 1, :] for i in range(rows)] + [far[i : i + 1, :] for i in range(far.shape[0] - rows, far.shape[0])]
     owner = jnp.concatenate(pieces[0::2], axis=1).astype(jnp.int32)
     block = jnp.concatenate(pieces[1::2], axis=1).astype(jnp.int32)
     entries = owner.shape[1]
-    hit_column = (iota((LANES, entries), 0) == lax.rem(block, 64)).astype(jnp.bfloat16)
-    at_row = lax.shift_right_arithmetic(block, 6)
-    here = lax.axis_index("dev")
+    hit_column = (iota((64, entries), 0) == lax.rem(block, 64)).astype(jnp.bfloat16)
+    reach = owner - lax.axis_index("dev") + 1
+    at_row = jnp.where((reach >= 0) & (reach < 3), reach * nx + lax.shift_right_arithmetic(block, 6), -1)
+    hit_row = (iota((3 * nx, entries), 0) == at_row).astype(jnp.bfloat16)
+    named = lax.dot_general(hit_row, hit_column, (((1,), (1,)), ((), ())), preferred_element_type=F32)
+    named = jnp.concatenate([named, jnp.zeros((3 * nx, LANES - 64), F32)], axis=1)
     for j in range(3):
-        mine = jnp.where(owner == here + j - 1, at_row, -1)
-        hit_row = (iota((nx, entries), 0) == mine).astype(jnp.bfloat16)
-        named = lax.dot_general(hit_row, hit_column, (((1,), (1,)), ((), ())), preferred_element_type=F32)
         for i in range(nx):
-            marked[j, i] = jnp.broadcast_to(named[i : i + 1, :], (8, LANES))
+            marked[j, i] = jnp.broadcast_to(named[j * nx + i : j * nx + i + 1, :], (8, LANES))
     is_row = lax.div(iota((32, LANES), 1), 2) == iota((32, LANES), 0)
     row, pair = iota((8, LANES), 0), lax.div(iota((8, LANES), 1), 2)
     is_after = (row < 3) & (pair == row)
@@ -380,7 +375,7 @@
         flux[i] = jnp.where(listed[0:32], flux_all[i], 0.0)
         halo_mask[i] = jnp.where(listed[32:40], 1.0, 0.0)
 
-    loop(0, nx, plane, 4)
+    loop(0, nx, plane, 16)
 
 
 def store_kernel(conc, flux, conc_out, flux_out, token, sems):
@@ -395,39 +390,48 @@
         c.wait()
 
 
-def ready_kernel(conc, label, phi, y_a, y_b, x_a, x_b, yy_a, yy_b, xx_a, xx_b, weight, scale, field, token):
+def ready_kernel(conc, label, y_a, y_b, x_a, x_b, weight, scale, token):
     nx = conc.shape[0]
     token[...] = jnp.zeros(token.shape, F32)
 
-    def put(x, rows, c, lab, p):
+    def put(x, rows, c, lab):
         conduct = c * pick(lab, CONDUCT_TABLE)
         factor = OMEGA / (MASS + 6.0 * conduct)
         weight[x, rows, :] = conduct * factor
         scale[x, rows, :] = factor
-        field[x, rows, :] = p
 
     def own(i):
-        put(HALO + i, slice(0, 32), conc[i], label[i], phi[i])
+        put(HALO + i, slice(0, 32), conc[i], label[i])
 
     loop(0, nx, own, 4)
-    low = slice(32, 40)
     for i in range(nx):
         c = halo_tile(*y_sides(y_a, y_b, 7 * i, 4))
         lab = halo_tile(*y_sides(y_a, y_b, 7 * i + 4, 3))
-        put(HALO + i, low, c, lab, second_halo(yy_a, yy_b, nx, 0, HALO + i, 0))
+        put(HALO + i, slice(32, 40), c, lab)
     for t in range(5):
         rows = slice(8 * t, 8 * t + 8)
         for k in range(HALO):
             c_after, c_before = x_sides(x_a, x_b, 5 * k + t)
             l_after = x_sides(x_a, x_b, 20 + 5 * min(k, 2) + t)[0]
             l_before = x_sides(x_a, x_b, 20 + 5 * max(k - 1, 0) + t)[1]
-            if t < 4:
-                p_after, p_before = x_sides(xx_a, xx_b, 4 * k + t)
-            else:
-                p_after = second_halo(yy_a, yy_b, nx, 0, HALO + nx + k, 0)
-                p_before = second_halo(yy_a, yy_b, nx, 0, k, 0)
-            put(k, rows, c_before, l_before, p_before)
-            put(HALO + nx + k, rows, c_after, l_after, p_after)
+            put(k, rows, c_before, l_before)
+            put(HALO + nx + k, rows, c_after, l_after)
+
+
+def place_phi(phi, yy_a, yy_b, xx_a, xx_b, field):
+    nx = phi.shape[0]
+
+    def own(i):
+        field[HALO + i, 0:32, :] = phi[i]
+
+    loop(0, nx, own)
+    for x in range(nx + 2 * HALO):
+        field[x, 32:40, :] = second_halo(yy_a, yy_b, nx, 0, x, 0)
+    for t in range(4):
+        for k in range(HALO):
+            after, before = x_sides(xx_a, xx_b, 4 * k + t)
+            field[k, 8 * t : 8 * t + 8, :] = before
+            field[HALO + nx + k, 8 * t : 8 * t + 8, :] = after
 
 
 def flux_pack_x_kernel(flux, r_a, r_b, mask, token, pay_a, pay_b):
@@ -450,8 +454,11 @@
     return b, 0.2 * p[rows, :] + weight[x, rows, :] * near[rows, :] + b
 
 
-def potential_inner_kernel(flux, mask, y_a, y_b, weight, scale, field, after_two, source, first, source_mid, far, pairs):
+def potential_inner_kernel(
+    flux, mask, y_a, y_b, phi, yy_a, yy_b, xx_a, xx_b, weight, scale, after_two, source, first, source_mid, field, far, pairs
+):
     nx = flux.shape[0]
+    place_phi(phi, yy_a, yy_b, xx_a, xx_b, field)
     for i in range(nx):
         far[i] = mask[i] * halo_tile(*y_sides(y_a, y_b, 3 * i, 3))
 
@@ -485,7 +492,7 @@
 
 def potential_edge_kernel(
     x_a, x_b, weight, scale, field, inner_two, inner_source, inner_first, inner_mid,
-    edge_two, edge_source, source_mid, pay_a, pay_b, first, pairs,
+    coarse, edge_two, edge_source, source_mid, pay_a, pay_b, first, pairs,
 ):
     half = source_mid.shape[0]
     nx = 2 * half
@@ -520,9 +527,13 @@
         source_mid[x] = inner_mid[x]
     for x in range(half):
         send_y(pay_a, pay_b, 4 * x, source_mid[x, 0:4, :], source_mid[x, 12:16, :])
-
-
-def mid_pack_x_kernel(field, r_a, r_b, token, token_2, pay_a, pay_b):
+    base = 4 * half
+    for x in range(8):
+        pay_a[base + 8 * x : base + 8 * x + 8, :] = coarse[x]
+        pay_b[base + 8 * x : base + 8 * x + 8, :] = coarse[x]
+
+
+def mid_pack_x_kernel(field, r_a, r_b, token, pay_a, pay_b):
     n = field.shape[0]
 
     def tile(x, t):
@@ -598,8 +609,7 @@
 COARSE_W = 0.0625
 
 
-def coarse_ready_kernel(own, r_a, r_b, rho, load, token, one, two, conduct, scale):
-    token[...] = jnp.zeros(token.shape, F32)
+def coarse_ready_kernel(own, r_a, r_b, rho, load, one, two, conduct, scale):
     base = r_a.shape[0] - 64
     for x in range(8):
         after, before = y_sides(r_a, r_b, base + 8 * x, 8)
@@ -841,22 +851,19 @@
         name="own",
     )
     xx_a, xx_b = swap(pay_a, pay_b, "grp")
-    distance = peers // 2
-    while distance > 1:
-        lists = jnp.concatenate([lists, exchange(lists, distance)], axis=0)
-        distance //= 2
-    far_rows = second_rows(nx)[2]
+    lists = jnp.concatenate([lists] + [exchange(lists, distance) for distance in range(peers - 2, 0, -2)], axis=0)
+    far_rows = second_rows(nx)[1]
     far_pay = call(
         second_pack_kernel,
-        [shaped(far_rows, 256), shaped(far_rows + peers, 256)],
-        [phi_old, conduct_mid, conduct_coarse, lists, xx_a, xx_b],
+        [shaped(far_rows, 256)] * 2,
+        [phi_old, conduct_mid, xx_a, xx_b],
         name="second_pack",
     )
     yy_a, yy_b = swap(*far_pay, "dev")
     pay_a, pay_b = call(
         first_pack_x_kernel,
         [shaped(35, 8, 256)] * 2,
-        [conc_old, phase_label, y_a, y_b, conduct_coarse],
+        [conc_old, phase_label, y_a, y_b, lists],
         name="first_pack_x",
     )
     x_a, x_b = swap(pay_a, pay_b, "grp")
@@ -871,8 +878,8 @@
     edge_args = [x_a, x_b, phase_label, phi_old, solid_pot, gain, base, zero, first, second, third]
     conc_new, flux_all, pay_a, pay_b = call(
         sweeps_edge_kernel,
-        [shaped(nx, nx, 256), shaped(nx, nx, 256), shaped(3 * nx, 256), shaped(3 * nx, 256)],
-        edge_args + [gain_far, base_far, conc_inner, flux_inner],
+        [shaped(nx, nx, 256), shaped(nx, nx, 256), shaped(3 * nx, 256), shaped(3 * nx + peers, 256)],
+        edge_args + [gain_far, base_far, conc_inner, flux_inner, lists],
         [vmem(16, nx + 2 * HALO, 256)] * 4,
         name="sweeps_edge",
     )
@@ -880,32 +887,32 @@
     flux_own, halo_mask = call(
         mask_kernel,
         [shaped(nx, nx, 256), shaped(nx, 8, 256)],
-        [flux_all, lists, yy_b],
+        [flux_all, lists, f_b, yy_a, yy_b],
         [vmem(3, nx, 8, LANES)],
         name="mask",
     )
-    weight, scale, field, made = call(
+    weight, scale, made = call(
         ready_kernel,
-        [shaped(*ext)] * 3 + [token_shape],
-        [conc_old, phase_label, phi_old, y_a, y_b, x_a, x_b, yy_a, yy_b, xx_a, xx_b],
+        [shaped(*ext)] * 2 + [token_shape],
+        [conc_old, phase_label, y_a, y_b, x_a, x_b],
         name="ready",
     )
     pay_a, pay_b = call(
         flux_pack_x_kernel, [shaped(15, 8, 256)] * 2, [flux_own, f_a, f_b, halo_mask, made], name="flux_pack_x"
     )
     fx_a, fx_b = swap(pay_a, pay_b, "grp")
-    fine_two, fine_source, fine_first, inner_mid = call(
+    fine_two, fine_source, fine_first, inner_mid, field = call(
         potential_inner_kernel,
-        [shaped(*ext)] * 3 + [shaped(half, half, 256)],
-        [flux_own, halo_mask, f_a, f_b, weight, scale, field],
+        [shaped(*ext)] * 3 + [shaped(half, half, 256), shaped(*ext)],
+        [flux_own, halo_mask, f_a, f_b, phi_old, yy_a, yy_b, xx_a, xx_b, weight, scale],
         [vmem(nx, 8, 256), vmem(half, 2, nx, LANES)],
         name="potential_inner",
     )
     edge = (16, nx + 2 * HALO, 256)
     edge_two, edge_source, source_mid, pay_a, pay_b = call(
         potential_edge_kernel,
-        [shaped(*edge), shaped(*edge), shaped(half, half, 256), shaped(4 * half, 256), shaped(4 * half, 256)],
-        [fx_a, fx_b, weight, scale, field, fine_two, fine_source, fine_first, inner_mid],
+        [shaped(*edge), shaped(*edge), shaped(half, half, 256)] + [shaped(4 * half + 64, 256)] * 2,
+        [fx_a, fx_b, weight, scale, field, fine_two, fine_source, fine_first, inner_mid, conduct_coarse],
         [vmem(*edge), vmem(2, 2, nx, LANES)],
         name="potential_edge",
     )
@@ -919,15 +926,15 @@
         name="store",
     )
     wide = (quarter, 32, 256)
-    rho, load, made = call(
+    rho, load = call(
         coarse_ready_kernel,
-        [shaped(quarter, quarter, 256), shaped(8, LANES), token_shape],
-        [conduct_coarse, yy_a, yy_b],
+        [shaped(quarter, quarter, 256), shaped(8, LANES)],
+        [conduct_coarse, m_a, m_b],
         [vmem(*wide)] * 4,
         name="coarse_ready",
     )
     pay_a, pay_b = call(
-        mid_pack_x_kernel, [shaped(3 * HALO, 8, 256)] * 2, [source_mid, m_a, m_b, made, stored], name="mid_pack_x"
+        mid_pack_x_kernel, [shaped(3 * HALO, 8, 256)] * 2, [source_mid, m_a, m_b, stored], name="mid_pack_x"
     )
     mx_a, mx_b = swap(pay_a, pay_b, "grp")
     mid_two, mid_source, mid_weight, source_coarse, wide_coarse, pay_a, pay_b, sums = call(
@@ -940,11 +947,11 @@
     )
     c_a, c_b = swap(pay_a, pay_b, "dev")
     sums = sums + c_b[72:80]
-    others = [exchange(sums, distance) for distance in range(2, peers, 2)]
+    others = [exchange(sums, distance) for distance in range(peers - 2, 0, -2)]
     (error,) = call(
         coarse_kernel,
         [shaped(8, 16, 256)],
-        [source_coarse, wide_coarse, yy_a, yy_b, c_a, c_b],
+        [source_coarse, wide_coarse, m_a, m_b, c_a, c_b],
         [vmem(*wide)] * 4,
         name="coarse",
     )

time: 88.5 us -> 90.5 us (1.023)
  waiting for transfers between devices: 9.01 us -> 16.2 us
  starting transfers between devices: 51.4 us -> 47.1 us
    ppermute x10, waiting for transfers between devices: 3.55 us -> 12.6 us  [swap(): lax.ppermute(pay_b, axis, both_ways(pairs_b))]
    ppermute x10, starting transfers between devices: 19.3 us -> 15.1 us  [swap(): lax.ppermute(pay_b, axis, both_ways(pairs_b))]
    ppermute x10, starting transfers between devices: 25.8 us -> 24.3 us  [swap(): lax.ppermute(pay_a, axis, both_ways(pairs_a))]
    ppermute x5 -> x6, starting transfers between devices: 6.36 us -> 7.75 us  [exchange(): lax.ppermute(value, 'dev', [(i, i ^ distance) for i in range(lax.axis_siz...]
    ppermute x5 -> x6, waiting for transfers between devices: 3.12 us -> 1.97 us  [exchange(): lax.ppermute(value, 'dev', [(i, i ^ distance) for i in range(lax.axis_siz...]
    pallas_call x19, Pallas kernels: 24.1 us -> 23.2 us  [call(): pl.pallas_call(kernel, out_shape=tuple(outs), in_specs=in_specs or [WHOLE...]
  transfers between devices with their start and end apart: 25 -> 26, of which waited for: 6 -> 7; matrix products, arithmetic and copies ran while one was open for 0% -> 0% of each run, Pallas kernels for 21% -> 19%
where the time goes in v7:
time: 90.5 us; the launch traced here: 89.6 us
  starting transfers between devices  47.1 us (52%)
  Pallas kernels  23.2 us (26%)
  waiting for transfers between devices  16.2 us (18%)
  local copies, waits for them, and re-layouts  1.94 us (2%)
  between operations  1.05 us (1%)
    ppermute x10, starting transfers between devices, swap(): lax.ppermute(pay_a, axis, both_ways(pairs_a))  24.3 us
    pallas_call x19, Pallas kernels, call(): pl.pallas_call(kernel, out_shape=tuple(outs), in_specs=in_specs or [WHOLE...  23.2 us
    ppermute x10, starting transfers between devices, swap(): lax.ppermute(pay_b, axis, both_ways(pairs_b))  15.1 us
    ppermute x10, waiting for transfers between devices, swap(): lax.ppermute(pay_b, axis, both_ways(pairs_b))  12.6 us
    ppermute x6, starting transfers between devices, exchange(): lax.ppermute(value, 'dev', [(i, i ^ distance) for i in range(lax.axis_siz...  7.75 us
    ppermute x6, waiting for transfers between devices, exchange(): lax.ppermute(value, 'dev', [(i, i ^ distance) for i in range(lax.axis_siz...  1.97 us
    unnamed x12, local copies, waits for them, and re-layouts  1.94 us
  transfers between devices with their start and end apart: 26, of which 7 were waited for; matrix products, arithmetic and copies ran while one was open for 0% of the time, Pallas kernels for 19%

profile of v7, /device:TPU:1, one launch (start us, length us, event | category | flops | bytes accessed | tf_op | source)
XLA Modules:
  0.0 89.6 jit_solution(11916151589224333250)
XLA Ops:
  0.7 2.2 %first_pack.1 = (f32[224,256]{1,0:T(8,128)}, f32[224,256]{1,0:T(8,128)}, f32[8,256]{1,0:T(8,128)}) custom-call(f32[32,32,256]{2,1,0:T(8,128)} %conc.9, s32[32,32,256]{2,1,0:T(8,128)} %label.11, s32[1,256]{1,0:T(1,128)} %bitcast.1, s32[1,256]{1,0:T(1,128)} %block.1), custom_call_target="tpu_custom_call" | custom-call | flops 1000000 | bytes 2566144 | tf_op jit(solution)/shard_map/first_pack/pallas_call | solution.py:36
  3.5 4.6 %collective-permute-start.1 = (f32[224,256]{1,0:T(8,128)}, f32[224,256]{1,0:T(8,128)S(1)}, u32[]{:S(2)}, u32[]{:S(2)}) collective-permute-start(f32[224,256]{1,0:T(8,128)} %get-tuple-element.70), channel_id=1, source_target_pairs={{0,1},{2,3},{4,5},{6,7},{1,0},{3,2},{5,4},{7,6},{8,9},{10,11},{12,... | collective-permute-start | bytes 688136 | tf_op jit(solution)/shard_map/ppermute | solution.py:816
  8.1 1.2 %copy-done.2 = f32[32,32,256]{2,1,0:T(8,128)S(1)} copy-done((f32[32,32,256]{2,1,0:T(8,128)S(1)}, f32[32,32,256]{2,1,0:T(8,128)}, u32[]{:S(2)}) %copy-start.2) | copy-done | bytes 1048600
  10.7 1.4 %collective-permute-start.4 = (f32[2,256]{1,0:T(2,128)S(1)}, f32[2,256]{1,0:T(2,128)S(1)}, u32[]{:S(2)}, u32[]{:S(2)}) collective-permute-start(f32[2,256]{1,0:T(2,128)S(1)} %get-tuple-element.72), channel_id=1, source_target_pairs={{0,2},{1,3},{2,0},{3,1},{4,6},{5,7},{6,4},{7,5},{8,10},{9,11},{10,... | collective-permute-start | bytes 6152 | tf_op jit(solution)/shard_map/ppermute | solution.py:820
  12.1 1.1 %collective-permute-start.3 = (f32[2,256]{1,0:T(2,128)S(1)}, f32[2,256]{1,0:T(2,128)S(1)}, u32[]{:S(2)}, u32[]{:S(2)}) collective-permute-start(f32[2,256]{1,0:T(2,128)S(1)} %get-tuple-element.72), channel_id=1, source_target_pairs={{0,4},{1,5},{2,6},{3,7},{4,0},{5,1},{6,2},{7,3},{8,12},{9,13},{10,... | collective-permute-start | bytes 6152 | tf_op jit(solution)/shard_map/ppermute | solution.py:820
  13.1 1.2 %collective-permute-start.2 = (f32[2,256]{1,0:T(2,128)S(1)}, f32[2,256]{1,0:T(2,128)S(1)}, u32[]{:S(2)}, u32[]{:S(2)}) collective-permute-start(f32[2,256]{1,0:T(2,128)S(1)} %get-tuple-element.72), channel_id=1, source_target_pairs={{0,6},{1,7},{2,4},{3,5},{4,2},{5,3},{6,0},{7,1},{8,14},{9,15},{10,... | collective-permute-start | bytes 6152 | tf_op jit(solution)/shard_map/ppermute | solution.py:820
  14.3 5.1 %collective-permute-start.8 = (f32[24,8,256]{2,1,0:T(8,128)S(1)}, f32[24,8,256]{2,1,0:T(8,128)S(1)}, u32[]{:S(2)}, u32[]{:S(2)}) collective-permute-start(f32[24,8,256]{2,1,0:T(8,128)S(1)} %get-tuple-element.89), channel_id=1, source_target_pairs={{8,16},{16,8},{9,17},{17,9},{10,18},{18,10},{11,19},{19,11},{12,20... | collective-permute-start | bytes 589832 | tf_op jit(solution)/shard_map/ppermute | solution.py:816
  19.6 3.7 %collective-permute-start.5 = (f32[35,8,256]{2,1,0:T(8,128)S(1)}, f32[35,8,256]{2,1,0:T(8,128)S(1)}, u32[]{:S(2)}, u32[]{:S(2)}) collective-permute-start(f32[35,8,256]{2,1,0:T(8,128)S(1)} %get-tuple-element.73), channel_id=1, source_target_pairs={{8,16},{16,8},{9,17},{17,9},{10,18},{18,10},{11,19},{19,11},{12,20... | collective-permute-start | bytes 860168 | tf_op jit(solution)/shard_map/ppermute | solution.py:816
  24.3 3.1 %collective-permute-start.11 = (f32[224,256]{1,0:T(8,128)S(1)}, f32[224,256]{1,0:T(8,128)S(1)}, u32[]{:S(2)}, u32[]{:S(2)}) collective-permute-start(f32[224,256]{1,0:T(8,128)S(1)} %get-tuple-element.92), channel_id=1, source_target_pairs={{0,1},{2,3},{4,5},{6,7},{1,0},{3,2},{5,4},{7,6},{8,9},{10,11},{12,... | collective-permute-start | bytes 688136 | tf_op jit(solution)/shard_map/ppermute | solution.py:816
  27.4 4.2 %sweeps_inner.1 = (f32[32,40,256]{2,1,0:T(8,128)S(1)}, f32[32,40,256]{2,1,0:T(8,128)S(1)}, f32[32,40,256]{2,1,0:T(8,128)S(1)}, f32[32,40,256]{2,1,0:T(8,128)S(1)...) custom-call(f32[32,32,256]{2,1,0:T(8,128)S(1)} %copy-done.1, ...), custom_call_target="tpu_custom_call" | custom-call | flops 1000000 | bytes 14614528 | tf_op jit(solution)/shard_map/sweeps_inner/pallas_call | solution.py:36
  31.7 1.2 %sweeps_edge.1 = (f32[32,32,256]{2,1,0:T(8,128)S(1)}, f32[32,32,256]{2,1,0:T(8,128)S(1)}, f32[96,256]{1,0:T(8,128)S(1)}, f32[104,256]{1,0:T(8,128)S(1)}) custom-call(f32[35,8,256]{2,1,0:T(8,128)S(1)} %collective-permute-done.5.x_a, f32[35,8,256]{2,1,0:T(8,128)S(1)} %collective-permute-done.6.x_b, s32[32,32,256]{2,1,0:T(8,128)S(1)} %copy-done, ...), custom_call_target="tpu_custom_call" | custom-call | flops 1000000 | bytes 15990784 | tf_op jit(solution)/shard_map/sweeps_edge/pallas_call | solution.py:36
  33.7 0.8 ready.1
  34.4 2.7 %collective-permute-done.11.token_2.yy_b = f32[224,256]{1,0:T(8,128)S(1)} collective-permute-done((f32[224,256]{1,0:T(8,128)S(1)}, f32[224,256]{1,0:T(8,128)S(1)}, u32[]{:S(2)}, u32[]{:S(2)}) %collective-permute-start.11) | collective-permute-done | bytes 229408 | tf_op jit(solution)/shard_map/ppermute | solution.py:816
  37.1 4.4 %collective-permute-done.7.far.r_b.y_b = f32[104,256]{1,0:T(8,128)S(1)} collective-permute-done((f32[104,256]{1,0:T(8,128)S(1)}, f32[104,256]{1,0:T(8,128)S(1)}, u32[]{:S(2)}, u32[]{:S(2)}) %collective-permute-start.7) | collective-permute-done | bytes 106528 | tf_op jit(solution)/shard_map/ppermute | solution.py:816
  41.5 0.8 mask.1
  42.4 3.1 %collective-permute-start.13 = (f32[15,8,256]{2,1,0:T(8,128)S(1)}, f32[15,8,256]{2,1,0:T(8,128)S(1)}, u32[]{:S(2)}, u32[]{:S(2)}) collective-permute-start(f32[15,8,256]{2,1,0:T(8,128)S(1)} %get-tuple-element.99), channel_id=1, source_target_pairs={{8,16},{16,8},{9,17},{17,9},{10,18},{18,10},{11,19},{19,11},{12,20... | collective-permute-start | bytes 368648 | tf_op jit(solution)/shard_map/ppermute | solution.py:816
  45.6 3.3 %potential_inner.1 = (f32[40,40,256]{2,1,0:T(8,128)S(1)}, f32[40,40,256]{2,1,0:T(8,128)S(1)}, f32[40,40,256]{2,1,0:T(8,128)S(1)}, f32[16,16,256]{2,1,0:T(8,128)S(1)}, f32[40,40,256]{2,1,0:T(8,128)S(1)}) custom-call(f32[32,32,256]{2,1,0:T(8,128)S(1)} %get-tuple-element.93.flux, f32[32,8,256]{2,1,0:T(8,128)S(1)} %get-tuple-element.97.mask, ...), custom_call_target="tpu_custom_call" | custom-call | flops 1000000 | bytes 13508608 | tf_op jit(solution)/shard_map/potential_inner/pallas_call | solution.py:36
  50.2 4.6 %collective-permute-start.16 = (f32[128,256]{1,0:T(8,128)S(1)}, f32[128,256]{1,0:T(8,128)S(1)}, u32[]{:S(2)}, u32[]{:S(2)}) collective-permute-start(f32[128,256]{1,0:T(8,128)S(1)} %get-tuple-element.111), channel_id=1, source_target_pairs={{0,1},{2,3},{4,5},{6,7},{1,0},{3,2},{5,4},{7,6},{8,9},{10,11},{12,... | collective-permute-start | bytes 393224 | tf_op jit(solution)/shard_map/ppermute | solution.py:816
  54.8 1.4 %store.1 = (f32[32,32,256]{2,1,0:T(8,128)}, f32[32,32,256]{2,1,0:T(8,128)}, f32[8,128]{1,0:T(8,128)S(1)}) custom-call(f32[32,32,256]{2,1,0:T(8,128)S(1)} %get-tuple-element.85.conc, f32[32,32,256]{2,1,0:T(8,128)S(1)} %get-tuple-element.93.flux), custom_call_target="tpu_custom_call" | custom-call | flops 1000000 | bytes 4198400 | tf_op jit(solution)/shard_map/store/pallas_call | solution.py:36
  56.2 4.3 %collective-permute-done.16.r_b.y_b.far_b = f32[128,256]{1,0:T(8,128)S(1)} collective-permute-done((f32[128,256]{1,0:T(8,128)S(1)}, f32[128,256]{1,0:T(8,128)S(1)}, u32[]{:S(2)}, u32[]{:S(2)}) %collective-permute-start.16) | collective-permute-done | bytes 131104 | tf_op jit(solution)/shard_map/ppermute | solution.py:816
  60.6 2.9 %collective-permute-start.17 = (f32[12,8,256]{2,1,0:T(8,128)S(1)}, f32[12,8,256]{2,1,0:T(8,128)S(1)}, u32[]{:S(2)}, u32[]{:S(2)}) collective-permute-start(f32[12,8,256]{2,1,0:T(8,128)S(1)} %get-tuple-element.113), channel_id=1, source_target_pairs={{8,16},{16,8},{9,17},{17,9},{10,18},{18,10},{11,19},{19,11},{12,20... | collective-permute-start | bytes 294920 | tf_op jit(solution)/shard_map/ppermute | solution.py:816
  63.6 1.2 %coarse_ready.1 = (f32[8,8,256]{2,1,0:T(8,128)S(1)}, f32[8,128]{1,0:T(8,128)S(1)}) custom-call(f32[8,8,256]{2,1,0:T(8,128)S(1)} %get-tuple-element.108.coarse.own, f32[128,256]{1,0:T(8,128)S(1)} %collective-permute-done.15.r_a.y_a.far_a, f32[128,256]{1,0:T(8,128)S(1)} %collective-permute-done.16.r_b.y_b.far_b), custom_call_target="tpu_custom_call" | custom-call | flops 1000000 | bytes 397312 | tf_op jit(solution)/shard_map/coarse_ready/pallas_call | solution.py:36
  64.8 1.7 %collective-permute-done.17.x_a = f32[12,8,256]{2,1,0:T(8,128)S(1)} collective-permute-done((f32[12,8,256]{2,1,0:T(8,128)S(1)}, f32[12,8,256]{2,1,0:T(8,128)S(1)}, u32[]{:S(2)}, u32[]{:S(2)}) %collective-permute-start.17) | collective-permute-done | bytes 98336 | tf_op jit(solution)/shard_map/ppermute | solution.py:816
  66.5 1.1 %middle.1 = (f32[24,24,256]{2,1,0:T(8,128)S(1)}, f32[24,24,256]{2,1,0:T(8,128)S(1)}, f32[24,24,256]{2,1,0:T(8,128)S(1)}, f32[8,12,256]{2,1,0:T(8,128)S(1)}, f32[...) custom-call(f32[16,16,256]{2,1,0:T(8,128)S(1)} %get-tuple-element.109.field.source_, ...), custom_call_target="tpu_custom_call" | custom-call | flops 1000000 | bytes 4034560 | tf_op jit(solution)/shard_map/middle/pallas_call | solution.py:36
  67.6 2.3 %collective-permute-start.20 = (f32[80,256]{1,0:T(8,128)S(1)}, f32[80,256]{1,0:T(8,128)S(1)}, u32[]{:S(2)}, u32[]{:S(2)}) collective-permute-start(f32[80,256]{1,0:T(8,128)S(1)} %get-tuple-element.120), channel_id=1, source_target_pairs={{0,1},{2,3},{4,5},{6,7},{1,0},{3,2},{5,4},{7,6},{8,9},{10,11},{12,... | collective-permute-start | bytes 245768 | tf_op jit(solution)/shard_map/ppermute | solution.py:816
  70.5 1.2 %collective-permute-done.20.r_b = f32[80,256]{1,0:T(8,128)S(1)} collective-permute-done((f32[80,256]{1,0:T(8,128)S(1)}, f32[80,256]{1,0:T(8,128)S(1)}, u32[]{:S(2)}, u32[]{:S(2)}) %collective-permute-start.20) | collective-permute-done | bytes 81952 | tf_op jit(solution)/shard_map/ppermute | solution.py:816
  71.7 3.9 %collective-permute-start.21 = (f32[8,256]{1,0:T(8,128)S(1)}, f32[8,256]{1,0:T(8,128)S(1)}, u32[]{:S(2)}, u32[]{:S(2)}) collective-permute-start(f32[8,256]{1,0:T(8,128)S(1)} %slice_add_fusion.rest_0_), channel_id=1, source_target_pairs={{0,6},{1,7},{2,4},{3,5},{4,2},{5,3},{6,0},{7,1},{8,14},{9,15},{10,... | collective-permute-start | bytes 24584 | tf_op jit(solution)/shard_map/ppermute | solution.py:820
  75.8 1.2 %coarse.1.error = f32[8,16,256]{2,1,0:T(8,128)S(1)} custom-call(f32[8,12,256]{2,1,0:T(8,128)S(1)} %get-tuple-element.117.own, f32[8,12,256]{2,1,0:T(8,128)S(1)} %get-tuple-element.118.conduct, f32[128,256]{1,0:T(8,128)S(1)} %collective-permute-done.15.r_a.y_a.far_a, f32[128,256]{1,0:T(8,128)S(1)} %collective-permute-done.16.r_b.y_b.far_b, ...), custom_call_target="tpu_custom_call" | custom-call | flops 1000000 | bytes 745472 | tf_op jit(solution)/shard_map/coarse/pallas_call | solution.py:36
  77.7 1.3 %collective-permute-done.22.rest_2_ = f32[8,256]{1,0:T(8,128)S(1)} collective-permute-done((f32[8,256]{1,0:T(8,128)S(1)}, f32[8,256]{1,0:T(8,128)S(1)}, u32[]{:S(2)}, u32[]{:S(2)}) %collective-permute-start.22) | collective-permute-done | bytes 8224 | tf_op jit(solution)/shard_map/ppermute | solution.py:820
  79.1 6.1 %collective-permute-start.24 = (f32[2,16,256]{2,1,0:T(8,128)S(1)}, f32[2,16,256]{2,1,0:T(8,128)S(1)}, u32[]{:S(2)}, u32[]{:S(2)}) collective-permute-start(f32[2,16,256]{2,1,0:T(8,128)S(1)} %get-tuple-element.122), channel_id=1, source_target_pairs={{8,16},{16,8},{9,17},{17,9},{10,18},{18,10},{11,19},{19,11},{12,20... | collective-permute-start | bytes 98312 | tf_op jit(solution)/shard_map/ppermute | solution.py:816
  85.3 2.6 %finish_inner.1 = (f32[32,32,256]{2,1,0:T(8,128)}, f32[24,24,256]{2,1,0:T(8,128)S(1)}, f32[24,24,256]{2,1,0:T(8,128)S(1)}, f32[40,40,256]{2,1,0:T(8,128)S(1)}, f32[40,40,256]{2,1,0:T(8,128)S(1)}) custom-call(f32[8,16,256]{2,1,0:T(8,128)S(1)} %get-tuple-element.129.error, f32[24,24,256]{2,1,0:T(8,128)S(1)} %get-tuple-element.124.mid_two, ...), custom_call_target="tpu_custom_call" | custom-call | flops 1000000 | bytes 12320768 | tf_op jit(solution)/shard_map/finish_inner/pallas_call | solution.py:36
  87.9 1.7 %finish_edge.1 = f32[32,32,256]{2,1,0:T(8,128)} custom-call(f32[2,16,256]{2,1,0:T(8,128)S(1)} %collective-permute-done.24.x_a, f32[2,16,256]{2,1,0:T(8,128)S(1)} %collective-permute-done.25.x_b, f32[24,24,256]{2,1,0:T(8,128)S(1)} %get-tuple-element.124.mid_two, f32[24,24,256]{2,1,0:T(8,128)S(1)} %get-tuple-element.125.mid_source, ...), custom_call_target="tpu_custom_call", output_to_operand_aliasing={{}: (14, {})} | custom-call | flops 1000000 | bytes 14614528 | tf_op jit(solution)/shard_map/finish_edge/pallas_call | solution.py:36
  (53 shorter events, 7.2 us)
Async XLA Ops:
  0.6 7.5 %copy-start.1 = (f32[32,32,256]{2,1,0:T(8,128)S(1)}, f32[32,32,256]{2,1,0:T(8,128)}, u32[]{:S(2)}) copy-start(f32[32,32,256]{2,1,0:T(8,128)} %conc.9) | copy-start | bytes 3145732
  0.6 7.5 %copy-start = (s32[32,32,256]{2,1,0:T(8,128)S(1)}, s32[32,32,256]{2,1,0:T(8,128)}, u32[]{:S(2)}) copy-start(s32[32,32,256]{2,1,0:T(8,128)} %label.11) | copy-start | bytes 3145732
  2.8 16.7 %collective-permute-start = (f32[224,256]{1,0:T(8,128)}, f32[224,256]{1,0:T(8,128)S(1)}, u32[]{:S(2)}, u32[]{:S(2)}) collective-permute-start(f32[224,256]{1,0:T(8,128)} %get-tuple-element.69), channel_id=1, source_target_pairs={{1,2},{3,4},{5,6},{2,1},{4,3},{6,5},{9,10},{11,12},{13,14},{10,9},... | collective-permute-start | bytes 688136 | tf_op jit(solution)/shard_map/ppermute | solution.py:816
  3.5 16.0 %collective-permute-start.1 = (f32[224,256]{1,0:T(8,128)}, f32[224,256]{1,0:T(8,128)S(1)}, u32[]{:S(2)}, u32[]{:S(2)}) collective-permute-start(f32[224,256]{1,0:T(8,128)} %get-tuple-element.70), channel_id=1, source_target_pairs={{0,1},{2,3},{4,5},{6,7},{1,0},{3,2},{5,4},{7,6},{8,9},{10,11},{12,... | collective-permute-start | bytes 688136 | tf_op jit(solution)/shard_map/ppermute | solution.py:816
  8.1 1.2 %copy-start.2 = (f32[32,32,256]{2,1,0:T(8,128)S(1)}, f32[32,32,256]{2,1,0:T(8,128)}, u32[]{:S(2)}) copy-start(f32[32,32,256]{2,1,0:T(8,128)} %phi.9) | copy-start | bytes 3145732
  9.3 0.7 copy-start.5
  10.7 12.8 %copy-start.3 = (f32[32,32,256]{2,1,0:T(8,128)S(1)}, f32[32,32,256]{2,1,0:T(8,128)}, u32[]{:S(2)}) copy-start(f32[32,32,256]{2,1,0:T(8,128)} %phi.9) | copy-start | bytes 3145732
  10.7 3.6 %collective-permute-start.4 = (f32[2,256]{1,0:T(2,128)S(1)}, f32[2,256]{1,0:T(2,128)S(1)}, u32[]{:S(2)}, u32[]{:S(2)}) collective-permute-start(f32[2,256]{1,0:T(2,128)S(1)} %get-tuple-element.72), channel_id=1, source_target_pairs={{0,2},{1,3},{2,0},{3,1},{4,6},{5,7},{6,4},{7,5},{8,10},{9,11},{10,... | collective-permute-start | bytes 6152 | tf_op jit(solution)/shard_map/ppermute | solution.py:820
  12.1 7.4 %collective-permute-start.3 = (f32[2,256]{1,0:T(2,128)S(1)}, f32[2,256]{1,0:T(2,128)S(1)}, u32[]{:S(2)}, u32[]{:S(2)}) collective-permute-start(f32[2,256]{1,0:T(2,128)S(1)} %get-tuple-element.72), channel_id=1, source_target_pairs={{0,4},{1,5},{2,6},{3,7},{4,0},{5,1},{6,2},{7,3},{8,12},{9,13},{10,... | collective-permute-start | bytes 6152 | tf_op jit(solution)/shard_map/ppermute | solution.py:820
  13.1 6.4 %collective-permute-start.2 = (f32[2,256]{1,0:T(2,128)S(1)}, f32[2,256]{1,0:T(2,128)S(1)}, u32[]{:S(2)}, u32[]{:S(2)}) collective-permute-start(f32[2,256]{1,0:T(2,128)S(1)} %get-tuple-element.72), channel_id=1, source_target_pairs={{0,6},{1,7},{2,4},{3,5},{4,2},{5,3},{6,0},{7,1},{8,14},{9,15},{10,... | collective-permute-start | bytes 6152 | tf_op jit(solution)/shard_map/ppermute | solution.py:820
  14.3 9.1 %collective-permute-start.8 = (f32[24,8,256]{2,1,0:T(8,128)S(1)}, f32[24,8,256]{2,1,0:T(8,128)S(1)}, u32[]{:S(2)}, u32[]{:S(2)}) collective-permute-start(f32[24,8,256]{2,1,0:T(8,128)S(1)} %get-tuple-element.89), channel_id=1, source_target_pairs={{8,16},{16,8},{9,17},{17,9},{10,18},{18,10},{11,19},{19,11},{12,20... | collective-permute-start | bytes 589832 | tf_op jit(solution)/shard_map/ppermute | solution.py:816
  19.4 4.0 %collective-permute-start.9 = (f32[24,8,256]{2,1,0:T(8,128)S(1)}, f32[24,8,256]{2,1,0:T(8,128)S(1)}, u32[]{:S(2)}, u32[]{:S(2)}) collective-permute-start(f32[24,8,256]{2,1,0:T(8,128)S(1)} %get-tuple-element.90), channel_id=1, source_target_pairs={{0,8},{16,24},{8,0},{24,16},{1,9},{17,25},{9,1},{25,17},{2,10},{18... | collective-permute-start | bytes 589832 | tf_op jit(solution)/shard_map/ppermute | solution.py:816
  19.5 7.9 %copy-start.4 = (f32[32,32,256]{2,1,0:T(8,128)S(1)}, f32[32,32,256]{2,1,0:T(8,128)}, u32[]{:S(2)}) copy-start(f32[32,32,256]{2,1,0:T(8,128)} %solid.3) | copy-start | bytes 3145732
  19.6 12.0 %collective-permute-start.5 = (f32[35,8,256]{2,1,0:T(8,128)S(1)}, f32[35,8,256]{2,1,0:T(8,128)S(1)}, u32[]{:S(2)}, u32[]{:S(2)}) collective-permute-start(f32[35,8,256]{2,1,0:T(8,128)S(1)} %get-tuple-element.73), channel_id=1, source_target_pairs={{8,16},{16,8},{9,17},{17,9},{10,18},{18,10},{11,19},{19,11},{12,20... | collective-permute-start | bytes 860168 | tf_op jit(solution)/shard_map/ppermute | solution.py:816
  23.3 8.3 %collective-permute-start.6 = (f32[35,8,256]{2,1,0:T(8,128)S(1)}, f32[35,8,256]{2,1,0:T(8,128)S(1)}, u32[]{:S(2)}, u32[]{:S(2)}) collective-permute-start(f32[35,8,256]{2,1,0:T(8,128)S(1)} %get-tuple-element.74), channel_id=1, source_target_pairs={{0,8},{16,24},{8,0},{24,16},{1,9},{17,25},{9,1},{25,17},{2,10},{18... | collective-permute-start | bytes 860168 | tf_op jit(solution)/shard_map/ppermute | solution.py:816
  23.6 10.8 %collective-permute-start.10 = (f32[224,256]{1,0:T(8,128)S(1)}, f32[224,256]{1,0:T(8,128)S(1)}, u32[]{:S(2)}, u32[]{:S(2)}) collective-permute-start(f32[224,256]{1,0:T(8,128)S(1)} %get-tuple-element.91), channel_id=1, source_target_pairs={{1,2},{3,4},{5,6},{2,1},{4,3},{6,5},{9,10},{11,12},{13,14},{10,9},... | collective-permute-start | bytes 688136 | tf_op jit(solution)/shard_map/ppermute | solution.py:816
  24.3 12.8 %collective-permute-start.11 = (f32[224,256]{1,0:T(8,128)S(1)}, f32[224,256]{1,0:T(8,128)S(1)}, u32[]{:S(2)}, u32[]{:S(2)}) collective-permute-start(f32[224,256]{1,0:T(8,128)S(1)} %get-tuple-element.92), channel_id=1, source_target_pairs={{0,1},{2,3},{4,5},{6,7},{1,0},{3,2},{5,4},{7,6},{8,9},{10,11},{12,... | collective-permute-start | bytes 688136 | tf_op jit(solution)/shard_map/ppermute | solution.py:816
  32.9 8.6 %collective-permute-start.7 = (f32[104,256]{1,0:T(8,128)S(1)}, f32[104,256]{1,0:T(8,128)S(1)}, u32[]{:S(2)}, u32[]{:S(2)}) collective-permute-start(f32[104,256]{1,0:T(8,128)S(1)} %get-tuple-element.87), channel_id=1, source_target_pairs={{0,1},{2,3},{4,5},{6,7},{1,0},{3,2},{5,4},{7,6},{8,9},{10,11},{12,... | collective-permute-start | bytes 319496 | tf_op jit(solution)/shard_map/ppermute | solution.py:816
  33.0 9.3 %collective-permute-start.12 = (f32[96,256]{1,0:T(8,128)S(1)}, f32[96,256]{1,0:T(8,128)S(1)}, u32[]{:S(2)}, u32[]{:S(2)}) collective-permute-start(f32[96,256]{1,0:T(8,128)S(1)} %get-tuple-element.96), channel_id=1, source_target_pairs={{1,2},{3,4},{5,6},{2,1},{4,3},{6,5},{9,10},{11,12},{13,14},{10,9},... | collective-permute-start | bytes 294920 | tf_op jit(solution)/shard_map/ppermute | solution.py:816
  42.4 6.4 %collective-permute-start.13 = (f32[15,8,256]{2,1,0:T(8,128)S(1)}, f32[15,8,256]{2,1,0:T(8,128)S(1)}, u32[]{:S(2)}, u32[]{:S(2)}) collective-permute-start(f32[15,8,256]{2,1,0:T(8,128)S(1)} %get-tuple-element.99), channel_id=1, source_target_pairs={{8,16},{16,8},{9,17},{17,9},{10,18},{18,10},{11,19},{19,11},{12,20... | collective-permute-start | bytes 368648 | tf_op jit(solution)/shard_map/ppermute | solution.py:816
  45.5 3.4 %collective-permute-start.14 = (f32[15,8,256]{2,1,0:T(8,128)S(1)}, f32[15,8,256]{2,1,0:T(8,128)S(1)}, u32[]{:S(2)}, u32[]{:S(2)}) collective-permute-start(f32[15,8,256]{2,1,0:T(8,128)S(1)} %get-tuple-element.100), channel_id=1, source_target_pairs={{0,8},{16,24},{8,0},{24,16},{1,9},{17,25},{9,1},{25,17},{2,10},{18... | collective-permute-start | bytes 368648 | tf_op jit(solution)/shard_map/ppermute | solution.py:816
  49.5 6.7 %collective-permute-start.15 = (f32[128,256]{1,0:T(8,128)S(1)}, f32[128,256]{1,0:T(8,128)S(1)}, u32[]{:S(2)}, u32[]{:S(2)}) collective-permute-start(f32[128,256]{1,0:T(8,128)S(1)} %get-tuple-element.110), channel_id=1, source_target_pairs={{1,2},{3,4},{5,6},{2,1},{4,3},{6,5},{9,10},{11,12},{13,14},{10,9},... | collective-permute-start | bytes 393224 | tf_op jit(solution)/shard_map/ppermute | solution.py:816
  50.2 10.4 %collective-permute-start.16 = (f32[128,256]{1,0:T(8,128)S(1)}, f32[128,256]{1,0:T(8,128)S(1)}, u32[]{:S(2)}, u32[]{:S(2)}) collective-permute-start(f32[128,256]{1,0:T(8,128)S(1)} %get-tuple-element.111), channel_id=1, source_target_pairs={{0,1},{2,3},{4,5},{6,7},{1,0},{3,2},{5,4},{7,6},{8,9},{10,11},{12,... | collective-permute-start | bytes 393224 | tf_op jit(solution)/shard_map/ppermute | solution.py:816
  60.6 5.9 %collective-permute-start.17 = (f32[12,8,256]{2,1,0:T(8,128)S(1)}, f32[12,8,256]{2,1,0:T(8,128)S(1)}, u32[]{:S(2)}, u32[]{:S(2)}) collective-permute-start(f32[12,8,256]{2,1,0:T(8,128)S(1)} %get-tuple-element.113), channel_id=1, source_target_pairs={{8,16},{16,8},{9,17},{17,9},{10,18},{18,10},{11,19},{19,11},{12,20... | collective-permute-start | bytes 294920 | tf_op jit(solution)/shard_map/ppermute | solution.py:816
  63.5 3.0 %collective-permute-start.18 = (f32[12,8,256]{2,1,0:T(8,128)S(1)}, f32[12,8,256]{2,1,0:T(8,128)S(1)}, u32[]{:S(2)}, u32[]{:S(2)}) collective-permute-start(f32[12,8,256]{2,1,0:T(8,128)S(1)} %get-tuple-element.114), channel_id=1, source_target_pairs={{0,8},{16,24},{8,0},{24,16},{1,9},{17,25},{9,1},{25,17},{2,10},{18... | collective-permute-start | bytes 294920 | tf_op jit(solution)/shard_map/ppermute | solution.py:816
  67.6 4.1 %collective-permute-start.20 = (f32[80,256]{1,0:T(8,128)S(1)}, f32[80,256]{1,0:T(8,128)S(1)}, u32[]{:S(2)}, u32[]{:S(2)}) collective-permute-start(f32[80,256]{1,0:T(8,128)S(1)} %get-tuple-element.120), channel_id=1, source_target_pairs={{0,1},{2,3},{4,5},{6,7},{1,0},{3,2},{5,4},{7,6},{8,9},{10,11},{12,... | collective-permute-start | bytes 245768 | tf_op jit(solution)/shard_map/ppermute | solution.py:816
  69.8 6.0 %collective-permute-start.19 = (f32[72,256]{1,0:T(8,128)S(1)}, f32[72,256]{1,0:T(8,128)S(1)}, u32[]{:S(2)}, u32[]{:S(2)}) collective-permute-start(f32[72,256]{1,0:T(8,128)S(1)} %get-tuple-element.119), channel_id=1, source_target_pairs={{1,2},{3,4},{5,6},{2,1},{4,3},{6,5},{9,10},{11,12},{13,14},{10,9},... | collective-permute-start | bytes 221192 | tf_op jit(solution)/shard_map/ppermute | solution.py:816
  71.7 6.0 %collective-permute-start.21 = (f32[8,256]{1,0:T(8,128)S(1)}, f32[8,256]{1,0:T(8,128)S(1)}, u32[]{:S(2)}, u32[]{:S(2)}) collective-permute-start(f32[8,256]{1,0:T(8,128)S(1)} %slice_add_fusion.rest_0_), channel_id=1, source_target_pairs={{0,6},{1,7},{2,4},{3,5},{4,2},{5,3},{6,0},{7,1},{8,14},{9,15},{10,... | collective-permute-start | bytes 24584 | tf_op jit(solution)/shard_map/ppermute | solution.py:820
  75.5 3.4 %collective-permute-start.22 = (f32[8,256]{1,0:T(8,128)S(1)}, f32[8,256]{1,0:T(8,128)S(1)}, u32[]{:S(2)}, u32[]{:S(2)}) collective-permute-start(f32[8,256]{1,0:T(8,128)S(1)} %slice_add_fusion.rest_0_), channel_id=1, source_target_pairs={{0,4},{1,5},{2,6},{3,7},{4,0},{5,1},{6,2},{7,3},{8,12},{9,13},{10,... | collective-permute-start | bytes 24584 | tf_op jit(solution)/shard_map/ppermute | solution.py:820
  75.5 3.4 %collective-permute-start.23 = (f32[8,256]{1,0:T(8,128)S(1)}, f32[8,256]{1,0:T(8,128)S(1)}, u32[]{:S(2)}, u32[]{:S(2)}) collective-permute-start(f32[8,256]{1,0:T(8,128)S(1)} %slice_add_fusion.rest_0_), channel_id=1, source_target_pairs={{0,2},{1,3},{2,0},{3,1},{4,6},{5,7},{6,4},{7,5},{8,10},{9,11},{10,... | collective-permute-start | bytes 24584 | tf_op jit(solution)/shard_map/ppermute | solution.py:820
  79.1 8.8 %collective-permute-start.24 = (f32[2,16,256]{2,1,0:T(8,128)S(1)}, f32[2,16,256]{2,1,0:T(8,128)S(1)}, u32[]{:S(2)}, u32[]{:S(2)}) collective-permute-start(f32[2,16,256]{2,1,0:T(8,128)S(1)} %get-tuple-element.122), channel_id=1, source_target_pairs={{8,16},{16,8},{9,17},{17,9},{10,18},{18,10},{11,19},{19,11},{12,20... | collective-permute-start | bytes 98312 | tf_op jit(solution)/shard_map/ppermute | solution.py:816
  85.2 2.7 %collective-permute-start.25 = (f32[2,16,256]{2,1,0:T(8,128)S(1)}, f32[2,16,256]{2,1,0:T(8,128)S(1)}, u32[]{:S(2)}, u32[]{:S(2)}) collective-permute-start(f32[2,16,256]{2,1,0:T(8,128)S(1)} %get-tuple-element.123), channel_id=1, source_target_pairs={{0,8},{16,24},{8,0},{24,16},{1,9},{17,25},{9,1},{25,17},{2,10},{18... | collective-permute-start | bytes 98312 | tf_op jit(solution)/shard_map/ppermute | solution.py:816

commit v8 on v4

--- a/solution.py
+++ b/solution.py
@@ -335,15 +335,15 @@
     owner = jnp.concatenate(pieces[0::2], axis=1).astype(jnp.int32)
     block = jnp.concatenate(pieces[1::2], axis=1).astype(jnp.int32)
     entries = owner.shape[1]
-    hit_column = (iota((LANES, entries), 0) == lax.rem(block, 64)).astype(jnp.bfloat16)
-    at_row = lax.shift_right_arithmetic(block, 6)
-    here = lax.axis_index("dev")
+    hit_column = (iota((64, entries), 0) == lax.rem(block, 64)).astype(jnp.bfloat16)
+    reach = owner - lax.axis_index("dev") + 1
+    at_row = jnp.where((reach >= 0) & (reach < 3), reach * nx + lax.shift_right_arithmetic(block, 6), -1)
+    hit_row = (iota((3 * nx, entries), 0) == at_row).astype(jnp.bfloat16)
+    named = lax.dot_general(hit_row, hit_column, (((1,), (1,)), ((), ())), preferred_element_type=F32)
+    named = jnp.concatenate([named, jnp.zeros((3 * nx, LANES - 64), F32)], axis=1)
     for j in range(3):
-        mine = jnp.where(owner == here + j - 1, at_row, -1)
-        hit_row = (iota((nx, entries), 0) == mine).astype(jnp.bfloat16)
-        named = lax.dot_general(hit_row, hit_column, (((1,), (1,)), ((), ())), preferred_element_type=F32)
         for i in range(nx):
-            marked[j, i] = jnp.broadcast_to(named[i : i + 1, :], (8, LANES))
+            marked[j, i] = jnp.broadcast_to(named[j * nx + i : j * nx + i + 1, :], (8, LANES))
     is_row = lax.div(iota((32, LANES), 1), 2) == iota((32, LANES), 0)
     row, pair = iota((8, LANES), 0), lax.div(iota((8, LANES), 1), 2)
     is_after = (row < 3) & (pair == row)
@@ -358,7 +358,7 @@
         flux[i] = jnp.where(listed[0:32], flux_all[i], 0.0)
         halo_mask[i] = jnp.where(listed[32:40], 1.0, 0.0)
 
-    loop(0, nx, plane, 4)
+    loop(0, nx, plane, 16)
 
 
 def store_kernel(conc, flux, conc_out, flux_out, token, sems):
@@ -373,39 +373,48 @@
         c.wait()
 
 
-def ready_kernel(conc, label, phi, y_a, y_b, x_a, x_b, yy_a, yy_b, xx_a, xx_b, weight, scale, field, token):
+def ready_kernel(conc, label, y_a, y_b, x_a, x_b, weight, scale, token):
     nx = conc.shape[0]
     token[...] = jnp.zeros(token.shape, F32)
 
-    def put(x, rows, c, lab, p):
+    def put(x, rows, c, lab):
         conduct = c * pick(lab, CONDUCT_TABLE)
         factor = OMEGA / (MASS + 6.0 * conduct)
         weight[x, rows, :] = conduct * factor
         scale[x, rows, :] = factor
-        field[x, rows, :] = p
 
     def own(i):
-        put(HALO + i, slice(0, 32), conc[i], label[i], phi[i])
+        put(HALO + i, slice(0, 32), conc[i], label[i])
 
     loop(0, nx, own, 4)
-    low = slice(32, 40)
     for i in range(nx):
         c = halo_tile(*y_sides(y_a, y_b, 7 * i, 4))
         lab = halo_tile(*y_sides(y_a, y_b, 7 * i + 4, 3))
-        put(HALO + i, low, c, lab, second_halo(yy_a, yy_b, nx, 0, HALO + i, 0))
+        put(HALO + i, slice(32, 40), c, lab)
     for t in range(5):
         rows = slice(8 * t, 8 * t + 8)
         for k in range(HALO):
             c_after, c_before = x_sides(x_a, x_b, 5 * k + t)
             l_after = x_sides(x_a, x_b, 20 + 5 * min(k, 2) + t)[0]
             l_before = x_sides(x_a, x_b, 20 + 5 * max(k - 1, 0) + t)[1]
-            if t < 4:
-                p_after, p_before = x_sides(xx_a, xx_b, 4 * k + t)
-            else:
-                p_after = second_halo(yy_a, yy_b, nx, 0, HALO + nx + k, 0)
-                p_before = second_halo(yy_a, yy_b, nx, 0, k, 0)
-            put(k, rows, c_before, l_before, p_before)
-            put(HALO + nx + k, rows, c_after, l_after, p_after)
+            put(k, rows, c_before, l_before)
+            put(HALO + nx + k, rows, c_after, l_after)
+
+
+def place_phi(phi, yy_a, yy_b, xx_a, xx_b, field):
+    nx = phi.shape[0]
+
+    def own(i):
+        field[HALO + i, 0:32, :] = phi[i]
+
+    loop(0, nx, own)
+    for x in range(nx + 2 * HALO):
+        field[x, 32:40, :] = second_halo(yy_a, yy_b, nx, 0, x, 0)
+    for t in range(4):
+        for k in range(HALO):
+            after, before = x_sides(xx_a, xx_b, 4 * k + t)
+            field[k, 8 * t : 8 * t + 8, :] = before
+            field[HALO + nx + k, 8 * t : 8 * t + 8, :] = after
 
 
 def flux_pack_x_kernel(flux, r_a, r_b, mask, token, pay_a, pay_b):
@@ -428,8 +437,11 @@
     return b, 0.2 * p[rows, :] + weight[x, rows, :] * near[rows, :] + b
 
 
-def potential_inner_kernel(flux, mask, y_a, y_b, weight, scale, field, after_two, source, first, source_mid, far, pairs):
+def potential_inner_kernel(
+    flux, mask, y_a, y_b, phi, yy_a, yy_b, xx_a, xx_b, weight, scale, after_two, source, first, source_mid, field, far, pairs
+):
     nx = flux.shape[0]
+    place_phi(phi, yy_a, yy_b, xx_a, xx_b, field)
     for i in range(nx):
         far[i] = mask[i] * halo_tile(*y_sides(y_a, y_b, 3 * i, 3))
 
@@ -569,7 +581,6 @@
         send_y(pay_a, pay_b, 9 * i + 8, k[8:9], k[11:12])
         total += rho[i] * value[0:8]
     sums = jnp.concatenate([total[:, :LANES] + total[:, LANES:], load[...]], axis=1)
-    pay_b[72:80, :] = sums
     part[...] = sums
 
 
@@ -607,6 +618,10 @@
     load[...] = total[:, :LANES] + total[:, LANES:]
 
 
+def late_kernel(pay, token, out):
+    out[...] = pay[...]
+
+
 def coarse_kernel(own, conduct, far_a, far_b, r_a, r_b, error, source, weight, one, two):
     base = far_a.shape[0] - 64
     for x in range(8):
@@ -637,7 +652,8 @@
         error[x, 8:16, :] = jnp.where(upper(), old[x, 8:16, :], old[x, 24:32, :])
 
 
-def shift_kernel(error, sums, out, pay_a, pay_b):
+def shift_kernel(error, sums_own, sums_other, out, pay_a, pay_b):
+    sums = sums_own[...] + sums_other[...]
     resid = jnp.sum(sums[:, :LANES])
     load = jnp.sum(sums[:, LANES:])
     shift_c = jnp.full((16, 256), resid, F32) / jnp.full((16, 256), load, F32)
@@ -858,20 +874,20 @@
         [vmem(3, nx, 8, LANES)],
         name="mask",
     )
-    weight, scale, field, made = call(
+    weight, scale, made = call(
         ready_kernel,
-        [shaped(*ext)] * 3 + [token_shape],
-        [conc_old, phase_label, phi_old, y_a, y_b, x_a, x_b, yy_a, yy_b, xx_a, xx_b],
+        [shaped(*ext)] * 2 + [token_shape],
+        [conc_old, phase_label, y_a, y_b, x_a, x_b],
         name="ready",
     )
     pay_a, pay_b = call(
         flux_pack_x_kernel, [shaped(15, 8, 256)] * 2, [flux_own, f_a, f_b, halo_mask, made], name="flux_pack_x"
     )
     fx_a, fx_b = swap(pay_a, pay_b, "grp")
-    fine_two, fine_source, fine_first, inner_mid = call(
+    fine_two, fine_source, fine_first, inner_mid, field = call(
         potential_inner_kernel,
-        [shaped(*ext)] * 3 + [shaped(half, half, 256)],
-        [flux_own, halo_mask, f_a, f_b, weight, scale, field],
+        [shaped(*ext)] * 3 + [shaped(half, half, 256), shaped(*ext)],
+        [flux_own, halo_mask, f_a, f_b, phi_old, yy_a, yy_b, xx_a, xx_b, weight, scale],
         [vmem(nx, 8, 256), vmem(half, 2, nx, LANES)],
         name="potential_inner",
     )
@@ -907,17 +923,19 @@
     mid_two, mid_source, mid_weight, source_coarse, wide_coarse, pay_a, pay_b, sums = call(
         mid_kernel,
         [shaped(*ext_mid)] * 3
-        + [shaped(quarter, 12, 256), shaped(quarter, 12, 256), shaped(72, 256), shaped(80, 256), shaped(8, 256)],
+        + [shaped(quarter, 12, 256), shaped(quarter, 12, 256), shaped(72, 256), shaped(72, 256), shaped(8, 256)],
         [source_mid, conduct_mid, yy_a, yy_b, xx_a, xx_b, m_a, m_b, mx_a, mx_b, rho, load],
         [vmem(*ext_mid)] * 2 + [vmem(8, 2, half + 2 * HALO, LANES)] * 2,
         name="middle",
     )
+    distance = peers // 2
+    early = sums = sums + exchange(sums, distance)
+    while distance > 2:
+        distance //= 2
+        sums = sums + exchange(sums, distance)
+    (pay_b,) = call(late_kernel, [shaped(72, 256)], [pay_b, early], name="late")
     c_a, c_b = swap(pay_a, pay_b, "dev")
-    sums = sums + c_b[72:80]
-    distance = 2
-    while distance < peers:
-        sums = sums + exchange(sums, distance)
-        distance *= 2
+    other_sums = exchange(sums, 1)
     (error,) = call(
         coarse_kernel,
         [shaped(8, 16, 256)],
@@ -926,7 +944,7 @@
         name="coarse",
     )
     error, pay_a, pay_b = call(
-        shift_kernel, [shaped(8, 16, 256), shaped(2, 16, 256), shaped(2, 16, 256)], [error, sums], name="shift"
+        shift_kernel, [shaped(8, 16, 256), shaped(2, 16, 256), shaped(2, 16, 256)], [error, sums, other_sums], name="shift"
     )
     e_a, e_b = swap(pay_a, pay_b, "grp")
     begun, zero, one, fine_one, fine_last = call(

time: 86 us -> 88.6 us (1.030)
  starting transfers between devices: 47.8 us -> 49.6 us
  waiting for transfers between devices: 10.1 us -> 11.7 us
    ppermute x4 -> x5, waiting for transfers between devices: 1.73 us -> 3.84 us  [exchange(): lax.ppermute(value, 'dev', [(i, i ^ distance) for i in range(lax.axis_siz...]
    ppermute x10, starting transfers between devices: 22.2 us -> 23.5 us  [swap(): lax.ppermute(pay_a, axis, both_ways(pairs_a))]
    ppermute x10, starting transfers between devices: 18.8 us -> 20 us  [swap(): lax.ppermute(pay_b, axis, both_ways(pairs_b))]
    pallas_call x19 -> x20, Pallas kernels: 24.2 us -> 23.4 us  [call(): pl.pallas_call(kernel, out_shape=tuple(outs), in_specs=in_specs or [WHOLE...]
    ppermute x4 -> x5, starting transfers between devices: 6.78 us -> 6.15 us  [exchange(): lax.ppermute(value, 'dev', [(i, i ^ distance) for i in range(lax.axis_siz...]
  transfers between devices with their start and end apart: 24 -> 25, of which waited for: 8 -> 9; matrix products, arithmetic and copies ran while one was open for 0% -> 0% of each run, Pallas kernels for 22% -> 20%
where the time goes in v8:
time: 88.6 us; the launch traced here: 87.7 us
  starting transfers between devices  49.6 us (56%)
  Pallas kernels  23.4 us (26%)
  waiting for transfers between devices  11.7 us (13%)
  local copies, waits for them, and re-layouts  1.94 us (2%)
  between operations  1.03 us (1%)
    ppermute x10, starting transfers between devices, swap(): lax.ppermute(pay_a, axis, both_ways(pairs_a))  23.5 us
    pallas_call x20, Pallas kernels, call(): pl.pallas_call(kernel, out_shape=tuple(outs), in_specs=in_specs or [WHOLE...  23.4 us
    ppermute x10, starting transfers between devices, swap(): lax.ppermute(pay_b, axis, both_ways(pairs_b))  20 us
    ppermute x5, starting transfers between devices, exchange(): lax.ppermute(value, 'dev', [(i, i ^ distance) for i in range(lax.axis_siz...  6.15 us
    ppermute x10, waiting for transfers between devices, swap(): lax.ppermute(pay_a, axis, both_ways(pairs_a))  4.49 us
    ppermute x5, waiting for transfers between devices, exchange(): lax.ppermute(value, 'dev', [(i, i ^ distance) for i in range(lax.axis_siz...  3.84 us
    ppermute x10, waiting for transfers between devices, swap(): lax.ppermute(pay_b, axis, both_ways(pairs_b))  3.35 us
    unnamed x12, local copies, waits for them, and re-layouts  1.94 us
  transfers between devices with their start and end apart: 25, of which 9 were waited for; matrix products, arithmetic and copies ran while one was open for 0% of the time, Pallas kernels for 20%

profile of v8, /device:TPU:1, one launch (start us, length us, event | category | flops | bytes accessed | tf_op | source)
XLA Modules:
  0.0 87.7 jit_solution(1932723069080746033)
XLA Ops:
  0.7 2.2 %first_pack.1 = (f32[224,256]{1,0:T(8,128)}, f32[224,256]{1,0:T(8,128)}, f32[8,256]{1,0:T(8,128)}) custom-call(f32[32,32,256]{2,1,0:T(8,128)} %conc.9, s32[32,32,256]{2,1,0:T(8,128)} %label.11, s32[1,256]{1,0:T(1,128)} %bitcast.1, s32[1,256]{1,0:T(1,128)} %block.1), custom_call_target="tpu_custom_call" | custom-call | flops 1000000 | bytes 2566144 | tf_op jit(solution)/shard_map/first_pack/pallas_call | solution.py:36
  2.8 0.7 collective-permute-start
  3.5 4.6 %collective-permute-start.1 = (f32[224,256]{1,0:T(8,128)}, f32[224,256]{1,0:T(8,128)S(1)}, u32[]{:S(2)}, u32[]{:S(2)}) collective-permute-start(f32[224,256]{1,0:T(8,128)} %get-tuple-element.65), channel_id=1, source_target_pairs={{0,1},{2,3},{4,5},{6,7},{1,0},{3,2},{5,4},{7,6},{8,9},{10,11},{12,... | collective-permute-start | bytes 688136 | tf_op jit(solution)/shard_map/ppermute | solution.py:798
  8.1 1.2 %copy-done.2 = f32[32,32,256]{2,1,0:T(8,128)S(1)} copy-done((f32[32,32,256]{2,1,0:T(8,128)S(1)}, f32[32,32,256]{2,1,0:T(8,128)}, u32[]{:S(2)}) %copy-start.2) | copy-done | bytes 1048600
  9.3 0.7 copy-done.5
  10.7 2.4 %collective-permute-start.4 = (f32[2,256]{1,0:T(2,128)S(1)}, f32[2,256]{1,0:T(2,128)S(1)}, u32[]{:S(2)}, u32[]{:S(2)}) collective-permute-start(f32[2,256]{1,0:T(2,128)S(1)} %get-tuple-element.70), channel_id=1, source_target_pairs={{0,4},{1,5},{2,6},{3,7},{4,0},{5,1},{6,2},{7,3},{8,12},{9,13},{10,... | collective-permute-start | bytes 6152 | tf_op jit(solution)/shard_map/ppermute | solution.py:802
  13.1 4.5 %collective-permute-start.6 = (f32[24,8,256]{2,1,0:T(8,128)S(1)}, f32[24,8,256]{2,1,0:T(8,128)S(1)}, u32[]{:S(2)}, u32[]{:S(2)}) collective-permute-start(f32[24,8,256]{2,1,0:T(8,128)S(1)} %get-tuple-element.72), channel_id=1, source_target_pairs={{8,16},{16,8},{9,17},{17,9},{10,18},{18,10},{11,19},{19,11},{12,20... | collective-permute-start | bytes 589832 | tf_op jit(solution)/shard_map/ppermute | solution.py:798
  18.3 3.5 %collective-permute-start.2 = (f32[35,8,256]{2,1,0:T(8,128)S(1)}, f32[35,8,256]{2,1,0:T(8,128)S(1)}, u32[]{:S(2)}, u32[]{:S(2)}) collective-permute-start(f32[35,8,256]{2,1,0:T(8,128)S(1)} %get-tuple-element.67), channel_id=1, source_target_pairs={{8,16},{16,8},{9,17},{17,9},{10,18},{18,10},{11,19},{19,11},{12,20... | collective-permute-start | bytes 860168 | tf_op jit(solution)/shard_map/ppermute | solution.py:798
  22.1 2.2 %collective-permute-start.8 = (f32[296,256]{1,0:T(8,128)S(1)}, f32[296,256]{1,0:T(8,128)S(1)}, u32[]{:S(2)}, u32[]{:S(2)}) collective-permute-start(f32[296,256]{1,0:T(8,128)S(1)} %get-tuple-element.74), channel_id=1, source_target_pairs={{0,1},{2,3},{4,5},{6,7},{1,0},{3,2},{5,4},{7,6},{8,9},{10,11},{12,... | collective-permute-start | bytes 909320 | tf_op jit(solution)/shard_map/ppermute | solution.py:798
  25.0 1.6 %collective-permute-done.2.x_a = f32[35,8,256]{2,1,0:T(8,128)S(1)} collective-permute-done((f32[35,8,256]{2,1,0:T(8,128)S(1)}, f32[35,8,256]{2,1,0:T(8,128)S(1)}, u32[]{:S(2)}, u32[]{:S(2)}) %collective-permute-start.2) | collective-permute-done | bytes 286752 | tf_op jit(solution)/shard_map/ppermute | solution.py:798
  26.5 4.7 %sweeps.1.conc = f32[32,32,256]{2,1,0:T(8,128)S(1)} custom-call(f32[32,32,256]{2,1,0:T(8,128)S(1)} %copy-done.1, s32[32,32,256]{2,1,0:T(8,128)S(1)} %copy-done, f32[32,32,256]{2,1,0:T(8,128)S(1)} %get-tuple-element.62.gain_own, f32[32,32,256]{2,1,0:T(8,128)S(1)} %get-tuple-element.63.base_own, f32[224,256]{1,0:T(8,128)S(1)} %collective-permute-done.r_a.y_a, ...), custom_call_target="tpu_custom_call" | custom-call | flops 1000000 | bytes 6275072 | tf_op jit(solution)/shard_map/sweeps/pallas_call | solution.py:36
  31.3 0.8 flux.1
  32.8 4.7 %collective-permute-start.10 = (f32[96,256]{1,0:T(8,128)S(1)}, f32[96,256]{1,0:T(8,128)S(1)}, u32[]{:S(2)}, u32[]{:S(2)}) collective-permute-start(f32[96,256]{1,0:T(8,128)S(1)} %get-tuple-element.79), channel_id=1, source_target_pairs={{0,1},{2,3},{4,5},{6,7},{1,0},{3,2},{5,4},{7,6},{8,9},{10,11},{12,... | collective-permute-start | bytes 294920 | tf_op jit(solution)/shard_map/ppermute | solution.py:798
  37.5 0.8 ready.1
  38.2 0.8 mask.1
  39.1 2.7 %collective-permute-done.10.r_b.y_b = f32[96,256]{1,0:T(8,128)S(1)} collective-permute-done((f32[96,256]{1,0:T(8,128)S(1)}, f32[96,256]{1,0:T(8,128)S(1)}, u32[]{:S(2)}, u32[]{:S(2)}) %collective-permute-start.10) | collective-permute-done | bytes 98336 | tf_op jit(solution)/shard_map/ppermute | solution.py:798
  41.8 2.4 %collective-permute-start.11 = (f32[15,8,256]{2,1,0:T(8,128)S(1)}, f32[15,8,256]{2,1,0:T(8,128)S(1)}, u32[]{:S(2)}, u32[]{:S(2)}) collective-permute-start(f32[15,8,256]{2,1,0:T(8,128)S(1)} %get-tuple-element.82), channel_id=1, source_target_pairs={{8,16},{16,8},{9,17},{17,9},{10,18},{18,10},{11,19},{19,11},{12,20... | collective-permute-start | bytes 368648 | tf_op jit(solution)/shard_map/ppermute | solution.py:798
  44.4 3.3 %potential_inner.1 = (f32[40,40,256]{2,1,0:T(8,128)S(1)}, f32[40,40,256]{2,1,0:T(8,128)S(1)}, f32[40,40,256]{2,1,0:T(8,128)S(1)}, f32[16,16,256]{2,1,0:T(8,128)S(1)}, f32[40,40,256]{2,1,0:T(8,128)S(1)}) custom-call(f32[32,32,256]{2,1,0:T(8,128)S(1)} %get-tuple-element.75.flux, f32[32,8,256]{2,1,0:T(8,128)S(1)} %get-tuple-element.80.mask, ...), custom_call_target="tpu_custom_call" | custom-call | flops 1000000 | bytes 13639680 | tf_op jit(solution)/shard_map/potential_inner/pallas_call | solution.py:36
  49.3 4.7 %collective-permute-start.15 = (f32[64,256]{1,0:T(8,128)S(1)}, f32[64,256]{1,0:T(8,128)S(1)}, u32[]{:S(2)}, u32[]{:S(2)}) collective-permute-start(f32[64,256]{1,0:T(8,128)S(1)} %get-tuple-element.94), channel_id=1, source_target_pairs={{0,1},{2,3},{4,5},{6,7},{1,0},{3,2},{5,4},{7,6},{8,9},{10,11},{12,... | collective-permute-start | bytes 196616 | tf_op jit(solution)/shard_map/ppermute | solution.py:798
  54.1 1.2 %coarse_ready.1 = (f32[8,8,256]{2,1,0:T(8,128)S(1)}, f32[8,128]{1,0:T(8,128)S(1)}, f32[8,128]{1,0:T(8,128)S(1)}) custom-call(f32[8,8,256]{2,1,0:T(8,128)S(1)} %get-tuple-element.66.token.coarse.own, f32[288,256]{1,0:T(8,128)S(1)} %collective-permute-done.13.yy_a.r_a.far_a, f32[296,256]{1,0:T(8,128)S(1)} %collective-permute-done.8.far.yy_b.r_b.far_b), custom_call_target="tpu_custom_call" | custom-call | flops 1000000 | bytes 737280 | tf_op jit(solution)/shard_map/coarse_ready/pallas_call | solution.py:36
  55.3 1.4 %store.1 = (f32[32,32,256]{2,1,0:T(8,128)}, f32[32,32,256]{2,1,0:T(8,128)}, f32[8,128]{1,0:T(8,128)S(1)}) custom-call(f32[32,32,256]{2,1,0:T(8,128)S(1)} %sweeps.1.conc, f32[32,32,256]{2,1,0:T(8,128)S(1)} %get-tuple-element.75.flux), custom_call_target="tpu_custom_call" | custom-call | flops 1000000 | bytes 4198400 | tf_op jit(solution)/shard_map/store/pallas_call | solution.py:36
  56.9 3.3 %collective-permute-start.16 = (f32[12,8,256]{2,1,0:T(8,128)S(1)}, f32[12,8,256]{2,1,0:T(8,128)S(1)}, u32[]{:S(2)}, u32[]{:S(2)}) collective-permute-start(f32[12,8,256]{2,1,0:T(8,128)S(1)} %get-tuple-element.97), channel_id=1, source_target_pairs={{8,16},{16,8},{9,17},{17,9},{10,18},{18,10},{11,19},{19,11},{12,20... | collective-permute-start | bytes 294920 | tf_op jit(solution)/shard_map/ppermute | solution.py:798
  60.3 2.6 %collective-permute-done.16.x_a = f32[12,8,256]{2,1,0:T(8,128)S(1)} collective-permute-done((f32[12,8,256]{2,1,0:T(8,128)S(1)}, f32[12,8,256]{2,1,0:T(8,128)S(1)}, u32[]{:S(2)}, u32[]{:S(2)}) %collective-permute-start.16) | collective-permute-done | bytes 98336 | tf_op jit(solution)/shard_map/ppermute | solution.py:798
  62.9 1.1 %middle.1 = (f32[24,24,256]{2,1,0:T(8,128)S(1)}, f32[24,24,256]{2,1,0:T(8,128)S(1)}, f32[24,24,256]{2,1,0:T(8,128)S(1)}, f32[8,12,256]{2,1,0:T(8,128)S(1)}, f32[...) custom-call(f32[16,16,256]{2,1,0:T(8,128)S(1)} %get-tuple-element.92.field.source_o, ...), custom_call_target="tpu_custom_call" | custom-call | flops 1000000 | bytes 4034560 | tf_op jit(solution)/shard_map/middle/pallas_call | solution.py:36
  63.9 3.3 %collective-permute-start.19 = (f32[8,256]{1,0:T(8,128)S(1)}, f32[8,256]{1,0:T(8,128)S(1)}, u32[]{:S(2)}, u32[]{:S(2)}) collective-permute-start(f32[8,256]{1,0:T(8,128)S(1)} %get-tuple-element.105), channel_id=1, source_target_pairs={{0,4},{1,5},{2,6},{3,7},{4,0},{5,1},{6,2},{7,3},{8,12},{9,13},{10,... | collective-permute-start | bytes 24584 | tf_op jit(solution)/shard_map/ppermute | solution.py:802
  68.3 3.4 %collective-permute-start.20 = (f32[72,256]{1,0:T(8,128)S(1)}, f32[72,256]{1,0:T(8,128)S(1)}, u32[]{:S(2)}, u32[]{:S(2)}) collective-permute-start(f32[72,256]{1,0:T(8,128)S(1)} %late.1), channel_id=1, source_target_pairs={{0,1},{2,3},{4,5},{6,7},{1,0},{3,2},{5,4},{7,6},{8,9},{10,11},{12,... | collective-permute-start | bytes 221192 | tf_op jit(solution)/shard_map/ppermute | solution.py:798
  71.8 2.5 %collective-permute-done.21 = f32[8,256]{1,0:T(8,128)S(1)} collective-permute-done((f32[8,256]{1,0:T(8,128)S(1)}, f32[8,256]{1,0:T(8,128)S(1)}, u32[]{:S(2)}, u32[]{:S(2)}) %collective-permute-start.21) | collective-permute-done | bytes 8224 | tf_op jit(solution)/shard_map/ppermute | solution.py:802
  74.6 1.2 %coarse.1.error = f32[8,16,256]{2,1,0:T(8,128)S(1)} custom-call(f32[8,12,256]{2,1,0:T(8,128)S(1)} %get-tuple-element.101.own, f32[8,12,256]{2,1,0:T(8,128)S(1)} %get-tuple-element.102.conduct, f32[288,256]{1,0:T(8,128)S(1)} %collective-permute-done.13.yy_a.r_a.far_a, f32[296,256]{1,0:T(8,128)S(1)} %collective-permute-done.8.far.yy_b.r_b.far_b, ...), custom_call_target="tpu_custom_call" | custom-call | flops 1000000 | bytes 1073152 | tf_op jit(solution)/shard_map/coarse/pallas_call | solution.py:36
  75.8 1.0 %collective-permute-done.22.sums_other = f32[8,256]{1,0:T(8,128)S(1)} collective-permute-done((f32[8,256]{1,0:T(8,128)S(1)}, f32[8,256]{1,0:T(8,128)S(1)}, u32[]{:S(2)}, u32[]{:S(2)}) %collective-permute-start.22) | collective-permute-done | bytes 8224 | tf_op jit(solution)/shard_map/ppermute | solution.py:802
  76.9 6.4 %collective-permute-start.23 = (f32[2,16,256]{2,1,0:T(8,128)S(1)}, f32[2,16,256]{2,1,0:T(8,128)S(1)}, u32[]{:S(2)}, u32[]{:S(2)}) collective-permute-start(f32[2,16,256]{2,1,0:T(8,128)S(1)} %get-tuple-element.106), channel_id=1, source_target_pairs={{8,16},{16,8},{9,17},{17,9},{10,18},{18,10},{11,19},{19,11},{12,20... | collective-permute-start | bytes 98312 | tf_op jit(solution)/shard_map/ppermute | solution.py:798
  83.4 2.6 %finish_inner.1 = (f32[32,32,256]{2,1,0:T(8,128)}, f32[24,24,256]{2,1,0:T(8,128)S(1)}, f32[24,24,256]{2,1,0:T(8,128)S(1)}, f32[40,40,256]{2,1,0:T(8,128)S(1)}, f32[40,40,256]{2,1,0:T(8,128)S(1)}) custom-call(f32[8,16,256]{2,1,0:T(8,128)S(1)} %get-tuple-element.113.error, f32[24,24,256]{2,1,0:T(8,128)S(1)} %get-tuple-element.108.mid_two, ...), custom_call_target="tpu_custom_call" | custom-call | flops 1000000 | bytes 12320768 | tf_op jit(solution)/shard_map/finish_inner/pallas_call | solution.py:36
  86.0 1.7 %finish_edge.1 = f32[32,32,256]{2,1,0:T(8,128)} custom-call(f32[2,16,256]{2,1,0:T(8,128)S(1)} %collective-permute-done.23.x_a, f32[2,16,256]{2,1,0:T(8,128)S(1)} %collective-permute-done.24.x_b, f32[24,24,256]{2,1,0:T(8,128)S(1)} %get-tuple-element.108.mid_two, f32[24,24,256]{2,1,0:T(8,128)S(1)} %get-tuple-element.109.mid_source, ...), custom_call_target="tpu_custom_call", output_to_operand_aliasing={{}: (14, {})} | custom-call | flops 1000000 | bytes 14614528 | tf_op jit(solution)/shard_map/finish_edge/pallas_call | solution.py:36
  (54 shorter events, 6.5 us)
Async XLA Ops:
  0.6 7.5 %copy-start = (s32[32,32,256]{2,1,0:T(8,128)S(1)}, s32[32,32,256]{2,1,0:T(8,128)}, u32[]{:S(2)}) copy-start(s32[32,32,256]{2,1,0:T(8,128)} %label.11) | copy-start | bytes 3145732
  0.6 7.5 %copy-start.1 = (f32[32,32,256]{2,1,0:T(8,128)S(1)}, f32[32,32,256]{2,1,0:T(8,128)}, u32[]{:S(2)}) copy-start(f32[32,32,256]{2,1,0:T(8,128)} %conc.9) | copy-start | bytes 3145732
  2.8 15.0 %collective-permute-start = (f32[224,256]{1,0:T(8,128)}, f32[224,256]{1,0:T(8,128)S(1)}, u32[]{:S(2)}, u32[]{:S(2)}) collective-permute-start(f32[224,256]{1,0:T(8,128)} %get-tuple-element.64), channel_id=1, source_target_pairs={{1,2},{3,4},{5,6},{2,1},{4,3},{6,5},{9,10},{11,12},{13,14},{10,9},... | collective-permute-start | bytes 688136 | tf_op jit(solution)/shard_map/ppermute | solution.py:798
  3.5 14.7 %collective-permute-start.1 = (f32[224,256]{1,0:T(8,128)}, f32[224,256]{1,0:T(8,128)S(1)}, u32[]{:S(2)}, u32[]{:S(2)}) collective-permute-start(f32[224,256]{1,0:T(8,128)} %get-tuple-element.65), channel_id=1, source_target_pairs={{0,1},{2,3},{4,5},{6,7},{1,0},{3,2},{5,4},{7,6},{8,9},{10,11},{12,... | collective-permute-start | bytes 688136 | tf_op jit(solution)/shard_map/ppermute | solution.py:798
  8.1 1.2 %copy-start.2 = (f32[32,32,256]{2,1,0:T(8,128)S(1)}, f32[32,32,256]{2,1,0:T(8,128)}, u32[]{:S(2)}) copy-start(f32[32,32,256]{2,1,0:T(8,128)} %phi.7) | copy-start | bytes 3145732
  9.3 0.7 copy-start.5
  10.7 11.3 %copy-start.3 = (f32[32,32,256]{2,1,0:T(8,128)S(1)}, f32[32,32,256]{2,1,0:T(8,128)}, u32[]{:S(2)}) copy-start(f32[32,32,256]{2,1,0:T(8,128)} %phi.7) | copy-start | bytes 3145732
  10.7 7.0 %collective-permute-start.4 = (f32[2,256]{1,0:T(2,128)S(1)}, f32[2,256]{1,0:T(2,128)S(1)}, u32[]{:S(2)}, u32[]{:S(2)}) collective-permute-start(f32[2,256]{1,0:T(2,128)S(1)} %get-tuple-element.70), channel_id=1, source_target_pairs={{0,4},{1,5},{2,6},{3,7},{4,0},{5,1},{6,2},{7,3},{8,12},{9,13},{10,... | collective-permute-start | bytes 6152 | tf_op jit(solution)/shard_map/ppermute | solution.py:802
  13.1 8.9 %collective-permute-start.6 = (f32[24,8,256]{2,1,0:T(8,128)S(1)}, f32[24,8,256]{2,1,0:T(8,128)S(1)}, u32[]{:S(2)}, u32[]{:S(2)}) collective-permute-start(f32[24,8,256]{2,1,0:T(8,128)S(1)} %get-tuple-element.72), channel_id=1, source_target_pairs={{8,16},{16,8},{9,17},{17,9},{10,18},{18,10},{11,19},{19,11},{12,20... | collective-permute-start | bytes 589832 | tf_op jit(solution)/shard_map/ppermute | solution.py:798
  17.6 4.3 %collective-permute-start.7 = (f32[24,8,256]{2,1,0:T(8,128)S(1)}, f32[24,8,256]{2,1,0:T(8,128)S(1)}, u32[]{:S(2)}, u32[]{:S(2)}) collective-permute-start(f32[24,8,256]{2,1,0:T(8,128)S(1)} %get-tuple-element.73), channel_id=1, source_target_pairs={{0,8},{16,24},{8,0},{24,16},{1,9},{17,25},{9,1},{25,17},{2,10},{18... | collective-permute-start | bytes 589832 | tf_op jit(solution)/shard_map/ppermute | solution.py:798
  17.7 4.2 %collective-permute-start.5 = (f32[4,256]{1,0:T(4,128)S(1)}, f32[4,256]{1,0:T(4,128)S(1)}, u32[]{:S(2)}, u32[]{:S(2)}) collective-permute-start(f32[4,256]{1,0:T(4,128)S(1)} %pad_maximum_fusion.1), channel_id=1, source_target_pairs={{0,2},{1,3},{2,0},{3,1},{4,6},{5,7},{6,4},{7,5},{8,10},{9,11},{10,... | collective-permute-start | bytes 12296 | tf_op jit(solution)/shard_map/ppermute | solution.py:802
  18.3 8.2 %collective-permute-start.2 = (f32[35,8,256]{2,1,0:T(8,128)S(1)}, f32[35,8,256]{2,1,0:T(8,128)S(1)}, u32[]{:S(2)}, u32[]{:S(2)}) collective-permute-start(f32[35,8,256]{2,1,0:T(8,128)S(1)} %get-tuple-element.67), channel_id=1, source_target_pairs={{8,16},{16,8},{9,17},{17,9},{10,18},{18,10},{11,19},{19,11},{12,20... | collective-permute-start | bytes 860168 | tf_op jit(solution)/shard_map/ppermute | solution.py:798
  21.8 4.7 %collective-permute-start.3 = (f32[35,8,256]{2,1,0:T(8,128)S(1)}, f32[35,8,256]{2,1,0:T(8,128)S(1)}, u32[]{:S(2)}, u32[]{:S(2)}) collective-permute-start(f32[35,8,256]{2,1,0:T(8,128)S(1)} %get-tuple-element.68), channel_id=1, source_target_pairs={{0,8},{16,24},{8,0},{24,16},{1,9},{17,25},{9,1},{25,17},{2,10},{18... | collective-permute-start | bytes 860168 | tf_op jit(solution)/shard_map/ppermute | solution.py:798
  22.1 16.1 %collective-permute-start.8 = (f32[296,256]{1,0:T(8,128)S(1)}, f32[296,256]{1,0:T(8,128)S(1)}, u32[]{:S(2)}, u32[]{:S(2)}) collective-permute-start(f32[296,256]{1,0:T(8,128)S(1)} %get-tuple-element.74), channel_id=1, source_target_pairs={{0,1},{2,3},{4,5},{6,7},{1,0},{3,2},{5,4},{7,6},{8,9},{10,11},{12,... | collective-permute-start | bytes 909320 | tf_op jit(solution)/shard_map/ppermute | solution.py:798
  24.3 20.1 %collective-permute-start.13 = (f32[288,256]{1,0:T(8,128)S(1)}, f32[288,256]{1,0:T(8,128)S(1)}, u32[]{:S(2)}, u32[]{:S(2)}) collective-permute-start(f32[288,256]{1,0:T(8,128)S(1)} %get-tuple-element.86), channel_id=1, source_target_pairs={{1,2},{3,4},{5,6},{2,1},{4,3},{6,5},{9,10},{11,12},{13,14},{10,9},... | collective-permute-start | bytes 884744 | tf_op jit(solution)/shard_map/ppermute | solution.py:798
  26.5 4.8 %copy-start.4 = (f32[32,32,256]{2,1,0:T(8,128)S(1)}, f32[32,32,256]{2,1,0:T(8,128)}, u32[]{:S(2)}) copy-start(f32[32,32,256]{2,1,0:T(8,128)} %solid.1) | copy-start | bytes 3145732
  32.1 7.0 %collective-permute-start.9 = (f32[96,256]{1,0:T(8,128)S(1)}, f32[96,256]{1,0:T(8,128)S(1)}, u32[]{:S(2)}, u32[]{:S(2)}) collective-permute-start(f32[96,256]{1,0:T(8,128)S(1)} %get-tuple-element.78), channel_id=1, source_target_pairs={{1,2},{3,4},{5,6},{2,1},{4,3},{6,5},{9,10},{11,12},{13,14},{10,9},... | collective-permute-start | bytes 294920 | tf_op jit(solution)/shard_map/ppermute | solution.py:798
  32.8 9.0 %collective-permute-start.10 = (f32[96,256]{1,0:T(8,128)S(1)}, f32[96,256]{1,0:T(8,128)S(1)}, u32[]{:S(2)}, u32[]{:S(2)}) collective-permute-start(f32[96,256]{1,0:T(8,128)S(1)} %get-tuple-element.79), channel_id=1, source_target_pairs={{0,1},{2,3},{4,5},{6,7},{1,0},{3,2},{5,4},{7,6},{8,9},{10,11},{12,... | collective-permute-start | bytes 294920 | tf_op jit(solution)/shard_map/ppermute | solution.py:798
  41.8 6.2 %collective-permute-start.11 = (f32[15,8,256]{2,1,0:T(8,128)S(1)}, f32[15,8,256]{2,1,0:T(8,128)S(1)}, u32[]{:S(2)}, u32[]{:S(2)}) collective-permute-start(f32[15,8,256]{2,1,0:T(8,128)S(1)} %get-tuple-element.82), channel_id=1, source_target_pairs={{8,16},{16,8},{9,17},{17,9},{10,18},{18,10},{11,19},{19,11},{12,20... | collective-permute-start | bytes 368648 | tf_op jit(solution)/shard_map/ppermute | solution.py:798
  44.3 3.8 %collective-permute-start.12 = (f32[15,8,256]{2,1,0:T(8,128)S(1)}, f32[15,8,256]{2,1,0:T(8,128)S(1)}, u32[]{:S(2)}, u32[]{:S(2)}) collective-permute-start(f32[15,8,256]{2,1,0:T(8,128)S(1)} %get-tuple-element.83), channel_id=1, source_target_pairs={{0,8},{16,24},{8,0},{24,16},{1,9},{17,25},{9,1},{25,17},{2,10},{18... | collective-permute-start | bytes 368648 | tf_op jit(solution)/shard_map/ppermute | solution.py:798
  48.7 8.0 %collective-permute-start.14 = (f32[64,256]{1,0:T(8,128)S(1)}, f32[64,256]{1,0:T(8,128)S(1)}, u32[]{:S(2)}, u32[]{:S(2)}) collective-permute-start(f32[64,256]{1,0:T(8,128)S(1)} %get-tuple-element.93), channel_id=1, source_target_pairs={{1,2},{3,4},{5,6},{2,1},{4,3},{6,5},{9,10},{11,12},{13,14},{10,9},... | collective-permute-start | bytes 196616 | tf_op jit(solution)/shard_map/ppermute | solution.py:798
  49.3 7.5 %collective-permute-start.15 = (f32[64,256]{1,0:T(8,128)S(1)}, f32[64,256]{1,0:T(8,128)S(1)}, u32[]{:S(2)}, u32[]{:S(2)}) collective-permute-start(f32[64,256]{1,0:T(8,128)S(1)} %get-tuple-element.94), channel_id=1, source_target_pairs={{0,1},{2,3},{4,5},{6,7},{1,0},{3,2},{5,4},{7,6},{8,9},{10,11},{12,... | collective-permute-start | bytes 196616 | tf_op jit(solution)/shard_map/ppermute | solution.py:798
  56.9 5.9 %collective-permute-start.16 = (f32[12,8,256]{2,1,0:T(8,128)S(1)}, f32[12,8,256]{2,1,0:T(8,128)S(1)}, u32[]{:S(2)}, u32[]{:S(2)}) collective-permute-start(f32[12,8,256]{2,1,0:T(8,128)S(1)} %get-tuple-element.97), channel_id=1, source_target_pairs={{8,16},{16,8},{9,17},{17,9},{10,18},{18,10},{11,19},{19,11},{12,20... | collective-permute-start | bytes 294920 | tf_op jit(solution)/shard_map/ppermute | solution.py:798
  60.2 2.7 %collective-permute-start.17 = (f32[12,8,256]{2,1,0:T(8,128)S(1)}, f32[12,8,256]{2,1,0:T(8,128)S(1)}, u32[]{:S(2)}, u32[]{:S(2)}) collective-permute-start(f32[12,8,256]{2,1,0:T(8,128)S(1)} %get-tuple-element.98), channel_id=1, source_target_pairs={{0,8},{16,24},{8,0},{24,16},{1,9},{17,25},{9,1},{25,17},{2,10},{18... | collective-permute-start | bytes 294920 | tf_op jit(solution)/shard_map/ppermute | solution.py:798
  63.9 4.4 %collective-permute-start.19 = (f32[8,256]{1,0:T(8,128)S(1)}, f32[8,256]{1,0:T(8,128)S(1)}, u32[]{:S(2)}, u32[]{:S(2)}) collective-permute-start(f32[8,256]{1,0:T(8,128)S(1)} %get-tuple-element.105), channel_id=1, source_target_pairs={{0,4},{1,5},{2,6},{3,7},{4,0},{5,1},{6,2},{7,3},{8,12},{9,13},{10,... | collective-permute-start | bytes 24584 | tf_op jit(solution)/shard_map/ppermute | solution.py:802
  67.3 7.4 %collective-permute-start.18 = (f32[72,256]{1,0:T(8,128)S(1)}, f32[72,256]{1,0:T(8,128)S(1)}, u32[]{:S(2)}, u32[]{:S(2)}) collective-permute-start(f32[72,256]{1,0:T(8,128)S(1)} %get-tuple-element.103), channel_id=1, source_target_pairs={{1,2},{3,4},{5,6},{2,1},{4,3},{6,5},{9,10},{11,12},{13,14},{10,9},... | collective-permute-start | bytes 221192 | tf_op jit(solution)/shard_map/ppermute | solution.py:798
  68.3 6.3 %collective-permute-start.20 = (f32[72,256]{1,0:T(8,128)S(1)}, f32[72,256]{1,0:T(8,128)S(1)}, u32[]{:S(2)}, u32[]{:S(2)}) collective-permute-start(f32[72,256]{1,0:T(8,128)S(1)} %late.1), channel_id=1, source_target_pairs={{0,1},{2,3},{4,5},{6,7},{1,0},{3,2},{5,4},{7,6},{8,9},{10,11},{12,... | collective-permute-start | bytes 221192 | tf_op jit(solution)/shard_map/ppermute | solution.py:798
  71.8 2.5 %collective-permute-start.21 = (f32[8,256]{1,0:T(8,128)S(1)}, f32[8,256]{1,0:T(8,128)S(1)}, u32[]{:S(2)}, u32[]{:S(2)}) collective-permute-start(f32[8,256]{1,0:T(8,128)S(1)} %add.6.token), channel_id=1, source_target_pairs={{0,2},{1,3},{2,0},{3,1},{4,6},{5,7},{6,4},{7,5},{8,10},{9,11},{10,... | collective-permute-start | bytes 24584 | tf_op jit(solution)/shard_map/ppermute | solution.py:802
  74.3 2.5 %collective-permute-start.22 = (f32[8,256]{1,0:T(8,128)S(1)}, f32[8,256]{1,0:T(8,128)S(1)}, u32[]{:S(2)}, u32[]{:S(2)}) collective-permute-start(f32[8,256]{1,0:T(8,128)S(1)} %add.7.sums_own), channel_id=1, source_target_pairs={{0,1},{1,0},{2,3},{3,2},{4,5},{5,4},{6,7},{7,6},{8,9},{9,8},{10,11... | collective-permute-start | bytes 24584 | tf_op jit(solution)/shard_map/ppermute | solution.py:802
  76.9 9.1 %collective-permute-start.23 = (f32[2,16,256]{2,1,0:T(8,128)S(1)}, f32[2,16,256]{2,1,0:T(8,128)S(1)}, u32[]{:S(2)}, u32[]{:S(2)}) collective-permute-start(f32[2,16,256]{2,1,0:T(8,128)S(1)} %get-tuple-element.106), channel_id=1, source_target_pairs={{8,16},{16,8},{9,17},{17,9},{10,18},{18,10},{11,19},{19,11},{12,20... | collective-permute-start | bytes 98312 | tf_op jit(solution)/shard_map/ppermute | solution.py:798
  83.3 2.7 %collective-permute-start.24 = (f32[2,16,256]{2,1,0:T(8,128)S(1)}, f32[2,16,256]{2,1,0:T(8,128)S(1)}, u32[]{:S(2)}, u32[]{:S(2)}) collective-permute-start(f32[2,16,256]{2,1,0:T(8,128)S(1)} %get-tuple-element.107), channel_id=1, source_target_pairs={{0,8},{16,24},{8,0},{24,16},{1,9},{17,25},{9,1},{25,17},{2,10},{18... | collective-permute-start | bytes 98312 | tf_op jit(solution)/shard_map/ppermute | solution.py:798

commit v9 on v8

--- a/solution.py
+++ b/solution.py
@@ -581,6 +581,7 @@
         send_y(pay_a, pay_b, 9 * i + 8, k[8:9], k[11:12])
         total += rho[i] * value[0:8]
     sums = jnp.concatenate([total[:, :LANES] + total[:, LANES:], load[...]], axis=1)
+    pay_b[72:80, :] = sums
     part[...] = sums
 
 
@@ -618,8 +619,12 @@
     load[...] = total[:, :LANES] + total[:, LANES:]
 
 
-def late_kernel(pay, token, out):
-    out[...] = pay[...]
+def pair_kernel(sums, other, out):
+    total = sums[...] + other[72:80, :]
+    resid, load = total[:, :LANES], total[:, LANES:]
+    tile = jnp.concatenate([resid[0:4] + resid[4:8], load[0:4] + load[4:8]], axis=0)
+    for i in range(out.shape[0]):
+        out[i] = tile
 
 
 def coarse_kernel(own, conduct, far_a, far_b, r_a, r_b, error, source, weight, one, two):
@@ -652,10 +657,10 @@
         error[x, 8:16, :] = jnp.where(upper(), old[x, 8:16, :], old[x, 24:32, :])
 
 
-def shift_kernel(error, sums_own, sums_other, out, pay_a, pay_b):
-    sums = sums_own[...] + sums_other[...]
-    resid = jnp.sum(sums[:, :LANES])
-    load = jnp.sum(sums[:, LANES:])
+def shift_kernel(error, sums, out, pay_a, pay_b):
+    total = jnp.sum(sums[...], axis=0)
+    resid = jnp.sum(total[0:4])
+    load = jnp.sum(total[4:8])
     shift_c = jnp.full((16, 256), resid, F32) / jnp.full((16, 256), load, F32)
     for x in range(8):
         out[x] = error[x] + shift_c
@@ -923,19 +928,15 @@
     mid_two, mid_source, mid_weight, source_coarse, wide_coarse, pay_a, pay_b, sums = call(
         mid_kernel,
         [shaped(*ext_mid)] * 3
-        + [shaped(quarter, 12, 256), shaped(quarter, 12, 256), shaped(72, 256), shaped(72, 256), shaped(8, 256)],
+        + [shaped(quarter, 12, 256), shaped(quarter, 12, 256), shaped(72, 256), shaped(80, 256), shaped(8, 256)],
         [source_mid, conduct_mid, yy_a, yy_b, xx_a, xx_b, m_a, m_b, mx_a, mx_b, rho, load],
         [vmem(*ext_mid)] * 2 + [vmem(8, 2, half + 2 * HALO, LANES)] * 2,
         name="middle",
     )
-    distance = peers // 2
-    early = sums = sums + exchange(sums, distance)
-    while distance > 2:
-        distance //= 2
-        sums = sums + exchange(sums, distance)
-    (pay_b,) = call(late_kernel, [shaped(72, 256)], [pay_b, early], name="late")
     c_a, c_b = swap(pay_a, pay_b, "dev")
-    other_sums = exchange(sums, 1)
+    groups = [list(range(0, peers, 2)), list(range(1, peers, 2))]
+    (sums,) = call(pair_kernel, [shaped(peers // 2, 8, LANES)], [sums, c_b], name="pair")
+    sums = lax.all_to_all(sums, "dev", 0, 0, axis_index_groups=groups, tiled=True)
     (error,) = call(
         coarse_kernel,
         [shaped(8, 16, 256)],
@@ -944,7 +945,7 @@
         name="coarse",
     )
     error, pay_a, pay_b = call(
-        shift_kernel, [shaped(8, 16, 256), shaped(2, 16, 256), shaped(2, 16, 256)], [error, sums, other_sums], name="shift"
+        shift_kernel, [shaped(8, 16, 256), shaped(2, 16, 256), shaped(2, 16, 256)], [error, sums], name="shift"
     )
     e_a, e_b = swap(pay_a, pay_b, "grp")
     begun, zero, one, fine_one, fine_last = call(

time: 88.6 us -> 100 us (1.13)
  local copies, waits for them, and re-layouts: 1.94 us -> 15.7 us
  waiting for transfers between devices: 11.7 us -> 8.98 us
  Pallas kernels: 23.4 us -> 24.4 us
  starting transfers between devices: 49.6 us -> 48.6 us
    unnamed x12 -> x56, local copies, waits for them, and re-layouts: 1.94 us -> 15.7 us
    all_to_all x0 -> x1, starting transfers between devices: none -> 5.16 us  [body(): lax.all_to_all(sums, 'dev', 0, 0, axis_index_groups=groups, tiled=True)]
    ppermute x5 -> x2, waiting for transfers between devices: 3.84 us -> 0.01 us  [exchange(): lax.ppermute(value, 'dev', [(i, i ^ distance) for i in range(lax.axis_siz...]
    ppermute x5 -> x2, starting transfers between devices: 6.15 us -> 2.45 us  [exchange(): lax.ppermute(value, 'dev', [(i, i ^ distance) for i in range(lax.axis_siz...]
    ppermute x10, waiting for transfers between devices: 3.35 us -> 4.73 us  [swap(): lax.ppermute(pay_b, axis, both_ways(pairs_b))]
    ppermute x10, starting transfers between devices: 23.5 us -> 22.3 us  [swap(): lax.ppermute(pay_a, axis, both_ways(pairs_a))]
    ppermute x10, starting transfers between devices: 20 us -> 18.8 us  [swap(): lax.ppermute(pay_b, axis, both_ways(pairs_b))]
  transfers between devices with their start and end apart: 25 -> 23, of which waited for: 9 -> 6; matrix products, arithmetic and copies ran while one was open for 0% -> 0% of each run, Pallas kernels for 20% -> 18%
where the time goes in v9:
time: 100 us; the launch traced here: 98.8 us
  starting transfers between devices  48.6 us (49%)
  Pallas kernels  24.4 us (24%)
  local copies, waits for them, and re-layouts  15.7 us (16%)
  waiting for transfers between devices  8.98 us (9%)
  between operations  1.1 us (1%)
    pallas_call x20, Pallas kernels, call(): pl.pallas_call(kernel, out_shape=tuple(outs), in_specs=in_specs or [WHOLE...  24.4 us
    ppermute x10, starting transfers between devices, swap(): lax.ppermute(pay_a, axis, both_ways(pairs_a))  22.3 us
    ppermute x10, starting transfers between devices, swap(): lax.ppermute(pay_b, axis, both_ways(pairs_b))  18.8 us
    unnamed x56, local copies, waits for them, and re-layouts  15.7 us
    all_to_all x1, starting transfers between devices, body(): lax.all_to_all(sums, 'dev', 0, 0, axis_index_groups=groups, tiled=True)  5.16 us
    ppermute x10, waiting for transfers between devices, swap(): lax.ppermute(pay_b, axis, both_ways(pairs_b))  4.73 us
    ppermute x10, waiting for transfers between devices, swap(): lax.ppermute(pay_a, axis, both_ways(pairs_a))  4.25 us
    ppermute x2, starting transfers between devices, exchange(): lax.ppermute(value, 'dev', [(i, i ^ distance) for i in range(lax.axis_siz...  2.45 us
  transfers between devices with their start and end apart: 23, of which 6 were waited for; matrix products, arithmetic and copies ran while one was open for 0% of the time, Pallas kernels for 18%

profile of v9, /device:TPU:1, one launch (start us, length us, event | category | flops | bytes accessed | tf_op | source)
XLA Modules:
  0.0 98.8 jit_solution(14046823733063998879)
XLA Ops:
  0.7 2.2 %first_pack.1 = (f32[224,256]{1,0:T(8,128)}, f32[224,256]{1,0:T(8,128)}, f32[8,256]{1,0:T(8,128)}) custom-call(f32[32,32,256]{2,1,0:T(8,128)} %conc.9, s32[32,32,256]{2,1,0:T(8,128)} %label.11, s32[1,256]{1,0:T(1,128)} %bitcast.1, s32[1,256]{1,0:T(1,128)} %block.1), custom_call_target="tpu_custom_call" | custom-call | flops 1000000 | bytes 2566144 | tf_op jit(solution)/shard_map/first_pack/pallas_call | solution.py:36
  3.5 4.6 %collective-permute-start.1 = (f32[224,256]{1,0:T(8,128)}, f32[224,256]{1,0:T(8,128)S(1)}, u32[]{:S(2)}, u32[]{:S(2)}) collective-permute-start(f32[224,256]{1,0:T(8,128)} %get-tuple-element.65), channel_id=1, source_target_pairs={{0,1},{2,3},{4,5},{6,7},{1,0},{3,2},{5,4},{7,6},{8,9},{10,11},{12,... | collective-permute-start | bytes 688136 | tf_op jit(solution)/shard_map/ppermute | solution.py:803
  8.1 1.2 %copy-done.2 = f32[32,32,256]{2,1,0:T(8,128)S(1)} copy-done((f32[32,32,256]{2,1,0:T(8,128)S(1)}, f32[32,32,256]{2,1,0:T(8,128)}, u32[]{:S(2)}) %copy-start.2) | copy-done | bytes 1048600
  10.7 2.4 %collective-permute-start.4 = (f32[2,256]{1,0:T(2,128)S(1)}, f32[2,256]{1,0:T(2,128)S(1)}, u32[]{:S(2)}, u32[]{:S(2)}) collective-permute-start(f32[2,256]{1,0:T(2,128)S(1)} %get-tuple-element.70), channel_id=1, source_target_pairs={{0,4},{1,5},{2,6},{3,7},{4,0},{5,1},{6,2},{7,3},{8,12},{9,13},{10,... | collective-permute-start | bytes 6152 | tf_op jit(solution)/shard_map/ppermute | solution.py:807
  13.1 4.5 %collective-permute-start.6 = (f32[24,8,256]{2,1,0:T(8,128)S(1)}, f32[24,8,256]{2,1,0:T(8,128)S(1)}, u32[]{:S(2)}, u32[]{:S(2)}) collective-permute-start(f32[24,8,256]{2,1,0:T(8,128)S(1)} %get-tuple-element.72), channel_id=1, source_target_pairs={{8,16},{16,8},{9,17},{17,9},{10,18},{18,10},{11,19},{19,11},{12,20... | collective-permute-start | bytes 589832 | tf_op jit(solution)/shard_map/ppermute | solution.py:803
  18.3 3.5 %collective-permute-start.2 = (f32[35,8,256]{2,1,0:T(8,128)S(1)}, f32[35,8,256]{2,1,0:T(8,128)S(1)}, u32[]{:S(2)}, u32[]{:S(2)}) collective-permute-start(f32[35,8,256]{2,1,0:T(8,128)S(1)} %get-tuple-element.67), channel_id=1, source_target_pairs={{8,16},{16,8},{9,17},{17,9},{10,18},{18,10},{11,19},{19,11},{12,20... | collective-permute-start | bytes 860168 | tf_op jit(solution)/shard_map/ppermute | solution.py:803
  22.1 2.2 %collective-permute-start.8 = (f32[296,256]{1,0:T(8,128)S(1)}, f32[296,256]{1,0:T(8,128)S(1)}, u32[]{:S(2)}, u32[]{:S(2)}) collective-permute-start(f32[296,256]{1,0:T(8,128)S(1)} %get-tuple-element.74), channel_id=1, source_target_pairs={{0,1},{2,3},{4,5},{6,7},{1,0},{3,2},{5,4},{7,6},{8,9},{10,11},{12,... | collective-permute-start | bytes 909320 | tf_op jit(solution)/shard_map/ppermute | solution.py:803
  25.0 1.6 %collective-permute-done.2.x_a = f32[35,8,256]{2,1,0:T(8,128)S(1)} collective-permute-done((f32[35,8,256]{2,1,0:T(8,128)S(1)}, f32[35,8,256]{2,1,0:T(8,128)S(1)}, u32[]{:S(2)}, u32[]{:S(2)}) %collective-permute-start.2) | collective-permute-done | bytes 286752 | tf_op jit(solution)/shard_map/ppermute | solution.py:803
  26.5 4.7 %sweeps.1.conc = f32[32,32,256]{2,1,0:T(8,128)S(1)} custom-call(f32[32,32,256]{2,1,0:T(8,128)S(1)} %copy-done.1, s32[32,32,256]{2,1,0:T(8,128)S(1)} %copy-done, f32[32,32,256]{2,1,0:T(8,128)S(1)} %get-tuple-element.62.gain_own, f32[32,32,256]{2,1,0:T(8,128)S(1)} %get-tuple-element.63.base_own, f32[224,256]{1,0:T(8,128)S(1)} %collective-permute-done.r_a.y_a, ...), custom_call_target="tpu_custom_call" | custom-call | flops 1000000 | bytes 6275072 | tf_op jit(solution)/shard_map/sweeps/pallas_call | solution.py:36
  32.7 4.7 %collective-permute-start.10 = (f32[96,256]{1,0:T(8,128)S(1)}, f32[96,256]{1,0:T(8,128)S(1)}, u32[]{:S(2)}, u32[]{:S(2)}) collective-permute-start(f32[96,256]{1,0:T(8,128)S(1)} %get-tuple-element.79), channel_id=1, source_target_pairs={{0,1},{2,3},{4,5},{6,7},{1,0},{3,2},{5,4},{7,6},{8,9},{10,11},{12,... | collective-permute-start | bytes 294920 | tf_op jit(solution)/shard_map/ppermute | solution.py:803
  39.0 2.9 %collective-permute-done.10.r_b.y_b = f32[96,256]{1,0:T(8,128)S(1)} collective-permute-done((f32[96,256]{1,0:T(8,128)S(1)}, f32[96,256]{1,0:T(8,128)S(1)}, u32[]{:S(2)}, u32[]{:S(2)}) %collective-permute-start.10) | collective-permute-done | bytes 98336 | tf_op jit(solution)/shard_map/ppermute | solution.py:803
  41.9 2.4 %collective-permute-start.11 = (f32[15,8,256]{2,1,0:T(8,128)S(1)}, f32[15,8,256]{2,1,0:T(8,128)S(1)}, u32[]{:S(2)}, u32[]{:S(2)}) collective-permute-start(f32[15,8,256]{2,1,0:T(8,128)S(1)} %get-tuple-element.82), channel_id=1, source_target_pairs={{8,16},{16,8},{9,17},{17,9},{10,18},{18,10},{11,19},{19,11},{12,20... | collective-permute-start | bytes 368648 | tf_op jit(solution)/shard_map/ppermute | solution.py:803
  44.4 3.3 %potential_inner.1 = (f32[40,40,256]{2,1,0:T(8,128)S(1)}, f32[40,40,256]{2,1,0:T(8,128)S(1)}, f32[40,40,256]{2,1,0:T(8,128)S(1)}, f32[16,16,256]{2,1,0:T(8,128)S(1)}, f32[40,40,256]{2,1,0:T(8,128)S(1)}) custom-call(f32[32,32,256]{2,1,0:T(8,128)S(1)} %get-tuple-element.75.flux, f32[32,8,256]{2,1,0:T(8,128)S(1)} %get-tuple-element.80.mask, ...), custom_call_target="tpu_custom_call" | custom-call | flops 1000000 | bytes 13639680 | tf_op jit(solution)/shard_map/potential_inner/pallas_call | solution.py:36
  49.5 4.8 %collective-permute-start.15 = (f32[64,256]{1,0:T(8,128)S(1)}, f32[64,256]{1,0:T(8,128)S(1)}, u32[]{:S(2)}, u32[]{:S(2)}) collective-permute-start(f32[64,256]{1,0:T(8,128)S(1)} %get-tuple-element.94), channel_id=1, source_target_pairs={{0,1},{2,3},{4,5},{6,7},{1,0},{3,2},{5,4},{7,6},{8,9},{10,11},{12,... | collective-permute-start | bytes 196616 | tf_op jit(solution)/shard_map/ppermute | solution.py:803
  54.3 1.2 %coarse_ready.1 = (f32[8,8,256]{2,1,0:T(8,128)S(1)}, f32[8,128]{1,0:T(8,128)S(1)}, f32[8,128]{1,0:T(8,128)S(1)}) custom-call(f32[8,8,256]{2,1,0:T(8,128)S(1)} %get-tuple-element.66.token.coarse.own, f32[288,256]{1,0:T(8,128)S(1)} %collective-permute-done.13.yy_a.r_a.far_a, f32[296,256]{1,0:T(8,128)S(1)} %collective-permute-done.8.far.yy_b.r_b.far_b), custom_call_target="tpu_custom_call" | custom-call | flops 1000000 | bytes 737280 | tf_op jit(solution)/shard_map/coarse_ready/pallas_call | solution.py:36
  55.5 1.4 %store.1 = (f32[32,32,256]{2,1,0:T(8,128)}, f32[32,32,256]{2,1,0:T(8,128)}, f32[8,128]{1,0:T(8,128)S(1)}) custom-call(f32[32,32,256]{2,1,0:T(8,128)S(1)} %sweeps.1.conc, f32[32,32,256]{2,1,0:T(8,128)S(1)} %get-tuple-element.75.flux), custom_call_target="tpu_custom_call" | custom-call | flops 1000000 | bytes 4198400 | tf_op jit(solution)/shard_map/store/pallas_call | solution.py:36
  56.9 3.7 %collective-permute-start.16 = (f32[12,8,256]{2,1,0:T(8,128)S(1)}, f32[12,8,256]{2,1,0:T(8,128)S(1)}, u32[]{:S(2)}, u32[]{:S(2)}) collective-permute-start(f32[12,8,256]{2,1,0:T(8,128)S(1)} %get-tuple-element.97), channel_id=1, source_target_pairs={{8,16},{16,8},{9,17},{17,9},{10,18},{18,10},{11,19},{19,11},{12,20... | collective-permute-start | bytes 294920 | tf_op jit(solution)/shard_map/ppermute | solution.py:803
  60.7 2.2 %collective-permute-done.16.x_a = f32[12,8,256]{2,1,0:T(8,128)S(1)} collective-permute-done((f32[12,8,256]{2,1,0:T(8,128)S(1)}, f32[12,8,256]{2,1,0:T(8,128)S(1)}, u32[]{:S(2)}, u32[]{:S(2)}) %collective-permute-start.16) | collective-permute-done | bytes 98336 | tf_op jit(solution)/shard_map/ppermute | solution.py:803
  62.9 1.7 %middle.1 = (f32[24,24,256]{2,1,0:T(8,128)S(1)}, f32[24,24,256]{2,1,0:T(8,128)S(1)}, f32[24,24,256]{2,1,0:T(8,128)S(1)}, f32[8,12,256]{2,1,0:T(8,128)S(1)}, f32[...) custom-call(f32[16,16,256]{2,1,0:T(8,128)S(1)} %get-tuple-element.92.field.source_own, ...), custom_call_target="tpu_custom_call" | custom-call | flops 1000000 | bytes 4042752 | tf_op jit(solution)/shard_map/middle/pallas_call | solution.py:36
  68.4 2.2 %collective-permute-start.19 = (f32[80,256]{1,0:T(8,128)S(1)}, f32[80,256]{1,0:T(8,128)S(1)}, u32[]{:S(2)}, u32[]{:S(2)}) collective-permute-start(f32[80,256]{1,0:T(8,128)S(1)} %get-tuple-element.104), channel_id=1, source_target_pairs={{0,1},{2,3},{4,5},{6,7},{1,0},{3,2},{5,4},{7,6},{8,9},{10,11},{12,... | collective-permute-start | bytes 245768 | tf_op jit(solution)/shard_map/ppermute | solution.py:803
  71.3 1.4 %collective-permute-done.19.r_b.other = f32[80,256]{1,0:T(8,128)S(1)} collective-permute-done((f32[80,256]{1,0:T(8,128)S(1)}, f32[80,256]{1,0:T(8,128)S(1)}, u32[]{:S(2)}, u32[]{:S(2)}) %collective-permute-start.19) | collective-permute-done | bytes 81952 | tf_op jit(solution)/shard_map/ppermute | solution.py:803
  73.3 5.2 %all-to-all-start = ((f32[4,8,128]{2,1,0:T(8,128)}), f32[4,8,128]{2,1,0:T(8,128)S(1)}, u32[]{:S(2)}, u32[]{:S(2)}) async-start(f32[4,8,128]{2,1,0:T(8,128)} %pair.1), calls=%async_computation | async-start | bytes 32768 | tf_op jit(solution)/shard_map/all_to_all | solution.py:939
  79.1 1.0 copy-done.7
  80.1 1.0 copy-done.9
  83.7 1.2 %coarse.1.error = f32[8,16,256]{2,1,0:T(8,128)S(1)} custom-call(f32[8,12,256]{2,1,0:T(8,128)S(1)} %copy-done.22, f32[8,12,256]{2,1,0:T(8,128)S(1)} %copy-done.24, f32[288,256]{1,0:T(8,128)S(1)} %copy-done.9, f32[296,256]{1,0:T(8,128)S(1)} %copy-done.7, f32[72,256]{1,0:T(8,128)S(1)} %copy-done.26, f32[80,256]{1,0:T(8,128)S(1)} %collective-permute-done.19.r_b.other), custom_call_target="tpu_custom_call" | custom-call | flops 1000000 | bytes 1081344 | tf_op jit(solution)/shard_map/coarse/pallas_call | solution.py:36
  85.1 4.8 %collective-permute-start.20 = (f32[2,16,256]{2,1,0:T(8,128)S(1)}, f32[2,16,256]{2,1,0:T(8,128)S(1)}, u32[]{:S(2)}, u32[]{:S(2)}) collective-permute-start(f32[2,16,256]{2,1,0:T(8,128)S(1)} %get-tuple-element.106), channel_id=1, source_target_pairs={{8,16},{16,8},{9,17},{17,9},{10,18},{18,10},{11,19},{19,11},{12,20... | collective-permute-start | bytes 98312 | tf_op jit(solution)/shard_map/ppermute | solution.py:803
  90.0 1.4 %copy-done.5 = f32[40,40,256]{2,1,0:T(8,128)S(1)} copy-done((f32[40,40,256]{2,1,0:T(8,128)S(1)}, f32[40,40,256]{2,1,0:T(8,128)}, u32[]{:S(2)}) %copy-start.5) | copy-done | bytes 1638424
  91.4 1.1 %copy-done.11 = f32[24,24,256]{2,1,0:T(8,128)S(1)} copy-done((f32[24,24,256]{2,1,0:T(8,128)S(1)}, f32[24,24,256]{2,1,0:T(8,128)}, u32[]{:S(2)}) %copy-start.11) | copy-done | bytes 589848
  92.5 1.1 %copy-done.13 = f32[24,24,256]{2,1,0:T(8,128)S(1)} copy-done((f32[24,24,256]{2,1,0:T(8,128)S(1)}, f32[24,24,256]{2,1,0:T(8,128)}, u32[]{:S(2)}) %copy-start.13) | copy-done | bytes 589848
  93.5 1.1 %copy-done.15 = f32[24,24,256]{2,1,0:T(8,128)S(1)} copy-done((f32[24,24,256]{2,1,0:T(8,128)S(1)}, f32[24,24,256]{2,1,0:T(8,128)}, u32[]{:S(2)}) %copy-start.15) | copy-done | bytes 589848
  94.6 2.5 %finish_inner.1 = (f32[32,32,256]{2,1,0:T(8,128)}, f32[24,24,256]{2,1,0:T(8,128)S(1)}, f32[24,24,256]{2,1,0:T(8,128)S(1)}, f32[40,40,256]{2,1,0:T(8,128)S(1)}, f32[40,40,256]{2,1,0:T(8,128)S(1)}) custom-call(f32[8,16,256]{2,1,0:T(8,128)S(1)} %get-tuple-element.113.error, f32[24,24,256]{2,1,0:T(8,128)S(1)} %copy-done.11, f32[24,24,256]{2,1,0:T(8,128)S(1)} %copy-done.13, ...), custom_call_target="tpu_custom_call" | custom-call | flops 1000000 | bytes 12320768 | tf_op jit(solution)/shard_map/finish_inner/pallas_call | solution.py:36
  97.1 1.7 %finish_edge.1 = f32[32,32,256]{2,1,0:T(8,128)} custom-call(f32[2,16,256]{2,1,0:T(8,128)S(1)} %collective-permute-done.20.x_a, f32[2,16,256]{2,1,0:T(8,128)S(1)} %collective-permute-done.21.x_b, f32[24,24,256]{2,1,0:T(8,128)S(1)} %copy-done.11, f32[24,24,256]{2,1,0:T(8,128)S(1)} %copy-done.13, ...), custom_call_target="tpu_custom_call", output_to_operand_aliasing={{}: (14, {})} | custom-call | flops 1000000 | bytes 14614528 | tf_op jit(solution)/shard_map/finish_edge/pallas_call | solution.py:36
  (92 shorter events, 17.3 us)
Async XLA Ops:
  0.6 7.5 %copy-start = (s32[32,32,256]{2,1,0:T(8,128)S(1)}, s32[32,32,256]{2,1,0:T(8,128)}, u32[]{:S(2)}) copy-start(s32[32,32,256]{2,1,0:T(8,128)} %label.11) | copy-start | bytes 3145732
  0.6 7.5 %copy-start.1 = (f32[32,32,256]{2,1,0:T(8,128)S(1)}, f32[32,32,256]{2,1,0:T(8,128)}, u32[]{:S(2)}) copy-start(f32[32,32,256]{2,1,0:T(8,128)} %conc.9) | copy-start | bytes 3145732
  2.8 15.0 %collective-permute-start = (f32[224,256]{1,0:T(8,128)}, f32[224,256]{1,0:T(8,128)S(1)}, u32[]{:S(2)}, u32[]{:S(2)}) collective-permute-start(f32[224,256]{1,0:T(8,128)} %get-tuple-element.64), channel_id=1, source_target_pairs={{1,2},{3,4},{5,6},{2,1},{4,3},{6,5},{9,10},{11,12},{13,14},{10,9},... | collective-permute-start | bytes 688136 | tf_op jit(solution)/shard_map/ppermute | solution.py:803
  3.5 14.7 %collective-permute-start.1 = (f32[224,256]{1,0:T(8,128)}, f32[224,256]{1,0:T(8,128)S(1)}, u32[]{:S(2)}, u32[]{:S(2)}) collective-permute-start(f32[224,256]{1,0:T(8,128)} %get-tuple-element.65), channel_id=1, source_target_pairs={{0,1},{2,3},{4,5},{6,7},{1,0},{3,2},{5,4},{7,6},{8,9},{10,11},{12,... | collective-permute-start | bytes 688136 | tf_op jit(solution)/shard_map/ppermute | solution.py:803
  10.7 11.3 %copy-start.3 = (f32[32,32,256]{2,1,0:T(8,128)S(1)}, f32[32,32,256]{2,1,0:T(8,128)}, u32[]{:S(2)}) copy-start(f32[32,32,256]{2,1,0:T(8,128)} %phi.7) | copy-start | bytes 3145732
  10.7 7.0 %collective-permute-start.4 = (f32[2,256]{1,0:T(2,128)S(1)}, f32[2,256]{1,0:T(2,128)S(1)}, u32[]{:S(2)}, u32[]{:S(2)}) collective-permute-start(f32[2,256]{1,0:T(2,128)S(1)} %get-tuple-element.70), channel_id=1, source_target_pairs={{0,4},{1,5},{2,6},{3,7},{4,0},{5,1},{6,2},{7,3},{8,12},{9,13},{10,... | collective-permute-start | bytes 6152 | tf_op jit(solution)/shard_map/ppermute | solution.py:807
  13.1 8.9 %collective-permute-start.6 = (f32[24,8,256]{2,1,0:T(8,128)S(1)}, f32[24,8,256]{2,1,0:T(8,128)S(1)}, u32[]{:S(2)}, u32[]{:S(2)}) collective-permute-start(f32[24,8,256]{2,1,0:T(8,128)S(1)} %get-tuple-element.72), channel_id=1, source_target_pairs={{8,16},{16,8},{9,17},{17,9},{10,18},{18,10},{11,19},{19,11},{12,20... | collective-permute-start | bytes 589832 | tf_op jit(solution)/shard_map/ppermute | solution.py:803
  17.6 4.3 %collective-permute-start.7 = (f32[24,8,256]{2,1,0:T(8,128)S(1)}, f32[24,8,256]{2,1,0:T(8,128)S(1)}, u32[]{:S(2)}, u32[]{:S(2)}) collective-permute-start(f32[24,8,256]{2,1,0:T(8,128)S(1)} %get-tuple-element.73), channel_id=1, source_target_pairs={{0,8},{16,24},{8,0},{24,16},{1,9},{17,25},{9,1},{25,17},{2,10},{18... | collective-permute-start | bytes 589832 | tf_op jit(solution)/shard_map/ppermute | solution.py:803
  17.7 4.2 %collective-permute-start.5 = (f32[4,256]{1,0:T(4,128)S(1)}, f32[4,256]{1,0:T(4,128)S(1)}, u32[]{:S(2)}, u32[]{:S(2)}) collective-permute-start(f32[4,256]{1,0:T(4,128)S(1)} %pad_maximum_fusion.1), channel_id=1, source_target_pairs={{0,2},{1,3},{2,0},{3,1},{4,6},{5,7},{6,4},{7,5},{8,10},{9,11},{10,... | collective-permute-start | bytes 12296 | tf_op jit(solution)/shard_map/ppermute | solution.py:807
  18.3 8.2 %collective-permute-start.2 = (f32[35,8,256]{2,1,0:T(8,128)S(1)}, f32[35,8,256]{2,1,0:T(8,128)S(1)}, u32[]{:S(2)}, u32[]{:S(2)}) collective-permute-start(f32[35,8,256]{2,1,0:T(8,128)S(1)} %get-tuple-element.67), channel_id=1, source_target_pairs={{8,16},{16,8},{9,17},{17,9},{10,18},{18,10},{11,19},{19,11},{12,20... | collective-permute-start | bytes 860168 | tf_op jit(solution)/shard_map/ppermute | solution.py:803
  21.8 4.7 %collective-permute-start.3 = (f32[35,8,256]{2,1,0:T(8,128)S(1)}, f32[35,8,256]{2,1,0:T(8,128)S(1)}, u32[]{:S(2)}, u32[]{:S(2)}) collective-permute-start(f32[35,8,256]{2,1,0:T(8,128)S(1)} %get-tuple-element.68), channel_id=1, source_target_pairs={{0,8},{16,24},{8,0},{24,16},{1,9},{17,25},{9,1},{25,17},{2,10},{18... | collective-permute-start | bytes 860168 | tf_op jit(solution)/shard_map/ppermute | solution.py:803
  22.1 16.0 %collective-permute-start.8 = (f32[296,256]{1,0:T(8,128)S(1)}, f32[296,256]{1,0:T(8,128)S(1)}, u32[]{:S(2)}, u32[]{:S(2)}) collective-permute-start(f32[296,256]{1,0:T(8,128)S(1)} %get-tuple-element.74), channel_id=1, source_target_pairs={{0,1},{2,3},{4,5},{6,7},{1,0},{3,2},{5,4},{7,6},{8,9},{10,11},{12,... | collective-permute-start | bytes 909320 | tf_op jit(solution)/shard_map/ppermute | solution.py:803
  24.3 20.1 %collective-permute-start.13 = (f32[288,256]{1,0:T(8,128)S(1)}, f32[288,256]{1,0:T(8,128)S(1)}, u32[]{:S(2)}, u32[]{:S(2)}) collective-permute-start(f32[288,256]{1,0:T(8,128)S(1)} %get-tuple-element.86), channel_id=1, source_target_pairs={{1,2},{3,4},{5,6},{2,1},{4,3},{6,5},{9,10},{11,12},{13,14},{10,9},... | collective-permute-start | bytes 884744 | tf_op jit(solution)/shard_map/ppermute | solution.py:803
  26.5 4.7 %copy-start.16 = (f32[32,32,256]{2,1,0:T(8,128)S(1)}, f32[32,32,256]{2,1,0:T(8,128)}, u32[]{:S(2)}) copy-start(f32[32,32,256]{2,1,0:T(8,128)} %solid.1) | copy-start | bytes 3145732
  32.0 7.0 %collective-permute-start.9 = (f32[96,256]{1,0:T(8,128)S(1)}, f32[96,256]{1,0:T(8,128)S(1)}, u32[]{:S(2)}, u32[]{:S(2)}) collective-permute-start(f32[96,256]{1,0:T(8,128)S(1)} %get-tuple-element.78), channel_id=1, source_target_pairs={{1,2},{3,4},{5,6},{2,1},{4,3},{6,5},{9,10},{11,12},{13,14},{10,9},... | collective-permute-start | bytes 294920 | tf_op jit(solution)/shard_map/ppermute | solution.py:803
  32.7 9.2 %collective-permute-start.10 = (f32[96,256]{1,0:T(8,128)S(1)}, f32[96,256]{1,0:T(8,128)S(1)}, u32[]{:S(2)}, u32[]{:S(2)}) collective-permute-start(f32[96,256]{1,0:T(8,128)S(1)} %get-tuple-element.79), channel_id=1, source_target_pairs={{0,1},{2,3},{4,5},{6,7},{1,0},{3,2},{5,4},{7,6},{8,9},{10,11},{12,... | collective-permute-start | bytes 294920 | tf_op jit(solution)/shard_map/ppermute | solution.py:803
  38.1 24.8 %copy-start.6 = (f32[296,256]{1,0:T(8,128)}, f32[296,256]{1,0:T(8,128)S(1)}, u32[]{:S(2)}) copy-start(f32[296,256]{1,0:T(8,128)S(1)} %collective-permute-done.8.far.yy_b.r_b.far_b) | copy-start | bytes 909316
  41.9 6.2 %collective-permute-start.11 = (f32[15,8,256]{2,1,0:T(8,128)S(1)}, f32[15,8,256]{2,1,0:T(8,128)S(1)}, u32[]{:S(2)}, u32[]{:S(2)}) collective-permute-start(f32[15,8,256]{2,1,0:T(8,128)S(1)} %get-tuple-element.82), channel_id=1, source_target_pairs={{8,16},{16,8},{9,17},{17,9},{10,18},{18,10},{11,19},{19,11},{12,20... | collective-permute-start | bytes 368648 | tf_op jit(solution)/shard_map/ppermute | solution.py:803
  44.3 3.8 %collective-permute-start.12 = (f32[15,8,256]{2,1,0:T(8,128)S(1)}, f32[15,8,256]{2,1,0:T(8,128)S(1)}, u32[]{:S(2)}, u32[]{:S(2)}) collective-permute-start(f32[15,8,256]{2,1,0:T(8,128)S(1)} %get-tuple-element.83), channel_id=1, source_target_pairs={{0,8},{16,24},{8,0},{24,16},{1,9},{17,25},{9,1},{25,17},{2,10},{18... | collective-permute-start | bytes 368648 | tf_op jit(solution)/shard_map/ppermute | solution.py:803
  44.4 18.6 %copy-start.8 = (f32[288,256]{1,0:T(8,128)}, f32[288,256]{1,0:T(8,128)S(1)}, u32[]{:S(2)}) copy-start(f32[288,256]{1,0:T(8,128)S(1)} %collective-permute-done.13.yy_a.r_a.far_a) | copy-start | bytes 884740
  48.8 15.8 %copy-start.17 = (f32[16,40,256]{2,1,0:T(8,128)}, f32[16,40,256]{2,1,0:T(8,128)S(1)}, u32[]{:S(2)}) copy-start(f32[16,40,256]{2,1,0:T(8,128)S(1)} %get-tuple-element.111.edge_two) | copy-start | bytes 1966084
  48.8 15.8 %copy-start.19 = (f32[16,40,256]{2,1,0:T(8,128)}, f32[16,40,256]{2,1,0:T(8,128)S(1)}, u32[]{:S(2)}) copy-start(f32[16,40,256]{2,1,0:T(8,128)S(1)} %get-tuple-element.112.edge_source) | copy-start | bytes 1966084
  48.8 8.0 %collective-permute-start.14 = (f32[64,256]{1,0:T(8,128)S(1)}, f32[64,256]{1,0:T(8,128)S(1)}, u32[]{:S(2)}, u32[]{:S(2)}) collective-permute-start(f32[64,256]{1,0:T(8,128)S(1)} %get-tuple-element.93), channel_id=1, source_target_pairs={{1,2},{3,4},{5,6},{2,1},{4,3},{6,5},{9,10},{11,12},{13,14},{10,9},... | collective-permute-start | bytes 196616 | tf_op jit(solution)/shard_map/ppermute | solution.py:803
  49.5 7.4 %collective-permute-start.15 = (f32[64,256]{1,0:T(8,128)S(1)}, f32[64,256]{1,0:T(8,128)S(1)}, u32[]{:S(2)}, u32[]{:S(2)}) collective-permute-start(f32[64,256]{1,0:T(8,128)S(1)} %get-tuple-element.94), channel_id=1, source_target_pairs={{0,1},{2,3},{4,5},{6,7},{1,0},{3,2},{5,4},{7,6},{8,9},{10,11},{12,... | collective-permute-start | bytes 196616 | tf_op jit(solution)/shard_map/ppermute | solution.py:803
  56.9 6.0 %collective-permute-start.16 = (f32[12,8,256]{2,1,0:T(8,128)S(1)}, f32[12,8,256]{2,1,0:T(8,128)S(1)}, u32[]{:S(2)}, u32[]{:S(2)}) collective-permute-start(f32[12,8,256]{2,1,0:T(8,128)S(1)} %get-tuple-element.97), channel_id=1, source_target_pairs={{8,16},{16,8},{9,17},{17,9},{10,18},{18,10},{11,19},{19,11},{12,20... | collective-permute-start | bytes 294920 | tf_op jit(solution)/shard_map/ppermute | solution.py:803
  60.6 2.3 %collective-permute-start.17 = (f32[12,8,256]{2,1,0:T(8,128)S(1)}, f32[12,8,256]{2,1,0:T(8,128)S(1)}, u32[]{:S(2)}, u32[]{:S(2)}) collective-permute-start(f32[12,8,256]{2,1,0:T(8,128)S(1)} %get-tuple-element.98), channel_id=1, source_target_pairs={{0,8},{16,24},{8,0},{24,16},{1,9},{17,25},{9,1},{25,17},{2,10},{18... | collective-permute-start | bytes 294920 | tf_op jit(solution)/shard_map/ppermute | solution.py:803
  68.4 4.3 %collective-permute-start.19 = (f32[80,256]{1,0:T(8,128)S(1)}, f32[80,256]{1,0:T(8,128)S(1)}, u32[]{:S(2)}, u32[]{:S(2)}) collective-permute-start(f32[80,256]{1,0:T(8,128)S(1)} %get-tuple-element.104), channel_id=1, source_target_pairs={{0,1},{2,3},{4,5},{6,7},{1,0},{3,2},{5,4},{7,6},{8,9},{10,11},{12,... | collective-permute-start | bytes 245768 | tf_op jit(solution)/shard_map/ppermute | solution.py:803
  70.6 7.9 %collective-permute-start.18 = (f32[72,256]{1,0:T(8,128)}, f32[72,256]{1,0:T(8,128)S(1)}, u32[]{:S(2)}, u32[]{:S(2)}) collective-permute-start(f32[72,256]{1,0:T(8,128)} %get-tuple-element.103), channel_id=1, source_target_pairs={{1,2},{3,4},{5,6},{2,1},{4,3},{6,5},{9,10},{11,12},{13,14},{10,9},... | collective-permute-start | bytes 221192 | tf_op jit(solution)/shard_map/ppermute | solution.py:803
  73.3 11.6 %all-to-all-start = ((f32[4,8,128]{2,1,0:T(8,128)}), f32[4,8,128]{2,1,0:T(8,128)S(1)}, u32[]{:S(2)}, u32[]{:S(2)}) async-start(f32[4,8,128]{2,1,0:T(8,128)} %pair.1), calls=%async_computation | async-start | bytes 32768 | tf_op jit(solution)/shard_map/all_to_all | solution.py:939
  85.1 12.0 %collective-permute-start.20 = (f32[2,16,256]{2,1,0:T(8,128)S(1)}, f32[2,16,256]{2,1,0:T(8,128)S(1)}, u32[]{:S(2)}, u32[]{:S(2)}) collective-permute-start(f32[2,16,256]{2,1,0:T(8,128)S(1)} %get-tuple-element.106), channel_id=1, source_target_pairs={{8,16},{16,8},{9,17},{17,9},{10,18},{18,10},{11,19},{19,11},{12,20... | collective-permute-start | bytes 98312 | tf_op jit(solution)/shard_map/ppermute | solution.py:803
  89.9 7.2 %collective-permute-start.21 = (f32[2,16,256]{2,1,0:T(8,128)S(1)}, f32[2,16,256]{2,1,0:T(8,128)S(1)}, u32[]{:S(2)}, u32[]{:S(2)}) collective-permute-start(f32[2,16,256]{2,1,0:T(8,128)S(1)} %get-tuple-element.107), channel_id=1, source_target_pairs={{0,8},{16,24},{8,0},{24,16},{1,9},{17,25},{9,1},{25,17},{2,10},{18... | collective-permute-start | bytes 98312 | tf_op jit(solution)/shard_map/ppermute | solution.py:803
  94.6 2.5 %copy-start.20 = (f32[16,40,256]{2,1,0:T(8,128)S(1)}, f32[16,40,256]{2,1,0:T(8,128)}, u32[]{:S(2)}) copy-start(f32[16,40,256]{2,1,0:T(8,128)} %copy-done.19) | copy-start | bytes 1966084
  (19 other events, 19.2 us)

commit v10 on v9

--- a/solution.py
+++ b/solution.py
@@ -619,14 +619,6 @@
     load[...] = total[:, :LANES] + total[:, LANES:]
 
 
-def pair_kernel(sums, other, out):
-    total = sums[...] + other[72:80, :]
-    resid, load = total[:, :LANES], total[:, LANES:]
-    tile = jnp.concatenate([resid[0:4] + resid[4:8], load[0:4] + load[4:8]], axis=0)
-    for i in range(out.shape[0]):
-        out[i] = tile
-
-
 def coarse_kernel(own, conduct, far_a, far_b, r_a, r_b, error, source, weight, one, two):
     base = far_a.shape[0] - 64
     for x in range(8):
@@ -657,17 +649,6 @@
         error[x, 8:16, :] = jnp.where(upper(), old[x, 8:16, :], old[x, 24:32, :])
 
 
-def shift_kernel(error, sums, out, pay_a, pay_b):
-    total = jnp.sum(sums[...], axis=0)
-    resid = jnp.sum(total[0:4])
-    load = jnp.sum(total[4:8])
-    shift_c = jnp.full((16, 256), resid, F32) / jnp.full((16, 256), load, F32)
-    for x in range(8):
-        out[x] = error[x] + shift_c
-    for k in range(2):
-        send_x(pay_a, pay_b, k, out[k], out[6 + k])
-
-
 def squeeze(tile):
     return jnp.where(iota((8, 256), 0) < 2, tile, pltpu.roll(tile, 4, 0))
 
@@ -686,10 +667,13 @@
     return source + (0.2 * v + weight * (w * inner + along_z(v)))
 
 
-def finish_inner_kernel(
-    error, mid_two, mid_source, mid_weight, fine_two, fine_source, fine_weight,
-    out, zero, one, fine_one, fine_last, two, dup, dup_2, result, sems,
-):
+def is_early():
+    return lax.axis_index("grp") < lax.axis_size("grp") // 2
+
+
+def finish_inner(error, fields, kept, out, scratch):
+    mid_two, mid_source, mid_weight, fine_two, fine_source, fine_weight = fields
+    zero, one, two, fine_one, fine_last, dup, dup_2, result, sems = scratch
     n = mid_two.shape[0]
     nf = fine_two.shape[0]
     for c in range(8):
@@ -718,6 +702,10 @@
 
     low, high = 2 * HALO + 1, nf - 2 * HALO - 1
     loop(low, high, sweep_one, 11)
+    for field, first, to in ((zero, 0, kept[0]), (one, 1, kept[1]), (fine_one, 4, kept[2]), (fine_last, 5, kept[3])):
+        for j in range(2):
+            to[j] = field[HALO + first + j]
+            to[2 + j] = field[field.shape[0] - HALO - 1 - first - j]
     copies = []
     low, high = low + 1, high - 1
     for j in range(2):
@@ -730,6 +718,34 @@
         copies[-1].start()
     for c in copies:
         c.wait()
+
+
+def finish_early_kernel(error, sums, *rest):
+    fields, (shifted, pay_a, pay_b, out), kept, scratch = rest[:6], rest[6:10], rest[10:14], rest[14:]
+    resid = jnp.sum(sums[:, :LANES])
+    load = jnp.sum(sums[:, LANES:])
+    shift_c = jnp.full((16, 256), resid, F32) / jnp.full((16, 256), load, F32)
+    for x in range(8):
+        shifted[x] = error[x] + shift_c
+    for k in range(2):
+        send_x(pay_a, pay_b, k, shifted[k], shifted[6 + k])
+
+    @pl.when(is_early())
+    def _():
+        finish_inner(shifted, fields, kept, out, scratch)
+
+
+def finish_late_kernel(error, *rest):
+    fields, kept_early, out, kept, scratch = rest[:6], rest[6:10], rest[11], rest[12:16], rest[16:]
+
+    @pl.when(is_early())
+    def _():
+        for a, b in zip(kept_early, kept):
+            b[...] = a[...]
+
+    @pl.when(jnp.logical_not(is_early()))
+    def _():
+        finish_inner(error, fields, kept, out, scratch)
 
 
 def finish_edge_kernel(
@@ -753,11 +769,11 @@
             for x in (first, first + 1):
                 zero_edge[x] = jnp.where(mid_weight[x] > 0.0, mid_two[x] + spread, 0.0)
 
-        def zero_of(k):
-            return zero[at(k)] if k >= 0 else zero_edge[at(k)]
-
-        def one_of(k):
-            return one[at(k)] if k >= 1 else one_edge[at(k)]
+        def zero_of(k, side=side):
+            return zero[2 * side + k] if k >= 0 else zero_edge[at(k)]
+
+        def one_of(k, side=side):
+            return one[2 * side + k - 1] if k >= 1 else one_edge[at(k)]
 
         for k in range(-2, 1):
             x = at(k)
@@ -771,11 +787,11 @@
                 before = fine_two[f] if inside else edge_two[base + f]
                 fine_edge[f] = before + spread
 
-        def fine_of(k):
-            return fine_one[fine(k)] if k >= 4 else fine_edge[fine(k)]
-
-        def last_of(k):
-            return fine_last[fine(k)] if k >= 5 else last_edge[fine(k)]
+        def fine_of(k, side=side):
+            return fine_one[2 * side + k - 4] if k >= 4 else fine_edge[fine(k)]
+
+        def last_of(k, side=side):
+            return fine_last[2 * side + k - 5] if k >= 5 else last_edge[fine(k)]
 
         for k in range(-1, 5):
             f = fine(k)
@@ -934,9 +950,11 @@
         name="middle",
     )
     c_a, c_b = swap(pay_a, pay_b, "dev")
-    groups = [list(range(0, peers, 2)), list(range(1, peers, 2))]
-    (sums,) = call(pair_kernel, [shaped(peers // 2, 8, LANES)], [sums, c_b], name="pair")
-    sums = lax.all_to_all(sums, "dev", 0, 0, axis_index_groups=groups, tiled=True)
+    sums = sums + c_b[72:80]
+    distance = 2
+    while distance < peers:
+        sums = sums + exchange(sums, distance)
+        distance *= 2
     (error,) = call(
         coarse_kernel,
         [shaped(8, 16, 256)],
@@ -944,18 +962,29 @@
         [vmem(*wide)] * 4,
         name="coarse",
     )
-    error, pay_a, pay_b = call(
-        shift_kernel, [shaped(8, 16, 256), shaped(2, 16, 256), shaped(2, 16, 256)], [error, sums], name="shift"
+    fields = [mid_two, mid_source, mid_weight, fine_two, fine_source, weight]
+    kept = [shaped(4, half + 2 * HALO, 256)] * 2 + [shaped(4, nx + 2 * HALO, 256)] * 2
+    scratch = [vmem(*ext_mid)] * 3 + [vmem(*ext)] * 2
+    scratch += [vmem(8, 2, 2, 16, LANES), vmem(half + 2 * HALO, 3, 2, 16, LANES), vmem(nx, nx, 256)]
+    scratch += [pltpu.SemaphoreType.DMA((2,))]
+    error, pay_a, pay_b, begun, *kept_early = call(
+        finish_early_kernel,
+        [shaped(8, 16, 256), shaped(2, 16, 256), shaped(2, 16, 256), shaped(nx, nx, 256)] + kept,
+        [error, sums] + fields,
+        scratch,
+        out_specs=[WHOLE] * 3 + [FAR] + [WHOLE] * 4,
+        name="finish_early",
     )
     e_a, e_b = swap(pay_a, pay_b, "grp")
     begun, zero, one, fine_one, fine_last = call(
-        finish_inner_kernel,
-        [shaped(nx, nx, 256), shaped(*ext_mid), shaped(*ext_mid), shaped(*ext), shaped(*ext)],
-        [error, mid_two, mid_source, mid_weight, fine_two, fine_source, weight],
-        [vmem(*ext_mid), vmem(8, 2, 2, 16, LANES), vmem(half + 2 * HALO, 3, 2, 16, LANES), vmem(nx, nx, 256)]
-        + [pltpu.SemaphoreType.DMA((2,))],
+        finish_late_kernel,
+        [shaped(nx, nx, 256)] + kept,
+        [error] + fields + kept_early + [begun],
+        scratch,
+        in_specs=[WHOLE] * 11 + [FAR],
         out_specs=[FAR] + [WHOLE] * 4,
-        name="finish_inner",
+        aliases={11: 0},
+        name="finish_late",
     )
     finish_args = [e_a, e_b, mid_two, mid_source, mid_weight, fine_two, edge_two, fine_source, edge_source, weight]
     finish_args += [zero, one, fine_one, fine_last, begun]

time: 100 us -> 84.8 us (0.85)
  local copies, waits for them, and re-layouts: 15.7 us -> 1.94 us
  waiting for transfers between devices: 8.98 us -> 13.9 us
  starting transfers between devices: 48.6 us -> 44 us
    unnamed x56 -> x12, local copies, waits for them, and re-layouts: 15.7 us -> 1.94 us
    all_to_all x1 -> x0, starting transfers between devices: 5.16 us -> none  [body(): lax.all_to_all(sums, 'dev', 0, 0, axis_index_groups=groups, tiled=True)]
    ppermute x2 -> x4, starting transfers between devices: 2.45 us -> 6.76 us  [exchange(): lax.ppermute(value, 'dev', [(i, i ^ distance) for i in range(lax.axis_siz...]
    ppermute x10, starting transfers between devices: 18.8 us -> 16.4 us  [swap(): lax.ppermute(pay_b, axis, both_ways(pairs_b))]
    ppermute x10, waiting for transfers between devices: 4.25 us -> 6.43 us  [swap(): lax.ppermute(pay_a, axis, both_ways(pairs_a))]
    ppermute x2 -> x4, waiting for transfers between devices: 0.01 us -> 1.67 us  [exchange(): lax.ppermute(value, 'dev', [(i, i ^ distance) for i in range(lax.axis_siz...]
    ppermute x10, starting transfers between devices: 22.3 us -> 20.9 us  [swap(): lax.ppermute(pay_a, axis, both_ways(pairs_a))]
    ppermute x10, waiting for transfers between devices: 4.73 us -> 5.78 us  [swap(): lax.ppermute(pay_b, axis, both_ways(pairs_b))]
  transfers between devices with their start and end apart: 23 -> 24, of which waited for: 6 -> 8; matrix products, arithmetic and copies ran while one was open for 0% -> 0% of each run, Pallas kernels for 18% -> 18%
where the time goes in v10:
time: 84.8 us; the launch traced here: 84.4 us
  starting transfers between devices  44 us (52%)
  Pallas kernels  23.5 us (28%)
  waiting for transfers between devices  13.9 us (16%)
  local copies, waits for them, and re-layouts  1.94 us (2%)
  between operations  1.02 us (1%)
    pallas_call x19, Pallas kernels, call(): pl.pallas_call(kernel, out_shape=tuple(outs), in_specs=in_specs or [WHOLE...  23.5 us
    ppermute x10, starting transfers between devices, swap(): lax.ppermute(pay_a, axis, both_ways(pairs_a))  20.9 us
    ppermute x10, starting transfers between devices, swap(): lax.ppermute(pay_b, axis, both_ways(pairs_b))  16.4 us
    ppermute x4, starting transfers between devices, exchange(): lax.ppermute(value, 'dev', [(i, i ^ distance) for i in range(lax.axis_siz...  6.76 us
    ppermute x10, waiting for transfers between devices, swap(): lax.ppermute(pay_a, axis, both_ways(pairs_a))  6.43 us
    ppermute x10, waiting for transfers between devices, swap(): lax.ppermute(pay_b, axis, both_ways(pairs_b))  5.78 us
    unnamed x12, local copies, waits for them, and re-layouts  1.94 us
  transfers between devices with their start and end apart: 24, of which 8 were waited for; matrix products, arithmetic and copies ran while one was open for 0% of the time, Pallas kernels for 18%

profile of v10, /device:TPU:1, one launch (start us, length us, event | category | flops | bytes accessed | tf_op | source)
XLA Modules:
  0.0 84.4 jit_solution(3810292135843598919)
XLA Ops:
  0.7 2.2 %first_pack.1 = (f32[224,256]{1,0:T(8,128)}, f32[224,256]{1,0:T(8,128)}, f32[8,256]{1,0:T(8,128)}) custom-call(f32[32,32,256]{2,1,0:T(8,128)} %conc.9, s32[32,32,256]{2,1,0:T(8,128)} %label.11, s32[1,256]{1,0:T(1,128)} %bitcast.1, s32[1,256]{1,0:T(1,128)} %block.1), custom_call_target="tpu_custom_call" | custom-call | flops 1000000 | bytes 2566144 | tf_op jit(solution)/shard_map/first_pack/pallas_call | solution.py:36
  3.5 4.6 %collective-permute-start.1 = (f32[224,256]{1,0:T(8,128)}, f32[224,256]{1,0:T(8,128)S(1)}, u32[]{:S(2)}, u32[]{:S(2)}) collective-permute-start(f32[224,256]{1,0:T(8,128)} %get-tuple-element.70), channel_id=1, source_target_pairs={{0,1},{2,3},{4,5},{6,7},{1,0},{3,2},{5,4},{7,6},{8,9},{10,11},{12,... | collective-permute-start | bytes 688136 | tf_op jit(solution)/shard_map/ppermute | solution.py:819
  8.1 1.2 %copy-done.2 = f32[32,32,256]{2,1,0:T(8,128)S(1)} copy-done((f32[32,32,256]{2,1,0:T(8,128)S(1)}, f32[32,32,256]{2,1,0:T(8,128)}, u32[]{:S(2)}) %copy-start.2) | copy-done | bytes 1048600
  10.7 2.4 %collective-permute-start.4 = (f32[2,256]{1,0:T(2,128)S(1)}, f32[2,256]{1,0:T(2,128)S(1)}, u32[]{:S(2)}, u32[]{:S(2)}) collective-permute-start(f32[2,256]{1,0:T(2,128)S(1)} %get-tuple-element.75), channel_id=1, source_target_pairs={{0,4},{1,5},{2,6},{3,7},{4,0},{5,1},{6,2},{7,3},{8,12},{9,13},{10,... | collective-permute-start | bytes 6152 | tf_op jit(solution)/shard_map/ppermute | solution.py:823
  13.1 4.5 %collective-permute-start.6 = (f32[24,8,256]{2,1,0:T(8,128)S(1)}, f32[24,8,256]{2,1,0:T(8,128)S(1)}, u32[]{:S(2)}, u32[]{:S(2)}) collective-permute-start(f32[24,8,256]{2,1,0:T(8,128)S(1)} %get-tuple-element.77), channel_id=1, source_target_pairs={{8,16},{16,8},{9,17},{17,9},{10,18},{18,10},{11,19},{19,11},{12,20... | collective-permute-start | bytes 589832 | tf_op jit(solution)/shard_map/ppermute | solution.py:819
  18.3 3.5 %collective-permute-start.2 = (f32[35,8,256]{2,1,0:T(8,128)S(1)}, f32[35,8,256]{2,1,0:T(8,128)S(1)}, u32[]{:S(2)}, u32[]{:S(2)}) collective-permute-start(f32[35,8,256]{2,1,0:T(8,128)S(1)} %get-tuple-element.72), channel_id=1, source_target_pairs={{8,16},{16,8},{9,17},{17,9},{10,18},{18,10},{11,19},{19,11},{12,20... | collective-permute-start | bytes 860168 | tf_op jit(solution)/shard_map/ppermute | solution.py:819
  22.1 2.2 %collective-permute-start.8 = (f32[296,256]{1,0:T(8,128)S(1)}, f32[296,256]{1,0:T(8,128)S(1)}, u32[]{:S(2)}, u32[]{:S(2)}) collective-permute-start(f32[296,256]{1,0:T(8,128)S(1)} %get-tuple-element.79), channel_id=1, source_target_pairs={{0,1},{2,3},{4,5},{6,7},{1,0},{3,2},{5,4},{7,6},{8,9},{10,11},{12,... | collective-permute-start | bytes 909320 | tf_op jit(solution)/shard_map/ppermute | solution.py:819
  25.0 1.6 %collective-permute-done.2.x_a = f32[35,8,256]{2,1,0:T(8,128)S(1)} collective-permute-done((f32[35,8,256]{2,1,0:T(8,128)S(1)}, f32[35,8,256]{2,1,0:T(8,128)S(1)}, u32[]{:S(2)}, u32[]{:S(2)}) %collective-permute-start.2) | collective-permute-done | bytes 286752 | tf_op jit(solution)/shard_map/ppermute | solution.py:819
  26.5 4.7 %sweeps.1.conc = f32[32,32,256]{2,1,0:T(8,128)S(1)} custom-call(f32[32,32,256]{2,1,0:T(8,128)S(1)} %copy-done.1, s32[32,32,256]{2,1,0:T(8,128)S(1)} %copy-done, f32[32,32,256]{2,1,0:T(8,128)S(1)} %get-tuple-element.67.gain_own, f32[32,32,256]{2,1,0:T(8,128)S(1)} %get-tuple-element.68.base_own, f32[224,256]{1,0:T(8,128)S(1)} %collective-permute-done.r_a.y_a, ...), custom_call_target="tpu_custom_call" | custom-call | flops 1000000 | bytes 6275072 | tf_op jit(solution)/shard_map/sweeps/pallas_call | solution.py:36
  31.3 0.8 flux.1
  32.1 2.2 %collective-permute-start.10 = (f32[96,256]{1,0:T(8,128)S(1)}, f32[96,256]{1,0:T(8,128)S(1)}, u32[]{:S(2)}, u32[]{:S(2)}) collective-permute-start(f32[96,256]{1,0:T(8,128)S(1)} %get-tuple-element.84), channel_id=1, source_target_pairs={{0,1},{2,3},{4,5},{6,7},{1,0},{3,2},{5,4},{7,6},{8,9},{10,11},{12,... | collective-permute-start | bytes 294920 | tf_op jit(solution)/shard_map/ppermute | solution.py:819
  35.8 0.9 %collective-permute-done.8.far.yy_b.r_b.far_b = f32[296,256]{1,0:T(8,128)S(1)} collective-permute-done((f32[296,256]{1,0:T(8,128)S(1)}, f32[296,256]{1,0:T(8,128)S(1)}, u32[]{:S(2)}, u32[]{:S(2)}) %collective-permute-start.8) | collective-permute-done | bytes 303136 | tf_op jit(solution)/shard_map/ppermute | solution.py:819
  36.7 0.8 %mask.1 = (f32[32,32,256]{2,1,0:T(8,128)S(1)}, f32[32,8,256]{2,1,0:T(8,128)S(1)}) custom-call(f32[32,32,256]{2,1,0:T(8,128)S(1)} %get-tuple-element.74.flux_all, f32[8,256]{1,0:T(8,128)S(1)} %pad_maximum_fusion.lists, f32[296,256]{1,0:T(8,128)S(1)} %collective-permute-done.8.far.yy_b.r_b.far_b), custom_call_target="tpu_custom_call" | custom-call | flops 1000000 | bytes 2670592 | tf_op jit(solution)/shard_map/mask/pallas_call | solution.py:36
  37.5 3.3 %collective-permute-done.10.r_b.y_b = f32[96,256]{1,0:T(8,128)S(1)} collective-permute-done((f32[96,256]{1,0:T(8,128)S(1)}, f32[96,256]{1,0:T(8,128)S(1)}, u32[]{:S(2)}, u32[]{:S(2)}) %collective-permute-start.10) | collective-permute-done | bytes 98336 | tf_op jit(solution)/shard_map/ppermute | solution.py:819
  40.9 3.4 %collective-permute-start.11 = (f32[15,8,256]{2,1,0:T(8,128)S(1)}, f32[15,8,256]{2,1,0:T(8,128)S(1)}, u32[]{:S(2)}, u32[]{:S(2)}) collective-permute-start(f32[15,8,256]{2,1,0:T(8,128)S(1)} %get-tuple-element.87), channel_id=1, source_target_pairs={{8,16},{16,8},{9,17},{17,9},{10,18},{18,10},{11,19},{19,11},{12,20... | collective-permute-start | bytes 368648 | tf_op jit(solution)/shard_map/ppermute | solution.py:819
  44.4 3.3 %potential_inner.1 = (f32[40,40,256]{2,1,0:T(8,128)S(1)}, f32[40,40,256]{2,1,0:T(8,128)S(1)}, f32[40,40,256]{2,1,0:T(8,128)S(1)}, f32[16,16,256]{2,1,0:T(8,128)S(1)}, f32[40,40,256]{2,1,0:T(8,128)S(1)}) custom-call(f32[32,32,256]{2,1,0:T(8,128)S(1)} %get-tuple-element.80.flux, f32[32,8,256]{2,1,0:T(8,128)S(1)} %get-tuple-element.85.mask, ...), custom_call_target="tpu_custom_call" | custom-call | flops 1000000 | bytes 13639680 | tf_op jit(solution)/shard_map/potential_inner/pallas_call | solution.py:36
  49.0 4.8 %collective-permute-start.15 = (f32[64,256]{1,0:T(8,128)S(1)}, f32[64,256]{1,0:T(8,128)S(1)}, u32[]{:S(2)}, u32[]{:S(2)}) collective-permute-start(f32[64,256]{1,0:T(8,128)S(1)} %get-tuple-element.99), channel_id=1, source_target_pairs={{0,1},{2,3},{4,5},{6,7},{1,0},{3,2},{5,4},{7,6},{8,9},{10,11},{12,... | collective-permute-start | bytes 196616 | tf_op jit(solution)/shard_map/ppermute | solution.py:819
  53.8 1.2 %coarse_ready.1 = (f32[8,8,256]{2,1,0:T(8,128)S(1)}, f32[8,128]{1,0:T(8,128)S(1)}, f32[8,128]{1,0:T(8,128)S(1)}) custom-call(f32[8,8,256]{2,1,0:T(8,128)S(1)} %get-tuple-element.71.token.coarse.own, f32[288,256]{1,0:T(8,128)S(1)} %collective-permute-done.13.yy_a.r_a.far_a, f32[296,256]{1,0:T(8,128)S(1)} %collective-permute-done.8.far.yy_b.r_b.far_b), custom_call_target="tpu_custom_call" | custom-call | flops 1000000 | bytes 737280 | tf_op jit(solution)/shard_map/coarse_ready/pallas_call | solution.py:36
  55.0 1.4 %store.1 = (f32[32,32,256]{2,1,0:T(8,128)}, f32[32,32,256]{2,1,0:T(8,128)}, f32[8,128]{1,0:T(8,128)S(1)}) custom-call(f32[32,32,256]{2,1,0:T(8,128)S(1)} %sweeps.1.conc, f32[32,32,256]{2,1,0:T(8,128)S(1)} %get-tuple-element.80.flux), custom_call_target="tpu_custom_call" | custom-call | flops 1000000 | bytes 4198400 | tf_op jit(solution)/shard_map/store/pallas_call | solution.py:36
  56.5 3.3 %collective-permute-start.16 = (f32[12,8,256]{2,1,0:T(8,128)S(1)}, f32[12,8,256]{2,1,0:T(8,128)S(1)}, u32[]{:S(2)}, u32[]{:S(2)}) collective-permute-start(f32[12,8,256]{2,1,0:T(8,128)S(1)} %get-tuple-element.102), channel_id=1, source_target_pairs={{8,16},{16,8},{9,17},{17,9},{10,18},{18,10},{11,19},{19,11},{12,20... | collective-permute-start | bytes 294920 | tf_op jit(solution)/shard_map/ppermute | solution.py:819
  59.9 2.5 %collective-permute-done.16.x_a = f32[12,8,256]{2,1,0:T(8,128)S(1)} collective-permute-done((f32[12,8,256]{2,1,0:T(8,128)S(1)}, f32[12,8,256]{2,1,0:T(8,128)S(1)}, u32[]{:S(2)}, u32[]{:S(2)}) %collective-permute-start.16) | collective-permute-done | bytes 98336 | tf_op jit(solution)/shard_map/ppermute | solution.py:819
  62.4 1.1 %middle.1 = (f32[24,24,256]{2,1,0:T(8,128)S(1)}, f32[24,24,256]{2,1,0:T(8,128)S(1)}, f32[24,24,256]{2,1,0:T(8,128)S(1)}, f32[8,12,256]{2,1,0:T(8,128)S(1)}, f32[...) custom-call(f32[16,16,256]{2,1,0:T(8,128)S(1)} %get-tuple-element.97.field.source_o, ...), custom_call_target="tpu_custom_call" | custom-call | flops 1000000 | bytes 4042752 | tf_op jit(solution)/shard_map/middle/pallas_call | solution.py:36
  63.5 2.2 %collective-permute-start.19 = (f32[80,256]{1,0:T(8,128)S(1)}, f32[80,256]{1,0:T(8,128)S(1)}, u32[]{:S(2)}, u32[]{:S(2)}) collective-permute-start(f32[80,256]{1,0:T(8,128)S(1)} %get-tuple-element.109), channel_id=1, source_target_pairs={{0,1},{2,3},{4,5},{6,7},{1,0},{3,2},{5,4},{7,6},{8,9},{10,11},{12,... | collective-permute-start | bytes 245768 | tf_op jit(solution)/shard_map/ppermute | solution.py:819
  66.4 1.2 %collective-permute-done.19.r_b = f32[80,256]{1,0:T(8,128)S(1)} collective-permute-done((f32[80,256]{1,0:T(8,128)S(1)}, f32[80,256]{1,0:T(8,128)S(1)}, u32[]{:S(2)}, u32[]{:S(2)}) %collective-permute-start.19) | collective-permute-done | bytes 81952 | tf_op jit(solution)/shard_map/ppermute | solution.py:819
  67.5 1.5 %collective-permute-start.20 = (f32[8,256]{1,0:T(8,128)S(1)}, f32[8,256]{1,0:T(8,128)S(1)}, u32[]{:S(2)}, u32[]{:S(2)}) collective-permute-start(f32[8,256]{1,0:T(8,128)S(1)} %slice_add_fusion), channel_id=1, source_target_pairs={{0,2},{1,3},{2,0},{3,1},{4,6},{5,7},{6,4},{7,5},{8,10},{9,11},{10,... | collective-permute-start | bytes 24584 | tf_op jit(solution)/shard_map/ppermute | solution.py:823
  69.1 1.6 %collective-permute-done.20 = f32[8,256]{1,0:T(8,128)S(1)} collective-permute-done((f32[8,256]{1,0:T(8,128)S(1)}, f32[8,256]{1,0:T(8,128)S(1)}, u32[]{:S(2)}, u32[]{:S(2)}) %collective-permute-start.20) | collective-permute-done | bytes 8224 | tf_op jit(solution)/shard_map/ppermute | solution.py:823
  70.7 2.8 %collective-permute-start.21 = (f32[8,256]{1,0:T(8,128)S(1)}, f32[8,256]{1,0:T(8,128)S(1)}, u32[]{:S(2)}, u32[]{:S(2)}) collective-permute-start(f32[8,256]{1,0:T(8,128)S(1)} %add.10), channel_id=1, source_target_pairs={{0,4},{1,5},{2,6},{3,7},{4,0},{5,1},{6,2},{7,3},{8,12},{9,13},{10,... | collective-permute-start | bytes 24584 | tf_op jit(solution)/shard_map/ppermute | solution.py:823
  73.5 1.2 %coarse.1.error = f32[8,16,256]{2,1,0:T(8,128)S(1)} custom-call(f32[8,12,256]{2,1,0:T(8,128)S(1)} %get-tuple-element.106.own, f32[8,12,256]{2,1,0:T(8,128)S(1)} %get-tuple-element.107.conduct, f32[288,256]{1,0:T(8,128)S(1)} %collective-permute-done.13.yy_a.r_a.far_a, f32[296,256]{1,0:T(8,128)S(1)} %collective-permute-done.8.far.yy_b.r_b.far_b, ...), custom_call_target="tpu_custom_call" | custom-call | flops 1000000 | bytes 1081344 | tf_op jit(solution)/shard_map/coarse/pallas_call | solution.py:36
  74.7 2.7 %finish_early.1 = (f32[8,16,256]{2,1,0:T(8,128)S(1)}, f32[2,16,256]{2,1,0:T(8,128)S(1)}, f32[2,16,256]{2,1,0:T(8,128)S(1)}, f32[32,32,256]{2,1,0:T(8,128)}, f32[...) custom-call(f32[8,16,256]{2,1,0:T(8,128)S(1)} %coarse.1.error, ...), custom_call_target="tpu_custom_call" | custom-call | flops 1000000 | bytes 8593408 | tf_op jit(solution)/shard_map/finish_early/pallas_call | solution.py:36
  77.4 2.8 %collective-permute-start.22 = (f32[2,16,256]{2,1,0:T(8,128)S(1)}, f32[2,16,256]{2,1,0:T(8,128)S(1)}, u32[]{:S(2)}, u32[]{:S(2)}) collective-permute-start(f32[2,16,256]{2,1,0:T(8,128)S(1)} %get-tuple-element.114), channel_id=1, source_target_pairs={{8,16},{16,8},{9,17},{17,9},{10,18},{18,10},{11,19},{19,11},{12,20... | collective-permute-start | bytes 98312 | tf_op jit(solution)/shard_map/ppermute | solution.py:819
  80.4 2.3 %collective-permute-done.22.x_a = f32[2,16,256]{2,1,0:T(8,128)S(1)} collective-permute-done((f32[2,16,256]{2,1,0:T(8,128)S(1)}, f32[2,16,256]{2,1,0:T(8,128)S(1)}, u32[]{:S(2)}, u32[]{:S(2)}) %collective-permute-start.22) | collective-permute-done | bytes 32800 | tf_op jit(solution)/shard_map/ppermute | solution.py:819
  82.7 1.7 %finish_edge.1 = f32[32,32,256]{2,1,0:T(8,128)} custom-call(f32[2,16,256]{2,1,0:T(8,128)S(1)} %collective-permute-done.22.x_a, f32[2,16,256]{2,1,0:T(8,128)S(1)} %collective-permute-done.23.x_b, f32[24,24,256]{2,1,0:T(8,128)S(1)} %get-tuple-element.111.rest_0_.mid_two, ...), custom_call_target="tpu_custom_call", output_to_operand_aliasing={{}: (14, {})} | custom-call | flops 1000000 | bytes 10682368 | tf_op jit(solution)/shard_map/finish_edge/pallas_call | solution.py:36
  (52 shorter events, 7.4 us)
Async XLA Ops:
  0.6 7.5 %copy-start.1 = (f32[32,32,256]{2,1,0:T(8,128)S(1)}, f32[32,32,256]{2,1,0:T(8,128)}, u32[]{:S(2)}) copy-start(f32[32,32,256]{2,1,0:T(8,128)} %conc.9) | copy-start | bytes 3145732
  0.6 7.5 %copy-start = (s32[32,32,256]{2,1,0:T(8,128)S(1)}, s32[32,32,256]{2,1,0:T(8,128)}, u32[]{:S(2)}) copy-start(s32[32,32,256]{2,1,0:T(8,128)} %label.11) | copy-start | bytes 3145732
  2.8 15.0 %collective-permute-start = (f32[224,256]{1,0:T(8,128)}, f32[224,256]{1,0:T(8,128)S(1)}, u32[]{:S(2)}, u32[]{:S(2)}) collective-permute-start(f32[224,256]{1,0:T(8,128)} %get-tuple-element.69), channel_id=1, source_target_pairs={{1,2},{3,4},{5,6},{2,1},{4,3},{6,5},{9,10},{11,12},{13,14},{10,9},... | collective-permute-start | bytes 688136 | tf_op jit(solution)/shard_map/ppermute | solution.py:819
  3.5 14.7 %collective-permute-start.1 = (f32[224,256]{1,0:T(8,128)}, f32[224,256]{1,0:T(8,128)S(1)}, u32[]{:S(2)}, u32[]{:S(2)}) collective-permute-start(f32[224,256]{1,0:T(8,128)} %get-tuple-element.70), channel_id=1, source_target_pairs={{0,1},{2,3},{4,5},{6,7},{1,0},{3,2},{5,4},{7,6},{8,9},{10,11},{12,... | collective-permute-start | bytes 688136 | tf_op jit(solution)/shard_map/ppermute | solution.py:819
  8.1 1.2 %copy-start.2 = (f32[32,32,256]{2,1,0:T(8,128)S(1)}, f32[32,32,256]{2,1,0:T(8,128)}, u32[]{:S(2)}) copy-start(f32[32,32,256]{2,1,0:T(8,128)} %phi.7) | copy-start | bytes 3145732
  9.3 0.7 copy-start.5
  10.7 11.3 %copy-start.3 = (f32[32,32,256]{2,1,0:T(8,128)S(1)}, f32[32,32,256]{2,1,0:T(8,128)}, u32[]{:S(2)}) copy-start(f32[32,32,256]{2,1,0:T(8,128)} %phi.7) | copy-start | bytes 3145732
  10.7 7.0 %collective-permute-start.4 = (f32[2,256]{1,0:T(2,128)S(1)}, f32[2,256]{1,0:T(2,128)S(1)}, u32[]{:S(2)}, u32[]{:S(2)}) collective-permute-start(f32[2,256]{1,0:T(2,128)S(1)} %get-tuple-element.75), channel_id=1, source_target_pairs={{0,4},{1,5},{2,6},{3,7},{4,0},{5,1},{6,2},{7,3},{8,12},{9,13},{10,... | collective-permute-start | bytes 6152 | tf_op jit(solution)/shard_map/ppermute | solution.py:823
  13.1 8.9 %collective-permute-start.6 = (f32[24,8,256]{2,1,0:T(8,128)S(1)}, f32[24,8,256]{2,1,0:T(8,128)S(1)}, u32[]{:S(2)}, u32[]{:S(2)}) collective-permute-start(f32[24,8,256]{2,1,0:T(8,128)S(1)} %get-tuple-element.77), channel_id=1, source_target_pairs={{8,16},{16,8},{9,17},{17,9},{10,18},{18,10},{11,19},{19,11},{12,20... | collective-permute-start | bytes 589832 | tf_op jit(solution)/shard_map/ppermute | solution.py:819
  17.6 4.3 %collective-permute-start.7 = (f32[24,8,256]{2,1,0:T(8,128)S(1)}, f32[24,8,256]{2,1,0:T(8,128)S(1)}, u32[]{:S(2)}, u32[]{:S(2)}) collective-permute-start(f32[24,8,256]{2,1,0:T(8,128)S(1)} %get-tuple-element.78), channel_id=1, source_target_pairs={{0,8},{16,24},{8,0},{24,16},{1,9},{17,25},{9,1},{25,17},{2,10},{18... | collective-permute-start | bytes 589832 | tf_op jit(solution)/shard_map/ppermute | solution.py:819
  17.7 4.2 %collective-permute-start.5 = (f32[4,256]{1,0:T(4,128)S(1)}, f32[4,256]{1,0:T(4,128)S(1)}, u32[]{:S(2)}, u32[]{:S(2)}) collective-permute-start(f32[4,256]{1,0:T(4,128)S(1)} %pad_maximum_fusion.1), channel_id=1, source_target_pairs={{0,2},{1,3},{2,0},{3,1},{4,6},{5,7},{6,4},{7,5},{8,10},{9,11},{10,... | collective-permute-start | bytes 12296 | tf_op jit(solution)/shard_map/ppermute | solution.py:823
  18.3 8.2 %collective-permute-start.2 = (f32[35,8,256]{2,1,0:T(8,128)S(1)}, f32[35,8,256]{2,1,0:T(8,128)S(1)}, u32[]{:S(2)}, u32[]{:S(2)}) collective-permute-start(f32[35,8,256]{2,1,0:T(8,128)S(1)} %get-tuple-element.72), channel_id=1, source_target_pairs={{8,16},{16,8},{9,17},{17,9},{10,18},{18,10},{11,19},{19,11},{12,20... | collective-permute-start | bytes 860168 | tf_op jit(solution)/shard_map/ppermute | solution.py:819
  21.8 4.7 %collective-permute-start.3 = (f32[35,8,256]{2,1,0:T(8,128)S(1)}, f32[35,8,256]{2,1,0:T(8,128)S(1)}, u32[]{:S(2)}, u32[]{:S(2)}) collective-permute-start(f32[35,8,256]{2,1,0:T(8,128)S(1)} %get-tuple-element.73), channel_id=1, source_target_pairs={{0,8},{16,24},{8,0},{24,16},{1,9},{17,25},{9,1},{25,17},{2,10},{18... | collective-permute-start | bytes 860168 | tf_op jit(solution)/shard_map/ppermute | solution.py:819
  22.1 14.5 %collective-permute-start.8 = (f32[296,256]{1,0:T(8,128)S(1)}, f32[296,256]{1,0:T(8,128)S(1)}, u32[]{:S(2)}, u32[]{:S(2)}) collective-permute-start(f32[296,256]{1,0:T(8,128)S(1)} %get-tuple-element.79), channel_id=1, source_target_pairs={{0,1},{2,3},{4,5},{6,7},{1,0},{3,2},{5,4},{7,6},{8,9},{10,11},{12,... | collective-permute-start | bytes 909320 | tf_op jit(solution)/shard_map/ppermute | solution.py:819
  24.3 20.1 %collective-permute-start.13 = (f32[288,256]{1,0:T(8,128)S(1)}, f32[288,256]{1,0:T(8,128)S(1)}, u32[]{:S(2)}, u32[]{:S(2)}) collective-permute-start(f32[288,256]{1,0:T(8,128)S(1)} %get-tuple-element.91), channel_id=1, source_target_pairs={{1,2},{3,4},{5,6},{2,1},{4,3},{6,5},{9,10},{11,12},{13,14},{10,9},... | collective-permute-start | bytes 884744 | tf_op jit(solution)/shard_map/ppermute | solution.py:819
  26.5 4.8 %copy-start.4 = (f32[32,32,256]{2,1,0:T(8,128)S(1)}, f32[32,32,256]{2,1,0:T(8,128)}, u32[]{:S(2)}) copy-start(f32[32,32,256]{2,1,0:T(8,128)} %solid.1) | copy-start | bytes 3145732
  32.1 8.7 %collective-permute-start.10 = (f32[96,256]{1,0:T(8,128)S(1)}, f32[96,256]{1,0:T(8,128)S(1)}, u32[]{:S(2)}, u32[]{:S(2)}) collective-permute-start(f32[96,256]{1,0:T(8,128)S(1)} %get-tuple-element.84), channel_id=1, source_target_pairs={{0,1},{2,3},{4,5},{6,7},{1,0},{3,2},{5,4},{7,6},{8,9},{10,11},{12,... | collective-permute-start | bytes 294920 | tf_op jit(solution)/shard_map/ppermute | solution.py:819
  34.3 6.5 %collective-permute-start.9 = (f32[96,256]{1,0:T(8,128)S(1)}, f32[96,256]{1,0:T(8,128)S(1)}, u32[]{:S(2)}, u32[]{:S(2)}) collective-permute-start(f32[96,256]{1,0:T(8,128)S(1)} %get-tuple-element.83), channel_id=1, source_target_pairs={{1,2},{3,4},{5,6},{2,1},{4,3},{6,5},{9,10},{11,12},{13,14},{10,9},... | collective-permute-start | bytes 294920 | tf_op jit(solution)/shard_map/ppermute | solution.py:819
  40.9 6.9 %collective-permute-start.11 = (f32[15,8,256]{2,1,0:T(8,128)S(1)}, f32[15,8,256]{2,1,0:T(8,128)S(1)}, u32[]{:S(2)}, u32[]{:S(2)}) collective-permute-start(f32[15,8,256]{2,1,0:T(8,128)S(1)} %get-tuple-element.87), channel_id=1, source_target_pairs={{8,16},{16,8},{9,17},{17,9},{10,18},{18,10},{11,19},{19,11},{12,20... | collective-permute-start | bytes 368648 | tf_op jit(solution)/shard_map/ppermute | solution.py:819
  44.3 3.4 %collective-permute-start.12 = (f32[15,8,256]{2,1,0:T(8,128)S(1)}, f32[15,8,256]{2,1,0:T(8,128)S(1)}, u32[]{:S(2)}, u32[]{:S(2)}) collective-permute-start(f32[15,8,256]{2,1,0:T(8,128)S(1)} %get-tuple-element.88), channel_id=1, source_target_pairs={{0,8},{16,24},{8,0},{24,16},{1,9},{17,25},{9,1},{25,17},{2,10},{18... | collective-permute-start | bytes 368648 | tf_op jit(solution)/shard_map/ppermute | solution.py:819
  48.4 8.0 %collective-permute-start.14 = (f32[64,256]{1,0:T(8,128)S(1)}, f32[64,256]{1,0:T(8,128)S(1)}, u32[]{:S(2)}, u32[]{:S(2)}) collective-permute-start(f32[64,256]{1,0:T(8,128)S(1)} %get-tuple-element.98), channel_id=1, source_target_pairs={{1,2},{3,4},{5,6},{2,1},{4,3},{6,5},{9,10},{11,12},{13,14},{10,9},... | collective-permute-start | bytes 196616 | tf_op jit(solution)/shard_map/ppermute | solution.py:819
  49.0 7.4 %collective-permute-start.15 = (f32[64,256]{1,0:T(8,128)S(1)}, f32[64,256]{1,0:T(8,128)S(1)}, u32[]{:S(2)}, u32[]{:S(2)}) collective-permute-start(f32[64,256]{1,0:T(8,128)S(1)} %get-tuple-element.99), channel_id=1, source_target_pairs={{0,1},{2,3},{4,5},{6,7},{1,0},{3,2},{5,4},{7,6},{8,9},{10,11},{12,... | collective-permute-start | bytes 196616 | tf_op jit(solution)/shard_map/ppermute | solution.py:819
  56.5 5.9 %collective-permute-start.16 = (f32[12,8,256]{2,1,0:T(8,128)S(1)}, f32[12,8,256]{2,1,0:T(8,128)S(1)}, u32[]{:S(2)}, u32[]{:S(2)}) collective-permute-start(f32[12,8,256]{2,1,0:T(8,128)S(1)} %get-tuple-element.102), channel_id=1, source_target_pairs={{8,16},{16,8},{9,17},{17,9},{10,18},{18,10},{11,19},{19,11},{12,20... | collective-permute-start | bytes 294920 | tf_op jit(solution)/shard_map/ppermute | solution.py:819
  59.8 2.6 %collective-permute-start.17 = (f32[12,8,256]{2,1,0:T(8,128)S(1)}, f32[12,8,256]{2,1,0:T(8,128)S(1)}, u32[]{:S(2)}, u32[]{:S(2)}) collective-permute-start(f32[12,8,256]{2,1,0:T(8,128)S(1)} %get-tuple-element.103), channel_id=1, source_target_pairs={{0,8},{16,24},{8,0},{24,16},{1,9},{17,25},{9,1},{25,17},{2,10},{18... | collective-permute-start | bytes 294920 | tf_op jit(solution)/shard_map/ppermute | solution.py:819
  63.5 4.1 %collective-permute-start.19 = (f32[80,256]{1,0:T(8,128)S(1)}, f32[80,256]{1,0:T(8,128)S(1)}, u32[]{:S(2)}, u32[]{:S(2)}) collective-permute-start(f32[80,256]{1,0:T(8,128)S(1)} %get-tuple-element.109), channel_id=1, source_target_pairs={{0,1},{2,3},{4,5},{6,7},{1,0},{3,2},{5,4},{7,6},{8,9},{10,11},{12,... | collective-permute-start | bytes 245768 | tf_op jit(solution)/shard_map/ppermute | solution.py:819
  65.7 7.8 %collective-permute-start.18 = (f32[72,256]{1,0:T(8,128)S(1)}, f32[72,256]{1,0:T(8,128)S(1)}, u32[]{:S(2)}, u32[]{:S(2)}) collective-permute-start(f32[72,256]{1,0:T(8,128)S(1)} %get-tuple-element.108), channel_id=1, source_target_pairs={{1,2},{3,4},{5,6},{2,1},{4,3},{6,5},{9,10},{11,12},{13,14},{10,9},... | collective-permute-start | bytes 221192 | tf_op jit(solution)/shard_map/ppermute | solution.py:819
  67.5 3.2 %collective-permute-start.20 = (f32[8,256]{1,0:T(8,128)S(1)}, f32[8,256]{1,0:T(8,128)S(1)}, u32[]{:S(2)}, u32[]{:S(2)}) collective-permute-start(f32[8,256]{1,0:T(8,128)S(1)} %slice_add_fusion), channel_id=1, source_target_pairs={{0,2},{1,3},{2,0},{3,1},{4,6},{5,7},{6,4},{7,5},{8,10},{9,11},{10,... | collective-permute-start | bytes 24584 | tf_op jit(solution)/shard_map/ppermute | solution.py:823
  70.7 4.0 %collective-permute-start.21 = (f32[8,256]{1,0:T(8,128)S(1)}, f32[8,256]{1,0:T(8,128)S(1)}, u32[]{:S(2)}, u32[]{:S(2)}) collective-permute-start(f32[8,256]{1,0:T(8,128)S(1)} %add.10), channel_id=1, source_target_pairs={{0,4},{1,5},{2,6},{3,7},{4,0},{5,1},{6,2},{7,3},{8,12},{9,13},{10,... | collective-permute-start | bytes 24584 | tf_op jit(solution)/shard_map/ppermute | solution.py:823
  77.4 5.2 %collective-permute-start.22 = (f32[2,16,256]{2,1,0:T(8,128)S(1)}, f32[2,16,256]{2,1,0:T(8,128)S(1)}, u32[]{:S(2)}, u32[]{:S(2)}) collective-permute-start(f32[2,16,256]{2,1,0:T(8,128)S(1)} %get-tuple-element.114), channel_id=1, source_target_pairs={{8,16},{16,8},{9,17},{17,9},{10,18},{18,10},{11,19},{19,11},{12,20... | collective-permute-start | bytes 98312 | tf_op jit(solution)/shard_map/ppermute | solution.py:819
  80.2 2.5 %collective-permute-start.23 = (f32[2,16,256]{2,1,0:T(8,128)S(1)}, f32[2,16,256]{2,1,0:T(8,128)S(1)}, u32[]{:S(2)}, u32[]{:S(2)}) collective-permute-start(f32[2,16,256]{2,1,0:T(8,128)S(1)} %get-tuple-element.115), channel_id=1, source_target_pairs={{0,8},{16,24},{8,0},{24,16},{1,9},{17,25},{9,1},{25,17},{2,10},{18... | collective-permute-start | bytes 98312 | tf_op jit(solution)/shard_map/ppermute | solution.py:819

commit v11 on v10

--- a/solution.py
+++ b/solution.py
@@ -190,9 +190,10 @@
         for t in range(4):
             rows = slice(8 * t, 8 * t + 8)
             send_x(pay_a, pay_b, 4 * k + t, phi[k, rows, :], phi[nx - HALO + k, rows, :])
+    for k in range(MID_HALO):
         for t in range(2):
             rows = slice(8 * t, 8 * t + 8)
-            send_x(pay_a, pay_b, 16 + 2 * k + t, mid[k, rows, :], mid[half - HALO + k, rows, :])
+            send_x(pay_a, pay_b, 16 + 2 * k + t, mid[k, rows, :], mid[half - MID_HALO + k, rows, :])
 
 
 def first_pack_x_kernel(conc, label, r_a, r_b, token, pay_a, pay_b):
@@ -210,14 +211,18 @@
             send_x(pay_a, pay_b, 20 + 5 * k + t, plane(label, k, t, 4, 3), plane(label, nx - 3 + k, t, 4, 3))
 
 
-def corner_rows(n, reach):
-    counts = [min(HALO, k + reach) for k in range(HALO)]
-    counts = counts + [HALO] * n + counts[::-1]
+MID_HALO = 3
+
+
+def corner_rows(n, width, reach):
+    counts = [min(width, k + reach) for k in range(width)]
+    counts = counts + [width] * n + counts[::-1]
     return counts, [sum(counts[:i]) for i in range(len(counts))]
 
 
 def second_rows(nx):
-    phi, mid = (sum(corner_rows(n, reach)[0]) for n, reach in ((nx, 0), (nx // 2, 1)))
+    phi = sum(corner_rows(nx, HALO, 0)[0])
+    mid = sum(corner_rows(nx // 2, MID_HALO, 1)[0])
     return phi, phi + mid, phi + mid + 64
 
 
@@ -225,20 +230,21 @@
     nx = phi.shape[0]
     starts = second_rows(nx)
 
-    def put(own, n, reach, index, base):
-        counts, at = corner_rows(n, reach)
+    def put(own, width, reach, index, base):
+        n = own.shape[0]
+        counts, at = corner_rows(n, width, reach)
         tiles = own.shape[1] // 8
         for x in range(n):
-            send_y(pay_a, pay_b, base + at[HALO + x], own[x, 0:4, :], own[x, 8 * tiles - 4 : 8 * tiles, :])
-        for k in range(HALO):
+            send_y(pay_a, pay_b, base + at[width + x], own[x, 0:width, :], own[x, 8 * tiles - width : 8 * tiles, :])
+        for k in range(width):
             first_after, first_before = x_sides(x_a, x_b, index + tiles * k)
             last_after, last_before = x_sides(x_a, x_b, index + tiles * k + tiles - 1)
-            for x, first, last in ((k, first_before, last_before), (HALO + n + k, first_after, last_after)):
+            for x, first, last in ((k, first_before, last_before), (width + n + k, first_after, last_after)):
                 if counts[x]:
                     send_y(pay_a, pay_b, base + at[x], first[0 : counts[x]], last[8 - counts[x] : 8])
 
-    put(phi, nx, 0, 0, 0)
-    put(mid, nx // 2, 1, 16, starts[0])
+    put(phi, HALO, 0, 0, 0)
+    put(mid, MID_HALO, 1, 16, starts[0])
     base = starts[1]
     for x in range(8):
         pay_a[base + 8 * x : base + 8 * x + 8, :] = coarse[x]
@@ -247,9 +253,10 @@
     pay_b[base : base + lists.shape[0], :] = lists[...]
 
 
-def second_halo(r_a, r_b, n, reach, x, base):
-    counts, at = corner_rows(n, reach)
-    if not counts[x]:
+def second_halo(r_a, r_b, n, width, reach, x, base):
+    counts, at = corner_rows(n, width, reach)
+    x = x - HALO + width
+    if x < 0 or x >= len(counts) or not counts[x]:
         return jnp.zeros((8, 256), F32)
     return halo_tile(*y_sides(r_a, r_b, base + at[x], counts[x]))
 
@@ -409,7 +416,7 @@
 
     loop(0, nx, own)
     for x in range(nx + 2 * HALO):
-        field[x, 32:40, :] = second_halo(yy_a, yy_b, nx, 0, x, 0)
+        field[x, 32:40, :] = second_halo(yy_a, yy_b, nx, HALO, 0, x, 0)
     for t in range(4):
         for k in range(HALO):
             after, before = x_sides(xx_a, xx_b, 4 * k + t)
@@ -473,8 +480,12 @@
     loop(1, nx // 2 - 1, coarsen, 4)
 
 
+def mid_factor(conduct):
+    return OMEGA / (MASS + 3.0 * conduct)
+
+
 def potential_edge_kernel(
-    x_a, x_b, weight, scale, field, inner_two, inner_source, inner_first, inner_mid,
+    x_a, x_b, weight, scale, field, inner_two, inner_source, inner_first, inner_mid, conduct_mid,
     edge_two, edge_source, source_mid, pay_a, pay_b, first, pairs,
 ):
     half = source_mid.shape[0]
@@ -505,9 +516,10 @@
             v = two_of(x)
             near = weight[x] * ((two_of(x - 1) + two_of(x + 1)) + (along_y(v) + along_z(v)))
             total = total + ((source_of(x) - OMEGA * v) + near)[0:32, :] / scale[x, 0:32, :]
-        source_mid[0 if side == 0 else half - 1] = 0.25 * pair_rows(total, pairs.at[side])
+        at = 0 if side == 0 else half - 1
+        source_mid[at] = mid_factor(conduct_mid[at]) * (0.25 * pair_rows(total, pairs.at[side]))
     for x in range(1, half - 1):
-        source_mid[x] = inner_mid[x]
+        source_mid[x] = mid_factor(conduct_mid[x]) * inner_mid[x]
     for x in range(half):
         send_y(pay_a, pay_b, 4 * x, source_mid[x, 0:4, :], source_mid[x, 12:16, :])
 
@@ -533,14 +545,14 @@
     base = second_rows(2 * n)[0]
 
     def put(x, rows, b, k):
-        factor = OMEGA / (MASS + 3.0 * k)
+        factor = mid_factor(k)
         weight[x, rows, :] = k * factor
         scale[x, rows, :] = factor
-        source[x, rows, :] = factor * b
+        source[x, rows, :] = b
         mid_conduct[x, rows, :] = k
 
     def far(x):
-        return second_halo(yy_a, yy_b, n, 1, x, base)
+        return second_halo(yy_a, yy_b, n, MID_HALO, 1, x, base)
 
     for i in range(n):
         put(HALO + i, slice(0, 16), source_own[i], conduct_own[i])
@@ -550,7 +562,9 @@
             rows = slice(8 * t, 8 * t + 8)
             b_after, b_before = x_sides(x_a, x_b, 3 * k + t)
             if t < 2:
-                c_after, c_before = x_sides(xx_a, xx_b, 16 + 2 * k + t)
+                none = jnp.zeros((8, 256), F32)
+                c_before = x_sides(xx_a, xx_b, 16 + 2 * (k - 1) + t)[1] if k > 0 else none
+                c_after = x_sides(xx_a, xx_b, 16 + 2 * k + t)[0] if k < MID_HALO else none
             else:
                 c_after, c_before = far(HALO + n + k), far(k)
             put(k, rows, b_before, c_before)
@@ -668,7 +682,7 @@
 
 
 def is_early():
-    return lax.axis_index("grp") < lax.axis_size("grp") // 2
+    return (lax.axis_index("grp") < lax.axis_size("grp") // 2) | odd("grp")
 
 
 def finish_inner(error, fields, kept, out, scratch):
@@ -748,64 +762,74 @@
         finish_inner(error, fields, kept, out, scratch)
 
 
-def finish_edge_kernel(
-    x_a, x_b, mid_two, mid_source, mid_weight, fine_two, edge_two, fine_source, edge_source, fine_weight,
-    zero, one, fine_one, fine_last, begun, out, zero_edge, one_edge, fine_edge, last_edge, dup, dup_2, result, sems,
+def finish_edge(
+    side, planes, mid_two, mid_source, mid_weight, fine_two, edge_two, fine_source, edge_source, fine_weight,
+    zero, one, fine_one, fine_last, out, zero_edge, one_edge, fine_edge, last_edge, dup, dup_2, result, sem,
 ):
     n = mid_two.shape[0]
     nf = fine_two.shape[0]
     nx = nf - 2 * HALO
-    copies = []
-    planes = x_sides(x_a, x_b, slice(0, 2))
-    for side in (0, 1):
-        sign = 1 if side == 0 else -1
-        at = lambda k, side=side: HALO + k if side == 0 else n - HALO - 1 - k
-        fine = lambda k, side=side: HALO + k if side == 0 else nf - HALO - 1 - k
-        base = 8 * side + (0 if side == 0 else HALO - HALO - nx)
-        for c in range(2):
-            plane = planes[1 - side][c]
-            spread = spread_coarse(plane, dup.at[2 * side + c])
-            first = 2 * c if side == 0 else n - HALO + 2 * c
-            for x in (first, first + 1):
-                zero_edge[x] = jnp.where(mid_weight[x] > 0.0, mid_two[x] + spread, 0.0)
-
-        def zero_of(k, side=side):
-            return zero[2 * side + k] if k >= 0 else zero_edge[at(k)]
-
-        def one_of(k, side=side):
-            return one[2 * side + k - 1] if k >= 1 else one_edge[at(k)]
-
-        for k in range(-2, 1):
-            x = at(k)
-            one_edge[x] = smoothed(zero_of(k - 1), zero_of(k), zero_of(k + 1), mid_weight[x], mid_source[x], 0.25)
-        for k in range(-1, 2):
-            x = at(k)
-            value = smoothed(one_of(k - 1), one_of(k), one_of(k + 1), mid_weight[x], mid_source[x], 0.25)
-            spread = spread_mid(value, dup_2.at[3 * side + k + 1])
-            for f in (fine(2 * k), fine(2 * k + 1)):
-                inside = HALO < f < nf - HALO - 1
-                before = fine_two[f] if inside else edge_two[base + f]
-                fine_edge[f] = before + spread
-
-        def fine_of(k, side=side):
-            return fine_one[2 * side + k - 4] if k >= 4 else fine_edge[fine(k)]
-
-        def last_of(k, side=side):
-            return fine_last[2 * side + k - 5] if k >= 5 else last_edge[fine(k)]
-
-        for k in range(-1, 5):
-            f = fine(k)
-            source = fine_source[f] if HALO <= f < nf - HALO else edge_source[base + f]
-            last_edge[f] = smoothed(fine_of(k - 1), fine_of(k), fine_of(k + 1), fine_weight[f], source, 1.0)
-        for k in range(6):
-            f = fine(k)
-            v = smoothed(last_of(k - 1), last_of(k), last_of(k + 1), fine_weight[f], fine_source[f], 1.0)
-            result[f - HALO] = v[0:32, :]
-        rows = pl.ds(0, 6) if side == 0 else pl.ds(nx - 6, 6)
-        copies.append(pltpu.make_async_copy(result.at[rows], out.at[rows], sems.at[side]))
-        copies[-1].start()
-    for c in copies:
-        c.wait()
+    at = lambda k: HALO + k if side == 0 else n - HALO - 1 - k
+    fine = lambda k: HALO + k if side == 0 else nf - HALO - 1 - k
+    base = 0 if side == 0 else 8 - nx
+    for c in range(2):
+        spread = spread_coarse(planes[c], dup.at[c])
+        first = 2 * c if side == 0 else n - HALO + 2 * c
+        for x in (first, first + 1):
+            zero_edge[x] = jnp.where(mid_weight[x] > 0.0, mid_two[x] + spread, 0.0)
+
+    def zero_of(k):
+        return zero[2 * side + k] if k >= 0 else zero_edge[at(k)]
+
+    def one_of(k):
+        return one[2 * side + k - 1] if k >= 1 else one_edge[at(k)]
+
+    for k in range(-2, 1):
+        x = at(k)
+        one_edge[x] = smoothed(zero_of(k - 1), zero_of(k), zero_of(k + 1), mid_weight[x], mid_source[x], 0.25)
+    for k in range(-1, 2):
+        x = at(k)
+        value = smoothed(one_of(k - 1), one_of(k), one_of(k + 1), mid_weight[x], mid_source[x], 0.25)
+        spread = spread_mid(value, dup_2.at[k + 1])
+        for f in (fine(2 * k), fine(2 * k + 1)):
+            inside = HALO < f < nf - HALO - 1
+            before = fine_two[f] if inside else edge_two[base + f]
+            fine_edge[f] = before + spread
+
+    def fine_of(k):
+        return fine_one[2 * side + k - 4] if k >= 4 else fine_edge[fine(k)]
+
+    def last_of(k):
+        return fine_last[2 * side + k - 5] if k >= 5 else last_edge[fine(k)]
+
+    for k in range(-1, 5):
+        f = fine(k)
+        source = fine_source[f] if HALO <= f < nf - HALO else edge_source[base + f]
+        last_edge[f] = smoothed(fine_of(k - 1), fine_of(k), fine_of(k + 1), fine_weight[f], source, 1.0)
+    for k in range(6):
+        f = fine(k)
+        v = smoothed(last_of(k - 1), last_of(k), last_of(k + 1), fine_weight[f], fine_source[f], 1.0)
+        result[f - HALO] = v[0:32, :]
+    rows = pl.ds(0, 6) if side == 0 else pl.ds(nx - 6, 6)
+    copy = pltpu.make_async_copy(result.at[rows], out.at[rows], sem)
+    copy.start()
+    copy.wait()
+
+
+def finish_edge_kernel(second):
+    def kernel(planes, *rest):
+        fields, out, scratch = rest[:12], rest[13], rest[14:]
+        after = odd("grp") if second else jnp.logical_not(odd("grp"))
+
+        @pl.when(after)
+        def _():
+            finish_edge(1, planes, *fields, out, *scratch)
+
+        @pl.when(jnp.logical_not(after))
+        def _():
+            finish_edge(0, planes, *fields, out, *scratch)
+
+    return kernel
 
 
 def both_ways(pairs):
@@ -847,7 +871,7 @@
     y_a, y_b = swap(pay_a, pay_b, "dev")
     conduct_mid, conduct_coarse, pay_a, pay_b, lists, gain, base = call(
         own_kernel,
-        [shaped(half, half, 256), shaped(quarter, quarter, 256), shaped(24, 8, 256), shaped(24, 8, 256)]
+        [shaped(half, half, 256), shaped(quarter, quarter, 256), shaped(22, 8, 256), shaped(22, 8, 256)]
         + [shaped(2, 256), shaped(nx, nx, 256), shaped(nx, nx, 256)],
         [conc_old, phase_label, phi_old, own_lists],
         [vmem(half, 2, nx, LANES), vmem(quarter, 2, half, LANES)],
@@ -916,7 +940,7 @@
     edge_two, edge_source, source_mid, pay_a, pay_b = call(
         potential_edge_kernel,
         [shaped(*edge), shaped(*edge), shaped(half, half, 256), shaped(4 * half, 256), shaped(4 * half, 256)],
-        [fx_a, fx_b, weight, scale, field, fine_two, fine_source, fine_first, inner_mid],
+        [fx_a, fx_b, weight, scale, field, fine_two, fine_source, fine_first, inner_mid, conduct_mid],
         [vmem(*edge), vmem(2, 2, nx, LANES)],
         name="potential_edge",
     )
@@ -986,20 +1010,21 @@
         aliases={11: 0},
         name="finish_late",
     )
-    finish_args = [e_a, e_b, mid_two, mid_source, mid_weight, fine_two, edge_two, fine_source, edge_source, weight]
-    finish_args += [zero, one, fine_one, fine_last, begun]
-    (potential,) = call(
-        finish_edge_kernel,
-        [shaped(nx, nx, 256)],
-        finish_args,
-        [vmem(*ext_mid), vmem(*ext_mid), vmem(*ext), vmem(*ext)]
-        + [vmem(4, 2, 2, 16, LANES), vmem(6, 3, 2, 16, LANES), vmem(nx, nx, 256)]
-        + [pltpu.SemaphoreType.DMA((2,))],
-        in_specs=[WHOLE] * (len(finish_args) - 1) + [FAR],
-        out_specs=[FAR],
-        aliases={len(finish_args) - 1: 0},
-        name="finish_edge",
-    )
+    potential = begun
+    finish_args = [mid_two, mid_source, mid_weight, fine_two, edge_two, fine_source, edge_source, weight]
+    finish_args += [zero, one, fine_one, fine_last]
+    for second, planes in ((False, e_b), (True, e_a)):
+        (potential,) = call(
+            finish_edge_kernel(second),
+            [shaped(nx, nx, 256)],
+            [planes] + finish_args + [potential],
+            [vmem(*ext_mid), vmem(*ext_mid), vmem(*ext), vmem(*ext)]
+            + [vmem(2, 2, 2, 16, LANES), vmem(3, 3, 2, 16, LANES), vmem(nx, nx, 256), pltpu.SemaphoreType.DMA],
+            in_specs=[WHOLE] * 13 + [FAR],
+            out_specs=[FAR],
+            aliases={13: 0},
+            name="finish_edge_2" if second else "finish_edge_1",
+        )
     return (concentration, flux, potential)
 
 

time: 84.8 us -> 85.5 us (level)
  waiting for transfers between devices: 13.9 us -> 10.7 us
  starting transfers between devices: 44 us -> 46.5 us
    ppermute x10, waiting for transfers between devices: 5.78 us -> 3.43 us  [swap(): lax.ppermute(pay_b, axis, both_ways(pairs_b))]
    ppermute x10, starting transfers between devices: 20.9 us -> 22.2 us  [swap(): lax.ppermute(pay_a, axis, both_ways(pairs_a))]
    ppermute x10, starting transfers between devices: 16.4 us -> 17.7 us  [swap(): lax.ppermute(pay_b, axis, both_ways(pairs_b))]
    pallas_call x19 -> x20, Pallas kernels: 23.5 us -> 24.3 us  [call(): pl.pallas_call(kernel, out_shape=tuple(outs), in_specs=in_specs or [WHOLE...]
  transfers between devices with their start and end apart: 24 -> 24, of which waited for: 8 -> 8; matrix products, arithmetic and copies ran while one was open for 0% -> 0% of each run, Pallas kernels for 18% -> 19%
where the time goes in v11:
time: 85.5 us; the launch traced here: 84.7 us
  starting transfers between devices  46.5 us (54%)
  Pallas kernels  24.3 us (28%)
  waiting for transfers between devices  10.7 us (13%)
  local copies, waits for them, and re-layouts  1.94 us (2%)
  between operations  1.19 us (1%)
    pallas_call x20, Pallas kernels, call(): pl.pallas_call(kernel, out_shape=tuple(outs), in_specs=in_specs or [WHOLE...  24.3 us
    ppermute x10, starting transfers between devices, swap(): lax.ppermute(pay_a, axis, both_ways(pairs_a))  22.2 us
    ppermute x10, starting transfers between devices, swap(): lax.ppermute(pay_b, axis, both_ways(pairs_b))  17.7 us
    ppermute x4, starting transfers between devices, exchange(): lax.ppermute(value, 'dev', [(i, i ^ distance) for i in range(lax.axis_siz...  6.66 us
    ppermute x10, waiting for transfers between devices, swap(): lax.ppermute(pay_a, axis, both_ways(pairs_a))  5.8 us
    ppermute x10, waiting for transfers between devices, swap(): lax.ppermute(pay_b, axis, both_ways(pairs_b))  3.43 us
    unnamed x12, local copies, waits for them, and re-layouts  1.94 us
  transfers between devices with their start and end apart: 24, of which 8 were waited for; matrix products, arithmetic and copies ran while one was open for 0% of the time, Pallas kernels for 19%

profile of v11, /device:TPU:1, one launch (start us, length us, event | category | flops | bytes accessed | tf_op | source)
XLA Modules:
  0.0 84.7 jit_solution(17237048724136980216)
XLA Ops:
  0.7 2.2 %first_pack.1 = (f32[224,256]{1,0:T(8,128)}, f32[224,256]{1,0:T(8,128)}, f32[8,256]{1,0:T(8,128)}) custom-call(f32[32,32,256]{2,1,0:T(8,128)} %conc.9, s32[32,32,256]{2,1,0:T(8,128)} %label.11, s32[1,256]{1,0:T(1,128)} %bitcast.1, s32[1,256]{1,0:T(1,128)} %block.1), custom_call_target="tpu_custom_call" | custom-call | flops 1000000 | bytes 2566144 | tf_op jit(solution)/shard_map/first_pack/pallas_call | solution.py:36
  3.5 4.6 %collective-permute-start.1 = (f32[224,256]{1,0:T(8,128)}, f32[224,256]{1,0:T(8,128)S(1)}, u32[]{:S(2)}, u32[]{:S(2)}) collective-permute-start(f32[224,256]{1,0:T(8,128)} %get-tuple-element.70), channel_id=1, source_target_pairs={{0,1},{2,3},{4,5},{6,7},{1,0},{3,2},{5,4},{7,6},{8,9},{10,11},{12,... | collective-permute-start | bytes 688136 | tf_op jit(solution)/shard_map/ppermute | solution.py:843
  8.1 1.2 %copy-done.2 = f32[32,32,256]{2,1,0:T(8,128)S(1)} copy-done((f32[32,32,256]{2,1,0:T(8,128)S(1)}, f32[32,32,256]{2,1,0:T(8,128)}, u32[]{:S(2)}) %copy-start.2) | copy-done | bytes 1048600
  10.7 2.4 %collective-permute-start.4 = (f32[2,256]{1,0:T(2,128)S(1)}, f32[2,256]{1,0:T(2,128)S(1)}, u32[]{:S(2)}, u32[]{:S(2)}) collective-permute-start(f32[2,256]{1,0:T(2,128)S(1)} %get-tuple-element.75), channel_id=1, source_target_pairs={{0,4},{1,5},{2,6},{3,7},{4,0},{5,1},{6,2},{7,3},{8,12},{9,13},{10,... | collective-permute-start | bytes 6152 | tf_op jit(solution)/shard_map/ppermute | solution.py:847
  13.1 4.5 %collective-permute-start.6 = (f32[22,8,256]{2,1,0:T(8,128)S(1)}, f32[22,8,256]{2,1,0:T(8,128)S(1)}, u32[]{:S(2)}, u32[]{:S(2)}) collective-permute-start(f32[22,8,256]{2,1,0:T(8,128)S(1)} %get-tuple-element.77), channel_id=1, source_target_pairs={{8,16},{16,8},{9,17},{17,9},{10,18},{18,10},{11,19},{19,11},{12,20... | collective-permute-start | bytes 540680 | tf_op jit(solution)/shard_map/ppermute | solution.py:843
  18.3 3.5 %collective-permute-start.2 = (f32[35,8,256]{2,1,0:T(8,128)S(1)}, f32[35,8,256]{2,1,0:T(8,128)S(1)}, u32[]{:S(2)}, u32[]{:S(2)}) collective-permute-start(f32[35,8,256]{2,1,0:T(8,128)S(1)} %get-tuple-element.72), channel_id=1, source_target_pairs={{8,16},{16,8},{9,17},{17,9},{10,18},{18,10},{11,19},{19,11},{12,20... | collective-permute-start | bytes 860168 | tf_op jit(solution)/shard_map/ppermute | solution.py:843
  22.1 2.2 %collective-permute-start.8 = (f32[272,256]{1,0:T(8,128)S(1)}, f32[272,256]{1,0:T(8,128)S(1)}, u32[]{:S(2)}, u32[]{:S(2)}) collective-permute-start(f32[272,256]{1,0:T(8,128)S(1)} %get-tuple-element.79), channel_id=1, source_target_pairs={{0,1},{2,3},{4,5},{6,7},{1,0},{3,2},{5,4},{7,6},{8,9},{10,11},{12,... | collective-permute-start | bytes 835592 | tf_op jit(solution)/shard_map/ppermute | solution.py:843
  25.0 1.6 %collective-permute-done.2.x_a = f32[35,8,256]{2,1,0:T(8,128)S(1)} collective-permute-done((f32[35,8,256]{2,1,0:T(8,128)S(1)}, f32[35,8,256]{2,1,0:T(8,128)S(1)}, u32[]{:S(2)}, u32[]{:S(2)}) %collective-permute-start.2) | collective-permute-done | bytes 286752 | tf_op jit(solution)/shard_map/ppermute | solution.py:843
  26.5 4.7 %sweeps.1.conc = f32[32,32,256]{2,1,0:T(8,128)S(1)} custom-call(f32[32,32,256]{2,1,0:T(8,128)S(1)} %copy-done.1, s32[32,32,256]{2,1,0:T(8,128)S(1)} %copy-done, f32[32,32,256]{2,1,0:T(8,128)S(1)} %get-tuple-element.67.gain_own, f32[32,32,256]{2,1,0:T(8,128)S(1)} %get-tuple-element.68.base_own, f32[224,256]{1,0:T(8,128)S(1)} %collective-permute-done.r_a.y_a, ...), custom_call_target="tpu_custom_call" | custom-call | flops 1000000 | bytes 6275072 | tf_op jit(solution)/shard_map/sweeps/pallas_call | solution.py:36
  32.0 2.2 %collective-permute-start.10 = (f32[96,256]{1,0:T(8,128)S(1)}, f32[96,256]{1,0:T(8,128)S(1)}, u32[]{:S(2)}, u32[]{:S(2)}) collective-permute-start(f32[96,256]{1,0:T(8,128)S(1)} %get-tuple-element.84), channel_id=1, source_target_pairs={{0,1},{2,3},{4,5},{6,7},{1,0},{3,2},{5,4},{7,6},{8,9},{10,11},{12,... | collective-permute-start | bytes 294920 | tf_op jit(solution)/shard_map/ppermute | solution.py:843
  35.7 0.8 mask.1
  36.5 1.2 %collective-permute-done.10.r_b.y_b = f32[96,256]{1,0:T(8,128)S(1)} collective-permute-done((f32[96,256]{1,0:T(8,128)S(1)}, f32[96,256]{1,0:T(8,128)S(1)}, u32[]{:S(2)}, u32[]{:S(2)}) %collective-permute-start.10) | collective-permute-done | bytes 98336 | tf_op jit(solution)/shard_map/ppermute | solution.py:843
  37.8 5.5 %collective-permute-start.11 = (f32[15,8,256]{2,1,0:T(8,128)S(1)}, f32[15,8,256]{2,1,0:T(8,128)S(1)}, u32[]{:S(2)}, u32[]{:S(2)}) collective-permute-start(f32[15,8,256]{2,1,0:T(8,128)S(1)} %get-tuple-element.87), channel_id=1, source_target_pairs={{8,16},{16,8},{9,17},{17,9},{10,18},{18,10},{11,19},{19,11},{12,20... | collective-permute-start | bytes 368648 | tf_op jit(solution)/shard_map/ppermute | solution.py:843
  43.3 3.3 %potential_inner.1 = (f32[40,40,256]{2,1,0:T(8,128)S(1)}, f32[40,40,256]{2,1,0:T(8,128)S(1)}, f32[40,40,256]{2,1,0:T(8,128)S(1)}, f32[16,16,256]{2,1,0:T(8,128)S(1)}, f32[40,40,256]{2,1,0:T(8,128)S(1)}) custom-call(f32[32,32,256]{2,1,0:T(8,128)S(1)} %get-tuple-element.80.flux, f32[32,8,256]{2,1,0:T(8,128)S(1)} %get-tuple-element.85.mask, ...), custom_call_target="tpu_custom_call" | custom-call | flops 1000000 | bytes 13557760 | tf_op jit(solution)/shard_map/potential_inner/pallas_call | solution.py:36
  48.0 5.7 %collective-permute-start.15 = (f32[64,256]{1,0:T(8,128)S(1)}, f32[64,256]{1,0:T(8,128)S(1)}, u32[]{:S(2)}, u32[]{:S(2)}) collective-permute-start(f32[64,256]{1,0:T(8,128)S(1)} %get-tuple-element.99), channel_id=1, source_target_pairs={{0,1},{2,3},{4,5},{6,7},{1,0},{3,2},{5,4},{7,6},{8,9},{10,11},{12,... | collective-permute-start | bytes 196616 | tf_op jit(solution)/shard_map/ppermute | solution.py:843
  53.7 1.2 %coarse_ready.1 = (f32[8,8,256]{2,1,0:T(8,128)S(1)}, f32[8,128]{1,0:T(8,128)S(1)}, f32[8,128]{1,0:T(8,128)S(1)}) custom-call(f32[8,8,256]{2,1,0:T(8,128)S(1)} %get-tuple-element.71.token.coarse.own, f32[264,256]{1,0:T(8,128)S(1)} %collective-permute-done.13.yy_a.r_a.far_a, f32[272,256]{1,0:T(8,128)S(1)} %collective-permute-done.8.far.yy_b.r_b.far_b), custom_call_target="tpu_custom_call" | custom-call | flops 1000000 | bytes 688128 | tf_op jit(solution)/shard_map/coarse_ready/pallas_call | solution.py:36
  54.9 1.4 %store.1 = (f32[32,32,256]{2,1,0:T(8,128)}, f32[32,32,256]{2,1,0:T(8,128)}, f32[8,128]{1,0:T(8,128)S(1)}) custom-call(f32[32,32,256]{2,1,0:T(8,128)S(1)} %sweeps.1.conc, f32[32,32,256]{2,1,0:T(8,128)S(1)} %get-tuple-element.80.flux), custom_call_target="tpu_custom_call" | custom-call | flops 1000000 | bytes 4198400 | tf_op jit(solution)/shard_map/store/pallas_call | solution.py:36
  56.4 3.3 %collective-permute-start.16 = (f32[12,8,256]{2,1,0:T(8,128)S(1)}, f32[12,8,256]{2,1,0:T(8,128)S(1)}, u32[]{:S(2)}, u32[]{:S(2)}) collective-permute-start(f32[12,8,256]{2,1,0:T(8,128)S(1)} %get-tuple-element.102), channel_id=1, source_target_pairs={{8,16},{16,8},{9,17},{17,9},{10,18},{18,10},{11,19},{19,11},{12,20... | collective-permute-start | bytes 294920 | tf_op jit(solution)/shard_map/ppermute | solution.py:843
  59.7 2.5 %collective-permute-done.16.x_a = f32[12,8,256]{2,1,0:T(8,128)S(1)} collective-permute-done((f32[12,8,256]{2,1,0:T(8,128)S(1)}, f32[12,8,256]{2,1,0:T(8,128)S(1)}, u32[]{:S(2)}, u32[]{:S(2)}) %collective-permute-start.16) | collective-permute-done | bytes 98336 | tf_op jit(solution)/shard_map/ppermute | solution.py:843
  62.3 1.1 %middle.1 = (f32[24,24,256]{2,1,0:T(8,128)S(1)}, f32[24,24,256]{2,1,0:T(8,128)S(1)}, f32[24,24,256]{2,1,0:T(8,128)S(1)}, f32[8,12,256]{2,1,0:T(8,128)S(1)}, f32[...) custom-call(f32[16,16,256]{2,1,0:T(8,128)S(1)} %get-tuple-element.97.field.source_o, ...), custom_call_target="tpu_custom_call" | custom-call | flops 1000000 | bytes 3960832 | tf_op jit(solution)/shard_map/middle/pallas_call | solution.py:36
  63.4 1.1 %collective-permute-start.19 = (f32[80,256]{1,0:T(8,128)S(1)}, f32[80,256]{1,0:T(8,128)S(1)}, u32[]{:S(2)}, u32[]{:S(2)}) collective-permute-start(f32[80,256]{1,0:T(8,128)S(1)} %get-tuple-element.109), channel_id=1, source_target_pairs={{0,1},{2,3},{4,5},{6,7},{1,0},{3,2},{5,4},{7,6},{8,9},{10,11},{12,... | collective-permute-start | bytes 245768 | tf_op jit(solution)/shard_map/ppermute | solution.py:843
  65.1 1.8 %collective-permute-done.19.r_b = f32[80,256]{1,0:T(8,128)S(1)} collective-permute-done((f32[80,256]{1,0:T(8,128)S(1)}, f32[80,256]{1,0:T(8,128)S(1)}, u32[]{:S(2)}, u32[]{:S(2)}) %collective-permute-start.19) | collective-permute-done | bytes 81952 | tf_op jit(solution)/shard_map/ppermute | solution.py:843
  66.9 2.0 %collective-permute-start.20 = (f32[8,256]{1,0:T(8,128)S(1)}, f32[8,256]{1,0:T(8,128)S(1)}, u32[]{:S(2)}, u32[]{:S(2)}) collective-permute-start(f32[8,256]{1,0:T(8,128)S(1)} %slice_add_fusion), channel_id=1, source_target_pairs={{0,2},{1,3},{2,0},{3,1},{4,6},{5,7},{6,4},{7,5},{8,10},{9,11},{10,... | collective-permute-start | bytes 24584 | tf_op jit(solution)/shard_map/ppermute | solution.py:847
  69.0 1.4 %collective-permute-done.20 = f32[8,256]{1,0:T(8,128)S(1)} collective-permute-done((f32[8,256]{1,0:T(8,128)S(1)}, f32[8,256]{1,0:T(8,128)S(1)}, u32[]{:S(2)}, u32[]{:S(2)}) %collective-permute-start.20) | collective-permute-done | bytes 8224 | tf_op jit(solution)/shard_map/ppermute | solution.py:847
  70.4 2.2 %collective-permute-start.21 = (f32[8,256]{1,0:T(8,128)S(1)}, f32[8,256]{1,0:T(8,128)S(1)}, u32[]{:S(2)}, u32[]{:S(2)}) collective-permute-start(f32[8,256]{1,0:T(8,128)S(1)} %add.10), channel_id=1, source_target_pairs={{0,4},{1,5},{2,6},{3,7},{4,0},{5,1},{6,2},{7,3},{8,12},{9,13},{10,... | collective-permute-start | bytes 24584 | tf_op jit(solution)/shard_map/ppermute | solution.py:847
  72.6 1.2 %coarse.1.error = f32[8,16,256]{2,1,0:T(8,128)S(1)} custom-call(f32[8,12,256]{2,1,0:T(8,128)S(1)} %get-tuple-element.106.own, f32[8,12,256]{2,1,0:T(8,128)S(1)} %get-tuple-element.107.conduct, f32[264,256]{1,0:T(8,128)S(1)} %collective-permute-done.13.yy_a.r_a.far_a, f32[272,256]{1,0:T(8,128)S(1)} %collective-permute-done.8.far.yy_b.r_b.far_b, ...), custom_call_target="tpu_custom_call" | custom-call | flops 1000000 | bytes 1032192 | tf_op jit(solution)/shard_map/coarse/pallas_call | solution.py:36
  73.8 2.7 %finish_early.1 = (f32[8,16,256]{2,1,0:T(8,128)S(1)}, f32[2,16,256]{2,1,0:T(8,128)S(1)}, f32[2,16,256]{2,1,0:T(8,128)S(1)}, f32[32,32,256]{2,1,0:T(8,128)}, f32[...) custom-call(f32[8,16,256]{2,1,0:T(8,128)S(1)} %coarse.1.error, ...), custom_call_target="tpu_custom_call" | custom-call | flops 1000000 | bytes 8593408 | tf_op jit(solution)/shard_map/finish_early/pallas_call | solution.py:36
  76.5 1.6 %collective-permute-start.23 = (f32[2,16,256]{2,1,0:T(8,128)S(1)}, f32[2,16,256]{2,1,0:T(8,128)S(1)}, u32[]{:S(2)}, u32[]{:S(2)}) collective-permute-start(f32[2,16,256]{2,1,0:T(8,128)S(1)} %get-tuple-element.127), channel_id=1, source_target_pairs={{0,8},{16,24},{8,0},{24,16},{1,9},{17,25},{9,1},{25,17},{2,10},{18... | collective-permute-start | bytes 98312 | tf_op jit(solution)/shard_map/ppermute | solution.py:843
  78.1 2.1 %collective-permute-start.22 = (f32[2,16,256]{2,1,0:T(8,128)S(1)}, f32[2,16,256]{2,1,0:T(8,128)S(1)}, u32[]{:S(2)}, u32[]{:S(2)}) collective-permute-start(f32[2,16,256]{2,1,0:T(8,128)S(1)} %get-tuple-element.114), channel_id=1, source_target_pairs={{8,16},{16,8},{9,17},{17,9},{10,18},{18,10},{11,19},{19,11},{12,20... | collective-permute-start | bytes 98312 | tf_op jit(solution)/shard_map/ppermute | solution.py:843
  80.5 1.2 %finish_edge_1.1.rest_12_ = f32[32,32,256]{2,1,0:T(8,128)} custom-call(f32[2,16,256]{2,1,0:T(8,128)S(1)} %collective-permute-done.23.planes, f32[24,24,256]{2,1,0:T(8,128)S(1)} %get-tuple-element.111.rest_0_, f32[24,24,256]{2,1,0:T(8,128)S(1)} %get-tuple-element.112.rest_1_, ...), custom_call_target="tpu_custom_call", output_to_operand_aliasing={{}: (13, {})} | custom-call | flops 1000000 | bytes 10649600 | tf_op jit(solution)/shard_map/finish_edge_1/pallas_call | solution.py:36
  81.7 1.7 %collective-permute-done.22.planes = f32[2,16,256]{2,1,0:T(8,128)S(1)} collective-permute-done((f32[2,16,256]{2,1,0:T(8,128)S(1)}, f32[2,16,256]{2,1,0:T(8,128)S(1)}, u32[]{:S(2)}, u32[]{:S(2)}) %collective-permute-start.22) | collective-permute-done | bytes 32800 | tf_op jit(solution)/shard_map/ppermute | solution.py:843
  83.4 1.2 %finish_edge_2.1 = f32[32,32,256]{2,1,0:T(8,128)} custom-call(f32[2,16,256]{2,1,0:T(8,128)S(1)} %collective-permute-done.22.planes, f32[24,24,256]{2,1,0:T(8,128)S(1)} %get-tuple-element.111.rest_0_, f32[24,24,256]{2,1,0:T(8,128)S(1)} %get-tuple-element.112.rest_1_, f32[24,24,256]{2,1,0:T(8,128)S(1)} %get-tuple-element.113.rest_2_, ...), custom_call_target="tpu_custom_call", output_to_operand_aliasing={{}: (13, {})} | custom-call | flops 1000000 | bytes 10649600 | tf_op jit(solution)/shard_map/finish_edge_2/pallas_call | solution.py:36
  (53 shorter events, 8.3 us)
Async XLA Ops:
  0.6 7.5 %copy-start.1 = (f32[32,32,256]{2,1,0:T(8,128)S(1)}, f32[32,32,256]{2,1,0:T(8,128)}, u32[]{:S(2)}) copy-start(f32[32,32,256]{2,1,0:T(8,128)} %conc.9) | copy-start | bytes 3145732
  0.6 7.5 %copy-start = (s32[32,32,256]{2,1,0:T(8,128)S(1)}, s32[32,32,256]{2,1,0:T(8,128)}, u32[]{:S(2)}) copy-start(s32[32,32,256]{2,1,0:T(8,128)} %label.11) | copy-start | bytes 3145732
  2.8 15.0 %collective-permute-start = (f32[224,256]{1,0:T(8,128)}, f32[224,256]{1,0:T(8,128)S(1)}, u32[]{:S(2)}, u32[]{:S(2)}) collective-permute-start(f32[224,256]{1,0:T(8,128)} %get-tuple-element.69), channel_id=1, source_target_pairs={{1,2},{3,4},{5,6},{2,1},{4,3},{6,5},{9,10},{11,12},{13,14},{10,9},... | collective-permute-start | bytes 688136 | tf_op jit(solution)/shard_map/ppermute | solution.py:843
  3.5 14.7 %collective-permute-start.1 = (f32[224,256]{1,0:T(8,128)}, f32[224,256]{1,0:T(8,128)S(1)}, u32[]{:S(2)}, u32[]{:S(2)}) collective-permute-start(f32[224,256]{1,0:T(8,128)} %get-tuple-element.70), channel_id=1, source_target_pairs={{0,1},{2,3},{4,5},{6,7},{1,0},{3,2},{5,4},{7,6},{8,9},{10,11},{12,... | collective-permute-start | bytes 688136 | tf_op jit(solution)/shard_map/ppermute | solution.py:843
  8.1 1.2 %copy-start.2 = (f32[32,32,256]{2,1,0:T(8,128)S(1)}, f32[32,32,256]{2,1,0:T(8,128)}, u32[]{:S(2)}) copy-start(f32[32,32,256]{2,1,0:T(8,128)} %phi.7) | copy-start | bytes 3145732
  9.3 0.7 copy-start.5
  10.7 11.3 %copy-start.3 = (f32[32,32,256]{2,1,0:T(8,128)S(1)}, f32[32,32,256]{2,1,0:T(8,128)}, u32[]{:S(2)}) copy-start(f32[32,32,256]{2,1,0:T(8,128)} %phi.7) | copy-start | bytes 3145732
  10.7 7.0 %collective-permute-start.4 = (f32[2,256]{1,0:T(2,128)S(1)}, f32[2,256]{1,0:T(2,128)S(1)}, u32[]{:S(2)}, u32[]{:S(2)}) collective-permute-start(f32[2,256]{1,0:T(2,128)S(1)} %get-tuple-element.75), channel_id=1, source_target_pairs={{0,4},{1,5},{2,6},{3,7},{4,0},{5,1},{6,2},{7,3},{8,12},{9,13},{10,... | collective-permute-start | bytes 6152 | tf_op jit(solution)/shard_map/ppermute | solution.py:847
  13.1 8.9 %collective-permute-start.6 = (f32[22,8,256]{2,1,0:T(8,128)S(1)}, f32[22,8,256]{2,1,0:T(8,128)S(1)}, u32[]{:S(2)}, u32[]{:S(2)}) collective-permute-start(f32[22,8,256]{2,1,0:T(8,128)S(1)} %get-tuple-element.77), channel_id=1, source_target_pairs={{8,16},{16,8},{9,17},{17,9},{10,18},{18,10},{11,19},{19,11},{12,20... | collective-permute-start | bytes 540680 | tf_op jit(solution)/shard_map/ppermute | solution.py:843
  17.6 4.3 %collective-permute-start.7 = (f32[22,8,256]{2,1,0:T(8,128)S(1)}, f32[22,8,256]{2,1,0:T(8,128)S(1)}, u32[]{:S(2)}, u32[]{:S(2)}) collective-permute-start(f32[22,8,256]{2,1,0:T(8,128)S(1)} %get-tuple-element.78), channel_id=1, source_target_pairs={{0,8},{16,24},{8,0},{24,16},{1,9},{17,25},{9,1},{25,17},{2,10},{18... | collective-permute-start | bytes 540680 | tf_op jit(solution)/shard_map/ppermute | solution.py:843
  17.7 4.2 %collective-permute-start.5 = (f32[4,256]{1,0:T(4,128)S(1)}, f32[4,256]{1,0:T(4,128)S(1)}, u32[]{:S(2)}, u32[]{:S(2)}) collective-permute-start(f32[4,256]{1,0:T(4,128)S(1)} %pad_maximum_fusion.1), channel_id=1, source_target_pairs={{0,2},{1,3},{2,0},{3,1},{4,6},{5,7},{6,4},{7,5},{8,10},{9,11},{10,... | collective-permute-start | bytes 12296 | tf_op jit(solution)/shard_map/ppermute | solution.py:847
  18.3 8.2 %collective-permute-start.2 = (f32[35,8,256]{2,1,0:T(8,128)S(1)}, f32[35,8,256]{2,1,0:T(8,128)S(1)}, u32[]{:S(2)}, u32[]{:S(2)}) collective-permute-start(f32[35,8,256]{2,1,0:T(8,128)S(1)} %get-tuple-element.72), channel_id=1, source_target_pairs={{8,16},{16,8},{9,17},{17,9},{10,18},{18,10},{11,19},{19,11},{12,20... | collective-permute-start | bytes 860168 | tf_op jit(solution)/shard_map/ppermute | solution.py:843
  21.8 4.7 %collective-permute-start.3 = (f32[35,8,256]{2,1,0:T(8,128)S(1)}, f32[35,8,256]{2,1,0:T(8,128)S(1)}, u32[]{:S(2)}, u32[]{:S(2)}) collective-permute-start(f32[35,8,256]{2,1,0:T(8,128)S(1)} %get-tuple-element.73), channel_id=1, source_target_pairs={{0,8},{16,24},{8,0},{24,16},{1,9},{17,25},{9,1},{25,17},{2,10},{18... | collective-permute-start | bytes 860168 | tf_op jit(solution)/shard_map/ppermute | solution.py:843
  22.1 13.6 %collective-permute-start.8 = (f32[272,256]{1,0:T(8,128)S(1)}, f32[272,256]{1,0:T(8,128)S(1)}, u32[]{:S(2)}, u32[]{:S(2)}) collective-permute-start(f32[272,256]{1,0:T(8,128)S(1)} %get-tuple-element.79), channel_id=1, source_target_pairs={{0,1},{2,3},{4,5},{6,7},{1,0},{3,2},{5,4},{7,6},{8,9},{10,11},{12,... | collective-permute-start | bytes 835592 | tf_op jit(solution)/shard_map/ppermute | solution.py:843
  24.3 19.1 %collective-permute-start.13 = (f32[264,256]{1,0:T(8,128)S(1)}, f32[264,256]{1,0:T(8,128)S(1)}, u32[]{:S(2)}, u32[]{:S(2)}) collective-permute-start(f32[264,256]{1,0:T(8,128)S(1)} %get-tuple-element.91), channel_id=1, source_target_pairs={{1,2},{3,4},{5,6},{2,1},{4,3},{6,5},{9,10},{11,12},{13,14},{10,9},... | collective-permute-start | bytes 811016 | tf_op jit(solution)/shard_map/ppermute | solution.py:843
  26.5 4.7 %copy-start.4 = (f32[32,32,256]{2,1,0:T(8,128)S(1)}, f32[32,32,256]{2,1,0:T(8,128)}, u32[]{:S(2)}) copy-start(f32[32,32,256]{2,1,0:T(8,128)} %solid.1) | copy-start | bytes 3145732
  32.0 5.7 %collective-permute-start.10 = (f32[96,256]{1,0:T(8,128)S(1)}, f32[96,256]{1,0:T(8,128)S(1)}, u32[]{:S(2)}, u32[]{:S(2)}) collective-permute-start(f32[96,256]{1,0:T(8,128)S(1)} %get-tuple-element.84), channel_id=1, source_target_pairs={{0,1},{2,3},{4,5},{6,7},{1,0},{3,2},{5,4},{7,6},{8,9},{10,11},{12,... | collective-permute-start | bytes 294920 | tf_op jit(solution)/shard_map/ppermute | solution.py:843
  34.3 3.5 %collective-permute-start.9 = (f32[96,256]{1,0:T(8,128)S(1)}, f32[96,256]{1,0:T(8,128)S(1)}, u32[]{:S(2)}, u32[]{:S(2)}) collective-permute-start(f32[96,256]{1,0:T(8,128)S(1)} %get-tuple-element.83), channel_id=1, source_target_pairs={{1,2},{3,4},{5,6},{2,1},{4,3},{6,5},{9,10},{11,12},{13,14},{10,9},... | collective-permute-start | bytes 294920 | tf_op jit(solution)/shard_map/ppermute | solution.py:843
  37.8 8.9 %collective-permute-start.11 = (f32[15,8,256]{2,1,0:T(8,128)S(1)}, f32[15,8,256]{2,1,0:T(8,128)S(1)}, u32[]{:S(2)}, u32[]{:S(2)}) collective-permute-start(f32[15,8,256]{2,1,0:T(8,128)S(1)} %get-tuple-element.87), channel_id=1, source_target_pairs={{8,16},{16,8},{9,17},{17,9},{10,18},{18,10},{11,19},{19,11},{12,20... | collective-permute-start | bytes 368648 | tf_op jit(solution)/shard_map/ppermute | solution.py:843
  43.3 3.4 %collective-permute-start.12 = (f32[15,8,256]{2,1,0:T(8,128)S(1)}, f32[15,8,256]{2,1,0:T(8,128)S(1)}, u32[]{:S(2)}, u32[]{:S(2)}) collective-permute-start(f32[15,8,256]{2,1,0:T(8,128)S(1)} %get-tuple-element.88), channel_id=1, source_target_pairs={{0,8},{16,24},{8,0},{24,16},{1,9},{17,25},{9,1},{25,17},{2,10},{18... | collective-permute-start | bytes 368648 | tf_op jit(solution)/shard_map/ppermute | solution.py:843
  47.4 8.9 %collective-permute-start.14 = (f32[64,256]{1,0:T(8,128)S(1)}, f32[64,256]{1,0:T(8,128)S(1)}, u32[]{:S(2)}, u32[]{:S(2)}) collective-permute-start(f32[64,256]{1,0:T(8,128)S(1)} %get-tuple-element.98), channel_id=1, source_target_pairs={{1,2},{3,4},{5,6},{2,1},{4,3},{6,5},{9,10},{11,12},{13,14},{10,9},... | collective-permute-start | bytes 196616 | tf_op jit(solution)/shard_map/ppermute | solution.py:843
  48.0 8.3 %collective-permute-start.15 = (f32[64,256]{1,0:T(8,128)S(1)}, f32[64,256]{1,0:T(8,128)S(1)}, u32[]{:S(2)}, u32[]{:S(2)}) collective-permute-start(f32[64,256]{1,0:T(8,128)S(1)} %get-tuple-element.99), channel_id=1, source_target_pairs={{0,1},{2,3},{4,5},{6,7},{1,0},{3,2},{5,4},{7,6},{8,9},{10,11},{12,... | collective-permute-start | bytes 196616 | tf_op jit(solution)/shard_map/ppermute | solution.py:843
  56.4 5.9 %collective-permute-start.16 = (f32[12,8,256]{2,1,0:T(8,128)S(1)}, f32[12,8,256]{2,1,0:T(8,128)S(1)}, u32[]{:S(2)}, u32[]{:S(2)}) collective-permute-start(f32[12,8,256]{2,1,0:T(8,128)S(1)} %get-tuple-element.102), channel_id=1, source_target_pairs={{8,16},{16,8},{9,17},{17,9},{10,18},{18,10},{11,19},{19,11},{12,20... | collective-permute-start | bytes 294920 | tf_op jit(solution)/shard_map/ppermute | solution.py:843
  59.7 2.6 %collective-permute-start.17 = (f32[12,8,256]{2,1,0:T(8,128)S(1)}, f32[12,8,256]{2,1,0:T(8,128)S(1)}, u32[]{:S(2)}, u32[]{:S(2)}) collective-permute-start(f32[12,8,256]{2,1,0:T(8,128)S(1)} %get-tuple-element.103), channel_id=1, source_target_pairs={{0,8},{16,24},{8,0},{24,16},{1,9},{17,25},{9,1},{25,17},{2,10},{18... | collective-permute-start | bytes 294920 | tf_op jit(solution)/shard_map/ppermute | solution.py:843
  63.4 3.6 %collective-permute-start.19 = (f32[80,256]{1,0:T(8,128)S(1)}, f32[80,256]{1,0:T(8,128)S(1)}, u32[]{:S(2)}, u32[]{:S(2)}) collective-permute-start(f32[80,256]{1,0:T(8,128)S(1)} %get-tuple-element.109), channel_id=1, source_target_pairs={{0,1},{2,3},{4,5},{6,7},{1,0},{3,2},{5,4},{7,6},{8,9},{10,11},{12,... | collective-permute-start | bytes 245768 | tf_op jit(solution)/shard_map/ppermute | solution.py:843
  64.5 8.1 %collective-permute-start.18 = (f32[72,256]{1,0:T(8,128)S(1)}, f32[72,256]{1,0:T(8,128)S(1)}, u32[]{:S(2)}, u32[]{:S(2)}) collective-permute-start(f32[72,256]{1,0:T(8,128)S(1)} %get-tuple-element.108), channel_id=1, source_target_pairs={{1,2},{3,4},{5,6},{2,1},{4,3},{6,5},{9,10},{11,12},{13,14},{10,9},... | collective-permute-start | bytes 221192 | tf_op jit(solution)/shard_map/ppermute | solution.py:843
  66.9 3.4 %collective-permute-start.20 = (f32[8,256]{1,0:T(8,128)S(1)}, f32[8,256]{1,0:T(8,128)S(1)}, u32[]{:S(2)}, u32[]{:S(2)}) collective-permute-start(f32[8,256]{1,0:T(8,128)S(1)} %slice_add_fusion), channel_id=1, source_target_pairs={{0,2},{1,3},{2,0},{3,1},{4,6},{5,7},{6,4},{7,5},{8,10},{9,11},{10,... | collective-permute-start | bytes 24584 | tf_op jit(solution)/shard_map/ppermute | solution.py:847
  70.4 3.4 %collective-permute-start.21 = (f32[8,256]{1,0:T(8,128)S(1)}, f32[8,256]{1,0:T(8,128)S(1)}, u32[]{:S(2)}, u32[]{:S(2)}) collective-permute-start(f32[8,256]{1,0:T(8,128)S(1)} %add.10), channel_id=1, source_target_pairs={{0,4},{1,5},{2,6},{3,7},{4,0},{5,1},{6,2},{7,3},{8,12},{9,13},{10,... | collective-permute-start | bytes 24584 | tf_op jit(solution)/shard_map/ppermute | solution.py:847
  76.5 3.9 %collective-permute-start.23 = (f32[2,16,256]{2,1,0:T(8,128)S(1)}, f32[2,16,256]{2,1,0:T(8,128)S(1)}, u32[]{:S(2)}, u32[]{:S(2)}) collective-permute-start(f32[2,16,256]{2,1,0:T(8,128)S(1)} %get-tuple-element.127), channel_id=1, source_target_pairs={{0,8},{16,24},{8,0},{24,16},{1,9},{17,25},{9,1},{25,17},{2,10},{18... | collective-permute-start | bytes 98312 | tf_op jit(solution)/shard_map/ppermute | solution.py:843
  78.1 5.2 %collective-permute-start.22 = (f32[2,16,256]{2,1,0:T(8,128)S(1)}, f32[2,16,256]{2,1,0:T(8,128)S(1)}, u32[]{:S(2)}, u32[]{:S(2)}) collective-permute-start(f32[2,16,256]{2,1,0:T(8,128)S(1)} %get-tuple-element.114), channel_id=1, source_target_pairs={{8,16},{16,8},{9,17},{17,9},{10,18},{18,10},{11,19},{19,11},{12,20... | collective-permute-start | bytes 98312 | tf_op jit(solution)/shard_map/ppermute | solution.py:843

commit v12 on v10

--- a/solution.py
+++ b/solution.py
@@ -151,21 +151,39 @@
 
 
 def first_pack_kernel(
-    conc, label, owner, block, pay_a, pay_b, own_lists, c_first, c_last, l_first, l_last, own_owner, own_block, sems
+    conc, label, owner, block, out_a, out_b, own_lists,
+    c_first, c_last, l_first, l_last, own_owner, own_block, pay_a, pay_b, named, sems,
 ):
     nx = conc.shape[0]
-    copies = [pltpu.make_async_copy(owner, own_owner, sems.at[4]), pltpu.make_async_copy(block, own_block, sems.at[5])]
-    for i, (ref, at, to) in enumerate(((conc, 0, c_first), (conc, 28, c_last), (label, 0, l_first), (label, 28, l_last))):
-        copies.append(pltpu.make_async_copy(ref.at[:, pl.ds(at, 4), :], to, sems.at[i]))
-    for c in copies:
+    half = nx // 2
+    lists = [pltpu.make_async_copy(owner, own_owner, sems.at[8]), pltpu.make_async_copy(block, own_block, sems.at[9])]
+    reads = []
+    for j in range(2):
+        planes = pl.ds(half * j, half)
+        for i, (ref, at, to) in enumerate(
+            ((conc, 0, c_first), (conc, 28, c_last), (label, 0, l_first), (label, 28, l_last))
+        ):
+            reads.append(pltpu.make_async_copy(ref.at[planes, pl.ds(at, 4), :], to.at[planes], sems.at[4 * j + i]))
+    for c in reads + lists:
         c.start()
-    for c in copies:
+    writes = []
+    for j in range(2):
+        for c in reads[4 * j : 4 * j + 4]:
+            c.wait()
+        for x in range(half * j, half * j + half):
+            send_y(pay_a, pay_b, 7 * x, c_first[x], c_last[x])
+            send_y(pay_a, pay_b, 7 * x + 4, l_first[x, 0:3, :].astype(F32), l_last[x, 1:4, :].astype(F32))
+        rows = pl.ds(7 * half * j, 7 * half)
+        for i, (pay, out) in enumerate(((pay_a, out_a), (pay_b, out_b))):
+            writes.append(pltpu.make_async_copy(pay.at[rows], out.at[rows], sems.at[10 + 2 * j + i]))
+            writes[-1].start()
+    for c in lists:
         c.wait()
-    named = jnp.concatenate([own_owner[...], own_block[...], jnp.zeros((6, 256), jnp.int32)], axis=0).astype(F32)
-    own_lists[...] = named
-    for x in range(nx):
-        send_y(pay_a, pay_b, 7 * x, c_first[x], c_last[x])
-        send_y(pay_a, pay_b, 7 * x + 4, l_first[x, 0:3, :].astype(F32), l_last[x, 1:4, :].astype(F32))
+    named[...] = jnp.concatenate([own_owner[...], own_block[...], jnp.zeros((6, 256), jnp.int32)], axis=0).astype(F32)
+    writes.append(pltpu.make_async_copy(named, own_lists, sems.at[14]))
+    writes[-1].start()
+    for c in writes:
+        c.wait()
 
 
 def own_kernel(conc, label, phi, named, mid, coarse, pay_a, pay_b, lists, gain, base, pairs, pairs_2):
@@ -190,9 +208,10 @@
         for t in range(4):
             rows = slice(8 * t, 8 * t + 8)
             send_x(pay_a, pay_b, 4 * k + t, phi[k, rows, :], phi[nx - HALO + k, rows, :])
+    for k in range(MID_HALO):
         for t in range(2):
             rows = slice(8 * t, 8 * t + 8)
-            send_x(pay_a, pay_b, 16 + 2 * k + t, mid[k, rows, :], mid[half - HALO + k, rows, :])
+            send_x(pay_a, pay_b, 16 + 2 * k + t, mid[k, rows, :], mid[half - MID_HALO + k, rows, :])
 
 
 def first_pack_x_kernel(conc, label, r_a, r_b, token, pay_a, pay_b):
@@ -210,14 +229,18 @@
             send_x(pay_a, pay_b, 20 + 5 * k + t, plane(label, k, t, 4, 3), plane(label, nx - 3 + k, t, 4, 3))
 
 
-def corner_rows(n, reach):
-    counts = [min(HALO, k + reach) for k in range(HALO)]
-    counts = counts + [HALO] * n + counts[::-1]
+MID_HALO = 3
+
+
+def corner_rows(n, width, reach):
+    counts = [min(width, k + reach) for k in range(width)]
+    counts = counts + [width] * n + counts[::-1]
     return counts, [sum(counts[:i]) for i in range(len(counts))]
 
 
 def second_rows(nx):
-    phi, mid = (sum(corner_rows(n, reach)[0]) for n, reach in ((nx, 0), (nx // 2, 1)))
+    phi = sum(corner_rows(nx, HALO, 0)[0])
+    mid = sum(corner_rows(nx // 2, MID_HALO, 1)[0])
     return phi, phi + mid, phi + mid + 64
 
 
@@ -225,20 +248,21 @@
     nx = phi.shape[0]
     starts = second_rows(nx)
 
-    def put(own, n, reach, index, base):
-        counts, at = corner_rows(n, reach)
+    def put(own, width, reach, index, base):
+        n = own.shape[0]
+        counts, at = corner_rows(n, width, reach)
         tiles = own.shape[1] // 8
         for x in range(n):
-            send_y(pay_a, pay_b, base + at[HALO + x], own[x, 0:4, :], own[x, 8 * tiles - 4 : 8 * tiles, :])
-        for k in range(HALO):
+            send_y(pay_a, pay_b, base + at[width + x], own[x, 0:width, :], own[x, 8 * tiles - width : 8 * tiles, :])
+        for k in range(width):
             first_after, first_before = x_sides(x_a, x_b, index + tiles * k)
             last_after, last_before = x_sides(x_a, x_b, index + tiles * k + tiles - 1)
-            for x, first, last in ((k, first_before, last_before), (HALO + n + k, first_after, last_after)):
+            for x, first, last in ((k, first_before, last_before), (width + n + k, first_after, last_after)):
                 if counts[x]:
                     send_y(pay_a, pay_b, base + at[x], first[0 : counts[x]], last[8 - counts[x] : 8])
 
-    put(phi, nx, 0, 0, 0)
-    put(mid, nx // 2, 1, 16, starts[0])
+    put(phi, HALO, 0, 0, 0)
+    put(mid, MID_HALO, 1, 16, starts[0])
     base = starts[1]
     for x in range(8):
         pay_a[base + 8 * x : base + 8 * x + 8, :] = coarse[x]
@@ -247,9 +271,10 @@
     pay_b[base : base + lists.shape[0], :] = lists[...]
 
 
-def second_halo(r_a, r_b, n, reach, x, base):
-    counts, at = corner_rows(n, reach)
-    if not counts[x]:
+def second_halo(r_a, r_b, n, width, reach, x, base):
+    counts, at = corner_rows(n, width, reach)
+    x = x - HALO + width
+    if x < 0 or x >= len(counts) or not counts[x]:
         return jnp.zeros((8, 256), F32)
     return halo_tile(*y_sides(r_a, r_b, base + at[x], counts[x]))
 
@@ -409,7 +434,7 @@
 
     loop(0, nx, own)
     for x in range(nx + 2 * HALO):
-        field[x, 32:40, :] = second_halo(yy_a, yy_b, nx, 0, x, 0)
+        field[x, 32:40, :] = second_halo(yy_a, yy_b, nx, HALO, 0, x, 0)
     for t in range(4):
         for k in range(HALO):
             after, before = x_sides(xx_a, xx_b, 4 * k + t)
@@ -473,8 +498,12 @@
     loop(1, nx // 2 - 1, coarsen, 4)
 
 
+def mid_factor(conduct):
+    return OMEGA / (MASS + 3.0 * conduct)
+
+
 def potential_edge_kernel(
-    x_a, x_b, weight, scale, field, inner_two, inner_source, inner_first, inner_mid,
+    x_a, x_b, weight, scale, field, inner_two, inner_source, inner_first, inner_mid, conduct_mid,
     edge_two, edge_source, source_mid, pay_a, pay_b, first, pairs,
 ):
     half = source_mid.shape[0]
@@ -505,9 +534,10 @@
             v = two_of(x)
             near = weight[x] * ((two_of(x - 1) + two_of(x + 1)) + (along_y(v) + along_z(v)))
             total = total + ((source_of(x) - OMEGA * v) + near)[0:32, :] / scale[x, 0:32, :]
-        source_mid[0 if side == 0 else half - 1] = 0.25 * pair_rows(total, pairs.at[side])
+        at = 0 if side == 0 else half - 1
+        source_mid[at] = mid_factor(conduct_mid[at]) * (0.25 * pair_rows(total, pairs.at[side]))
     for x in range(1, half - 1):
-        source_mid[x] = inner_mid[x]
+        source_mid[x] = mid_factor(conduct_mid[x]) * inner_mid[x]
     for x in range(half):
         send_y(pay_a, pay_b, 4 * x, source_mid[x, 0:4, :], source_mid[x, 12:16, :])
 
@@ -533,14 +563,14 @@
     base = second_rows(2 * n)[0]
 
     def put(x, rows, b, k):
-        factor = OMEGA / (MASS + 3.0 * k)
+        factor = mid_factor(k)
         weight[x, rows, :] = k * factor
         scale[x, rows, :] = factor
-        source[x, rows, :] = factor * b
+        source[x, rows, :] = b
         mid_conduct[x, rows, :] = k
 
     def far(x):
-        return second_halo(yy_a, yy_b, n, 1, x, base)
+        return second_halo(yy_a, yy_b, n, MID_HALO, 1, x, base)
 
     for i in range(n):
         put(HALO + i, slice(0, 16), source_own[i], conduct_own[i])
@@ -550,7 +580,9 @@
             rows = slice(8 * t, 8 * t + 8)
             b_after, b_before = x_sides(x_a, x_b, 3 * k + t)
             if t < 2:
-                c_after, c_before = x_sides(xx_a, xx_b, 16 + 2 * k + t)
+                none = jnp.zeros((8, 256), F32)
+                c_before = x_sides(xx_a, xx_b, 16 + 2 * (k - 1) + t)[1] if k > 0 else none
+                c_after = x_sides(xx_a, xx_b, 16 + 2 * k + t)[0] if k < MID_HALO else none
             else:
                 c_after, c_before = far(HALO + n + k), far(k)
             put(k, rows, b_before, c_before)
@@ -668,7 +700,7 @@
 
 
 def is_early():
-    return lax.axis_index("grp") < lax.axis_size("grp") // 2
+    return (lax.axis_index("grp") < lax.axis_size("grp") // 2) | odd("grp")
 
 
 def finish_inner(error, fields, kept, out, scratch):
@@ -839,15 +871,17 @@
         [vmem(nx, HALO, 256)] * 2
         + [pltpu.VMEM((nx, HALO, 256), jnp.int32)] * 2
         + [pltpu.VMEM((1, 256), jnp.int32)] * 2
-        + [pltpu.SemaphoreType.DMA((6,))],
+        + [vmem(7 * nx, 256)] * 2
+        + [vmem(8, 256), pltpu.SemaphoreType.DMA((15,))],
         in_specs=[FAR] * 4,
+        out_specs=[FAR] * 3,
         limit=VMEM_MOST,
         name="first_pack",
     )
     y_a, y_b = swap(pay_a, pay_b, "dev")
     conduct_mid, conduct_coarse, pay_a, pay_b, lists, gain, base = call(
         own_kernel,
-        [shaped(half, half, 256), shaped(quarter, quarter, 256), shaped(24, 8, 256), shaped(24, 8, 256)]
+        [shaped(half, half, 256), shaped(quarter, quarter, 256), shaped(22, 8, 256), shaped(22, 8, 256)]
         + [shaped(2, 256), shaped(nx, nx, 256), shaped(nx, nx, 256)],
         [conc_old, phase_label, phi_old, own_lists],
         [vmem(half, 2, nx, LANES), vmem(quarter, 2, half, LANES)],
@@ -916,7 +950,7 @@
     edge_two, edge_source, source_mid, pay_a, pay_b = call(
         potential_edge_kernel,
         [shaped(*edge), shaped(*edge), shaped(half, half, 256), shaped(4 * half, 256), shaped(4 * half, 256)],
-        [fx_a, fx_b, weight, scale, field, fine_two, fine_source, fine_first, inner_mid],
+        [fx_a, fx_b, weight, scale, field, fine_two, fine_source, fine_first, inner_mid, conduct_mid],
         [vmem(*edge), vmem(2, 2, nx, LANES)],
         name="potential_edge",
     )

time: 84.8 us -> 83.8 us (0.988)
  waiting for transfers between devices: 13.9 us -> 10.5 us
  starting transfers between devices: 44 us -> 46.5 us
    ppermute x10, starting transfers between devices: 20.9 us -> 23.7 us  [swap(): lax.ppermute(pay_a, axis, both_ways(pairs_a))]
    ppermute x10, waiting for transfers between devices: 5.78 us -> 3.42 us  [swap(): lax.ppermute(pay_b, axis, both_ways(pairs_b))]
where the time goes in v12:
time: 83.8 us; the launch traced here: 83.3 us
  starting transfers between devices  46.5 us (55%)
  Pallas kernels  23.3 us (28%)
  waiting for transfers between devices  10.5 us (13%)
  local copies, waits for them, and re-layouts  1.94 us (2%)
  between operations  1.03 us (1%)
    ppermute x10, starting transfers between devices, swap(): lax.ppermute(pay_a, axis, both_ways(pairs_a))  23.7 us
    pallas_call x19, Pallas kernels, call(): pl.pallas_call(kernel, out_shape=tuple(outs), in_specs=in_specs or [WHOLE...  23.3 us
    ppermute x10, starting transfers between devices, swap(): lax.ppermute(pay_b, axis, both_ways(pairs_b))  16.1 us
    ppermute x4, starting transfers between devices, exchange(): lax.ppermute(value, 'dev', [(i, i ^ distance) for i in range(lax.axis_siz...  6.66 us
    ppermute x10, waiting for transfers between devices, swap(): lax.ppermute(pay_a, axis, both_ways(pairs_a))  5.63 us
    ppermute x10, waiting for transfers between devices, swap(): lax.ppermute(pay_b, axis, both_ways(pairs_b))  3.42 us
    unnamed x12, local copies, waits for them, and re-layouts  1.94 us
  transfers between devices with their start and end apart: 24, of which 8 were waited for; matrix products, arithmetic and copies ran while one was open for 0% of the time, Pallas kernels for 18%

profile of v12, /device:TPU:1, one launch (start us, length us, event | category | flops | bytes accessed | tf_op | source)
XLA Modules:
  0.0 83.3 jit_solution(17184829883682160964)
XLA Ops:
  0.7 2.1 %first_pack.1 = (f32[224,256]{1,0:T(8,128)}, f32[224,256]{1,0:T(8,128)}, f32[8,256]{1,0:T(8,128)}) custom-call(f32[32,32,256]{2,1,0:T(8,128)} %conc.9, s32[32,32,256]{2,1,0:T(8,128)} %label.11, s32[1,256]{1,0:T(1,128)} %bitcast.1, s32[1,256]{1,0:T(1,128)} %block.1), custom_call_target="tpu_custom_call" | custom-call | flops 1000000 | bytes 2566144 | tf_op jit(solution)/shard_map/first_pack/pallas_call | solution.py:36
  3.4 4.6 %collective-permute-start.1 = (f32[224,256]{1,0:T(8,128)}, f32[224,256]{1,0:T(8,128)S(1)}, u32[]{:S(2)}, u32[]{:S(2)}) collective-permute-start(f32[224,256]{1,0:T(8,128)} %get-tuple-element.70), channel_id=1, source_target_pairs={{0,1},{2,3},{4,5},{6,7},{1,0},{3,2},{5,4},{7,6},{8,9},{10,11},{12,... | collective-permute-start | bytes 688136 | tf_op jit(solution)/shard_map/ppermute | solution.py:851
  8.0 1.2 %copy-done.2 = f32[32,32,256]{2,1,0:T(8,128)S(1)} copy-done((f32[32,32,256]{2,1,0:T(8,128)S(1)}, f32[32,32,256]{2,1,0:T(8,128)}, u32[]{:S(2)}) %copy-start.2) | copy-done | bytes 1048600
  10.6 2.4 %collective-permute-start.4 = (f32[2,256]{1,0:T(2,128)S(1)}, f32[2,256]{1,0:T(2,128)S(1)}, u32[]{:S(2)}, u32[]{:S(2)}) collective-permute-start(f32[2,256]{1,0:T(2,128)S(1)} %get-tuple-element.75), channel_id=1, source_target_pairs={{0,4},{1,5},{2,6},{3,7},{4,0},{5,1},{6,2},{7,3},{8,12},{9,13},{10,... | collective-permute-start | bytes 6152 | tf_op jit(solution)/shard_map/ppermute | solution.py:855
  13.0 4.5 %collective-permute-start.6 = (f32[22,8,256]{2,1,0:T(8,128)S(1)}, f32[22,8,256]{2,1,0:T(8,128)S(1)}, u32[]{:S(2)}, u32[]{:S(2)}) collective-permute-start(f32[22,8,256]{2,1,0:T(8,128)S(1)} %get-tuple-element.77), channel_id=1, source_target_pairs={{8,16},{16,8},{9,17},{17,9},{10,18},{18,10},{11,19},{19,11},{12,20... | collective-permute-start | bytes 540680 | tf_op jit(solution)/shard_map/ppermute | solution.py:851
  18.2 3.5 %collective-permute-start.2 = (f32[35,8,256]{2,1,0:T(8,128)S(1)}, f32[35,8,256]{2,1,0:T(8,128)S(1)}, u32[]{:S(2)}, u32[]{:S(2)}) collective-permute-start(f32[35,8,256]{2,1,0:T(8,128)S(1)} %get-tuple-element.72), channel_id=1, source_target_pairs={{8,16},{16,8},{9,17},{17,9},{10,18},{18,10},{11,19},{19,11},{12,20... | collective-permute-start | bytes 860168 | tf_op jit(solution)/shard_map/ppermute | solution.py:851
  22.0 2.2 %collective-permute-start.8 = (f32[272,256]{1,0:T(8,128)S(1)}, f32[272,256]{1,0:T(8,128)S(1)}, u32[]{:S(2)}, u32[]{:S(2)}) collective-permute-start(f32[272,256]{1,0:T(8,128)S(1)} %get-tuple-element.79), channel_id=1, source_target_pairs={{0,1},{2,3},{4,5},{6,7},{1,0},{3,2},{5,4},{7,6},{8,9},{10,11},{12,... | collective-permute-start | bytes 835592 | tf_op jit(solution)/shard_map/ppermute | solution.py:851
  24.9 1.6 %collective-permute-done.2.x_a = f32[35,8,256]{2,1,0:T(8,128)S(1)} collective-permute-done((f32[35,8,256]{2,1,0:T(8,128)S(1)}, f32[35,8,256]{2,1,0:T(8,128)S(1)}, u32[]{:S(2)}, u32[]{:S(2)}) %collective-permute-start.2) | collective-permute-done | bytes 286752 | tf_op jit(solution)/shard_map/ppermute | solution.py:851
  26.4 4.7 %sweeps.1.conc = f32[32,32,256]{2,1,0:T(8,128)S(1)} custom-call(f32[32,32,256]{2,1,0:T(8,128)S(1)} %copy-done.1, s32[32,32,256]{2,1,0:T(8,128)S(1)} %copy-done, f32[32,32,256]{2,1,0:T(8,128)S(1)} %get-tuple-element.67.gain_own, f32[32,32,256]{2,1,0:T(8,128)S(1)} %get-tuple-element.68.base_own, f32[224,256]{1,0:T(8,128)S(1)} %collective-permute-done.r_a.y_a, ...), custom_call_target="tpu_custom_call" | custom-call | flops 1000000 | bytes 6275072 | tf_op jit(solution)/shard_map/sweeps/pallas_call | solution.py:36
  31.1 0.8 flux.1
  31.9 2.2 %collective-permute-start.10 = (f32[96,256]{1,0:T(8,128)S(1)}, f32[96,256]{1,0:T(8,128)S(1)}, u32[]{:S(2)}, u32[]{:S(2)}) collective-permute-start(f32[96,256]{1,0:T(8,128)S(1)} %get-tuple-element.84), channel_id=1, source_target_pairs={{0,1},{2,3},{4,5},{6,7},{1,0},{3,2},{5,4},{7,6},{8,9},{10,11},{12,... | collective-permute-start | bytes 294920 | tf_op jit(solution)/shard_map/ppermute | solution.py:851
  34.8 0.8 ready.1
  35.6 0.8 %mask.1 = (f32[32,32,256]{2,1,0:T(8,128)S(1)}, f32[32,8,256]{2,1,0:T(8,128)S(1)}) custom-call(f32[32,32,256]{2,1,0:T(8,128)S(1)} %get-tuple-element.74.flux_all, f32[8,256]{1,0:T(8,128)S(1)} %pad_maximum_fusion.lists, f32[272,256]{1,0:T(8,128)S(1)} %collective-permute-done.8.far.yy_b.r_b.far_b), custom_call_target="tpu_custom_call" | custom-call | flops 1000000 | bytes 2646016 | tf_op jit(solution)/shard_map/mask/pallas_call | solution.py:36
  36.4 1.2 %collective-permute-done.10.r_b.y_b = f32[96,256]{1,0:T(8,128)S(1)} collective-permute-done((f32[96,256]{1,0:T(8,128)S(1)}, f32[96,256]{1,0:T(8,128)S(1)}, u32[]{:S(2)}, u32[]{:S(2)}) %collective-permute-start.10) | collective-permute-done | bytes 98336 | tf_op jit(solution)/shard_map/ppermute | solution.py:851
  37.7 5.5 %collective-permute-start.11 = (f32[15,8,256]{2,1,0:T(8,128)S(1)}, f32[15,8,256]{2,1,0:T(8,128)S(1)}, u32[]{:S(2)}, u32[]{:S(2)}) collective-permute-start(f32[15,8,256]{2,1,0:T(8,128)S(1)} %get-tuple-element.87), channel_id=1, source_target_pairs={{8,16},{16,8},{9,17},{17,9},{10,18},{18,10},{11,19},{19,11},{12,20... | collective-permute-start | bytes 368648 | tf_op jit(solution)/shard_map/ppermute | solution.py:851
  43.2 3.3 %potential_inner.1 = (f32[40,40,256]{2,1,0:T(8,128)S(1)}, f32[40,40,256]{2,1,0:T(8,128)S(1)}, f32[40,40,256]{2,1,0:T(8,128)S(1)}, f32[16,16,256]{2,1,0:T(8,128)S(1)}, f32[40,40,256]{2,1,0:T(8,128)S(1)}) custom-call(f32[32,32,256]{2,1,0:T(8,128)S(1)} %get-tuple-element.80.flux, f32[32,8,256]{2,1,0:T(8,128)S(1)} %get-tuple-element.85.mask, ...), custom_call_target="tpu_custom_call" | custom-call | flops 1000000 | bytes 13557760 | tf_op jit(solution)/shard_map/potential_inner/pallas_call | solution.py:36
  47.9 5.7 %collective-permute-start.15 = (f32[64,256]{1,0:T(8,128)S(1)}, f32[64,256]{1,0:T(8,128)S(1)}, u32[]{:S(2)}, u32[]{:S(2)}) collective-permute-start(f32[64,256]{1,0:T(8,128)S(1)} %get-tuple-element.99), channel_id=1, source_target_pairs={{0,1},{2,3},{4,5},{6,7},{1,0},{3,2},{5,4},{7,6},{8,9},{10,11},{12,... | collective-permute-start | bytes 196616 | tf_op jit(solution)/shard_map/ppermute | solution.py:851
  53.6 1.2 %coarse_ready.1 = (f32[8,8,256]{2,1,0:T(8,128)S(1)}, f32[8,128]{1,0:T(8,128)S(1)}, f32[8,128]{1,0:T(8,128)S(1)}) custom-call(f32[8,8,256]{2,1,0:T(8,128)S(1)} %get-tuple-element.71.token.coarse.own, f32[264,256]{1,0:T(8,128)S(1)} %collective-permute-done.13.yy_a.r_a.far_a, f32[272,256]{1,0:T(8,128)S(1)} %collective-permute-done.8.far.yy_b.r_b.far_b), custom_call_target="tpu_custom_call" | custom-call | flops 1000000 | bytes 688128 | tf_op jit(solution)/shard_map/coarse_ready/pallas_call | solution.py:36
  54.8 1.4 %store.1 = (f32[32,32,256]{2,1,0:T(8,128)}, f32[32,32,256]{2,1,0:T(8,128)}, f32[8,128]{1,0:T(8,128)S(1)}) custom-call(f32[32,32,256]{2,1,0:T(8,128)S(1)} %sweeps.1.conc, f32[32,32,256]{2,1,0:T(8,128)S(1)} %get-tuple-element.80.flux), custom_call_target="tpu_custom_call" | custom-call | flops 1000000 | bytes 4198400 | tf_op jit(solution)/shard_map/store/pallas_call | solution.py:36
  56.3 3.3 %collective-permute-start.16 = (f32[12,8,256]{2,1,0:T(8,128)S(1)}, f32[12,8,256]{2,1,0:T(8,128)S(1)}, u32[]{:S(2)}, u32[]{:S(2)}) collective-permute-start(f32[12,8,256]{2,1,0:T(8,128)S(1)} %get-tuple-element.102), channel_id=1, source_target_pairs={{8,16},{16,8},{9,17},{17,9},{10,18},{18,10},{11,19},{19,11},{12,20... | collective-permute-start | bytes 294920 | tf_op jit(solution)/shard_map/ppermute | solution.py:851
  59.6 2.5 %collective-permute-done.16.x_a = f32[12,8,256]{2,1,0:T(8,128)S(1)} collective-permute-done((f32[12,8,256]{2,1,0:T(8,128)S(1)}, f32[12,8,256]{2,1,0:T(8,128)S(1)}, u32[]{:S(2)}, u32[]{:S(2)}) %collective-permute-start.16) | collective-permute-done | bytes 98336 | tf_op jit(solution)/shard_map/ppermute | solution.py:851
  62.2 1.1 %middle.1 = (f32[24,24,256]{2,1,0:T(8,128)S(1)}, f32[24,24,256]{2,1,0:T(8,128)S(1)}, f32[24,24,256]{2,1,0:T(8,128)S(1)}, f32[8,12,256]{2,1,0:T(8,128)S(1)}, f32[...) custom-call(f32[16,16,256]{2,1,0:T(8,128)S(1)} %get-tuple-element.97.field.source_o, ...), custom_call_target="tpu_custom_call" | custom-call | flops 1000000 | bytes 3960832 | tf_op jit(solution)/shard_map/middle/pallas_call | solution.py:36
  63.3 1.1 %collective-permute-start.19 = (f32[80,256]{1,0:T(8,128)S(1)}, f32[80,256]{1,0:T(8,128)S(1)}, u32[]{:S(2)}, u32[]{:S(2)}) collective-permute-start(f32[80,256]{1,0:T(8,128)S(1)} %get-tuple-element.109), channel_id=1, source_target_pairs={{0,1},{2,3},{4,5},{6,7},{1,0},{3,2},{5,4},{7,6},{8,9},{10,11},{12,... | collective-permute-start | bytes 245768 | tf_op jit(solution)/shard_map/ppermute | solution.py:851
  65.0 1.8 %collective-permute-done.19.r_b = f32[80,256]{1,0:T(8,128)S(1)} collective-permute-done((f32[80,256]{1,0:T(8,128)S(1)}, f32[80,256]{1,0:T(8,128)S(1)}, u32[]{:S(2)}, u32[]{:S(2)}) %collective-permute-start.19) | collective-permute-done | bytes 81952 | tf_op jit(solution)/shard_map/ppermute | solution.py:851
  66.8 2.0 %collective-permute-start.20 = (f32[8,256]{1,0:T(8,128)S(1)}, f32[8,256]{1,0:T(8,128)S(1)}, u32[]{:S(2)}, u32[]{:S(2)}) collective-permute-start(f32[8,256]{1,0:T(8,128)S(1)} %slice_add_fusion), channel_id=1, source_target_pairs={{0,2},{1,3},{2,0},{3,1},{4,6},{5,7},{6,4},{7,5},{8,10},{9,11},{10,... | collective-permute-start | bytes 24584 | tf_op jit(solution)/shard_map/ppermute | solution.py:855
  68.9 1.4 %collective-permute-done.20 = f32[8,256]{1,0:T(8,128)S(1)} collective-permute-done((f32[8,256]{1,0:T(8,128)S(1)}, f32[8,256]{1,0:T(8,128)S(1)}, u32[]{:S(2)}, u32[]{:S(2)}) %collective-permute-start.20) | collective-permute-done | bytes 8224 | tf_op jit(solution)/shard_map/ppermute | solution.py:855
  70.3 2.2 %collective-permute-start.21 = (f32[8,256]{1,0:T(8,128)S(1)}, f32[8,256]{1,0:T(8,128)S(1)}, u32[]{:S(2)}, u32[]{:S(2)}) collective-permute-start(f32[8,256]{1,0:T(8,128)S(1)} %add.10), channel_id=1, source_target_pairs={{0,4},{1,5},{2,6},{3,7},{4,0},{5,1},{6,2},{7,3},{8,12},{9,13},{10,... | collective-permute-start | bytes 24584 | tf_op jit(solution)/shard_map/ppermute | solution.py:855
  72.5 1.2 %coarse.1.error = f32[8,16,256]{2,1,0:T(8,128)S(1)} custom-call(f32[8,12,256]{2,1,0:T(8,128)S(1)} %get-tuple-element.106.own, f32[8,12,256]{2,1,0:T(8,128)S(1)} %get-tuple-element.107.conduct, f32[264,256]{1,0:T(8,128)S(1)} %collective-permute-done.13.yy_a.r_a.far_a, f32[272,256]{1,0:T(8,128)S(1)} %collective-permute-done.8.far.yy_b.r_b.far_b, ...), custom_call_target="tpu_custom_call" | custom-call | flops 1000000 | bytes 1032192 | tf_op jit(solution)/shard_map/coarse/pallas_call | solution.py:36
  73.7 2.7 %finish_early.1 = (f32[8,16,256]{2,1,0:T(8,128)S(1)}, f32[2,16,256]{2,1,0:T(8,128)S(1)}, f32[2,16,256]{2,1,0:T(8,128)S(1)}, f32[32,32,256]{2,1,0:T(8,128)}, f32[...) custom-call(f32[8,16,256]{2,1,0:T(8,128)S(1)} %coarse.1.error, ...), custom_call_target="tpu_custom_call" | custom-call | flops 1000000 | bytes 8593408 | tf_op jit(solution)/shard_map/finish_early/pallas_call | solution.py:36
  76.4 3.6 %collective-permute-start.22 = (f32[2,16,256]{2,1,0:T(8,128)S(1)}, f32[2,16,256]{2,1,0:T(8,128)S(1)}, u32[]{:S(2)}, u32[]{:S(2)}) collective-permute-start(f32[2,16,256]{2,1,0:T(8,128)S(1)} %get-tuple-element.114), channel_id=1, source_target_pairs={{8,16},{16,8},{9,17},{17,9},{10,18},{18,10},{11,19},{19,11},{12,20... | collective-permute-start | bytes 98312 | tf_op jit(solution)/shard_map/ppermute | solution.py:851
  80.2 1.5 %collective-permute-done.22.x_a = f32[2,16,256]{2,1,0:T(8,128)S(1)} collective-permute-done((f32[2,16,256]{2,1,0:T(8,128)S(1)}, f32[2,16,256]{2,1,0:T(8,128)S(1)}, u32[]{:S(2)}, u32[]{:S(2)}) %collective-permute-start.22) | collective-permute-done | bytes 32800 | tf_op jit(solution)/shard_map/ppermute | solution.py:851
  81.7 1.7 %finish_edge.1 = f32[32,32,256]{2,1,0:T(8,128)} custom-call(f32[2,16,256]{2,1,0:T(8,128)S(1)} %collective-permute-done.22.x_a, f32[2,16,256]{2,1,0:T(8,128)S(1)} %collective-permute-done.23.x_b, f32[24,24,256]{2,1,0:T(8,128)S(1)} %get-tuple-element.111.rest_0_.mid_two, ...), custom_call_target="tpu_custom_call", output_to_operand_aliasing={{}: (14, {})} | custom-call | flops 1000000 | bytes 10682368 | tf_op jit(solution)/shard_map/finish_edge/pallas_call | solution.py:36
  (52 shorter events, 6.6 us)
Async XLA Ops:
  0.6 7.4 %copy-start.1 = (f32[32,32,256]{2,1,0:T(8,128)S(1)}, f32[32,32,256]{2,1,0:T(8,128)}, u32[]{:S(2)}) copy-start(f32[32,32,256]{2,1,0:T(8,128)} %conc.9) | copy-start | bytes 3145732
  0.6 7.4 %copy-start = (s32[32,32,256]{2,1,0:T(8,128)S(1)}, s32[32,32,256]{2,1,0:T(8,128)}, u32[]{:S(2)}) copy-start(s32[32,32,256]{2,1,0:T(8,128)} %label.11) | copy-start | bytes 3145732
  2.7 15.0 %collective-permute-start = (f32[224,256]{1,0:T(8,128)}, f32[224,256]{1,0:T(8,128)S(1)}, u32[]{:S(2)}, u32[]{:S(2)}) collective-permute-start(f32[224,256]{1,0:T(8,128)} %get-tuple-element.69), channel_id=1, source_target_pairs={{1,2},{3,4},{5,6},{2,1},{4,3},{6,5},{9,10},{11,12},{13,14},{10,9},... | collective-permute-start | bytes 688136 | tf_op jit(solution)/shard_map/ppermute | solution.py:851
  3.4 14.7 %collective-permute-start.1 = (f32[224,256]{1,0:T(8,128)}, f32[224,256]{1,0:T(8,128)S(1)}, u32[]{:S(2)}, u32[]{:S(2)}) collective-permute-start(f32[224,256]{1,0:T(8,128)} %get-tuple-element.70), channel_id=1, source_target_pairs={{0,1},{2,3},{4,5},{6,7},{1,0},{3,2},{5,4},{7,6},{8,9},{10,11},{12,... | collective-permute-start | bytes 688136 | tf_op jit(solution)/shard_map/ppermute | solution.py:851
  8.0 1.2 %copy-start.2 = (f32[32,32,256]{2,1,0:T(8,128)S(1)}, f32[32,32,256]{2,1,0:T(8,128)}, u32[]{:S(2)}) copy-start(f32[32,32,256]{2,1,0:T(8,128)} %phi.7) | copy-start | bytes 3145732
  9.2 0.7 copy-start.5
  10.6 11.3 %copy-start.3 = (f32[32,32,256]{2,1,0:T(8,128)S(1)}, f32[32,32,256]{2,1,0:T(8,128)}, u32[]{:S(2)}) copy-start(f32[32,32,256]{2,1,0:T(8,128)} %phi.7) | copy-start | bytes 3145732
  10.6 7.0 %collective-permute-start.4 = (f32[2,256]{1,0:T(2,128)S(1)}, f32[2,256]{1,0:T(2,128)S(1)}, u32[]{:S(2)}, u32[]{:S(2)}) collective-permute-start(f32[2,256]{1,0:T(2,128)S(1)} %get-tuple-element.75), channel_id=1, source_target_pairs={{0,4},{1,5},{2,6},{3,7},{4,0},{5,1},{6,2},{7,3},{8,12},{9,13},{10,... | collective-permute-start | bytes 6152 | tf_op jit(solution)/shard_map/ppermute | solution.py:855
  13.0 8.9 %collective-permute-start.6 = (f32[22,8,256]{2,1,0:T(8,128)S(1)}, f32[22,8,256]{2,1,0:T(8,128)S(1)}, u32[]{:S(2)}, u32[]{:S(2)}) collective-permute-start(f32[22,8,256]{2,1,0:T(8,128)S(1)} %get-tuple-element.77), channel_id=1, source_target_pairs={{8,16},{16,8},{9,17},{17,9},{10,18},{18,10},{11,19},{19,11},{12,20... | collective-permute-start | bytes 540680 | tf_op jit(solution)/shard_map/ppermute | solution.py:851
  17.5 4.3 %collective-permute-start.7 = (f32[22,8,256]{2,1,0:T(8,128)S(1)}, f32[22,8,256]{2,1,0:T(8,128)S(1)}, u32[]{:S(2)}, u32[]{:S(2)}) collective-permute-start(f32[22,8,256]{2,1,0:T(8,128)S(1)} %get-tuple-element.78), channel_id=1, source_target_pairs={{0,8},{16,24},{8,0},{24,16},{1,9},{17,25},{9,1},{25,17},{2,10},{18... | collective-permute-start | bytes 540680 | tf_op jit(solution)/shard_map/ppermute | solution.py:851
  17.6 4.2 %collective-permute-start.5 = (f32[4,256]{1,0:T(4,128)S(1)}, f32[4,256]{1,0:T(4,128)S(1)}, u32[]{:S(2)}, u32[]{:S(2)}) collective-permute-start(f32[4,256]{1,0:T(4,128)S(1)} %pad_maximum_fusion.1), channel_id=1, source_target_pairs={{0,2},{1,3},{2,0},{3,1},{4,6},{5,7},{6,4},{7,5},{8,10},{9,11},{10,... | collective-permute-start | bytes 12296 | tf_op jit(solution)/shard_map/ppermute | solution.py:855
  18.2 8.2 %collective-permute-start.2 = (f32[35,8,256]{2,1,0:T(8,128)S(1)}, f32[35,8,256]{2,1,0:T(8,128)S(1)}, u32[]{:S(2)}, u32[]{:S(2)}) collective-permute-start(f32[35,8,256]{2,1,0:T(8,128)S(1)} %get-tuple-element.72), channel_id=1, source_target_pairs={{8,16},{16,8},{9,17},{17,9},{10,18},{18,10},{11,19},{19,11},{12,20... | collective-permute-start | bytes 860168 | tf_op jit(solution)/shard_map/ppermute | solution.py:851
  21.7 4.7 %collective-permute-start.3 = (f32[35,8,256]{2,1,0:T(8,128)S(1)}, f32[35,8,256]{2,1,0:T(8,128)S(1)}, u32[]{:S(2)}, u32[]{:S(2)}) collective-permute-start(f32[35,8,256]{2,1,0:T(8,128)S(1)} %get-tuple-element.73), channel_id=1, source_target_pairs={{0,8},{16,24},{8,0},{24,16},{1,9},{17,25},{9,1},{25,17},{2,10},{18... | collective-permute-start | bytes 860168 | tf_op jit(solution)/shard_map/ppermute | solution.py:851
  22.0 13.6 %collective-permute-start.8 = (f32[272,256]{1,0:T(8,128)S(1)}, f32[272,256]{1,0:T(8,128)S(1)}, u32[]{:S(2)}, u32[]{:S(2)}) collective-permute-start(f32[272,256]{1,0:T(8,128)S(1)} %get-tuple-element.79), channel_id=1, source_target_pairs={{0,1},{2,3},{4,5},{6,7},{1,0},{3,2},{5,4},{7,6},{8,9},{10,11},{12,... | collective-permute-start | bytes 835592 | tf_op jit(solution)/shard_map/ppermute | solution.py:851
  24.2 19.1 %collective-permute-start.13 = (f32[264,256]{1,0:T(8,128)S(1)}, f32[264,256]{1,0:T(8,128)S(1)}, u32[]{:S(2)}, u32[]{:S(2)}) collective-permute-start(f32[264,256]{1,0:T(8,128)S(1)} %get-tuple-element.91), channel_id=1, source_target_pairs={{1,2},{3,4},{5,6},{2,1},{4,3},{6,5},{9,10},{11,12},{13,14},{10,9},... | collective-permute-start | bytes 811016 | tf_op jit(solution)/shard_map/ppermute | solution.py:851
  26.4 4.7 %copy-start.4 = (f32[32,32,256]{2,1,0:T(8,128)S(1)}, f32[32,32,256]{2,1,0:T(8,128)}, u32[]{:S(2)}) copy-start(f32[32,32,256]{2,1,0:T(8,128)} %solid.1) | copy-start | bytes 3145732
  31.9 5.7 %collective-permute-start.10 = (f32[96,256]{1,0:T(8,128)S(1)}, f32[96,256]{1,0:T(8,128)S(1)}, u32[]{:S(2)}, u32[]{:S(2)}) collective-permute-start(f32[96,256]{1,0:T(8,128)S(1)} %get-tuple-element.84), channel_id=1, source_target_pairs={{0,1},{2,3},{4,5},{6,7},{1,0},{3,2},{5,4},{7,6},{8,9},{10,11},{12,... | collective-permute-start | bytes 294920 | tf_op jit(solution)/shard_map/ppermute | solution.py:851
  34.2 3.5 %collective-permute-start.9 = (f32[96,256]{1,0:T(8,128)S(1)}, f32[96,256]{1,0:T(8,128)S(1)}, u32[]{:S(2)}, u32[]{:S(2)}) collective-permute-start(f32[96,256]{1,0:T(8,128)S(1)} %get-tuple-element.83), channel_id=1, source_target_pairs={{1,2},{3,4},{5,6},{2,1},{4,3},{6,5},{9,10},{11,12},{13,14},{10,9},... | collective-permute-start | bytes 294920 | tf_op jit(solution)/shard_map/ppermute | solution.py:851
  37.7 8.9 %collective-permute-start.11 = (f32[15,8,256]{2,1,0:T(8,128)S(1)}, f32[15,8,256]{2,1,0:T(8,128)S(1)}, u32[]{:S(2)}, u32[]{:S(2)}) collective-permute-start(f32[15,8,256]{2,1,0:T(8,128)S(1)} %get-tuple-element.87), channel_id=1, source_target_pairs={{8,16},{16,8},{9,17},{17,9},{10,18},{18,10},{11,19},{19,11},{12,20... | collective-permute-start | bytes 368648 | tf_op jit(solution)/shard_map/ppermute | solution.py:851
  43.2 3.4 %collective-permute-start.12 = (f32[15,8,256]{2,1,0:T(8,128)S(1)}, f32[15,8,256]{2,1,0:T(8,128)S(1)}, u32[]{:S(2)}, u32[]{:S(2)}) collective-permute-start(f32[15,8,256]{2,1,0:T(8,128)S(1)} %get-tuple-element.88), channel_id=1, source_target_pairs={{0,8},{16,24},{8,0},{24,16},{1,9},{17,25},{9,1},{25,17},{2,10},{18... | collective-permute-start | bytes 368648 | tf_op jit(solution)/shard_map/ppermute | solution.py:851
  47.2 8.9 %collective-permute-start.14 = (f32[64,256]{1,0:T(8,128)S(1)}, f32[64,256]{1,0:T(8,128)S(1)}, u32[]{:S(2)}, u32[]{:S(2)}) collective-permute-start(f32[64,256]{1,0:T(8,128)S(1)} %get-tuple-element.98), channel_id=1, source_target_pairs={{1,2},{3,4},{5,6},{2,1},{4,3},{6,5},{9,10},{11,12},{13,14},{10,9},... | collective-permute-start | bytes 196616 | tf_op jit(solution)/shard_map/ppermute | solution.py:851
  47.9 8.3 %collective-permute-start.15 = (f32[64,256]{1,0:T(8,128)S(1)}, f32[64,256]{1,0:T(8,128)S(1)}, u32[]{:S(2)}, u32[]{:S(2)}) collective-permute-start(f32[64,256]{1,0:T(8,128)S(1)} %get-tuple-element.99), channel_id=1, source_target_pairs={{0,1},{2,3},{4,5},{6,7},{1,0},{3,2},{5,4},{7,6},{8,9},{10,11},{12,... | collective-permute-start | bytes 196616 | tf_op jit(solution)/shard_map/ppermute | solution.py:851
  56.3 5.9 %collective-permute-start.16 = (f32[12,8,256]{2,1,0:T(8,128)S(1)}, f32[12,8,256]{2,1,0:T(8,128)S(1)}, u32[]{:S(2)}, u32[]{:S(2)}) collective-permute-start(f32[12,8,256]{2,1,0:T(8,128)S(1)} %get-tuple-element.102), channel_id=1, source_target_pairs={{8,16},{16,8},{9,17},{17,9},{10,18},{18,10},{11,19},{19,11},{12,20... | collective-permute-start | bytes 294920 | tf_op jit(solution)/shard_map/ppermute | solution.py:851
  59.6 2.6 %collective-permute-start.17 = (f32[12,8,256]{2,1,0:T(8,128)S(1)}, f32[12,8,256]{2,1,0:T(8,128)S(1)}, u32[]{:S(2)}, u32[]{:S(2)}) collective-permute-start(f32[12,8,256]{2,1,0:T(8,128)S(1)} %get-tuple-element.103), channel_id=1, source_target_pairs={{0,8},{16,24},{8,0},{24,16},{1,9},{17,25},{9,1},{25,17},{2,10},{18... | collective-permute-start | bytes 294920 | tf_op jit(solution)/shard_map/ppermute | solution.py:851
  63.3 3.6 %collective-permute-start.19 = (f32[80,256]{1,0:T(8,128)S(1)}, f32[80,256]{1,0:T(8,128)S(1)}, u32[]{:S(2)}, u32[]{:S(2)}) collective-permute-start(f32[80,256]{1,0:T(8,128)S(1)} %get-tuple-element.109), channel_id=1, source_target_pairs={{0,1},{2,3},{4,5},{6,7},{1,0},{3,2},{5,4},{7,6},{8,9},{10,11},{12,... | collective-permute-start | bytes 245768 | tf_op jit(solution)/shard_map/ppermute | solution.py:851
  64.4 8.1 %collective-permute-start.18 = (f32[72,256]{1,0:T(8,128)S(1)}, f32[72,256]{1,0:T(8,128)S(1)}, u32[]{:S(2)}, u32[]{:S(2)}) collective-permute-start(f32[72,256]{1,0:T(8,128)S(1)} %get-tuple-element.108), channel_id=1, source_target_pairs={{1,2},{3,4},{5,6},{2,1},{4,3},{6,5},{9,10},{11,12},{13,14},{10,9},... | collective-permute-start | bytes 221192 | tf_op jit(solution)/shard_map/ppermute | solution.py:851
  66.8 3.4 %collective-permute-start.20 = (f32[8,256]{1,0:T(8,128)S(1)}, f32[8,256]{1,0:T(8,128)S(1)}, u32[]{:S(2)}, u32[]{:S(2)}) collective-permute-start(f32[8,256]{1,0:T(8,128)S(1)} %slice_add_fusion), channel_id=1, source_target_pairs={{0,2},{1,3},{2,0},{3,1},{4,6},{5,7},{6,4},{7,5},{8,10},{9,11},{10,... | collective-permute-start | bytes 24584 | tf_op jit(solution)/shard_map/ppermute | solution.py:855
  70.3 3.4 %collective-permute-start.21 = (f32[8,256]{1,0:T(8,128)S(1)}, f32[8,256]{1,0:T(8,128)S(1)}, u32[]{:S(2)}, u32[]{:S(2)}) collective-permute-start(f32[8,256]{1,0:T(8,128)S(1)} %add.10), channel_id=1, source_target_pairs={{0,4},{1,5},{2,6},{3,7},{4,0},{5,1},{6,2},{7,3},{8,12},{9,13},{10,... | collective-permute-start | bytes 24584 | tf_op jit(solution)/shard_map/ppermute | solution.py:855
  76.4 5.2 %collective-permute-start.22 = (f32[2,16,256]{2,1,0:T(8,128)S(1)}, f32[2,16,256]{2,1,0:T(8,128)S(1)}, u32[]{:S(2)}, u32[]{:S(2)}) collective-permute-start(f32[2,16,256]{2,1,0:T(8,128)S(1)} %get-tuple-element.114), channel_id=1, source_target_pairs={{8,16},{16,8},{9,17},{17,9},{10,18},{18,10},{11,19},{19,11},{12,20... | collective-permute-start | bytes 98312 | tf_op jit(solution)/shard_map/ppermute | solution.py:851
  80.0 1.6 %collective-permute-start.23 = (f32[2,16,256]{2,1,0:T(8,128)S(1)}, f32[2,16,256]{2,1,0:T(8,128)S(1)}, u32[]{:S(2)}, u32[]{:S(2)}) collective-permute-start(f32[2,16,256]{2,1,0:T(8,128)S(1)} %get-tuple-element.115), channel_id=1, source_target_pairs={{0,8},{16,24},{8,0},{24,16},{1,9},{17,25},{9,1},{25,17},{2,10},{18... | collective-permute-start | bytes 98312 | tf_op jit(solution)/shard_map/ppermute | solution.py:851

commit v13 on v12

--- a/solution.py
+++ b/solution.py
@@ -121,6 +121,12 @@
 def y_sides(r_a, r_b, at, count):
     flag = odd("dev")
     a, b = r_a[at : at + count, :], r_b[at : at + count, :]
+    return either(flag, a, b), either(flag, b, a)
+
+
+def y_planes(r_a, r_b, index):
+    flag = odd("dev")
+    a, b = r_a[index], r_b[index]
     return either(flag, a, b), either(flag, b, a)
 
 
@@ -241,10 +247,10 @@
 def second_rows(nx):
     phi = sum(corner_rows(nx, HALO, 0)[0])
     mid = sum(corner_rows(nx // 2, MID_HALO, 1)[0])
-    return phi, phi + mid, phi + mid + 64
-
-
-def second_pack_kernel(phi, mid, coarse, lists, x_a, x_b, pay_a, pay_b):
+    return phi, phi + mid
+
+
+def second_pack_kernel(phi, mid, lists, x_a, x_b, pay_a, pay_b):
     nx = phi.shape[0]
     starts = second_rows(nx)
 
@@ -264,10 +270,6 @@
     put(phi, HALO, 0, 0, 0)
     put(mid, MID_HALO, 1, 16, starts[0])
     base = starts[1]
-    for x in range(8):
-        pay_a[base + 8 * x : base + 8 * x + 8, :] = coarse[x]
-        pay_b[base + 8 * x : base + 8 * x + 8, :] = coarse[x]
-    base = starts[2]
     pay_b[base : base + lists.shape[0], :] = lists[...]
 
 
@@ -284,76 +286,98 @@
     return jnp.concatenate([own, after_own, after, gap, before, before_own], axis=0)
 
 
-def sweeps_kernel(conc, label, gain_own, base_own, y_a, y_b, x_a, x_b, out, one, two, gain_far, base_far, gain_x, base_x):
+def flux_plane(c, solid, phi, label):
+    drive = 0.5 * (solid - phi)
+    logc = jnp.log(c)
+    return pick(label, KINETIC_TABLE) * (jnp.exp(drive + 0.4 * logc) - jnp.exp(0.6 * logc - drive))
+
+
+def around_plane(before, v, after):
+    return (before + after) + (along_y(v) + along_z(v))
+
+
+def sweeps_inner_kernel(
+    conc, label, phi, solid, gain, base, y_a, y_b, zero, first, second, third, gain_far, base_far, out, flux
+):
     nx = conc.shape[0]
 
     def own(i):
-        one[HALO + i, 0:32, :] = conc[i]
+        zero[i, 0:32, :] = conc[i]
 
     loop(0, nx, own)
     for i in range(nx):
         c = halo_tile(*y_sides(y_a, y_b, 7 * i, 4))
         lab = halo_tile(*y_sides(y_a, y_b, 7 * i + 4, 3))
-        one[HALO + i, 32:40, :] = c
+        zero[i, 32:40, :] = c
         gain_far[i] = jnp.where(c > 0.0, pick(lab, RATIO_TABLE), 0.0)
         base_far[i] = c * pick(lab, INVERSE_TABLE)
-
-    def put(x, rows, c, lab):
-        one[x, rows, :] = c
-        at = x if x < HALO else x - nx
-        gain_x[at, rows, :] = jnp.where(c > 0.0, pick(lab, RATIO_TABLE), 0.0)
-        base_x[at, rows, :] = c * pick(lab, INVERSE_TABLE)
-
-    for t in range(5):
-        rows = slice(8 * t, 8 * t + 8)
-        for k in range(HALO):
-            c_after, c_before = x_sides(x_a, x_b, 5 * k + t)
-            l_after = x_sides(x_a, x_b, 20 + 5 * min(k, 2) + t)[0]
-            l_before = x_sides(x_a, x_b, 20 + 5 * max(k - 1, 0) + t)[1]
-            put(k, rows, c_before, l_before)
-            put(HALO + nx + k, rows, c_after, l_after)
-
-    def neighbours(old, x):
-        mid = old[x]
-        return (old[x - 1] + old[x + 1]) + (along_y(mid) + along_z(mid))
-
-    fields = (one, two)
+    fields = (zero, first, second, third)
     for s in range(1, SWEEPS):
-        old, new = fields[(s - 1) % 2], fields[s % 2]
+        old, new = fields[s - 1], fields[s]
 
         def sweep(i, old=old, new=new):
-            gain = jnp.concatenate([gain_own[i], gain_far[i]], axis=0)
-            base = jnp.concatenate([base_own[i], base_far[i]], axis=0)
-            new[HALO + i] = base + gain * neighbours(old, HALO + i)
-
-        loop(0, nx, sweep)
-        for k in range(s, HALO):
-            for x, at in ((k, k), (2 * HALO + nx - 1 - k, 2 * HALO - 1 - k)):
-                new[x] = base_x[at] + gain_x[at] * neighbours(old, x)
-
-    old = fields[(SWEEPS - 1) % 2]
+            g = jnp.concatenate([gain[i], gain_far[i]], axis=0)
+            b = jnp.concatenate([base[i], base_far[i]], axis=0)
+            new[i] = b + g * around_plane(old[i - 1], old[i], old[i + 1])
+
+        loop(s, nx - s, sweep)
 
     def last(i):
-        out[i] = base_own[i] + gain_own[i] * neighbours(old, HALO + i)[0:32, :]
-
-    loop(0, nx, last)
-
-
-def flux_kernel(conc, label, phi, solid, flux, pay_a, pay_b):
-    nx = conc.shape[0]
-
-    def plane(i):
-        drive = 0.5 * (solid[i] - phi[i])
-        logc = jnp.log(conc[i])
-        value = jnp.exp(drive + 0.4 * logc) - jnp.exp(0.6 * logc - drive)
-        flux[i] = pick(label[i], KINETIC_TABLE) * value
-
-    loop(0, nx, plane, 4)
+        c = base[i] + gain[i] * around_plane(third[i - 1], third[i], third[i + 1])[0:32, :]
+        out[i] = c
+        flux[i] = flux_plane(c, solid[i], phi[i], label[i])
+
+    loop(SWEEPS, nx - SWEEPS, last, 4)
+
+
+def sweeps_edge_kernel(
+    x_a, x_b, label, phi, solid, gain, base, zero, first, second, third, gain_far, base_far, out_inner, flux_inner,
+    out, flux, pay_a, pay_b, zero_x, first_x, second_x, third_x,
+):
+    nx = out.shape[0]
+    inner = (zero, first, second, third)
+    edge = (zero_x, first_x, second_x, third_x)
+
+    def copy(i):
+        out[i] = out_inner[i]
+        flux[i] = flux_inner[i]
+
+    loop(SWEEPS, nx - SWEEPS, copy)
+    for side in range(2):
+        plane = lambda k, side=side: k if side == 0 else nx - 1 - k
+        row = lambda k, side=side: 8 * side + HALO + k
+        far = lambda k, index, side=side: x_sides(x_a, x_b, index)[1 - side]
+        gains, bases = {}, {}
+        for j in range(1, HALO + 1):
+            k = HALO - j if side == 0 else j - 1
+            zero_x[row(-j)] = jnp.concatenate([far(k, 5 * k + t) for t in range(5)], axis=0)
+            if j < HALO:
+                k = HALO - 1 - j if side == 0 else j - 1
+                lab = jnp.concatenate([far(k, 20 + 5 * k + t) for t in range(5)], axis=0)
+                c = zero_x[row(-j)]
+                gains[-j] = jnp.where(c > 0.0, pick(lab, RATIO_TABLE), 0.0)
+                bases[-j] = c * pick(lab, INVERSE_TABLE)
+        for k in range(SWEEPS):
+            gains[k] = jnp.concatenate([gain[plane(k)], gain_far[plane(k)]], axis=0)
+            bases[k] = jnp.concatenate([base[plane(k)], base_far[plane(k)]], axis=0)
+        for s in range(1, SWEEPS + 1):
+
+            def old(k, s=s):
+                return inner[s - 1][plane(k)] if k >= s - 1 else edge[s - 1][row(k)]
+
+            for k in range(s - SWEEPS, s):
+                c = bases[k] + gains[k] * around_plane(old(k - 1), old(k), old(k + 1))
+                if s < SWEEPS:
+                    edge[s][row(k)] = c
+                else:
+                    c = c[0:32, :]
+                    out[plane(k)] = c
+                    flux[plane(k)] = flux_plane(c, solid[plane(k)], phi[plane(k)], label[plane(k)])
     for x in range(nx):
         send_y(pay_a, pay_b, 3 * x, flux[x, 0:3, :], flux[x, 29:32, :])
 
 
-def mask_kernel(flux_all, lists, far, flux, halo_mask, marked):
+def mask_kernel(flux_all, lists, far, token, flux, halo_mask, marked):
     nx = flux_all.shape[0]
     rows = lists.shape[0]
     pieces = [lists[i : i + 1, :] for i in range(rows)] + [far[i : i + 1, :] for i in range(far.shape[0] - rows, far.shape[0])]
@@ -504,7 +528,7 @@
 
 def potential_edge_kernel(
     x_a, x_b, weight, scale, field, inner_two, inner_source, inner_first, inner_mid, conduct_mid,
-    edge_two, edge_source, source_mid, pay_a, pay_b, first, pairs,
+    token, token_2, edge_two, edge_source, source_mid, pay_a, pay_b, first, pairs,
 ):
     half = source_mid.shape[0]
     nx = 2 * half
@@ -542,7 +566,7 @@
         send_y(pay_a, pay_b, 4 * x, source_mid[x, 0:4, :], source_mid[x, 12:16, :])
 
 
-def mid_pack_x_kernel(field, r_a, r_b, token, token_2, pay_a, pay_b):
+def mid_pack_x_kernel(field, r_a, r_b, pay_a, pay_b):
     n = field.shape[0]
 
     def tile(x, t):
@@ -556,7 +580,7 @@
 
 
 def mid_kernel(
-    source_own, conduct_own, yy_a, yy_b, xx_a, xx_b, y_a, y_b, x_a, x_b, rho, load,
+    source_own, conduct_own, yy_a, yy_b, xx_a, xx_b, y_a, y_b, x_a, x_b, rho, load, token,
     after_two, source, weight, coarse, conduct, pay_a, pay_b, part, scale, mid_conduct, pairs, pairs_2,
 ):
     n = source_own.shape[0]
@@ -620,11 +644,9 @@
 COARSE_W = 0.0625
 
 
-def coarse_ready_kernel(own, r_a, r_b, rho, load, token, one, two, conduct, scale):
-    token[...] = jnp.zeros(token.shape, F32)
-    base = r_a.shape[0] - 64
+def coarse_ready_kernel(own, r_a, r_b, rho, load, one, two, conduct, scale):
     for x in range(8):
-        after, before = y_sides(r_a, r_b, base + 8 * x, 8)
+        after, before = y_planes(r_a, r_b, x)
         k = jnp.concatenate([own[x], after, jnp.zeros((8, 256), F32), before], axis=0)
         conduct[x] = k
         scale[x] = OMEGA / (MASS + 2.25 * k)
@@ -652,12 +674,11 @@
 
 
 def coarse_kernel(own, conduct, far_a, far_b, r_a, r_b, error, source, weight, one, two):
-    base = far_a.shape[0] - 64
     for x in range(8):
         after, before = y_sides(r_a, r_b, 9 * x, 8)
         b = wide_rows(own[x, 0:8, :], own[x, 8:9, :], own[x, 11:12, :], after, before)
         last_after, last_before = y_sides(r_a, r_b, 9 * x + 8, 1)
-        after, before = y_sides(far_a, far_b, base + 8 * x, 8)
+        after, before = y_planes(far_a, far_b, x)
         after = jnp.concatenate([after[1:8], last_after], axis=0)
         before = jnp.concatenate([last_before, before[0:7]], axis=0)
         k = wide_rows(conduct[x, 0:8, :], conduct[x, 8:9, :], conduct[x, 11:12, :], after, before)
@@ -888,44 +909,43 @@
         name="own",
     )
     xx_a, xx_b = swap(pay_a, pay_b, "grp")
-    distance = peers // 2
-    while distance > 1:
-        lists = jnp.concatenate([lists, exchange(lists, distance)], axis=0)
-        distance //= 2
-    far_rows = second_rows(nx)[2]
+    lists = jnp.concatenate([lists] + [exchange(lists, distance) for distance in range(peers - 2, 0, -2)], axis=0)
+    far_rows = second_rows(nx)[1]
     far_pay = call(
         second_pack_kernel,
         [shaped(far_rows, 256), shaped(far_rows + peers, 256)],
-        [phi_old, conduct_mid, conduct_coarse, lists, xx_a, xx_b],
+        [phi_old, conduct_mid, lists, xx_a, xx_b],
         name="second_pack",
     )
     yy_a, yy_b = swap(*far_pay, "dev")
     pay_a, pay_b = call(
         first_pack_x_kernel,
         [shaped(35, 8, 256)] * 2,
-        [conc_old, phase_label, y_a, y_b, conduct_coarse],
+        [conc_old, phase_label, y_a, y_b, lists],
         name="first_pack_x",
     )
     x_a, x_b = swap(pay_a, pay_b, "grp")
 
-    (conc_new,) = call(
-        sweeps_kernel,
-        [shaped(nx, nx, 256)],
-        [conc_old, phase_label, gain, base, y_a, y_b, x_a, x_b],
-        [vmem(*ext)] * 2 + [vmem(nx, 8, 256)] * 2 + [vmem(2 * HALO, nx + 2 * HALO, 256)] * 2,
-        name="sweeps",
-    )
-    flux_all, pay_a, pay_b = call(
-        flux_kernel,
-        [shaped(nx, nx, 256), shaped(3 * nx, 256), shaped(3 * nx, 256)],
-        [conc_new, phase_label, phi_old, solid_pot],
-        name="flux",
+    ext_y = (nx, nx + 2 * HALO, 256)
+    zero, first, second, third, gain_far, base_far, conc_inner, flux_inner = call(
+        sweeps_inner_kernel,
+        [shaped(*ext_y)] * 4 + [shaped(nx, 8, 256)] * 2 + [shaped(nx, nx, 256)] * 2,
+        [conc_old, phase_label, phi_old, solid_pot, gain, base, y_a, y_b],
+        name="sweeps_inner",
+    )
+    edge_args = [x_a, x_b, phase_label, phi_old, solid_pot, gain, base, zero, first, second, third]
+    conc_new, flux_all, pay_a, pay_b = call(
+        sweeps_edge_kernel,
+        [shaped(nx, nx, 256), shaped(nx, nx, 256), shaped(3 * nx, 256), shaped(3 * nx, 256)],
+        edge_args + [gain_far, base_far, conc_inner, flux_inner],
+        [vmem(16, nx + 2 * HALO, 256)] * 4,
+        name="sweeps_edge",
     )
     f_a, f_b = swap(pay_a, pay_b, "dev")
     flux_own, halo_mask = call(
         mask_kernel,
         [shaped(nx, nx, 256), shaped(nx, 8, 256)],
-        [flux_all, lists, yy_b],
+        [flux_all, lists, yy_b, yy_a],
         [vmem(3, nx, 8, LANES)],
         name="mask",
     )
@@ -946,11 +966,12 @@
         [vmem(nx, 8, 256), vmem(half, 2, nx, LANES)],
         name="potential_inner",
     )
+    k_a, k_b = swap(conduct_coarse, conduct_coarse, "dev")
     edge = (16, nx + 2 * HALO, 256)
     edge_two, edge_source, source_mid, pay_a, pay_b = call(
         potential_edge_kernel,
         [shaped(*edge), shaped(*edge), shaped(half, half, 256), shaped(4 * half, 256), shaped(4 * half, 256)],
-        [fx_a, fx_b, weight, scale, field, fine_two, fine_source, fine_first, inner_mid, conduct_mid],
+        [fx_a, fx_b, weight, scale, field, fine_two, fine_source, fine_first, inner_mid, conduct_mid, k_a, k_b],
         [vmem(*edge), vmem(2, 2, nx, LANES)],
         name="potential_edge",
     )
@@ -964,22 +985,22 @@
         name="store",
     )
     wide = (quarter, 32, 256)
-    rho, load, made = call(
+    rho, load = call(
         coarse_ready_kernel,
-        [shaped(quarter, quarter, 256), shaped(8, LANES), token_shape],
-        [conduct_coarse, yy_a, yy_b],
+        [shaped(quarter, quarter, 256), shaped(8, LANES)],
+        [conduct_coarse, k_a, k_b],
         [vmem(*wide)] * 4,
         name="coarse_ready",
     )
     pay_a, pay_b = call(
-        mid_pack_x_kernel, [shaped(3 * HALO, 8, 256)] * 2, [source_mid, m_a, m_b, made, stored], name="mid_pack_x"
+        mid_pack_x_kernel, [shaped(3 * HALO, 8, 256)] * 2, [source_mid, m_a, m_b], name="mid_pack_x"
     )
     mx_a, mx_b = swap(pay_a, pay_b, "grp")
     mid_two, mid_source, mid_weight, source_coarse, wide_coarse, pay_a, pay_b, sums = call(
         mid_kernel,
         [shaped(*ext_mid)] * 3
         + [shaped(quarter, 12, 256), shaped(quarter, 12, 256), shaped(72, 256), shaped(80, 256), shaped(8, 256)],
-        [source_mid, conduct_mid, yy_a, yy_b, xx_a, xx_b, m_a, m_b, mx_a, mx_b, rho, load],
+        [source_mid, conduct_mid, yy_a, yy_b, xx_a, xx_b, m_a, m_b, mx_a, mx_b, rho, load, stored],
         [vmem(*ext_mid)] * 2 + [vmem(8, 2, half + 2 * HALO, LANES)] * 2,
         name="middle",
     )
@@ -992,7 +1013,7 @@
     (error,) = call(
         coarse_kernel,
         [shaped(8, 16, 256)],
-        [source_coarse, wide_coarse, yy_a, yy_b, c_a, c_b],
+        [source_coarse, wide_coarse, k_a, k_b, c_a, c_b],
         [vmem(*wide)] * 4,
         name="coarse",
     )

time: 83.8 us -> 88.9 us (1.061)
  starting transfers between devices: 46.5 us -> 50.8 us
    ppermute x10 -> x11, starting transfers between devices: 16.1 us -> 23.1 us  [swap(): lax.ppermute(pay_b, axis, both_ways(pairs_b))]
    ppermute x10 -> x11, waiting for transfers between devices: 5.63 us -> 1.96 us  [swap(): lax.ppermute(pay_a, axis, both_ways(pairs_a))]
    ppermute x10 -> x11, waiting for transfers between devices: 3.42 us -> 6.29 us  [swap(): lax.ppermute(pay_b, axis, both_ways(pairs_b))]
    ppermute x10 -> x11, starting transfers between devices: 23.7 us -> 21.7 us  [swap(): lax.ppermute(pay_a, axis, both_ways(pairs_a))]
    ppermute x4 -> x5, waiting for transfers between devices: 1.45 us -> 3.09 us  [exchange(): lax.ppermute(value, 'dev', [(i, i ^ distance) for i in range(lax.axis_siz...]
    ppermute x4 -> x5, starting transfers between devices: 6.66 us -> 6.07 us  [exchange(): lax.ppermute(value, 'dev', [(i, i ^ distance) for i in range(lax.axis_siz...]
  transfers between devices with their start and end apart: 24 -> 27, of which waited for: 8 -> 8; matrix products, arithmetic and copies ran while one was open for 0% -> 0% of each run, Pallas kernels for 18% -> 17%
where the time goes in v13:
time: 88.9 us; the launch traced here: 88.4 us
  starting transfers between devices  50.8 us (57%)
  Pallas kernels  23.1 us (26%)
  waiting for transfers between devices  11.3 us (13%)
  local copies, waits for them, and re-layouts  1.94 us (2%)
  between operations  1.2 us (1%)
    pallas_call x19, Pallas kernels, call(): pl.pallas_call(kernel, out_shape=tuple(outs), in_specs=in_specs or [WHOLE...  23.1 us
    ppermute x11, starting transfers between devices, swap(): lax.ppermute(pay_b, axis, both_ways(pairs_b))  23.1 us
    ppermute x11, starting transfers between devices, swap(): lax.ppermute(pay_a, axis, both_ways(pairs_a))  21.7 us
    ppermute x11, waiting for transfers between devices, swap(): lax.ppermute(pay_b, axis, both_ways(pairs_b))  6.29 us
    ppermute x5, starting transfers between devices, exchange(): lax.ppermute(value, 'dev', [(i, i ^ distance) for i in range(lax.axis_siz...  6.07 us
    ppermute x5, waiting for transfers between devices, exchange(): lax.ppermute(value, 'dev', [(i, i ^ distance) for i in range(lax.axis_siz...  3.09 us
    ppermute x11, waiting for transfers between devices, swap(): lax.ppermute(pay_a, axis, both_ways(pairs_a))  1.96 us
    unnamed x12, local copies, waits for them, and re-layouts  1.94 us
  transfers between devices with their start and end apart: 27, of which 8 were waited for; matrix products, arithmetic and copies ran while one was open for 0% of the time, Pallas kernels for 17%

profile of v13, /device:TPU:1, one launch (start us, length us, event | category | flops | bytes accessed | tf_op | source)
XLA Modules:
  0.0 88.4 jit_solution(6262959550564621995)
XLA Ops:
  0.7 2.1 %first_pack.1 = (f32[224,256]{1,0:T(8,128)}, f32[224,256]{1,0:T(8,128)}, f32[8,256]{1,0:T(8,128)}) custom-call(f32[32,32,256]{2,1,0:T(8,128)} %conc.9, s32[32,32,256]{2,1,0:T(8,128)} %label.11, s32[1,256]{1,0:T(1,128)} %bitcast.1, s32[1,256]{1,0:T(1,128)} %block.1), custom_call_target="tpu_custom_call" | custom-call | flops 1000000 | bytes 2566144 | tf_op jit(solution)/shard_map/first_pack/pallas_call | solution.py:36
  3.4 4.6 %collective-permute-start.1 = (f32[224,256]{1,0:T(8,128)}, f32[224,256]{1,0:T(8,128)S(1)}, u32[]{:S(2)}, u32[]{:S(2)}) collective-permute-start(f32[224,256]{1,0:T(8,128)} %get-tuple-element.75), channel_id=1, source_target_pairs={{0,1},{2,3},{4,5},{6,7},{1,0},{3,2},{5,4},{7,6},{8,9},{10,11},{12,... | collective-permute-start | bytes 688136 | tf_op jit(solution)/shard_map/ppermute | solution.py:872
  8.0 1.2 %copy-done.2 = f32[32,32,256]{2,1,0:T(8,128)S(1)} copy-done((f32[32,32,256]{2,1,0:T(8,128)S(1)}, f32[32,32,256]{2,1,0:T(8,128)}, u32[]{:S(2)}) %copy-start.2) | copy-done | bytes 1048600
  10.6 2.0 %collective-permute-start.2 = (f32[2,256]{1,0:T(2,128)S(1)}, f32[2,256]{1,0:T(2,128)S(1)}, u32[]{:S(2)}, u32[]{:S(2)}) collective-permute-start(f32[2,256]{1,0:T(2,128)S(1)} %get-tuple-element.77), channel_id=1, source_target_pairs={{0,6},{1,7},{2,4},{3,5},{4,2},{5,3},{6,0},{7,1},{8,14},{9,15},{10,... | collective-permute-start | bytes 6152 | tf_op jit(solution)/shard_map/ppermute | solution.py:876
  13.1 1.1 %collective-permute-start.4 = (f32[2,256]{1,0:T(2,128)S(1)}, f32[2,256]{1,0:T(2,128)S(1)}, u32[]{:S(2)}, u32[]{:S(2)}) collective-permute-start(f32[2,256]{1,0:T(2,128)S(1)} %get-tuple-element.77), channel_id=1, source_target_pairs={{0,2},{1,3},{2,0},{3,1},{4,6},{5,7},{6,4},{7,5},{8,10},{9,11},{10,... | collective-permute-start | bytes 6152 | tf_op jit(solution)/shard_map/ppermute | solution.py:876
  15.0 5.3 %collective-permute-start.7 = (f32[22,8,256]{2,1,0:T(8,128)S(1)}, f32[22,8,256]{2,1,0:T(8,128)S(1)}, u32[]{:S(2)}, u32[]{:S(2)}) collective-permute-start(f32[22,8,256]{2,1,0:T(8,128)S(1)} %get-tuple-element.93), channel_id=1, source_target_pairs={{8,16},{16,8},{9,17},{17,9},{10,18},{18,10},{11,19},{19,11},{12,20... | collective-permute-start | bytes 540680 | tf_op jit(solution)/shard_map/ppermute | solution.py:872
  20.5 2.1 %collective-permute-start.5 = (f32[35,8,256]{2,1,0:T(8,128)S(1)}, f32[35,8,256]{2,1,0:T(8,128)S(1)}, u32[]{:S(2)}, u32[]{:S(2)}) collective-permute-start(f32[35,8,256]{2,1,0:T(8,128)S(1)} %get-tuple-element.78), channel_id=1, source_target_pairs={{8,16},{16,8},{9,17},{17,9},{10,18},{18,10},{11,19},{19,11},{12,20... | collective-permute-start | bytes 860168 | tf_op jit(solution)/shard_map/ppermute | solution.py:872
  22.7 0.8 collective-permute-done.7.x_a.xx_a
  24.8 4.1 %sweeps_inner.1 = (f32[32,40,256]{2,1,0:T(8,128)S(1)}, f32[32,40,256]{2,1,0:T(8,128)S(1)}, f32[32,40,256]{2,1,0:T(8,128)S(1)}, f32[32,40,256]{2,1,0:T(8,128)S(1)...) custom-call(f32[32,32,256]{2,1,0:T(8,128)S(1)} %copy-done.1, ...), custom_call_target="tpu_custom_call" | custom-call | flops 1000000 | bytes 14614528 | tf_op jit(solution)/shard_map/sweeps_inner/pallas_call | solution.py:36
  28.9 1.2 %sweeps_edge.1 = (f32[32,32,256]{2,1,0:T(8,128)S(1)}, f32[32,32,256]{2,1,0:T(8,128)S(1)}, f32[96,256]{1,0:T(8,128)S(1)}, f32[96,256]{1,0:T(8,128)S(1)}) custom-call(f32[35,8,256]{2,1,0:T(8,128)S(1)} %collective-permute-done.5.x_a, f32[35,8,256]{2,1,0:T(8,128)S(1)} %collective-permute-done.6.x_b, s32[32,32,256]{2,1,0:T(8,128)S(1)} %copy-done, ...), custom_call_target="tpu_custom_call" | custom-call | flops 1000000 | bytes 15974400 | tf_op jit(solution)/shard_map/sweeps_edge/pallas_call | solution.py:36
  30.8 5.9 %collective-permute-start.12 = (f32[96,256]{1,0:T(8,128)S(1)}, f32[96,256]{1,0:T(8,128)S(1)}, u32[]{:S(2)}, u32[]{:S(2)}) collective-permute-start(f32[96,256]{1,0:T(8,128)S(1)} %get-tuple-element.101), channel_id=1, source_target_pairs={{0,1},{2,3},{4,5},{6,7},{1,0},{3,2},{5,4},{7,6},{8,9},{10,11},{12,... | collective-permute-start | bytes 294920 | tf_op jit(solution)/shard_map/ppermute | solution.py:872
  37.5 0.8 mask.1
  38.4 2.9 %collective-permute-done.12.r_b.y_b = f32[96,256]{1,0:T(8,128)S(1)} collective-permute-done((f32[96,256]{1,0:T(8,128)S(1)}, f32[96,256]{1,0:T(8,128)S(1)}, u32[]{:S(2)}, u32[]{:S(2)}) %collective-permute-start.12) | collective-permute-done | bytes 98336 | tf_op jit(solution)/shard_map/ppermute | solution.py:872
  41.3 2.8 %collective-permute-start.13 = (f32[15,8,256]{2,1,0:T(8,128)S(1)}, f32[15,8,256]{2,1,0:T(8,128)S(1)}, u32[]{:S(2)}, u32[]{:S(2)}) collective-permute-start(f32[15,8,256]{2,1,0:T(8,128)S(1)} %get-tuple-element.104), channel_id=1, source_target_pairs={{8,16},{16,8},{9,17},{17,9},{10,18},{18,10},{11,19},{19,11},{12,20... | collective-permute-start | bytes 368648 | tf_op jit(solution)/shard_map/ppermute | solution.py:872
  44.9 4.7 %collective-permute-start.16 = (f32[8,8,256]{2,1,0:T(8,128)S(1)}, f32[8,8,256]{2,1,0:T(8,128)S(1)}, u32[]{:S(2)}, u32[]{:S(2)}) collective-permute-start(f32[8,8,256]{2,1,0:T(8,128)S(1)} %get-tuple-element.113.own), channel_id=1, source_target_pairs={{0,1},{2,3},{4,5},{6,7},{1,0},{3,2},{5,4},{7,6},{8,9},{10,11},{12,... | collective-permute-start | bytes 196616 | tf_op jit(solution)/shard_map/ppermute | solution.py:872
  49.7 3.3 %potential_inner.1 = (f32[40,40,256]{2,1,0:T(8,128)S(1)}, f32[40,40,256]{2,1,0:T(8,128)S(1)}, f32[40,40,256]{2,1,0:T(8,128)S(1)}, f32[16,16,256]{2,1,0:T(8,128)S(1)}, f32[40,40,256]{2,1,0:T(8,128)S(1)}) custom-call(f32[32,32,256]{2,1,0:T(8,128)S(1)} %get-tuple-element.97.flux, f32[32,8,256]{2,1,0:T(8,128)S(1)} %get-tuple-element.102.mask, ...), custom_call_target="tpu_custom_call" | custom-call | flops 1000000 | bytes 13426688 | tf_op jit(solution)/shard_map/potential_inner/pallas_call | solution.py:36
  54.3 4.0 %collective-permute-start.18 = (f32[64,256]{1,0:T(8,128)S(1)}, f32[64,256]{1,0:T(8,128)S(1)}, u32[]{:S(2)}, u32[]{:S(2)}) collective-permute-start(f32[64,256]{1,0:T(8,128)S(1)} %get-tuple-element.116), channel_id=1, source_target_pairs={{0,1},{2,3},{4,5},{6,7},{1,0},{3,2},{5,4},{7,6},{8,9},{10,11},{12,... | collective-permute-start | bytes 196616 | tf_op jit(solution)/shard_map/ppermute | solution.py:872
  58.4 1.7 %collective-permute-done.18.r_b.y_b = f32[64,256]{1,0:T(8,128)S(1)} collective-permute-done((f32[64,256]{1,0:T(8,128)S(1)}, f32[64,256]{1,0:T(8,128)S(1)}, u32[]{:S(2)}, u32[]{:S(2)}) %collective-permute-start.18) | collective-permute-done | bytes 65568 | tf_op jit(solution)/shard_map/ppermute | solution.py:872
  60.0 4.2 %collective-permute-start.19 = (f32[12,8,256]{2,1,0:T(8,128)S(1)}, f32[12,8,256]{2,1,0:T(8,128)S(1)}, u32[]{:S(2)}, u32[]{:S(2)}) collective-permute-start(f32[12,8,256]{2,1,0:T(8,128)S(1)} %get-tuple-element.117), channel_id=1, source_target_pairs={{8,16},{16,8},{9,17},{17,9},{10,18},{18,10},{11,19},{19,11},{12,20... | collective-permute-start | bytes 294920 | tf_op jit(solution)/shard_map/ppermute | solution.py:872
  64.3 1.2 %coarse_ready.1 = (f32[8,8,256]{2,1,0:T(8,128)S(1)}, f32[8,128]{1,0:T(8,128)S(1)}) custom-call(f32[8,8,256]{2,1,0:T(8,128)S(1)} %get-tuple-element.113.own, f32[8,8,256]{2,1,0:T(8,128)S(1)} %collective-permute-done.15.token.r_a.far_a, f32[8,8,256]{2,1,0:T(8,128)S(1)} %collective-permute-done.16.token_2.r_b.far_b), custom_call_target="tpu_custom_call" | custom-call | flops 1000000 | bytes 266240 | tf_op jit(solution)/shard_map/coarse_ready/pallas_call | solution.py:36
  65.5 1.4 %store.1 = (f32[32,32,256]{2,1,0:T(8,128)}, f32[32,32,256]{2,1,0:T(8,128)}, f32[8,128]{1,0:T(8,128)S(1)}) custom-call(f32[32,32,256]{2,1,0:T(8,128)S(1)} %get-tuple-element.90.conc, f32[32,32,256]{2,1,0:T(8,128)S(1)} %get-tuple-element.97.flux), custom_call_target="tpu_custom_call" | custom-call | flops 1000000 | bytes 4198400 | tf_op jit(solution)/shard_map/store/pallas_call | solution.py:36
  66.9 1.0 %middle.1 = (f32[24,24,256]{2,1,0:T(8,128)S(1)}, f32[24,24,256]{2,1,0:T(8,128)S(1)}, f32[24,24,256]{2,1,0:T(8,128)S(1)}, f32[8,12,256]{2,1,0:T(8,128)S(1)}, f32[...) custom-call(f32[16,16,256]{2,1,0:T(8,128)S(1)} %get-tuple-element.114.field.source_, ...), custom_call_target="tpu_custom_call" | custom-call | flops 1000000 | bytes 3833856 | tf_op jit(solution)/shard_map/middle/pallas_call | solution.py:36
  67.9 2.3 %collective-permute-start.22 = (f32[80,256]{1,0:T(8,128)S(1)}, f32[80,256]{1,0:T(8,128)S(1)}, u32[]{:S(2)}, u32[]{:S(2)}) collective-permute-start(f32[80,256]{1,0:T(8,128)S(1)} %get-tuple-element.125), channel_id=1, source_target_pairs={{0,1},{2,3},{4,5},{6,7},{1,0},{3,2},{5,4},{7,6},{8,9},{10,11},{12,... | collective-permute-start | bytes 245768 | tf_op jit(solution)/shard_map/ppermute | solution.py:872
  70.9 1.7 %collective-permute-done.22.r_b = f32[80,256]{1,0:T(8,128)S(1)} collective-permute-done((f32[80,256]{1,0:T(8,128)S(1)}, f32[80,256]{1,0:T(8,128)S(1)}, u32[]{:S(2)}, u32[]{:S(2)}) %collective-permute-start.22) | collective-permute-done | bytes 81952 | tf_op jit(solution)/shard_map/ppermute | solution.py:872
  72.6 0.8 collective-permute-start.23
  73.4 1.7 %collective-permute-done.23 = f32[8,256]{1,0:T(8,128)S(1)} collective-permute-done((f32[8,256]{1,0:T(8,128)S(1)}, f32[8,256]{1,0:T(8,128)S(1)}, u32[]{:S(2)}, u32[]{:S(2)}) %collective-permute-start.23) | collective-permute-done | bytes 8224 | tf_op jit(solution)/shard_map/ppermute | solution.py:876
  75.1 1.6 %collective-permute-start.24 = (f32[8,256]{1,0:T(8,128)S(1)}, f32[8,256]{1,0:T(8,128)S(1)}, u32[]{:S(2)}, u32[]{:S(2)}) collective-permute-start(f32[8,256]{1,0:T(8,128)S(1)} %add.10), channel_id=1, source_target_pairs={{0,4},{1,5},{2,6},{3,7},{4,0},{5,1},{6,2},{7,3},{8,12},{9,13},{10,... | collective-permute-start | bytes 24584 | tf_op jit(solution)/shard_map/ppermute | solution.py:876
  76.8 1.2 %coarse.1.error = f32[8,16,256]{2,1,0:T(8,128)S(1)} custom-call(f32[8,12,256]{2,1,0:T(8,128)S(1)} %get-tuple-element.122.own, f32[8,12,256]{2,1,0:T(8,128)S(1)} %get-tuple-element.123.conduct, f32[8,8,256]{2,1,0:T(8,128)S(1)} %collective-permute-done.15.token.r_a.far_a, f32[8,8,256]{2,1,0:T(8,128)S(1)} %collective-permute-done.16.token_2.r_b.far_b, ...), custom_call_target="tpu_custom_call" | custom-call | flops 1000000 | bytes 614400 | tf_op jit(solution)/shard_map/coarse/pallas_call | solution.py:36
  78.5 2.8 %finish_early.1 = (f32[8,16,256]{2,1,0:T(8,128)S(1)}, f32[2,16,256]{2,1,0:T(8,128)S(1)}, f32[2,16,256]{2,1,0:T(8,128)S(1)}, f32[32,32,256]{2,1,0:T(8,128)}, f32[...) custom-call(f32[8,16,256]{2,1,0:T(8,128)S(1)} %coarse.1.error, ...), custom_call_target="tpu_custom_call" | custom-call | flops 1000000 | bytes 8593408 | tf_op jit(solution)/shard_map/finish_early/pallas_call | solution.py:36
  81.4 3.3 %collective-permute-start.25 = (f32[2,16,256]{2,1,0:T(8,128)S(1)}, f32[2,16,256]{2,1,0:T(8,128)S(1)}, u32[]{:S(2)}, u32[]{:S(2)}) collective-permute-start(f32[2,16,256]{2,1,0:T(8,128)S(1)} %get-tuple-element.130), channel_id=1, source_target_pairs={{8,16},{16,8},{9,17},{17,9},{10,18},{18,10},{11,19},{19,11},{12,20... | collective-permute-start | bytes 98312 | tf_op jit(solution)/shard_map/ppermute | solution.py:872
  85.5 1.1 %collective-permute-done.25.x_a = f32[2,16,256]{2,1,0:T(8,128)S(1)} collective-permute-done((f32[2,16,256]{2,1,0:T(8,128)S(1)}, f32[2,16,256]{2,1,0:T(8,128)S(1)}, u32[]{:S(2)}, u32[]{:S(2)}) %collective-permute-start.25) | collective-permute-done | bytes 32800 | tf_op jit(solution)/shard_map/ppermute | solution.py:872
  86.6 1.7 %finish_edge.1 = f32[32,32,256]{2,1,0:T(8,128)} custom-call(f32[2,16,256]{2,1,0:T(8,128)S(1)} %collective-permute-done.25.x_a, f32[2,16,256]{2,1,0:T(8,128)S(1)} %collective-permute-done.26.x_b, f32[24,24,256]{2,1,0:T(8,128)S(1)} %get-tuple-element.127.rest_0_.mid_two, ...), custom_call_target="tpu_custom_call", output_to_operand_aliasing={{}: (14, {})} | custom-call | flops 1000000 | bytes 10682368 | tf_op jit(solution)/shard_map/finish_edge/pallas_call | solution.py:36
  (57 shorter events, 10.5 us)
Async XLA Ops:
  0.6 7.4 %copy-start.1 = (f32[32,32,256]{2,1,0:T(8,128)S(1)}, f32[32,32,256]{2,1,0:T(8,128)}, u32[]{:S(2)}) copy-start(f32[32,32,256]{2,1,0:T(8,128)} %conc.9) | copy-start | bytes 3145732
  0.6 7.4 %copy-start = (s32[32,32,256]{2,1,0:T(8,128)S(1)}, s32[32,32,256]{2,1,0:T(8,128)}, u32[]{:S(2)}) copy-start(s32[32,32,256]{2,1,0:T(8,128)} %label.11) | copy-start | bytes 3145732
  2.7 17.7 %collective-permute-start = (f32[224,256]{1,0:T(8,128)}, f32[224,256]{1,0:T(8,128)S(1)}, u32[]{:S(2)}, u32[]{:S(2)}) collective-permute-start(f32[224,256]{1,0:T(8,128)} %get-tuple-element.74), channel_id=1, source_target_pairs={{1,2},{3,4},{5,6},{2,1},{4,3},{6,5},{9,10},{11,12},{13,14},{10,9},... | collective-permute-start | bytes 688136 | tf_op jit(solution)/shard_map/ppermute | solution.py:872
  3.4 17.0 %collective-permute-start.1 = (f32[224,256]{1,0:T(8,128)}, f32[224,256]{1,0:T(8,128)S(1)}, u32[]{:S(2)}, u32[]{:S(2)}) collective-permute-start(f32[224,256]{1,0:T(8,128)} %get-tuple-element.75), channel_id=1, source_target_pairs={{0,1},{2,3},{4,5},{6,7},{1,0},{3,2},{5,4},{7,6},{8,9},{10,11},{12,... | collective-permute-start | bytes 688136 | tf_op jit(solution)/shard_map/ppermute | solution.py:872
  8.0 1.2 %copy-start.2 = (f32[32,32,256]{2,1,0:T(8,128)S(1)}, f32[32,32,256]{2,1,0:T(8,128)}, u32[]{:S(2)}) copy-start(f32[32,32,256]{2,1,0:T(8,128)} %phi.9) | copy-start | bytes 3145732
  10.6 12.9 %copy-start.3 = (f32[32,32,256]{2,1,0:T(8,128)S(1)}, f32[32,32,256]{2,1,0:T(8,128)}, u32[]{:S(2)}) copy-start(f32[32,32,256]{2,1,0:T(8,128)} %phi.9) | copy-start | bytes 3145732
  10.6 4.4 %collective-permute-start.2 = (f32[2,256]{1,0:T(2,128)S(1)}, f32[2,256]{1,0:T(2,128)S(1)}, u32[]{:S(2)}, u32[]{:S(2)}) collective-permute-start(f32[2,256]{1,0:T(2,128)S(1)} %get-tuple-element.77), channel_id=1, source_target_pairs={{0,6},{1,7},{2,4},{3,5},{4,2},{5,3},{6,0},{7,1},{8,14},{9,15},{10,... | collective-permute-start | bytes 6152 | tf_op jit(solution)/shard_map/ppermute | solution.py:876
  12.6 7.7 %collective-permute-start.3 = (f32[2,256]{1,0:T(2,128)S(1)}, f32[2,256]{1,0:T(2,128)S(1)}, u32[]{:S(2)}, u32[]{:S(2)}) collective-permute-start(f32[2,256]{1,0:T(2,128)S(1)} %get-tuple-element.77), channel_id=1, source_target_pairs={{0,4},{1,5},{2,6},{3,7},{4,0},{5,1},{6,2},{7,3},{8,12},{9,13},{10,... | collective-permute-start | bytes 6152 | tf_op jit(solution)/shard_map/ppermute | solution.py:876
  13.1 7.3 %collective-permute-start.4 = (f32[2,256]{1,0:T(2,128)S(1)}, f32[2,256]{1,0:T(2,128)S(1)}, u32[]{:S(2)}, u32[]{:S(2)}) collective-permute-start(f32[2,256]{1,0:T(2,128)S(1)} %get-tuple-element.77), channel_id=1, source_target_pairs={{0,2},{1,3},{2,0},{3,1},{4,6},{5,7},{6,4},{7,5},{8,10},{9,11},{10,... | collective-permute-start | bytes 6152 | tf_op jit(solution)/shard_map/ppermute | solution.py:876
  15.0 8.5 %collective-permute-start.7 = (f32[22,8,256]{2,1,0:T(8,128)S(1)}, f32[22,8,256]{2,1,0:T(8,128)S(1)}, u32[]{:S(2)}, u32[]{:S(2)}) collective-permute-start(f32[22,8,256]{2,1,0:T(8,128)S(1)} %get-tuple-element.93), channel_id=1, source_target_pairs={{8,16},{16,8},{9,17},{17,9},{10,18},{18,10},{11,19},{19,11},{12,20... | collective-permute-start | bytes 540680 | tf_op jit(solution)/shard_map/ppermute | solution.py:872
  20.3 3.2 %collective-permute-start.8 = (f32[22,8,256]{2,1,0:T(8,128)S(1)}, f32[22,8,256]{2,1,0:T(8,128)S(1)}, u32[]{:S(2)}, u32[]{:S(2)}) collective-permute-start(f32[22,8,256]{2,1,0:T(8,128)S(1)} %get-tuple-element.94), channel_id=1, source_target_pairs={{0,8},{16,24},{8,0},{24,16},{1,9},{17,25},{9,1},{25,17},{2,10},{18... | collective-permute-start | bytes 540680 | tf_op jit(solution)/shard_map/ppermute | solution.py:872
  20.4 4.4 %copy-start.4 = (f32[32,32,256]{2,1,0:T(8,128)S(1)}, f32[32,32,256]{2,1,0:T(8,128)}, u32[]{:S(2)}) copy-start(f32[32,32,256]{2,1,0:T(8,128)} %solid.3) | copy-start | bytes 3145732
  20.5 8.4 %collective-permute-start.5 = (f32[35,8,256]{2,1,0:T(8,128)S(1)}, f32[35,8,256]{2,1,0:T(8,128)S(1)}, u32[]{:S(2)}, u32[]{:S(2)}) collective-permute-start(f32[35,8,256]{2,1,0:T(8,128)S(1)} %get-tuple-element.78), channel_id=1, source_target_pairs={{8,16},{16,8},{9,17},{17,9},{10,18},{18,10},{11,19},{19,11},{12,20... | collective-permute-start | bytes 860168 | tf_op jit(solution)/shard_map/ppermute | solution.py:872
  22.6 6.3 %collective-permute-start.6 = (f32[35,8,256]{2,1,0:T(8,128)S(1)}, f32[35,8,256]{2,1,0:T(8,128)S(1)}, u32[]{:S(2)}, u32[]{:S(2)}) collective-permute-start(f32[35,8,256]{2,1,0:T(8,128)S(1)} %get-tuple-element.79), channel_id=1, source_target_pairs={{0,8},{16,24},{8,0},{24,16},{1,9},{17,25},{9,1},{25,17},{2,10},{18... | collective-permute-start | bytes 860168 | tf_op jit(solution)/shard_map/ppermute | solution.py:872
  23.6 13.9 %collective-permute-start.9 = (f32[208,256]{1,0:T(8,128)S(1)}, f32[208,256]{1,0:T(8,128)S(1)}, u32[]{:S(2)}, u32[]{:S(2)}) collective-permute-start(f32[208,256]{1,0:T(8,128)S(1)} %get-tuple-element.95), channel_id=1, source_target_pairs={{0,1},{2,3},{4,5},{6,7},{1,0},{3,2},{5,4},{7,6},{8,9},{10,11},{12,... | collective-permute-start | bytes 638984 | tf_op jit(solution)/shard_map/ppermute | solution.py:872
  24.1 13.4 %collective-permute-start.10 = (f32[200,256]{1,0:T(8,128)S(1)}, f32[200,256]{1,0:T(8,128)S(1)}, u32[]{:S(2)}, u32[]{:S(2)}) collective-permute-start(f32[200,256]{1,0:T(8,128)S(1)} %get-tuple-element.96), channel_id=1, source_target_pairs={{1,2},{3,4},{5,6},{2,1},{4,3},{6,5},{9,10},{11,12},{13,14},{10,9},... | collective-permute-start | bytes 614408 | tf_op jit(solution)/shard_map/ppermute | solution.py:872
  30.2 8.2 %collective-permute-start.11 = (f32[96,256]{1,0:T(8,128)S(1)}, f32[96,256]{1,0:T(8,128)S(1)}, u32[]{:S(2)}, u32[]{:S(2)}) collective-permute-start(f32[96,256]{1,0:T(8,128)S(1)} %get-tuple-element.100), channel_id=1, source_target_pairs={{1,2},{3,4},{5,6},{2,1},{4,3},{6,5},{9,10},{11,12},{13,14},{10,9},... | collective-permute-start | bytes 294920 | tf_op jit(solution)/shard_map/ppermute | solution.py:872
  30.8 10.5 %collective-permute-start.12 = (f32[96,256]{1,0:T(8,128)S(1)}, f32[96,256]{1,0:T(8,128)S(1)}, u32[]{:S(2)}, u32[]{:S(2)}) collective-permute-start(f32[96,256]{1,0:T(8,128)S(1)} %get-tuple-element.101), channel_id=1, source_target_pairs={{0,1},{2,3},{4,5},{6,7},{1,0},{3,2},{5,4},{7,6},{8,9},{10,11},{12,... | collective-permute-start | bytes 294920 | tf_op jit(solution)/shard_map/ppermute | solution.py:872
  41.3 11.6 %collective-permute-start.13 = (f32[15,8,256]{2,1,0:T(8,128)S(1)}, f32[15,8,256]{2,1,0:T(8,128)S(1)}, u32[]{:S(2)}, u32[]{:S(2)}) collective-permute-start(f32[15,8,256]{2,1,0:T(8,128)S(1)} %get-tuple-element.104), channel_id=1, source_target_pairs={{8,16},{16,8},{9,17},{17,9},{10,18},{18,10},{11,19},{19,11},{12,20... | collective-permute-start | bytes 368648 | tf_op jit(solution)/shard_map/ppermute | solution.py:872
  44.2 8.8 %collective-permute-start.14 = (f32[15,8,256]{2,1,0:T(8,128)S(1)}, f32[15,8,256]{2,1,0:T(8,128)S(1)}, u32[]{:S(2)}, u32[]{:S(2)}) collective-permute-start(f32[15,8,256]{2,1,0:T(8,128)S(1)} %get-tuple-element.105), channel_id=1, source_target_pairs={{0,8},{16,24},{8,0},{24,16},{1,9},{17,25},{9,1},{25,17},{2,10},{18... | collective-permute-start | bytes 368648 | tf_op jit(solution)/shard_map/ppermute | solution.py:872
  44.2 8.7 %collective-permute-start.15 = (f32[8,8,256]{2,1,0:T(8,128)S(1)}, f32[8,8,256]{2,1,0:T(8,128)S(1)}, u32[]{:S(2)}, u32[]{:S(2)}) collective-permute-start(f32[8,8,256]{2,1,0:T(8,128)S(1)} %get-tuple-element.113.own), channel_id=1, source_target_pairs={{1,2},{3,4},{5,6},{2,1},{4,3},{6,5},{9,10},{11,12},{13,14},{10,9},... | collective-permute-start | bytes 196616 | tf_op jit(solution)/shard_map/ppermute | solution.py:872
  44.9 8.0 %collective-permute-start.16 = (f32[8,8,256]{2,1,0:T(8,128)S(1)}, f32[8,8,256]{2,1,0:T(8,128)S(1)}, u32[]{:S(2)}, u32[]{:S(2)}) collective-permute-start(f32[8,8,256]{2,1,0:T(8,128)S(1)} %get-tuple-element.113.own), channel_id=1, source_target_pairs={{0,1},{2,3},{4,5},{6,7},{1,0},{3,2},{5,4},{7,6},{8,9},{10,11},{12,... | collective-permute-start | bytes 196616 | tf_op jit(solution)/shard_map/ppermute | solution.py:872
  53.6 4.7 %collective-permute-start.17 = (f32[64,256]{1,0:T(8,128)S(1)}, f32[64,256]{1,0:T(8,128)S(1)}, u32[]{:S(2)}, u32[]{:S(2)}) collective-permute-start(f32[64,256]{1,0:T(8,128)S(1)} %get-tuple-element.115), channel_id=1, source_target_pairs={{1,2},{3,4},{5,6},{2,1},{4,3},{6,5},{9,10},{11,12},{13,14},{10,9},... | collective-permute-start | bytes 196616 | tf_op jit(solution)/shard_map/ppermute | solution.py:872
  54.3 5.7 %collective-permute-start.18 = (f32[64,256]{1,0:T(8,128)S(1)}, f32[64,256]{1,0:T(8,128)S(1)}, u32[]{:S(2)}, u32[]{:S(2)}) collective-permute-start(f32[64,256]{1,0:T(8,128)S(1)} %get-tuple-element.116), channel_id=1, source_target_pairs={{0,1},{2,3},{4,5},{6,7},{1,0},{3,2},{5,4},{7,6},{8,9},{10,11},{12,... | collective-permute-start | bytes 196616 | tf_op jit(solution)/shard_map/ppermute | solution.py:872
  60.0 6.9 %collective-permute-start.19 = (f32[12,8,256]{2,1,0:T(8,128)S(1)}, f32[12,8,256]{2,1,0:T(8,128)S(1)}, u32[]{:S(2)}, u32[]{:S(2)}) collective-permute-start(f32[12,8,256]{2,1,0:T(8,128)S(1)} %get-tuple-element.117), channel_id=1, source_target_pairs={{8,16},{16,8},{9,17},{17,9},{10,18},{18,10},{11,19},{19,11},{12,20... | collective-permute-start | bytes 294920 | tf_op jit(solution)/shard_map/ppermute | solution.py:872
  64.2 2.7 %collective-permute-start.20 = (f32[12,8,256]{2,1,0:T(8,128)S(1)}, f32[12,8,256]{2,1,0:T(8,128)S(1)}, u32[]{:S(2)}, u32[]{:S(2)}) collective-permute-start(f32[12,8,256]{2,1,0:T(8,128)S(1)} %get-tuple-element.118), channel_id=1, source_target_pairs={{0,8},{16,24},{8,0},{24,16},{1,9},{17,25},{9,1},{25,17},{2,10},{18... | collective-permute-start | bytes 294920 | tf_op jit(solution)/shard_map/ppermute | solution.py:872
  67.9 4.6 %collective-permute-start.22 = (f32[80,256]{1,0:T(8,128)S(1)}, f32[80,256]{1,0:T(8,128)S(1)}, u32[]{:S(2)}, u32[]{:S(2)}) collective-permute-start(f32[80,256]{1,0:T(8,128)S(1)} %get-tuple-element.125), channel_id=1, source_target_pairs={{0,1},{2,3},{4,5},{6,7},{1,0},{3,2},{5,4},{7,6},{8,9},{10,11},{12,... | collective-permute-start | bytes 245768 | tf_op jit(solution)/shard_map/ppermute | solution.py:872
  70.2 6.6 %collective-permute-start.21 = (f32[72,256]{1,0:T(8,128)S(1)}, f32[72,256]{1,0:T(8,128)S(1)}, u32[]{:S(2)}, u32[]{:S(2)}) collective-permute-start(f32[72,256]{1,0:T(8,128)S(1)} %get-tuple-element.124), channel_id=1, source_target_pairs={{1,2},{3,4},{5,6},{2,1},{4,3},{6,5},{9,10},{11,12},{13,14},{10,9},... | collective-permute-start | bytes 221192 | tf_op jit(solution)/shard_map/ppermute | solution.py:872
  72.6 2.5 %collective-permute-start.23 = (f32[8,256]{1,0:T(8,128)S(1)}, f32[8,256]{1,0:T(8,128)S(1)}, u32[]{:S(2)}, u32[]{:S(2)}) collective-permute-start(f32[8,256]{1,0:T(8,128)S(1)} %slice_add_fusion), channel_id=1, source_target_pairs={{0,2},{1,3},{2,0},{3,1},{4,6},{5,7},{6,4},{7,5},{8,10},{9,11},{10,... | collective-permute-start | bytes 24584 | tf_op jit(solution)/shard_map/ppermute | solution.py:876
  75.1 3.4 %collective-permute-start.24 = (f32[8,256]{1,0:T(8,128)S(1)}, f32[8,256]{1,0:T(8,128)S(1)}, u32[]{:S(2)}, u32[]{:S(2)}) collective-permute-start(f32[8,256]{1,0:T(8,128)S(1)} %add.10), channel_id=1, source_target_pairs={{0,4},{1,5},{2,6},{3,7},{4,0},{5,1},{6,2},{7,3},{8,12},{9,13},{10,... | collective-permute-start | bytes 24584 | tf_op jit(solution)/shard_map/ppermute | solution.py:876
  81.4 5.2 %collective-permute-start.25 = (f32[2,16,256]{2,1,0:T(8,128)S(1)}, f32[2,16,256]{2,1,0:T(8,128)S(1)}, u32[]{:S(2)}, u32[]{:S(2)}) collective-permute-start(f32[2,16,256]{2,1,0:T(8,128)S(1)} %get-tuple-element.130), channel_id=1, source_target_pairs={{8,16},{16,8},{9,17},{17,9},{10,18},{18,10},{11,19},{19,11},{12,20... | collective-permute-start | bytes 98312 | tf_op jit(solution)/shard_map/ppermute | solution.py:872
  84.7 1.9 %collective-permute-start.26 = (f32[2,16,256]{2,1,0:T(8,128)S(1)}, f32[2,16,256]{2,1,0:T(8,128)S(1)}, u32[]{:S(2)}, u32[]{:S(2)}) collective-permute-start(f32[2,16,256]{2,1,0:T(8,128)S(1)} %get-tuple-element.131), channel_id=1, source_target_pairs={{0,8},{16,24},{8,0},{24,16},{1,9},{17,25},{9,1},{25,17},{2,10},{18... | collective-permute-start | bytes 98312 | tf_op jit(solution)/shard_map/ppermute | solution.py:872
  (1 other events, 0.7 us)

commit v14 on v13

--- a/solution.py
+++ b/solution.py
@@ -121,12 +121,6 @@
 def y_sides(r_a, r_b, at, count):
     flag = odd("dev")
     a, b = r_a[at : at + count, :], r_b[at : at + count, :]
-    return either(flag, a, b), either(flag, b, a)
-
-
-def y_planes(r_a, r_b, index):
-    flag = odd("dev")
-    a, b = r_a[index], r_b[index]
     return either(flag, a, b), either(flag, b, a)
 
 
@@ -247,10 +241,10 @@
 def second_rows(nx):
     phi = sum(corner_rows(nx, HALO, 0)[0])
     mid = sum(corner_rows(nx // 2, MID_HALO, 1)[0])
-    return phi, phi + mid
-
-
-def second_pack_kernel(phi, mid, lists, x_a, x_b, pay_a, pay_b):
+    return phi, phi + mid, phi + mid + 64
+
+
+def second_pack_kernel(phi, mid, coarse, lists, x_a, x_b, pay_a, pay_b):
     nx = phi.shape[0]
     starts = second_rows(nx)
 
@@ -270,6 +264,10 @@
     put(phi, HALO, 0, 0, 0)
     put(mid, MID_HALO, 1, 16, starts[0])
     base = starts[1]
+    for x in range(8):
+        pay_a[base + 8 * x : base + 8 * x + 8, :] = coarse[x]
+        pay_b[base + 8 * x : base + 8 * x + 8, :] = coarse[x]
+    base = starts[2]
     pay_b[base : base + lists.shape[0], :] = lists[...]
 
 
@@ -377,7 +375,7 @@
         send_y(pay_a, pay_b, 3 * x, flux[x, 0:3, :], flux[x, 29:32, :])
 
 
-def mask_kernel(flux_all, lists, far, token, flux, halo_mask, marked):
+def mask_kernel(flux_all, lists, far, flux, halo_mask, marked):
     nx = flux_all.shape[0]
     rows = lists.shape[0]
     pieces = [lists[i : i + 1, :] for i in range(rows)] + [far[i : i + 1, :] for i in range(far.shape[0] - rows, far.shape[0])]
@@ -528,7 +526,7 @@
 
 def potential_edge_kernel(
     x_a, x_b, weight, scale, field, inner_two, inner_source, inner_first, inner_mid, conduct_mid,
-    token, token_2, edge_two, edge_source, source_mid, pay_a, pay_b, first, pairs,
+    edge_two, edge_source, source_mid, pay_a, pay_b, first, pairs,
 ):
     half = source_mid.shape[0]
     nx = 2 * half
@@ -566,7 +564,7 @@
         send_y(pay_a, pay_b, 4 * x, source_mid[x, 0:4, :], source_mid[x, 12:16, :])
 
 
-def mid_pack_x_kernel(field, r_a, r_b, pay_a, pay_b):
+def mid_pack_x_kernel(field, r_a, r_b, token, token_2, pay_a, pay_b):
     n = field.shape[0]
 
     def tile(x, t):
@@ -580,7 +578,7 @@
 
 
 def mid_kernel(
-    source_own, conduct_own, yy_a, yy_b, xx_a, xx_b, y_a, y_b, x_a, x_b, rho, load, token,
+    source_own, conduct_own, yy_a, yy_b, xx_a, xx_b, y_a, y_b, x_a, x_b, rho, load,
     after_two, source, weight, coarse, conduct, pay_a, pay_b, part, scale, mid_conduct, pairs, pairs_2,
 ):
     n = source_own.shape[0]
@@ -644,9 +642,11 @@
 COARSE_W = 0.0625
 
 
-def coarse_ready_kernel(own, r_a, r_b, rho, load, one, two, conduct, scale):
+def coarse_ready_kernel(own, r_a, r_b, rho, load, token, one, two, conduct, scale):
+    token[...] = jnp.zeros(token.shape, F32)
+    base = r_a.shape[0] - 64
     for x in range(8):
-        after, before = y_planes(r_a, r_b, x)
+        after, before = y_sides(r_a, r_b, base + 8 * x, 8)
         k = jnp.concatenate([own[x], after, jnp.zeros((8, 256), F32), before], axis=0)
         conduct[x] = k
         scale[x] = OMEGA / (MASS + 2.25 * k)
@@ -674,11 +674,12 @@
 
 
 def coarse_kernel(own, conduct, far_a, far_b, r_a, r_b, error, source, weight, one, two):
+    base = far_a.shape[0] - 64
     for x in range(8):
         after, before = y_sides(r_a, r_b, 9 * x, 8)
         b = wide_rows(own[x, 0:8, :], own[x, 8:9, :], own[x, 11:12, :], after, before)
         last_after, last_before = y_sides(r_a, r_b, 9 * x + 8, 1)
-        after, before = y_planes(far_a, far_b, x)
+        after, before = y_sides(far_a, far_b, base + 8 * x, 8)
         after = jnp.concatenate([after[1:8], last_after], axis=0)
         before = jnp.concatenate([last_before, before[0:7]], axis=0)
         k = wide_rows(conduct[x, 0:8, :], conduct[x, 8:9, :], conduct[x, 11:12, :], after, before)
@@ -909,19 +910,22 @@
         name="own",
     )
     xx_a, xx_b = swap(pay_a, pay_b, "grp")
-    lists = jnp.concatenate([lists] + [exchange(lists, distance) for distance in range(peers - 2, 0, -2)], axis=0)
-    far_rows = second_rows(nx)[1]
+    distance = peers // 2
+    while distance > 1:
+        lists = jnp.concatenate([lists, exchange(lists, distance)], axis=0)
+        distance //= 2
+    far_rows = second_rows(nx)[2]
     far_pay = call(
         second_pack_kernel,
         [shaped(far_rows, 256), shaped(far_rows + peers, 256)],
-        [phi_old, conduct_mid, lists, xx_a, xx_b],
+        [phi_old, conduct_mid, conduct_coarse, lists, xx_a, xx_b],
         name="second_pack",
     )
     yy_a, yy_b = swap(*far_pay, "dev")
     pay_a, pay_b = call(
         first_pack_x_kernel,
         [shaped(35, 8, 256)] * 2,
-        [conc_old, phase_label, y_a, y_b, lists],
+        [conc_old, phase_label, y_a, y_b, conduct_coarse],
         name="first_pack_x",
     )
     x_a, x_b = swap(pay_a, pay_b, "grp")
@@ -945,7 +949,7 @@
     flux_own, halo_mask = call(
         mask_kernel,
         [shaped(nx, nx, 256), shaped(nx, 8, 256)],
-        [flux_all, lists, yy_b, yy_a],
+        [flux_all, lists, yy_b],
         [vmem(3, nx, 8, LANES)],
         name="mask",
     )
@@ -966,12 +970,11 @@
         [vmem(nx, 8, 256), vmem(half, 2, nx, LANES)],
         name="potential_inner",
     )
-    k_a, k_b = swap(conduct_coarse, conduct_coarse, "dev")
     edge = (16, nx + 2 * HALO, 256)
     edge_two, edge_source, source_mid, pay_a, pay_b = call(
         potential_edge_kernel,
         [shaped(*edge), shaped(*edge), shaped(half, half, 256), shaped(4 * half, 256), shaped(4 * half, 256)],
-        [fx_a, fx_b, weight, scale, field, fine_two, fine_source, fine_first, inner_mid, conduct_mid, k_a, k_b],
+        [fx_a, fx_b, weight, scale, field, fine_two, fine_source, fine_first, inner_mid, conduct_mid],
         [vmem(*edge), vmem(2, 2, nx, LANES)],
         name="potential_edge",
     )
@@ -985,22 +988,22 @@
         name="store",
     )
     wide = (quarter, 32, 256)
-    rho, load = call(
+    rho, load, made = call(
         coarse_ready_kernel,
-        [shaped(quarter, quarter, 256), shaped(8, LANES)],
-        [conduct_coarse, k_a, k_b],
+        [shaped(quarter, quarter, 256), shaped(8, LANES), token_shape],
+        [conduct_coarse, yy_a, yy_b],
         [vmem(*wide)] * 4,
         name="coarse_ready",
     )
     pay_a, pay_b = call(
-        mid_pack_x_kernel, [shaped(3 * HALO, 8, 256)] * 2, [source_mid, m_a, m_b], name="mid_pack_x"
+        mid_pack_x_kernel, [shaped(3 * HALO, 8, 256)] * 2, [source_mid, m_a, m_b, made, stored], name="mid_pack_x"
     )
     mx_a, mx_b = swap(pay_a, pay_b, "grp")
     mid_two, mid_source, mid_weight, source_coarse, wide_coarse, pay_a, pay_b, sums = call(
         mid_kernel,
         [shaped(*ext_mid)] * 3
         + [shaped(quarter, 12, 256), shaped(quarter, 12, 256), shaped(72, 256), shaped(80, 256), shaped(8, 256)],
-        [source_mid, conduct_mid, yy_a, yy_b, xx_a, xx_b, m_a, m_b, mx_a, mx_b, rho, load, stored],
+        [source_mid, conduct_mid, yy_a, yy_b, xx_a, xx_b, m_a, m_b, mx_a, mx_b, rho, load],
         [vmem(*ext_mid)] * 2 + [vmem(8, 2, half + 2 * HALO, LANES)] * 2,
         name="middle",
     )
@@ -1013,7 +1016,7 @@
     (error,) = call(
         coarse_kernel,
         [shaped(8, 16, 256)],
-        [source_coarse, wide_coarse, k_a, k_b, c_a, c_b],
+        [source_coarse, wide_coarse, yy_a, yy_b, c_a, c_b],
         [vmem(*wide)] * 4,
         name="coarse",
     )

time: 88.9 us -> 84.3 us (0.948)
  waiting for transfers between devices: 11.3 us -> 8.3 us
  starting transfers between devices: 50.8 us -> 49.1 us
    ppermute x11 -> x10, waiting for transfers between devices: 6.29 us -> 1.97 us  [swap(): lax.ppermute(pay_b, axis, both_ways(pairs_b))]
    ppermute x11 -> x10, starting transfers between devices: 23.1 us -> 19.2 us  [swap(): lax.ppermute(pay_b, axis, both_ways(pairs_b))]
    ppermute x11 -> x10, waiting for transfers between devices: 1.96 us -> 4.52 us  [swap(): lax.ppermute(pay_a, axis, both_ways(pairs_a))]
    ppermute x11 -> x10, starting transfers between devices: 21.7 us -> 23.1 us  [swap(): lax.ppermute(pay_a, axis, both_ways(pairs_a))]
    ppermute x5 -> x4, waiting for transfers between devices: 3.09 us -> 1.81 us  [exchange(): lax.ppermute(value, 'dev', [(i, i ^ distance) for i in range(lax.axis_siz...]
    ppermute x5 -> x4, starting transfers between devices: 6.07 us -> 6.89 us  [exchange(): lax.ppermute(value, 'dev', [(i, i ^ distance) for i in range(lax.axis_siz...]
  transfers between devices with their start and end apart: 27 -> 24, of which waited for: 8 -> 6; matrix products, arithmetic and copies ran while one was open for 0% -> 0% of each run, Pallas kernels for 17% -> 18%
where the time goes in v14:
time: 84.3 us; the launch traced here: 83.8 us
  starting transfers between devices  49.1 us (58%)
  Pallas kernels  23.2 us (28%)
  waiting for transfers between devices  8.3 us (10%)
  local copies, waits for them, and re-layouts  1.94 us (2%)
  between operations  1.22 us (1%)
    pallas_call x19, Pallas kernels, call(): pl.pallas_call(kernel, out_shape=tuple(outs), in_specs=in_specs or [WHOLE...  23.2 us
    ppermute x10, starting transfers between devices, swap(): lax.ppermute(pay_a, axis, both_ways(pairs_a))  23.1 us
    ppermute x10, starting transfers between devices, swap(): lax.ppermute(pay_b, axis, both_ways(pairs_b))  19.2 us
    ppermute x4, starting transfers between devices, exchange(): lax.ppermute(value, 'dev', [(i, i ^ distance) for i in range(lax.axis_siz...  6.89 us
    ppermute x10, waiting for transfers between devices, swap(): lax.ppermute(pay_a, axis, both_ways(pairs_a))  4.52 us
    ppermute x10, waiting for transfers between devices, swap(): lax.ppermute(pay_b, axis, both_ways(pairs_b))  1.97 us
    unnamed x12, local copies, waits for them, and re-layouts  1.94 us
    ppermute x4, waiting for transfers between devices, exchange(): lax.ppermute(value, 'dev', [(i, i ^ distance) for i in range(lax.axis_siz...  1.81 us
  transfers between devices with their start and end apart: 24, of which 6 were waited for; matrix products, arithmetic and copies ran while one was open for 0% of the time, Pallas kernels for 18%

profile of v14, /device:TPU:1, one launch (start us, length us, event | category | flops | bytes accessed | tf_op | source)
XLA Modules:
  0.0 83.8 jit_solution(16391434624160094408)
XLA Ops:
  0.7 2.1 %first_pack.1 = (f32[224,256]{1,0:T(8,128)}, f32[224,256]{1,0:T(8,128)}, f32[8,256]{1,0:T(8,128)}) custom-call(f32[32,32,256]{2,1,0:T(8,128)} %conc.9, s32[32,32,256]{2,1,0:T(8,128)} %label.11, s32[1,256]{1,0:T(1,128)} %bitcast.1, s32[1,256]{1,0:T(1,128)} %block.1), custom_call_target="tpu_custom_call" | custom-call | flops 1000000 | bytes 2566144 | tf_op jit(solution)/shard_map/first_pack/pallas_call | solution.py:36
  2.7 0.7 collective-permute-start
  3.4 4.6 %collective-permute-start.1 = (f32[224,256]{1,0:T(8,128)}, f32[224,256]{1,0:T(8,128)S(1)}, u32[]{:S(2)}, u32[]{:S(2)}) collective-permute-start(f32[224,256]{1,0:T(8,128)} %get-tuple-element.76), channel_id=1, source_target_pairs={{0,1},{2,3},{4,5},{6,7},{1,0},{3,2},{5,4},{7,6},{8,9},{10,11},{12,... | collective-permute-start | bytes 688136 | tf_op jit(solution)/shard_map/ppermute | solution.py:873
  8.0 1.2 %copy-done.2 = f32[32,32,256]{2,1,0:T(8,128)S(1)} copy-done((f32[32,32,256]{2,1,0:T(8,128)S(1)}, f32[32,32,256]{2,1,0:T(8,128)}, u32[]{:S(2)}) %copy-start.2) | copy-done | bytes 1048600
  9.2 0.7 copy-done.5
  10.6 2.4 %collective-permute-start.4 = (f32[2,256]{1,0:T(2,128)S(1)}, f32[2,256]{1,0:T(2,128)S(1)}, u32[]{:S(2)}, u32[]{:S(2)}) collective-permute-start(f32[2,256]{1,0:T(2,128)S(1)} %get-tuple-element.93), channel_id=1, source_target_pairs={{0,4},{1,5},{2,6},{3,7},{4,0},{5,1},{6,2},{7,3},{8,12},{9,13},{10,... | collective-permute-start | bytes 6152 | tf_op jit(solution)/shard_map/ppermute | solution.py:877
  13.0 4.5 %collective-permute-start.6 = (f32[22,8,256]{2,1,0:T(8,128)S(1)}, f32[22,8,256]{2,1,0:T(8,128)S(1)}, u32[]{:S(2)}, u32[]{:S(2)}) collective-permute-start(f32[22,8,256]{2,1,0:T(8,128)S(1)} %get-tuple-element.95), channel_id=1, source_target_pairs={{8,16},{16,8},{9,17},{17,9},{10,18},{18,10},{11,19},{19,11},{12,20... | collective-permute-start | bytes 540680 | tf_op jit(solution)/shard_map/ppermute | solution.py:873
  18.2 3.7 %collective-permute-start.2 = (f32[35,8,256]{2,1,0:T(8,128)S(1)}, f32[35,8,256]{2,1,0:T(8,128)S(1)}, u32[]{:S(2)}, u32[]{:S(2)}) collective-permute-start(f32[35,8,256]{2,1,0:T(8,128)S(1)} %get-tuple-element.79), channel_id=1, source_target_pairs={{8,16},{16,8},{9,17},{17,9},{10,18},{18,10},{11,19},{19,11},{12,20... | collective-permute-start | bytes 860168 | tf_op jit(solution)/shard_map/ppermute | solution.py:873
  22.1 2.2 %collective-permute-start.8 = (f32[272,256]{1,0:T(8,128)S(1)}, f32[272,256]{1,0:T(8,128)S(1)}, u32[]{:S(2)}, u32[]{:S(2)}) collective-permute-start(f32[272,256]{1,0:T(8,128)S(1)} %get-tuple-element.97), channel_id=1, source_target_pairs={{0,1},{2,3},{4,5},{6,7},{1,0},{3,2},{5,4},{7,6},{8,9},{10,11},{12,... | collective-permute-start | bytes 835592 | tf_op jit(solution)/shard_map/ppermute | solution.py:873
  25.0 4.1 %sweeps_inner.1 = (f32[32,40,256]{2,1,0:T(8,128)S(1)}, f32[32,40,256]{2,1,0:T(8,128)S(1)}, f32[32,40,256]{2,1,0:T(8,128)S(1)}, f32[32,40,256]{2,1,0:T(8,128)S(1)...) custom-call(f32[32,32,256]{2,1,0:T(8,128)S(1)} %copy-done.1, ...), custom_call_target="tpu_custom_call" | custom-call | flops 1000000 | bytes 14614528 | tf_op jit(solution)/shard_map/sweeps_inner/pallas_call | solution.py:36
  29.1 1.2 %sweeps_edge.1 = (f32[32,32,256]{2,1,0:T(8,128)S(1)}, f32[32,32,256]{2,1,0:T(8,128)S(1)}, f32[96,256]{1,0:T(8,128)S(1)}, f32[96,256]{1,0:T(8,128)S(1)}) custom-call(f32[35,8,256]{2,1,0:T(8,128)S(1)} %collective-permute-done.2.x_a, f32[35,8,256]{2,1,0:T(8,128)S(1)} %collective-permute-done.3.x_b, s32[32,32,256]{2,1,0:T(8,128)S(1)} %copy-done, ...), custom_call_target="tpu_custom_call" | custom-call | flops 1000000 | bytes 15974400 | tf_op jit(solution)/shard_map/sweeps_edge/pallas_call | solution.py:36
  31.0 5.0 %collective-permute-start.10 = (f32[96,256]{1,0:T(8,128)S(1)}, f32[96,256]{1,0:T(8,128)S(1)}, u32[]{:S(2)}, u32[]{:S(2)}) collective-permute-start(f32[96,256]{1,0:T(8,128)S(1)} %get-tuple-element.102), channel_id=1, source_target_pairs={{0,1},{2,3},{4,5},{6,7},{1,0},{3,2},{5,4},{7,6},{8,9},{10,11},{12,... | collective-permute-start | bytes 294920 | tf_op jit(solution)/shard_map/ppermute | solution.py:873
  36.0 0.8 ready.1
  36.8 0.8 %mask.1 = (f32[32,32,256]{2,1,0:T(8,128)S(1)}, f32[32,8,256]{2,1,0:T(8,128)S(1)}) custom-call(f32[32,32,256]{2,1,0:T(8,128)S(1)} %get-tuple-element.92.flux_all, f32[8,256]{1,0:T(8,128)S(1)} %pad_maximum_fusion.lists, f32[272,256]{1,0:T(8,128)S(1)} %collective-permute-done.8.far.yy_b.r_b.far_b), custom_call_target="tpu_custom_call" | custom-call | flops 1000000 | bytes 2646016 | tf_op jit(solution)/shard_map/mask/pallas_call | solution.py:36
  38.1 5.2 %collective-permute-start.11 = (f32[15,8,256]{2,1,0:T(8,128)S(1)}, f32[15,8,256]{2,1,0:T(8,128)S(1)}, u32[]{:S(2)}, u32[]{:S(2)}) collective-permute-start(f32[15,8,256]{2,1,0:T(8,128)S(1)} %get-tuple-element.105), channel_id=1, source_target_pairs={{8,16},{16,8},{9,17},{17,9},{10,18},{18,10},{11,19},{19,11},{12,20... | collective-permute-start | bytes 368648 | tf_op jit(solution)/shard_map/ppermute | solution.py:873
  43.3 3.3 %potential_inner.1 = (f32[40,40,256]{2,1,0:T(8,128)S(1)}, f32[40,40,256]{2,1,0:T(8,128)S(1)}, f32[40,40,256]{2,1,0:T(8,128)S(1)}, f32[16,16,256]{2,1,0:T(8,128)S(1)}, f32[40,40,256]{2,1,0:T(8,128)S(1)}) custom-call(f32[32,32,256]{2,1,0:T(8,128)S(1)} %get-tuple-element.98.flux, f32[32,8,256]{2,1,0:T(8,128)S(1)} %get-tuple-element.103.mask, ...), custom_call_target="tpu_custom_call" | custom-call | flops 1000000 | bytes 13557760 | tf_op jit(solution)/shard_map/potential_inner/pallas_call | solution.py:36
  47.9 4.8 %collective-permute-start.15 = (f32[64,256]{1,0:T(8,128)S(1)}, f32[64,256]{1,0:T(8,128)S(1)}, u32[]{:S(2)}, u32[]{:S(2)}) collective-permute-start(f32[64,256]{1,0:T(8,128)S(1)} %get-tuple-element.117), channel_id=1, source_target_pairs={{0,1},{2,3},{4,5},{6,7},{1,0},{3,2},{5,4},{7,6},{8,9},{10,11},{12,... | collective-permute-start | bytes 196616 | tf_op jit(solution)/shard_map/ppermute | solution.py:873
  52.7 1.2 %coarse_ready.1 = (f32[8,8,256]{2,1,0:T(8,128)S(1)}, f32[8,128]{1,0:T(8,128)S(1)}, f32[8,128]{1,0:T(8,128)S(1)}) custom-call(f32[8,8,256]{2,1,0:T(8,128)S(1)} %get-tuple-element.78.token.coarse.own, f32[264,256]{1,0:T(8,128)S(1)} %collective-permute-done.13.yy_a.r_a.far_a, f32[272,256]{1,0:T(8,128)S(1)} %collective-permute-done.8.far.yy_b.r_b.far_b), custom_call_target="tpu_custom_call" | custom-call | flops 1000000 | bytes 688128 | tf_op jit(solution)/shard_map/coarse_ready/pallas_call | solution.py:36
  53.9 1.4 %store.1 = (f32[32,32,256]{2,1,0:T(8,128)}, f32[32,32,256]{2,1,0:T(8,128)}, f32[8,128]{1,0:T(8,128)S(1)}) custom-call(f32[32,32,256]{2,1,0:T(8,128)S(1)} %get-tuple-element.91.conc, f32[32,32,256]{2,1,0:T(8,128)S(1)} %get-tuple-element.98.flux), custom_call_target="tpu_custom_call" | custom-call | flops 1000000 | bytes 4198400 | tf_op jit(solution)/shard_map/store/pallas_call | solution.py:36
  55.4 3.4 %collective-permute-start.16 = (f32[12,8,256]{2,1,0:T(8,128)S(1)}, f32[12,8,256]{2,1,0:T(8,128)S(1)}, u32[]{:S(2)}, u32[]{:S(2)}) collective-permute-start(f32[12,8,256]{2,1,0:T(8,128)S(1)} %get-tuple-element.120), channel_id=1, source_target_pairs={{8,16},{16,8},{9,17},{17,9},{10,18},{18,10},{11,19},{19,11},{12,20... | collective-permute-start | bytes 294920 | tf_op jit(solution)/shard_map/ppermute | solution.py:873
  58.8 2.5 %collective-permute-done.16.x_a = f32[12,8,256]{2,1,0:T(8,128)S(1)} collective-permute-done((f32[12,8,256]{2,1,0:T(8,128)S(1)}, f32[12,8,256]{2,1,0:T(8,128)S(1)}, u32[]{:S(2)}, u32[]{:S(2)}) %collective-permute-start.16) | collective-permute-done | bytes 98336 | tf_op jit(solution)/shard_map/ppermute | solution.py:873
  61.3 1.1 %middle.1 = (f32[24,24,256]{2,1,0:T(8,128)S(1)}, f32[24,24,256]{2,1,0:T(8,128)S(1)}, f32[24,24,256]{2,1,0:T(8,128)S(1)}, f32[8,12,256]{2,1,0:T(8,128)S(1)}, f32[...) custom-call(f32[16,16,256]{2,1,0:T(8,128)S(1)} %get-tuple-element.115.field.source_, ...), custom_call_target="tpu_custom_call" | custom-call | flops 1000000 | bytes 3960832 | tf_op jit(solution)/shard_map/middle/pallas_call | solution.py:36
  62.3 2.2 %collective-permute-start.19 = (f32[80,256]{1,0:T(8,128)S(1)}, f32[80,256]{1,0:T(8,128)S(1)}, u32[]{:S(2)}, u32[]{:S(2)}) collective-permute-start(f32[80,256]{1,0:T(8,128)S(1)} %get-tuple-element.127), channel_id=1, source_target_pairs={{0,1},{2,3},{4,5},{6,7},{1,0},{3,2},{5,4},{7,6},{8,9},{10,11},{12,... | collective-permute-start | bytes 245768 | tf_op jit(solution)/shard_map/ppermute | solution.py:873
  65.2 1.2 %collective-permute-done.19.r_b = f32[80,256]{1,0:T(8,128)S(1)} collective-permute-done((f32[80,256]{1,0:T(8,128)S(1)}, f32[80,256]{1,0:T(8,128)S(1)}, u32[]{:S(2)}, u32[]{:S(2)}) %collective-permute-start.19) | collective-permute-done | bytes 81952 | tf_op jit(solution)/shard_map/ppermute | solution.py:873
  66.4 1.6 %collective-permute-start.20 = (f32[8,256]{1,0:T(8,128)S(1)}, f32[8,256]{1,0:T(8,128)S(1)}, u32[]{:S(2)}, u32[]{:S(2)}) collective-permute-start(f32[8,256]{1,0:T(8,128)S(1)} %slice_add_fusion), channel_id=1, source_target_pairs={{0,2},{1,3},{2,0},{3,1},{4,6},{5,7},{6,4},{7,5},{8,10},{9,11},{10,... | collective-permute-start | bytes 24584 | tf_op jit(solution)/shard_map/ppermute | solution.py:877
  68.0 1.8 %collective-permute-done.20 = f32[8,256]{1,0:T(8,128)S(1)} collective-permute-done((f32[8,256]{1,0:T(8,128)S(1)}, f32[8,256]{1,0:T(8,128)S(1)}, u32[]{:S(2)}, u32[]{:S(2)}) %collective-permute-start.20) | collective-permute-done | bytes 8224 | tf_op jit(solution)/shard_map/ppermute | solution.py:877
  69.8 2.9 %collective-permute-start.21 = (f32[8,256]{1,0:T(8,128)S(1)}, f32[8,256]{1,0:T(8,128)S(1)}, u32[]{:S(2)}, u32[]{:S(2)}) collective-permute-start(f32[8,256]{1,0:T(8,128)S(1)} %add.10), channel_id=1, source_target_pairs={{0,4},{1,5},{2,6},{3,7},{4,0},{5,1},{6,2},{7,3},{8,12},{9,13},{10,... | collective-permute-start | bytes 24584 | tf_op jit(solution)/shard_map/ppermute | solution.py:877
  72.7 1.2 %coarse.1.error = f32[8,16,256]{2,1,0:T(8,128)S(1)} custom-call(f32[8,12,256]{2,1,0:T(8,128)S(1)} %get-tuple-element.124.own, f32[8,12,256]{2,1,0:T(8,128)S(1)} %get-tuple-element.125.conduct, f32[264,256]{1,0:T(8,128)S(1)} %collective-permute-done.13.yy_a.r_a.far_a, f32[272,256]{1,0:T(8,128)S(1)} %collective-permute-done.8.far.yy_b.r_b.far_b, ...), custom_call_target="tpu_custom_call" | custom-call | flops 1000000 | bytes 1032192 | tf_op jit(solution)/shard_map/coarse/pallas_call | solution.py:36
  73.8 2.9 %finish_early.1 = (f32[8,16,256]{2,1,0:T(8,128)S(1)}, f32[2,16,256]{2,1,0:T(8,128)S(1)}, f32[2,16,256]{2,1,0:T(8,128)S(1)}, f32[32,32,256]{2,1,0:T(8,128)}, f32[...) custom-call(f32[8,16,256]{2,1,0:T(8,128)S(1)} %coarse.1.error, ...), custom_call_target="tpu_custom_call" | custom-call | flops 1000000 | bytes 8593408 | tf_op jit(solution)/shard_map/finish_early/pallas_call | solution.py:36
  76.7 3.0 %collective-permute-start.22 = (f32[2,16,256]{2,1,0:T(8,128)S(1)}, f32[2,16,256]{2,1,0:T(8,128)S(1)}, u32[]{:S(2)}, u32[]{:S(2)}) collective-permute-start(f32[2,16,256]{2,1,0:T(8,128)S(1)} %get-tuple-element.132), channel_id=1, source_target_pairs={{8,16},{16,8},{9,17},{17,9},{10,18},{18,10},{11,19},{19,11},{12,20... | collective-permute-start | bytes 98312 | tf_op jit(solution)/shard_map/ppermute | solution.py:873
  79.9 2.0 %collective-permute-done.22.x_a = f32[2,16,256]{2,1,0:T(8,128)S(1)} collective-permute-done((f32[2,16,256]{2,1,0:T(8,128)S(1)}, f32[2,16,256]{2,1,0:T(8,128)S(1)}, u32[]{:S(2)}, u32[]{:S(2)}) %collective-permute-start.22) | collective-permute-done | bytes 32800 | tf_op jit(solution)/shard_map/ppermute | solution.py:873
  82.0 1.7 %finish_edge.1 = f32[32,32,256]{2,1,0:T(8,128)} custom-call(f32[2,16,256]{2,1,0:T(8,128)S(1)} %collective-permute-done.22.x_a, f32[2,16,256]{2,1,0:T(8,128)S(1)} %collective-permute-done.23.x_b, f32[24,24,256]{2,1,0:T(8,128)S(1)} %get-tuple-element.129.rest_0_.mid_two, ...), custom_call_target="tpu_custom_call", output_to_operand_aliasing={{}: (14, {})} | custom-call | flops 1000000 | bytes 10682368 | tf_op jit(solution)/shard_map/finish_edge/pallas_call | solution.py:36
  (52 shorter events, 5.6 us)
Async XLA Ops:
  0.6 7.4 %copy-start.1 = (f32[32,32,256]{2,1,0:T(8,128)S(1)}, f32[32,32,256]{2,1,0:T(8,128)}, u32[]{:S(2)}) copy-start(f32[32,32,256]{2,1,0:T(8,128)} %conc.9) | copy-start | bytes 3145732
  0.6 7.4 %copy-start = (s32[32,32,256]{2,1,0:T(8,128)S(1)}, s32[32,32,256]{2,1,0:T(8,128)}, u32[]{:S(2)}) copy-start(s32[32,32,256]{2,1,0:T(8,128)} %label.11) | copy-start | bytes 3145732
  2.7 15.0 %collective-permute-start = (f32[224,256]{1,0:T(8,128)}, f32[224,256]{1,0:T(8,128)S(1)}, u32[]{:S(2)}, u32[]{:S(2)}) collective-permute-start(f32[224,256]{1,0:T(8,128)} %get-tuple-element.75), channel_id=1, source_target_pairs={{1,2},{3,4},{5,6},{2,1},{4,3},{6,5},{9,10},{11,12},{13,14},{10,9},... | collective-permute-start | bytes 688136 | tf_op jit(solution)/shard_map/ppermute | solution.py:873
  3.4 14.7 %collective-permute-start.1 = (f32[224,256]{1,0:T(8,128)}, f32[224,256]{1,0:T(8,128)S(1)}, u32[]{:S(2)}, u32[]{:S(2)}) collective-permute-start(f32[224,256]{1,0:T(8,128)} %get-tuple-element.76), channel_id=1, source_target_pairs={{0,1},{2,3},{4,5},{6,7},{1,0},{3,2},{5,4},{7,6},{8,9},{10,11},{12,... | collective-permute-start | bytes 688136 | tf_op jit(solution)/shard_map/ppermute | solution.py:873
  8.0 1.2 %copy-start.2 = (f32[32,32,256]{2,1,0:T(8,128)S(1)}, f32[32,32,256]{2,1,0:T(8,128)}, u32[]{:S(2)}) copy-start(f32[32,32,256]{2,1,0:T(8,128)} %phi.9) | copy-start | bytes 3145732
  9.2 0.7 copy-start.5
  10.6 11.4 %copy-start.3 = (f32[32,32,256]{2,1,0:T(8,128)S(1)}, f32[32,32,256]{2,1,0:T(8,128)}, u32[]{:S(2)}) copy-start(f32[32,32,256]{2,1,0:T(8,128)} %phi.9) | copy-start | bytes 3145732
  10.6 7.0 %collective-permute-start.4 = (f32[2,256]{1,0:T(2,128)S(1)}, f32[2,256]{1,0:T(2,128)S(1)}, u32[]{:S(2)}, u32[]{:S(2)}) collective-permute-start(f32[2,256]{1,0:T(2,128)S(1)} %get-tuple-element.93), channel_id=1, source_target_pairs={{0,4},{1,5},{2,6},{3,7},{4,0},{5,1},{6,2},{7,3},{8,12},{9,13},{10,... | collective-permute-start | bytes 6152 | tf_op jit(solution)/shard_map/ppermute | solution.py:877
  13.0 9.0 %collective-permute-start.6 = (f32[22,8,256]{2,1,0:T(8,128)S(1)}, f32[22,8,256]{2,1,0:T(8,128)S(1)}, u32[]{:S(2)}, u32[]{:S(2)}) collective-permute-start(f32[22,8,256]{2,1,0:T(8,128)S(1)} %get-tuple-element.95), channel_id=1, source_target_pairs={{8,16},{16,8},{9,17},{17,9},{10,18},{18,10},{11,19},{19,11},{12,20... | collective-permute-start | bytes 540680 | tf_op jit(solution)/shard_map/ppermute | solution.py:873
  17.5 4.5 %collective-permute-start.7 = (f32[22,8,256]{2,1,0:T(8,128)S(1)}, f32[22,8,256]{2,1,0:T(8,128)S(1)}, u32[]{:S(2)}, u32[]{:S(2)}) collective-permute-start(f32[22,8,256]{2,1,0:T(8,128)S(1)} %get-tuple-element.96), channel_id=1, source_target_pairs={{0,8},{16,24},{8,0},{24,16},{1,9},{17,25},{9,1},{25,17},{2,10},{18... | collective-permute-start | bytes 540680 | tf_op jit(solution)/shard_map/ppermute | solution.py:873
  17.6 4.3 %collective-permute-start.5 = (f32[4,256]{1,0:T(4,128)S(1)}, f32[4,256]{1,0:T(4,128)S(1)}, u32[]{:S(2)}, u32[]{:S(2)}) collective-permute-start(f32[4,256]{1,0:T(4,128)S(1)} %pad_maximum_fusion.1), channel_id=1, source_target_pairs={{0,2},{1,3},{2,0},{3,1},{4,6},{5,7},{6,4},{7,5},{8,10},{9,11},{10,... | collective-permute-start | bytes 12296 | tf_op jit(solution)/shard_map/ppermute | solution.py:877
  18.1 6.9 %copy-start.4 = (f32[32,32,256]{2,1,0:T(8,128)S(1)}, f32[32,32,256]{2,1,0:T(8,128)}, u32[]{:S(2)}) copy-start(f32[32,32,256]{2,1,0:T(8,128)} %solid.3) | copy-start | bytes 3145732
  18.2 10.9 %collective-permute-start.2 = (f32[35,8,256]{2,1,0:T(8,128)S(1)}, f32[35,8,256]{2,1,0:T(8,128)S(1)}, u32[]{:S(2)}, u32[]{:S(2)}) collective-permute-start(f32[35,8,256]{2,1,0:T(8,128)S(1)} %get-tuple-element.79), channel_id=1, source_target_pairs={{8,16},{16,8},{9,17},{17,9},{10,18},{18,10},{11,19},{19,11},{12,20... | collective-permute-start | bytes 860168 | tf_op jit(solution)/shard_map/ppermute | solution.py:873
  21.9 7.2 %collective-permute-start.3 = (f32[35,8,256]{2,1,0:T(8,128)S(1)}, f32[35,8,256]{2,1,0:T(8,128)S(1)}, u32[]{:S(2)}, u32[]{:S(2)}) collective-permute-start(f32[35,8,256]{2,1,0:T(8,128)S(1)} %get-tuple-element.80), channel_id=1, source_target_pairs={{0,8},{16,24},{8,0},{24,16},{1,9},{17,25},{9,1},{25,17},{2,10},{18... | collective-permute-start | bytes 860168 | tf_op jit(solution)/shard_map/ppermute | solution.py:873
  22.1 14.6 %collective-permute-start.8 = (f32[272,256]{1,0:T(8,128)S(1)}, f32[272,256]{1,0:T(8,128)S(1)}, u32[]{:S(2)}, u32[]{:S(2)}) collective-permute-start(f32[272,256]{1,0:T(8,128)S(1)} %get-tuple-element.97), channel_id=1, source_target_pairs={{0,1},{2,3},{4,5},{6,7},{1,0},{3,2},{5,4},{7,6},{8,9},{10,11},{12,... | collective-permute-start | bytes 835592 | tf_op jit(solution)/shard_map/ppermute | solution.py:873
  24.3 19.0 %collective-permute-start.13 = (f32[264,256]{1,0:T(8,128)S(1)}, f32[264,256]{1,0:T(8,128)S(1)}, u32[]{:S(2)}, u32[]{:S(2)}) collective-permute-start(f32[264,256]{1,0:T(8,128)S(1)} %get-tuple-element.109), channel_id=1, source_target_pairs={{1,2},{3,4},{5,6},{2,1},{4,3},{6,5},{9,10},{11,12},{13,14},{10,9},... | collective-permute-start | bytes 811016 | tf_op jit(solution)/shard_map/ppermute | solution.py:873
  30.3 7.3 %collective-permute-start.9 = (f32[96,256]{1,0:T(8,128)S(1)}, f32[96,256]{1,0:T(8,128)S(1)}, u32[]{:S(2)}, u32[]{:S(2)}) collective-permute-start(f32[96,256]{1,0:T(8,128)S(1)} %get-tuple-element.101), channel_id=1, source_target_pairs={{1,2},{3,4},{5,6},{2,1},{4,3},{6,5},{9,10},{11,12},{13,14},{10,9},... | collective-permute-start | bytes 294920 | tf_op jit(solution)/shard_map/ppermute | solution.py:873
  31.0 7.0 %collective-permute-start.10 = (f32[96,256]{1,0:T(8,128)S(1)}, f32[96,256]{1,0:T(8,128)S(1)}, u32[]{:S(2)}, u32[]{:S(2)}) collective-permute-start(f32[96,256]{1,0:T(8,128)S(1)} %get-tuple-element.102), channel_id=1, source_target_pairs={{0,1},{2,3},{4,5},{6,7},{1,0},{3,2},{5,4},{7,6},{8,9},{10,11},{12,... | collective-permute-start | bytes 294920 | tf_op jit(solution)/shard_map/ppermute | solution.py:873
  38.1 8.5 %collective-permute-start.11 = (f32[15,8,256]{2,1,0:T(8,128)S(1)}, f32[15,8,256]{2,1,0:T(8,128)S(1)}, u32[]{:S(2)}, u32[]{:S(2)}) collective-permute-start(f32[15,8,256]{2,1,0:T(8,128)S(1)} %get-tuple-element.105), channel_id=1, source_target_pairs={{8,16},{16,8},{9,17},{17,9},{10,18},{18,10},{11,19},{19,11},{12,20... | collective-permute-start | bytes 368648 | tf_op jit(solution)/shard_map/ppermute | solution.py:873
  43.2 3.4 %collective-permute-start.12 = (f32[15,8,256]{2,1,0:T(8,128)S(1)}, f32[15,8,256]{2,1,0:T(8,128)S(1)}, u32[]{:S(2)}, u32[]{:S(2)}) collective-permute-start(f32[15,8,256]{2,1,0:T(8,128)S(1)} %get-tuple-element.106), channel_id=1, source_target_pairs={{0,8},{16,24},{8,0},{24,16},{1,9},{17,25},{9,1},{25,17},{2,10},{18... | collective-permute-start | bytes 368648 | tf_op jit(solution)/shard_map/ppermute | solution.py:873
  47.3 8.0 %collective-permute-start.14 = (f32[64,256]{1,0:T(8,128)S(1)}, f32[64,256]{1,0:T(8,128)S(1)}, u32[]{:S(2)}, u32[]{:S(2)}) collective-permute-start(f32[64,256]{1,0:T(8,128)S(1)} %get-tuple-element.116), channel_id=1, source_target_pairs={{1,2},{3,4},{5,6},{2,1},{4,3},{6,5},{9,10},{11,12},{13,14},{10,9},... | collective-permute-start | bytes 196616 | tf_op jit(solution)/shard_map/ppermute | solution.py:873
  47.9 7.4 %collective-permute-start.15 = (f32[64,256]{1,0:T(8,128)S(1)}, f32[64,256]{1,0:T(8,128)S(1)}, u32[]{:S(2)}, u32[]{:S(2)}) collective-permute-start(f32[64,256]{1,0:T(8,128)S(1)} %get-tuple-element.117), channel_id=1, source_target_pairs={{0,1},{2,3},{4,5},{6,7},{1,0},{3,2},{5,4},{7,6},{8,9},{10,11},{12,... | collective-permute-start | bytes 196616 | tf_op jit(solution)/shard_map/ppermute | solution.py:873
  55.4 5.9 %collective-permute-start.16 = (f32[12,8,256]{2,1,0:T(8,128)S(1)}, f32[12,8,256]{2,1,0:T(8,128)S(1)}, u32[]{:S(2)}, u32[]{:S(2)}) collective-permute-start(f32[12,8,256]{2,1,0:T(8,128)S(1)} %get-tuple-element.120), channel_id=1, source_target_pairs={{8,16},{16,8},{9,17},{17,9},{10,18},{18,10},{11,19},{19,11},{12,20... | collective-permute-start | bytes 294920 | tf_op jit(solution)/shard_map/ppermute | solution.py:873
  58.7 2.6 %collective-permute-start.17 = (f32[12,8,256]{2,1,0:T(8,128)S(1)}, f32[12,8,256]{2,1,0:T(8,128)S(1)}, u32[]{:S(2)}, u32[]{:S(2)}) collective-permute-start(f32[12,8,256]{2,1,0:T(8,128)S(1)} %get-tuple-element.121), channel_id=1, source_target_pairs={{0,8},{16,24},{8,0},{24,16},{1,9},{17,25},{9,1},{25,17},{2,10},{18... | collective-permute-start | bytes 294920 | tf_op jit(solution)/shard_map/ppermute | solution.py:873
  62.3 4.1 %collective-permute-start.19 = (f32[80,256]{1,0:T(8,128)S(1)}, f32[80,256]{1,0:T(8,128)S(1)}, u32[]{:S(2)}, u32[]{:S(2)}) collective-permute-start(f32[80,256]{1,0:T(8,128)S(1)} %get-tuple-element.127), channel_id=1, source_target_pairs={{0,1},{2,3},{4,5},{6,7},{1,0},{3,2},{5,4},{7,6},{8,9},{10,11},{12,... | collective-permute-start | bytes 245768 | tf_op jit(solution)/shard_map/ppermute | solution.py:873
  64.6 8.1 %collective-permute-start.18 = (f32[72,256]{1,0:T(8,128)S(1)}, f32[72,256]{1,0:T(8,128)S(1)}, u32[]{:S(2)}, u32[]{:S(2)}) collective-permute-start(f32[72,256]{1,0:T(8,128)S(1)} %get-tuple-element.126), channel_id=1, source_target_pairs={{1,2},{3,4},{5,6},{2,1},{4,3},{6,5},{9,10},{11,12},{13,14},{10,9},... | collective-permute-start | bytes 221192 | tf_op jit(solution)/shard_map/ppermute | solution.py:873
  66.4 3.4 %collective-permute-start.20 = (f32[8,256]{1,0:T(8,128)S(1)}, f32[8,256]{1,0:T(8,128)S(1)}, u32[]{:S(2)}, u32[]{:S(2)}) collective-permute-start(f32[8,256]{1,0:T(8,128)S(1)} %slice_add_fusion), channel_id=1, source_target_pairs={{0,2},{1,3},{2,0},{3,1},{4,6},{5,7},{6,4},{7,5},{8,10},{9,11},{10,... | collective-permute-start | bytes 24584 | tf_op jit(solution)/shard_map/ppermute | solution.py:877
  69.8 4.1 %collective-permute-start.21 = (f32[8,256]{1,0:T(8,128)S(1)}, f32[8,256]{1,0:T(8,128)S(1)}, u32[]{:S(2)}, u32[]{:S(2)}) collective-permute-start(f32[8,256]{1,0:T(8,128)S(1)} %add.10), channel_id=1, source_target_pairs={{0,4},{1,5},{2,6},{3,7},{4,0},{5,1},{6,2},{7,3},{8,12},{9,13},{10,... | collective-permute-start | bytes 24584 | tf_op jit(solution)/shard_map/ppermute | solution.py:877
  76.7 5.2 %collective-permute-start.22 = (f32[2,16,256]{2,1,0:T(8,128)S(1)}, f32[2,16,256]{2,1,0:T(8,128)S(1)}, u32[]{:S(2)}, u32[]{:S(2)}) collective-permute-start(f32[2,16,256]{2,1,0:T(8,128)S(1)} %get-tuple-element.132), channel_id=1, source_target_pairs={{8,16},{16,8},{9,17},{17,9},{10,18},{18,10},{11,19},{19,11},{12,20... | collective-permute-start | bytes 98312 | tf_op jit(solution)/shard_map/ppermute | solution.py:873
  79.8 2.2 %collective-permute-start.23 = (f32[2,16,256]{2,1,0:T(8,128)S(1)}, f32[2,16,256]{2,1,0:T(8,128)S(1)}, u32[]{:S(2)}, u32[]{:S(2)}) collective-permute-start(f32[2,16,256]{2,1,0:T(8,128)S(1)} %get-tuple-element.133), channel_id=1, source_target_pairs={{0,8},{16,24},{8,0},{24,16},{1,9},{17,25},{9,1},{25,17},{2,10},{18... | collective-permute-start | bytes 98312 | tf_op jit(solution)/shard_map/ppermute | solution.py:873

commit v15 on v14

--- a/solution.py
+++ b/solution.py
@@ -464,7 +464,7 @@
             field[HALO + nx + k, 8 * t : 8 * t + 8, :] = after
 
 
-def flux_pack_x_kernel(flux, r_a, r_b, mask, token, pay_a, pay_b):
+def flux_pack_x_kernel(flux, r_b, r_a, mask, token, pay_a, pay_b):
     nx = flux.shape[0]
 
     def tile(x, t):
@@ -960,7 +960,7 @@
         name="ready",
     )
     pay_a, pay_b = call(
-        flux_pack_x_kernel, [shaped(15, 8, 256)] * 2, [flux_own, f_a, f_b, halo_mask, made], name="flux_pack_x"
+        flux_pack_x_kernel, [shaped(15, 8, 256)] * 2, [flux_own, f_b, f_a, halo_mask, made], name="flux_pack_x"
     )
     fx_a, fx_b = swap(pay_a, pay_b, "grp")
     fine_two, fine_source, fine_first, inner_mid, field = call(

time: 84.3 us -> 84 us (level)
  starting transfers between devices: 49.1 us -> 47.9 us
  waiting for transfers between devices: 8.3 us -> 9.22 us
    ppermute x10, starting transfers between devices: 19.2 us -> 17.7 us  [swap(): lax.ppermute(pay_b, axis, both_ways(pairs_b))]
    ppermute x10, waiting for transfers between devices: 1.97 us -> 2.94 us  [swap(): lax.ppermute(pay_b, axis, both_ways(pairs_b))]
  transfers between devices with their start and end apart: 24 -> 24, of which waited for: 6 -> 7; matrix products, arithmetic and copies ran while one was open for 0% -> 0% of each run, Pallas kernels for 18% -> 18%
where the time goes in v15:
time: 84 us; the launch traced here: 83.5 us
  starting transfers between devices  47.9 us (57%)
  Pallas kernels  23.2 us (28%)
  waiting for transfers between devices  9.22 us (11%)
  local copies, waits for them, and re-layouts  1.94 us (2%)
  between operations  1.21 us (1%)
    pallas_call x19, Pallas kernels, call(): pl.pallas_call(kernel, out_shape=tuple(outs), in_specs=in_specs or [WHOLE...  23.2 us
    ppermute x10, starting transfers between devices, swap(): lax.ppermute(pay_a, axis, both_ways(pairs_a))  23.2 us
    ppermute x10, starting transfers between devices, swap(): lax.ppermute(pay_b, axis, both_ways(pairs_b))  17.7 us
    ppermute x4, starting transfers between devices, exchange(): lax.ppermute(value, 'dev', [(i, i ^ distance) for i in range(lax.axis_siz...  7.06 us
    ppermute x10, waiting for transfers between devices, swap(): lax.ppermute(pay_a, axis, both_ways(pairs_a))  4.74 us
    ppermute x10, waiting for transfers between devices, swap(): lax.ppermute(pay_b, axis, both_ways(pairs_b))  2.94 us
    unnamed x12, local copies, waits for them, and re-layouts  1.94 us
  transfers between devices with their start and end apart: 24, of which 7 were waited for; matrix products, arithmetic and copies ran while one was open for 0% of the time, Pallas kernels for 18%

profile of v15, /device:TPU:1, one launch (start us, length us, event | category | flops | bytes accessed | tf_op | source)
XLA Modules:
  0.0 83.5 jit_solution(11922192038446860357)
XLA Ops:
  0.7 2.1 %first_pack.1 = (f32[224,256]{1,0:T(8,128)}, f32[224,256]{1,0:T(8,128)}, f32[8,256]{1,0:T(8,128)}) custom-call(f32[32,32,256]{2,1,0:T(8,128)} %conc.9, s32[32,32,256]{2,1,0:T(8,128)} %label.11, s32[1,256]{1,0:T(1,128)} %bitcast.1, s32[1,256]{1,0:T(1,128)} %block.1), custom_call_target="tpu_custom_call" | custom-call | flops 1000000 | bytes 2566144 | tf_op jit(solution)/shard_map/first_pack/pallas_call | solution.py:36
  3.4 4.6 %collective-permute-start.1 = (f32[224,256]{1,0:T(8,128)}, f32[224,256]{1,0:T(8,128)S(1)}, u32[]{:S(2)}, u32[]{:S(2)}) collective-permute-start(f32[224,256]{1,0:T(8,128)} %get-tuple-element.76), channel_id=1, source_target_pairs={{0,1},{2,3},{4,5},{6,7},{1,0},{3,2},{5,4},{7,6},{8,9},{10,11},{12,... | collective-permute-start | bytes 688136 | tf_op jit(solution)/shard_map/ppermute | solution.py:873
  8.0 1.2 %copy-done.2 = f32[32,32,256]{2,1,0:T(8,128)S(1)} copy-done((f32[32,32,256]{2,1,0:T(8,128)S(1)}, f32[32,32,256]{2,1,0:T(8,128)}, u32[]{:S(2)}) %copy-start.2) | copy-done | bytes 1048600
  9.2 0.7 copy-done.5
  10.6 2.4 %collective-permute-start.4 = (f32[2,256]{1,0:T(2,128)S(1)}, f32[2,256]{1,0:T(2,128)S(1)}, u32[]{:S(2)}, u32[]{:S(2)}) collective-permute-start(f32[2,256]{1,0:T(2,128)S(1)} %get-tuple-element.93), channel_id=1, source_target_pairs={{0,4},{1,5},{2,6},{3,7},{4,0},{5,1},{6,2},{7,3},{8,12},{9,13},{10,... | collective-permute-start | bytes 6152 | tf_op jit(solution)/shard_map/ppermute | solution.py:877
  13.0 4.5 %collective-permute-start.6 = (f32[22,8,256]{2,1,0:T(8,128)S(1)}, f32[22,8,256]{2,1,0:T(8,128)S(1)}, u32[]{:S(2)}, u32[]{:S(2)}) collective-permute-start(f32[22,8,256]{2,1,0:T(8,128)S(1)} %get-tuple-element.95), channel_id=1, source_target_pairs={{8,16},{16,8},{9,17},{17,9},{10,18},{18,10},{11,19},{19,11},{12,20... | collective-permute-start | bytes 540680 | tf_op jit(solution)/shard_map/ppermute | solution.py:873
  18.2 3.7 %collective-permute-start.2 = (f32[35,8,256]{2,1,0:T(8,128)S(1)}, f32[35,8,256]{2,1,0:T(8,128)S(1)}, u32[]{:S(2)}, u32[]{:S(2)}) collective-permute-start(f32[35,8,256]{2,1,0:T(8,128)S(1)} %get-tuple-element.79), channel_id=1, source_target_pairs={{8,16},{16,8},{9,17},{17,9},{10,18},{18,10},{11,19},{19,11},{12,20... | collective-permute-start | bytes 860168 | tf_op jit(solution)/shard_map/ppermute | solution.py:873
  22.1 2.2 %collective-permute-start.8 = (f32[272,256]{1,0:T(8,128)S(1)}, f32[272,256]{1,0:T(8,128)S(1)}, u32[]{:S(2)}, u32[]{:S(2)}) collective-permute-start(f32[272,256]{1,0:T(8,128)S(1)} %get-tuple-element.97), channel_id=1, source_target_pairs={{0,1},{2,3},{4,5},{6,7},{1,0},{3,2},{5,4},{7,6},{8,9},{10,11},{12,... | collective-permute-start | bytes 835592 | tf_op jit(solution)/shard_map/ppermute | solution.py:873
  25.0 4.1 %sweeps_inner.1 = (f32[32,40,256]{2,1,0:T(8,128)S(1)}, f32[32,40,256]{2,1,0:T(8,128)S(1)}, f32[32,40,256]{2,1,0:T(8,128)S(1)}, f32[32,40,256]{2,1,0:T(8,128)S(1)...) custom-call(f32[32,32,256]{2,1,0:T(8,128)S(1)} %copy-done.1, ...), custom_call_target="tpu_custom_call" | custom-call | flops 1000000 | bytes 14614528 | tf_op jit(solution)/shard_map/sweeps_inner/pallas_call | solution.py:36
  29.1 1.2 %sweeps_edge.1 = (f32[32,32,256]{2,1,0:T(8,128)S(1)}, f32[32,32,256]{2,1,0:T(8,128)S(1)}, f32[96,256]{1,0:T(8,128)S(1)}, f32[96,256]{1,0:T(8,128)S(1)}) custom-call(f32[35,8,256]{2,1,0:T(8,128)S(1)} %collective-permute-done.2.x_a, f32[35,8,256]{2,1,0:T(8,128)S(1)} %collective-permute-done.3.x_b, s32[32,32,256]{2,1,0:T(8,128)S(1)} %copy-done, ...), custom_call_target="tpu_custom_call" | custom-call | flops 1000000 | bytes 15974400 | tf_op jit(solution)/shard_map/sweeps_edge/pallas_call | solution.py:36
  30.3 3.8 %collective-permute-start.9 = (f32[96,256]{1,0:T(8,128)S(1)}, f32[96,256]{1,0:T(8,128)S(1)}, u32[]{:S(2)}, u32[]{:S(2)}) collective-permute-start(f32[96,256]{1,0:T(8,128)S(1)} %get-tuple-element.101), channel_id=1, source_target_pairs={{0,1},{2,3},{4,5},{6,7},{1,0},{3,2},{5,4},{7,6},{8,9},{10,11},{12,... | collective-permute-start | bytes 294920 | tf_op jit(solution)/shard_map/ppermute | solution.py:873
  34.8 0.8 ready.1
  35.6 0.8 %mask.1 = (f32[32,32,256]{2,1,0:T(8,128)S(1)}, f32[32,8,256]{2,1,0:T(8,128)S(1)}) custom-call(f32[32,32,256]{2,1,0:T(8,128)S(1)} %get-tuple-element.92.flux_all, f32[8,256]{1,0:T(8,128)S(1)} %pad_maximum_fusion.lists, f32[272,256]{1,0:T(8,128)S(1)} %collective-permute-done.8.far.yy_b.r_b.far_b), custom_call_target="tpu_custom_call" | custom-call | flops 1000000 | bytes 2646016 | tf_op jit(solution)/shard_map/mask/pallas_call | solution.py:36
  36.5 1.2 %collective-permute-done.9.r_b.y_b = f32[96,256]{1,0:T(8,128)S(1)} collective-permute-done((f32[96,256]{1,0:T(8,128)S(1)}, f32[96,256]{1,0:T(8,128)S(1)}, u32[]{:S(2)}, u32[]{:S(2)}) %collective-permute-start.9) | collective-permute-done | bytes 98336 | tf_op jit(solution)/shard_map/ppermute | solution.py:873
  37.8 5.5 %collective-permute-start.11 = (f32[15,8,256]{2,1,0:T(8,128)S(1)}, f32[15,8,256]{2,1,0:T(8,128)S(1)}, u32[]{:S(2)}, u32[]{:S(2)}) collective-permute-start(f32[15,8,256]{2,1,0:T(8,128)S(1)} %get-tuple-element.105), channel_id=1, source_target_pairs={{8,16},{16,8},{9,17},{17,9},{10,18},{18,10},{11,19},{19,11},{12,20... | collective-permute-start | bytes 368648 | tf_op jit(solution)/shard_map/ppermute | solution.py:873
  43.3 3.3 %potential_inner.1 = (f32[40,40,256]{2,1,0:T(8,128)S(1)}, f32[40,40,256]{2,1,0:T(8,128)S(1)}, f32[40,40,256]{2,1,0:T(8,128)S(1)}, f32[16,16,256]{2,1,0:T(8,128)S(1)}, f32[40,40,256]{2,1,0:T(8,128)S(1)}) custom-call(f32[32,32,256]{2,1,0:T(8,128)S(1)} %get-tuple-element.98.flux, f32[32,8,256]{2,1,0:T(8,128)S(1)} %get-tuple-element.103.mask, ...), custom_call_target="tpu_custom_call" | custom-call | flops 1000000 | bytes 13557760 | tf_op jit(solution)/shard_map/potential_inner/pallas_call | solution.py:36
  47.9 5.0 %collective-permute-start.15 = (f32[64,256]{1,0:T(8,128)S(1)}, f32[64,256]{1,0:T(8,128)S(1)}, u32[]{:S(2)}, u32[]{:S(2)}) collective-permute-start(f32[64,256]{1,0:T(8,128)S(1)} %get-tuple-element.117), channel_id=1, source_target_pairs={{0,1},{2,3},{4,5},{6,7},{1,0},{3,2},{5,4},{7,6},{8,9},{10,11},{12,... | collective-permute-start | bytes 196616 | tf_op jit(solution)/shard_map/ppermute | solution.py:873
  52.9 1.2 %coarse_ready.1 = (f32[8,8,256]{2,1,0:T(8,128)S(1)}, f32[8,128]{1,0:T(8,128)S(1)}, f32[8,128]{1,0:T(8,128)S(1)}) custom-call(f32[8,8,256]{2,1,0:T(8,128)S(1)} %get-tuple-element.78.token.coarse.own, f32[264,256]{1,0:T(8,128)S(1)} %collective-permute-done.13.yy_a.r_a.far_a, f32[272,256]{1,0:T(8,128)S(1)} %collective-permute-done.8.far.yy_b.r_b.far_b), custom_call_target="tpu_custom_call" | custom-call | flops 1000000 | bytes 688128 | tf_op jit(solution)/shard_map/coarse_ready/pallas_call | solution.py:36
  54.1 1.4 %store.1 = (f32[32,32,256]{2,1,0:T(8,128)}, f32[32,32,256]{2,1,0:T(8,128)}, f32[8,128]{1,0:T(8,128)S(1)}) custom-call(f32[32,32,256]{2,1,0:T(8,128)S(1)} %get-tuple-element.91.conc, f32[32,32,256]{2,1,0:T(8,128)S(1)} %get-tuple-element.98.flux), custom_call_target="tpu_custom_call" | custom-call | flops 1000000 | bytes 4198400 | tf_op jit(solution)/shard_map/store/pallas_call | solution.py:36
  55.5 3.4 %collective-permute-start.16 = (f32[12,8,256]{2,1,0:T(8,128)S(1)}, f32[12,8,256]{2,1,0:T(8,128)S(1)}, u32[]{:S(2)}, u32[]{:S(2)}) collective-permute-start(f32[12,8,256]{2,1,0:T(8,128)S(1)} %get-tuple-element.120), channel_id=1, source_target_pairs={{8,16},{16,8},{9,17},{17,9},{10,18},{18,10},{11,19},{19,11},{12,20... | collective-permute-start | bytes 294920 | tf_op jit(solution)/shard_map/ppermute | solution.py:873
  59.0 2.5 %collective-permute-done.16.x_a = f32[12,8,256]{2,1,0:T(8,128)S(1)} collective-permute-done((f32[12,8,256]{2,1,0:T(8,128)S(1)}, f32[12,8,256]{2,1,0:T(8,128)S(1)}, u32[]{:S(2)}, u32[]{:S(2)}) %collective-permute-start.16) | collective-permute-done | bytes 98336 | tf_op jit(solution)/shard_map/ppermute | solution.py:873
  61.5 1.1 %middle.1 = (f32[24,24,256]{2,1,0:T(8,128)S(1)}, f32[24,24,256]{2,1,0:T(8,128)S(1)}, f32[24,24,256]{2,1,0:T(8,128)S(1)}, f32[8,12,256]{2,1,0:T(8,128)S(1)}, f32[...) custom-call(f32[16,16,256]{2,1,0:T(8,128)S(1)} %get-tuple-element.115.field.source_, ...), custom_call_target="tpu_custom_call" | custom-call | flops 1000000 | bytes 3960832 | tf_op jit(solution)/shard_map/middle/pallas_call | solution.py:36
  62.5 1.8 %collective-permute-start.19 = (f32[80,256]{1,0:T(8,128)S(1)}, f32[80,256]{1,0:T(8,128)S(1)}, u32[]{:S(2)}, u32[]{:S(2)}) collective-permute-start(f32[80,256]{1,0:T(8,128)S(1)} %get-tuple-element.127), channel_id=1, source_target_pairs={{0,1},{2,3},{4,5},{6,7},{1,0},{3,2},{5,4},{7,6},{8,9},{10,11},{12,... | collective-permute-start | bytes 245768 | tf_op jit(solution)/shard_map/ppermute | solution.py:873
  65.0 1.2 %collective-permute-done.19.r_b = f32[80,256]{1,0:T(8,128)S(1)} collective-permute-done((f32[80,256]{1,0:T(8,128)S(1)}, f32[80,256]{1,0:T(8,128)S(1)}, u32[]{:S(2)}, u32[]{:S(2)}) %collective-permute-start.19) | collective-permute-done | bytes 81952 | tf_op jit(solution)/shard_map/ppermute | solution.py:873
  66.2 1.9 %collective-permute-start.20 = (f32[8,256]{1,0:T(8,128)S(1)}, f32[8,256]{1,0:T(8,128)S(1)}, u32[]{:S(2)}, u32[]{:S(2)}) collective-permute-start(f32[8,256]{1,0:T(8,128)S(1)} %slice_add_fusion), channel_id=1, source_target_pairs={{0,2},{1,3},{2,0},{3,1},{4,6},{5,7},{6,4},{7,5},{8,10},{9,11},{10,... | collective-permute-start | bytes 24584 | tf_op jit(solution)/shard_map/ppermute | solution.py:877
  68.2 1.5 %collective-permute-done.20 = f32[8,256]{1,0:T(8,128)S(1)} collective-permute-done((f32[8,256]{1,0:T(8,128)S(1)}, f32[8,256]{1,0:T(8,128)S(1)}, u32[]{:S(2)}, u32[]{:S(2)}) %collective-permute-start.20) | collective-permute-done | bytes 8224 | tf_op jit(solution)/shard_map/ppermute | solution.py:877
  69.7 2.7 %collective-permute-start.21 = (f32[8,256]{1,0:T(8,128)S(1)}, f32[8,256]{1,0:T(8,128)S(1)}, u32[]{:S(2)}, u32[]{:S(2)}) collective-permute-start(f32[8,256]{1,0:T(8,128)S(1)} %add.10), channel_id=1, source_target_pairs={{0,4},{1,5},{2,6},{3,7},{4,0},{5,1},{6,2},{7,3},{8,12},{9,13},{10,... | collective-permute-start | bytes 24584 | tf_op jit(solution)/shard_map/ppermute | solution.py:877
  72.4 1.2 %coarse.1.error = f32[8,16,256]{2,1,0:T(8,128)S(1)} custom-call(f32[8,12,256]{2,1,0:T(8,128)S(1)} %get-tuple-element.124.own, f32[8,12,256]{2,1,0:T(8,128)S(1)} %get-tuple-element.125.conduct, f32[264,256]{1,0:T(8,128)S(1)} %collective-permute-done.13.yy_a.r_a.far_a, f32[272,256]{1,0:T(8,128)S(1)} %collective-permute-done.8.far.yy_b.r_b.far_b, ...), custom_call_target="tpu_custom_call" | custom-call | flops 1000000 | bytes 1032192 | tf_op jit(solution)/shard_map/coarse/pallas_call | solution.py:36
  73.6 2.9 %finish_early.1 = (f32[8,16,256]{2,1,0:T(8,128)S(1)}, f32[2,16,256]{2,1,0:T(8,128)S(1)}, f32[2,16,256]{2,1,0:T(8,128)S(1)}, f32[32,32,256]{2,1,0:T(8,128)}, f32[...) custom-call(f32[8,16,256]{2,1,0:T(8,128)S(1)} %coarse.1.error, ...), custom_call_target="tpu_custom_call" | custom-call | flops 1000000 | bytes 8593408 | tf_op jit(solution)/shard_map/finish_early/pallas_call | solution.py:36
  76.4 2.8 %collective-permute-start.22 = (f32[2,16,256]{2,1,0:T(8,128)S(1)}, f32[2,16,256]{2,1,0:T(8,128)S(1)}, u32[]{:S(2)}, u32[]{:S(2)}) collective-permute-start(f32[2,16,256]{2,1,0:T(8,128)S(1)} %get-tuple-element.132), channel_id=1, source_target_pairs={{8,16},{16,8},{9,17},{17,9},{10,18},{18,10},{11,19},{19,11},{12,20... | collective-permute-start | bytes 98312 | tf_op jit(solution)/shard_map/ppermute | solution.py:873
  79.4 2.3 %collective-permute-done.22.x_a = f32[2,16,256]{2,1,0:T(8,128)S(1)} collective-permute-done((f32[2,16,256]{2,1,0:T(8,128)S(1)}, f32[2,16,256]{2,1,0:T(8,128)S(1)}, u32[]{:S(2)}, u32[]{:S(2)}) %collective-permute-start.22) | collective-permute-done | bytes 32800 | tf_op jit(solution)/shard_map/ppermute | solution.py:873
  81.7 1.7 %finish_edge.1 = f32[32,32,256]{2,1,0:T(8,128)} custom-call(f32[2,16,256]{2,1,0:T(8,128)S(1)} %collective-permute-done.22.x_a, f32[2,16,256]{2,1,0:T(8,128)S(1)} %collective-permute-done.23.x_b, f32[24,24,256]{2,1,0:T(8,128)S(1)} %get-tuple-element.129.rest_0_.mid_two, ...), custom_call_target="tpu_custom_call", output_to_operand_aliasing={{}: (14, {})} | custom-call | flops 1000000 | bytes 10682368 | tf_op jit(solution)/shard_map/finish_edge/pallas_call | solution.py:36
  (52 shorter events, 6.0 us)
Async XLA Ops:
  0.6 7.4 %copy-start.1 = (f32[32,32,256]{2,1,0:T(8,128)S(1)}, f32[32,32,256]{2,1,0:T(8,128)}, u32[]{:S(2)}) copy-start(f32[32,32,256]{2,1,0:T(8,128)} %conc.9) | copy-start | bytes 3145732
  0.6 7.4 %copy-start = (s32[32,32,256]{2,1,0:T(8,128)S(1)}, s32[32,32,256]{2,1,0:T(8,128)}, u32[]{:S(2)}) copy-start(s32[32,32,256]{2,1,0:T(8,128)} %label.11) | copy-start | bytes 3145732
  2.7 15.0 %collective-permute-start = (f32[224,256]{1,0:T(8,128)}, f32[224,256]{1,0:T(8,128)S(1)}, u32[]{:S(2)}, u32[]{:S(2)}) collective-permute-start(f32[224,256]{1,0:T(8,128)} %get-tuple-element.75), channel_id=1, source_target_pairs={{1,2},{3,4},{5,6},{2,1},{4,3},{6,5},{9,10},{11,12},{13,14},{10,9},... | collective-permute-start | bytes 688136 | tf_op jit(solution)/shard_map/ppermute | solution.py:873
  3.4 14.7 %collective-permute-start.1 = (f32[224,256]{1,0:T(8,128)}, f32[224,256]{1,0:T(8,128)S(1)}, u32[]{:S(2)}, u32[]{:S(2)}) collective-permute-start(f32[224,256]{1,0:T(8,128)} %get-tuple-element.76), channel_id=1, source_target_pairs={{0,1},{2,3},{4,5},{6,7},{1,0},{3,2},{5,4},{7,6},{8,9},{10,11},{12,... | collective-permute-start | bytes 688136 | tf_op jit(solution)/shard_map/ppermute | solution.py:873
  8.0 1.2 %copy-start.2 = (f32[32,32,256]{2,1,0:T(8,128)S(1)}, f32[32,32,256]{2,1,0:T(8,128)}, u32[]{:S(2)}) copy-start(f32[32,32,256]{2,1,0:T(8,128)} %phi.9) | copy-start | bytes 3145732
  9.2 0.7 copy-start.5
  10.6 11.4 %copy-start.3 = (f32[32,32,256]{2,1,0:T(8,128)S(1)}, f32[32,32,256]{2,1,0:T(8,128)}, u32[]{:S(2)}) copy-start(f32[32,32,256]{2,1,0:T(8,128)} %phi.9) | copy-start | bytes 3145732
  10.6 7.0 %collective-permute-start.4 = (f32[2,256]{1,0:T(2,128)S(1)}, f32[2,256]{1,0:T(2,128)S(1)}, u32[]{:S(2)}, u32[]{:S(2)}) collective-permute-start(f32[2,256]{1,0:T(2,128)S(1)} %get-tuple-element.93), channel_id=1, source_target_pairs={{0,4},{1,5},{2,6},{3,7},{4,0},{5,1},{6,2},{7,3},{8,12},{9,13},{10,... | collective-permute-start | bytes 6152 | tf_op jit(solution)/shard_map/ppermute | solution.py:877
  13.0 9.0 %collective-permute-start.6 = (f32[22,8,256]{2,1,0:T(8,128)S(1)}, f32[22,8,256]{2,1,0:T(8,128)S(1)}, u32[]{:S(2)}, u32[]{:S(2)}) collective-permute-start(f32[22,8,256]{2,1,0:T(8,128)S(1)} %get-tuple-element.95), channel_id=1, source_target_pairs={{8,16},{16,8},{9,17},{17,9},{10,18},{18,10},{11,19},{19,11},{12,20... | collective-permute-start | bytes 540680 | tf_op jit(solution)/shard_map/ppermute | solution.py:873
  17.5 4.5 %collective-permute-start.7 = (f32[22,8,256]{2,1,0:T(8,128)S(1)}, f32[22,8,256]{2,1,0:T(8,128)S(1)}, u32[]{:S(2)}, u32[]{:S(2)}) collective-permute-start(f32[22,8,256]{2,1,0:T(8,128)S(1)} %get-tuple-element.96), channel_id=1, source_target_pairs={{0,8},{16,24},{8,0},{24,16},{1,9},{17,25},{9,1},{25,17},{2,10},{18... | collective-permute-start | bytes 540680 | tf_op jit(solution)/shard_map/ppermute | solution.py:873
  17.6 4.3 %collective-permute-start.5 = (f32[4,256]{1,0:T(4,128)S(1)}, f32[4,256]{1,0:T(4,128)S(1)}, u32[]{:S(2)}, u32[]{:S(2)}) collective-permute-start(f32[4,256]{1,0:T(4,128)S(1)} %pad_maximum_fusion.1), channel_id=1, source_target_pairs={{0,2},{1,3},{2,0},{3,1},{4,6},{5,7},{6,4},{7,5},{8,10},{9,11},{10,... | collective-permute-start | bytes 12296 | tf_op jit(solution)/shard_map/ppermute | solution.py:877
  18.1 6.9 %copy-start.4 = (f32[32,32,256]{2,1,0:T(8,128)S(1)}, f32[32,32,256]{2,1,0:T(8,128)}, u32[]{:S(2)}) copy-start(f32[32,32,256]{2,1,0:T(8,128)} %solid.3) | copy-start | bytes 3145732
  18.2 10.9 %collective-permute-start.2 = (f32[35,8,256]{2,1,0:T(8,128)S(1)}, f32[35,8,256]{2,1,0:T(8,128)S(1)}, u32[]{:S(2)}, u32[]{:S(2)}) collective-permute-start(f32[35,8,256]{2,1,0:T(8,128)S(1)} %get-tuple-element.79), channel_id=1, source_target_pairs={{8,16},{16,8},{9,17},{17,9},{10,18},{18,10},{11,19},{19,11},{12,20... | collective-permute-start | bytes 860168 | tf_op jit(solution)/shard_map/ppermute | solution.py:873
  21.9 7.2 %collective-permute-start.3 = (f32[35,8,256]{2,1,0:T(8,128)S(1)}, f32[35,8,256]{2,1,0:T(8,128)S(1)}, u32[]{:S(2)}, u32[]{:S(2)}) collective-permute-start(f32[35,8,256]{2,1,0:T(8,128)S(1)} %get-tuple-element.80), channel_id=1, source_target_pairs={{0,8},{16,24},{8,0},{24,16},{1,9},{17,25},{9,1},{25,17},{2,10},{18... | collective-permute-start | bytes 860168 | tf_op jit(solution)/shard_map/ppermute | solution.py:873
  22.1 13.5 %collective-permute-start.8 = (f32[272,256]{1,0:T(8,128)S(1)}, f32[272,256]{1,0:T(8,128)S(1)}, u32[]{:S(2)}, u32[]{:S(2)}) collective-permute-start(f32[272,256]{1,0:T(8,128)S(1)} %get-tuple-element.97), channel_id=1, source_target_pairs={{0,1},{2,3},{4,5},{6,7},{1,0},{3,2},{5,4},{7,6},{8,9},{10,11},{12,... | collective-permute-start | bytes 835592 | tf_op jit(solution)/shard_map/ppermute | solution.py:873
  24.3 19.0 %collective-permute-start.13 = (f32[264,256]{1,0:T(8,128)S(1)}, f32[264,256]{1,0:T(8,128)S(1)}, u32[]{:S(2)}, u32[]{:S(2)}) collective-permute-start(f32[264,256]{1,0:T(8,128)S(1)} %get-tuple-element.109), channel_id=1, source_target_pairs={{1,2},{3,4},{5,6},{2,1},{4,3},{6,5},{9,10},{11,12},{13,14},{10,9},... | collective-permute-start | bytes 811016 | tf_op jit(solution)/shard_map/ppermute | solution.py:873
  30.3 7.4 %collective-permute-start.9 = (f32[96,256]{1,0:T(8,128)S(1)}, f32[96,256]{1,0:T(8,128)S(1)}, u32[]{:S(2)}, u32[]{:S(2)}) collective-permute-start(f32[96,256]{1,0:T(8,128)S(1)} %get-tuple-element.101), channel_id=1, source_target_pairs={{0,1},{2,3},{4,5},{6,7},{1,0},{3,2},{5,4},{7,6},{8,9},{10,11},{12,... | collective-permute-start | bytes 294920 | tf_op jit(solution)/shard_map/ppermute | solution.py:873
  34.1 3.6 %collective-permute-start.10 = (f32[96,256]{1,0:T(8,128)S(1)}, f32[96,256]{1,0:T(8,128)S(1)}, u32[]{:S(2)}, u32[]{:S(2)}) collective-permute-start(f32[96,256]{1,0:T(8,128)S(1)} %get-tuple-element.102), channel_id=1, source_target_pairs={{1,2},{3,4},{5,6},{2,1},{4,3},{6,5},{9,10},{11,12},{13,14},{10,9},... | collective-permute-start | bytes 294920 | tf_op jit(solution)/shard_map/ppermute | solution.py:873
  37.8 8.8 %collective-permute-start.11 = (f32[15,8,256]{2,1,0:T(8,128)S(1)}, f32[15,8,256]{2,1,0:T(8,128)S(1)}, u32[]{:S(2)}, u32[]{:S(2)}) collective-permute-start(f32[15,8,256]{2,1,0:T(8,128)S(1)} %get-tuple-element.105), channel_id=1, source_target_pairs={{8,16},{16,8},{9,17},{17,9},{10,18},{18,10},{11,19},{19,11},{12,20... | collective-permute-start | bytes 368648 | tf_op jit(solution)/shard_map/ppermute | solution.py:873
  43.3 3.4 %collective-permute-start.12 = (f32[15,8,256]{2,1,0:T(8,128)S(1)}, f32[15,8,256]{2,1,0:T(8,128)S(1)}, u32[]{:S(2)}, u32[]{:S(2)}) collective-permute-start(f32[15,8,256]{2,1,0:T(8,128)S(1)} %get-tuple-element.106), channel_id=1, source_target_pairs={{0,8},{16,24},{8,0},{24,16},{1,9},{17,25},{9,1},{25,17},{2,10},{18... | collective-permute-start | bytes 368648 | tf_op jit(solution)/shard_map/ppermute | solution.py:873
  47.3 8.2 %collective-permute-start.14 = (f32[64,256]{1,0:T(8,128)S(1)}, f32[64,256]{1,0:T(8,128)S(1)}, u32[]{:S(2)}, u32[]{:S(2)}) collective-permute-start(f32[64,256]{1,0:T(8,128)S(1)} %get-tuple-element.116), channel_id=1, source_target_pairs={{1,2},{3,4},{5,6},{2,1},{4,3},{6,5},{9,10},{11,12},{13,14},{10,9},... | collective-permute-start | bytes 196616 | tf_op jit(solution)/shard_map/ppermute | solution.py:873
  47.9 7.6 %collective-permute-start.15 = (f32[64,256]{1,0:T(8,128)S(1)}, f32[64,256]{1,0:T(8,128)S(1)}, u32[]{:S(2)}, u32[]{:S(2)}) collective-permute-start(f32[64,256]{1,0:T(8,128)S(1)} %get-tuple-element.117), channel_id=1, source_target_pairs={{0,1},{2,3},{4,5},{6,7},{1,0},{3,2},{5,4},{7,6},{8,9},{10,11},{12,... | collective-permute-start | bytes 196616 | tf_op jit(solution)/shard_map/ppermute | solution.py:873
  55.5 5.9 %collective-permute-start.16 = (f32[12,8,256]{2,1,0:T(8,128)S(1)}, f32[12,8,256]{2,1,0:T(8,128)S(1)}, u32[]{:S(2)}, u32[]{:S(2)}) collective-permute-start(f32[12,8,256]{2,1,0:T(8,128)S(1)} %get-tuple-element.120), channel_id=1, source_target_pairs={{8,16},{16,8},{9,17},{17,9},{10,18},{18,10},{11,19},{19,11},{12,20... | collective-permute-start | bytes 294920 | tf_op jit(solution)/shard_map/ppermute | solution.py:873
  58.9 2.6 %collective-permute-start.17 = (f32[12,8,256]{2,1,0:T(8,128)S(1)}, f32[12,8,256]{2,1,0:T(8,128)S(1)}, u32[]{:S(2)}, u32[]{:S(2)}) collective-permute-start(f32[12,8,256]{2,1,0:T(8,128)S(1)} %get-tuple-element.121), channel_id=1, source_target_pairs={{0,8},{16,24},{8,0},{24,16},{1,9},{17,25},{9,1},{25,17},{2,10},{18... | collective-permute-start | bytes 294920 | tf_op jit(solution)/shard_map/ppermute | solution.py:873
  62.5 3.7 %collective-permute-start.19 = (f32[80,256]{1,0:T(8,128)S(1)}, f32[80,256]{1,0:T(8,128)S(1)}, u32[]{:S(2)}, u32[]{:S(2)}) collective-permute-start(f32[80,256]{1,0:T(8,128)S(1)} %get-tuple-element.127), channel_id=1, source_target_pairs={{0,1},{2,3},{4,5},{6,7},{1,0},{3,2},{5,4},{7,6},{8,9},{10,11},{12,... | collective-permute-start | bytes 245768 | tf_op jit(solution)/shard_map/ppermute | solution.py:873
  64.4 8.0 %collective-permute-start.18 = (f32[72,256]{1,0:T(8,128)S(1)}, f32[72,256]{1,0:T(8,128)S(1)}, u32[]{:S(2)}, u32[]{:S(2)}) collective-permute-start(f32[72,256]{1,0:T(8,128)S(1)} %get-tuple-element.126), channel_id=1, source_target_pairs={{1,2},{3,4},{5,6},{2,1},{4,3},{6,5},{9,10},{11,12},{13,14},{10,9},... | collective-permute-start | bytes 221192 | tf_op jit(solution)/shard_map/ppermute | solution.py:873
  66.2 3.5 %collective-permute-start.20 = (f32[8,256]{1,0:T(8,128)S(1)}, f32[8,256]{1,0:T(8,128)S(1)}, u32[]{:S(2)}, u32[]{:S(2)}) collective-permute-start(f32[8,256]{1,0:T(8,128)S(1)} %slice_add_fusion), channel_id=1, source_target_pairs={{0,2},{1,3},{2,0},{3,1},{4,6},{5,7},{6,4},{7,5},{8,10},{9,11},{10,... | collective-permute-start | bytes 24584 | tf_op jit(solution)/shard_map/ppermute | solution.py:877
  69.7 3.9 %collective-permute-start.21 = (f32[8,256]{1,0:T(8,128)S(1)}, f32[8,256]{1,0:T(8,128)S(1)}, u32[]{:S(2)}, u32[]{:S(2)}) collective-permute-start(f32[8,256]{1,0:T(8,128)S(1)} %add.10), channel_id=1, source_target_pairs={{0,4},{1,5},{2,6},{3,7},{4,0},{5,1},{6,2},{7,3},{8,12},{9,13},{10,... | collective-permute-start | bytes 24584 | tf_op jit(solution)/shard_map/ppermute | solution.py:877
  76.4 5.2 %collective-permute-start.22 = (f32[2,16,256]{2,1,0:T(8,128)S(1)}, f32[2,16,256]{2,1,0:T(8,128)S(1)}, u32[]{:S(2)}, u32[]{:S(2)}) collective-permute-start(f32[2,16,256]{2,1,0:T(8,128)S(1)} %get-tuple-element.132), channel_id=1, source_target_pairs={{8,16},{16,8},{9,17},{17,9},{10,18},{18,10},{11,19},{19,11},{12,20... | collective-permute-start | bytes 98312 | tf_op jit(solution)/shard_map/ppermute | solution.py:873
  79.3 2.4 %collective-permute-start.23 = (f32[2,16,256]{2,1,0:T(8,128)S(1)}, f32[2,16,256]{2,1,0:T(8,128)S(1)}, u32[]{:S(2)}, u32[]{:S(2)}) collective-permute-start(f32[2,16,256]{2,1,0:T(8,128)S(1)} %get-tuple-element.133), channel_id=1, source_target_pairs={{0,8},{16,24},{8,0},{24,16},{1,9},{17,25},{9,1},{25,17},{2,10},{18... | collective-permute-start | bytes 98312 | tf_op jit(solution)/shard_map/ppermute | solution.py:873

commit v16 on v15

--- a/solution.py
+++ b/solution.py
@@ -564,7 +564,7 @@
         send_y(pay_a, pay_b, 4 * x, source_mid[x, 0:4, :], source_mid[x, 12:16, :])
 
 
-def mid_pack_x_kernel(field, r_a, r_b, token, token_2, pay_a, pay_b):
+def mid_pack_x_kernel(field, r_a, r_b, token, pay_a, pay_b):
     n = field.shape[0]
 
     def tile(x, t):
@@ -578,7 +578,7 @@
 
 
 def mid_kernel(
-    source_own, conduct_own, yy_a, yy_b, xx_a, xx_b, y_a, y_b, x_a, x_b, rho, load,
+    source_own, conduct_own, yy_a, yy_b, xx_a, xx_b, y_a, y_b, x_a, x_b, rho, load, token,
     after_two, source, weight, coarse, conduct, pay_a, pay_b, part, scale, mid_conduct, pairs, pairs_2,
 ):
     n = source_own.shape[0]
@@ -996,14 +996,14 @@
         name="coarse_ready",
     )
     pay_a, pay_b = call(
-        mid_pack_x_kernel, [shaped(3 * HALO, 8, 256)] * 2, [source_mid, m_a, m_b, made, stored], name="mid_pack_x"
+        mid_pack_x_kernel, [shaped(3 * HALO, 8, 256)] * 2, [source_mid, m_a, m_b, made], name="mid_pack_x"
     )
     mx_a, mx_b = swap(pay_a, pay_b, "grp")
     mid_two, mid_source, mid_weight, source_coarse, wide_coarse, pay_a, pay_b, sums = call(
         mid_kernel,
         [shaped(*ext_mid)] * 3
         + [shaped(quarter, 12, 256), shaped(quarter, 12, 256), shaped(72, 256), shaped(80, 256), shaped(8, 256)],
-        [source_mid, conduct_mid, yy_a, yy_b, xx_a, xx_b, m_a, m_b, mx_a, mx_b, rho, load],
+        [source_mid, conduct_mid, yy_a, yy_b, xx_a, xx_b, m_a, m_b, mx_a, mx_b, rho, load, stored],
         [vmem(*ext_mid)] * 2 + [vmem(8, 2, half + 2 * HALO, LANES)] * 2,
         name="middle",
     )

time: 84 us -> 84.1 us (level)
    ppermute x10, waiting for transfers between devices: 4.74 us -> 3.34 us  [swap(): lax.ppermute(pay_a, axis, both_ways(pairs_a))]
    ppermute x10, waiting for transfers between devices: 2.94 us -> 3.86 us  [swap(): lax.ppermute(pay_b, axis, both_ways(pairs_b))]
  transfers between devices with their start and end apart: 24 -> 24, of which waited for: 7 -> 8; matrix products, arithmetic and copies ran while one was open for 0% -> 0% of each run, Pallas kernels for 18% -> 18%
where the time goes in v16:
time: 84.1 us; the launch traced here: 83.6 us
  starting transfers between devices  48.6 us (58%)
  Pallas kernels  23.1 us (27%)
  waiting for transfers between devices  8.74 us (10%)
  local copies, waits for them, and re-layouts  1.94 us (2%)
  between operations  1.2 us (1%)
    ppermute x10, starting transfers between devices, swap(): lax.ppermute(pay_a, axis, both_ways(pairs_a))  23.2 us
    pallas_call x19, Pallas kernels, call(): pl.pallas_call(kernel, out_shape=tuple(outs), in_specs=in_specs or [WHOLE...  23.1 us
    ppermute x10, starting transfers between devices, swap(): lax.ppermute(pay_b, axis, both_ways(pairs_b))  18.3 us
    ppermute x4, starting transfers between devices, exchange(): lax.ppermute(value, 'dev', [(i, i ^ distance) for i in range(lax.axis_siz...  7.19 us
    ppermute x10, waiting for transfers between devices, swap(): lax.ppermute(pay_b, axis, both_ways(pairs_b))  3.86 us
    ppermute x10, waiting for transfers between devices, swap(): lax.ppermute(pay_a, axis, both_ways(pairs_a))  3.34 us
    unnamed x12, local copies, waits for them, and re-layouts  1.94 us
  transfers between devices with their start and end apart: 24, of which 8 were waited for; matrix products, arithmetic and copies ran while one was open for 0% of the time, Pallas kernels for 18%

profile of v16, /device:TPU:1, one launch (start us, length us, event | category | flops | bytes accessed | tf_op | source)
XLA Modules:
  0.0 83.6 jit_solution(9312960110131511736)
XLA Ops:
  0.7 2.1 %first_pack.1 = (f32[224,256]{1,0:T(8,128)}, f32[224,256]{1,0:T(8,128)}, f32[8,256]{1,0:T(8,128)}) custom-call(f32[32,32,256]{2,1,0:T(8,128)} %conc.9, s32[32,32,256]{2,1,0:T(8,128)} %label.11, s32[1,256]{1,0:T(1,128)} %bitcast.1, s32[1,256]{1,0:T(1,128)} %block.1), custom_call_target="tpu_custom_call" | custom-call | flops 1000000 | bytes 2566144 | tf_op jit(solution)/shard_map/first_pack/pallas_call | solution.py:36
  3.4 4.6 %collective-permute-start.1 = (f32[224,256]{1,0:T(8,128)}, f32[224,256]{1,0:T(8,128)S(1)}, u32[]{:S(2)}, u32[]{:S(2)}) collective-permute-start(f32[224,256]{1,0:T(8,128)} %get-tuple-element.76), channel_id=1, source_target_pairs={{0,1},{2,3},{4,5},{6,7},{1,0},{3,2},{5,4},{7,6},{8,9},{10,11},{12,... | collective-permute-start | bytes 688136 | tf_op jit(solution)/shard_map/ppermute | solution.py:873
  8.0 1.2 %copy-done.2 = f32[32,32,256]{2,1,0:T(8,128)S(1)} copy-done((f32[32,32,256]{2,1,0:T(8,128)S(1)}, f32[32,32,256]{2,1,0:T(8,128)}, u32[]{:S(2)}) %copy-start.2) | copy-done | bytes 1048600
  10.6 2.4 %collective-permute-start.4 = (f32[2,256]{1,0:T(2,128)S(1)}, f32[2,256]{1,0:T(2,128)S(1)}, u32[]{:S(2)}, u32[]{:S(2)}) collective-permute-start(f32[2,256]{1,0:T(2,128)S(1)} %get-tuple-element.93), channel_id=1, source_target_pairs={{0,4},{1,5},{2,6},{3,7},{4,0},{5,1},{6,2},{7,3},{8,12},{9,13},{10,... | collective-permute-start | bytes 6152 | tf_op jit(solution)/shard_map/ppermute | solution.py:877
  13.0 4.5 %collective-permute-start.6 = (f32[22,8,256]{2,1,0:T(8,128)S(1)}, f32[22,8,256]{2,1,0:T(8,128)S(1)}, u32[]{:S(2)}, u32[]{:S(2)}) collective-permute-start(f32[22,8,256]{2,1,0:T(8,128)S(1)} %get-tuple-element.95), channel_id=1, source_target_pairs={{8,16},{16,8},{9,17},{17,9},{10,18},{18,10},{11,19},{19,11},{12,20... | collective-permute-start | bytes 540680 | tf_op jit(solution)/shard_map/ppermute | solution.py:873
  18.2 3.7 %collective-permute-start.2 = (f32[35,8,256]{2,1,0:T(8,128)S(1)}, f32[35,8,256]{2,1,0:T(8,128)S(1)}, u32[]{:S(2)}, u32[]{:S(2)}) collective-permute-start(f32[35,8,256]{2,1,0:T(8,128)S(1)} %get-tuple-element.79), channel_id=1, source_target_pairs={{8,16},{16,8},{9,17},{17,9},{10,18},{18,10},{11,19},{19,11},{12,20... | collective-permute-start | bytes 860168 | tf_op jit(solution)/shard_map/ppermute | solution.py:873
  22.1 2.2 %collective-permute-start.8 = (f32[272,256]{1,0:T(8,128)S(1)}, f32[272,256]{1,0:T(8,128)S(1)}, u32[]{:S(2)}, u32[]{:S(2)}) collective-permute-start(f32[272,256]{1,0:T(8,128)S(1)} %get-tuple-element.97), channel_id=1, source_target_pairs={{0,1},{2,3},{4,5},{6,7},{1,0},{3,2},{5,4},{7,6},{8,9},{10,11},{12,... | collective-permute-start | bytes 835592 | tf_op jit(solution)/shard_map/ppermute | solution.py:873
  25.0 4.1 %sweeps_inner.1 = (f32[32,40,256]{2,1,0:T(8,128)S(1)}, f32[32,40,256]{2,1,0:T(8,128)S(1)}, f32[32,40,256]{2,1,0:T(8,128)S(1)}, f32[32,40,256]{2,1,0:T(8,128)S(1)...) custom-call(f32[32,32,256]{2,1,0:T(8,128)S(1)} %copy-done.1, ...), custom_call_target="tpu_custom_call" | custom-call | flops 1000000 | bytes 14614528 | tf_op jit(solution)/shard_map/sweeps_inner/pallas_call | solution.py:36
  29.1 1.2 %sweeps_edge.1 = (f32[32,32,256]{2,1,0:T(8,128)S(1)}, f32[32,32,256]{2,1,0:T(8,128)S(1)}, f32[96,256]{1,0:T(8,128)S(1)}, f32[96,256]{1,0:T(8,128)S(1)}) custom-call(f32[35,8,256]{2,1,0:T(8,128)S(1)} %collective-permute-done.2.x_a, f32[35,8,256]{2,1,0:T(8,128)S(1)} %collective-permute-done.3.x_b, s32[32,32,256]{2,1,0:T(8,128)S(1)} %copy-done, ...), custom_call_target="tpu_custom_call" | custom-call | flops 1000000 | bytes 15974400 | tf_op jit(solution)/shard_map/sweeps_edge/pallas_call | solution.py:36
  30.3 3.8 %collective-permute-start.9 = (f32[96,256]{1,0:T(8,128)S(1)}, f32[96,256]{1,0:T(8,128)S(1)}, u32[]{:S(2)}, u32[]{:S(2)}) collective-permute-start(f32[96,256]{1,0:T(8,128)S(1)} %get-tuple-element.101), channel_id=1, source_target_pairs={{0,1},{2,3},{4,5},{6,7},{1,0},{3,2},{5,4},{7,6},{8,9},{10,11},{12,... | collective-permute-start | bytes 294920 | tf_op jit(solution)/shard_map/ppermute | solution.py:873
  34.8 0.8 ready.1
  35.6 0.8 %mask.1 = (f32[32,32,256]{2,1,0:T(8,128)S(1)}, f32[32,8,256]{2,1,0:T(8,128)S(1)}) custom-call(f32[32,32,256]{2,1,0:T(8,128)S(1)} %get-tuple-element.92.flux_all, f32[8,256]{1,0:T(8,128)S(1)} %pad_maximum_fusion.lists, f32[272,256]{1,0:T(8,128)S(1)} %collective-permute-done.8.far.yy_b.r_b.far_b), custom_call_target="tpu_custom_call" | custom-call | flops 1000000 | bytes 2646016 | tf_op jit(solution)/shard_map/mask/pallas_call | solution.py:36
  36.5 1.2 %collective-permute-done.9.r_b.y_b = f32[96,256]{1,0:T(8,128)S(1)} collective-permute-done((f32[96,256]{1,0:T(8,128)S(1)}, f32[96,256]{1,0:T(8,128)S(1)}, u32[]{:S(2)}, u32[]{:S(2)}) %collective-permute-start.9) | collective-permute-done | bytes 98336 | tf_op jit(solution)/shard_map/ppermute | solution.py:873
  37.8 5.5 %collective-permute-start.11 = (f32[15,8,256]{2,1,0:T(8,128)S(1)}, f32[15,8,256]{2,1,0:T(8,128)S(1)}, u32[]{:S(2)}, u32[]{:S(2)}) collective-permute-start(f32[15,8,256]{2,1,0:T(8,128)S(1)} %get-tuple-element.105), channel_id=1, source_target_pairs={{8,16},{16,8},{9,17},{17,9},{10,18},{18,10},{11,19},{19,11},{12,20... | collective-permute-start | bytes 368648 | tf_op jit(solution)/shard_map/ppermute | solution.py:873
  43.3 3.3 %potential_inner.1 = (f32[40,40,256]{2,1,0:T(8,128)S(1)}, f32[40,40,256]{2,1,0:T(8,128)S(1)}, f32[40,40,256]{2,1,0:T(8,128)S(1)}, f32[16,16,256]{2,1,0:T(8,128)S(1)}, f32[40,40,256]{2,1,0:T(8,128)S(1)}) custom-call(f32[32,32,256]{2,1,0:T(8,128)S(1)} %get-tuple-element.98.flux, f32[32,8,256]{2,1,0:T(8,128)S(1)} %get-tuple-element.103.mask, ...), custom_call_target="tpu_custom_call" | custom-call | flops 1000000 | bytes 13557760 | tf_op jit(solution)/shard_map/potential_inner/pallas_call | solution.py:36
  47.9 5.0 %collective-permute-start.15 = (f32[64,256]{1,0:T(8,128)S(1)}, f32[64,256]{1,0:T(8,128)S(1)}, u32[]{:S(2)}, u32[]{:S(2)}) collective-permute-start(f32[64,256]{1,0:T(8,128)S(1)} %get-tuple-element.117), channel_id=1, source_target_pairs={{0,1},{2,3},{4,5},{6,7},{1,0},{3,2},{5,4},{7,6},{8,9},{10,11},{12,... | collective-permute-start | bytes 196616 | tf_op jit(solution)/shard_map/ppermute | solution.py:873
  52.9 1.2 %coarse_ready.1 = (f32[8,8,256]{2,1,0:T(8,128)S(1)}, f32[8,128]{1,0:T(8,128)S(1)}, f32[8,128]{1,0:T(8,128)S(1)}) custom-call(f32[8,8,256]{2,1,0:T(8,128)S(1)} %get-tuple-element.78.token.coarse.own, f32[264,256]{1,0:T(8,128)S(1)} %collective-permute-done.13.yy_a.r_a.far_a, f32[272,256]{1,0:T(8,128)S(1)} %collective-permute-done.8.far.yy_b.r_b.far_b), custom_call_target="tpu_custom_call" | custom-call | flops 1000000 | bytes 688128 | tf_op jit(solution)/shard_map/coarse_ready/pallas_call | solution.py:36
  54.1 0.8 %collective-permute-done.15.r_b.y_b = f32[64,256]{1,0:T(8,128)S(1)} collective-permute-done((f32[64,256]{1,0:T(8,128)S(1)}, f32[64,256]{1,0:T(8,128)S(1)}, u32[]{:S(2)}, u32[]{:S(2)}) %collective-permute-start.15) | collective-permute-done | bytes 65568 | tf_op jit(solution)/shard_map/ppermute | solution.py:873
  55.0 3.6 %collective-permute-start.16 = (f32[12,8,256]{2,1,0:T(8,128)S(1)}, f32[12,8,256]{2,1,0:T(8,128)S(1)}, u32[]{:S(2)}, u32[]{:S(2)}) collective-permute-start(f32[12,8,256]{2,1,0:T(8,128)S(1)} %get-tuple-element.119), channel_id=1, source_target_pairs={{8,16},{16,8},{9,17},{17,9},{10,18},{18,10},{11,19},{19,11},{12,20... | collective-permute-start | bytes 294920 | tf_op jit(solution)/shard_map/ppermute | solution.py:873
  58.6 1.4 %store.1 = (f32[32,32,256]{2,1,0:T(8,128)}, f32[32,32,256]{2,1,0:T(8,128)}, f32[8,128]{1,0:T(8,128)S(1)}) custom-call(f32[32,32,256]{2,1,0:T(8,128)S(1)} %get-tuple-element.91.conc, f32[32,32,256]{2,1,0:T(8,128)S(1)} %get-tuple-element.98.flux), custom_call_target="tpu_custom_call" | custom-call | flops 1000000 | bytes 4198400 | tf_op jit(solution)/shard_map/store/pallas_call | solution.py:36
  60.0 0.9 %collective-permute-done.16.x_a = f32[12,8,256]{2,1,0:T(8,128)S(1)} collective-permute-done((f32[12,8,256]{2,1,0:T(8,128)S(1)}, f32[12,8,256]{2,1,0:T(8,128)S(1)}, u32[]{:S(2)}, u32[]{:S(2)}) %collective-permute-start.16) | collective-permute-done | bytes 98336 | tf_op jit(solution)/shard_map/ppermute | solution.py:873
  60.9 1.0 %middle.1 = (f32[24,24,256]{2,1,0:T(8,128)S(1)}, f32[24,24,256]{2,1,0:T(8,128)S(1)}, f32[24,24,256]{2,1,0:T(8,128)S(1)}, f32[8,12,256]{2,1,0:T(8,128)S(1)}, f32[...) custom-call(f32[16,16,256]{2,1,0:T(8,128)S(1)} %get-tuple-element.115.field.source_, ...), custom_call_target="tpu_custom_call" | custom-call | flops 1000000 | bytes 3964928 | tf_op jit(solution)/shard_map/middle/pallas_call | solution.py:36
  61.9 2.4 %collective-permute-start.19 = (f32[80,256]{1,0:T(8,128)S(1)}, f32[80,256]{1,0:T(8,128)S(1)}, u32[]{:S(2)}, u32[]{:S(2)}) collective-permute-start(f32[80,256]{1,0:T(8,128)S(1)} %get-tuple-element.127), channel_id=1, source_target_pairs={{0,1},{2,3},{4,5},{6,7},{1,0},{3,2},{5,4},{7,6},{8,9},{10,11},{12,... | collective-permute-start | bytes 245768 | tf_op jit(solution)/shard_map/ppermute | solution.py:873
  65.0 1.2 %collective-permute-done.19.r_b = f32[80,256]{1,0:T(8,128)S(1)} collective-permute-done((f32[80,256]{1,0:T(8,128)S(1)}, f32[80,256]{1,0:T(8,128)S(1)}, u32[]{:S(2)}, u32[]{:S(2)}) %collective-permute-start.19) | collective-permute-done | bytes 81952 | tf_op jit(solution)/shard_map/ppermute | solution.py:873
  66.3 1.9 %collective-permute-start.20 = (f32[8,256]{1,0:T(8,128)S(1)}, f32[8,256]{1,0:T(8,128)S(1)}, u32[]{:S(2)}, u32[]{:S(2)}) collective-permute-start(f32[8,256]{1,0:T(8,128)S(1)} %slice_add_fusion), channel_id=1, source_target_pairs={{0,2},{1,3},{2,0},{3,1},{4,6},{5,7},{6,4},{7,5},{8,10},{9,11},{10,... | collective-permute-start | bytes 24584 | tf_op jit(solution)/shard_map/ppermute | solution.py:877
  68.1 1.5 %collective-permute-done.20 = f32[8,256]{1,0:T(8,128)S(1)} collective-permute-done((f32[8,256]{1,0:T(8,128)S(1)}, f32[8,256]{1,0:T(8,128)S(1)}, u32[]{:S(2)}, u32[]{:S(2)}) %collective-permute-start.20) | collective-permute-done | bytes 8224 | tf_op jit(solution)/shard_map/ppermute | solution.py:877
  69.6 2.9 %collective-permute-start.21 = (f32[8,256]{1,0:T(8,128)S(1)}, f32[8,256]{1,0:T(8,128)S(1)}, u32[]{:S(2)}, u32[]{:S(2)}) collective-permute-start(f32[8,256]{1,0:T(8,128)S(1)} %add.10), channel_id=1, source_target_pairs={{0,4},{1,5},{2,6},{3,7},{4,0},{5,1},{6,2},{7,3},{8,12},{9,13},{10,... | collective-permute-start | bytes 24584 | tf_op jit(solution)/shard_map/ppermute | solution.py:877
  72.5 1.1 %coarse.1.error = f32[8,16,256]{2,1,0:T(8,128)S(1)} custom-call(f32[8,12,256]{2,1,0:T(8,128)S(1)} %get-tuple-element.124.own, f32[8,12,256]{2,1,0:T(8,128)S(1)} %get-tuple-element.125.conduct, f32[264,256]{1,0:T(8,128)S(1)} %collective-permute-done.13.yy_a.r_a.far_a, f32[272,256]{1,0:T(8,128)S(1)} %collective-permute-done.8.far.yy_b.r_b.far_b, ...), custom_call_target="tpu_custom_call" | custom-call | flops 1000000 | bytes 1032192 | tf_op jit(solution)/shard_map/coarse/pallas_call | solution.py:36
  73.7 2.9 %finish_early.1 = (f32[8,16,256]{2,1,0:T(8,128)S(1)}, f32[2,16,256]{2,1,0:T(8,128)S(1)}, f32[2,16,256]{2,1,0:T(8,128)S(1)}, f32[32,32,256]{2,1,0:T(8,128)}, f32[...) custom-call(f32[8,16,256]{2,1,0:T(8,128)S(1)} %coarse.1.error, ...), custom_call_target="tpu_custom_call" | custom-call | flops 1000000 | bytes 8593408 | tf_op jit(solution)/shard_map/finish_early/pallas_call | solution.py:36
  76.6 2.6 %collective-permute-start.22 = (f32[2,16,256]{2,1,0:T(8,128)S(1)}, f32[2,16,256]{2,1,0:T(8,128)S(1)}, u32[]{:S(2)}, u32[]{:S(2)}) collective-permute-start(f32[2,16,256]{2,1,0:T(8,128)S(1)} %get-tuple-element.132), channel_id=1, source_target_pairs={{8,16},{16,8},{9,17},{17,9},{10,18},{18,10},{11,19},{19,11},{12,20... | collective-permute-start | bytes 98312 | tf_op jit(solution)/shard_map/ppermute | solution.py:873
  79.4 2.4 %collective-permute-done.22.x_a = f32[2,16,256]{2,1,0:T(8,128)S(1)} collective-permute-done((f32[2,16,256]{2,1,0:T(8,128)S(1)}, f32[2,16,256]{2,1,0:T(8,128)S(1)}, u32[]{:S(2)}, u32[]{:S(2)}) %collective-permute-start.22) | collective-permute-done | bytes 32800 | tf_op jit(solution)/shard_map/ppermute | solution.py:873
  81.8 1.7 %finish_edge.1 = f32[32,32,256]{2,1,0:T(8,128)} custom-call(f32[2,16,256]{2,1,0:T(8,128)S(1)} %collective-permute-done.22.x_a, f32[2,16,256]{2,1,0:T(8,128)S(1)} %collective-permute-done.23.x_b, f32[24,24,256]{2,1,0:T(8,128)S(1)} %get-tuple-element.129.rest_0_.mid_two, ...), custom_call_target="tpu_custom_call", output_to_operand_aliasing={{}: (14, {})} | custom-call | flops 1000000 | bytes 10682368 | tf_op jit(solution)/shard_map/finish_edge/pallas_call | solution.py:36
  (52 shorter events, 6.7 us)
Async XLA Ops:
  0.6 7.4 %copy-start.1 = (f32[32,32,256]{2,1,0:T(8,128)S(1)}, f32[32,32,256]{2,1,0:T(8,128)}, u32[]{:S(2)}) copy-start(f32[32,32,256]{2,1,0:T(8,128)} %conc.9) | copy-start | bytes 3145732
  0.6 7.4 %copy-start = (s32[32,32,256]{2,1,0:T(8,128)S(1)}, s32[32,32,256]{2,1,0:T(8,128)}, u32[]{:S(2)}) copy-start(s32[32,32,256]{2,1,0:T(8,128)} %label.11) | copy-start | bytes 3145732
  2.7 15.0 %collective-permute-start = (f32[224,256]{1,0:T(8,128)}, f32[224,256]{1,0:T(8,128)S(1)}, u32[]{:S(2)}, u32[]{:S(2)}) collective-permute-start(f32[224,256]{1,0:T(8,128)} %get-tuple-element.75), channel_id=1, source_target_pairs={{1,2},{3,4},{5,6},{2,1},{4,3},{6,5},{9,10},{11,12},{13,14},{10,9},... | collective-permute-start | bytes 688136 | tf_op jit(solution)/shard_map/ppermute | solution.py:873
  3.4 14.7 %collective-permute-start.1 = (f32[224,256]{1,0:T(8,128)}, f32[224,256]{1,0:T(8,128)S(1)}, u32[]{:S(2)}, u32[]{:S(2)}) collective-permute-start(f32[224,256]{1,0:T(8,128)} %get-tuple-element.76), channel_id=1, source_target_pairs={{0,1},{2,3},{4,5},{6,7},{1,0},{3,2},{5,4},{7,6},{8,9},{10,11},{12,... | collective-permute-start | bytes 688136 | tf_op jit(solution)/shard_map/ppermute | solution.py:873
  8.0 1.2 %copy-start.2 = (f32[32,32,256]{2,1,0:T(8,128)S(1)}, f32[32,32,256]{2,1,0:T(8,128)}, u32[]{:S(2)}) copy-start(f32[32,32,256]{2,1,0:T(8,128)} %phi.9) | copy-start | bytes 3145732
  9.2 0.7 copy-start.5
  10.6 11.4 %copy-start.3 = (f32[32,32,256]{2,1,0:T(8,128)S(1)}, f32[32,32,256]{2,1,0:T(8,128)}, u32[]{:S(2)}) copy-start(f32[32,32,256]{2,1,0:T(8,128)} %phi.9) | copy-start | bytes 3145732
  10.6 7.0 %collective-permute-start.4 = (f32[2,256]{1,0:T(2,128)S(1)}, f32[2,256]{1,0:T(2,128)S(1)}, u32[]{:S(2)}, u32[]{:S(2)}) collective-permute-start(f32[2,256]{1,0:T(2,128)S(1)} %get-tuple-element.93), channel_id=1, source_target_pairs={{0,4},{1,5},{2,6},{3,7},{4,0},{5,1},{6,2},{7,3},{8,12},{9,13},{10,... | collective-permute-start | bytes 6152 | tf_op jit(solution)/shard_map/ppermute | solution.py:877
  13.0 9.0 %collective-permute-start.6 = (f32[22,8,256]{2,1,0:T(8,128)S(1)}, f32[22,8,256]{2,1,0:T(8,128)S(1)}, u32[]{:S(2)}, u32[]{:S(2)}) collective-permute-start(f32[22,8,256]{2,1,0:T(8,128)S(1)} %get-tuple-element.95), channel_id=1, source_target_pairs={{8,16},{16,8},{9,17},{17,9},{10,18},{18,10},{11,19},{19,11},{12,20... | collective-permute-start | bytes 540680 | tf_op jit(solution)/shard_map/ppermute | solution.py:873
  17.5 4.5 %collective-permute-start.7 = (f32[22,8,256]{2,1,0:T(8,128)S(1)}, f32[22,8,256]{2,1,0:T(8,128)S(1)}, u32[]{:S(2)}, u32[]{:S(2)}) collective-permute-start(f32[22,8,256]{2,1,0:T(8,128)S(1)} %get-tuple-element.96), channel_id=1, source_target_pairs={{0,8},{16,24},{8,0},{24,16},{1,9},{17,25},{9,1},{25,17},{2,10},{18... | collective-permute-start | bytes 540680 | tf_op jit(solution)/shard_map/ppermute | solution.py:873
  17.6 4.3 %collective-permute-start.5 = (f32[4,256]{1,0:T(4,128)S(1)}, f32[4,256]{1,0:T(4,128)S(1)}, u32[]{:S(2)}, u32[]{:S(2)}) collective-permute-start(f32[4,256]{1,0:T(4,128)S(1)} %pad_maximum_fusion.1), channel_id=1, source_target_pairs={{0,2},{1,3},{2,0},{3,1},{4,6},{5,7},{6,4},{7,5},{8,10},{9,11},{10,... | collective-permute-start | bytes 12296 | tf_op jit(solution)/shard_map/ppermute | solution.py:877
  18.1 6.9 %copy-start.4 = (f32[32,32,256]{2,1,0:T(8,128)S(1)}, f32[32,32,256]{2,1,0:T(8,128)}, u32[]{:S(2)}) copy-start(f32[32,32,256]{2,1,0:T(8,128)} %solid.3) | copy-start | bytes 3145732
  18.2 10.9 %collective-permute-start.2 = (f32[35,8,256]{2,1,0:T(8,128)S(1)}, f32[35,8,256]{2,1,0:T(8,128)S(1)}, u32[]{:S(2)}, u32[]{:S(2)}) collective-permute-start(f32[35,8,256]{2,1,0:T(8,128)S(1)} %get-tuple-element.79), channel_id=1, source_target_pairs={{8,16},{16,8},{9,17},{17,9},{10,18},{18,10},{11,19},{19,11},{12,20... | collective-permute-start | bytes 860168 | tf_op jit(solution)/shard_map/ppermute | solution.py:873
  21.9 7.2 %collective-permute-start.3 = (f32[35,8,256]{2,1,0:T(8,128)S(1)}, f32[35,8,256]{2,1,0:T(8,128)S(1)}, u32[]{:S(2)}, u32[]{:S(2)}) collective-permute-start(f32[35,8,256]{2,1,0:T(8,128)S(1)} %get-tuple-element.80), channel_id=1, source_target_pairs={{0,8},{16,24},{8,0},{24,16},{1,9},{17,25},{9,1},{25,17},{2,10},{18... | collective-permute-start | bytes 860168 | tf_op jit(solution)/shard_map/ppermute | solution.py:873
  22.1 13.5 %collective-permute-start.8 = (f32[272,256]{1,0:T(8,128)S(1)}, f32[272,256]{1,0:T(8,128)S(1)}, u32[]{:S(2)}, u32[]{:S(2)}) collective-permute-start(f32[272,256]{1,0:T(8,128)S(1)} %get-tuple-element.97), channel_id=1, source_target_pairs={{0,1},{2,3},{4,5},{6,7},{1,0},{3,2},{5,4},{7,6},{8,9},{10,11},{12,... | collective-permute-start | bytes 835592 | tf_op jit(solution)/shard_map/ppermute | solution.py:873
  24.3 19.0 %collective-permute-start.13 = (f32[264,256]{1,0:T(8,128)S(1)}, f32[264,256]{1,0:T(8,128)S(1)}, u32[]{:S(2)}, u32[]{:S(2)}) collective-permute-start(f32[264,256]{1,0:T(8,128)S(1)} %get-tuple-element.109), channel_id=1, source_target_pairs={{1,2},{3,4},{5,6},{2,1},{4,3},{6,5},{9,10},{11,12},{13,14},{10,9},... | collective-permute-start | bytes 811016 | tf_op jit(solution)/shard_map/ppermute | solution.py:873
  30.3 7.4 %collective-permute-start.9 = (f32[96,256]{1,0:T(8,128)S(1)}, f32[96,256]{1,0:T(8,128)S(1)}, u32[]{:S(2)}, u32[]{:S(2)}) collective-permute-start(f32[96,256]{1,0:T(8,128)S(1)} %get-tuple-element.101), channel_id=1, source_target_pairs={{0,1},{2,3},{4,5},{6,7},{1,0},{3,2},{5,4},{7,6},{8,9},{10,11},{12,... | collective-permute-start | bytes 294920 | tf_op jit(solution)/shard_map/ppermute | solution.py:873
  34.1 3.6 %collective-permute-start.10 = (f32[96,256]{1,0:T(8,128)S(1)}, f32[96,256]{1,0:T(8,128)S(1)}, u32[]{:S(2)}, u32[]{:S(2)}) collective-permute-start(f32[96,256]{1,0:T(8,128)S(1)} %get-tuple-element.102), channel_id=1, source_target_pairs={{1,2},{3,4},{5,6},{2,1},{4,3},{6,5},{9,10},{11,12},{13,14},{10,9},... | collective-permute-start | bytes 294920 | tf_op jit(solution)/shard_map/ppermute | solution.py:873
  37.8 8.8 %collective-permute-start.11 = (f32[15,8,256]{2,1,0:T(8,128)S(1)}, f32[15,8,256]{2,1,0:T(8,128)S(1)}, u32[]{:S(2)}, u32[]{:S(2)}) collective-permute-start(f32[15,8,256]{2,1,0:T(8,128)S(1)} %get-tuple-element.105), channel_id=1, source_target_pairs={{8,16},{16,8},{9,17},{17,9},{10,18},{18,10},{11,19},{19,11},{12,20... | collective-permute-start | bytes 368648 | tf_op jit(solution)/shard_map/ppermute | solution.py:873
  43.3 3.4 %collective-permute-start.12 = (f32[15,8,256]{2,1,0:T(8,128)S(1)}, f32[15,8,256]{2,1,0:T(8,128)S(1)}, u32[]{:S(2)}, u32[]{:S(2)}) collective-permute-start(f32[15,8,256]{2,1,0:T(8,128)S(1)} %get-tuple-element.106), channel_id=1, source_target_pairs={{0,8},{16,24},{8,0},{24,16},{1,9},{17,25},{9,1},{25,17},{2,10},{18... | collective-permute-start | bytes 368648 | tf_op jit(solution)/shard_map/ppermute | solution.py:873
  47.3 6.8 %collective-permute-start.14 = (f32[64,256]{1,0:T(8,128)S(1)}, f32[64,256]{1,0:T(8,128)S(1)}, u32[]{:S(2)}, u32[]{:S(2)}) collective-permute-start(f32[64,256]{1,0:T(8,128)S(1)} %get-tuple-element.116), channel_id=1, source_target_pairs={{1,2},{3,4},{5,6},{2,1},{4,3},{6,5},{9,10},{11,12},{13,14},{10,9},... | collective-permute-start | bytes 196616 | tf_op jit(solution)/shard_map/ppermute | solution.py:873
  47.9 7.0 %collective-permute-start.15 = (f32[64,256]{1,0:T(8,128)S(1)}, f32[64,256]{1,0:T(8,128)S(1)}, u32[]{:S(2)}, u32[]{:S(2)}) collective-permute-start(f32[64,256]{1,0:T(8,128)S(1)} %get-tuple-element.117), channel_id=1, source_target_pairs={{0,1},{2,3},{4,5},{6,7},{1,0},{3,2},{5,4},{7,6},{8,9},{10,11},{12,... | collective-permute-start | bytes 196616 | tf_op jit(solution)/shard_map/ppermute | solution.py:873
  55.0 5.9 %collective-permute-start.16 = (f32[12,8,256]{2,1,0:T(8,128)S(1)}, f32[12,8,256]{2,1,0:T(8,128)S(1)}, u32[]{:S(2)}, u32[]{:S(2)}) collective-permute-start(f32[12,8,256]{2,1,0:T(8,128)S(1)} %get-tuple-element.119), channel_id=1, source_target_pairs={{8,16},{16,8},{9,17},{17,9},{10,18},{18,10},{11,19},{19,11},{12,20... | collective-permute-start | bytes 294920 | tf_op jit(solution)/shard_map/ppermute | solution.py:873
  58.6 2.4 %collective-permute-start.17 = (f32[12,8,256]{2,1,0:T(8,128)S(1)}, f32[12,8,256]{2,1,0:T(8,128)S(1)}, u32[]{:S(2)}, u32[]{:S(2)}) collective-permute-start(f32[12,8,256]{2,1,0:T(8,128)S(1)} %get-tuple-element.120), channel_id=1, source_target_pairs={{0,8},{16,24},{8,0},{24,16},{1,9},{17,25},{9,1},{25,17},{2,10},{18... | collective-permute-start | bytes 294920 | tf_op jit(solution)/shard_map/ppermute | solution.py:873
  61.9 4.3 %collective-permute-start.19 = (f32[80,256]{1,0:T(8,128)S(1)}, f32[80,256]{1,0:T(8,128)S(1)}, u32[]{:S(2)}, u32[]{:S(2)}) collective-permute-start(f32[80,256]{1,0:T(8,128)S(1)} %get-tuple-element.127), channel_id=1, source_target_pairs={{0,1},{2,3},{4,5},{6,7},{1,0},{3,2},{5,4},{7,6},{8,9},{10,11},{12,... | collective-permute-start | bytes 245768 | tf_op jit(solution)/shard_map/ppermute | solution.py:873
  64.3 8.2 %collective-permute-start.18 = (f32[72,256]{1,0:T(8,128)S(1)}, f32[72,256]{1,0:T(8,128)S(1)}, u32[]{:S(2)}, u32[]{:S(2)}) collective-permute-start(f32[72,256]{1,0:T(8,128)S(1)} %get-tuple-element.126), channel_id=1, source_target_pairs={{1,2},{3,4},{5,6},{2,1},{4,3},{6,5},{9,10},{11,12},{13,14},{10,9},... | collective-permute-start | bytes 221192 | tf_op jit(solution)/shard_map/ppermute | solution.py:873
  66.3 3.4 %collective-permute-start.20 = (f32[8,256]{1,0:T(8,128)S(1)}, f32[8,256]{1,0:T(8,128)S(1)}, u32[]{:S(2)}, u32[]{:S(2)}) collective-permute-start(f32[8,256]{1,0:T(8,128)S(1)} %slice_add_fusion), channel_id=1, source_target_pairs={{0,2},{1,3},{2,0},{3,1},{4,6},{5,7},{6,4},{7,5},{8,10},{9,11},{10,... | collective-permute-start | bytes 24584 | tf_op jit(solution)/shard_map/ppermute | solution.py:877
  69.6 4.1 %collective-permute-start.21 = (f32[8,256]{1,0:T(8,128)S(1)}, f32[8,256]{1,0:T(8,128)S(1)}, u32[]{:S(2)}, u32[]{:S(2)}) collective-permute-start(f32[8,256]{1,0:T(8,128)S(1)} %add.10), channel_id=1, source_target_pairs={{0,4},{1,5},{2,6},{3,7},{4,0},{5,1},{6,2},{7,3},{8,12},{9,13},{10,... | collective-permute-start | bytes 24584 | tf_op jit(solution)/shard_map/ppermute | solution.py:877
  76.6 5.2 %collective-permute-start.22 = (f32[2,16,256]{2,1,0:T(8,128)S(1)}, f32[2,16,256]{2,1,0:T(8,128)S(1)}, u32[]{:S(2)}, u32[]{:S(2)}) collective-permute-start(f32[2,16,256]{2,1,0:T(8,128)S(1)} %get-tuple-element.132), channel_id=1, source_target_pairs={{8,16},{16,8},{9,17},{17,9},{10,18},{18,10},{11,19},{19,11},{12,20... | collective-permute-start | bytes 98312 | tf_op jit(solution)/shard_map/ppermute | solution.py:873
  79.2 2.6 %collective-permute-start.23 = (f32[2,16,256]{2,1,0:T(8,128)S(1)}, f32[2,16,256]{2,1,0:T(8,128)S(1)}, u32[]{:S(2)}, u32[]{:S(2)}) collective-permute-start(f32[2,16,256]{2,1,0:T(8,128)S(1)} %get-tuple-element.133), channel_id=1, source_target_pairs={{0,8},{16,24},{8,0},{24,16},{1,9},{17,25},{9,1},{25,17},{2,10},{18... | collective-permute-start | bytes 98312 | tf_op jit(solution)/shard_map/ppermute | solution.py:873
